TPU v7x, 32 devices: a whole 2x2x4 slice. The times are simulated.
32 devices in a mesh: hyp: 2 (over y), prow: 4 (over x, core), pcol: 4 (over z).
Axes of the slice: x: 2, y: 2, z: 4, core: 2. Of those that a mesh axis runs over, the one named last changes fastest.
Arguments:
- sigma_rows: bfloat16 [2, 2048, 2048], P('hyp', 'prow', 'pcol'), may hold values from -1 to 1, as said below
- panel: bfloat16 [2, 2048, 2, 384], P('hyp', ('prow', 'pcol')), may hold values from -0.59765625 to 0.59765625
- live_block_rows: int32 [2, 16], P(None, ('prow', 'pcol')), may hold values from 1 to 128, 1536 in all within a row
- inv_diag: bfloat16 [2, 2, 384, 384], P('hyp', None, ('prow', 'pcol')), may hold values from -0.3125 to 0.3125
- quad_weight: float32 [2], P('hyp'), may hold values from 0.05 to 0.5
Outputs:
- sigma_panel: bfloat16 [2, 2048, 2, 384], P('hyp', ('prow', 'pcol'))
- marginal: float32 [2, 384, 384], replicated
Inputs may be any that keep to these rules, and one draw needn't show every extreme that they name: `sigma_rows`: each quadrature point's matrix is symmetric.
All inputs are finite; a program needn't handle non-finite values. No bound on the sum of `live_block_rows` on one device may be relied on, other than what follows from the above.
Results may differ from a plain program's by a relative error of at most 0.0004.
Values may be sent and summed in bfloat16 or wider, within the bound.
No kernel may reach another device: no remote copies, remote signals or barrier semaphores. Data moves between devices by JAX's collectives and lax.ppermute only.
A program may use at most 64 MiB of HBM per device.

v0:
```python
import jax
import jax.numpy as jnp
from jax import lax
from jax.sharding import PartitionSpec as P


def on_device(sigma_rows, panel, live_block_rows, inv_diag, quad_weight):
    height = panel.shape[1]
    width = panel.shape[3]
    supernode_list = panel.shape[2]
    offsets = lax.broadcasted_iota(jnp.int32, (height, supernode_list), 0)
    active = offsets < live_block_rows[:, 0][None, :]
    masked_panel = jnp.where(active[:, :, None], panel[0], jnp.zeros_like(panel[0]))
    grid_rows = lax.axis_size("prow")
    column = lax.axis_index("pcol")
    gathered = lax.all_gather(masked_panel, ("prow", "pcol"), axis=0, tiled=True)
    extent = height * grid_rows
    column_panel = lax.dynamic_slice_in_dim(gathered, column * extent, extent, 0)
    flattened = column_panel.reshape(column_panel.shape[0], supernode_list * width)
    covariance_block = sigma_rows[0]
    applied = lax.psum_scatter(
        jnp.dot(covariance_block, flattened, preferred_element_type=jnp.float32),
        "pcol",
        scatter_dimension=0,
        tiled=True,
    )
    applied_full = applied.reshape(height, supernode_list, width)
    half_applied_product = applied_full.astype(jnp.bfloat16)
    sigma_panel = jnp.where(
        active[:, :, None], -half_applied_product, jnp.zeros_like(half_applied_product)
    )[None]
    coupling_block = jnp.einsum(
        "vwg,vwe->wge",
        masked_panel.astype(jnp.float32),
        applied_full,
        precision=lax.Precision.HIGHEST,
    )
    inverse_local = inv_diag[0]
    diagonal = jnp.einsum(
        "skp,skq->spq", inverse_local, inverse_local, preferred_element_type=jnp.float32
    )
    partial_sum = coupling_block + diagonal
    marginal = lax.psum(quad_weight[0] * partial_sum, ("hyp", "prow", "pcol"))
    return (sigma_panel, marginal)


def solution(mesh):
    in_specs = (
        P("hyp", "prow", "pcol"),
        P("hyp", ("prow", "pcol"), None, None),
        P(None, ("prow", "pcol")),
        P("hyp", None, ("prow", "pcol"), None),
        P("hyp"),
    )
    out_specs = (P("hyp", ("prow", "pcol"), None, None), P())
    return jax.shard_map(
        on_device, mesh=mesh, in_specs=in_specs, out_specs=out_specs, check_vma=False
    )
```

profile of v0, /device:TPU:0, one launch (start us, length us, event | category | flops | bytes accessed | tf_op | source)
XLA Modules:
  0.0 241.6 jit_solution(2163418031371615276)
XLA Ops:
  7.2 0.0 copy-start
  7.2 0.0 all-gather.2.cloned.1.call-start
  7.2 0.7 iota_compare_fusion
  7.9 1.9 broadcast_select_fusion
  9.8 0.0 all-gather.2.cloned.1.call-update
  9.9 0.0 reduce-scatter.2.cloned.1.call-start
  9.9 48.9 %all-gather.2.cloned.1.call-done = bf16[2048,2,384]{2,1,0:T(2,128)(2,1)} async-done(((bf16[128,2,384]{2,1,0:T(2,128)(2,1)}), bf16[2048,2,384]{2,1,0:T(2,128)(2,1)}) %all-gather.2.cloned.1.call-update) | async-done | bytes 3145744 | tf_op jit(solution)/shard_map/all_gather | solution.py:16
  58.8 1.7 constant_dynamic-slice_fusion
  60.5 0.1 copy.14
  60.6 0.0 copy-done
  60.6 1.8 convolution_bitcast_fusion
  62.4 0.0 copy-start.3
  62.4 0.0 copy-start.1
  62.4 0.0 reduce-scatter.2.cloned.1.call-update
  62.4 0.0 all-reduce.2.cloned.1.call-start
  63.2 0.0 copy-done.3
  63.2 0.4 fusion.3
  63.5 33.2 %reduce-scatter.2.cloned.1.call-done = f32[128,768]{0,1:T(8,128)} async-done(((f32[512,768]{0,1:T(8,128)}), f32[128,768]{0,1:T(8,128)}) %reduce-scatter.2.cloned.1.call-update) | async-done | bytes 393232 | tf_op jit(solution)/shard_map/reduce_scatter | solution.py:21
  96.7 0.0 copy-done.1
  96.7 2.7 %fusion = f32[2,384,384]{2,1,0:T(8,128)} fusion(f32[2,384,384]{2,1,0:T(8,128)S(1)} %fusion.3, f32[128,2,384]{0,2,1:T(8,128)} %bitcast.21, f32[]{:T(128)} %bitcast.18, bf16[128,2,384]{2,1,0:T(2,128)(2,1)S(1)} %copy-done.1), kind=kOutput, calls=%fused_computation.2 | convolution fusion | flops 453574656 | bytes 2949124 | tf_op jit(solution)/shard_map/vwg,vwe->wge/dot_general | solution.py:32
  99.4 0.0 copy-start.2
  99.4 0.0 all-reduce.2.cloned.1.call-update
  99.4 1.0 copy-done.2
  100.4 0.2 copy.10
  100.6 1.0 broadcast_select_fusion.1
  101.6 131.2 %all-reduce.2.cloned.1.call-done = f32[2,384,384]{2,1,0:T(8,128)} async-done(((f32[2,384,384]{2,1,0:T(8,128)}), f32[2,384,384]{2,1,0:T(8,128)}) %all-reduce.2.cloned.1.call-update) | async-done | bytes 1179664 | tf_op jit(solution)/shard_map/psum | solution.py:43
  232.8 2.4 copy.19
  (1 shorter events, 0.0 us)
Async XLA Ops:
  7.2 53.4 %copy-start = (bf16[1,512,512]{2,1,0:T(8,128)(2,1)S(1)}, bf16[1,512,512]{2,1,0:T(8,128)(2,1)}, u32[]{:S(2)}) copy-start(bf16[1,512,512]{2,1,0:T(8,128)(2,1)} %param.5) | copy-start | bytes 1572868
  7.2 51.6 %all-gather.2.cloned.1.call-start = ((), (), s32[]{:S(2)}) async-start(), calls=%async_computation.1 | async-start | bytes 3342336 | tf_op jit(solution)/shard_map/all_gather | solution.py:16
  9.9 86.8 %reduce-scatter.2.cloned.1.call-start = ((), (), s32[]{:S(2)}) async-start(), calls=%async_computation.2 | async-start | bytes 1966080 | tf_op jit(solution)/shard_map/reduce_scatter | solution.py:21
  62.4 0.8 copy-start.3
  62.4 34.3 %copy-start.1 = (bf16[128,2,384]{2,1,0:T(2,128)(2,1)S(1)}, bf16[128,2,384]{2,1,0:T(2,128)(2,1)}, u32[]{:S(2)}) copy-start(bf16[128,2,384]{2,1,0:T(2,128)(2,1)} %broadcast_select_fusion) | copy-start | bytes 589828
  62.4 170.3 %all-reduce.2.cloned.1.call-start = ((), (), s32[]{:S(2)}) async-start(), calls=%async_computation.3 | async-start | bytes 2359296 | tf_op jit(solution)/shard_map/psum | solution.py:43
  99.4 1.0 copy-start.2
Sparse Core Ops, SparseCore 0:
  10.9 47.8 all-gather.1
  62.5 34.0 reduce-scatter.1
  102.7 130.0 all-reduce.1
where the time goes:
time: 242 us
  waiting for transfers between devices  213 us (88%)
  between operations  14.5 us (6%)
  local copies, waits for them, and re-layouts  5.34 us (2%)
  matrix products  4.83 us (2%)
  other arithmetic  3.63 us (2%)
    psum x1, waiting for transfers between devices, on_device(): marginal = lax.psum(quad_weight[0] * partial_sum, ('hyp', 'prow', 'pcol'))  131 us
    all_gather x1, waiting for transfers between devices, on_device(): lax.all_gather(masked_panel, ('prow', 'pcol'), axis=0, tiled=True)  48.9 us
    reduce_scatter x1, waiting for transfers between devices, on_device(): lax.psum_scatter(jnp.dot(covariance_block, flattened, preferred_element_t...  33.2 us
  transfers between devices with their start and end apart: 3, of which 3 were waited for; matrix products, arithmetic and copies ran while one was open for 1% of the time, Pallas kernels for 0%

commit v1 on v0

v1 whole, which is shorter than its diff:
```python
import functools

import jax
import jax.numpy as jnp
from jax import lax
from jax.experimental import pallas as pl
from jax.experimental.pallas import tpu as pltpu
from jax.sharding import PartitionSpec as P

LANES = 128
VMEM = pl.BlockSpec(memory_space=pltpu.VMEM)
SMEM = pl.BlockSpec(memory_space=pltpu.SMEM)


def call(kernel, outs, specs, *operands, scratch=()):
    many = isinstance(outs, (list, tuple))
    return pl.pallas_call(
        kernel,
        out_shape=outs,
        in_specs=specs,
        out_specs=[VMEM] * len(outs) if many else VMEM,
        scratch_shapes=scratch,
        compiler_params=pltpu.CompilerParams(vmem_limit_bytes=32 * 2**20),
    )(*operands)


def transposed_dot(left, right):
    return lax.dot_general(
        left, right, (((0,), (0,)), ((), ())), preferred_element_type=jnp.float32
    )


def tiles(width):
    count = width // LANES
    return [(a, b) for a in range(count) for b in range(a, count)]


def general(sigma_rows, panel, live_block_rows, inv_diag, quad_weight):
    height, count, width = panel.shape[1:]
    offsets = lax.broadcasted_iota(jnp.int32, (height, count), 0)
    active = offsets < live_block_rows[:, 0][None, :]
    masked = jnp.where(active[:, :, None], panel[0], jnp.zeros_like(panel[0]))
    extent = height * lax.axis_size("prow")
    gathered = lax.all_gather(masked, ("prow", "pcol"), axis=0, tiled=True)
    start = lax.axis_index("pcol") * sigma_rows.shape[2]
    column_panel = lax.dynamic_slice_in_dim(gathered, start, sigma_rows.shape[2], 0)
    applied = lax.psum_scatter(
        jnp.dot(
            sigma_rows[0],
            column_panel.reshape(sigma_rows.shape[2], count * width),
            preferred_element_type=jnp.float32,
        ),
        "pcol",
        scatter_dimension=0,
        tiled=True,
    ).reshape(height, count, width)
    half = applied.astype(jnp.bfloat16)
    sigma_panel = jnp.where(active[:, :, None], -half, jnp.zeros_like(half))[None]
    coupling = jnp.einsum(
        "vwg,vwe->wge",
        masked.astype(jnp.float32),
        applied,
        precision=lax.Precision.HIGHEST,
    )
    diagonal = jnp.einsum(
        "skp,skq->spq", inv_diag[0], inv_diag[0], preferred_element_type=jnp.float32
    )
    marginal = lax.psum(quad_weight[0] * (coupling + diagonal), ("hyp", "prow", "pcol"))
    return sigma_panel, marginal


def apply_kernel(height, place, own_sigma, far_sigma, *refs):
    blocks, applied, own_rows, panel = refs[:12], refs[12], refs[13], refs[14]
    column, family = place[0], place[1]
    inner = (column == 1) | (column == 2)
    spots = (column, place[2], place[3], place[4])
    extent = 4 * height
    for one in range(2):
        own, near, second_in, second_out, third_in, third_out = blocks[6 * one : 6 * one + 6]
        second = jnp.where(inner, second_in[...], second_out[...])
        third = jnp.where(inner, third_in[...], third_out[...])
        for spot, value in zip(spots, (own[...], near[...], second, third)):
            start = pl.multiple_of(one * extent + spot * height, height)
            panel[pl.ds(start, height), :] = value
    total = transposed_dot(own_sigma[0], panel[pl.ds(0, extent), :])
    total += transposed_dot(far_sigma[0], panel[pl.ds(extent, extent), :])
    applied[...] = total
    own_rows[...] = panel[pl.ds(pl.multiple_of(family * extent, extent), extent), :]


def couple_kernel(height, place, weight, mine, other, rows, inverse_a, inverse_b, *refs):
    outs, keep, send, packed = refs[:4], refs[4], refs[5], refs[6]
    column, point = place[0], place[5]
    applied = mine[...] + other[...]
    high = applied.astype(jnp.bfloat16)
    low = (applied - high.astype(jnp.float32)).astype(jnp.bfloat16)
    packed_half = -high
    scale = weight[0]
    width = applied.shape[1]
    at = 0
    for first in range(width // LANES):
        left = rows[:, first * LANES : (first + 1) * LANES]
        part = transposed_dot(left, high[:, first * LANES :])
        part += transposed_dot(left, low[:, first * LANES :])
        for inverse in (inverse_a, inverse_b):
            part += transposed_dot(
                inverse[:, first * LANES : (first + 1) * LANES], inverse[:, first * LANES :]
            )
        part = scale * part
        for block in range(part.shape[1] // LANES):
            packed[pl.ds(at * LANES, LANES), :] = part[:, block * LANES : (block + 1) * LANES]
            at += 1
    half = packed.shape[0] // 2
    keep[...] = packed[pl.ds(pl.multiple_of(point * half, LANES), half), :]
    send[...] = packed[pl.ds(pl.multiple_of((1 - point) * half, LANES), half), :]
    for block in range(4):
        for step in range(4):
            @pl.when(lax.rem(column + step, 4) == block)
            def _():
                outs[step][...] = packed_half[block * height : (block + 1) * height]


def split_kernel(place, keep, came, *refs):
    outs, whole = refs[:4], refs[4]
    whole[...] = keep[...] + came[...]
    size = outs[0].shape[0]
    for step in range(4):
        spot = place[0] if step == 0 else place[5 + step]
        outs[step][...] = whole[pl.ds(pl.multiple_of(spot * size, 8), size), :]


def sum_kernel(a, b, c, d, out):
    out[...] = (a[...] + b[...]) + (c[...] + d[...])


def join_kernel(place, *refs):
    out = refs[4]
    size = refs[0].shape[0]
    for step in range(4):
        spot = place[0] if step == 0 else place[5 + step]
        out[pl.ds(pl.multiple_of(spot * size, 8), size), :] = refs[step][...]


def spread_kernel(place, *refs):
    out = refs[8]
    width = out.shape[1]
    lead = place[9] == 1
    point, side = place[5], place[10]
    per = len(tiles(width)) // 2
    for half in range(2):
        for node in range(2):
            at_point = half == point
            at_side = node == side
            for same_point in range(2):
                for same_side in range(2):
                    source = (1 - same_point) + 2 * (1 - same_side)
                    for from_lead in range(2):
                        ref = refs[source] if from_lead else refs[4 + source]
                        hit = (at_point == bool(same_point)) & (at_side == bool(same_side))

                        @pl.when(hit & (lead == bool(from_lead)))
                        def _():
                            for index in range(per):
                                a, b = tiles(width)[half * per + index]
                                tile = ref[index * LANES : (index + 1) * LANES, :]
                                out[node, a * LANES : (a + 1) * LANES, b * LANES : (b + 1) * LANES] = tile
                                if a != b:
                                    out[node, b * LANES : (b + 1) * LANES, a * LANES : (a + 1) * LANES] = tile.T


def square(sigma_rows, panel, live_block_rows, inv_diag, quad_weight):
    height, count, width = panel.shape[1:]
    grid = lax.axis_size("pcol")
    points = lax.axis_size("hyp")
    cores = lax.axis_size("prow") // count
    row, column, point = lax.axis_index("prow"), lax.axis_index("pcol"), lax.axis_index("hyp")
    side, core = row // cores, row % cores
    f32, bf16 = jnp.float32, jnp.bfloat16
    shape = jax.ShapeDtypeStruct

    def lead(side, column):
        return side * cores + column % cores

    def move(x, pairs):
        flat = [(a * grid + b, c * grid + d) for (a, b), (c, d) in pairs]
        return lax.ppermute(x, ("prow", "pcol"), flat)

    def along_columns(x, pairs):
        return lax.ppermute(x, "pcol", pairs)

    def across_points(x):
        pairs = []
        for h in range(points):
            for s in range(count):
                for c in range(grid):
                    tail = lead(s, c) * grid + c
                    size = count * cores * grid
                    pairs.append((h * size + tail, (1 - h) * size + tail))
        return lax.ppermute(x, ("hyp", "prow", "pcol"), pairs)

    sides = [(r, (r + cores) % (count * cores)) for r in range(count * cores)]
    leads = [(s, c) for s in range(count) for c in range(grid)]
    to_lead = [((s * cores + 1 - c % cores, c), (lead(s, c), c)) for s, c in leads]
    from_lead = [(b, a) for a, b in to_lead]
    second = jnp.where(column < 2, 2, 1)
    third = jnp.where(column < 2, 3, 0)
    place = jnp.stack(
        [
            column,
            (side != column // cores).astype(jnp.int32),
            column ^ 1,
            second,
            third,
            point,
            column ^ 1,
            column ^ 2,
            column ^ 3,
            (core == column % cores).astype(jnp.int32),
            side,
        ]
    ).astype(jnp.int32)

    far_sigma = lax.ppermute(sigma_rows, "prow", sides)

    offsets = lax.broadcasted_iota(jnp.int32, (height, count), 0)
    active = offsets < live_block_rows[:, 0][None, :]
    masked = jnp.where(active[:, :, None], panel[0], jnp.zeros_like(panel[0]))
    masked = jnp.transpose(masked, (1, 0, 2))
    own = lax.dynamic_index_in_dim(masked, side, 0, keepdims=False)
    give = lax.dynamic_index_in_dim(masked, 1 - side, 0, keepdims=False)
    got = lax.ppermute(give, "prow", sides)
    own_inverse = lax.dynamic_index_in_dim(inv_diag[0], side, 0, keepdims=False)
    got_inverse = lax.ppermute(
        lax.dynamic_index_in_dim(inv_diag[0], 1 - side, 0, keepdims=False), "prow", sides
    )
    inverse = jnp.concatenate([own_inverse, got_inverse], 0)
    other_inverse = move(inverse, to_lead)

    blocks = []
    for block in (own, got):
        near = along_columns(block, [(0, 1), (1, 0), (2, 3), (3, 2)])
        second_in = along_columns(block, [(1, 2), (2, 1)])
        third_in = along_columns(near, [(1, 2), (2, 1)])
        second_out = along_columns(second_in, [(1, 0), (2, 3)])
        third_out = along_columns(third_in, [(1, 0), (2, 3)])
        blocks += [block, near, second_in, second_out, third_in, third_out]

    extent = sigma_rows.shape[2]
    applied, rows = call(
        functools.partial(apply_kernel, height),
        [shape((extent, width), f32), shape((extent, width), bf16)],
        [SMEM] + [VMEM] * 14,
        place,
        sigma_rows,
        far_sigma,
        *blocks,
        scratch=[pltpu.VMEM((2 * extent, width), bf16)],
    )
    other = move(applied, to_lead)

    packed = len(tiles(width)) * LANES
    *pieces, keep, send = call(
        functools.partial(couple_kernel, height),
        [shape((height, width), bf16)] * 4 + [shape((packed // 2, LANES), f32)] * 2,
        [SMEM, SMEM] + [VMEM] * 5,
        place,
        quad_weight,
        applied,
        other,
        rows,
        inverse,
        other_inverse,
        scratch=[pltpu.VMEM((packed, LANES), f32)],
    )

    came = across_points(send)
    steps = [
        [((lead(s, c), c), (lead(s, c ^ step), c ^ step)) for s, c in leads] for step in (1, 2, 3)
    ]
    size = packed // 2 // grid
    part = call(
        split_kernel,
        [shape((size, LANES), f32)] * 4,
        [SMEM, VMEM, VMEM],
        place,
        keep,
        came,
        scratch=[pltpu.VMEM((packed // 2, LANES), f32)],
    )
    arrived = [move(x, pairs) for x, pairs in zip(part[1:], steps)]
    done = call(sum_kernel, shape((size, LANES), f32), [VMEM] * 4, part[0], *arrived)
    others = [move(done, pairs) for pairs in steps]
    own_half = call(
        join_kernel,
        shape((packed // 2, LANES), f32),
        [SMEM] + [VMEM] * 4,
        place,
        done,
        *others,
    )
    cross = [((lead(s, c), c), (lead(1 - s, c), c)) for s, c in leads]
    point_half = across_points(own_half)
    side_half = move(own_half, cross)
    both_half = move(point_half, cross)
    halves = [own_half, point_half, side_half, both_half]
    copies = [move(x, from_lead) for x in halves]
    marginal = call(
        spread_kernel,
        shape((count, width, width), f32),
        [SMEM] + [VMEM] * 8,
        place,
        *halves,
        *copies,
    )

    landed = []
    for s in range(count):
        total = None
        for step in range(4):
            pairs = [((lead(s, c), c), (c, (c + step) % grid)) for c in range(grid)]
            value = move(pieces[step], pairs)
            total = value if total is None else total + value
        landed.append(total)
    sigma_panel = jnp.stack(landed, 1)
    sigma_panel = jnp.where(active[:, :, None], sigma_panel, jnp.zeros_like(sigma_panel))
    return sigma_panel[None], marginal


def solution(mesh):
    sizes = dict(mesh.shape)

    def on_device(sigma_rows, panel, live_block_rows, inv_diag, quad_weight):
        height, count, width = panel.shape[1:]
        grid = sizes["pcol"]
        fits = (
            sizes["hyp"] == 2
            and grid == 4
            and sizes["prow"] == grid
            and count == 2
            and sigma_rows.shape[1] == sigma_rows.shape[2] == grid * height
            and width % LANES == 0
            and len(tiles(width)) % 2 == 0
            and len(tiles(width)) // 2 * LANES % (8 * grid) == 0
        )
        body = square if fits else general
        return body(sigma_rows, panel, live_block_rows, inv_diag, quad_weight)

    in_specs = (
        P("hyp", "prow", "pcol"),
        P("hyp", ("prow", "pcol"), None, None),
        P(None, ("prow", "pcol")),
        P("hyp", None, ("prow", "pcol"), None),
        P("hyp"),
    )
    out_specs = (P("hyp", ("prow", "pcol"), None, None), P())
    return jax.shard_map(
        on_device, mesh=mesh, in_specs=in_specs, out_specs=out_specs, check_vma=False
    )
```

time: 242 us -> 119 us (0.49)
  the two profiles are of different devices: /device:TPU:0 before, /device:TPU:21 now
where the time goes in v1:
time: 119 us
  waiting for transfers between devices  61.1 us (51%)
  starting transfers between devices  46.8 us (39%)
  Pallas kernels  5.92 us (5%)
  other arithmetic  1.93 us (2%)
  between operations  1.89 us (2%)
    ppermute x22, waiting for transfers between devices, move(): return lax.ppermute(x, ('prow', 'pcol'), flat)  46.3 us
    ppermute x22, starting transfers between devices, move(): return lax.ppermute(x, ('prow', 'pcol'), flat)  24.3 us
    ppermute x10, starting transfers between devices, along_columns(): return lax.ppermute(x, 'pcol', pairs)  18.3 us
    ppermute x1, waiting for transfers between devices, square(): got = lax.ppermute(give, 'prow', sides)  10.4 us
    pallas_call x6, Pallas kernels, call(): pl.pallas_call(kernel, out_shape=outs, in_specs=specs, out_specs=[VMEM] *...  5.92 us
    ppermute x10, waiting for transfers between devices, along_columns(): return lax.ppermute(x, 'pcol', pairs)  2.82 us
  transfers between devices with their start and end apart: 37, of which 11 were waited for; matrix products, arithmetic and copies ran while one was open for 2% of the time, Pallas kernels for 0%

profile of v1, /device:TPU:21, one launch (start us, length us, event | category | flops | bytes accessed | tf_op | source)
XLA Modules:
  0.0 118.7 jit_solution(10156981060775324822)
XLA Ops:
  0.6 1.3 %collective-permute-start = (bf16[1,512,512]{2,1,0:T(8,128)(2,1)}, bf16[1,512,512]{2,1,0:T(8,128)(2,1)S(1)}, u32[]{:S(2)}, u32[]{:S(2)}) collective-permute-start(bf16[1,512,512]{2,1,0:T(8,128)(2,1)} %own_sigma.1), channel_id=1, source_target_pairs={{0,8},{4,12},{8,0},{12,4},{1,9},{5,13},{9,1},{13,5},{2,10},{6,14},... | collective-permute-start | bytes 1572872 | tf_op jit(solution)/shard_map/ppermute | solution.py:223
  4.1 1.3 %collective-permute-start.1 = (bf16[128,384]{1,0:T(8,128)(2,1)S(1)}, bf16[128,384]{1,0:T(8,128)(2,1)S(1)}, u32[]{:S(2)}, u32[]{:S(2)}) collective-permute-start(bf16[128,384]{1,0:T(8,128)(2,1)S(1)} %get-tuple-element.31.refs_0_), channel_id=1, source_target_pairs={{0,1},{1,0},{2,3},{3,2},{4,5},{5,4},{6,7},{7,6},{8,9},{9,8},{10,11... | collective-permute-start | bytes 294920 | tf_op jit(solution)/shard_map/ppermute | solution.py:189
  5.4 10.4 %collective-permute-done.6.refs_6_ = bf16[128,384]{1,0:T(8,128)(2,1)S(1)} collective-permute-done((bf16[128,384]{1,0:T(8,128)(2,1)S(1)}, bf16[128,384]{1,0:T(8,128)(2,1)S(1)}, u32[]{:S(2)}, u32[]{:S(2)}) %collective-permute-start.6) | collective-permute-done | bytes 98336 | tf_op jit(solution)/shard_map/ppermute | solution.py:231
  15.8 1.3 %collective-permute-start.7 = (bf16[128,384]{1,0:T(8,128)(2,1)S(1)}, bf16[128,384]{1,0:T(8,128)(2,1)S(1)}, u32[]{:S(2)}, u32[]{:S(2)}) collective-permute-start(bf16[128,384]{1,0:T(8,128)(2,1)S(1)} %collective-permute-done.6.refs_6_), channel_id=1, source_target_pairs={{0,1},{1,0},{2,3},{3,2},{4,5},{5,4},{6,7},{7,6},{8,9},{9,8},{10,11... | collective-permute-start | bytes 294920 | tf_op jit(solution)/shard_map/ppermute | solution.py:189
  17.1 1.9 %collective-permute-start.2 = (bf16[128,384]{1,0:T(8,128)(2,1)S(1)}, bf16[128,384]{1,0:T(8,128)(2,1)S(1)}, u32[]{:S(2)}, u32[]{:S(2)}) collective-permute-start(bf16[128,384]{1,0:T(8,128)(2,1)S(1)} %get-tuple-element.31.refs_0_), channel_id=1, source_target_pairs={{1,2},{2,1},{5,6},{6,5},{9,10},{10,9},{13,14},{14,13},{17,18},{18,... | collective-permute-start | bytes 294920 | tf_op jit(solution)/shard_map/ppermute | solution.py:189
  19.0 3.4 %collective-permute-start.4 = (bf16[128,384]{1,0:T(8,128)(2,1)S(1)}, bf16[128,384]{1,0:T(8,128)(2,1)S(1)}, u32[]{:S(2)}, u32[]{:S(2)}) collective-permute-start(bf16[128,384]{1,0:T(8,128)(2,1)S(1)} %collective-permute-done.1.refs_1_), channel_id=1, source_target_pairs={{1,2},{2,1},{5,6},{6,5},{9,10},{10,9},{13,14},{14,13},{17,18},{18,... | collective-permute-start | bytes 294920 | tf_op jit(solution)/shard_map/ppermute | solution.py:189
  22.4 1.9 %collective-permute-start.8 = (bf16[128,384]{1,0:T(8,128)(2,1)S(1)}, bf16[128,384]{1,0:T(8,128)(2,1)S(1)}, u32[]{:S(2)}, u32[]{:S(2)}) collective-permute-start(bf16[128,384]{1,0:T(8,128)(2,1)S(1)} %collective-permute-done.6.refs_6_), channel_id=1, source_target_pairs={{1,2},{2,1},{5,6},{6,5},{9,10},{10,9},{13,14},{14,13},{17,18},{18,... | collective-permute-start | bytes 294920 | tf_op jit(solution)/shard_map/ppermute | solution.py:189
  24.3 3.4 %collective-permute-start.10 = (bf16[128,384]{1,0:T(8,128)(2,1)S(1)}, bf16[128,384]{1,0:T(8,128)(2,1)S(1)}, u32[]{:S(2)}, u32[]{:S(2)}) collective-permute-start(bf16[128,384]{1,0:T(8,128)(2,1)S(1)} %collective-permute-done.7.refs_7_), channel_id=1, source_target_pairs={{1,2},{2,1},{5,6},{6,5},{9,10},{10,9},{13,14},{14,13},{17,18},{18,... | collective-permute-start | bytes 294920 | tf_op jit(solution)/shard_map/ppermute | solution.py:189
  27.7 1.3 %collective-permute-start.3 = (bf16[128,384]{1,0:T(8,128)(2,1)S(1)}, bf16[128,384]{1,0:T(8,128)(2,1)S(1)}, u32[]{:S(2)}, u32[]{:S(2)}) collective-permute-start(bf16[128,384]{1,0:T(8,128)(2,1)S(1)} %collective-permute-done.2.refs_2_), channel_id=1, source_target_pairs={{1,0},{2,3},{5,4},{6,7},{9,8},{10,11},{13,12},{14,15},{17,16},{18,... | collective-permute-start | bytes 294920 | tf_op jit(solution)/shard_map/ppermute | solution.py:189
  29.0 1.3 %collective-permute-start.5 = (bf16[128,384]{1,0:T(8,128)(2,1)S(1)}, bf16[128,384]{1,0:T(8,128)(2,1)S(1)}, u32[]{:S(2)}, u32[]{:S(2)}) collective-permute-start(bf16[128,384]{1,0:T(8,128)(2,1)S(1)} %collective-permute-done.4.refs_4_), channel_id=1, source_target_pairs={{1,0},{2,3},{5,4},{6,7},{9,8},{10,11},{13,12},{14,15},{17,16},{18,... | collective-permute-start | bytes 294920 | tf_op jit(solution)/shard_map/ppermute | solution.py:189
  30.4 1.3 %collective-permute-start.9 = (bf16[128,384]{1,0:T(8,128)(2,1)S(1)}, bf16[128,384]{1,0:T(8,128)(2,1)S(1)}, u32[]{:S(2)}, u32[]{:S(2)}) collective-permute-start(bf16[128,384]{1,0:T(8,128)(2,1)S(1)} %collective-permute-done.8.refs_8_), channel_id=1, source_target_pairs={{1,0},{2,3},{5,4},{6,7},{9,8},{10,11},{13,12},{14,15},{17,16},{18,... | collective-permute-start | bytes 294920 | tf_op jit(solution)/shard_map/ppermute | solution.py:189
  31.7 1.3 %collective-permute-start.11 = (bf16[128,384]{1,0:T(8,128)(2,1)S(1)}, bf16[128,384]{1,0:T(8,128)(2,1)S(1)}, u32[]{:S(2)}, u32[]{:S(2)}) collective-permute-start(bf16[128,384]{1,0:T(8,128)(2,1)S(1)} %collective-permute-done.10.refs_10_), channel_id=1, source_target_pairs={{1,0},{2,3},{5,4},{6,7},{9,8},{10,11},{13,12},{14,15},{17,16},{18,... | collective-permute-start | bytes 294920 | tf_op jit(solution)/shard_map/ppermute | solution.py:189
  33.8 2.1 %collective-permute-done.11.refs_11_ = bf16[128,384]{1,0:T(8,128)(2,1)S(1)} collective-permute-done((bf16[128,384]{1,0:T(8,128)(2,1)S(1)}, bf16[128,384]{1,0:T(8,128)(2,1)S(1)}, u32[]{:S(2)}, u32[]{:S(2)}) %collective-permute-start.11) | collective-permute-done | bytes 98336 | tf_op jit(solution)/shard_map/ppermute | solution.py:189
  35.9 1.4 %shard_map.68 = (f32[512,384]{1,0:T(8,128)S(1)}, bf16[512,384]{1,0:T(8,128)(2,1)S(1)}) custom-call(s32[11]{0:T(128)S(1)} %stack.61.place, bf16[1,512,512]{2,1,0:T(8,128)(2,1)S(1)} %copy-done, bf16[1,512,512]{2,1,0:T(8,128)(2,1)S(1)} %collective-permute-done.far_sigma, bf16[128,384]{1,0:T(8,128)(2,1)S(1)} %get-tuple-element.31.refs_0_, ...), custom_call_target="tpu_custom_call" | custom-call | tf_op jit(solution)/shard_map/pallas_call | solution.py:17
  37.3 4.9 %collective-permute-start.12 = (f32[512,384]{1,0:T(8,128)S(1)}, f32[512,384]{1,0:T(8,128)S(1)}, u32[]{:S(2)}, u32[]{:S(2)}) collective-permute-start(f32[512,384]{1,0:T(8,128)S(1)} %get-tuple-element.14.mine), channel_id=1, source_target_pairs={{4,0},{1,5},{6,2},{3,7},{12,8},{9,13},{14,10},{11,15},{20,16},{17,... | collective-permute-start | bytes 2359304 | tf_op jit(solution)/shard_map/ppermute | solution.py:186
  42.2 1.3 %collective-permute-start.13 = (bf16[24,384]{1,0:T(8,128)(2,1)S(1)}, bf16[24,384]{1,0:T(8,128)(2,1)S(1)}, u32[]{:S(2)}, u32[]{:S(2)}) collective-permute-start(bf16[24,384]{1,0:T(8,128)(2,1)S(1)} %get-tuple-element.33), channel_id=1, source_target_pairs={{0,8},{4,12},{8,0},{12,4},{1,9},{5,13},{9,1},{13,5},{2,10},{6,14},... | collective-permute-start | bytes 55304 | tf_op jit(solution)/shard_map/ppermute | solution.py:233
  43.5 1.5 %collective-permute-done.13 = bf16[24,384]{1,0:T(8,128)(2,1)S(1)} collective-permute-done((bf16[24,384]{1,0:T(8,128)(2,1)S(1)}, bf16[24,384]{1,0:T(8,128)(2,1)S(1)}, u32[]{:S(2)}, u32[]{:S(2)}) %collective-permute-start.13) | collective-permute-done | bytes 18464 | tf_op jit(solution)/shard_map/ppermute | solution.py:233
  45.0 2.3 %collective-permute-start.14 = (bf16[48,384]{1,0:T(8,128)(2,1)S(1)}, bf16[48,384]{1,0:T(8,128)(2,1)S(1)}, u32[]{:S(2)}, u32[]{:S(2)}) collective-permute-start(bf16[48,384]{1,0:T(8,128)(2,1)S(1)} %pad_maximum_fusion.inverse_a), channel_id=1, source_target_pairs={{4,0},{1,5},{6,2},{3,7},{12,8},{9,13},{14,10},{11,15},{20,16},{17,... | collective-permute-start | bytes 110600 | tf_op jit(solution)/shard_map/ppermute | solution.py:186
  48.2 1.3 %shard_map.69 = (bf16[128,384]{1,0:T(8,128)(2,1)S(1)}, bf16[128,384]{1,0:T(8,128)(2,1)S(1)}, bf16[128,384]{1,0:T(8,128)(2,1)S(1)}, bf16[128,384]{1,0:T(8,128)(2,...) custom-call(s32[11]{0:T(128)S(1)} %stack.61.place, f32[1]{0:T(128)S(6)} %copy.12.weight, ...), custom_call_target="tpu_custom_call" | custom-call | tf_op jit(solution)/shard_map/pallas_call | solution.py:17
  56.2 1.3 %collective-permute-start.20 = (bf16[128,384]{1,0:T(8,128)(2,1)S(1)}, bf16[128,384]{1,0:T(8,128)(2,1)S(1)}, u32[]{:S(2)}, u32[]{:S(2)}) collective-permute-start(bf16[128,384]{1,0:T(8,128)(2,1)S(1)} %get-tuple-element.17), channel_id=1, source_target_pairs={{8,1},{13,6},{10,11},{15,12},{24,17},{29,22},{26,27},{31,28}} | collective-permute-start | bytes 294920 | tf_op jit(solution)/shard_map/ppermute | solution.py:186
  60.8 1.3 %collective-permute-start.16 = (bf16[128,384]{1,0:T(8,128)(2,1)S(1)}, bf16[128,384]{1,0:T(8,128)(2,1)S(1)}, u32[]{:S(2)}, u32[]{:S(2)}) collective-permute-start(bf16[128,384]{1,0:T(8,128)(2,1)S(1)} %get-tuple-element.17), channel_id=1, source_target_pairs={{0,1},{5,6},{2,11},{7,12},{16,17},{21,22},{18,27},{23,28}} | collective-permute-start | bytes 294920 | tf_op jit(solution)/shard_map/ppermute | solution.py:186
  62.1 24.6 %collective-permute-done.20 = bf16[128,384]{1,0:T(8,128)(2,1)S(1)} collective-permute-done((bf16[128,384]{1,0:T(8,128)(2,1)S(1)}, bf16[128,384]{1,0:T(8,128)(2,1)S(1)}, u32[]{:S(2)}, u32[]{:S(2)}) %collective-permute-start.20) | collective-permute-done | bytes 98336 | tf_op jit(solution)/shard_map/ppermute | solution.py:186
  88.8 8.2 %collective-permute-done.16 = bf16[128,384]{1,0:T(8,128)(2,1)S(1)} collective-permute-done((bf16[128,384]{1,0:T(8,128)(2,1)S(1)}, bf16[128,384]{1,0:T(8,128)(2,1)S(1)}, u32[]{:S(2)}, u32[]{:S(2)}) %collective-permute-start.16) | collective-permute-done | bytes 98336 | tf_op jit(solution)/shard_map/ppermute | solution.py:186
  97.1 1.3 %collective-permute-start.33 = (f32[384,128]{1,0:T(8,128)S(1)}, f32[384,128]{1,0:T(8,128)S(1)}, u32[]{:S(2)}, u32[]{:S(2)}) collective-permute-start(f32[384,128]{1,0:T(8,128)S(1)} %shard_map.72.refs_0_), channel_id=1, source_target_pairs={{0,4},{5,1},{2,6},{7,3},{8,12},{13,9},{10,14},{15,11},{16,20},{21,... | collective-permute-start | bytes 589832 | tf_op jit(solution)/shard_map/ppermute | solution.py:186
  98.4 1.3 %collective-permute-start.34 = (f32[384,128]{1,0:T(8,128)S(1)}, f32[384,128]{1,0:T(8,128)S(1)}, u32[]{:S(2)}, u32[]{:S(2)}) collective-permute-start(f32[384,128]{1,0:T(8,128)S(1)} %collective-permute-done.30.refs_1_), channel_id=1, source_target_pairs={{0,4},{5,1},{2,6},{7,3},{8,12},{13,9},{10,14},{15,11},{16,20},{21,... | collective-permute-start | bytes 589832 | tf_op jit(solution)/shard_map/ppermute | solution.py:186
  99.7 1.3 %collective-permute-start.35 = (f32[384,128]{1,0:T(8,128)S(1)}, f32[384,128]{1,0:T(8,128)S(1)}, u32[]{:S(2)}, u32[]{:S(2)}) collective-permute-start(f32[384,128]{1,0:T(8,128)S(1)} %collective-permute-done.31.refs_2_), channel_id=1, source_target_pairs={{0,4},{5,1},{2,6},{7,3},{8,12},{13,9},{10,14},{15,11},{16,20},{21,... | collective-permute-start | bytes 589832 | tf_op jit(solution)/shard_map/ppermute | solution.py:186
  101.0 1.3 %collective-permute-start.36 = (f32[384,128]{1,0:T(8,128)S(1)}, f32[384,128]{1,0:T(8,128)S(1)}, u32[]{:S(2)}, u32[]{:S(2)}) collective-permute-start(f32[384,128]{1,0:T(8,128)S(1)} %collective-permute-done.32.refs_3_), channel_id=1, source_target_pairs={{0,4},{5,1},{2,6},{7,3},{8,12},{13,9},{10,14},{15,11},{16,20},{21,... | collective-permute-start | bytes 589832 | tf_op jit(solution)/shard_map/ppermute | solution.py:186
  103.3 7.7 %collective-permute-done.33.refs_4_ = f32[384,128]{1,0:T(8,128)S(1)} collective-permute-done((f32[384,128]{1,0:T(8,128)S(1)}, f32[384,128]{1,0:T(8,128)S(1)}, u32[]{:S(2)}, u32[]{:S(2)}) %collective-permute-start.33) | collective-permute-done | bytes 196640 | tf_op jit(solution)/shard_map/ppermute | solution.py:186
  111.0 1.3 %collective-permute-done.34.refs_5_ = f32[384,128]{1,0:T(8,128)S(1)} collective-permute-done((f32[384,128]{1,0:T(8,128)S(1)}, f32[384,128]{1,0:T(8,128)S(1)}, u32[]{:S(2)}, u32[]{:S(2)}) %collective-permute-start.34) | collective-permute-done | bytes 196640 | tf_op jit(solution)/shard_map/ppermute | solution.py:186
  112.3 1.3 %collective-permute-done.35.refs_6_ = f32[384,128]{1,0:T(8,128)S(1)} collective-permute-done((f32[384,128]{1,0:T(8,128)S(1)}, f32[384,128]{1,0:T(8,128)S(1)}, u32[]{:S(2)}, u32[]{:S(2)}) %collective-permute-start.35) | collective-permute-done | bytes 196640 | tf_op jit(solution)/shard_map/ppermute | solution.py:186
  113.6 2.9 %collective-permute-done.36.refs_7_ = f32[384,128]{1,0:T(8,128)S(1)} collective-permute-done((f32[384,128]{1,0:T(8,128)S(1)}, f32[384,128]{1,0:T(8,128)S(1)}, u32[]{:S(2)}, u32[]{:S(2)}) %collective-permute-start.36) | collective-permute-done | bytes 196640 | tf_op jit(solution)/shard_map/ppermute | solution.py:186
  116.6 2.1 %shard_map.73 = f32[2,384,384]{2,1,0:T(8,128)} custom-call(s32[11]{0:T(128)S(1)} %stack.61.place, f32[384,128]{1,0:T(8,128)S(1)} %shard_map.72.refs_0_, f32[384,128]{1,0:T(8,128)S(1)} %collective-permute-done.30.refs_1_, f32[384,128]{1,0:T(8,128)S(1)} %collective-permute-done.31.refs_2_, f32[384,128]{1,0:T(8,128)S(1)} %collective-permute-done.32.refs_3_, ...), custom_call_target="tpu_custom_call" | custom-call | tf_op jit(solution)/shard_map/pallas_call | solution.py:17
  (62 shorter events, 16.1 us)
Async XLA Ops:
  0.6 35.3 %collective-permute-start = (bf16[1,512,512]{2,1,0:T(8,128)(2,1)}, bf16[1,512,512]{2,1,0:T(8,128)(2,1)S(1)}, u32[]{:S(2)}, u32[]{:S(2)}) collective-permute-start(bf16[1,512,512]{2,1,0:T(8,128)(2,1)} %own_sigma.1), channel_id=1, source_target_pairs={{0,8},{4,12},{8,0},{12,4},{1,9},{5,13},{9,1},{13,5},{2,10},{6,14},... | collective-permute-start | bytes 1572872 | tf_op jit(solution)/shard_map/ppermute | solution.py:223
  3.8 12.1 %collective-permute-start.6 = (bf16[128,384]{1,0:T(8,128)(2,1)S(1)}, bf16[128,384]{1,0:T(8,128)(2,1)S(1)}, u32[]{:S(2)}, u32[]{:S(2)}) collective-permute-start(bf16[128,384]{1,0:T(8,128)(2,1)S(1)} %get-tuple-element.30), channel_id=1, source_target_pairs={{0,8},{4,12},{8,0},{12,4},{1,9},{5,13},{9,1},{13,5},{2,10},{6,14},... | collective-permute-start | bytes 294920 | tf_op jit(solution)/shard_map/ppermute | solution.py:231
  4.1 15.0 %collective-permute-start.1 = (bf16[128,384]{1,0:T(8,128)(2,1)S(1)}, bf16[128,384]{1,0:T(8,128)(2,1)S(1)}, u32[]{:S(2)}, u32[]{:S(2)}) collective-permute-start(bf16[128,384]{1,0:T(8,128)(2,1)S(1)} %get-tuple-element.31.refs_0_), channel_id=1, source_target_pairs={{0,1},{1,0},{2,3},{3,2},{4,5},{5,4},{6,7},{7,6},{8,9},{9,8},{10,11... | collective-permute-start | bytes 294920 | tf_op jit(solution)/shard_map/ppermute | solution.py:189
  15.8 8.5 %collective-permute-start.7 = (bf16[128,384]{1,0:T(8,128)(2,1)S(1)}, bf16[128,384]{1,0:T(8,128)(2,1)S(1)}, u32[]{:S(2)}, u32[]{:S(2)}) collective-permute-start(bf16[128,384]{1,0:T(8,128)(2,1)S(1)} %collective-permute-done.6.refs_6_), channel_id=1, source_target_pairs={{0,1},{1,0},{2,3},{3,2},{4,5},{5,4},{6,7},{7,6},{8,9},{9,8},{10,11... | collective-permute-start | bytes 294920 | tf_op jit(solution)/shard_map/ppermute | solution.py:189
  17.1 10.6 %collective-permute-start.2 = (bf16[128,384]{1,0:T(8,128)(2,1)S(1)}, bf16[128,384]{1,0:T(8,128)(2,1)S(1)}, u32[]{:S(2)}, u32[]{:S(2)}) collective-permute-start(bf16[128,384]{1,0:T(8,128)(2,1)S(1)} %get-tuple-element.31.refs_0_), channel_id=1, source_target_pairs={{1,2},{2,1},{5,6},{6,5},{9,10},{10,9},{13,14},{14,13},{17,18},{18,... | collective-permute-start | bytes 294920 | tf_op jit(solution)/shard_map/ppermute | solution.py:189
  19.0 10.0 %collective-permute-start.4 = (bf16[128,384]{1,0:T(8,128)(2,1)S(1)}, bf16[128,384]{1,0:T(8,128)(2,1)S(1)}, u32[]{:S(2)}, u32[]{:S(2)}) collective-permute-start(bf16[128,384]{1,0:T(8,128)(2,1)S(1)} %collective-permute-done.1.refs_1_), channel_id=1, source_target_pairs={{1,2},{2,1},{5,6},{6,5},{9,10},{10,9},{13,14},{14,13},{17,18},{18,... | collective-permute-start | bytes 294920 | tf_op jit(solution)/shard_map/ppermute | solution.py:189
  22.4 7.9 %collective-permute-start.8 = (bf16[128,384]{1,0:T(8,128)(2,1)S(1)}, bf16[128,384]{1,0:T(8,128)(2,1)S(1)}, u32[]{:S(2)}, u32[]{:S(2)}) collective-permute-start(bf16[128,384]{1,0:T(8,128)(2,1)S(1)} %collective-permute-done.6.refs_6_), channel_id=1, source_target_pairs={{1,2},{2,1},{5,6},{6,5},{9,10},{10,9},{13,14},{14,13},{17,18},{18,... | collective-permute-start | bytes 294920 | tf_op jit(solution)/shard_map/ppermute | solution.py:189
  24.3 7.3 %collective-permute-start.10 = (bf16[128,384]{1,0:T(8,128)(2,1)S(1)}, bf16[128,384]{1,0:T(8,128)(2,1)S(1)}, u32[]{:S(2)}, u32[]{:S(2)}) collective-permute-start(bf16[128,384]{1,0:T(8,128)(2,1)S(1)} %collective-permute-done.7.refs_7_), channel_id=1, source_target_pairs={{1,2},{2,1},{5,6},{6,5},{9,10},{10,9},{13,14},{14,13},{17,18},{18,... | collective-permute-start | bytes 294920 | tf_op jit(solution)/shard_map/ppermute | solution.py:189
  27.7 5.4 %collective-permute-start.3 = (bf16[128,384]{1,0:T(8,128)(2,1)S(1)}, bf16[128,384]{1,0:T(8,128)(2,1)S(1)}, u32[]{:S(2)}, u32[]{:S(2)}) collective-permute-start(bf16[128,384]{1,0:T(8,128)(2,1)S(1)} %collective-permute-done.2.refs_2_), channel_id=1, source_target_pairs={{1,0},{2,3},{5,4},{6,7},{9,8},{10,11},{13,12},{14,15},{17,16},{18,... | collective-permute-start | bytes 294920 | tf_op jit(solution)/shard_map/ppermute | solution.py:189
  29.0 4.1 %collective-permute-start.5 = (bf16[128,384]{1,0:T(8,128)(2,1)S(1)}, bf16[128,384]{1,0:T(8,128)(2,1)S(1)}, u32[]{:S(2)}, u32[]{:S(2)}) collective-permute-start(bf16[128,384]{1,0:T(8,128)(2,1)S(1)} %collective-permute-done.4.refs_4_), channel_id=1, source_target_pairs={{1,0},{2,3},{5,4},{6,7},{9,8},{10,11},{13,12},{14,15},{17,16},{18,... | collective-permute-start | bytes 294920 | tf_op jit(solution)/shard_map/ppermute | solution.py:189
  30.4 3.5 %collective-permute-start.9 = (bf16[128,384]{1,0:T(8,128)(2,1)S(1)}, bf16[128,384]{1,0:T(8,128)(2,1)S(1)}, u32[]{:S(2)}, u32[]{:S(2)}) collective-permute-start(bf16[128,384]{1,0:T(8,128)(2,1)S(1)} %collective-permute-done.8.refs_8_), channel_id=1, source_target_pairs={{1,0},{2,3},{5,4},{6,7},{9,8},{10,11},{13,12},{14,15},{17,16},{18,... | collective-permute-start | bytes 294920 | tf_op jit(solution)/shard_map/ppermute | solution.py:189
  31.7 4.3 %collective-permute-start.11 = (bf16[128,384]{1,0:T(8,128)(2,1)S(1)}, bf16[128,384]{1,0:T(8,128)(2,1)S(1)}, u32[]{:S(2)}, u32[]{:S(2)}) collective-permute-start(bf16[128,384]{1,0:T(8,128)(2,1)S(1)} %collective-permute-done.10.refs_10_), channel_id=1, source_target_pairs={{1,0},{2,3},{5,4},{6,7},{9,8},{10,11},{13,12},{14,15},{17,16},{18,... | collective-permute-start | bytes 294920 | tf_op jit(solution)/shard_map/ppermute | solution.py:189
  37.3 10.9 %collective-permute-start.12 = (f32[512,384]{1,0:T(8,128)S(1)}, f32[512,384]{1,0:T(8,128)S(1)}, u32[]{:S(2)}, u32[]{:S(2)}) collective-permute-start(f32[512,384]{1,0:T(8,128)S(1)} %get-tuple-element.14.mine), channel_id=1, source_target_pairs={{4,0},{1,5},{6,2},{3,7},{12,8},{9,13},{14,10},{11,15},{20,16},{17,... | collective-permute-start | bytes 2359304 | tf_op jit(solution)/shard_map/ppermute | solution.py:186
  42.2 2.8 %collective-permute-start.13 = (bf16[24,384]{1,0:T(8,128)(2,1)S(1)}, bf16[24,384]{1,0:T(8,128)(2,1)S(1)}, u32[]{:S(2)}, u32[]{:S(2)}) collective-permute-start(bf16[24,384]{1,0:T(8,128)(2,1)S(1)} %get-tuple-element.33), channel_id=1, source_target_pairs={{0,8},{4,12},{8,0},{12,4},{1,9},{5,13},{9,1},{13,5},{2,10},{6,14},... | collective-permute-start | bytes 55304 | tf_op jit(solution)/shard_map/ppermute | solution.py:233
  45.0 3.1 %collective-permute-start.14 = (bf16[48,384]{1,0:T(8,128)(2,1)S(1)}, bf16[48,384]{1,0:T(8,128)(2,1)S(1)}, u32[]{:S(2)}, u32[]{:S(2)}) collective-permute-start(bf16[48,384]{1,0:T(8,128)(2,1)S(1)} %pad_maximum_fusion.inverse_a), channel_id=1, source_target_pairs={{4,0},{1,5},{6,2},{3,7},{12,8},{9,13},{14,10},{11,15},{20,16},{17,... | collective-permute-start | bytes 110600 | tf_op jit(solution)/shard_map/ppermute | solution.py:186
  50.8 2.0 %collective-permute-start.24 = (f32[96,128]{1,0:T(8,128)S(1)}, f32[96,128]{1,0:T(8,128)S(1)}, u32[]{:S(2)}, u32[]{:S(2)}) collective-permute-start(f32[96,128]{1,0:T(8,128)S(1)} %get-tuple-element.23), channel_id=1, source_target_pairs={{0,5},{5,0},{2,7},{7,2},{8,13},{13,8},{10,15},{15,10},{16,21},{21,... | collective-permute-start | bytes 147464 | tf_op jit(solution)/shard_map/ppermute | solution.py:186
  52.8 3.4 %collective-permute-start.27 = (f32[96,128]{1,0:T(8,128)S(1)}, f32[96,128]{1,0:T(8,128)S(1)}, u32[]{:S(2)}, u32[]{:S(2)}) collective-permute-start(f32[96,128]{1,0:T(8,128)S(1)} %shard_map.71.refs_0_), channel_id=1, source_target_pairs={{0,5},{5,0},{2,7},{7,2},{8,13},{13,8},{10,15},{15,10},{16,21},{21,... | collective-permute-start | bytes 147464 | tf_op jit(solution)/shard_map/ppermute | solution.py:186
  53.5 4.0 %collective-permute-start.28 = (f32[96,128]{1,0:T(8,128)S(1)}, f32[96,128]{1,0:T(8,128)S(1)}, u32[]{:S(2)}, u32[]{:S(2)}) collective-permute-start(f32[96,128]{1,0:T(8,128)S(1)} %shard_map.71.refs_0_), channel_id=1, source_target_pairs={{0,2},{5,7},{2,0},{7,5},{8,10},{13,15},{10,8},{15,13},{16,18},{21,... | collective-permute-start | bytes 147464 | tf_op jit(solution)/shard_map/ppermute | solution.py:186
  54.2 5.3 %collective-permute-start.22 = (bf16[128,384]{1,0:T(8,128)(2,1)S(1)}, bf16[128,384]{1,0:T(8,128)(2,1)S(1)}, u32[]{:S(2)}, u32[]{:S(2)}) collective-permute-start(bf16[128,384]{1,0:T(8,128)(2,1)S(1)} %get-tuple-element.19), channel_id=1, source_target_pairs={{8,3},{13,4},{10,9},{15,14},{24,19},{29,20},{26,25},{31,30}} | collective-permute-start | bytes 294920 | tf_op jit(solution)/shard_map/ppermute | solution.py:186
  54.8 5.3 %collective-permute-start.21 = (bf16[128,384]{1,0:T(8,128)(2,1)S(1)}, bf16[128,384]{1,0:T(8,128)(2,1)S(1)}, u32[]{:S(2)}, u32[]{:S(2)}) collective-permute-start(bf16[128,384]{1,0:T(8,128)(2,1)S(1)} %get-tuple-element.18), channel_id=1, source_target_pairs={{8,2},{13,7},{10,8},{15,13},{24,18},{29,23},{26,24},{31,29}} | collective-permute-start | bytes 294920 | tf_op jit(solution)/shard_map/ppermute | solution.py:186
  55.5 5.3 %collective-permute-start.19 = (bf16[128,384]{1,0:T(8,128)(2,1)S(1)}, bf16[128,384]{1,0:T(8,128)(2,1)S(1)}, u32[]{:S(2)}, u32[]{:S(2)}) collective-permute-start(bf16[128,384]{1,0:T(8,128)(2,1)S(1)} %get-tuple-element.16), channel_id=1, source_target_pairs={{8,0},{13,5},{10,10},{15,15},{24,16},{29,21},{26,26},{31,31}} | collective-permute-start | bytes 294920 | tf_op jit(solution)/shard_map/ppermute | solution.py:186
  56.2 30.5 %collective-permute-start.20 = (bf16[128,384]{1,0:T(8,128)(2,1)S(1)}, bf16[128,384]{1,0:T(8,128)(2,1)S(1)}, u32[]{:S(2)}, u32[]{:S(2)}) collective-permute-start(bf16[128,384]{1,0:T(8,128)(2,1)S(1)} %get-tuple-element.17), channel_id=1, source_target_pairs={{8,1},{13,6},{10,11},{15,12},{24,17},{29,22},{26,27},{31,28}} | collective-permute-start | bytes 294920 | tf_op jit(solution)/shard_map/ppermute | solution.py:186
  58.2 29.2 %collective-permute-start.18 = (bf16[128,384]{1,0:T(8,128)(2,1)S(1)}, bf16[128,384]{1,0:T(8,128)(2,1)S(1)}, u32[]{:S(2)}, u32[]{:S(2)}) collective-permute-start(bf16[128,384]{1,0:T(8,128)(2,1)S(1)} %get-tuple-element.19), channel_id=1, source_target_pairs={{0,3},{5,4},{2,9},{7,14},{16,19},{21,20},{18,25},{23,30}} | collective-permute-start | bytes 294920 | tf_op jit(solution)/shard_map/ppermute | solution.py:186
  59.5 29.4 %collective-permute-start.17 = (bf16[128,384]{1,0:T(8,128)(2,1)S(1)}, bf16[128,384]{1,0:T(8,128)(2,1)S(1)}, u32[]{:S(2)}, u32[]{:S(2)}) collective-permute-start(bf16[128,384]{1,0:T(8,128)(2,1)S(1)} %get-tuple-element.18), channel_id=1, source_target_pairs={{0,2},{5,7},{2,8},{7,13},{16,18},{21,23},{18,24},{23,29}} | collective-permute-start | bytes 294920 | tf_op jit(solution)/shard_map/ppermute | solution.py:186
  60.1 28.7 %collective-permute-start.15 = (bf16[128,384]{1,0:T(8,128)(2,1)S(1)}, bf16[128,384]{1,0:T(8,128)(2,1)S(1)}, u32[]{:S(2)}, u32[]{:S(2)}) collective-permute-start(bf16[128,384]{1,0:T(8,128)(2,1)S(1)} %get-tuple-element.16), channel_id=1, source_target_pairs={{0,0},{5,5},{2,10},{7,15},{16,16},{21,21},{18,26},{23,31}} | collective-permute-start | bytes 294920 | tf_op jit(solution)/shard_map/ppermute | solution.py:186
  60.8 36.3 %collective-permute-start.16 = (bf16[128,384]{1,0:T(8,128)(2,1)S(1)}, bf16[128,384]{1,0:T(8,128)(2,1)S(1)}, u32[]{:S(2)}, u32[]{:S(2)}) collective-permute-start(bf16[128,384]{1,0:T(8,128)(2,1)S(1)} %get-tuple-element.17), channel_id=1, source_target_pairs={{0,1},{5,6},{2,11},{7,12},{16,17},{21,22},{18,27},{23,28}} | collective-permute-start | bytes 294920 | tf_op jit(solution)/shard_map/ppermute | solution.py:186
  87.5 12.3 %collective-permute-start.31 = (f32[384,128]{1,0:T(8,128)S(1)}, f32[384,128]{1,0:T(8,128)S(1)}, u32[]{:S(2)}, u32[]{:S(2)}) collective-permute-start(f32[384,128]{1,0:T(8,128)S(1)} %shard_map.72.refs_0_), channel_id=1, source_target_pairs={{0,8},{5,13},{2,10},{7,15},{8,0},{13,5},{10,2},{15,7},{16,24},{21,... | collective-permute-start | bytes 589832 | tf_op jit(solution)/shard_map/ppermute | solution.py:186
  88.1 12.9 %collective-permute-start.32 = (f32[384,128]{1,0:T(8,128)S(1)}, f32[384,128]{1,0:T(8,128)S(1)}, u32[]{:S(2)}, u32[]{:S(2)}) collective-permute-start(f32[384,128]{1,0:T(8,128)S(1)} %collective-permute-done.30.refs_1_), channel_id=1, source_target_pairs={{0,8},{5,13},{2,10},{7,15},{8,0},{13,5},{10,2},{15,7},{16,24},{21,... | collective-permute-start | bytes 589832 | tf_op jit(solution)/shard_map/ppermute | solution.py:186
  97.1 13.9 %collective-permute-start.33 = (f32[384,128]{1,0:T(8,128)S(1)}, f32[384,128]{1,0:T(8,128)S(1)}, u32[]{:S(2)}, u32[]{:S(2)}) collective-permute-start(f32[384,128]{1,0:T(8,128)S(1)} %shard_map.72.refs_0_), channel_id=1, source_target_pairs={{0,4},{5,1},{2,6},{7,3},{8,12},{13,9},{10,14},{15,11},{16,20},{21,... | collective-permute-start | bytes 589832 | tf_op jit(solution)/shard_map/ppermute | solution.py:186
  98.4 13.9 %collective-permute-start.34 = (f32[384,128]{1,0:T(8,128)S(1)}, f32[384,128]{1,0:T(8,128)S(1)}, u32[]{:S(2)}, u32[]{:S(2)}) collective-permute-start(f32[384,128]{1,0:T(8,128)S(1)} %collective-permute-done.30.refs_1_), channel_id=1, source_target_pairs={{0,4},{5,1},{2,6},{7,3},{8,12},{13,9},{10,14},{15,11},{16,20},{21,... | collective-permute-start | bytes 589832 | tf_op jit(solution)/shard_map/ppermute | solution.py:186
  99.7 13.9 %collective-permute-start.35 = (f32[384,128]{1,0:T(8,128)S(1)}, f32[384,128]{1,0:T(8,128)S(1)}, u32[]{:S(2)}, u32[]{:S(2)}) collective-permute-start(f32[384,128]{1,0:T(8,128)S(1)} %collective-permute-done.31.refs_2_), channel_id=1, source_target_pairs={{0,4},{5,1},{2,6},{7,3},{8,12},{13,9},{10,14},{15,11},{16,20},{21,... | collective-permute-start | bytes 589832 | tf_op jit(solution)/shard_map/ppermute | solution.py:186
  101.0 15.5 %collective-permute-start.36 = (f32[384,128]{1,0:T(8,128)S(1)}, f32[384,128]{1,0:T(8,128)S(1)}, u32[]{:S(2)}, u32[]{:S(2)}) collective-permute-start(f32[384,128]{1,0:T(8,128)S(1)} %collective-permute-done.32.refs_3_), channel_id=1, source_target_pairs={{0,4},{5,1},{2,6},{7,3},{8,12},{13,9},{10,14},{15,11},{16,20},{21,... | collective-permute-start | bytes 589832 | tf_op jit(solution)/shard_map/ppermute | solution.py:186
  (7 other events, 78.6 us)

commit v2 on v0

v2 whole, which is shorter than its diff:
```python
import functools

import jax
import jax.numpy as jnp
from jax import lax
from jax.experimental import pallas as pl
from jax.experimental.pallas import tpu as pltpu
from jax.sharding import PartitionSpec as P

LANES = 128
VMEM = pl.BlockSpec(memory_space=pltpu.VMEM)
SMEM = pl.BlockSpec(memory_space=pltpu.SMEM)


def call(kernel, outs, specs, *operands, scratch=()):
    many = isinstance(outs, (list, tuple))
    return pl.pallas_call(
        kernel,
        out_shape=outs,
        in_specs=specs,
        out_specs=[VMEM] * len(outs) if many else VMEM,
        scratch_shapes=scratch,
        compiler_params=pltpu.CompilerParams(vmem_limit_bytes=32 * 2**20),
    )(*operands)


def transposed_dot(left, right):
    return lax.dot_general(
        left, right, (((0,), (0,)), ((), ())), preferred_element_type=jnp.float32
    )


def tiles(width):
    count = width // LANES
    return [(a, b) for a in range(count) for b in range(a, count)]


def general(sigma_rows, panel, live_block_rows, inv_diag, quad_weight):
    height, count, width = panel.shape[1:]
    offsets = lax.broadcasted_iota(jnp.int32, (height, count), 0)
    active = offsets < live_block_rows[:, 0][None, :]
    masked = jnp.where(active[:, :, None], panel[0], jnp.zeros_like(panel[0]))
    extent = height * lax.axis_size("prow")
    gathered = lax.all_gather(masked, ("prow", "pcol"), axis=0, tiled=True)
    start = lax.axis_index("pcol") * sigma_rows.shape[2]
    column_panel = lax.dynamic_slice_in_dim(gathered, start, sigma_rows.shape[2], 0)
    applied = lax.psum_scatter(
        jnp.dot(
            sigma_rows[0],
            column_panel.reshape(sigma_rows.shape[2], count * width),
            preferred_element_type=jnp.float32,
        ),
        "pcol",
        scatter_dimension=0,
        tiled=True,
    ).reshape(height, count, width)
    half = applied.astype(jnp.bfloat16)
    sigma_panel = jnp.where(active[:, :, None], -half, jnp.zeros_like(half))[None]
    coupling = jnp.einsum(
        "vwg,vwe->wge",
        masked.astype(jnp.float32),
        applied,
        precision=lax.Precision.HIGHEST,
    )
    diagonal = jnp.einsum(
        "skp,skq->spq", inv_diag[0], inv_diag[0], preferred_element_type=jnp.float32
    )
    marginal = lax.psum(quad_weight[0] * (coupling + diagonal), ("hyp", "prow", "pcol"))
    return sigma_panel, marginal


def apply_kernel(place, own_sigma, far_sigma, rows, applied):
    side = place[0]
    applied[...] = transposed_dot(own_sigma[0], rows[side])
    applied[...] += transposed_dot(far_sigma[0], rows[1 - side])


def couple_kernel(place, weight, mine, other, rows, inverse_a, inverse_b, *refs):
    half_out, keep, send, packed = refs
    core, column = place[1], place[2]
    finishes = column % 2 == core
    width = mine.shape[1]
    firsts = range(width // LANES)

    def store(first, part, at):
        for block in range(part.shape[1] // LANES):
            packed[pl.ds((at + block) * LANES, LANES), :] = (
                weight[0] * part[:, block * LANES : (block + 1) * LANES]
            )

    at = 0
    for first in firsts:
        part = jnp.zeros((LANES, width - first * LANES), jnp.float32)
        for inverse in (inverse_a, inverse_b):
            part += transposed_dot(
                inverse[:, first * LANES : (first + 1) * LANES], inverse[:, first * LANES :]
            )
        store(first, part, at)
        at += width // LANES - first

    @pl.when(finishes)
    def _():
        applied = mine[...] + other[...]
        high = applied.astype(jnp.bfloat16)
        low = (applied - high.astype(jnp.float32)).astype(jnp.bfloat16)
        half_out[...] = (-high).reshape(half_out.shape)
        panel = rows[column // 2]
        at = 0
        for first in firsts:
            left = panel[:, first * LANES : (first + 1) * LANES]
            part = transposed_dot(left, high[:, first * LANES :])
            part += transposed_dot(left, low[:, first * LANES :])
            for block in range(part.shape[1] // LANES):
                packed[pl.ds((at + block) * LANES, LANES), :] += (
                    weight[0] * part[:, block * LANES : (block + 1) * LANES]
                )
            at += width // LANES - first

    @pl.when(jnp.logical_not(finishes))
    def _():
        half_out[...] = jnp.zeros_like(half_out)

    half = packed.shape[0] // 2
    keep[...] = packed[pl.ds(pl.multiple_of(core * half, LANES), half), :]
    send[...] = packed[pl.ds(pl.multiple_of((1 - core) * half, LANES), half), :]


def add_kernel(a, b, out):
    out[...] = (a[...] + b[...]).reshape(out.shape)


def total_kernel(parts, out):
    total = jnp.sum(parts[...], axis=0)
    for copy in range(out.shape[0]):
        out[copy] = total


def spread_kernel(place, own, across, own_other, across_other, out):
    width = out.shape[1]
    blocks = tiles(width)
    per = len(blocks) // 2
    for core in range(2):
        for refs, same_core in (((own, across), True), ((own_other, across_other), False)):

            @pl.when((place[1] == core) == same_core)
            def _():
                for ref, node in zip(refs, (place[0], 1 - place[0])):
                    for index in range(per):
                        a, b = blocks[core * per + index]
                        tile = ref[index * LANES : (index + 1) * LANES, :]
                        out[node, a * LANES : (a + 1) * LANES, b * LANES : (b + 1) * LANES] = tile
                        if a != b:
                            out[node, b * LANES : (b + 1) * LANES, a * LANES : (a + 1) * LANES] = tile.T


def square(sigma_rows, panel, live_block_rows, inv_diag, quad_weight):
    height, count, width = panel.shape[1:]
    grid = lax.axis_size("pcol")
    points = lax.axis_size("hyp")
    cores = lax.axis_size("core")
    side, core, column = (lax.axis_index(name) for name in ("side", "core", "pcol"))
    f32, bf16 = jnp.float32, jnp.bfloat16
    shape = jax.ShapeDtypeStruct
    place = jnp.stack([side, core, column]).astype(jnp.int32)
    swap = [(0, 1), (1, 0)]
    pick = functools.partial(lax.dynamic_index_in_dim, axis=0, keepdims=False)

    far_sigma = lax.ppermute(sigma_rows, "side", swap)

    offsets = lax.broadcasted_iota(jnp.int32, (height, count), 0)
    active = offsets < live_block_rows[:, 0][None, :]
    masked = jnp.where(active[:, :, None], panel[0], jnp.zeros_like(panel[0]))
    masked = jnp.transpose(masked, (1, 0, 2))
    copies = jnp.broadcast_to(masked[:, None], (count, grid, height, width))
    rows = lax.all_to_all(
        copies.reshape(count * grid, height, width), ("side", "pcol"), 0, 0, tiled=True
    ).reshape(count, grid * height, width)
    own_inverse = pick(inv_diag[0], side)
    got_inverse = lax.ppermute(pick(inv_diag[0], 1 - side), "side", swap)

    extent = sigma_rows.shape[2]
    applied = call(
        apply_kernel,
        shape((extent, width), f32),
        [SMEM] + [VMEM] * 3,
        place,
        sigma_rows,
        far_sigma,
        rows,
    )
    to_lead = [((1 - c % cores) * grid + c, c % cores * grid + c) for c in range(grid)]
    other = lax.ppermute(applied, ("core", "pcol"), to_lead)

    packed = len(tiles(width)) * LANES
    half, keep, send = call(
        couple_kernel,
        [shape((grid, height, width), bf16)] + [shape((packed // 2, LANES), f32)] * 2,
        [SMEM, SMEM] + [VMEM] * 5,
        place,
        quad_weight,
        applied,
        other,
        rows,
        own_inverse,
        got_inverse,
        scratch=[pltpu.VMEM((packed, LANES), f32)],
    )
    came = lax.ppermute(send, "core", swap)
    shares = points * grid
    size = packed // 2 // shares
    parts = call(
        add_kernel, shape((shares, size, LANES), f32), [VMEM] * 2, keep, came
    )
    parts = lax.all_to_all(parts, ("hyp", "pcol"), 0, 0, tiled=True)
    total = call(total_kernel, shape((shares, size, LANES), f32), [VMEM], parts)
    own = lax.all_to_all(total, ("hyp", "pcol"), 0, 0, tiled=True)
    own = own.reshape(packed // 2, LANES)
    across = lax.ppermute(own, "side", swap)
    own_other = lax.ppermute(own, "core", swap)
    across_other = lax.ppermute(across, "core", swap)
    marginal = call(
        spread_kernel,
        shape((count, width, width), f32),
        [SMEM] + [VMEM] * 4,
        place,
        own,
        across,
        own_other,
        across_other,
    )

    landed = lax.all_to_all(half, "pcol", 0, 0, tiled=True)
    mine = pick(landed, core + cores * side)
    theirs = lax.ppermute(pick(landed, core + cores * (1 - side)), "side", swap)
    first = jnp.where(side == 0, mine, theirs)
    last = jnp.where(side == 0, theirs, mine)
    sigma_panel = jnp.stack([first, last], 1)
    sigma_panel = jnp.where(active[:, :, None], sigma_panel, jnp.zeros_like(sigma_panel))
    return sigma_panel[None], marginal


def solution(mesh):
    sizes = dict(mesh.shape)
    prow, pcol = ("prow",), ("pcol",)

    def on_device(sigma_rows, panel, live_block_rows, inv_diag, quad_weight):
        body = square if split else general
        return body(sigma_rows, panel, live_block_rows, inv_diag, quad_weight)

    split = sizes["hyp"] == 2 and sizes["pcol"] == 4 and sizes["prow"] == 4
    if split:
        prow = ("side", "core")
        mesh = jax.sharding.Mesh(
            mesh.devices.reshape(sizes["hyp"], 2, 2, sizes["pcol"]),
            ("hyp", "side", "core", "pcol"),
        )
    in_specs = (
        P("hyp", prow, pcol),
        P("hyp", prow + pcol, None, None),
        P(None, prow + pcol),
        P("hyp", None, prow + pcol, None),
        P("hyp"),
    )
    out_specs = (P("hyp", prow + pcol, None, None), P())
    return jax.shard_map(
        on_device, mesh=mesh, in_specs=in_specs, out_specs=out_specs, check_vma=False
    )
```

time: 242 us -> 92 us (0.38)
  waiting for transfers between devices: 213 us -> 47.5 us
  starting transfers between devices: 0.12 us -> 18.3 us
  blocking collectives: 0 us -> 14.1 us
  between operations: 14.5 us -> 1.4 us
  Pallas kernels: 0 us -> 5.99 us
  matrix products: 4.83 us -> 0 us
  local copies, waits for them, and re-layouts: 5.34 us -> 2.04 us
    psum x1 -> x0, waiting for transfers between devices: 131 us -> none  [on_device(): marginal = lax.psum(quad_weight[0] * partial_sum, ('hyp', 'prow', 'pcol'))]
    all_gather x1 -> x0, waiting for transfers between devices: 48.9 us -> none  [on_device(): lax.all_gather(masked_panel, ('prow', 'pcol'), axis=0, tiled=True)]
    reduce_scatter x1 -> x0, waiting for transfers between devices: 33.2 us -> none  [on_device(): lax.psum_scatter(jnp.dot(covariance_block, flattened, preferred_element_t...]
    ppermute x0 -> x8, waiting for transfers between devices: none -> 29.9 us  [the longest x1 19.9 us: square(): far_sigma = lax.ppermute(sigma_rows, 'side', swap)]
    all_to_all x0 -> x3, waiting for transfers between devices: none -> 17.6 us  [the longest x1 9.88 us: square(): landed = lax.all_to_all(half, 'pcol', 0, 0, tiled=True)]
    all_to_all x0 -> x3, starting transfers between devices: none -> 14.1 us  [the longest x1 7.25 us: square(): lax.all_to_all(copies.reshape(count * grid, height, width), ('side', 'pco...]
    all_to_all x0 -> x1, blocking collectives: none -> 14.1 us  [square(): parts = lax.all_to_all(parts, ('hyp', 'pcol'), 0, 0, tiled=True)]
    pallas_call x0 -> x5, Pallas kernels: none -> 5.99 us  [call(): pl.pallas_call(kernel, out_shape=outs, in_specs=specs, out_specs=[VMEM] *...]
  transfers between devices with their start and end apart: 3 -> 11, of which waited for: 3 -> 7; matrix products, arithmetic and copies ran while one was open for 1% -> 1% of each run, Pallas kernels for 0% -> 1%
where the time goes in v2:
time: 92 us; the launch traced here: 91.5 us
  waiting for transfers between devices  47.5 us (52%)
  starting transfers between devices  18.3 us (20%)
  blocking collectives  14.1 us (15%)
  Pallas kernels  5.99 us (7%)
  other arithmetic  2.15 us (2%)
  local copies, waits for them, and re-layouts  2.04 us (2%)
  between operations  1.4 us (2%)
    ppermute x1, waiting for transfers between devices, square(): far_sigma = lax.ppermute(sigma_rows, 'side', swap)  19.9 us
    all_to_all x1, blocking collectives, square(): parts = lax.all_to_all(parts, ('hyp', 'pcol'), 0, 0, tiled=True)  14.1 us
    all_to_all x1, waiting for transfers between devices, square(): landed = lax.all_to_all(half, 'pcol', 0, 0, tiled=True)  9.88 us
    all_to_all x1, waiting for transfers between devices, square(): own = lax.all_to_all(total, ('hyp', 'pcol'), 0, 0, tiled=True)  7.7 us
    all_to_all x1, starting transfers between devices, square(): lax.all_to_all(copies.reshape(count * grid, height, width), ('side', 'pco...  7.25 us
    pallas_call x5, Pallas kernels, call(): pl.pallas_call(kernel, out_shape=outs, in_specs=specs, out_specs=[VMEM] *...  5.99 us
    ppermute x1, waiting for transfers between devices, square(): across = lax.ppermute(own, 'side', swap)  5.38 us
    all_to_all x1, starting transfers between devices, square(): landed = lax.all_to_all(half, 'pcol', 0, 0, tiled=True)  3.46 us
  transfers between devices with their start and end apart: 11, of which 7 were waited for; matrix products, arithmetic and copies ran while one was open for 1% of the time, Pallas kernels for 1%

profile of v2, /device:TPU:0, one launch (start us, length us, event | category | flops | bytes accessed | tf_op | source)
XLA Modules:
  0.0 91.5 jit_solution(1490990401225773264)
XLA Ops:
  0.6 0.7 iota_compare_fusion
  1.4 0.1 copy.9
  1.5 1.2 %fusion = bf16[2,128,384]{2,0,1:T(2,128)(2,1)S(1)} fusion(pred[128,2]{1,0:T(8,128)(4,1)S(1)} %copy.9, bf16[1,128,2,384]{3,2,1,0:T(2,128)(2,1)} %param.6), kind=kLoop, calls=%fused_computation.1 | loop fusion | flops 98304 | bytes 393472 | tf_op jit(solution)/shard_map/transpose | solution.py:173
  2.8 0.0 copy-start
  2.8 1.0 %broadcast_in_dim.24 = bf16[2,4,128,384]{3,2,1,0:T(8,128)(2,1)} broadcast(bf16[2,128,384]{2,1,0:T(8,128)(2,1)S(1)} %copy.10), dimensions={0,2,3} | broadcast | bytes 983040 | tf_op jit(solution)/shard_map/broadcast_in_dim | solution.py:174
  3.7 7.3 %all-to-all-start = ((bf16[8,128,384]{2,1,0:T(8,128)(2,1)}), bf16[8,128,384]{2,1,0:T(8,128)(2,1)S(1)}, u32[]{:S(2)}, u32[]{:S(2)}) async-start(bf16[8,128,384]{2,1,0:T(8,128)(2,1)} %bitcast.6), calls=%async_computation | async-start | bytes 1572864 | tf_op jit(solution)/shard_map/all_to_all | solution.py:175
  11.0 2.0 %collective-permute-start = (bf16[1,512,512]{2,1,0:T(8,128)(2,1)S(1)}, bf16[1,512,512]{2,1,0:T(8,128)(2,1)S(1)}, u32[]{:S(2)}, u32[]{:S(2)}) collective-permute-start(bf16[1,512,512]{2,1,0:T(8,128)(2,1)S(1)} %copy-done), channel_id=1, source_target_pairs={{0,8},{8,0},{1,9},{9,1},{2,10},{10,2},{3,11},{11,3},{4,12},{12,4},... | collective-permute-start | bytes 1572872 | tf_op jit(solution)/shard_map/ppermute | solution.py:168
  13.0 0.1 pad_add_fusion.place
  13.1 19.9 %collective-permute-done.far_sigma = bf16[1,512,512]{2,1,0:T(8,128)(2,1)S(1)} collective-permute-done((bf16[1,512,512]{2,1,0:T(8,128)(2,1)S(1)}, bf16[1,512,512]{2,1,0:T(8,128)(2,1)S(1)}, u32[]{:S(2)}, u32[]{:S(2)}) %collective-permute-start) | collective-permute-done | bytes 524320 | tf_op jit(solution)/shard_map/ppermute | solution.py:168
  33.0 0.0 all-to-all-done
  33.0 1.3 %shard_map.68.mine = f32[512,384]{1,0:T(8,128)S(1)} custom-call(s32[3]{0:T(128)S(1)} %pad_add_fusion.place, bf16[1,512,512]{2,1,0:T(8,128)(2,1)S(1)} %copy-done, bf16[1,512,512]{2,1,0:T(8,128)(2,1)S(1)} %collective-permute-done.far_sigma, bf16[2,512,384]{2,1,0:T(8,128)(2,1)S(1)} %bitcast.28), custom_call_target="tpu_custom_call" | custom-call | tf_op jit(solution)/shard_map/pallas_call | solution.py:17
  34.3 1.3 %collective-permute-start.1 = (f32[512,384]{1,0:T(8,128)S(1)}, f32[512,384]{1,0:T(8,128)S(1)}, u32[]{:S(2)}, u32[]{:S(2)}) collective-permute-start(f32[512,384]{1,0:T(8,128)S(1)} %shard_map.68.mine), channel_id=1, source_target_pairs={{4,0},{1,5},{6,2},{3,7},{12,8},{9,13},{14,10},{11,15},{20,16},{17,... | collective-permute-start | bytes 2359304 | tf_op jit(solution)/shard_map/ppermute | solution.py:192
  35.6 0.4 collective-permute-start.2
  36.7 2.7 %collective-permute-done.2.inverse_b = bf16[24,384]{1,0:T(8,128)(2,1)S(1)} collective-permute-done((bf16[24,384]{1,0:T(8,128)(2,1)S(1)}, bf16[24,384]{1,0:T(8,128)(2,1)S(1)}, u32[]{:S(2)}, u32[]{:S(2)}) %collective-permute-start.2) | collective-permute-done | bytes 18464 | tf_op jit(solution)/shard_map/ppermute | solution.py:179
  39.4 0.0 collective-permute-done.1.other
  39.4 2.2 %shard_map.69 = (bf16[4,128,384]{2,1,0:T(8,128)(2,1)}, f32[384,128]{1,0:T(8,128)S(1)}, f32[384,128]{1,0:T(8,128)S(1)}) custom-call(s32[3]{0:T(128)S(1)} %pad_add_fusion.place, f32[1]{0:T(128)S(6)} %copy.12.weight, f32[512,384]{1,0:T(8,128)S(1)} %shard_map.68.mine, f32[512,384]{1,0:T(8,128)S(1)} %collective-permute-done.1.other, ...), custom_call_target="tpu_custom_call" | custom-call | tf_op jit(solution)/shard_map/pallas_call | solution.py:17
  41.6 1.4 %collective-permute-done.4.b = f32[384,128]{1,0:T(8,128)S(1)} collective-permute-done((f32[384,128]{1,0:T(8,128)S(1)}, f32[384,128]{1,0:T(8,128)S(1)}, u32[]{:S(2)}, u32[]{:S(2)}) %collective-permute-start.4) | collective-permute-done | bytes 196640 | tf_op jit(solution)/shard_map/ppermute | solution.py:208
  43.1 14.1 %all_to_all.20.parts = f32[8,48,128]{2,1,0:T(8,128)S(1)} all-to-all(f32[8,48,128]{2,1,0:T(8,128)S(1)} %shard_map.70), channel_id=1, replica_groups=mesh['hyp'=2,'side'=2,'core'=2,'pcol'=4] {'hyp','pcol'}, dimensions={0} | all-to-all | bytes 393216 | tf_op jit(solution)/shard_map/all_to_all | solution.py:214
  57.2 3.5 %all-to-all-start.1 = ((bf16[4,128,384]{2,1,0:T(8,128)(2,1)}), bf16[4,128,384]{2,1,0:T(8,128)(2,1)S(1)}, u32[]{:S(2)}, u32[]{:S(2)}) async-start(bf16[4,128,384]{2,1,0:T(8,128)(2,1)} %get-tuple-element.5), calls=%async_computation.1 | async-start | bytes 786432 | tf_op jit(solution)/shard_map/all_to_all | solution.py:232
  60.6 0.7 shard_map.71
  61.3 9.9 %all-to-all-done.1 = bf16[4,128,384]{2,1,0:T(8,128)(2,1)S(1)} async-done(((bf16[4,128,384]{2,1,0:T(8,128)(2,1)}), bf16[4,128,384]{2,1,0:T(8,128)(2,1)S(1)}, u32[]{:S(2)}, u32[]{:S(2)}) %all-to-all-start.1) | async-done | bytes 393248 | tf_op jit(solution)/shard_map/all_to_all | solution.py:232
  71.2 3.4 %all-to-all-start.3 = ((f32[8,48,128]{2,1,0:T(8,128)}), f32[8,48,128]{2,1,0:T(8,128)S(1)}, u32[]{:S(2)}, u32[]{:S(2)}) async-start(f32[8,48,128]{2,1,0:T(8,128)} %shard_map.71), calls=%async_computation.3 | async-start | bytes 393216 | tf_op jit(solution)/shard_map/all_to_all | solution.py:216
  74.7 0.2 collective-permute-start.3
  74.9 7.7 %all-to-all-done.3 = f32[8,48,128]{2,1,0:T(8,128)S(1)} async-done(((f32[8,48,128]{2,1,0:T(8,128)}), f32[8,48,128]{2,1,0:T(8,128)S(1)}, u32[]{:S(2)}, u32[]{:S(2)}) %all-to-all-start.3) | async-done | bytes 196640 | tf_op jit(solution)/shard_map/all_to_all | solution.py:216
  82.6 0.2 collective-permute-start.5
  82.8 0.1 collective-permute-start.6
  82.9 5.4 %collective-permute-done.5.across = f32[384,128]{1,0:T(8,128)S(1)} collective-permute-done((f32[384,128]{1,0:T(8,128)S(1)}, f32[384,128]{1,0:T(8,128)S(1)}, u32[]{:S(2)}, u32[]{:S(2)}) %collective-permute-start.5) | collective-permute-done | bytes 196640 | tf_op jit(solution)/shard_map/ppermute | solution.py:218
  88.3 0.0 collective-permute-start.7
  88.3 0.1 maximum_select_fusion
  88.4 0.9 copy.11
  89.3 0.4 collective-permute-done.7.across_other
  89.7 1.8 %shard_map.72 = f32[2,384,384]{2,1,0:T(8,128)} custom-call(s32[3]{0:T(128)S(1)} %pad_add_fusion.place, f32[384,128]{1,0:T(8,128)S(1)} %bitcast.32, f32[384,128]{1,0:T(8,128)S(1)} %collective-permute-done.5.across, f32[384,128]{1,0:T(8,128)S(1)} %collective-permute-done.6.own_other, f32[384,128]{1,0:T(8,128)S(1)} %collective-permute-done.7.across_other), custom_call_target="tpu_custom_call" | custom-call | tf_op jit(solution)/shard_map/pallas_call | solution.py:17
  (11 shorter events, 0.1 us)
Async XLA Ops:
  2.8 8.2 %copy-start = (bf16[1,512,512]{2,1,0:T(8,128)(2,1)S(1)}, bf16[1,512,512]{2,1,0:T(8,128)(2,1)}, u32[]{:S(2)}) copy-start(bf16[1,512,512]{2,1,0:T(8,128)(2,1)} %own_sigma.1) | copy-start | bytes 1572868
  3.7 29.3 %all-to-all-start = ((bf16[8,128,384]{2,1,0:T(8,128)(2,1)}), bf16[8,128,384]{2,1,0:T(8,128)(2,1)S(1)}, u32[]{:S(2)}, u32[]{:S(2)}) async-start(bf16[8,128,384]{2,1,0:T(8,128)(2,1)} %bitcast.6), calls=%async_computation | async-start | bytes 1572864 | tf_op jit(solution)/shard_map/all_to_all | solution.py:175
  11.0 22.0 %collective-permute-start = (bf16[1,512,512]{2,1,0:T(8,128)(2,1)S(1)}, bf16[1,512,512]{2,1,0:T(8,128)(2,1)S(1)}, u32[]{:S(2)}, u32[]{:S(2)}) collective-permute-start(bf16[1,512,512]{2,1,0:T(8,128)(2,1)S(1)} %copy-done), channel_id=1, source_target_pairs={{0,8},{8,0},{1,9},{9,1},{2,10},{10,2},{3,11},{11,3},{4,12},{12,4},... | collective-permute-start | bytes 1572872 | tf_op jit(solution)/shard_map/ppermute | solution.py:168
  33.0 2.6 %copy-start.1 = (bf16[1,2,24,384]{3,2,1,0:T(8,128)(2,1)S(1)}, bf16[1,2,24,384]{3,2,1,0:T(8,128)(2,1)}, u32[]{:S(2)}) copy-start(bf16[1,2,24,384]{3,2,1,0:T(8,128)(2,1)} %param.8) | copy-start | bytes 110596
  34.3 5.2 %collective-permute-start.1 = (f32[512,384]{1,0:T(8,128)S(1)}, f32[512,384]{1,0:T(8,128)S(1)}, u32[]{:S(2)}, u32[]{:S(2)}) collective-permute-start(f32[512,384]{1,0:T(8,128)S(1)} %shard_map.68.mine), channel_id=1, source_target_pairs={{4,0},{1,5},{6,2},{3,7},{12,8},{9,13},{14,10},{11,15},{20,16},{17,... | collective-permute-start | bytes 2359304 | tf_op jit(solution)/shard_map/ppermute | solution.py:192
  35.6 3.8 %collective-permute-start.2 = (bf16[24,384]{1,0:T(8,128)(2,1)S(1)}, bf16[24,384]{1,0:T(8,128)(2,1)S(1)}, u32[]{:S(2)}, u32[]{:S(2)}) collective-permute-start(bf16[24,384]{1,0:T(8,128)(2,1)S(1)} %get-tuple-element.12), channel_id=1, source_target_pairs={{0,8},{8,0},{1,9},{9,1},{2,10},{10,2},{3,11},{11,3},{4,12},{12,4},... | collective-permute-start | bytes 55304 | tf_op jit(solution)/shard_map/ppermute | solution.py:179
  41.6 1.4 %collective-permute-start.4 = (f32[384,128]{1,0:T(8,128)S(1)}, f32[384,128]{1,0:T(8,128)S(1)}, u32[]{:S(2)}, u32[]{:S(2)}) collective-permute-start(f32[384,128]{1,0:T(8,128)S(1)} %get-tuple-element.7), channel_id=1, source_target_pairs={{0,4},{4,0},{1,5},{5,1},{2,6},{6,2},{3,7},{7,3},{8,12},{12,8},{9,1... | collective-permute-start | bytes 589832 | tf_op jit(solution)/shard_map/ppermute | solution.py:208
  57.2 14.0 %all-to-all-start.1 = ((bf16[4,128,384]{2,1,0:T(8,128)(2,1)}), bf16[4,128,384]{2,1,0:T(8,128)(2,1)S(1)}, u32[]{:S(2)}, u32[]{:S(2)}) async-start(bf16[4,128,384]{2,1,0:T(8,128)(2,1)} %get-tuple-element.5), calls=%async_computation.1 | async-start | bytes 786432 | tf_op jit(solution)/shard_map/all_to_all | solution.py:232
  71.2 11.4 %all-to-all-start.3 = ((f32[8,48,128]{2,1,0:T(8,128)}), f32[8,48,128]{2,1,0:T(8,128)S(1)}, u32[]{:S(2)}, u32[]{:S(2)}) async-start(f32[8,48,128]{2,1,0:T(8,128)} %shard_map.71), calls=%async_computation.3 | async-start | bytes 393216 | tf_op jit(solution)/shard_map/all_to_all | solution.py:216
  74.7 8.1 %collective-permute-start.3 = (bf16[128,384]{1,0:T(8,128)(2,1)S(1)}, bf16[128,384]{1,0:T(8,128)(2,1)S(1)}, u32[]{:S(2)}, u32[]{:S(2)}) collective-permute-start(bf16[128,384]{1,0:T(8,128)(2,1)S(1)} %dynamic-slice_bitcast_fusion), channel_id=1, source_target_pairs={{0,8},{8,0},{1,9},{9,1},{2,10},{10,2},{3,11},{11,3},{4,12},{12,4},... | collective-permute-start | bytes 294920 | tf_op jit(solution)/shard_map/ppermute | solution.py:234
  82.6 5.7 %collective-permute-start.5 = (f32[384,128]{1,0:T(8,128)S(1)}, f32[384,128]{1,0:T(8,128)S(1)}, u32[]{:S(2)}, u32[]{:S(2)}) collective-permute-start(f32[384,128]{1,0:T(8,128)S(1)} %bitcast.30), channel_id=1, source_target_pairs={{0,8},{8,0},{1,9},{9,1},{2,10},{10,2},{3,11},{11,3},{4,12},{12,4},... | collective-permute-start | bytes 589832 | tf_op jit(solution)/shard_map/ppermute | solution.py:218
  82.8 6.5 %collective-permute-start.6 = (f32[384,128]{1,0:T(8,128)S(1)}, f32[384,128]{1,0:T(8,128)S(1)}, u32[]{:S(2)}, u32[]{:S(2)}) collective-permute-start(f32[384,128]{1,0:T(8,128)S(1)} %bitcast.31), channel_id=1, source_target_pairs={{0,4},{4,0},{1,5},{5,1},{2,6},{6,2},{3,7},{7,3},{8,12},{12,8},{9,1... | collective-permute-start | bytes 589832 | tf_op jit(solution)/shard_map/ppermute | solution.py:219
  88.3 1.4 %collective-permute-start.7 = (f32[384,128]{1,0:T(8,128)S(1)}, f32[384,128]{1,0:T(8,128)S(1)}, u32[]{:S(2)}, u32[]{:S(2)}) collective-permute-start(f32[384,128]{1,0:T(8,128)S(1)} %collective-permute-done.5.across), channel_id=1, source_target_pairs={{0,4},{4,0},{1,5},{5,1},{2,6},{6,2},{3,7},{7,3},{8,12},{12,8},{9,1... | collective-permute-start | bytes 589832 | tf_op jit(solution)/shard_map/ppermute | solution.py:220

commit v3 on v2

v3 whole, which is shorter than its diff:
```python
import functools

import jax
import jax.numpy as jnp
from jax import lax
from jax.experimental import pallas as pl
from jax.experimental.pallas import tpu as pltpu
from jax.sharding import PartitionSpec as P

LANES = 128
VMEM = pl.BlockSpec(memory_space=pltpu.VMEM)
SMEM = pl.BlockSpec(memory_space=pltpu.SMEM)


def call(kernel, outs, specs, *operands, scratch=()):
    many = isinstance(outs, (list, tuple))
    return pl.pallas_call(
        kernel,
        out_shape=outs,
        in_specs=specs,
        out_specs=[VMEM] * len(outs) if many else VMEM,
        scratch_shapes=scratch,
        compiler_params=pltpu.CompilerParams(vmem_limit_bytes=32 * 2**20),
    )(*operands)


def transposed_dot(left, right):
    return lax.dot_general(
        left, right, (((0,), (0,)), ((), ())), preferred_element_type=jnp.float32
    )


def tiles(width):
    count = width // LANES
    return [(a, b) for a in range(count) for b in range(a, count)]


def general(sigma_rows, panel, live_block_rows, inv_diag, quad_weight):
    height, count, width = panel.shape[1:]
    offsets = lax.broadcasted_iota(jnp.int32, (height, count), 0)
    active = offsets < live_block_rows[:, 0][None, :]
    masked = jnp.where(active[:, :, None], panel[0], jnp.zeros_like(panel[0]))
    extent = height * lax.axis_size("prow")
    gathered = lax.all_gather(masked, ("prow", "pcol"), axis=0, tiled=True)
    start = lax.axis_index("pcol") * sigma_rows.shape[2]
    column_panel = lax.dynamic_slice_in_dim(gathered, start, sigma_rows.shape[2], 0)
    applied = lax.psum_scatter(
        jnp.dot(
            sigma_rows[0],
            column_panel.reshape(sigma_rows.shape[2], count * width),
            preferred_element_type=jnp.float32,
        ),
        "pcol",
        scatter_dimension=0,
        tiled=True,
    ).reshape(height, count, width)
    half = applied.astype(jnp.bfloat16)
    sigma_panel = jnp.where(active[:, :, None], -half, jnp.zeros_like(half))[None]
    coupling = jnp.einsum(
        "vwg,vwe->wge",
        masked.astype(jnp.float32),
        applied,
        precision=lax.Precision.HIGHEST,
    )
    diagonal = jnp.einsum(
        "skp,skq->spq", inv_diag[0], inv_diag[0], preferred_element_type=jnp.float32
    )
    marginal = lax.psum(quad_weight[0] * (coupling + diagonal), ("hyp", "prow", "pcol"))
    return sigma_panel, marginal


def mask_kernel(place, live, panel, inverse, own, give, own_inverse, give_inverse):
    first = place[0] == 0
    row = lax.broadcasted_iota(jnp.int32, own.shape, 0)
    rows = panel[0]
    zero = jnp.zeros(own.shape, own.dtype)
    one, two = (jnp.where(row < live[s, 0], rows[:, s, :], zero) for s in range(2))
    own[...] = jnp.where(first, one, two)
    give[...] = jnp.where(first, two, one)
    own_inverse[...] = inverse[0, place[0]]
    give_inverse[...] = inverse[0, 1 - place[0]]


def scaled_blocks(weight, product, out):
    at = 0
    for first in range(out.shape[0]):
        part = product(first)
        for block in range(part.shape[1] // LANES):
            out[at] = weight * part[:, block * LANES : (block + 1) * LANES]
            at += 1
        if at == out.shape[0]:
            return


def inverse_kernel(weight, own, got, out):
    def product(first):
        lanes = pl.ds(first * LANES, LANES)
        rest = pl.ds(first * LANES, own.shape[1] - first * LANES)
        return transposed_dot(own[:, lanes], own[:, rest]) + transposed_dot(got[:, lanes], got[:, rest])

    scaled_blocks(weight[0], product, out)


def apply_kernel(place, own_sigma, far_sigma, *refs):
    blocks, (keep, send, keep_rows, send_rows, panel) = refs[:8], refs[8:]
    core, column = place[1], place[2]
    height = blocks[0].shape[0]
    for index, block in enumerate(blocks):
        spot = jnp.bitwise_xor(column, index % 4)
        panel[index // 4, pl.ds(pl.multiple_of(spot * height, height), height), :] = block[...]
    half = keep.shape[0]
    family = jnp.where(column // 2 == place[0], 0, 1)
    for out, out_rows, part in ((send, send_rows, 1 - core), (keep, keep_rows, core)):
        spot = pl.ds(pl.multiple_of(part * half, half), half)
        out_rows[...] = panel[family, spot, :]
        total = transposed_dot(own_sigma[0, :, spot], panel[0])
        out[...] = total + transposed_dot(far_sigma[0, :, spot], panel[1])


def couple_kernel(place, weight, mine, other, keep_rows, got_rows, inverse, *refs):
    out_a, out_b, keep, send, packed = refs
    core, column = place[1], place[2]
    applied = mine[...] + other[...]
    high = applied.astype(jnp.bfloat16)
    low = (applied - high.astype(jnp.float32)).astype(jnp.bfloat16)
    rows = jnp.where(column % 2 == core, keep_rows[...], got_rows[...])

    def product(first):
        left = rows[:, first * LANES : (first + 1) * LANES]
        rest = slice(first * LANES, None)
        return transposed_dot(left, high[:, rest]) + transposed_dot(left, low[:, rest])

    scaled_blocks(weight[0], product, packed)
    half = packed.shape[0] // 2
    for out, part in ((send, 1 - core), (keep, core)):
        out[...] = packed[pl.ds(part * half, half)] + inverse[pl.ds(part * half, half)]
    height = out_a.shape[0]
    near = core == column // 2
    for out, steps in ((out_a, (0, 3)), (out_b, (1, 2))):
        spot = jnp.where(near, jnp.bitwise_xor(column, steps[0]), jnp.bitwise_xor(column, steps[1]))
        first = spot % 2 == 0
        out[...] = jnp.where(first, -high[:height], -high[height:])


def share_kernel(place, keep, came, *refs):
    outs, whole = refs[:8], refs[8]
    whole[...] = keep[...].reshape(whole.shape) + came[...].reshape(whole.shape)
    size = outs[0].shape[0]
    for index, out in enumerate(outs):
        spot = jnp.bitwise_xor(place[3], index)
        out[...] = whole[pl.ds(pl.multiple_of(spot * size, 8), size), :]


def sum_kernel(*refs):
    parts, out = refs[:8], refs[8]
    sums = [part[...] for part in parts]
    while len(sums) > 1:
        sums = [left + right for left, right in zip(sums[::2], sums[1::2])]
    out[...] = sums[0]


def join_kernel(place, *refs):
    parts, out = refs[:8], refs[8]
    size = parts[0].shape[0]
    for index, part in enumerate(parts):
        spot = jnp.bitwise_xor(place[3], index)
        out[pl.ds(pl.multiple_of(spot * size, 8), size), :] = part[...]


def spread_kernel(place, own, across, own_other, across_other, out):
    width = out.shape[1]
    blocks = tiles(width)
    per = len(blocks) // 2
    for core in range(2):
        for refs, same_core in (((own, across), True), ((own_other, across_other), False)):

            @pl.when((place[1] == core) == same_core)
            def _():
                for ref, node in zip(refs, (place[0], 1 - place[0])):
                    for index in range(per):
                        a, b = blocks[core * per + index]
                        tile = ref[index * LANES : (index + 1) * LANES, :]
                        out[node, a * LANES : (a + 1) * LANES, b * LANES : (b + 1) * LANES] = tile
                        if a != b:
                            out[node, b * LANES : (b + 1) * LANES, a * LANES : (a + 1) * LANES] = tile.T


def finish_kernel(place, live, a, b, out):
    row = lax.broadcasted_iota(jnp.int32, a.shape, 0)
    for s, block in enumerate((a, b)):
        out[0, :, s, :] = jnp.where(row < live[s, 0], block[...], jnp.zeros(a.shape, a.dtype))


AXES = ("hyp", "side", "core", "pcol")


def square(sigma_rows, panel, live_block_rows, inv_diag, quad_weight):
    height, count, width = panel.shape[1:]
    grid = lax.axis_size("pcol")
    points = lax.axis_size("hyp")
    point, side, core, column = (lax.axis_index(name) for name in AXES)
    f32, bf16 = jnp.float32, jnp.bfloat16
    shape = jax.ShapeDtypeStruct
    place = jnp.stack([side, core, column, point * grid + column]).astype(jnp.int32)
    total = points * 2 * 2 * grid

    def swap(x, point=0, side=0, core=0, column=0):
        mask = ((point * 2 + side) * 2 + core) * grid + column
        return lax.ppermute(x, AXES, [(i, i ^ mask) for i in range(total)])

    block = shape((height, width), bf16)
    rows = shape(inv_diag.shape[2:], bf16)
    far_sigma = swap(sigma_rows, side=1)
    own, give, own_inverse, give_inverse = call(
        mask_kernel, [block, block, rows, rows], [SMEM, SMEM, VMEM, VMEM],
        place, live_block_rows, panel, inv_diag,
    )
    got_inverse = swap(give_inverse, side=1)
    blocks = [own if z == 0 else swap(own, column=z) for z in range(grid)]
    blocks += [swap(give, side=1, column=z) for z in range(grid)]

    upper = len(tiles(width))
    inverse = call(
        inverse_kernel, shape((upper, LANES, LANES), f32), [SMEM, VMEM, VMEM],
        quad_weight, own_inverse, got_inverse,
    )
    extent = sigma_rows.shape[2]
    half = shape((extent // 2, width), f32)
    half_rows = shape((extent // 2, width), bf16)
    mine, send, keep_rows, send_rows = call(
        apply_kernel, [half, half, half_rows, half_rows], [SMEM] + [VMEM] * 10,
        place, sigma_rows, far_sigma, *blocks,
        scratch=[pltpu.VMEM((2, extent, width), bf16)],
    )
    got_rows = swap(send_rows, core=1)
    other = swap(send, core=1)

    few = shape((upper // 2, LANES, LANES), f32)
    out_a, out_b, keep, send = call(
        couple_kernel, [block, block, few, few], [SMEM, SMEM] + [VMEM] * 5,
        place, quad_weight, mine, other, keep_rows, got_rows, inverse,
        scratch=[pltpu.VMEM((upper, LANES, LANES), f32)],
    )
    came = swap(send, core=1)
    shares = points * grid
    lines = upper // 2 * LANES
    piece = shape((lines // shares, LANES), f32)
    pieces = call(
        share_kernel, [piece] * shares, [SMEM, VMEM, VMEM], place, keep, came,
        scratch=[pltpu.VMEM((lines, LANES), f32)],
    )

    def exchange(index, x):
        return x if index == 0 else swap(x, point=index // grid, column=index % grid)

    parts = [exchange(i, x) for i, x in enumerate(pieces)]
    done = call(sum_kernel, piece, [VMEM] * shares, *parts)
    parts = [exchange(i, done) for i in range(shares)]
    own_half = call(join_kernel, shape((lines, LANES), f32), [SMEM] + [VMEM] * shares, place, *parts)
    across = swap(own_half, side=1)
    own_other = swap(own_half, core=1)
    across_other = swap(across, core=1)
    marginal = call(
        spread_kernel, shape((count, width, width), f32), [SMEM] + [VMEM] * 4,
        place, own_half, across, own_other, across_other,
    )

    def output_pairs(steps):
        pairs = []
        for h in range(points):
            for s in range(2):
                for c in range(grid):
                    for core, step in ((c // 2, steps[0]), (1 - c // 2, steps[1])):
                        base = (h * 2 + s) * 2
                        pairs.append(((base + core) * grid + c, (base + c % 2) * grid + (c ^ step)))
        return pairs

    land_a = lax.ppermute(out_a, AXES, output_pairs((0, 3)))
    land_b = lax.ppermute(out_b, AXES, output_pairs((1, 2)))
    from_a = jnp.where(column % 2 == core, column, column ^ 3) // 2
    mine = jnp.where(from_a == side, land_a, land_b)
    theirs = swap(jnp.where(from_a == side, land_b, land_a), side=1)
    first = jnp.where(side == 0, mine, theirs)
    last = jnp.where(side == 0, theirs, mine)
    sigma_panel = call(
        finish_kernel, shape((1, height, count, width), bf16), [SMEM, SMEM, VMEM, VMEM],
        place, live_block_rows, first, last,
    )
    return sigma_panel, marginal


def solution(mesh):
    sizes = dict(mesh.shape)
    prow, pcol = ("prow",), ("pcol",)

    def on_device(sigma_rows, panel, live_block_rows, inv_diag, quad_weight):
        body = square if split else general
        return body(sigma_rows, panel, live_block_rows, inv_diag, quad_weight)

    split = sizes["hyp"] == 2 and sizes["pcol"] == 4 and sizes["prow"] == 4
    if split:
        prow = ("side", "core")
        mesh = jax.sharding.Mesh(
            mesh.devices.reshape(sizes["hyp"], 2, 2, sizes["pcol"]),
            ("hyp", "side", "core", "pcol"),
        )
    in_specs = (
        P("hyp", prow, pcol),
        P("hyp", prow + pcol, None, None),
        P(None, prow + pcol),
        P("hyp", None, prow + pcol, None),
        P("hyp"),
    )
    out_specs = (P("hyp", prow + pcol, None, None), P())
    return jax.shard_map(
        on_device, mesh=mesh, in_specs=in_specs, out_specs=out_specs, check_vma=False
    )
```

time: 92 us -> 81.8 us (0.89)
  starting transfers between devices: 18.3 us -> 41 us
  waiting for transfers between devices: 47.5 us -> 27.4 us
  blocking collectives: 14.1 us -> 0 us
  Pallas kernels: 5.99 us -> 8.2 us
  other arithmetic: 2.15 us -> 0.13 us
  local copies, waits for them, and re-layouts: 2.04 us -> 3.48 us
    ppermute x8 -> x32, starting transfers between devices: 4.24 us -> 41 us  [the longest x30 39.3 us: swap(): return lax.ppermute(x, AXES, [(i, i ^ mask) for i in range(total)])]
    all_to_all x3 -> x0, waiting for transfers between devices: 17.6 us -> none  [the longest x1 9.88 us: square(): landed = lax.all_to_all(half, 'pcol', 0, 0, tiled=True)]
    all_to_all x3 -> x0, starting transfers between devices: 14.1 us -> none  [the longest x1 7.25 us: square(): lax.all_to_all(copies.reshape(count * grid, height, width), ('side', 'pco...]
    all_to_all x1 -> x0, blocking collectives: 14.1 us -> none  [square(): parts = lax.all_to_all(parts, ('hyp', 'pcol'), 0, 0, tiled=True)]
    unnamed x5 -> x7, local copies, waits for them, and re-layouts: 0.89 us -> 3.48 us
    ppermute x8 -> x32, waiting for transfers between devices: 29.9 us -> 27.4 us  [the longest x30 27.3 us: swap(): return lax.ppermute(x, AXES, [(i, i ^ mask) for i in range(total)])]
    pallas_call x5 -> x9, Pallas kernels: 5.99 us -> 8.2 us  [call(): pl.pallas_call(kernel, out_shape=outs, in_specs=specs, out_specs=[VMEM] *...]
    transpose x1 -> x0, other arithmetic: 1.22 us -> none  [square(): masked = jnp.transpose(masked, (1, 0, 2))]
  transfers between devices with their start and end apart: 11 -> 32, of which waited for: 7 -> 12; matrix products, arithmetic and copies ran while one was open for 1% -> 1% of each run, Pallas kernels for 1% -> 4%
where the time goes in v3:
time: 81.8 us; the launch traced here: 81.5 us
  starting transfers between devices  41 us (50%)
  waiting for transfers between devices  27.4 us (33%)
  Pallas kernels  8.2 us (10%)
  local copies, waits for them, and re-layouts  3.48 us (4%)
  between operations  1.42 us (2%)
    ppermute x30, starting transfers between devices, swap(): return lax.ppermute(x, AXES, [(i, i ^ mask) for i in range(total)])  39.3 us
    ppermute x30, waiting for transfers between devices, swap(): return lax.ppermute(x, AXES, [(i, i ^ mask) for i in range(total)])  27.3 us
    pallas_call x9, Pallas kernels, call(): pl.pallas_call(kernel, out_shape=outs, in_specs=specs, out_specs=[VMEM] *...  8.2 us
    unnamed x7, local copies, waits for them, and re-layouts  3.48 us
  transfers between devices with their start and end apart: 32, of which 12 were waited for; matrix products, arithmetic and copies ran while one was open for 1% of the time, Pallas kernels for 4%

profile of v3, /device:TPU:0, one launch (start us, length us, event | category | flops | bytes accessed | tf_op | source)
XLA Modules:
  0.0 81.5 jit_solution(14079295881203158162)
XLA Ops:
  0.6 3.0 %collective-permute-start = (bf16[1,512,512]{2,1,0:T(8,128)(2,1)}, bf16[1,512,512]{2,1,0:T(8,128)(2,1)S(1)}, u32[]{:S(2)}, u32[]{:S(2)}) collective-permute-start(bf16[1,512,512]{2,1,0:T(8,128)(2,1)} %own_sigma.1), channel_id=1, source_target_pairs={{0,8},{1,9},{2,10},{3,11},{4,12},{5,13},{6,14},{7,15},{8,0},{9,1},... | collective-permute-start | bytes 1572872 | tf_op jit(solution)/shard_map/ppermute | solution.py:209
  6.1 1.1 %shard_map.68 = (bf16[128,384]{1,0:T(8,128)(2,1)S(1)}, bf16[128,384]{1,0:T(8,128)(2,1)S(1)}, bf16[24,384]{1,0:T(8,128)(2,1)S(1)}, bf16[24,384]{1,0:T(8,128)(2,1)S(1)}) custom-call(s32[4]{0:T(128)S(1)} %pad_add_fusion.place, s32[2,1]{1,0:T(2,128)S(1)} %copy.8.live, bf16[1,128,2,384]{3,2,1,0:T(2,128)(2,1)S(1)} %copy-done.1, bf16[1,2,24,384]{3,2,1,0:T(8,128)(2,1)S(1)} %copy-done.2), custom_call_target="tpu_custom_call" | custom-call | tf_op jit(solution)/shard_map/pallas_call | solution.py:17
  7.2 1.6 %collective-permute-start.1 = (bf16[128,384]{1,0:T(8,128)(2,1)S(1)}, bf16[128,384]{1,0:T(8,128)(2,1)S(1)}, u32[]{:S(2)}, u32[]{:S(2)}) collective-permute-start(bf16[128,384]{1,0:T(8,128)(2,1)S(1)} %get-tuple-element.22.refs_0_), channel_id=1, source_target_pairs={{0,1},{1,0},{2,3},{3,2},{4,5},{5,4},{6,7},{7,6},{8,9},{9,8},{10,11... | collective-permute-start | bytes 294920 | tf_op jit(solution)/shard_map/ppermute | solution.py:209
  8.9 2.6 %collective-permute-start.2 = (bf16[128,384]{1,0:T(8,128)(2,1)S(1)}, bf16[128,384]{1,0:T(8,128)(2,1)S(1)}, u32[]{:S(2)}, u32[]{:S(2)}) collective-permute-start(bf16[128,384]{1,0:T(8,128)(2,1)S(1)} %get-tuple-element.22.refs_0_), channel_id=1, source_target_pairs={{0,2},{1,3},{2,0},{3,1},{4,6},{5,7},{6,4},{7,5},{8,10},{9,11},{10,... | collective-permute-start | bytes 294920 | tf_op jit(solution)/shard_map/ppermute | solution.py:209
  13.8 5.7 %collective-permute-done.2.refs_2_ = bf16[128,384]{1,0:T(8,128)(2,1)S(1)} collective-permute-done((bf16[128,384]{1,0:T(8,128)(2,1)S(1)}, bf16[128,384]{1,0:T(8,128)(2,1)S(1)}, u32[]{:S(2)}, u32[]{:S(2)}) %collective-permute-start.2) | collective-permute-done | bytes 98336 | tf_op jit(solution)/shard_map/ppermute | solution.py:209
  19.5 3.8 %collective-permute-start.7 = (bf16[128,384]{1,0:T(8,128)(2,1)S(1)}, bf16[128,384]{1,0:T(8,128)(2,1)S(1)}, u32[]{:S(2)}, u32[]{:S(2)}) collective-permute-start(bf16[128,384]{1,0:T(8,128)(2,1)S(1)} %get-tuple-element.23), channel_id=1, source_target_pairs={{0,11},{1,10},{2,9},{3,8},{4,15},{5,14},{6,13},{7,12},{8,3},{9,2},... | collective-permute-start | bytes 294920 | tf_op jit(solution)/shard_map/ppermute | solution.py:209
  23.3 4.7 %collective-permute-done.6.refs_6_ = bf16[128,384]{1,0:T(8,128)(2,1)S(1)} collective-permute-done((bf16[128,384]{1,0:T(8,128)(2,1)S(1)}, bf16[128,384]{1,0:T(8,128)(2,1)S(1)}, u32[]{:S(2)}, u32[]{:S(2)}) %collective-permute-start.6) | collective-permute-done | bytes 98336 | tf_op jit(solution)/shard_map/ppermute | solution.py:209
  28.0 1.0 %copy-done = bf16[1,512,512]{2,1,0:T(8,128)(2,1)S(1)} copy-done((bf16[1,512,512]{2,1,0:T(8,128)(2,1)S(1)}, bf16[1,512,512]{2,1,0:T(8,128)(2,1)}, u32[]{:S(2)}) %copy-start) | copy-done | bytes 524312
  29.0 1.4 %shard_map.69 = (f32[256,384]{1,0:T(8,128)S(1)}, f32[256,384]{1,0:T(8,128)S(1)}, bf16[256,384]{1,0:T(8,128)(2,1)S(1)}, bf16[256,384]{1,0:T(8,128)(2,1)S(1)}) custom-call(s32[4]{0:T(128)S(1)} %pad_add_fusion.place, bf16[1,512,512]{2,1,0:T(8,128)(2,1)S(1)} %copy-done, bf16[1,512,512]{2,1,0:T(8,128)(2,1)S(1)} %collective-permute-done.far_sigma, ...), custom_call_target="tpu_custom_call" | custom-call | tf_op jit(solution)/shard_map/pallas_call | solution.py:17
  32.6 2.2 %collective-permute-done.10.got = bf16[24,384]{1,0:T(8,128)(2,1)S(1)} collective-permute-done((bf16[24,384]{1,0:T(8,128)(2,1)S(1)}, bf16[24,384]{1,0:T(8,128)(2,1)S(1)}, u32[]{:S(2)}, u32[]{:S(2)}) %collective-permute-start.10) | collective-permute-done | bytes 18464 | tf_op jit(solution)/shard_map/ppermute | solution.py:209
  36.2 1.4 %collective-permute-done.14.came = f32[3,128,128]{2,1,0:T(8,128)S(1)} collective-permute-done((f32[3,128,128]{2,1,0:T(8,128)S(1)}, f32[3,128,128]{2,1,0:T(8,128)S(1)}, u32[]{:S(2)}, u32[]{:S(2)}) %collective-permute-start.14) | collective-permute-done | bytes 196640 | tf_op jit(solution)/shard_map/ppermute | solution.py:209
  38.2 1.7 %collective-permute-start.15 = (f32[48,128]{1,0:T(8,128)S(1)}, f32[48,128]{1,0:T(8,128)S(1)}, u32[]{:S(2)}, u32[]{:S(2)}) collective-permute-start(f32[48,128]{1,0:T(8,128)S(1)} %get-tuple-element.35), channel_id=1, source_target_pairs={{0,1},{1,0},{2,3},{3,2},{4,5},{5,4},{6,7},{7,6},{8,9},{9,8},{10,11... | collective-permute-start | bytes 73736 | tf_op jit(solution)/shard_map/ppermute | solution.py:209
  39.9 2.2 %collective-permute-start.16 = (f32[48,128]{1,0:T(8,128)S(1)}, f32[48,128]{1,0:T(8,128)S(1)}, u32[]{:S(2)}, u32[]{:S(2)}) collective-permute-start(f32[48,128]{1,0:T(8,128)S(1)} %get-tuple-element.36), channel_id=1, source_target_pairs={{0,2},{1,3},{2,0},{3,1},{4,6},{5,7},{6,4},{7,5},{8,10},{9,11},{10,... | collective-permute-start | bytes 73736 | tf_op jit(solution)/shard_map/ppermute | solution.py:209
  42.1 1.2 %collective-permute-start.17 = (f32[48,128]{1,0:T(8,128)S(1)}, f32[48,128]{1,0:T(8,128)S(1)}, u32[]{:S(2)}, u32[]{:S(2)}) collective-permute-start(f32[48,128]{1,0:T(8,128)S(1)} %get-tuple-element.37), channel_id=1, source_target_pairs={{0,3},{1,2},{2,1},{3,0},{4,7},{5,6},{6,5},{7,4},{8,11},{9,10},{10,... | collective-permute-start | bytes 73736 | tf_op jit(solution)/shard_map/ppermute | solution.py:209
  43.3 1.5 %collective-permute-start.18 = (f32[48,128]{1,0:T(8,128)S(1)}, f32[48,128]{1,0:T(8,128)S(1)}, u32[]{:S(2)}, u32[]{:S(2)}) collective-permute-start(f32[48,128]{1,0:T(8,128)S(1)} %get-tuple-element.38), channel_id=1, source_target_pairs={{0,16},{1,17},{2,18},{3,19},{4,20},{5,21},{6,22},{7,23},{8,24},{9,... | collective-permute-start | bytes 73736 | tf_op jit(solution)/shard_map/ppermute | solution.py:209
  45.3 3.6 %collective-permute-start.20 = (f32[48,128]{1,0:T(8,128)S(1)}, f32[48,128]{1,0:T(8,128)S(1)}, u32[]{:S(2)}, u32[]{:S(2)}) collective-permute-start(f32[48,128]{1,0:T(8,128)S(1)} %get-tuple-element.40), channel_id=1, source_target_pairs={{0,18},{1,19},{2,16},{3,17},{4,22},{5,23},{6,20},{7,21},{8,26},{9,... | collective-permute-start | bytes 73736 | tf_op jit(solution)/shard_map/ppermute | solution.py:209
  48.9 1.1 %collective-permute-start.21 = (f32[48,128]{1,0:T(8,128)S(1)}, f32[48,128]{1,0:T(8,128)S(1)}, u32[]{:S(2)}, u32[]{:S(2)}) collective-permute-start(f32[48,128]{1,0:T(8,128)S(1)} %get-tuple-element.41), channel_id=1, source_target_pairs={{0,19},{1,18},{2,17},{3,16},{4,23},{5,22},{6,21},{7,20},{8,27},{9,... | collective-permute-start | bytes 73736 | tf_op jit(solution)/shard_map/ppermute | solution.py:209
  50.7 1.0 %collective-permute-start.12 = (bf16[128,384]{1,0:T(8,128)(2,1)S(1)}, bf16[128,384]{1,0:T(8,128)(2,1)S(1)}, u32[]{:S(2)}, u32[]{:S(2)}) collective-permute-start(bf16[128,384]{1,0:T(8,128)(2,1)S(1)} %get-tuple-element.31), channel_id=1, source_target_pairs={{0,1},{4,2},{1,4},{5,7},{6,3},{2,0},{7,6},{3,5},{8,9},{12,10},{9,1... | collective-permute-start | bytes 294920 | tf_op jit(solution)/shard_map/ppermute | solution.py:279
  51.8 3.6 %collective-permute-done.21.refs_7_ = f32[48,128]{1,0:T(8,128)S(1)} collective-permute-done((f32[48,128]{1,0:T(8,128)S(1)}, f32[48,128]{1,0:T(8,128)S(1)}, u32[]{:S(2)}, u32[]{:S(2)}) %collective-permute-start.21) | collective-permute-done | bytes 24608 | tf_op jit(solution)/shard_map/ppermute | solution.py:209
  55.5 1.0 %collective-permute-start.22 = (f32[48,128]{1,0:T(8,128)S(1)}, f32[48,128]{1,0:T(8,128)S(1)}, u32[]{:S(2)}, u32[]{:S(2)}) collective-permute-start(f32[48,128]{1,0:T(8,128)S(1)} %shard_map.74.refs_0_), channel_id=1, source_target_pairs={{0,1},{1,0},{2,3},{3,2},{4,5},{5,4},{6,7},{7,6},{8,9},{9,8},{10,11... | collective-permute-start | bytes 73736 | tf_op jit(solution)/shard_map/ppermute | solution.py:209
  57.4 2.5 %collective-permute-start.24 = (f32[48,128]{1,0:T(8,128)S(1)}, f32[48,128]{1,0:T(8,128)S(1)}, u32[]{:S(2)}, u32[]{:S(2)}) collective-permute-start(f32[48,128]{1,0:T(8,128)S(1)} %shard_map.74.refs_0_), channel_id=1, source_target_pairs={{0,3},{1,2},{2,1},{3,0},{4,7},{5,6},{6,5},{7,4},{8,11},{9,10},{10,... | collective-permute-start | bytes 73736 | tf_op jit(solution)/shard_map/ppermute | solution.py:209
  59.9 1.3 %collective-permute-start.25 = (f32[48,128]{1,0:T(8,128)S(1)}, f32[48,128]{1,0:T(8,128)S(1)}, u32[]{:S(2)}, u32[]{:S(2)}) collective-permute-start(f32[48,128]{1,0:T(8,128)S(1)} %shard_map.74.refs_0_), channel_id=1, source_target_pairs={{0,16},{1,17},{2,18},{3,19},{4,20},{5,21},{6,22},{7,23},{8,24},{9,... | collective-permute-start | bytes 73736 | tf_op jit(solution)/shard_map/ppermute | solution.py:209
  61.2 1.0 %collective-permute-start.26 = (f32[48,128]{1,0:T(8,128)S(1)}, f32[48,128]{1,0:T(8,128)S(1)}, u32[]{:S(2)}, u32[]{:S(2)}) collective-permute-start(f32[48,128]{1,0:T(8,128)S(1)} %shard_map.74.refs_0_), channel_id=1, source_target_pairs={{0,17},{1,16},{2,19},{3,18},{4,21},{5,20},{6,23},{7,22},{8,25},{9,... | collective-permute-start | bytes 73736 | tf_op jit(solution)/shard_map/ppermute | solution.py:209
  63.0 1.2 %collective-permute-start.27 = (f32[48,128]{1,0:T(8,128)S(1)}, f32[48,128]{1,0:T(8,128)S(1)}, u32[]{:S(2)}, u32[]{:S(2)}) collective-permute-start(f32[48,128]{1,0:T(8,128)S(1)} %shard_map.74.refs_0_), channel_id=1, source_target_pairs={{0,18},{1,19},{2,16},{3,17},{4,22},{5,23},{6,20},{7,21},{8,26},{9,... | collective-permute-start | bytes 73736 | tf_op jit(solution)/shard_map/ppermute | solution.py:209
  64.2 3.3 %collective-permute-start.28 = (f32[48,128]{1,0:T(8,128)S(1)}, f32[48,128]{1,0:T(8,128)S(1)}, u32[]{:S(2)}, u32[]{:S(2)}) collective-permute-start(f32[48,128]{1,0:T(8,128)S(1)} %shard_map.74.refs_0_), channel_id=1, source_target_pairs={{0,19},{1,18},{2,17},{3,16},{4,23},{5,22},{6,21},{7,20},{8,27},{9,... | collective-permute-start | bytes 73736 | tf_op jit(solution)/shard_map/ppermute | solution.py:209
  67.5 1.4 %collective-permute-done.27.refs_6_ = f32[48,128]{1,0:T(8,128)S(1)} collective-permute-done((f32[48,128]{1,0:T(8,128)S(1)}, f32[48,128]{1,0:T(8,128)S(1)}, u32[]{:S(2)}, u32[]{:S(2)}) %collective-permute-start.27) | collective-permute-done | bytes 24608 | tf_op jit(solution)/shard_map/ppermute | solution.py:209
  68.9 1.8 %collective-permute-done.28.refs_7_ = f32[48,128]{1,0:T(8,128)S(1)} collective-permute-done((f32[48,128]{1,0:T(8,128)S(1)}, f32[48,128]{1,0:T(8,128)S(1)}, u32[]{:S(2)}, u32[]{:S(2)}) %collective-permute-start.28) | collective-permute-done | bytes 24608 | tf_op jit(solution)/shard_map/ppermute | solution.py:209
  72.1 1.3 %collective-permute-start.13 = (bf16[128,384]{1,0:T(8,128)(2,1)S(1)}, bf16[128,384]{1,0:T(8,128)(2,1)S(1)}, u32[]{:S(2)}, u32[]{:S(2)}) collective-permute-start(bf16[128,384]{1,0:T(8,128)(2,1)S(1)} %broadcast_select_fusion), channel_id=1, source_target_pairs={{0,8},{1,9},{2,10},{3,11},{4,12},{5,13},{6,14},{7,15},{8,0},{9,1},... | collective-permute-start | bytes 294920 | tf_op jit(solution)/shard_map/ppermute | solution.py:209
  73.5 3.7 %collective-permute-done.29.across = f32[384,128]{1,0:T(8,128)S(1)} collective-permute-done((f32[384,128]{1,0:T(8,128)S(1)}, f32[384,128]{1,0:T(8,128)S(1)}, u32[]{:S(2)}, u32[]{:S(2)}) %collective-permute-start.29) | collective-permute-done | bytes 196640 | tf_op jit(solution)/shard_map/ppermute | solution.py:209
  77.1 1.0 %collective-permute-done.13 = bf16[128,384]{1,0:T(8,128)(2,1)S(1)} collective-permute-done((bf16[128,384]{1,0:T(8,128)(2,1)S(1)}, bf16[128,384]{1,0:T(8,128)(2,1)S(1)}, u32[]{:S(2)}, u32[]{:S(2)}) %collective-permute-start.13) | collective-permute-done | bytes 98336 | tf_op jit(solution)/shard_map/ppermute | solution.py:209
  78.2 1.5 %shard_map.72 = bf16[1,128,2,384]{3,2,1,0:T(2,128)(2,1)} custom-call(s32[4]{0:T(128)S(1)} %pad_add_fusion.place, s32[2,1]{1,0:T(2,128)S(1)} %copy.8.live, bf16[128,384]{1,0:T(8,128)(2,1)S(1)} %get-tuple-element.43.a, bf16[128,384]{1,0:T(8,128)(2,1)S(1)} %get-tuple-element.42.b), custom_call_target="tpu_custom_call" | custom-call | tf_op jit(solution)/shard_map/pallas_call | solution.py:17
  79.7 1.8 %shard_map.76 = f32[2,384,384]{2,1,0:T(8,128)} custom-call(s32[4]{0:T(128)S(1)} %pad_add_fusion.place, f32[384,128]{1,0:T(8,128)S(1)} %shard_map.75.own, f32[384,128]{1,0:T(8,128)S(1)} %collective-permute-done.29.across, f32[384,128]{1,0:T(8,128)S(1)} %collective-permute-done.30.own_other, f32[384,128]{1,0:T(8,128)S(1)} %collective-permute-done.31.across_other), custom_call_target="tpu_custom_call" | custom-call | tf_op jit(solution)/shard_map/pallas_call | solution.py:17
  (51 shorter events, 12.7 us)
Async XLA Ops:
  0.6 27.4 %collective-permute-start = (bf16[1,512,512]{2,1,0:T(8,128)(2,1)}, bf16[1,512,512]{2,1,0:T(8,128)(2,1)S(1)}, u32[]{:S(2)}, u32[]{:S(2)}) collective-permute-start(bf16[1,512,512]{2,1,0:T(8,128)(2,1)} %own_sigma.1), channel_id=1, source_target_pairs={{0,8},{1,9},{2,10},{3,11},{4,12},{5,13},{6,14},{7,15},{8,0},{9,1},... | collective-permute-start | bytes 1572872 | tf_op jit(solution)/shard_map/ppermute | solution.py:209
  7.2 5.7 %collective-permute-start.1 = (bf16[128,384]{1,0:T(8,128)(2,1)S(1)}, bf16[128,384]{1,0:T(8,128)(2,1)S(1)}, u32[]{:S(2)}, u32[]{:S(2)}) collective-permute-start(bf16[128,384]{1,0:T(8,128)(2,1)S(1)} %get-tuple-element.22.refs_0_), channel_id=1, source_target_pairs={{0,1},{1,0},{2,3},{3,2},{4,5},{5,4},{6,7},{7,6},{8,9},{9,8},{10,11... | collective-permute-start | bytes 294920 | tf_op jit(solution)/shard_map/ppermute | solution.py:209
  8.9 10.6 %collective-permute-start.2 = (bf16[128,384]{1,0:T(8,128)(2,1)S(1)}, bf16[128,384]{1,0:T(8,128)(2,1)S(1)}, u32[]{:S(2)}, u32[]{:S(2)}) collective-permute-start(bf16[128,384]{1,0:T(8,128)(2,1)S(1)} %get-tuple-element.22.refs_0_), channel_id=1, source_target_pairs={{0,2},{1,3},{2,0},{3,1},{4,6},{5,7},{6,4},{7,5},{8,10},{9,11},{10,... | collective-permute-start | bytes 294920 | tf_op jit(solution)/shard_map/ppermute | solution.py:209
  11.5 8.1 %collective-permute-start.3 = (bf16[128,384]{1,0:T(8,128)(2,1)S(1)}, bf16[128,384]{1,0:T(8,128)(2,1)S(1)}, u32[]{:S(2)}, u32[]{:S(2)}) collective-permute-start(bf16[128,384]{1,0:T(8,128)(2,1)S(1)} %get-tuple-element.22.refs_0_), channel_id=1, source_target_pairs={{0,3},{1,2},{2,1},{3,0},{4,7},{5,6},{6,5},{7,4},{8,11},{9,10},{10,... | collective-permute-start | bytes 294920 | tf_op jit(solution)/shard_map/ppermute | solution.py:209
  11.7 11.6 %collective-permute-start.4 = (bf16[128,384]{1,0:T(8,128)(2,1)S(1)}, bf16[128,384]{1,0:T(8,128)(2,1)S(1)}, u32[]{:S(2)}, u32[]{:S(2)}) collective-permute-start(bf16[128,384]{1,0:T(8,128)(2,1)S(1)} %get-tuple-element.23), channel_id=1, source_target_pairs={{0,8},{1,9},{2,10},{3,11},{4,12},{5,13},{6,14},{7,15},{8,0},{9,1},... | collective-permute-start | bytes 294920 | tf_op jit(solution)/shard_map/ppermute | solution.py:209
  12.9 10.4 %collective-permute-start.5 = (bf16[128,384]{1,0:T(8,128)(2,1)S(1)}, bf16[128,384]{1,0:T(8,128)(2,1)S(1)}, u32[]{:S(2)}, u32[]{:S(2)}) collective-permute-start(bf16[128,384]{1,0:T(8,128)(2,1)S(1)} %get-tuple-element.23), channel_id=1, source_target_pairs={{0,9},{1,8},{2,11},{3,10},{4,13},{5,12},{6,15},{7,14},{8,1},{9,0},... | collective-permute-start | bytes 294920 | tf_op jit(solution)/shard_map/ppermute | solution.py:209
  19.5 8.5 %collective-permute-start.6 = (bf16[128,384]{1,0:T(8,128)(2,1)S(1)}, bf16[128,384]{1,0:T(8,128)(2,1)S(1)}, u32[]{:S(2)}, u32[]{:S(2)}) collective-permute-start(bf16[128,384]{1,0:T(8,128)(2,1)S(1)} %get-tuple-element.23), channel_id=1, source_target_pairs={{0,10},{1,11},{2,8},{3,9},{4,14},{5,15},{6,12},{7,13},{8,2},{9,3},... | collective-permute-start | bytes 294920 | tf_op jit(solution)/shard_map/ppermute | solution.py:209
  19.5 8.5 %collective-permute-start.7 = (bf16[128,384]{1,0:T(8,128)(2,1)S(1)}, bf16[128,384]{1,0:T(8,128)(2,1)S(1)}, u32[]{:S(2)}, u32[]{:S(2)}) collective-permute-start(bf16[128,384]{1,0:T(8,128)(2,1)S(1)} %get-tuple-element.23), channel_id=1, source_target_pairs={{0,11},{1,10},{2,9},{3,8},{4,15},{5,14},{6,13},{7,12},{8,3},{9,2},... | collective-permute-start | bytes 294920 | tf_op jit(solution)/shard_map/ppermute | solution.py:209
  30.4 4.7 %collective-permute-start.8 = (f32[256,384]{1,0:T(8,128)S(1)}, f32[256,384]{1,0:T(8,128)S(1)}, u32[]{:S(2)}, u32[]{:S(2)}) collective-permute-start(f32[256,384]{1,0:T(8,128)S(1)} %get-tuple-element.25), channel_id=1, source_target_pairs={{0,4},{1,5},{2,6},{3,7},{4,0},{5,1},{6,2},{7,3},{8,12},{9,13},{10,... | collective-permute-start | bytes 1179656 | tf_op jit(solution)/shard_map/ppermute | solution.py:209
  30.5 4.6 %collective-permute-start.9 = (bf16[256,384]{1,0:T(8,128)(2,1)S(1)}, bf16[256,384]{1,0:T(8,128)(2,1)S(1)}, u32[]{:S(2)}, u32[]{:S(2)}) collective-permute-start(bf16[256,384]{1,0:T(8,128)(2,1)S(1)} %get-tuple-element.27), channel_id=1, source_target_pairs={{0,4},{1,5},{2,6},{3,7},{4,0},{5,1},{6,2},{7,3},{8,12},{9,13},{10,... | collective-permute-start | bytes 589832 | tf_op jit(solution)/shard_map/ppermute | solution.py:209
  31.0 3.8 %collective-permute-start.10 = (bf16[24,384]{1,0:T(8,128)(2,1)S(1)}, bf16[24,384]{1,0:T(8,128)(2,1)S(1)}, u32[]{:S(2)}, u32[]{:S(2)}) collective-permute-start(bf16[24,384]{1,0:T(8,128)(2,1)S(1)} %get-tuple-element.29), channel_id=1, source_target_pairs={{0,8},{1,9},{2,10},{3,11},{4,12},{5,13},{6,14},{7,15},{8,0},{9,1},... | collective-permute-start | bytes 55304 | tf_op jit(solution)/shard_map/ppermute | solution.py:209
  36.1 1.5 %collective-permute-start.14 = (f32[3,128,128]{2,1,0:T(8,128)S(1)}, f32[3,128,128]{2,1,0:T(8,128)S(1)}, u32[]{:S(2)}, u32[]{:S(2)}) collective-permute-start(f32[3,128,128]{2,1,0:T(8,128)S(1)} %get-tuple-element.33), channel_id=1, source_target_pairs={{0,4},{1,5},{2,6},{3,7},{4,0},{5,1},{6,2},{7,3},{8,12},{9,13},{10,... | collective-permute-start | bytes 589832 | tf_op jit(solution)/shard_map/ppermute | solution.py:209
  38.2 7.2 %collective-permute-start.15 = (f32[48,128]{1,0:T(8,128)S(1)}, f32[48,128]{1,0:T(8,128)S(1)}, u32[]{:S(2)}, u32[]{:S(2)}) collective-permute-start(f32[48,128]{1,0:T(8,128)S(1)} %get-tuple-element.35), channel_id=1, source_target_pairs={{0,1},{1,0},{2,3},{3,2},{4,5},{5,4},{6,7},{7,6},{8,9},{9,8},{10,11... | collective-permute-start | bytes 73736 | tf_op jit(solution)/shard_map/ppermute | solution.py:209
  39.9 9.0 %collective-permute-start.16 = (f32[48,128]{1,0:T(8,128)S(1)}, f32[48,128]{1,0:T(8,128)S(1)}, u32[]{:S(2)}, u32[]{:S(2)}) collective-permute-start(f32[48,128]{1,0:T(8,128)S(1)} %get-tuple-element.36), channel_id=1, source_target_pairs={{0,2},{1,3},{2,0},{3,1},{4,6},{5,7},{6,4},{7,5},{8,10},{9,11},{10,... | collective-permute-start | bytes 73736 | tf_op jit(solution)/shard_map/ppermute | solution.py:209
  42.1 8.0 %collective-permute-start.17 = (f32[48,128]{1,0:T(8,128)S(1)}, f32[48,128]{1,0:T(8,128)S(1)}, u32[]{:S(2)}, u32[]{:S(2)}) collective-permute-start(f32[48,128]{1,0:T(8,128)S(1)} %get-tuple-element.37), channel_id=1, source_target_pairs={{0,3},{1,2},{2,1},{3,0},{4,7},{5,6},{6,5},{7,4},{8,11},{9,10},{10,... | collective-permute-start | bytes 73736 | tf_op jit(solution)/shard_map/ppermute | solution.py:209
  43.3 7.4 %collective-permute-start.18 = (f32[48,128]{1,0:T(8,128)S(1)}, f32[48,128]{1,0:T(8,128)S(1)}, u32[]{:S(2)}, u32[]{:S(2)}) collective-permute-start(f32[48,128]{1,0:T(8,128)S(1)} %get-tuple-element.38), channel_id=1, source_target_pairs={{0,16},{1,17},{2,18},{3,19},{4,20},{5,21},{6,22},{7,23},{8,24},{9,... | collective-permute-start | bytes 73736 | tf_op jit(solution)/shard_map/ppermute | solution.py:209
  44.8 7.0 %collective-permute-start.19 = (f32[48,128]{1,0:T(8,128)S(1)}, f32[48,128]{1,0:T(8,128)S(1)}, u32[]{:S(2)}, u32[]{:S(2)}) collective-permute-start(f32[48,128]{1,0:T(8,128)S(1)} %get-tuple-element.39), channel_id=1, source_target_pairs={{0,17},{1,16},{2,19},{3,18},{4,21},{5,20},{6,23},{7,22},{8,25},{9,... | collective-permute-start | bytes 73736 | tf_op jit(solution)/shard_map/ppermute | solution.py:209
  45.3 6.5 %collective-permute-start.20 = (f32[48,128]{1,0:T(8,128)S(1)}, f32[48,128]{1,0:T(8,128)S(1)}, u32[]{:S(2)}, u32[]{:S(2)}) collective-permute-start(f32[48,128]{1,0:T(8,128)S(1)} %get-tuple-element.40), channel_id=1, source_target_pairs={{0,18},{1,19},{2,16},{3,17},{4,22},{5,23},{6,20},{7,21},{8,26},{9,... | collective-permute-start | bytes 73736 | tf_op jit(solution)/shard_map/ppermute | solution.py:209
  48.9 6.5 %collective-permute-start.21 = (f32[48,128]{1,0:T(8,128)S(1)}, f32[48,128]{1,0:T(8,128)S(1)}, u32[]{:S(2)}, u32[]{:S(2)}) collective-permute-start(f32[48,128]{1,0:T(8,128)S(1)} %get-tuple-element.41), channel_id=1, source_target_pairs={{0,19},{1,18},{2,17},{3,16},{4,23},{5,22},{6,21},{7,20},{8,27},{9,... | collective-permute-start | bytes 73736 | tf_op jit(solution)/shard_map/ppermute | solution.py:209
  50.1 22.1 %collective-permute-start.11 = (bf16[128,384]{1,0:T(8,128)(2,1)S(1)}, bf16[128,384]{1,0:T(8,128)(2,1)S(1)}, u32[]{:S(2)}, u32[]{:S(2)}) collective-permute-start(bf16[128,384]{1,0:T(8,128)(2,1)S(1)} %get-tuple-element.30), channel_id=1, source_target_pairs={{0,0},{4,3},{1,5},{5,6},{6,2},{2,1},{7,7},{3,4},{8,8},{12,11},{9,1... | collective-permute-start | bytes 294920 | tf_op jit(solution)/shard_map/ppermute | solution.py:278
  50.7 21.4 %collective-permute-start.12 = (bf16[128,384]{1,0:T(8,128)(2,1)S(1)}, bf16[128,384]{1,0:T(8,128)(2,1)S(1)}, u32[]{:S(2)}, u32[]{:S(2)}) collective-permute-start(bf16[128,384]{1,0:T(8,128)(2,1)S(1)} %get-tuple-element.31), channel_id=1, source_target_pairs={{0,1},{4,2},{1,4},{5,7},{6,3},{2,0},{7,6},{3,5},{8,9},{12,10},{9,1... | collective-permute-start | bytes 294920 | tf_op jit(solution)/shard_map/ppermute | solution.py:279
  55.5 4.5 %collective-permute-start.22 = (f32[48,128]{1,0:T(8,128)S(1)}, f32[48,128]{1,0:T(8,128)S(1)}, u32[]{:S(2)}, u32[]{:S(2)}) collective-permute-start(f32[48,128]{1,0:T(8,128)S(1)} %shard_map.74.refs_0_), channel_id=1, source_target_pairs={{0,1},{1,0},{2,3},{3,2},{4,5},{5,4},{6,7},{7,6},{8,9},{9,8},{10,11... | collective-permute-start | bytes 73736 | tf_op jit(solution)/shard_map/ppermute | solution.py:209
  56.5 4.7 %collective-permute-start.23 = (f32[48,128]{1,0:T(8,128)S(1)}, f32[48,128]{1,0:T(8,128)S(1)}, u32[]{:S(2)}, u32[]{:S(2)}) collective-permute-start(f32[48,128]{1,0:T(8,128)S(1)} %shard_map.74.refs_0_), channel_id=1, source_target_pairs={{0,2},{1,3},{2,0},{3,1},{4,6},{5,7},{6,4},{7,5},{8,10},{9,11},{10,... | collective-permute-start | bytes 73736 | tf_op jit(solution)/shard_map/ppermute | solution.py:209
  57.4 5.6 %collective-permute-start.24 = (f32[48,128]{1,0:T(8,128)S(1)}, f32[48,128]{1,0:T(8,128)S(1)}, u32[]{:S(2)}, u32[]{:S(2)}) collective-permute-start(f32[48,128]{1,0:T(8,128)S(1)} %shard_map.74.refs_0_), channel_id=1, source_target_pairs={{0,3},{1,2},{2,1},{3,0},{4,7},{5,6},{6,5},{7,4},{8,11},{9,10},{10,... | collective-permute-start | bytes 73736 | tf_op jit(solution)/shard_map/ppermute | solution.py:209
  59.9 4.3 %collective-permute-start.25 = (f32[48,128]{1,0:T(8,128)S(1)}, f32[48,128]{1,0:T(8,128)S(1)}, u32[]{:S(2)}, u32[]{:S(2)}) collective-permute-start(f32[48,128]{1,0:T(8,128)S(1)} %shard_map.74.refs_0_), channel_id=1, source_target_pairs={{0,16},{1,17},{2,18},{3,19},{4,20},{5,21},{6,22},{7,23},{8,24},{9,... | collective-permute-start | bytes 73736 | tf_op jit(solution)/shard_map/ppermute | solution.py:209
  61.2 6.3 %collective-permute-start.26 = (f32[48,128]{1,0:T(8,128)S(1)}, f32[48,128]{1,0:T(8,128)S(1)}, u32[]{:S(2)}, u32[]{:S(2)}) collective-permute-start(f32[48,128]{1,0:T(8,128)S(1)} %shard_map.74.refs_0_), channel_id=1, source_target_pairs={{0,17},{1,16},{2,19},{3,18},{4,21},{5,20},{6,23},{7,22},{8,25},{9,... | collective-permute-start | bytes 73736 | tf_op jit(solution)/shard_map/ppermute | solution.py:209
  63.0 5.9 %collective-permute-start.27 = (f32[48,128]{1,0:T(8,128)S(1)}, f32[48,128]{1,0:T(8,128)S(1)}, u32[]{:S(2)}, u32[]{:S(2)}) collective-permute-start(f32[48,128]{1,0:T(8,128)S(1)} %shard_map.74.refs_0_), channel_id=1, source_target_pairs={{0,18},{1,19},{2,16},{3,17},{4,22},{5,23},{6,20},{7,21},{8,26},{9,... | collective-permute-start | bytes 73736 | tf_op jit(solution)/shard_map/ppermute | solution.py:209
  64.2 6.5 %collective-permute-start.28 = (f32[48,128]{1,0:T(8,128)S(1)}, f32[48,128]{1,0:T(8,128)S(1)}, u32[]{:S(2)}, u32[]{:S(2)}) collective-permute-start(f32[48,128]{1,0:T(8,128)S(1)} %shard_map.74.refs_0_), channel_id=1, source_target_pairs={{0,19},{1,18},{2,17},{3,16},{4,23},{5,22},{6,21},{7,20},{8,27},{9,... | collective-permute-start | bytes 73736 | tf_op jit(solution)/shard_map/ppermute | solution.py:209
  71.3 5.8 %collective-permute-start.29 = (f32[384,128]{1,0:T(8,128)S(1)}, f32[384,128]{1,0:T(8,128)S(1)}, u32[]{:S(2)}, u32[]{:S(2)}) collective-permute-start(f32[384,128]{1,0:T(8,128)S(1)} %shard_map.75.own), channel_id=1, source_target_pairs={{0,8},{1,9},{2,10},{3,11},{4,12},{5,13},{6,14},{7,15},{8,0},{9,1},... | collective-permute-start | bytes 589832 | tf_op jit(solution)/shard_map/ppermute | solution.py:209
  72.1 6.1 %collective-permute-start.13 = (bf16[128,384]{1,0:T(8,128)(2,1)S(1)}, bf16[128,384]{1,0:T(8,128)(2,1)S(1)}, u32[]{:S(2)}, u32[]{:S(2)}) collective-permute-start(bf16[128,384]{1,0:T(8,128)(2,1)S(1)} %broadcast_select_fusion), channel_id=1, source_target_pairs={{0,8},{1,9},{2,10},{3,11},{4,12},{5,13},{6,14},{7,15},{8,0},{9,1},... | collective-permute-start | bytes 294920 | tf_op jit(solution)/shard_map/ppermute | solution.py:209
  73.5 6.2 %collective-permute-start.30 = (f32[384,128]{1,0:T(8,128)S(1)}, f32[384,128]{1,0:T(8,128)S(1)}, u32[]{:S(2)}, u32[]{:S(2)}) collective-permute-start(f32[384,128]{1,0:T(8,128)S(1)} %shard_map.75.own), channel_id=1, source_target_pairs={{0,4},{1,5},{2,6},{3,7},{4,0},{5,1},{6,2},{7,3},{8,12},{9,13},{10,... | collective-permute-start | bytes 589832 | tf_op jit(solution)/shard_map/ppermute | solution.py:209
  77.1 2.6 %collective-permute-start.31 = (f32[384,128]{1,0:T(8,128)S(1)}, f32[384,128]{1,0:T(8,128)S(1)}, u32[]{:S(2)}, u32[]{:S(2)}) collective-permute-start(f32[384,128]{1,0:T(8,128)S(1)} %collective-permute-done.29.across), channel_id=1, source_target_pairs={{0,4},{1,5},{2,6},{3,7},{4,0},{5,1},{6,2},{7,3},{8,12},{9,13},{10,... | collective-permute-start | bytes 589832 | tf_op jit(solution)/shard_map/ppermute | solution.py:209
  (3 other events, 2.7 us)

commit v4 on v3

v4 whole, which is shorter than its diff:
```python
import functools

import jax
import jax.numpy as jnp
from jax import lax
from jax.experimental import pallas as pl
from jax.experimental.pallas import tpu as pltpu
from jax.sharding import PartitionSpec as P

LANES = 128
ROWS = 16
VMEM = pl.BlockSpec(memory_space=pltpu.VMEM)
SMEM = pl.BlockSpec(memory_space=pltpu.SMEM)
ANY = pl.BlockSpec(memory_space=pl.ANY)
AXES = ("hyp", "side", "core", "pcol")


def call(kernel, outs, specs, *operands, scratch=(), out_specs=None, after=()):
    many = isinstance(outs, (list, tuple))
    count = len(specs)

    def body(*refs):
        kernel(*refs[:count], *refs[count + len(after) :])

    if out_specs is None:
        out_specs = [VMEM] * len(outs) if many else VMEM
    return pl.pallas_call(
        body,
        out_shape=outs,
        in_specs=list(specs) + [ANY] * len(after),
        out_specs=out_specs,
        scratch_shapes=scratch,
        compiler_params=pltpu.CompilerParams(vmem_limit_bytes=32 * 2**20),
    )(*operands, *after)


def transposed_dot(left, right):
    return lax.dot_general(
        left, right, (((0,), (0,)), ((), ())), preferred_element_type=jnp.float32
    )


def tiles(width):
    count = width // LANES
    return [(a, b) for a in range(count) for b in range(a, count)]


def general(sigma_rows, panel, live_block_rows, inv_diag, quad_weight):
    height, count, width = panel.shape[1:]
    offsets = lax.broadcasted_iota(jnp.int32, (height, count), 0)
    active = offsets < live_block_rows[:, 0][None, :]
    masked = jnp.where(active[:, :, None], panel[0], jnp.zeros_like(panel[0]))
    extent = height * lax.axis_size("prow")
    gathered = lax.all_gather(masked, ("prow", "pcol"), axis=0, tiled=True)
    start = lax.axis_index("pcol") * sigma_rows.shape[2]
    column_panel = lax.dynamic_slice_in_dim(gathered, start, sigma_rows.shape[2], 0)
    applied = lax.psum_scatter(
        jnp.dot(
            sigma_rows[0],
            column_panel.reshape(sigma_rows.shape[2], count * width),
            preferred_element_type=jnp.float32,
        ),
        "pcol",
        scatter_dimension=0,
        tiled=True,
    ).reshape(height, count, width)
    half = applied.astype(jnp.bfloat16)
    sigma_panel = jnp.where(active[:, :, None], -half, jnp.zeros_like(half))[None]
    coupling = jnp.einsum(
        "vwg,vwe->wge",
        masked.astype(jnp.float32),
        applied,
        precision=lax.Precision.HIGHEST,
    )
    diagonal = jnp.einsum(
        "skp,skq->spq", inv_diag[0], inv_diag[0], preferred_element_type=jnp.float32
    )
    marginal = lax.psum(quad_weight[0] * (coupling + diagonal), ("hyp", "prow", "pcol"))
    return sigma_panel, marginal


def mask_kernel(live_hbm, panel_hbm, own, give, live, panel, sems):
    copies = [
        pltpu.make_async_copy(panel_hbm.at[0], panel, sems.at[0]),
        pltpu.make_async_copy(live_hbm, live, sems.at[1]),
    ]
    for copy in copies:
        copy.start()
    for copy in copies:
        copy.wait()
    first = lax.axis_index("side") == 0
    row = lax.broadcasted_iota(jnp.int32, own.shape, 0)
    rows = panel[...]
    zero = jnp.zeros(own.shape, own.dtype)
    one, two = (jnp.where(row < live[s], rows[:, s, :], zero) for s in range(2))
    own[...] = jnp.where(first, one, two)
    give[...] = jnp.where(first, two, one)


def flip_kernel(matrix, out):
    out[...] = matrix[0].T


def apply_kernel(own_sigma, far_sigma, *refs):
    blocks, (own_inverse, got_inverse, applied, pack, panel) = refs[:8], refs[8:]
    column = lax.axis_index("pcol")
    height = blocks[0].shape[0]
    for index, block in enumerate(blocks):
        spot = jnp.bitwise_xor(column, (0, 2, 1, 3)[index % 4])
        panel[index // 4, pl.ds(pl.multiple_of(spot * height, height), height), :] = block[...]
    applied[...] = jnp.dot(own_sigma[...], panel[0], preferred_element_type=jnp.float32)
    applied[...] += jnp.dot(far_sigma[...], panel[1], preferred_element_type=jnp.float32)
    extent = panel.shape[1]
    size = own_inverse.shape[0]
    pack[:extent] = panel[jnp.where(column // 2 == lax.axis_index("side"), 0, 1)]
    pack[extent : extent + size] = own_inverse[...]
    pack[extent + size :] = got_inverse[...]


def couple_kernel(weight, mine, other, pack, got_pack, out_a, out_b, keep, send, half, packed):
    core, column, point = (lax.axis_index(name) for name in ("core", "pcol", "hyp"))
    applied = mine[...] + other[...]
    high = applied.astype(jnp.bfloat16)
    low = (applied - high.astype(jnp.float32)).astype(jnp.bfloat16)
    half[...] = -high
    extent = applied.shape[0]
    rows = jnp.where(column % 2 == core, pack[:extent], got_pack[:extent])
    inverse = (pack[extent:], got_pack[extent:])
    blocks = tiles(applied.shape[1])
    per = len(blocks) // 2
    for part in range(2):

        @pl.when(core == part)
        def _():
            mine_blocks = blocks[part * per : (part + 1) * per]
            at = 0
            for first in sorted({a for a, _ in mine_blocks}):
                seconds = [b for a, b in mine_blocks if a == first]
                left = slice(first * LANES, (first + 1) * LANES)
                right = slice(seconds[0] * LANES, (seconds[-1] + 1) * LANES)
                total = transposed_dot(rows[:, left], high[:, right])
                total += transposed_dot(rows[:, left], low[:, right])
                for lines in inverse:
                    total += transposed_dot(lines[:, left], lines[:, right])
                for index in range(len(seconds)):
                    packed[at * LANES : (at + 1) * LANES, :] = (
                        weight[0] * total[:, index * LANES : (index + 1) * LANES]
                    )
                    at += 1

    size = keep.shape[0]
    keep[...] = packed[pl.ds(pl.multiple_of(point * size, 8), size), :]
    send[...] = packed[pl.ds(pl.multiple_of((1 - point) * size, 8), size), :]
    height = out_a.shape[0]
    near = core == column // 2
    for out, steps in ((out_a, (0, 3)), (out_b, (1, 2))):
        spot = jnp.bitwise_xor(column, jnp.where(near, steps[0], steps[1]))
        out[...] = half[pl.ds(pl.multiple_of(spot * height, height), height), :]


def halve_kernel(mine, came, keep, send, whole):
    whole[...] = mine[...] + came[...]
    size = keep.shape[0]
    bit = lax.axis_index("pcol") // 2
    keep[...] = whole[pl.ds(pl.multiple_of(bit * size, 8), size), :]
    send[...] = whole[pl.ds(pl.multiple_of((1 - bit) * size, 8), size), :]


def add_kernel(mine, came, out):
    out[...] = mine[...] + came[...]


def join_kernel(mine, came, out):
    size = mine.shape[0]
    bit = lax.axis_index("pcol") // 2
    out[pl.ds(pl.multiple_of(bit * size, 8), size), :] = mine[...]
    out[pl.ds(pl.multiple_of((1 - bit) * size, 8), size), :] = came[...]


def spread_kernel(*refs):
    parts, (out, lines, result, sems) = refs[:8], refs[8:]
    point, side, core = (lax.axis_index(name) for name in ("hyp", "side", "core"))
    width = result.shape[1]
    blocks = tiles(width)
    per = len(blocks) // 2
    size = parts[0].shape[0]
    for other_core in range(2):
        for index in range(4):
            part = jnp.where(other_core, 1 - core, core)
            node = jnp.where(index % 2, 1 - side, side)
            slot = jnp.where(index // 2, 1 - point, point)
            start = pl.multiple_of((part * 2 + slot) * size, 8)
            lines[node, pl.ds(start, size), :] = parts[4 * other_core + index][...]
    copies = []
    for node in range(2):
        for index, (a, b) in enumerate(blocks):
            tile = lines[node, index * LANES : (index + 1) * LANES, :]
            result[node, a * LANES : (a + 1) * LANES, b * LANES : (b + 1) * LANES] = tile
            if a != b:
                result[node, b * LANES : (b + 1) * LANES, a * LANES : (a + 1) * LANES] = tile.T
        copies.append(pltpu.make_async_copy(result.at[node], out.at[node], sems.at[node]))
        copies[-1].start()
    for copy in copies:
        copy.wait()


def finish_kernel(live, a, b, out):
    row = lax.broadcasted_iota(jnp.int32, a.shape, 0)
    for s, block in enumerate((a, b)):
        out[0, :, s, :] = jnp.where(row < live[s], block[...], jnp.zeros(a.shape, a.dtype))


def square(sigma_rows, panel, live_block_rows, inv_diag, quad_weight):
    height, count, width = panel.shape[1:]
    grid = lax.axis_size("pcol")
    points = lax.axis_size("hyp")
    point, side, core, column = (lax.axis_index(name) for name in AXES)
    f32, bf16 = jnp.float32, jnp.bfloat16
    shape = jax.ShapeDtypeStruct
    dma = pltpu.SemaphoreType.DMA
    total = points * 2 * 2 * grid
    live = live_block_rows[:, 0]
    pick = functools.partial(lax.dynamic_index_in_dim, axis=0, keepdims=False)

    def swap(x, point=0, side=0, core=0, column=0):
        mask = ((point * 2 + side) * 2 + core) * grid + column
        return lax.ppermute(x, AXES, [(i, i ^ mask) for i in range(total)])

    block = shape((height, width), bf16)
    own, give = call(
        mask_kernel, [block, block], [ANY, ANY], live, panel,
        scratch=[pltpu.SMEM((2,), jnp.int32), pltpu.VMEM((height, count, width), bf16), dma((2,))],
    )
    got = swap(give, side=1)
    blocks = []
    for start in (own, got):
        second = swap(start, column=2)
        blocks += [start, second, swap(start, column=1), swap(second, column=1)]

    extent = sigma_rows.shape[2]
    sigma = call(flip_kernel, shape((extent, extent), bf16), [VMEM], sigma_rows, after=[own])
    far_sigma = swap(sigma, side=1)
    inverse = jnp.pad(inv_diag[0], ((0, 0), (0, -inv_diag.shape[2] % ROWS), (0, 0)))
    got_inverse = swap(pick(inverse, 1 - side), side=1)

    product = shape((extent, width), f32)
    pack = shape((extent + 2 * inverse.shape[1], width), bf16)
    mine, pack = call(
        apply_kernel, [product, pack], [VMEM] * 12,
        sigma, far_sigma, *blocks, pick(inverse, side), got_inverse,
        scratch=[pltpu.VMEM((2, extent, width), bf16)],
    )
    other = swap(mine, core=1)
    got_pack = swap(pack, core=1)

    lines = len(tiles(width)) // 2 * LANES

    def part(count):
        return shape((count, LANES), f32)

    out_a, out_b, keep, send = call(
        couple_kernel, [block, block, part(lines // 2), part(lines // 2)], [SMEM] + [VMEM] * 4,
        quad_weight, mine, other, pack, got_pack,
        scratch=[pltpu.VMEM((extent, width), bf16), pltpu.VMEM((lines, LANES), f32)],
    )
    keep, send = call(
        halve_kernel, [part(lines // 4)] * 2, [VMEM] * 2, keep, swap(send, point=1),
        scratch=[pltpu.VMEM((lines // 2, LANES), f32)],
    )

    def output_pairs(steps):
        pairs = []
        for h in range(points):
            for s in range(2):
                for c in range(grid):
                    for core, step in ((c // 2, steps[0]), (1 - c // 2, steps[1])):
                        base = (h * 2 + s) * 2
                        pairs.append(((base + core) * grid + c, (base + c % 2) * grid + (c ^ step)))
        return pairs

    land_a = lax.ppermute(out_a, AXES, output_pairs((0, 3)))
    land_b = lax.ppermute(out_b, AXES, output_pairs((1, 2)))
    from_a = jnp.where(column % 2 == core, column, column ^ 3) // 2

    sum_two = call(add_kernel, part(lines // 4), [VMEM] * 2, keep, swap(send, column=2))
    sum_all = call(add_kernel, part(lines // 4), [VMEM] * 2, sum_two, swap(sum_two, column=1))
    here = call(
        join_kernel, part(lines // 2), [VMEM] * 2, sum_all, swap(sum_all, column=2),
        after=[land_a, land_b],
    )
    across = swap(here, side=1)
    there = swap(here, point=1)
    both = swap(across, point=1)
    quarters = [here, across, there, both]
    quarters += [swap(x, core=1) for x in quarters]

    theirs = swap(jnp.where(from_a == side, land_b, land_a), side=1)
    mine = jnp.where(from_a == side, land_a, land_b)
    first = jnp.where(side == 0, mine, theirs)
    last = jnp.where(side == 0, theirs, mine)
    sigma_panel = call(
        finish_kernel, shape((1, height, count, width), bf16), [SMEM, VMEM, VMEM], live, first, last
    )
    marginal = call(
        spread_kernel, shape((count, width, width), f32), [VMEM] * 8, *quarters,
        scratch=[
            pltpu.VMEM((count, 2 * lines, LANES), f32),
            pltpu.VMEM((count, width, width), f32),
            dma((2,)),
        ],
        out_specs=ANY,
        after=[sigma_panel],
    )
    return sigma_panel, marginal


def solution(mesh):
    sizes = dict(mesh.shape)
    prow, pcol = ("prow",), ("pcol",)

    def on_device(sigma_rows, panel, live_block_rows, inv_diag, quad_weight):
        body = square if split else general
        return body(sigma_rows, panel, live_block_rows, inv_diag, quad_weight)

    split = sizes["hyp"] == 2 and sizes["pcol"] == 4 and sizes["prow"] == 4
    if split:
        prow = ("side", "core")
        mesh = jax.sharding.Mesh(
            mesh.devices.reshape(sizes["hyp"], 2, 2, sizes["pcol"]),
            ("hyp", "side", "core", "pcol"),
        )
    in_specs = (
        P("hyp", prow, pcol),
        P("hyp", prow + pcol, None, None),
        P(None, prow + pcol),
        P("hyp", None, prow + pcol, None),
        P("hyp"),
    )
    out_specs = (P("hyp", prow + pcol, None, None), P())
    return jax.shard_map(
        on_device, mesh=mesh, in_specs=in_specs, out_specs=out_specs, check_vma=False
    )
```

time: 81.8 us -> 75.6 us (0.924)
  starting transfers between devices: 41 us -> 29.9 us
  waiting for transfers between devices: 27.4 us -> 34.7 us
  Pallas kernels: 8.2 us -> 5.68 us
    ppermute x30 -> x23, starting transfers between devices: 39.3 us -> 28.8 us  [swap(): return lax.ppermute(x, AXES, [(i, i ^ mask) for i in range(total)])]
    ppermute x30 -> x23, waiting for transfers between devices: 27.3 us -> 33.4 us  [swap(): return lax.ppermute(x, AXES, [(i, i ^ mask) for i in range(total)])]
    pallas_call x9 -> x10, Pallas kernels: 8.2 us -> 5.68 us  [call(): pl.pallas_call(body, out_shape=outs, in_specs=list(specs) + [ANY] * len(a...]
    ppermute x1, waiting for transfers between devices: 0.01 us -> 1.3 us  [square(): land_b = lax.ppermute(out_b, AXES, output_pairs((1, 2)))]
    unnamed x7 -> x12, local copies, waits for them, and re-layouts: 3.48 us -> 3.54 us
  transfers between devices with their start and end apart: 32 -> 25, of which waited for: 12 -> 13; matrix products, arithmetic and copies ran while one was open for 1% -> 0% of each run, Pallas kernels for 4% -> 2%
where the time goes in v4:
time: 75.6 us; the launch traced here: 75.4 us
  waiting for transfers between devices  34.7 us (46%)
  starting transfers between devices  29.9 us (40%)
  Pallas kernels  5.68 us (8%)
  local copies, waits for them, and re-layouts  3.55 us (5%)
  between operations  1.42 us (2%)
    ppermute x23, waiting for transfers between devices, swap(): return lax.ppermute(x, AXES, [(i, i ^ mask) for i in range(total)])  33.4 us
    ppermute x23, starting transfers between devices, swap(): return lax.ppermute(x, AXES, [(i, i ^ mask) for i in range(total)])  28.8 us
    pallas_call x10, Pallas kernels, call(): pl.pallas_call(body, out_shape=outs, in_specs=list(specs) + [ANY] * len(a...  5.68 us
    unnamed x12, local copies, waits for them, and re-layouts  3.54 us
  transfers between devices with their start and end apart: 25, of which 13 were waited for; matrix products, arithmetic and copies ran while one was open for 0% of the time, Pallas kernels for 2%

profile of v4, /device:TPU:0, one launch (start us, length us, event | category | flops | bytes accessed | tf_op | source)
XLA Modules:
  0.0 75.4 jit_solution(2895614380809596281)
XLA Ops:
  0.6 0.9 %copy-done.2 = bf16[1,128,2,384]{3,2,1,0:T(2,128)(2,1)S(1)} copy-done((bf16[1,128,2,384]{3,2,1,0:T(2,128)(2,1)S(1)}, bf16[1,128,2,384]{3,2,1,0:T(2,128)(2,1)}, u32[]{:S(2)}) %copy-start.2) | copy-done | bytes 196632
  2.2 1.3 %shard_map.68 = (bf16[128,384]{1,0:T(8,128)(2,1)S(1)}, bf16[128,384]{1,0:T(8,128)(2,1)S(1)}) custom-call(s32[2]{0:T(128)S(1)} %bitcast.6, bf16[1,128,2,384]{3,2,1,0:T(2,128)(2,1)S(1)} %copy-done.2), custom_call_target="tpu_custom_call" | custom-call | tf_op jit(solution)/shard_map/pallas_call | solution.py:27
  3.6 1.0 %copy-done.1 = bf16[1,512,512]{2,1,0:T(8,128)(2,1)S(1)} copy-done((bf16[1,512,512]{2,1,0:T(8,128)(2,1)S(1)}, bf16[1,512,512]{2,1,0:T(8,128)(2,1)}, u32[]{:S(2)}) %copy-start.1) | copy-done | bytes 524312
  4.8 3.0 %collective-permute-start = (bf16[512,512]{1,0:T(8,128)(2,1)S(1)}, bf16[512,512]{1,0:T(8,128)(2,1)S(1)}, u32[]{:S(2)}, u32[]{:S(2)}) collective-permute-start(bf16[512,512]{1,0:T(8,128)(2,1)S(1)} %shard_map.69.refs_0_), channel_id=1, source_target_pairs={{0,8},{1,9},{2,10},{3,11},{4,12},{5,13},{6,14},{7,15},{8,0},{9,1},... | collective-permute-start | bytes 1572872 | tf_op jit(solution)/shard_map/ppermute | solution.py:227
  7.9 3.0 %collective-permute-start.1 = (bf16[128,384]{1,0:T(8,128)(2,1)S(1)}, bf16[128,384]{1,0:T(8,128)(2,1)S(1)}, u32[]{:S(2)}, u32[]{:S(2)}) collective-permute-start(bf16[128,384]{1,0:T(8,128)(2,1)S(1)} %get-tuple-element.12.refs_1_.refs_2_), channel_id=1, source_target_pairs={{0,2},{1,3},{2,0},{3,1},{4,6},{5,7},{6,4},{7,5},{8,10},{9,11},{10,... | collective-permute-start | bytes 294920 | tf_op jit(solution)/shard_map/ppermute | solution.py:227
  10.9 10.9 %collective-permute-done.4.refs_6_ = bf16[128,384]{1,0:T(8,128)(2,1)S(1)} collective-permute-done((bf16[128,384]{1,0:T(8,128)(2,1)S(1)}, bf16[128,384]{1,0:T(8,128)(2,1)S(1)}, u32[]{:S(2)}, u32[]{:S(2)}) %collective-permute-start.4) | collective-permute-done | bytes 98336 | tf_op jit(solution)/shard_map/ppermute | solution.py:227
  21.8 2.8 %collective-permute-start.5 = (bf16[128,384]{1,0:T(8,128)(2,1)S(1)}, bf16[128,384]{1,0:T(8,128)(2,1)S(1)}, u32[]{:S(2)}, u32[]{:S(2)}) collective-permute-start(bf16[128,384]{1,0:T(8,128)(2,1)S(1)} %collective-permute-done.4.refs_6_), channel_id=1, source_target_pairs={{0,2},{1,3},{2,0},{3,1},{4,6},{5,7},{6,4},{7,5},{8,10},{9,11},{10,... | collective-permute-start | bytes 294920 | tf_op jit(solution)/shard_map/ppermute | solution.py:227
  24.7 1.6 %collective-permute-start.8 = (bf16[32,384]{1,0:T(8,128)(2,1)S(1)}, bf16[32,384]{1,0:T(8,128)(2,1)S(1)}, u32[]{:S(2)}, u32[]{:S(2)}) collective-permute-start(bf16[32,384]{1,0:T(8,128)(2,1)S(1)} %get-tuple-element.24), channel_id=1, source_target_pairs={{0,8},{1,9},{2,10},{3,11},{4,12},{5,13},{6,14},{7,15},{8,0},{9,1},... | collective-permute-start | bytes 73736 | tf_op jit(solution)/shard_map/ppermute | solution.py:227
  26.2 1.6 %collective-permute-start.2 = (bf16[128,384]{1,0:T(8,128)(2,1)S(1)}, bf16[128,384]{1,0:T(8,128)(2,1)S(1)}, u32[]{:S(2)}, u32[]{:S(2)}) collective-permute-start(bf16[128,384]{1,0:T(8,128)(2,1)S(1)} %get-tuple-element.12.refs_1_.refs_2_), channel_id=1, source_target_pairs={{0,1},{1,0},{2,3},{3,2},{4,5},{5,4},{6,7},{7,6},{8,9},{9,8},{10,11... | collective-permute-start | bytes 294920 | tf_op jit(solution)/shard_map/ppermute | solution.py:227
  28.6 1.6 %collective-permute-start.6 = (bf16[128,384]{1,0:T(8,128)(2,1)S(1)}, bf16[128,384]{1,0:T(8,128)(2,1)S(1)}, u32[]{:S(2)}, u32[]{:S(2)}) collective-permute-start(bf16[128,384]{1,0:T(8,128)(2,1)S(1)} %collective-permute-done.4.refs_6_), channel_id=1, source_target_pairs={{0,1},{1,0},{2,3},{3,2},{4,5},{5,4},{6,7},{7,6},{8,9},{9,8},{10,11... | collective-permute-start | bytes 294920 | tf_op jit(solution)/shard_map/ppermute | solution.py:227
  30.6 1.6 %collective-permute-start.7 = (bf16[128,384]{1,0:T(8,128)(2,1)S(1)}, bf16[128,384]{1,0:T(8,128)(2,1)S(1)}, u32[]{:S(2)}, u32[]{:S(2)}) collective-permute-start(bf16[128,384]{1,0:T(8,128)(2,1)S(1)} %collective-permute-done.5.refs_7_), channel_id=1, source_target_pairs={{0,1},{1,0},{2,3},{3,2},{4,5},{5,4},{6,7},{7,6},{8,9},{9,8},{10,11... | collective-permute-start | bytes 294920 | tf_op jit(solution)/shard_map/ppermute | solution.py:227
  32.2 3.0 %collective-permute-done.3.refs_5_ = bf16[128,384]{1,0:T(8,128)(2,1)S(1)} collective-permute-done((bf16[128,384]{1,0:T(8,128)(2,1)S(1)}, bf16[128,384]{1,0:T(8,128)(2,1)S(1)}, u32[]{:S(2)}, u32[]{:S(2)}) %collective-permute-start.3) | collective-permute-done | bytes 98336 | tf_op jit(solution)/shard_map/ppermute | solution.py:227
  35.1 1.0 %collective-permute-done.7.refs_9_ = bf16[128,384]{1,0:T(8,128)(2,1)S(1)} collective-permute-done((bf16[128,384]{1,0:T(8,128)(2,1)S(1)}, bf16[128,384]{1,0:T(8,128)(2,1)S(1)}, u32[]{:S(2)}, u32[]{:S(2)}) %collective-permute-start.7) | collective-permute-done | bytes 98336 | tf_op jit(solution)/shard_map/ppermute | solution.py:227
  38.2 1.8 %collective-permute-done.10.refs_4_ = bf16[576,384]{1,0:T(8,128)(2,1)S(1)} collective-permute-done((bf16[576,384]{1,0:T(8,128)(2,1)S(1)}, bf16[576,384]{1,0:T(8,128)(2,1)S(1)}, u32[]{:S(2)}, u32[]{:S(2)}) %collective-permute-start.10) | collective-permute-done | bytes 442400 | tf_op jit(solution)/shard_map/ppermute | solution.py:227
  40.6 1.5 %collective-permute-start.14 = (f32[192,128]{1,0:T(8,128)S(1)}, f32[192,128]{1,0:T(8,128)S(1)}, u32[]{:S(2)}, u32[]{:S(2)}) collective-permute-start(f32[192,128]{1,0:T(8,128)S(1)} %get-tuple-element.19), channel_id=1, source_target_pairs={{0,16},{1,17},{2,18},{3,19},{4,20},{5,21},{6,22},{7,23},{8,24},{9,... | collective-permute-start | bytes 294920 | tf_op jit(solution)/shard_map/ppermute | solution.py:227
  42.1 3.4 %collective-permute-done.14.refs_1_ = f32[192,128]{1,0:T(8,128)S(1)} collective-permute-done((f32[192,128]{1,0:T(8,128)S(1)}, f32[192,128]{1,0:T(8,128)S(1)}, u32[]{:S(2)}, u32[]{:S(2)}) %collective-permute-start.14) | collective-permute-done | bytes 98336 | tf_op jit(solution)/shard_map/ppermute | solution.py:227
  45.5 1.0 %collective-permute-start.15 = (f32[96,128]{1,0:T(8,128)S(1)}, f32[96,128]{1,0:T(8,128)S(1)}, u32[]{:S(2)}, u32[]{:S(2)}) collective-permute-start(f32[96,128]{1,0:T(8,128)S(1)} %get-tuple-element.21), channel_id=1, source_target_pairs={{0,2},{1,3},{2,0},{3,1},{4,6},{5,7},{6,4},{7,5},{8,10},{9,11},{10,... | collective-permute-start | bytes 147464 | tf_op jit(solution)/shard_map/ppermute | solution.py:227
  47.2 3.4 %collective-permute-done.15.refs_1_ = f32[96,128]{1,0:T(8,128)S(1)} collective-permute-done((f32[96,128]{1,0:T(8,128)S(1)}, f32[96,128]{1,0:T(8,128)S(1)}, u32[]{:S(2)}, u32[]{:S(2)}) %collective-permute-start.15) | collective-permute-done | bytes 49184 | tf_op jit(solution)/shard_map/ppermute | solution.py:227
  50.6 1.6 %collective-permute-start.16 = (f32[96,128]{1,0:T(8,128)S(1)}, f32[96,128]{1,0:T(8,128)S(1)}, u32[]{:S(2)}, u32[]{:S(2)}) collective-permute-start(f32[96,128]{1,0:T(8,128)S(1)} %shard_map.74.refs_0_), channel_id=1, source_target_pairs={{0,1},{1,0},{2,3},{3,2},{4,5},{5,4},{6,7},{7,6},{8,9},{9,8},{10,11... | collective-permute-start | bytes 147464 | tf_op jit(solution)/shard_map/ppermute | solution.py:227
  52.7 2.9 %collective-permute-done.16.refs_1_ = f32[96,128]{1,0:T(8,128)S(1)} collective-permute-done((f32[96,128]{1,0:T(8,128)S(1)}, f32[96,128]{1,0:T(8,128)S(1)}, u32[]{:S(2)}, u32[]{:S(2)}) %collective-permute-start.16) | collective-permute-done | bytes 49184 | tf_op jit(solution)/shard_map/ppermute | solution.py:227
  55.6 1.8 %collective-permute-start.17 = (f32[96,128]{1,0:T(8,128)S(1)}, f32[96,128]{1,0:T(8,128)S(1)}, u32[]{:S(2)}, u32[]{:S(2)}) collective-permute-start(f32[96,128]{1,0:T(8,128)S(1)} %shard_map.75.refs_0_), channel_id=1, source_target_pairs={{0,2},{1,3},{2,0},{3,1},{4,6},{5,7},{6,4},{7,5},{8,10},{9,11},{10,... | collective-permute-start | bytes 147464 | tf_op jit(solution)/shard_map/ppermute | solution.py:227
  57.5 1.3 %collective-permute-done.12.refs_3_ = bf16[128,384]{1,0:T(8,128)(2,1)S(1)} collective-permute-done((bf16[128,384]{1,0:T(8,128)(2,1)S(1)}, bf16[128,384]{1,0:T(8,128)(2,1)S(1)}, u32[]{:S(2)}, u32[]{:S(2)}) %collective-permute-start.12) | collective-permute-done | bytes 98336 | tf_op jit(solution)/shard_map/ppermute | solution.py:282
  58.8 2.0 %collective-permute-done.17.refs_1_ = f32[96,128]{1,0:T(8,128)S(1)} collective-permute-done((f32[96,128]{1,0:T(8,128)S(1)}, f32[96,128]{1,0:T(8,128)S(1)}, u32[]{:S(2)}, u32[]{:S(2)}) %collective-permute-start.17) | collective-permute-done | bytes 49184 | tf_op jit(solution)/shard_map/ppermute | solution.py:227
  60.8 1.5 %collective-permute-start.18 = (f32[192,128]{1,0:T(8,128)S(1)}, f32[192,128]{1,0:T(8,128)S(1)}, u32[]{:S(2)}, u32[]{:S(2)}) collective-permute-start(f32[192,128]{1,0:T(8,128)S(1)} %shard_map.76.refs_0_), channel_id=1, source_target_pairs={{0,8},{1,9},{2,10},{3,11},{4,12},{5,13},{6,14},{7,15},{8,0},{9,1},... | collective-permute-start | bytes 294920 | tf_op jit(solution)/shard_map/ppermute | solution.py:227
  62.3 1.5 %collective-permute-start.19 = (f32[192,128]{1,0:T(8,128)S(1)}, f32[192,128]{1,0:T(8,128)S(1)}, u32[]{:S(2)}, u32[]{:S(2)}) collective-permute-start(f32[192,128]{1,0:T(8,128)S(1)} %shard_map.76.refs_0_), channel_id=1, source_target_pairs={{0,16},{1,17},{2,18},{3,19},{4,20},{5,21},{6,22},{7,23},{8,24},{9,... | collective-permute-start | bytes 294920 | tf_op jit(solution)/shard_map/ppermute | solution.py:227
  63.8 1.7 %collective-permute-done.18.refs_1_ = f32[192,128]{1,0:T(8,128)S(1)} collective-permute-done((f32[192,128]{1,0:T(8,128)S(1)}, f32[192,128]{1,0:T(8,128)S(1)}, u32[]{:S(2)}, u32[]{:S(2)}) %collective-permute-start.18) | collective-permute-done | bytes 98336 | tf_op jit(solution)/shard_map/ppermute | solution.py:227
  65.5 1.5 %collective-permute-start.20 = (f32[192,128]{1,0:T(8,128)S(1)}, f32[192,128]{1,0:T(8,128)S(1)}, u32[]{:S(2)}, u32[]{:S(2)}) collective-permute-start(f32[192,128]{1,0:T(8,128)S(1)} %collective-permute-done.18.refs_1_), channel_id=1, source_target_pairs={{0,16},{1,17},{2,18},{3,19},{4,20},{5,21},{6,22},{7,23},{8,24},{9,... | collective-permute-start | bytes 294920 | tf_op jit(solution)/shard_map/ppermute | solution.py:227
  67.0 1.5 %collective-permute-start.13 = (bf16[128,384]{1,0:T(8,128)(2,1)S(1)}, bf16[128,384]{1,0:T(8,128)(2,1)S(1)}, u32[]{:S(2)}, u32[]{:S(2)}) collective-permute-start(bf16[128,384]{1,0:T(8,128)(2,1)S(1)} %broadcast_select_fusion), channel_id=1, source_target_pairs={{0,8},{1,9},{2,10},{3,11},{4,12},{5,13},{6,14},{7,15},{8,0},{9,1},... | collective-permute-start | bytes 294920 | tf_op jit(solution)/shard_map/ppermute | solution.py:227
  69.0 1.1 %collective-permute-done.20.refs_3_ = f32[192,128]{1,0:T(8,128)S(1)} collective-permute-done((f32[192,128]{1,0:T(8,128)S(1)}, f32[192,128]{1,0:T(8,128)S(1)}, u32[]{:S(2)}, u32[]{:S(2)}) %collective-permute-start.20) | collective-permute-done | bytes 98336 | tf_op jit(solution)/shard_map/ppermute | solution.py:227
  70.1 1.6 %collective-permute-done.13 = bf16[128,384]{1,0:T(8,128)(2,1)S(1)} collective-permute-done((bf16[128,384]{1,0:T(8,128)(2,1)S(1)}, bf16[128,384]{1,0:T(8,128)(2,1)S(1)}, u32[]{:S(2)}, u32[]{:S(2)}) %collective-permute-start.13) | collective-permute-done | bytes 98336 | tf_op jit(solution)/shard_map/ppermute | solution.py:227
  71.7 1.5 %shard_map.72.refs_8_ = bf16[1,128,2,384]{3,2,1,0:T(2,128)(2,1)} custom-call(s32[2]{0:T(128)S(1)} %bitcast.7, bf16[128,384]{1,0:T(8,128)(2,1)S(1)} %get-tuple-element.23.refs_1_, bf16[128,384]{1,0:T(8,128)(2,1)S(1)} %get-tuple-element.22.refs_2_), custom_call_target="tpu_custom_call" | custom-call | tf_op jit(solution)/shard_map/pallas_call | solution.py:27
  74.1 1.2 %shard_map.77 = f32[2,384,384]{2,1,0:T(8,128)} custom-call(f32[192,128]{1,0:T(8,128)S(1)} %shard_map.76.refs_0_, f32[192,128]{1,0:T(8,128)S(1)} %collective-permute-done.18.refs_1_, f32[192,128]{1,0:T(8,128)S(1)} %collective-permute-done.19.refs_2_, f32[192,128]{1,0:T(8,128)S(1)} %collective-permute-done.20.refs_3_, ...), custom_call_target="tpu_custom_call" | custom-call | tf_op jit(solution)/shard_map/pallas_call | solution.py:27
  (43 shorter events, 6.9 us)
Async XLA Ops:
  0.6 0.9 %copy-start.2 = (bf16[1,128,2,384]{3,2,1,0:T(2,128)(2,1)S(1)}, bf16[1,128,2,384]{3,2,1,0:T(2,128)(2,1)}, u32[]{:S(2)}) copy-start(bf16[1,128,2,384]{3,2,1,0:T(2,128)(2,1)} %refs_1_.1) | copy-start | bytes 589828
  1.6 0.7 copy-start.3
  2.2 22.4 %copy-start.5 = (bf16[1,2,24,384]{3,2,1,0:T(8,128)(2,1)S(1)}, bf16[1,2,24,384]{3,2,1,0:T(8,128)(2,1)}, u32[]{:S(2)}) copy-start(bf16[1,2,24,384]{3,2,1,0:T(8,128)(2,1)} %param.8) | copy-start | bytes 110596
  3.5 1.0 %copy-start.1 = (bf16[1,512,512]{2,1,0:T(8,128)(2,1)S(1)}, bf16[1,512,512]{2,1,0:T(8,128)(2,1)}, u32[]{:S(2)}) copy-start(bf16[1,512,512]{2,1,0:T(8,128)(2,1)} %refs_0_.2) | copy-start | bytes 1572868
  4.8 31.4 %collective-permute-start = (bf16[512,512]{1,0:T(8,128)(2,1)S(1)}, bf16[512,512]{1,0:T(8,128)(2,1)S(1)}, u32[]{:S(2)}, u32[]{:S(2)}) collective-permute-start(bf16[512,512]{1,0:T(8,128)(2,1)S(1)} %shard_map.69.refs_0_), channel_id=1, source_target_pairs={{0,8},{1,9},{2,10},{3,11},{4,12},{5,13},{6,14},{7,15},{8,0},{9,1},... | collective-permute-start | bytes 1572872 | tf_op jit(solution)/shard_map/ppermute | solution.py:227
  7.8 14.0 %collective-permute-start.4 = (bf16[128,384]{1,0:T(8,128)(2,1)S(1)}, bf16[128,384]{1,0:T(8,128)(2,1)S(1)}, u32[]{:S(2)}, u32[]{:S(2)}) collective-permute-start(bf16[128,384]{1,0:T(8,128)(2,1)S(1)} %get-tuple-element.13), channel_id=1, source_target_pairs={{0,8},{1,9},{2,10},{3,11},{4,12},{5,13},{6,14},{7,15},{8,0},{9,1},... | collective-permute-start | bytes 294920 | tf_op jit(solution)/shard_map/ppermute | solution.py:227
  7.9 22.3 %collective-permute-start.1 = (bf16[128,384]{1,0:T(8,128)(2,1)S(1)}, bf16[128,384]{1,0:T(8,128)(2,1)S(1)}, u32[]{:S(2)}, u32[]{:S(2)}) collective-permute-start(bf16[128,384]{1,0:T(8,128)(2,1)S(1)} %get-tuple-element.12.refs_1_.refs_2_), channel_id=1, source_target_pairs={{0,2},{1,3},{2,0},{3,1},{4,6},{5,7},{6,4},{7,5},{8,10},{9,11},{10,... | collective-permute-start | bytes 294920 | tf_op jit(solution)/shard_map/ppermute | solution.py:227
  21.8 8.8 %collective-permute-start.5 = (bf16[128,384]{1,0:T(8,128)(2,1)S(1)}, bf16[128,384]{1,0:T(8,128)(2,1)S(1)}, u32[]{:S(2)}, u32[]{:S(2)}) collective-permute-start(bf16[128,384]{1,0:T(8,128)(2,1)S(1)} %collective-permute-done.4.refs_6_), channel_id=1, source_target_pairs={{0,2},{1,3},{2,0},{3,1},{4,6},{5,7},{6,4},{7,5},{8,10},{9,11},{10,... | collective-permute-start | bytes 294920 | tf_op jit(solution)/shard_map/ppermute | solution.py:227
  24.7 3.9 %collective-permute-start.8 = (bf16[32,384]{1,0:T(8,128)(2,1)S(1)}, bf16[32,384]{1,0:T(8,128)(2,1)S(1)}, u32[]{:S(2)}, u32[]{:S(2)}) collective-permute-start(bf16[32,384]{1,0:T(8,128)(2,1)S(1)} %get-tuple-element.24), channel_id=1, source_target_pairs={{0,8},{1,9},{2,10},{3,11},{4,12},{5,13},{6,14},{7,15},{8,0},{9,1},... | collective-permute-start | bytes 73736 | tf_op jit(solution)/shard_map/ppermute | solution.py:227
  26.2 5.9 %collective-permute-start.2 = (bf16[128,384]{1,0:T(8,128)(2,1)S(1)}, bf16[128,384]{1,0:T(8,128)(2,1)S(1)}, u32[]{:S(2)}, u32[]{:S(2)}) collective-permute-start(bf16[128,384]{1,0:T(8,128)(2,1)S(1)} %get-tuple-element.12.refs_1_.refs_2_), channel_id=1, source_target_pairs={{0,1},{1,0},{2,3},{3,2},{4,5},{5,4},{6,7},{7,6},{8,9},{9,8},{10,11... | collective-permute-start | bytes 294920 | tf_op jit(solution)/shard_map/ppermute | solution.py:227
  28.6 6.6 %collective-permute-start.6 = (bf16[128,384]{1,0:T(8,128)(2,1)S(1)}, bf16[128,384]{1,0:T(8,128)(2,1)S(1)}, u32[]{:S(2)}, u32[]{:S(2)}) collective-permute-start(bf16[128,384]{1,0:T(8,128)(2,1)S(1)} %collective-permute-done.4.refs_6_), channel_id=1, source_target_pairs={{0,1},{1,0},{2,3},{3,2},{4,5},{5,4},{6,7},{7,6},{8,9},{9,8},{10,11... | collective-permute-start | bytes 294920 | tf_op jit(solution)/shard_map/ppermute | solution.py:227
  30.1 5.0 %collective-permute-start.3 = (bf16[128,384]{1,0:T(8,128)(2,1)S(1)}, bf16[128,384]{1,0:T(8,128)(2,1)S(1)}, u32[]{:S(2)}, u32[]{:S(2)}) collective-permute-start(bf16[128,384]{1,0:T(8,128)(2,1)S(1)} %collective-permute-done.1.refs_3_), channel_id=1, source_target_pairs={{0,1},{1,0},{2,3},{3,2},{4,5},{5,4},{6,7},{7,6},{8,9},{9,8},{10,11... | collective-permute-start | bytes 294920 | tf_op jit(solution)/shard_map/ppermute | solution.py:227
  30.6 5.6 %collective-permute-start.7 = (bf16[128,384]{1,0:T(8,128)(2,1)S(1)}, bf16[128,384]{1,0:T(8,128)(2,1)S(1)}, u32[]{:S(2)}, u32[]{:S(2)}) collective-permute-start(bf16[128,384]{1,0:T(8,128)(2,1)S(1)} %collective-permute-done.5.refs_7_), channel_id=1, source_target_pairs={{0,1},{1,0},{2,3},{3,2},{4,5},{5,4},{6,7},{7,6},{8,9},{9,8},{10,11... | collective-permute-start | bytes 294920 | tf_op jit(solution)/shard_map/ppermute | solution.py:227
  37.0 3.0 %collective-permute-start.9 = (f32[512,384]{1,0:T(8,128)S(1)}, f32[512,384]{1,0:T(8,128)S(1)}, u32[]{:S(2)}, u32[]{:S(2)}) collective-permute-start(f32[512,384]{1,0:T(8,128)S(1)} %get-tuple-element.14.refs_1_), channel_id=1, source_target_pairs={{0,4},{1,5},{2,6},{3,7},{4,0},{5,1},{6,2},{7,3},{8,12},{9,13},{10,... | collective-permute-start | bytes 2359304 | tf_op jit(solution)/shard_map/ppermute | solution.py:227
  37.1 2.9 %collective-permute-start.10 = (bf16[576,384]{1,0:T(8,128)(2,1)S(1)}, bf16[576,384]{1,0:T(8,128)(2,1)S(1)}, u32[]{:S(2)}, u32[]{:S(2)}) collective-permute-start(bf16[576,384]{1,0:T(8,128)(2,1)S(1)} %get-tuple-element.15.refs_3_), channel_id=1, source_target_pairs={{0,4},{1,5},{2,6},{3,7},{4,0},{5,1},{6,2},{7,3},{8,12},{9,13},{10,... | collective-permute-start | bytes 1327112 | tf_op jit(solution)/shard_map/ppermute | solution.py:227
  40.6 31.1 %copy-start.4 = (s32[2,1]{0,1:T(1,128)S(1)}, s32[2,1]{0,1:T(1,128)}, u32[]{:S(2)}) copy-start(s32[2,1]{0,1:T(1,128)} %param.7) | copy-start | bytes 28
  40.6 4.9 %collective-permute-start.14 = (f32[192,128]{1,0:T(8,128)S(1)}, f32[192,128]{1,0:T(8,128)S(1)}, u32[]{:S(2)}, u32[]{:S(2)}) collective-permute-start(f32[192,128]{1,0:T(8,128)S(1)} %get-tuple-element.19), channel_id=1, source_target_pairs={{0,16},{1,17},{2,18},{3,19},{4,20},{5,21},{6,22},{7,23},{8,24},{9,... | collective-permute-start | bytes 294920 | tf_op jit(solution)/shard_map/ppermute | solution.py:227
  45.5 5.1 %collective-permute-start.15 = (f32[96,128]{1,0:T(8,128)S(1)}, f32[96,128]{1,0:T(8,128)S(1)}, u32[]{:S(2)}, u32[]{:S(2)}) collective-permute-start(f32[96,128]{1,0:T(8,128)S(1)} %get-tuple-element.21), channel_id=1, source_target_pairs={{0,2},{1,3},{2,0},{3,1},{4,6},{5,7},{6,4},{7,5},{8,10},{9,11},{10,... | collective-permute-start | bytes 147464 | tf_op jit(solution)/shard_map/ppermute | solution.py:227
  46.6 10.9 %collective-permute-start.11 = (bf16[128,384]{1,0:T(8,128)(2,1)S(1)}, bf16[128,384]{1,0:T(8,128)(2,1)S(1)}, u32[]{:S(2)}, u32[]{:S(2)}) collective-permute-start(bf16[128,384]{1,0:T(8,128)(2,1)S(1)} %get-tuple-element.16), channel_id=1, source_target_pairs={{0,0},{4,3},{1,5},{5,6},{6,2},{2,1},{7,7},{3,4},{8,8},{12,11},{9,1... | collective-permute-start | bytes 294920 | tf_op jit(solution)/shard_map/ppermute | solution.py:281
  50.6 5.0 %collective-permute-start.16 = (f32[96,128]{1,0:T(8,128)S(1)}, f32[96,128]{1,0:T(8,128)S(1)}, u32[]{:S(2)}, u32[]{:S(2)}) collective-permute-start(f32[96,128]{1,0:T(8,128)S(1)} %shard_map.74.refs_0_), channel_id=1, source_target_pairs={{0,1},{1,0},{2,3},{3,2},{4,5},{5,4},{6,7},{7,6},{8,9},{9,8},{10,11... | collective-permute-start | bytes 147464 | tf_op jit(solution)/shard_map/ppermute | solution.py:227
  52.2 6.6 %collective-permute-start.12 = (bf16[128,384]{1,0:T(8,128)(2,1)S(1)}, bf16[128,384]{1,0:T(8,128)(2,1)S(1)}, u32[]{:S(2)}, u32[]{:S(2)}) collective-permute-start(bf16[128,384]{1,0:T(8,128)(2,1)S(1)} %get-tuple-element.17), channel_id=1, source_target_pairs={{0,1},{4,2},{1,4},{5,7},{6,3},{2,0},{7,6},{3,5},{8,9},{12,10},{9,1... | collective-permute-start | bytes 294920 | tf_op jit(solution)/shard_map/ppermute | solution.py:282
  55.6 5.2 %collective-permute-start.17 = (f32[96,128]{1,0:T(8,128)S(1)}, f32[96,128]{1,0:T(8,128)S(1)}, u32[]{:S(2)}, u32[]{:S(2)}) collective-permute-start(f32[96,128]{1,0:T(8,128)S(1)} %shard_map.75.refs_0_), channel_id=1, source_target_pairs={{0,2},{1,3},{2,0},{3,1},{4,6},{5,7},{6,4},{7,5},{8,10},{9,11},{10,... | collective-permute-start | bytes 147464 | tf_op jit(solution)/shard_map/ppermute | solution.py:227
  60.8 4.7 %collective-permute-start.18 = (f32[192,128]{1,0:T(8,128)S(1)}, f32[192,128]{1,0:T(8,128)S(1)}, u32[]{:S(2)}, u32[]{:S(2)}) collective-permute-start(f32[192,128]{1,0:T(8,128)S(1)} %shard_map.76.refs_0_), channel_id=1, source_target_pairs={{0,8},{1,9},{2,10},{3,11},{4,12},{5,13},{6,14},{7,15},{8,0},{9,1},... | collective-permute-start | bytes 294920 | tf_op jit(solution)/shard_map/ppermute | solution.py:227
  62.3 6.7 %collective-permute-start.19 = (f32[192,128]{1,0:T(8,128)S(1)}, f32[192,128]{1,0:T(8,128)S(1)}, u32[]{:S(2)}, u32[]{:S(2)}) collective-permute-start(f32[192,128]{1,0:T(8,128)S(1)} %shard_map.76.refs_0_), channel_id=1, source_target_pairs={{0,16},{1,17},{2,18},{3,19},{4,20},{5,21},{6,22},{7,23},{8,24},{9,... | collective-permute-start | bytes 294920 | tf_op jit(solution)/shard_map/ppermute | solution.py:227
  65.5 4.6 %collective-permute-start.20 = (f32[192,128]{1,0:T(8,128)S(1)}, f32[192,128]{1,0:T(8,128)S(1)}, u32[]{:S(2)}, u32[]{:S(2)}) collective-permute-start(f32[192,128]{1,0:T(8,128)S(1)} %collective-permute-done.18.refs_1_), channel_id=1, source_target_pairs={{0,16},{1,17},{2,18},{3,19},{4,20},{5,21},{6,22},{7,23},{8,24},{9,... | collective-permute-start | bytes 294920 | tf_op jit(solution)/shard_map/ppermute | solution.py:227
  67.0 4.7 %collective-permute-start.13 = (bf16[128,384]{1,0:T(8,128)(2,1)S(1)}, bf16[128,384]{1,0:T(8,128)(2,1)S(1)}, u32[]{:S(2)}, u32[]{:S(2)}) collective-permute-start(bf16[128,384]{1,0:T(8,128)(2,1)S(1)} %broadcast_select_fusion), channel_id=1, source_target_pairs={{0,8},{1,9},{2,10},{3,11},{4,12},{5,13},{6,14},{7,15},{8,0},{9,1},... | collective-permute-start | bytes 294920 | tf_op jit(solution)/shard_map/ppermute | solution.py:227
  68.5 4.7 %collective-permute-start.21 = (f32[192,128]{1,0:T(8,128)S(1)}, f32[192,128]{1,0:T(8,128)S(1)}, u32[]{:S(2)}, u32[]{:S(2)}) collective-permute-start(f32[192,128]{1,0:T(8,128)S(1)} %shard_map.76.refs_0_), channel_id=1, source_target_pairs={{0,4},{1,5},{2,6},{3,7},{4,0},{5,1},{6,2},{7,3},{8,12},{9,13},{10,... | collective-permute-start | bytes 294920 | tf_op jit(solution)/shard_map/ppermute | solution.py:227
  68.5 4.7 %collective-permute-start.22 = (f32[192,128]{1,0:T(8,128)S(1)}, f32[192,128]{1,0:T(8,128)S(1)}, u32[]{:S(2)}, u32[]{:S(2)}) collective-permute-start(f32[192,128]{1,0:T(8,128)S(1)} %collective-permute-done.18.refs_1_), channel_id=1, source_target_pairs={{0,4},{1,5},{2,6},{3,7},{4,0},{5,1},{6,2},{7,3},{8,12},{9,13},{10,... | collective-permute-start | bytes 294920 | tf_op jit(solution)/shard_map/ppermute | solution.py:227
  69.0 4.2 %collective-permute-start.23 = (f32[192,128]{1,0:T(8,128)S(1)}, f32[192,128]{1,0:T(8,128)S(1)}, u32[]{:S(2)}, u32[]{:S(2)}) collective-permute-start(f32[192,128]{1,0:T(8,128)S(1)} %collective-permute-done.19.refs_2_), channel_id=1, source_target_pairs={{0,4},{1,5},{2,6},{3,7},{4,0},{5,1},{6,2},{7,3},{8,12},{9,13},{10,... | collective-permute-start | bytes 294920 | tf_op jit(solution)/shard_map/ppermute | solution.py:227
  70.1 3.1 %collective-permute-start.24 = (f32[192,128]{1,0:T(8,128)S(1)}, f32[192,128]{1,0:T(8,128)S(1)}, u32[]{:S(2)}, u32[]{:S(2)}) collective-permute-start(f32[192,128]{1,0:T(8,128)S(1)} %collective-permute-done.20.refs_3_), channel_id=1, source_target_pairs={{0,4},{1,5},{2,6},{3,7},{4,0},{5,1},{6,2},{7,3},{8,12},{9,13},{10,... | collective-permute-start | bytes 294920 | tf_op jit(solution)/shard_map/ppermute | solution.py:227
  73.2 0.9 %copy-start = (bf16[1,128,2,384]{3,2,1,0:T(2,128)(2,1)S(1)}, bf16[1,128,2,384]{3,2,1,0:T(2,128)(2,1)}, u32[]{:S(2)}) copy-start(bf16[1,128,2,384]{3,2,1,0:T(2,128)(2,1)} %shard_map.72.refs_8_) | copy-start | bytes 589828

commit v5 on v4

--- a/solution.py
+++ b/solution.py
@@ -12,6 +12,7 @@
 VMEM = pl.BlockSpec(memory_space=pltpu.VMEM)
 SMEM = pl.BlockSpec(memory_space=pltpu.SMEM)
 ANY = pl.BlockSpec(memory_space=pl.ANY)
+HBM = pl.BlockSpec(memory_space=pltpu.HBM)
 AXES = ("hyp", "side", "core", "pcol")
 
 
@@ -79,42 +80,57 @@
     return sigma_panel, marginal
 
 
-def mask_kernel(live_hbm, panel_hbm, own, give, live, panel, sems):
+def start_kernel(*refs):
+    sources, (own, give, own_inverse, low, high), buffers, sems = refs[:4], refs[4:9], refs[9:13], refs[13]
     copies = [
-        pltpu.make_async_copy(panel_hbm.at[0], panel, sems.at[0]),
-        pltpu.make_async_copy(live_hbm, live, sems.at[1]),
+        pltpu.make_async_copy(source, buffer, sems.at[index])
+        for index, (source, buffer) in enumerate(zip(sources, buffers))
     ]
     for copy in copies:
         copy.start()
-    for copy in copies:
+    for copy in copies[:3]:
         copy.wait()
+    live, panel, inverse, matrix = buffers
     first = lax.axis_index("side") == 0
     row = lax.broadcasted_iota(jnp.int32, own.shape, 0)
-    rows = panel[...]
+    rows = panel[0]
     zero = jnp.zeros(own.shape, own.dtype)
     one, two = (jnp.where(row < live[s], rows[:, s, :], zero) for s in range(2))
+    height = own.shape[0]
     own[...] = jnp.where(first, one, two)
-    give[...] = jnp.where(first, two, one)
-
-
-def flip_kernel(matrix, out):
-    out[...] = matrix[0].T
-
-
-def apply_kernel(own_sigma, far_sigma, *refs):
-    blocks, (own_inverse, got_inverse, applied, pack, panel) = refs[:8], refs[8:]
+    give[:height] = jnp.where(first, two, one)
+    spare = jnp.zeros((own_inverse.shape[0] - inverse.shape[2], own.shape[1]), own.dtype)
+    one, two = (jnp.concatenate([inverse[0, s], spare], 0) for s in range(2))
+    own_inverse[...] = jnp.where(first, one, two)
+    give[height:] = jnp.where(first, two, one)
+    copies[3].wait()
+    half = matrix.shape[1] // 2
+    low[...] = matrix[0, :half].T
+    high[...] = matrix[0, half:].T
+
+
+def gather_kernel(*refs):
+    blocks, (own_inverse, got_inverse, rows, pack) = refs[:8], refs[8:]
     column = lax.axis_index("pcol")
     height = blocks[0].shape[0]
     for index, block in enumerate(blocks):
         spot = jnp.bitwise_xor(column, (0, 2, 1, 3)[index % 4])
-        panel[index // 4, pl.ds(pl.multiple_of(spot * height, height), height), :] = block[...]
-    applied[...] = jnp.dot(own_sigma[...], panel[0], preferred_element_type=jnp.float32)
-    applied[...] += jnp.dot(far_sigma[...], panel[1], preferred_element_type=jnp.float32)
-    extent = panel.shape[1]
+        rows[index // 4, pl.ds(pl.multiple_of(spot * height, height), height), :] = block[...]
+    extent = rows.shape[1]
     size = own_inverse.shape[0]
-    pack[:extent] = panel[jnp.where(column // 2 == lax.axis_index("side"), 0, 1)]
+    pack[:extent] = rows[jnp.where(column // 2 == lax.axis_index("side"), 0, 1)]
     pack[extent : extent + size] = own_inverse[...]
     pack[extent + size :] = got_inverse[...]
+
+
+def apply_kernel(rows, *refs):
+    parts, applied = refs[:4], refs[4]
+    half = rows.shape[1] // 2
+    total = 0
+    for index, part in enumerate(parts):
+        lines = rows[index // 2, index % 2 * half : (index % 2 + 1) * half, :]
+        total += jnp.dot(part[...], lines, preferred_element_type=jnp.float32)
+    applied[...] = total
 
 
 def couple_kernel(weight, mine, other, pack, got_pack, out_a, out_b, keep, send, half, packed):
@@ -158,39 +174,24 @@
         out[...] = half[pl.ds(pl.multiple_of(spot * height, height), height), :]
 
 
-def halve_kernel(mine, came, keep, send, whole):
-    whole[...] = mine[...] + came[...]
-    size = keep.shape[0]
-    bit = lax.axis_index("pcol") // 2
-    keep[...] = whole[pl.ds(pl.multiple_of(bit * size, 8), size), :]
-    send[...] = whole[pl.ds(pl.multiple_of((1 - bit) * size, 8), size), :]
-
-
 def add_kernel(mine, came, out):
     out[...] = mine[...] + came[...]
 
 
-def join_kernel(mine, came, out):
-    size = mine.shape[0]
-    bit = lax.axis_index("pcol") // 2
-    out[pl.ds(pl.multiple_of(bit * size, 8), size), :] = mine[...]
-    out[pl.ds(pl.multiple_of((1 - bit) * size, 8), size), :] = came[...]
-
-
-def spread_kernel(*refs):
-    parts, (out, lines, result, sems) = refs[:8], refs[8:]
+def finish_kernel(*refs):
+    parts, (live_hbm, mine, theirs, rows_out, out, live, block, lines, result, sems) = refs[:8], refs[8:]
     point, side, core = (lax.axis_index(name) for name in ("hyp", "side", "core"))
+    copy = pltpu.make_async_copy(live_hbm, live, sems.at[0])
+    copy.start()
     width = result.shape[1]
     blocks = tiles(width)
-    per = len(blocks) // 2
     size = parts[0].shape[0]
-    for other_core in range(2):
-        for index in range(4):
-            part = jnp.where(other_core, 1 - core, core)
-            node = jnp.where(index % 2, 1 - side, side)
-            slot = jnp.where(index // 2, 1 - point, point)
-            start = pl.multiple_of((part * 2 + slot) * size, 8)
-            lines[node, pl.ds(start, size), :] = parts[4 * other_core + index][...]
+    for index, part in enumerate(parts):
+        owner = core if index < 4 else 1 - core
+        node = 1 - side if index % 2 else side
+        slot = 1 - point if index // 2 % 2 else point
+        start = pl.multiple_of((owner * 2 + slot) * size, 8)
+        lines[node, pl.ds(start, size), :] = part[...]
     copies = []
     for node in range(2):
         for index, (a, b) in enumerate(blocks):
@@ -198,16 +199,18 @@
             result[node, a * LANES : (a + 1) * LANES, b * LANES : (b + 1) * LANES] = tile
             if a != b:
                 result[node, b * LANES : (b + 1) * LANES, a * LANES : (a + 1) * LANES] = tile.T
-        copies.append(pltpu.make_async_copy(result.at[node], out.at[node], sems.at[node]))
+        copies.append(pltpu.make_async_copy(result.at[node], out.at[node], sems.at[1 + node]))
         copies[-1].start()
+    copy.wait()
+    row = lax.broadcasted_iota(jnp.int32, mine.shape, 0)
+    first = side == 0
+    pair = (jnp.where(first, mine[...], theirs[...]), jnp.where(first, theirs[...], mine[...]))
+    for s, value in enumerate(pair):
+        block[:, s, :] = jnp.where(row < live[s], value, jnp.zeros(value.shape, value.dtype))
+    copies.append(pltpu.make_async_copy(block, rows_out.at[0], sems.at[3]))
+    copies[-1].start()
     for copy in copies:
         copy.wait()
-
-
-def finish_kernel(live, a, b, out):
-    row = lax.broadcasted_iota(jnp.int32, a.shape, 0)
-    for s, block in enumerate((a, b)):
-        out[0, :, s, :] = jnp.where(row < live[s], block[...], jnp.zeros(a.shape, a.dtype))
 
 
 def square(sigma_rows, panel, live_block_rows, inv_diag, quad_weight):
@@ -218,55 +221,53 @@
     f32, bf16 = jnp.float32, jnp.bfloat16
     shape = jax.ShapeDtypeStruct
     dma = pltpu.SemaphoreType.DMA
-    total = points * 2 * 2 * grid
+    stay = functools.partial(pltpu.with_memory_space_constraint, memory_space=pltpu.HBM)
+    devices = points * 2 * 2 * grid
     live = live_block_rows[:, 0]
-    pick = functools.partial(lax.dynamic_index_in_dim, axis=0, keepdims=False)
 
     def swap(x, point=0, side=0, core=0, column=0):
         mask = ((point * 2 + side) * 2 + core) * grid + column
-        return lax.ppermute(x, AXES, [(i, i ^ mask) for i in range(total)])
-
+        return lax.ppermute(x, AXES, [(i, i ^ mask) for i in range(devices)])
+
+    extent = sigma_rows.shape[2]
     block = shape((height, width), bf16)
-    own, give = call(
-        mask_kernel, [block, block], [ANY, ANY], live, panel,
-        scratch=[pltpu.SMEM((2,), jnp.int32), pltpu.VMEM((height, count, width), bf16), dma((2,))],
+    part = shape((extent, extent // 2), bf16)
+    size = pl.cdiv(inv_diag.shape[2], ROWS) * ROWS
+    own, give, own_inverse, low, high = call(
+        start_kernel,
+        [block, shape((height + size, width), bf16), shape((size, width), bf16), part, part],
+        [HBM] * 4,
+        *map(stay, (live, panel, inv_diag, sigma_rows)),
+        scratch=[pltpu.SMEM(live.shape, jnp.int32)]
+        + [pltpu.VMEM(x.shape, bf16) for x in (panel, inv_diag, sigma_rows)]
+        + [dma((4,))],
     )
     got = swap(give, side=1)
+    got, got_inverse = got[:height], got[height:]
+    far_low, far_high = swap(low, side=1), swap(high, side=1)
     blocks = []
     for start in (own, got):
         second = swap(start, column=2)
         blocks += [start, second, swap(start, column=1), swap(second, column=1)]
-
-    extent = sigma_rows.shape[2]
-    sigma = call(flip_kernel, shape((extent, extent), bf16), [VMEM], sigma_rows, after=[own])
-    far_sigma = swap(sigma, side=1)
-    inverse = jnp.pad(inv_diag[0], ((0, 0), (0, -inv_diag.shape[2] % ROWS), (0, 0)))
-    got_inverse = swap(pick(inverse, 1 - side), side=1)
-
-    product = shape((extent, width), f32)
-    pack = shape((extent + 2 * inverse.shape[1], width), bf16)
-    mine, pack = call(
-        apply_kernel, [product, pack], [VMEM] * 12,
-        sigma, far_sigma, *blocks, pick(inverse, side), got_inverse,
-        scratch=[pltpu.VMEM((2, extent, width), bf16)],
+    pack = shape((extent + 2 * size, width), bf16)
+    rows, pack = call(
+        gather_kernel, [shape((2, extent, width), bf16), pack], [VMEM] * 10,
+        *blocks, own_inverse, got_inverse,
+    )
+    got_pack = swap(pack, core=1)
+    mine = call(
+        apply_kernel, shape((extent, width), f32), [VMEM] * 5, rows, low, high, far_low, far_high
     )
     other = swap(mine, core=1)
-    got_pack = swap(pack, core=1)
 
     lines = len(tiles(width)) // 2 * LANES
-
-    def part(count):
-        return shape((count, LANES), f32)
-
+    part = shape((lines // 2, LANES), f32)
     out_a, out_b, keep, send = call(
-        couple_kernel, [block, block, part(lines // 2), part(lines // 2)], [SMEM] + [VMEM] * 4,
+        couple_kernel, [block, block, part, part], [SMEM] + [VMEM] * 4,
         quad_weight, mine, other, pack, got_pack,
         scratch=[pltpu.VMEM((extent, width), bf16), pltpu.VMEM((lines, LANES), f32)],
     )
-    keep, send = call(
-        halve_kernel, [part(lines // 4)] * 2, [VMEM] * 2, keep, swap(send, point=1),
-        scratch=[pltpu.VMEM((lines // 2, LANES), f32)],
-    )
+    came = swap(send, point=1)
 
     def output_pairs(steps):
         pairs = []
@@ -282,36 +283,28 @@
     land_b = lax.ppermute(out_b, AXES, output_pairs((1, 2)))
     from_a = jnp.where(column % 2 == core, column, column ^ 3) // 2
 
-    sum_two = call(add_kernel, part(lines // 4), [VMEM] * 2, keep, swap(send, column=2))
-    sum_all = call(add_kernel, part(lines // 4), [VMEM] * 2, sum_two, swap(sum_two, column=1))
-    here = call(
-        join_kernel, part(lines // 2), [VMEM] * 2, sum_all, swap(sum_all, column=2),
-        after=[land_a, land_b],
-    )
-    across = swap(here, side=1)
-    there = swap(here, point=1)
-    both = swap(across, point=1)
-    quarters = [here, across, there, both]
+    add = functools.partial(call, add_kernel, part, [VMEM] * 2)
+    total = add(keep, came)
+    total = add(total, swap(total, column=2))
+    total = add(total, swap(total, column=1), after=[land_a, land_b])
+    quarters = [total, swap(total, side=1), swap(total, point=1), swap(total, side=1, point=1)]
     quarters += [swap(x, core=1) for x in quarters]
-
     theirs = swap(jnp.where(from_a == side, land_b, land_a), side=1)
     mine = jnp.where(from_a == side, land_a, land_b)
-    first = jnp.where(side == 0, mine, theirs)
-    last = jnp.where(side == 0, theirs, mine)
-    sigma_panel = call(
-        finish_kernel, shape((1, height, count, width), bf16), [SMEM, VMEM, VMEM], live, first, last
-    )
-    marginal = call(
-        spread_kernel, shape((count, width, width), f32), [VMEM] * 8, *quarters,
+    return call(
+        finish_kernel,
+        [shape((1, height, count, width), bf16), shape((count, width, width), f32)],
+        [VMEM] * 8 + [HBM] + [VMEM] * 2,
+        *quarters, live, mine, theirs,
         scratch=[
+            pltpu.SMEM((2,), jnp.int32),
+            pltpu.VMEM((height, count, width), bf16),
             pltpu.VMEM((count, 2 * lines, LANES), f32),
             pltpu.VMEM((count, width, width), f32),
-            dma((2,)),
+            dma((4,)),
         ],
-        out_specs=ANY,
-        after=[sigma_panel],
-    )
-    return sigma_panel, marginal
+        out_specs=[HBM, HBM],
+    )
 
 
 def solution(mesh):

time: 75.6 us -> 58.4 us (0.77)
  waiting for transfers between devices: 34.7 us -> 20.8 us
  local copies, waits for them, and re-layouts: 3.55 us -> 0.02 us
  starting transfers between devices: 29.9 us -> 31.3 us
  Pallas kernels: 5.68 us -> 4.72 us
    ppermute x23 -> x22, waiting for transfers between devices: 33.4 us -> 17.4 us  [swap(): return lax.ppermute(x, AXES, [(i, i ^ mask) for i in range(devices)])]
    unnamed x12 -> x2, local copies, waits for them, and re-layouts: 3.54 us -> 0.01 us
    ppermute x1, starting transfers between devices: 0.51 us -> 2.65 us  [square(): land_b = lax.ppermute(out_b, AXES, output_pairs((1, 2)))]
    ppermute x1, waiting for transfers between devices: 1.3 us -> 3.4 us  [square(): land_b = lax.ppermute(out_b, AXES, output_pairs((1, 2)))]
    pallas_call x10 -> x8, Pallas kernels: 5.68 us -> 4.72 us  [call(): pl.pallas_call(body, out_shape=outs, in_specs=list(specs) + [ANY] * len(a...]
    ppermute x23 -> x22, starting transfers between devices: 28.8 us -> 28 us  [swap(): return lax.ppermute(x, AXES, [(i, i ^ mask) for i in range(devices)])]
  transfers between devices with their start and end apart: 25 -> 24, of which waited for: 13 -> 14; matrix products, arithmetic and copies ran while one was open for 0% -> 0% of each run, Pallas kernels for 2% -> 0%
where the time goes in v5:
time: 58.4 us; the launch traced here: 58.3 us
  starting transfers between devices  31.3 us (54%)
  waiting for transfers between devices  20.8 us (36%)
  Pallas kernels  4.72 us (8%)
  between operations  1.39 us (2%)
    ppermute x22, starting transfers between devices, swap(): return lax.ppermute(x, AXES, [(i, i ^ mask) for i in range(devices)])  28 us
    ppermute x22, waiting for transfers between devices, swap(): return lax.ppermute(x, AXES, [(i, i ^ mask) for i in range(devices)])  17.4 us
    pallas_call x8, Pallas kernels, call(): pl.pallas_call(body, out_shape=outs, in_specs=list(specs) + [ANY] * len(a...  4.72 us
    ppermute x1, waiting for transfers between devices, square(): land_b = lax.ppermute(out_b, AXES, output_pairs((1, 2)))  3.4 us
    ppermute x1, starting transfers between devices, square(): land_b = lax.ppermute(out_b, AXES, output_pairs((1, 2)))  2.65 us
  transfers between devices with their start and end apart: 24, of which 14 were waited for; matrix products, arithmetic and copies ran while one was open for 0% of the time, Pallas kernels for 0%

profile of v5, /device:TPU:0, one launch (start us, length us, event | category | flops | bytes accessed | tf_op | source)
XLA Modules:
  0.0 58.3 jit_solution(5026631678162828724)
XLA Ops:
  0.6 1.7 %shard_map.68 = (bf16[128,384]{1,0:T(8,128)(2,1)S(1)}, bf16[160,384]{1,0:T(8,128)(2,1)S(1)}, bf16[32,384]{1,0:T(8,128)(2,1)S(1)}, bf16[512,256]{1,0:T(8,128)(2,1)S(1)}, bf16[512,256]{1,0:T(8,128)(2,1)S(1)}) custom-call(s32[2]{0:T(128)} %bitcast.1, bf16[1,128,2,384]{3,2,1,0:T(2,128)(2,1)} %refs_1_.1, bf16[1,2,24,384]{3,2,1,0:T(8,128)(2,1)} %refs_2_.1, ...), custom_call_target="tpu_custom_call" | custom-call | tf_op jit(solution)/shard_map/pallas_call | solution.py:28
  2.3 3.0 %collective-permute-start.3 = (bf16[160,384]{1,0:T(8,128)(2,1)S(1)}, bf16[160,384]{1,0:T(8,128)(2,1)S(1)}, u32[]{:S(2)}, u32[]{:S(2)}) collective-permute-start(bf16[160,384]{1,0:T(8,128)(2,1)S(1)} %get-tuple-element.14), channel_id=1, source_target_pairs={{0,8},{1,9},{2,10},{3,11},{4,12},{5,13},{6,14},{7,15},{8,0},{9,1},... | collective-permute-start | bytes 368648 | tf_op jit(solution)/shard_map/ppermute | solution.py:230
  5.4 1.9 %collective-permute-start.8 = (bf16[512,256]{1,0:T(8,128)(2,1)S(1)}, bf16[512,256]{1,0:T(8,128)(2,1)S(1)}, u32[]{:S(2)}, u32[]{:S(2)}) collective-permute-start(bf16[512,256]{1,0:T(8,128)(2,1)S(1)} %get-tuple-element.18.refs_2_), channel_id=1, source_target_pairs={{0,8},{1,9},{2,10},{3,11},{4,12},{5,13},{6,14},{7,15},{8,0},{9,1},... | collective-permute-start | bytes 786440 | tf_op jit(solution)/shard_map/ppermute | solution.py:230
  7.4 2.6 %collective-permute-start = (bf16[128,384]{1,0:T(8,128)(2,1)S(1)}, bf16[128,384]{1,0:T(8,128)(2,1)S(1)}, u32[]{:S(2)}, u32[]{:S(2)}) collective-permute-start(bf16[128,384]{1,0:T(8,128)(2,1)S(1)} %get-tuple-element.13.refs_0_), channel_id=1, source_target_pairs={{0,2},{1,3},{2,0},{3,1},{4,6},{5,7},{6,4},{7,5},{8,10},{9,11},{10,... | collective-permute-start | bytes 294920 | tf_op jit(solution)/shard_map/ppermute | solution.py:230
  10.0 1.6 %collective-permute-start.1 = (bf16[128,384]{1,0:T(8,128)(2,1)S(1)}, bf16[128,384]{1,0:T(8,128)(2,1)S(1)}, u32[]{:S(2)}, u32[]{:S(2)}) collective-permute-start(bf16[128,384]{1,0:T(8,128)(2,1)S(1)} %get-tuple-element.13.refs_0_), channel_id=1, source_target_pairs={{0,1},{1,0},{2,3},{3,2},{4,5},{5,4},{6,7},{7,6},{8,9},{9,8},{10,11... | collective-permute-start | bytes 294920 | tf_op jit(solution)/shard_map/ppermute | solution.py:230
  11.6 1.2 %collective-permute-start.4 = (bf16[128,384]{1,0:T(8,128)(2,1)S(1)}, bf16[128,384]{1,0:T(8,128)(2,1)S(1)}, u32[]{:S(2)}, u32[]{:S(2)}) collective-permute-start(bf16[128,384]{1,0:T(8,128)(2,1)S(1)} %slice.8.refs_4_), channel_id=1, source_target_pairs={{0,2},{1,3},{2,0},{3,1},{4,6},{5,7},{6,4},{7,5},{8,10},{9,11},{10,... | collective-permute-start | bytes 294920 | tf_op jit(solution)/shard_map/ppermute | solution.py:230
  13.1 3.8 %collective-permute-start.2 = (bf16[128,384]{1,0:T(8,128)(2,1)S(1)}, bf16[128,384]{1,0:T(8,128)(2,1)S(1)}, u32[]{:S(2)}, u32[]{:S(2)}) collective-permute-start(bf16[128,384]{1,0:T(8,128)(2,1)S(1)} %collective-permute-done.refs_1_), channel_id=1, source_target_pairs={{0,1},{1,0},{2,3},{3,2},{4,5},{5,4},{6,7},{7,6},{8,9},{9,8},{10,11... | collective-permute-start | bytes 294920 | tf_op jit(solution)/shard_map/ppermute | solution.py:230
  17.0 0.7 %collective-permute-start.5 = (bf16[128,384]{1,0:T(8,128)(2,1)S(1)}, bf16[128,384]{1,0:T(8,128)(2,1)S(1)}, u32[]{:S(2)}, u32[]{:S(2)}) collective-permute-start(bf16[128,384]{1,0:T(8,128)(2,1)S(1)} %slice.8.refs_4_), channel_id=1, source_target_pairs={{0,1},{1,0},{2,3},{3,2},{4,5},{5,4},{6,7},{7,6},{8,9},{9,8},{10,11... | collective-permute-start | bytes 294920 | tf_op jit(solution)/shard_map/ppermute | solution.py:230
  17.7 0.6 %collective-permute-done.4.refs_5_ = bf16[128,384]{1,0:T(8,128)(2,1)S(1)} collective-permute-done((bf16[128,384]{1,0:T(8,128)(2,1)S(1)}, bf16[128,384]{1,0:T(8,128)(2,1)S(1)}, u32[]{:S(2)}, u32[]{:S(2)}) %collective-permute-start.4) | collective-permute-done | bytes 98336 | tf_op jit(solution)/shard_map/ppermute | solution.py:230
  18.3 0.7 %collective-permute-start.6 = (bf16[128,384]{1,0:T(8,128)(2,1)S(1)}, bf16[128,384]{1,0:T(8,128)(2,1)S(1)}, u32[]{:S(2)}, u32[]{:S(2)}) collective-permute-start(bf16[128,384]{1,0:T(8,128)(2,1)S(1)} %collective-permute-done.4.refs_5_), channel_id=1, source_target_pairs={{0,1},{1,0},{2,3},{3,2},{4,5},{5,4},{6,7},{7,6},{8,9},{9,8},{10,11... | collective-permute-start | bytes 294920 | tf_op jit(solution)/shard_map/ppermute | solution.py:230
  19.0 1.6 %collective-permute-done.2.refs_3_ = bf16[128,384]{1,0:T(8,128)(2,1)S(1)} collective-permute-done((bf16[128,384]{1,0:T(8,128)(2,1)S(1)}, bf16[128,384]{1,0:T(8,128)(2,1)S(1)}, u32[]{:S(2)}, u32[]{:S(2)}) %collective-permute-start.2) | collective-permute-done | bytes 98336 | tf_op jit(solution)/shard_map/ppermute | solution.py:230
  20.7 1.3 %collective-permute-done.5.refs_6_ = bf16[128,384]{1,0:T(8,128)(2,1)S(1)} collective-permute-done((bf16[128,384]{1,0:T(8,128)(2,1)S(1)}, bf16[128,384]{1,0:T(8,128)(2,1)S(1)}, u32[]{:S(2)}, u32[]{:S(2)}) %collective-permute-start.5) | collective-permute-done | bytes 98336 | tf_op jit(solution)/shard_map/ppermute | solution.py:230
  22.0 1.1 %collective-permute-done.6.refs_7_ = bf16[128,384]{1,0:T(8,128)(2,1)S(1)} collective-permute-done((bf16[128,384]{1,0:T(8,128)(2,1)S(1)}, bf16[128,384]{1,0:T(8,128)(2,1)S(1)}, u32[]{:S(2)}, u32[]{:S(2)}) %collective-permute-start.6) | collective-permute-done | bytes 98336 | tf_op jit(solution)/shard_map/ppermute | solution.py:230
  23.1 0.7 %shard_map.70.refs_1_ = f32[512,384]{1,0:T(8,128)S(1)} custom-call(bf16[2,512,384]{2,1,0:T(8,128)(2,1)S(1)} %get-tuple-element.16.refs_0_, bf16[512,256]{1,0:T(8,128)(2,1)S(1)} %get-tuple-element.17.refs_1_, bf16[512,256]{1,0:T(8,128)(2,1)S(1)} %get-tuple-element.18.refs_2_, bf16[512,256]{1,0:T(8,128)(2,1)S(1)} %collective-permute-done.7.refs_3_, ...), custom_call_target="tpu_custom_call" | custom-call | tf_op jit(solution)/shard_map/pallas_call | solution.py:28
  25.1 1.8 %collective-permute-done.10.refs_4_ = bf16[576,384]{1,0:T(8,128)(2,1)S(1)} collective-permute-done((bf16[576,384]{1,0:T(8,128)(2,1)S(1)}, bf16[576,384]{1,0:T(8,128)(2,1)S(1)}, u32[]{:S(2)}, u32[]{:S(2)}) %collective-permute-start.10) | collective-permute-done | bytes 442400 | tf_op jit(solution)/shard_map/ppermute | solution.py:230
  26.8 0.6 %shard_map.71 = (bf16[128,384]{1,0:T(8,128)(2,1)S(1)}, bf16[128,384]{1,0:T(8,128)(2,1)S(1)}, f32[192,128]{1,0:T(8,128)S(1)}, f32[192,128]{1,0:T(8,128)S(1)}) custom-call(f32[1]{0:T(128)S(6)} %copy.7.refs_0_, f32[512,384]{1,0:T(8,128)S(1)} %shard_map.70.refs_1_, f32[512,384]{1,0:T(8,128)S(1)} %collective-permute-done.9.refs_2_, ...), custom_call_target="tpu_custom_call" | custom-call | tf_op jit(solution)/shard_map/pallas_call | solution.py:28
  27.5 1.6 %collective-permute-start.11 = (f32[192,128]{1,0:T(8,128)S(1)}, f32[192,128]{1,0:T(8,128)S(1)}, u32[]{:S(2)}, u32[]{:S(2)}) collective-permute-start(f32[192,128]{1,0:T(8,128)S(1)} %get-tuple-element.21), channel_id=1, source_target_pairs={{0,16},{1,17},{2,18},{3,19},{4,20},{5,21},{6,22},{7,23},{8,24},{9,... | collective-permute-start | bytes 294920 | tf_op jit(solution)/shard_map/ppermute | solution.py:230
  29.1 3.3 %collective-permute-done.11.refs_1_ = f32[192,128]{1,0:T(8,128)S(1)} collective-permute-done((f32[192,128]{1,0:T(8,128)S(1)}, f32[192,128]{1,0:T(8,128)S(1)}, u32[]{:S(2)}, u32[]{:S(2)}) %collective-permute-start.11) | collective-permute-done | bytes 98336 | tf_op jit(solution)/shard_map/ppermute | solution.py:230
  32.4 3.2 %collective-permute-start.12 = (f32[192,128]{1,0:T(8,128)S(1)}, f32[192,128]{1,0:T(8,128)S(1)}, u32[]{:S(2)}, u32[]{:S(2)}) collective-permute-start(f32[192,128]{1,0:T(8,128)S(1)} %shard_map.72.refs_0_), channel_id=1, source_target_pairs={{0,2},{1,3},{2,0},{3,1},{4,6},{5,7},{6,4},{7,5},{8,10},{9,11},{10,... | collective-permute-start | bytes 294920 | tf_op jit(solution)/shard_map/ppermute | solution.py:230
  35.6 0.7 %collective-permute-start.14 = (bf16[128,384]{1,0:T(8,128)(2,1)S(1)}, bf16[128,384]{1,0:T(8,128)(2,1)S(1)}, u32[]{:S(2)}, u32[]{:S(2)}) collective-permute-start(bf16[128,384]{1,0:T(8,128)(2,1)S(1)} %get-tuple-element.22), channel_id=1, source_target_pairs={{0,0},{4,3},{1,5},{5,6},{6,2},{2,1},{7,7},{3,4},{8,8},{12,11},{9,1... | collective-permute-start | bytes 294920 | tf_op jit(solution)/shard_map/ppermute | solution.py:282
  36.3 2.6 %collective-permute-start.15 = (bf16[128,384]{1,0:T(8,128)(2,1)S(1)}, bf16[128,384]{1,0:T(8,128)(2,1)S(1)}, u32[]{:S(2)}, u32[]{:S(2)}) collective-permute-start(bf16[128,384]{1,0:T(8,128)(2,1)S(1)} %get-tuple-element.23), channel_id=1, source_target_pairs={{0,1},{4,2},{1,4},{5,7},{6,3},{2,0},{7,6},{3,5},{8,9},{12,10},{9,1... | collective-permute-start | bytes 294920 | tf_op jit(solution)/shard_map/ppermute | solution.py:283
  38.9 1.0 %collective-permute-done.12.refs_1_ = f32[192,128]{1,0:T(8,128)S(1)} collective-permute-done((f32[192,128]{1,0:T(8,128)S(1)}, f32[192,128]{1,0:T(8,128)S(1)}, u32[]{:S(2)}, u32[]{:S(2)}) %collective-permute-start.12) | collective-permute-done | bytes 98336 | tf_op jit(solution)/shard_map/ppermute | solution.py:230
  40.0 2.4 %collective-permute-start.13 = (f32[192,128]{1,0:T(8,128)S(1)}, f32[192,128]{1,0:T(8,128)S(1)}, u32[]{:S(2)}, u32[]{:S(2)}) collective-permute-start(f32[192,128]{1,0:T(8,128)S(1)} %shard_map.73.refs_0_), channel_id=1, source_target_pairs={{0,1},{1,0},{2,3},{3,2},{4,5},{5,4},{6,7},{7,6},{8,9},{9,8},{10,11... | collective-permute-start | bytes 294920 | tf_op jit(solution)/shard_map/ppermute | solution.py:230
  42.4 3.4 %collective-permute-done.15.refs_3_ = bf16[128,384]{1,0:T(8,128)(2,1)S(1)} collective-permute-done((bf16[128,384]{1,0:T(8,128)(2,1)S(1)}, bf16[128,384]{1,0:T(8,128)(2,1)S(1)}, u32[]{:S(2)}, u32[]{:S(2)}) %collective-permute-start.15) | collective-permute-done | bytes 98336 | tf_op jit(solution)/shard_map/ppermute | solution.py:283
  45.8 0.9 %collective-permute-done.13.refs_1_ = f32[192,128]{1,0:T(8,128)S(1)} collective-permute-done((f32[192,128]{1,0:T(8,128)S(1)}, f32[192,128]{1,0:T(8,128)S(1)}, u32[]{:S(2)}, u32[]{:S(2)}) %collective-permute-start.13) | collective-permute-done | bytes 98336 | tf_op jit(solution)/shard_map/ppermute | solution.py:230
  47.2 1.5 %collective-permute-start.17 = (f32[192,128]{1,0:T(8,128)S(1)}, f32[192,128]{1,0:T(8,128)S(1)}, u32[]{:S(2)}, u32[]{:S(2)}) collective-permute-start(f32[192,128]{1,0:T(8,128)S(1)} %shard_map.74.refs_0_), channel_id=1, source_target_pairs={{0,16},{1,17},{2,18},{3,19},{4,20},{5,21},{6,22},{7,23},{8,24},{9,... | collective-permute-start | bytes 294920 | tf_op jit(solution)/shard_map/ppermute | solution.py:230
  48.8 1.6 %collective-permute-start.18 = (f32[192,128]{1,0:T(8,128)S(1)}, f32[192,128]{1,0:T(8,128)S(1)}, u32[]{:S(2)}, u32[]{:S(2)}) collective-permute-start(f32[192,128]{1,0:T(8,128)S(1)} %shard_map.74.refs_0_), channel_id=1, source_target_pairs={{0,24},{1,25},{2,26},{3,27},{4,28},{5,29},{6,30},{7,31},{8,16},{9,... | collective-permute-start | bytes 294920 | tf_op jit(solution)/shard_map/ppermute | solution.py:230
  50.8 1.5 %collective-permute-done.16.refs_1_ = f32[192,128]{1,0:T(8,128)S(1)} collective-permute-done((f32[192,128]{1,0:T(8,128)S(1)}, f32[192,128]{1,0:T(8,128)S(1)}, u32[]{:S(2)}, u32[]{:S(2)}) %collective-permute-start.16) | collective-permute-done | bytes 98336 | tf_op jit(solution)/shard_map/ppermute | solution.py:230
  52.4 0.5 collective-permute-start.21
  52.9 2.6 %collective-permute-done.18.refs_3_ = f32[192,128]{1,0:T(8,128)S(1)} collective-permute-done((f32[192,128]{1,0:T(8,128)S(1)}, f32[192,128]{1,0:T(8,128)S(1)}, u32[]{:S(2)}, u32[]{:S(2)}) %collective-permute-start.18) | collective-permute-done | bytes 98336 | tf_op jit(solution)/shard_map/ppermute | solution.py:230
  55.7 1.0 %collective-permute-done.22.refs_7_ = f32[192,128]{1,0:T(8,128)S(1)} collective-permute-done((f32[192,128]{1,0:T(8,128)S(1)}, f32[192,128]{1,0:T(8,128)S(1)}, u32[]{:S(2)}, u32[]{:S(2)}) %collective-permute-start.22) | collective-permute-done | bytes 98336 | tf_op jit(solution)/shard_map/ppermute | solution.py:230
  56.7 1.5 %shard_map.75 = (bf16[1,128,2,384]{3,2,1,0:T(2,128)(2,1)}, f32[2,384,384]{2,1,0:T(8,128)}) custom-call(f32[192,128]{1,0:T(8,128)S(1)} %shard_map.74.refs_0_, f32[192,128]{1,0:T(8,128)S(1)} %collective-permute-done.16.refs_1_, f32[192,128]{1,0:T(8,128)S(1)} %collective-permute-done.17.refs_2_, f32[192,128]{1,0:T(8,128)S(1)} %collective-permute-done.18.refs_3_, ...), custom_call_target="tpu_custom_call" | custom-call | tf_op jit(solution)/shard_map/pallas_call | solution.py:28
  (29 shorter events, 2.5 us)
Async XLA Ops:
  2.3 9.2 %collective-permute-start.3 = (bf16[160,384]{1,0:T(8,128)(2,1)S(1)}, bf16[160,384]{1,0:T(8,128)(2,1)S(1)}, u32[]{:S(2)}, u32[]{:S(2)}) collective-permute-start(bf16[160,384]{1,0:T(8,128)(2,1)S(1)} %get-tuple-element.14), channel_id=1, source_target_pairs={{0,8},{1,9},{2,10},{3,11},{4,12},{5,13},{6,14},{7,15},{8,0},{9,1},... | collective-permute-start | bytes 368648 | tf_op jit(solution)/shard_map/ppermute | solution.py:230
  5.3 17.8 %collective-permute-start.7 = (bf16[512,256]{1,0:T(8,128)(2,1)S(1)}, bf16[512,256]{1,0:T(8,128)(2,1)S(1)}, u32[]{:S(2)}, u32[]{:S(2)}) collective-permute-start(bf16[512,256]{1,0:T(8,128)(2,1)S(1)} %get-tuple-element.17.refs_1_), channel_id=1, source_target_pairs={{0,8},{1,9},{2,10},{3,11},{4,12},{5,13},{6,14},{7,15},{8,0},{9,1},... | collective-permute-start | bytes 786440 | tf_op jit(solution)/shard_map/ppermute | solution.py:230
  5.4 17.7 %collective-permute-start.8 = (bf16[512,256]{1,0:T(8,128)(2,1)S(1)}, bf16[512,256]{1,0:T(8,128)(2,1)S(1)}, u32[]{:S(2)}, u32[]{:S(2)}) collective-permute-start(bf16[512,256]{1,0:T(8,128)(2,1)S(1)} %get-tuple-element.18.refs_2_), channel_id=1, source_target_pairs={{0,8},{1,9},{2,10},{3,11},{4,12},{5,13},{6,14},{7,15},{8,0},{9,1},... | collective-permute-start | bytes 786440 | tf_op jit(solution)/shard_map/ppermute | solution.py:230
  7.4 5.8 %collective-permute-start = (bf16[128,384]{1,0:T(8,128)(2,1)S(1)}, bf16[128,384]{1,0:T(8,128)(2,1)S(1)}, u32[]{:S(2)}, u32[]{:S(2)}) collective-permute-start(bf16[128,384]{1,0:T(8,128)(2,1)S(1)} %get-tuple-element.13.refs_0_), channel_id=1, source_target_pairs={{0,2},{1,3},{2,0},{3,1},{4,6},{5,7},{6,4},{7,5},{8,10},{9,11},{10,... | collective-permute-start | bytes 294920 | tf_op jit(solution)/shard_map/ppermute | solution.py:230
  10.0 7.0 %collective-permute-start.1 = (bf16[128,384]{1,0:T(8,128)(2,1)S(1)}, bf16[128,384]{1,0:T(8,128)(2,1)S(1)}, u32[]{:S(2)}, u32[]{:S(2)}) collective-permute-start(bf16[128,384]{1,0:T(8,128)(2,1)S(1)} %get-tuple-element.13.refs_0_), channel_id=1, source_target_pairs={{0,1},{1,0},{2,3},{3,2},{4,5},{5,4},{6,7},{7,6},{8,9},{9,8},{10,11... | collective-permute-start | bytes 294920 | tf_op jit(solution)/shard_map/ppermute | solution.py:230
  11.6 6.8 %collective-permute-start.4 = (bf16[128,384]{1,0:T(8,128)(2,1)S(1)}, bf16[128,384]{1,0:T(8,128)(2,1)S(1)}, u32[]{:S(2)}, u32[]{:S(2)}) collective-permute-start(bf16[128,384]{1,0:T(8,128)(2,1)S(1)} %slice.8.refs_4_), channel_id=1, source_target_pairs={{0,2},{1,3},{2,0},{3,1},{4,6},{5,7},{6,4},{7,5},{8,10},{9,11},{10,... | collective-permute-start | bytes 294920 | tf_op jit(solution)/shard_map/ppermute | solution.py:230
  13.1 7.6 %collective-permute-start.2 = (bf16[128,384]{1,0:T(8,128)(2,1)S(1)}, bf16[128,384]{1,0:T(8,128)(2,1)S(1)}, u32[]{:S(2)}, u32[]{:S(2)}) collective-permute-start(bf16[128,384]{1,0:T(8,128)(2,1)S(1)} %collective-permute-done.refs_1_), channel_id=1, source_target_pairs={{0,1},{1,0},{2,3},{3,2},{4,5},{5,4},{6,7},{7,6},{8,9},{9,8},{10,11... | collective-permute-start | bytes 294920 | tf_op jit(solution)/shard_map/ppermute | solution.py:230
  17.0 5.0 %collective-permute-start.5 = (bf16[128,384]{1,0:T(8,128)(2,1)S(1)}, bf16[128,384]{1,0:T(8,128)(2,1)S(1)}, u32[]{:S(2)}, u32[]{:S(2)}) collective-permute-start(bf16[128,384]{1,0:T(8,128)(2,1)S(1)} %slice.8.refs_4_), channel_id=1, source_target_pairs={{0,1},{1,0},{2,3},{3,2},{4,5},{5,4},{6,7},{7,6},{8,9},{9,8},{10,11... | collective-permute-start | bytes 294920 | tf_op jit(solution)/shard_map/ppermute | solution.py:230
  18.3 4.7 %collective-permute-start.6 = (bf16[128,384]{1,0:T(8,128)(2,1)S(1)}, bf16[128,384]{1,0:T(8,128)(2,1)S(1)}, u32[]{:S(2)}, u32[]{:S(2)}) collective-permute-start(bf16[128,384]{1,0:T(8,128)(2,1)S(1)} %collective-permute-done.4.refs_5_), channel_id=1, source_target_pairs={{0,1},{1,0},{2,3},{3,2},{4,5},{5,4},{6,7},{7,6},{8,9},{9,8},{10,11... | collective-permute-start | bytes 294920 | tf_op jit(solution)/shard_map/ppermute | solution.py:230
  23.9 3.0 %collective-permute-start.9 = (f32[512,384]{1,0:T(8,128)S(1)}, f32[512,384]{1,0:T(8,128)S(1)}, u32[]{:S(2)}, u32[]{:S(2)}) collective-permute-start(f32[512,384]{1,0:T(8,128)S(1)} %shard_map.70.refs_1_), channel_id=1, source_target_pairs={{0,4},{1,5},{2,6},{3,7},{4,0},{5,1},{6,2},{7,3},{8,12},{9,13},{10,... | collective-permute-start | bytes 2359304 | tf_op jit(solution)/shard_map/ppermute | solution.py:230
  23.9 2.9 %collective-permute-start.10 = (bf16[576,384]{1,0:T(8,128)(2,1)S(1)}, bf16[576,384]{1,0:T(8,128)(2,1)S(1)}, u32[]{:S(2)}, u32[]{:S(2)}) collective-permute-start(bf16[576,384]{1,0:T(8,128)(2,1)S(1)} %get-tuple-element.19.refs_3_), channel_id=1, source_target_pairs={{0,4},{1,5},{2,6},{3,7},{4,0},{5,1},{6,2},{7,3},{8,12},{9,13},{10,... | collective-permute-start | bytes 1327112 | tf_op jit(solution)/shard_map/ppermute | solution.py:230
  27.5 29.2 %copy-start = (s32[2,1]{0,1:T(1,128)S(1)}, s32[2,1]{0,1:T(1,128)}, u32[]{:S(2)}) copy-start(s32[2,1]{0,1:T(1,128)} %param.7) | copy-start | bytes 28
  27.5 4.9 %collective-permute-start.11 = (f32[192,128]{1,0:T(8,128)S(1)}, f32[192,128]{1,0:T(8,128)S(1)}, u32[]{:S(2)}, u32[]{:S(2)}) collective-permute-start(f32[192,128]{1,0:T(8,128)S(1)} %get-tuple-element.21), channel_id=1, source_target_pairs={{0,16},{1,17},{2,18},{3,19},{4,20},{5,21},{6,22},{7,23},{8,24},{9,... | collective-permute-start | bytes 294920 | tf_op jit(solution)/shard_map/ppermute | solution.py:230
  32.4 7.6 %collective-permute-start.12 = (f32[192,128]{1,0:T(8,128)S(1)}, f32[192,128]{1,0:T(8,128)S(1)}, u32[]{:S(2)}, u32[]{:S(2)}) collective-permute-start(f32[192,128]{1,0:T(8,128)S(1)} %shard_map.72.refs_0_), channel_id=1, source_target_pairs={{0,2},{1,3},{2,0},{3,1},{4,6},{5,7},{6,4},{7,5},{8,10},{9,11},{10,... | collective-permute-start | bytes 294920 | tf_op jit(solution)/shard_map/ppermute | solution.py:230
  35.6 6.8 %collective-permute-start.14 = (bf16[128,384]{1,0:T(8,128)(2,1)S(1)}, bf16[128,384]{1,0:T(8,128)(2,1)S(1)}, u32[]{:S(2)}, u32[]{:S(2)}) collective-permute-start(bf16[128,384]{1,0:T(8,128)(2,1)S(1)} %get-tuple-element.22), channel_id=1, source_target_pairs={{0,0},{4,3},{1,5},{5,6},{6,2},{2,1},{7,7},{3,4},{8,8},{12,11},{9,1... | collective-permute-start | bytes 294920 | tf_op jit(solution)/shard_map/ppermute | solution.py:282
  36.3 9.5 %collective-permute-start.15 = (bf16[128,384]{1,0:T(8,128)(2,1)S(1)}, bf16[128,384]{1,0:T(8,128)(2,1)S(1)}, u32[]{:S(2)}, u32[]{:S(2)}) collective-permute-start(bf16[128,384]{1,0:T(8,128)(2,1)S(1)} %get-tuple-element.23), channel_id=1, source_target_pairs={{0,1},{4,2},{1,4},{5,7},{6,3},{2,0},{7,6},{3,5},{8,9},{12,10},{9,1... | collective-permute-start | bytes 294920 | tf_op jit(solution)/shard_map/ppermute | solution.py:283
  40.0 6.8 %collective-permute-start.13 = (f32[192,128]{1,0:T(8,128)S(1)}, f32[192,128]{1,0:T(8,128)S(1)}, u32[]{:S(2)}, u32[]{:S(2)}) collective-permute-start(f32[192,128]{1,0:T(8,128)S(1)} %shard_map.73.refs_0_), channel_id=1, source_target_pairs={{0,1},{1,0},{2,3},{3,2},{4,5},{5,4},{6,7},{7,6},{8,9},{9,8},{10,11... | collective-permute-start | bytes 294920 | tf_op jit(solution)/shard_map/ppermute | solution.py:230
  46.8 5.6 %collective-permute-start.16 = (f32[192,128]{1,0:T(8,128)S(1)}, f32[192,128]{1,0:T(8,128)S(1)}, u32[]{:S(2)}, u32[]{:S(2)}) collective-permute-start(f32[192,128]{1,0:T(8,128)S(1)} %shard_map.74.refs_0_), channel_id=1, source_target_pairs={{0,8},{1,9},{2,10},{3,11},{4,12},{5,13},{6,14},{7,15},{8,0},{9,1},... | collective-permute-start | bytes 294920 | tf_op jit(solution)/shard_map/ppermute | solution.py:230
  47.2 5.1 %collective-permute-start.17 = (f32[192,128]{1,0:T(8,128)S(1)}, f32[192,128]{1,0:T(8,128)S(1)}, u32[]{:S(2)}, u32[]{:S(2)}) collective-permute-start(f32[192,128]{1,0:T(8,128)S(1)} %shard_map.74.refs_0_), channel_id=1, source_target_pairs={{0,16},{1,17},{2,18},{3,19},{4,20},{5,21},{6,22},{7,23},{8,24},{9,... | collective-permute-start | bytes 294920 | tf_op jit(solution)/shard_map/ppermute | solution.py:230
  48.8 6.7 %collective-permute-start.18 = (f32[192,128]{1,0:T(8,128)S(1)}, f32[192,128]{1,0:T(8,128)S(1)}, u32[]{:S(2)}, u32[]{:S(2)}) collective-permute-start(f32[192,128]{1,0:T(8,128)S(1)} %shard_map.74.refs_0_), channel_id=1, source_target_pairs={{0,24},{1,25},{2,26},{3,27},{4,28},{5,29},{6,30},{7,31},{8,16},{9,... | collective-permute-start | bytes 294920 | tf_op jit(solution)/shard_map/ppermute | solution.py:230
  50.4 5.3 %collective-permute-start.23 = (bf16[128,384]{1,0:T(8,128)(2,1)S(1)}, bf16[128,384]{1,0:T(8,128)(2,1)S(1)}, u32[]{:S(2)}, u32[]{:S(2)}) collective-permute-start(bf16[128,384]{1,0:T(8,128)(2,1)S(1)} %get-tuple-element.24), channel_id=1, source_target_pairs={{0,8},{1,9},{2,10},{3,11},{4,12},{5,13},{6,14},{7,15},{8,0},{9,1},... | collective-permute-start | bytes 294920 | tf_op jit(solution)/shard_map/ppermute | solution.py:230
  50.8 4.8 %collective-permute-start.19 = (f32[192,128]{1,0:T(8,128)S(1)}, f32[192,128]{1,0:T(8,128)S(1)}, u32[]{:S(2)}, u32[]{:S(2)}) collective-permute-start(f32[192,128]{1,0:T(8,128)S(1)} %shard_map.74.refs_0_), channel_id=1, source_target_pairs={{0,4},{1,5},{2,6},{3,7},{4,0},{5,1},{6,2},{7,3},{8,12},{9,13},{10,... | collective-permute-start | bytes 294920 | tf_op jit(solution)/shard_map/ppermute | solution.py:230
  52.3 3.3 %collective-permute-start.20 = (f32[192,128]{1,0:T(8,128)S(1)}, f32[192,128]{1,0:T(8,128)S(1)}, u32[]{:S(2)}, u32[]{:S(2)}) collective-permute-start(f32[192,128]{1,0:T(8,128)S(1)} %collective-permute-done.16.refs_1_), channel_id=1, source_target_pairs={{0,4},{1,5},{2,6},{3,7},{4,0},{5,1},{6,2},{7,3},{8,12},{9,13},{10,... | collective-permute-start | bytes 294920 | tf_op jit(solution)/shard_map/ppermute | solution.py:230
  52.4 3.3 %collective-permute-start.21 = (f32[192,128]{1,0:T(8,128)S(1)}, f32[192,128]{1,0:T(8,128)S(1)}, u32[]{:S(2)}, u32[]{:S(2)}) collective-permute-start(f32[192,128]{1,0:T(8,128)S(1)} %collective-permute-done.17.refs_2_), channel_id=1, source_target_pairs={{0,4},{1,5},{2,6},{3,7},{4,0},{5,1},{6,2},{7,3},{8,12},{9,13},{10,... | collective-permute-start | bytes 294920 | tf_op jit(solution)/shard_map/ppermute | solution.py:230
  55.4 1.3 %collective-permute-start.22 = (f32[192,128]{1,0:T(8,128)S(1)}, f32[192,128]{1,0:T(8,128)S(1)}, u32[]{:S(2)}, u32[]{:S(2)}) collective-permute-start(f32[192,128]{1,0:T(8,128)S(1)} %collective-permute-done.18.refs_3_), channel_id=1, source_target_pairs={{0,4},{1,5},{2,6},{3,7},{4,0},{5,1},{6,2},{7,3},{8,12},{9,13},{10,... | collective-permute-start | bytes 294920 | tf_op jit(solution)/shard_map/ppermute | solution.py:230

commit v6 on v5

--- a/solution.py
+++ b/solution.py
@@ -16,7 +16,7 @@
 AXES = ("hyp", "side", "core", "pcol")
 
 
-def call(kernel, outs, specs, *operands, scratch=(), out_specs=None, after=()):
+def call(kernel, outs, specs, *operands, scratch=(), out_specs=None, after=(), alias={}):
     many = isinstance(outs, (list, tuple))
     count = len(specs)
 
@@ -31,6 +31,7 @@
         in_specs=list(specs) + [ANY] * len(after),
         out_specs=out_specs,
         scratch_shapes=scratch,
+        input_output_aliases=alias,
         compiler_params=pltpu.CompilerParams(vmem_limit_bytes=32 * 2**20),
     )(*operands, *after)
 
@@ -81,7 +82,7 @@
 
 
 def start_kernel(*refs):
-    sources, (own, give, own_inverse, low, high), buffers, sems = refs[:4], refs[4:9], refs[9:13], refs[13]
+    sources, (own, give, own_inverse), pieces, buffers, sems = refs[:4], refs[4:7], refs[7:-5], refs[-5:-1], refs[-1]
     copies = [
         pltpu.make_async_copy(source, buffer, sems.at[index])
         for index, (source, buffer) in enumerate(zip(sources, buffers))
@@ -104,9 +105,10 @@
     own_inverse[...] = jnp.where(first, one, two)
     give[height:] = jnp.where(first, two, one)
     copies[3].wait()
-    half = matrix.shape[1] // 2
-    low[...] = matrix[0, :half].T
-    high[...] = matrix[0, half:].T
+    at = 0
+    for piece in pieces:
+        piece[...] = matrix[0, :, at : at + piece.shape[0]].T
+        at += piece.shape[0]
 
 
 def gather_kernel(*refs):
@@ -124,13 +126,14 @@
 
 
 def apply_kernel(rows, *refs):
-    parts, applied = refs[:4], refs[4]
-    half = rows.shape[1] // 2
-    total = 0
-    for index, part in enumerate(parts):
-        lines = rows[index // 2, index % 2 * half : (index % 2 + 1) * half, :]
-        total += jnp.dot(part[...], lines, preferred_element_type=jnp.float32)
-    applied[...] = total
+    pieces, applied = refs[:-1], refs[-1]
+    count = len(pieces) // 2
+    at = 0
+    for own, far in zip(pieces[:count], pieces[count:]):
+        total = jnp.dot(own[...], rows[0], preferred_element_type=jnp.float32)
+        total += jnp.dot(far[...], rows[1], preferred_element_type=jnp.float32)
+        applied[at : at + own.shape[0]] = total
+        at += own.shape[0]
 
 
 def couple_kernel(weight, mine, other, pack, got_pack, out_a, out_b, keep, send, half, packed):
@@ -231,11 +234,12 @@
 
     extent = sigma_rows.shape[2]
     block = shape((height, width), bf16)
-    part = shape((extent, extent // 2), bf16)
+    cuts = (extent * 9 // 16, extent * 7 // 32, extent * 7 // 32)
     size = pl.cdiv(inv_diag.shape[2], ROWS) * ROWS
-    own, give, own_inverse, low, high = call(
+    own, give, own_inverse, *pieces = call(
         start_kernel,
-        [block, shape((height + size, width), bf16), shape((size, width), bf16), part, part],
+        [block, shape((height + size, width), bf16), shape((size, width), bf16)]
+        + [shape((lines, extent), bf16) for lines in cuts],
         [HBM] * 4,
         *map(stay, (live, panel, inv_diag, sigma_rows)),
         scratch=[pltpu.SMEM(live.shape, jnp.int32)]
@@ -244,11 +248,12 @@
     )
     got = swap(give, side=1)
     got, got_inverse = got[:height], got[height:]
-    far_low, far_high = swap(low, side=1), swap(high, side=1)
     blocks = []
     for start in (own, got):
         second = swap(start, column=2)
         blocks += [start, second, swap(start, column=1), swap(second, column=1)]
+    far = [swap(piece, side=1) for piece in pieces]
+
     pack = shape((extent + 2 * size, width), bf16)
     rows, pack = call(
         gather_kernel, [shape((2, extent, width), bf16), pack], [VMEM] * 10,
@@ -256,7 +261,7 @@
     )
     got_pack = swap(pack, core=1)
     mine = call(
-        apply_kernel, shape((extent, width), f32), [VMEM] * 5, rows, low, high, far_low, far_high
+        apply_kernel, shape((extent, width), f32), [VMEM] * (1 + 2 * len(cuts)), rows, *pieces, *far
     )
     other = swap(mine, core=1)
 
@@ -285,11 +290,11 @@
 
     add = functools.partial(call, add_kernel, part, [VMEM] * 2)
     total = add(keep, came)
-    total = add(total, swap(total, column=2))
-    total = add(total, swap(total, column=1), after=[land_a, land_b])
+    total = add(total, swap(total, column=2), after=[land_a, land_b])
+    theirs = swap(jnp.where(from_a == side, land_b, land_a), side=1)
+    total = add(total, swap(total, column=1), after=[theirs])
     quarters = [total, swap(total, side=1), swap(total, point=1), swap(total, side=1, point=1)]
     quarters += [swap(x, core=1) for x in quarters]
-    theirs = swap(jnp.where(from_a == side, land_b, land_a), side=1)
     mine = jnp.where(from_a == side, land_a, land_b)
     return call(
         finish_kernel,

time: 58.4 us -> 60.9 us (1.043)
  waiting for transfers between devices: 20.8 us -> 27.8 us
  starting transfers between devices: 31.3 us -> 26.4 us
    ppermute x22 -> x23, starting transfers between devices: 28 us -> 23.3 us  [swap(): return lax.ppermute(x, AXES, [(i, i ^ mask) for i in range(devices)])]
    ppermute x1, waiting for transfers between devices: 3.4 us -> 7.35 us  [square(): land_b = lax.ppermute(out_b, AXES, output_pairs((1, 2)))]
    ppermute x22 -> x23, waiting for transfers between devices: 17.4 us -> 20.5 us  [swap(): return lax.ppermute(x, AXES, [(i, i ^ mask) for i in range(devices)])]
  transfers between devices with their start and end apart: 24 -> 25, of which waited for: 14 -> 14; matrix products, arithmetic and copies ran while one was open for 0% -> 0% of each run, Pallas kernels for 0% -> 0%
where the time goes in v6:
time: 60.9 us; the launch traced here: 60.7 us
  waiting for transfers between devices  27.8 us (46%)
  starting transfers between devices  26.4 us (43%)
  Pallas kernels  4.95 us (8%)
  between operations  1.42 us (2%)
    ppermute x23, starting transfers between devices, swap(): return lax.ppermute(x, AXES, [(i, i ^ mask) for i in range(devices)])  23.3 us
    ppermute x23, waiting for transfers between devices, swap(): return lax.ppermute(x, AXES, [(i, i ^ mask) for i in range(devices)])  20.5 us
    ppermute x1, waiting for transfers between devices, square(): land_b = lax.ppermute(out_b, AXES, output_pairs((1, 2)))  7.35 us
    pallas_call x8, Pallas kernels, call(): pl.pallas_call(body, out_shape=outs, in_specs=list(specs) + [ANY] * len(a...  4.95 us
    ppermute x1, starting transfers between devices, square(): land_b = lax.ppermute(out_b, AXES, output_pairs((1, 2)))  2.46 us
  transfers between devices with their start and end apart: 25, of which 14 were waited for; matrix products, arithmetic and copies ran while one was open for 0% of the time, Pallas kernels for 0%

profile of v6, /device:TPU:0, one launch (start us, length us, event | category | flops | bytes accessed | tf_op | source)
XLA Modules:
  0.0 60.7 jit_solution(4429029074022861475)
XLA Ops:
  0.6 1.9 %shard_map.68 = (bf16[128,384]{1,0:T(8,128)(2,1)S(1)}, bf16[160,384]{1,0:T(8,128)(2,1)S(1)}, bf16[32,384]{1,0:T(8,128)(2,1)S(1)}, bf16[288,512]{1,0:T(8,128)(2,1...) custom-call(s32[2]{0:T(128)} %bitcast.1, bf16[1,128,2,384]{3,2,1,0:T(2,128)(2,1)} %refs_1_.1, ...), custom_call_target="tpu_custom_call" | custom-call | tf_op jit(solution)/shard_map/pallas_call | solution.py:28
  2.6 3.0 %collective-permute-start.3 = (bf16[160,384]{1,0:T(8,128)(2,1)S(1)}, bf16[160,384]{1,0:T(8,128)(2,1)S(1)}, u32[]{:S(2)}, u32[]{:S(2)}) collective-permute-start(bf16[160,384]{1,0:T(8,128)(2,1)S(1)} %get-tuple-element.15), channel_id=1, source_target_pairs={{0,8},{1,9},{2,10},{3,11},{4,12},{5,13},{6,14},{7,15},{8,0},{9,1},... | collective-permute-start | bytes 368648 | tf_op jit(solution)/shard_map/ppermute | solution.py:233
  5.6 2.6 %collective-permute-start = (bf16[128,384]{1,0:T(8,128)(2,1)S(1)}, bf16[128,384]{1,0:T(8,128)(2,1)S(1)}, u32[]{:S(2)}, u32[]{:S(2)}) collective-permute-start(bf16[128,384]{1,0:T(8,128)(2,1)S(1)} %get-tuple-element.14.refs_0_), channel_id=1, source_target_pairs={{0,2},{1,3},{2,0},{3,1},{4,6},{5,7},{6,4},{7,5},{8,10},{9,11},{10,... | collective-permute-start | bytes 294920 | tf_op jit(solution)/shard_map/ppermute | solution.py:233
  8.2 0.5 collective-permute-start.7
  8.7 1.6 %collective-permute-start.1 = (bf16[128,384]{1,0:T(8,128)(2,1)S(1)}, bf16[128,384]{1,0:T(8,128)(2,1)S(1)}, u32[]{:S(2)}, u32[]{:S(2)}) collective-permute-start(bf16[128,384]{1,0:T(8,128)(2,1)S(1)} %get-tuple-element.14.refs_0_), channel_id=1, source_target_pairs={{0,1},{1,0},{2,3},{3,2},{4,5},{5,4},{6,7},{7,6},{8,9},{9,8},{10,11... | collective-permute-start | bytes 294920 | tf_op jit(solution)/shard_map/ppermute | solution.py:233
  10.3 2.6 %collective-permute-done.refs_1_ = bf16[128,384]{1,0:T(8,128)(2,1)S(1)} collective-permute-done((bf16[128,384]{1,0:T(8,128)(2,1)S(1)}, bf16[128,384]{1,0:T(8,128)(2,1)S(1)}, u32[]{:S(2)}, u32[]{:S(2)}) %collective-permute-start) | collective-permute-done | bytes 98336 | tf_op jit(solution)/shard_map/ppermute | solution.py:233
  12.8 0.7 %collective-permute-start.2 = (bf16[128,384]{1,0:T(8,128)(2,1)S(1)}, bf16[128,384]{1,0:T(8,128)(2,1)S(1)}, u32[]{:S(2)}, u32[]{:S(2)}) collective-permute-start(bf16[128,384]{1,0:T(8,128)(2,1)S(1)} %collective-permute-done.refs_1_), channel_id=1, source_target_pairs={{0,1},{1,0},{2,3},{3,2},{4,5},{5,4},{6,7},{7,6},{8,9},{9,8},{10,11... | collective-permute-start | bytes 294920 | tf_op jit(solution)/shard_map/ppermute | solution.py:233
  13.5 3.5 %collective-permute-start.4 = (bf16[128,384]{1,0:T(8,128)(2,1)S(1)}, bf16[128,384]{1,0:T(8,128)(2,1)S(1)}, u32[]{:S(2)}, u32[]{:S(2)}) collective-permute-start(bf16[128,384]{1,0:T(8,128)(2,1)S(1)} %slice.8.refs_4_), channel_id=1, source_target_pairs={{0,2},{1,3},{2,0},{3,1},{4,6},{5,7},{6,4},{7,5},{8,10},{9,11},{10,... | collective-permute-start | bytes 294920 | tf_op jit(solution)/shard_map/ppermute | solution.py:233
  17.0 0.6 collective-permute-start.8
  17.6 1.5 %collective-permute-start.9 = (bf16[112,512]{1,0:T(8,128)(2,1)S(1)}, bf16[112,512]{1,0:T(8,128)(2,1)S(1)}, u32[]{:S(2)}, u32[]{:S(2)}) collective-permute-start(bf16[112,512]{1,0:T(8,128)(2,1)S(1)} %get-tuple-element.20.refs_3_), channel_id=1, source_target_pairs={{0,8},{1,9},{2,10},{3,11},{4,12},{5,13},{6,14},{7,15},{8,0},{9,1},... | collective-permute-start | bytes 344072 | tf_op jit(solution)/shard_map/ppermute | solution.py:233
  19.1 2.1 %collective-permute-done.4.refs_5_ = bf16[128,384]{1,0:T(8,128)(2,1)S(1)} collective-permute-done((bf16[128,384]{1,0:T(8,128)(2,1)S(1)}, bf16[128,384]{1,0:T(8,128)(2,1)S(1)}, u32[]{:S(2)}, u32[]{:S(2)}) %collective-permute-start.4) | collective-permute-done | bytes 98336 | tf_op jit(solution)/shard_map/ppermute | solution.py:233
  21.1 1.2 %collective-permute-start.6 = (bf16[128,384]{1,0:T(8,128)(2,1)S(1)}, bf16[128,384]{1,0:T(8,128)(2,1)S(1)}, u32[]{:S(2)}, u32[]{:S(2)}) collective-permute-start(bf16[128,384]{1,0:T(8,128)(2,1)S(1)} %collective-permute-done.4.refs_5_), channel_id=1, source_target_pairs={{0,1},{1,0},{2,3},{3,2},{4,5},{5,4},{6,7},{7,6},{8,9},{9,8},{10,11... | collective-permute-start | bytes 294920 | tf_op jit(solution)/shard_map/ppermute | solution.py:233
  22.3 1.4 %collective-permute-done.5.refs_6_ = bf16[128,384]{1,0:T(8,128)(2,1)S(1)} collective-permute-done((bf16[128,384]{1,0:T(8,128)(2,1)S(1)}, bf16[128,384]{1,0:T(8,128)(2,1)S(1)}, u32[]{:S(2)}, u32[]{:S(2)}) %collective-permute-start.5) | collective-permute-done | bytes 98336 | tf_op jit(solution)/shard_map/ppermute | solution.py:233
  23.7 2.1 %collective-permute-done.6.refs_7_ = bf16[128,384]{1,0:T(8,128)(2,1)S(1)} collective-permute-done((bf16[128,384]{1,0:T(8,128)(2,1)S(1)}, bf16[128,384]{1,0:T(8,128)(2,1)S(1)}, u32[]{:S(2)}, u32[]{:S(2)}) %collective-permute-start.6) | collective-permute-done | bytes 98336 | tf_op jit(solution)/shard_map/ppermute | solution.py:233
  25.9 0.7 %shard_map.70.refs_1_ = f32[512,384]{1,0:T(8,128)S(1)} custom-call(bf16[2,512,384]{2,1,0:T(8,128)(2,1)S(1)} %get-tuple-element.17.refs_0_, bf16[288,512]{1,0:T(8,128)(2,1)S(1)} %get-tuple-element.18.refs_1_, bf16[112,512]{1,0:T(8,128)(2,1)S(1)} %get-tuple-element.19.refs_2_, bf16[112,512]{1,0:T(8,128)(2,1)S(1)} %get-tuple-element.20.refs_3_, ...), custom_call_target="tpu_custom_call" | custom-call | tf_op jit(solution)/shard_map/pallas_call | solution.py:28
  27.9 1.8 %collective-permute-done.11.refs_4_ = bf16[576,384]{1,0:T(8,128)(2,1)S(1)} collective-permute-done((bf16[576,384]{1,0:T(8,128)(2,1)S(1)}, bf16[576,384]{1,0:T(8,128)(2,1)S(1)}, u32[]{:S(2)}, u32[]{:S(2)}) %collective-permute-start.11) | collective-permute-done | bytes 442400 | tf_op jit(solution)/shard_map/ppermute | solution.py:233
  29.6 0.6 %shard_map.71 = (bf16[128,384]{1,0:T(8,128)(2,1)S(1)}, bf16[128,384]{1,0:T(8,128)(2,1)S(1)}, f32[192,128]{1,0:T(8,128)S(1)}, f32[192,128]{1,0:T(8,128)S(1)}) custom-call(f32[1]{0:T(128)S(6)} %copy.7.refs_0_, f32[512,384]{1,0:T(8,128)S(1)} %shard_map.70.refs_1_, f32[512,384]{1,0:T(8,128)S(1)} %collective-permute-done.10.refs_2_, ...), custom_call_target="tpu_custom_call" | custom-call | tf_op jit(solution)/shard_map/pallas_call | solution.py:28
  30.3 1.6 %collective-permute-start.12 = (f32[192,128]{1,0:T(8,128)S(1)}, f32[192,128]{1,0:T(8,128)S(1)}, u32[]{:S(2)}, u32[]{:S(2)}) collective-permute-start(f32[192,128]{1,0:T(8,128)S(1)} %get-tuple-element.23), channel_id=1, source_target_pairs={{0,16},{1,17},{2,18},{3,19},{4,20},{5,21},{6,22},{7,23},{8,24},{9,... | collective-permute-start | bytes 294920 | tf_op jit(solution)/shard_map/ppermute | solution.py:233
  31.9 0.7 %collective-permute-start.14 = (bf16[128,384]{1,0:T(8,128)(2,1)S(1)}, bf16[128,384]{1,0:T(8,128)(2,1)S(1)}, u32[]{:S(2)}, u32[]{:S(2)}) collective-permute-start(bf16[128,384]{1,0:T(8,128)(2,1)S(1)} %get-tuple-element.24), channel_id=1, source_target_pairs={{0,0},{4,3},{1,5},{5,6},{6,2},{2,1},{7,7},{3,4},{8,8},{12,11},{9,1... | collective-permute-start | bytes 294920 | tf_op jit(solution)/shard_map/ppermute | solution.py:287
  32.5 2.5 %collective-permute-start.15 = (bf16[128,384]{1,0:T(8,128)(2,1)S(1)}, bf16[128,384]{1,0:T(8,128)(2,1)S(1)}, u32[]{:S(2)}, u32[]{:S(2)}) collective-permute-start(bf16[128,384]{1,0:T(8,128)(2,1)S(1)} %get-tuple-element.25), channel_id=1, source_target_pairs={{0,1},{4,2},{1,4},{5,7},{6,3},{2,0},{7,6},{3,5},{8,9},{12,10},{9,1... | collective-permute-start | bytes 294920 | tf_op jit(solution)/shard_map/ppermute | solution.py:288
  35.2 2.4 %collective-permute-start.13 = (f32[192,128]{1,0:T(8,128)S(1)}, f32[192,128]{1,0:T(8,128)S(1)}, u32[]{:S(2)}, u32[]{:S(2)}) collective-permute-start(f32[192,128]{1,0:T(8,128)S(1)} %shard_map.72.refs_0_), channel_id=1, source_target_pairs={{0,2},{1,3},{2,0},{3,1},{4,6},{5,7},{6,4},{7,5},{8,10},{9,11},{10,... | collective-permute-start | bytes 294920 | tf_op jit(solution)/shard_map/ppermute | solution.py:233
  37.6 7.4 %collective-permute-done.15.refs_3_ = bf16[128,384]{1,0:T(8,128)(2,1)S(1)} collective-permute-done((bf16[128,384]{1,0:T(8,128)(2,1)S(1)}, bf16[128,384]{1,0:T(8,128)(2,1)S(1)}, u32[]{:S(2)}, u32[]{:S(2)}) %collective-permute-start.15) | collective-permute-done | bytes 98336 | tf_op jit(solution)/shard_map/ppermute | solution.py:288
  45.0 1.4 %collective-permute-done.13.refs_1_ = f32[192,128]{1,0:T(8,128)S(1)} collective-permute-done((f32[192,128]{1,0:T(8,128)S(1)}, f32[192,128]{1,0:T(8,128)S(1)}, u32[]{:S(2)}, u32[]{:S(2)}) %collective-permute-start.13) | collective-permute-done | bytes 98336 | tf_op jit(solution)/shard_map/ppermute | solution.py:233
  46.5 3.2 %collective-permute-done.17.refs_2_.refs_10_ = bf16[128,384]{1,0:T(8,128)(2,1)S(1)} collective-permute-done((bf16[128,384]{1,0:T(8,128)(2,1)S(1)}, bf16[128,384]{1,0:T(8,128)(2,1)S(1)}, u32[]{:S(2)}, u32[]{:S(2)}) %collective-permute-start.17) | collective-permute-done | bytes 98336 | tf_op jit(solution)/shard_map/ppermute | solution.py:233
  49.6 1.4 %collective-permute-done.16.refs_1_ = f32[192,128]{1,0:T(8,128)S(1)} collective-permute-done((f32[192,128]{1,0:T(8,128)S(1)}, f32[192,128]{1,0:T(8,128)S(1)}, u32[]{:S(2)}, u32[]{:S(2)}) %collective-permute-start.16) | collective-permute-done | bytes 98336 | tf_op jit(solution)/shard_map/ppermute | solution.py:233
  51.1 0.7 %collective-permute-start.18 = (f32[192,128]{1,0:T(8,128)S(1)}, f32[192,128]{1,0:T(8,128)S(1)}, u32[]{:S(2)}, u32[]{:S(2)}) collective-permute-start(f32[192,128]{1,0:T(8,128)S(1)} %shard_map.74.refs_0_), channel_id=1, source_target_pairs={{0,8},{1,9},{2,10},{3,11},{4,12},{5,13},{6,14},{7,15},{8,0},{9,1},... | collective-permute-start | bytes 294920 | tf_op jit(solution)/shard_map/ppermute | solution.py:233
  52.3 2.3 %collective-permute-start.20 = (f32[192,128]{1,0:T(8,128)S(1)}, f32[192,128]{1,0:T(8,128)S(1)}, u32[]{:S(2)}, u32[]{:S(2)}) collective-permute-start(f32[192,128]{1,0:T(8,128)S(1)} %shard_map.74.refs_0_), channel_id=1, source_target_pairs={{0,24},{1,25},{2,26},{3,27},{4,28},{5,29},{6,30},{7,31},{8,16},{9,... | collective-permute-start | bytes 294920 | tf_op jit(solution)/shard_map/ppermute | solution.py:233
  54.6 1.1 %collective-permute-done.18.refs_1_ = f32[192,128]{1,0:T(8,128)S(1)} collective-permute-done((f32[192,128]{1,0:T(8,128)S(1)}, f32[192,128]{1,0:T(8,128)S(1)}, u32[]{:S(2)}, u32[]{:S(2)}) %collective-permute-start.18) | collective-permute-done | bytes 98336 | tf_op jit(solution)/shard_map/ppermute | solution.py:233
  55.8 0.7 %collective-permute-done.19.refs_2_ = f32[192,128]{1,0:T(8,128)S(1)} collective-permute-done((f32[192,128]{1,0:T(8,128)S(1)}, f32[192,128]{1,0:T(8,128)S(1)}, u32[]{:S(2)}, u32[]{:S(2)}) %collective-permute-start.19) | collective-permute-done | bytes 98336 | tf_op jit(solution)/shard_map/ppermute | solution.py:233
  56.4 1.4 %collective-permute-done.20.refs_3_ = f32[192,128]{1,0:T(8,128)S(1)} collective-permute-done((f32[192,128]{1,0:T(8,128)S(1)}, f32[192,128]{1,0:T(8,128)S(1)}, u32[]{:S(2)}, u32[]{:S(2)}) %collective-permute-start.20) | collective-permute-done | bytes 98336 | tf_op jit(solution)/shard_map/ppermute | solution.py:233
  57.9 1.3 %collective-permute-done.24.refs_7_ = f32[192,128]{1,0:T(8,128)S(1)} collective-permute-done((f32[192,128]{1,0:T(8,128)S(1)}, f32[192,128]{1,0:T(8,128)S(1)}, u32[]{:S(2)}, u32[]{:S(2)}) %collective-permute-start.24) | collective-permute-done | bytes 98336 | tf_op jit(solution)/shard_map/ppermute | solution.py:233
  59.1 1.5 %shard_map.75 = (bf16[1,128,2,384]{3,2,1,0:T(2,128)(2,1)}, f32[2,384,384]{2,1,0:T(8,128)}) custom-call(f32[192,128]{1,0:T(8,128)S(1)} %shard_map.74.refs_0_, f32[192,128]{1,0:T(8,128)S(1)} %collective-permute-done.18.refs_1_, f32[192,128]{1,0:T(8,128)S(1)} %collective-permute-done.19.refs_2_, f32[192,128]{1,0:T(8,128)S(1)} %collective-permute-done.20.refs_3_, ...), custom_call_target="tpu_custom_call" | custom-call | tf_op jit(solution)/shard_map/pallas_call | solution.py:28
  (31 shorter events, 1.6 us)
Async XLA Ops:
  2.6 10.9 %collective-permute-start.3 = (bf16[160,384]{1,0:T(8,128)(2,1)S(1)}, bf16[160,384]{1,0:T(8,128)(2,1)S(1)}, u32[]{:S(2)}, u32[]{:S(2)}) collective-permute-start(bf16[160,384]{1,0:T(8,128)(2,1)S(1)} %get-tuple-element.15), channel_id=1, source_target_pairs={{0,8},{1,9},{2,10},{3,11},{4,12},{5,13},{6,14},{7,15},{8,0},{9,1},... | collective-permute-start | bytes 368648 | tf_op jit(solution)/shard_map/ppermute | solution.py:233
  5.6 7.3 %collective-permute-start = (bf16[128,384]{1,0:T(8,128)(2,1)S(1)}, bf16[128,384]{1,0:T(8,128)(2,1)S(1)}, u32[]{:S(2)}, u32[]{:S(2)}) collective-permute-start(bf16[128,384]{1,0:T(8,128)(2,1)S(1)} %get-tuple-element.14.refs_0_), channel_id=1, source_target_pairs={{0,2},{1,3},{2,0},{3,1},{4,6},{5,7},{6,4},{7,5},{8,10},{9,11},{10,... | collective-permute-start | bytes 294920 | tf_op jit(solution)/shard_map/ppermute | solution.py:233
  8.2 17.8 %collective-permute-start.7 = (bf16[288,512]{1,0:T(8,128)(2,1)S(1)}, bf16[288,512]{1,0:T(8,128)(2,1)S(1)}, u32[]{:S(2)}, u32[]{:S(2)}) collective-permute-start(bf16[288,512]{1,0:T(8,128)(2,1)S(1)} %get-tuple-element.18.refs_1_), channel_id=1, source_target_pairs={{0,8},{1,9},{2,10},{3,11},{4,12},{5,13},{6,14},{7,15},{8,0},{9,1},... | collective-permute-start | bytes 884744 | tf_op jit(solution)/shard_map/ppermute | solution.py:233
  8.7 8.9 %collective-permute-start.1 = (bf16[128,384]{1,0:T(8,128)(2,1)S(1)}, bf16[128,384]{1,0:T(8,128)(2,1)S(1)}, u32[]{:S(2)}, u32[]{:S(2)}) collective-permute-start(bf16[128,384]{1,0:T(8,128)(2,1)S(1)} %get-tuple-element.14.refs_0_), channel_id=1, source_target_pairs={{0,1},{1,0},{2,3},{3,2},{4,5},{5,4},{6,7},{7,6},{8,9},{9,8},{10,11... | collective-permute-start | bytes 294920 | tf_op jit(solution)/shard_map/ppermute | solution.py:233
  12.8 6.3 %collective-permute-start.2 = (bf16[128,384]{1,0:T(8,128)(2,1)S(1)}, bf16[128,384]{1,0:T(8,128)(2,1)S(1)}, u32[]{:S(2)}, u32[]{:S(2)}) collective-permute-start(bf16[128,384]{1,0:T(8,128)(2,1)S(1)} %collective-permute-done.refs_1_), channel_id=1, source_target_pairs={{0,1},{1,0},{2,3},{3,2},{4,5},{5,4},{6,7},{7,6},{8,9},{9,8},{10,11... | collective-permute-start | bytes 294920 | tf_op jit(solution)/shard_map/ppermute | solution.py:233
  13.5 7.6 %collective-permute-start.4 = (bf16[128,384]{1,0:T(8,128)(2,1)S(1)}, bf16[128,384]{1,0:T(8,128)(2,1)S(1)}, u32[]{:S(2)}, u32[]{:S(2)}) collective-permute-start(bf16[128,384]{1,0:T(8,128)(2,1)S(1)} %slice.8.refs_4_), channel_id=1, source_target_pairs={{0,2},{1,3},{2,0},{3,1},{4,6},{5,7},{6,4},{7,5},{8,10},{9,11},{10,... | collective-permute-start | bytes 294920 | tf_op jit(solution)/shard_map/ppermute | solution.py:233
  17.0 8.8 %collective-permute-start.8 = (bf16[112,512]{1,0:T(8,128)(2,1)S(1)}, bf16[112,512]{1,0:T(8,128)(2,1)S(1)}, u32[]{:S(2)}, u32[]{:S(2)}) collective-permute-start(bf16[112,512]{1,0:T(8,128)(2,1)S(1)} %get-tuple-element.19.refs_2_), channel_id=1, source_target_pairs={{0,8},{1,9},{2,10},{3,11},{4,12},{5,13},{6,14},{7,15},{8,0},{9,1},... | collective-permute-start | bytes 344072 | tf_op jit(solution)/shard_map/ppermute | solution.py:233
  17.6 8.3 %collective-permute-start.9 = (bf16[112,512]{1,0:T(8,128)(2,1)S(1)}, bf16[112,512]{1,0:T(8,128)(2,1)S(1)}, u32[]{:S(2)}, u32[]{:S(2)}) collective-permute-start(bf16[112,512]{1,0:T(8,128)(2,1)S(1)} %get-tuple-element.20.refs_3_), channel_id=1, source_target_pairs={{0,8},{1,9},{2,10},{3,11},{4,12},{5,13},{6,14},{7,15},{8,0},{9,1},... | collective-permute-start | bytes 344072 | tf_op jit(solution)/shard_map/ppermute | solution.py:233
  19.1 4.6 %collective-permute-start.5 = (bf16[128,384]{1,0:T(8,128)(2,1)S(1)}, bf16[128,384]{1,0:T(8,128)(2,1)S(1)}, u32[]{:S(2)}, u32[]{:S(2)}) collective-permute-start(bf16[128,384]{1,0:T(8,128)(2,1)S(1)} %slice.8.refs_4_), channel_id=1, source_target_pairs={{0,1},{1,0},{2,3},{3,2},{4,5},{5,4},{6,7},{7,6},{8,9},{9,8},{10,11... | collective-permute-start | bytes 294920 | tf_op jit(solution)/shard_map/ppermute | solution.py:233
  21.1 4.6 %collective-permute-start.6 = (bf16[128,384]{1,0:T(8,128)(2,1)S(1)}, bf16[128,384]{1,0:T(8,128)(2,1)S(1)}, u32[]{:S(2)}, u32[]{:S(2)}) collective-permute-start(bf16[128,384]{1,0:T(8,128)(2,1)S(1)} %collective-permute-done.4.refs_5_), channel_id=1, source_target_pairs={{0,1},{1,0},{2,3},{3,2},{4,5},{5,4},{6,7},{7,6},{8,9},{9,8},{10,11... | collective-permute-start | bytes 294920 | tf_op jit(solution)/shard_map/ppermute | solution.py:233
  26.7 3.0 %collective-permute-start.10 = (f32[512,384]{1,0:T(8,128)S(1)}, f32[512,384]{1,0:T(8,128)S(1)}, u32[]{:S(2)}, u32[]{:S(2)}) collective-permute-start(f32[512,384]{1,0:T(8,128)S(1)} %shard_map.70.refs_1_), channel_id=1, source_target_pairs={{0,4},{1,5},{2,6},{3,7},{4,0},{5,1},{6,2},{7,3},{8,12},{9,13},{10,... | collective-permute-start | bytes 2359304 | tf_op jit(solution)/shard_map/ppermute | solution.py:233
  26.7 2.9 %collective-permute-start.11 = (bf16[576,384]{1,0:T(8,128)(2,1)S(1)}, bf16[576,384]{1,0:T(8,128)(2,1)S(1)}, u32[]{:S(2)}, u32[]{:S(2)}) collective-permute-start(bf16[576,384]{1,0:T(8,128)(2,1)S(1)} %get-tuple-element.21.refs_3_), channel_id=1, source_target_pairs={{0,4},{1,5},{2,6},{3,7},{4,0},{5,1},{6,2},{7,3},{8,12},{9,13},{10,... | collective-permute-start | bytes 1327112 | tf_op jit(solution)/shard_map/ppermute | solution.py:233
  30.3 28.9 %copy-start = (s32[2,1]{0,1:T(1,128)S(1)}, s32[2,1]{0,1:T(1,128)}, u32[]{:S(2)}) copy-start(s32[2,1]{0,1:T(1,128)} %param.7) | copy-start | bytes 28
  30.3 4.9 %collective-permute-start.12 = (f32[192,128]{1,0:T(8,128)S(1)}, f32[192,128]{1,0:T(8,128)S(1)}, u32[]{:S(2)}, u32[]{:S(2)}) collective-permute-start(f32[192,128]{1,0:T(8,128)S(1)} %get-tuple-element.23), channel_id=1, source_target_pairs={{0,16},{1,17},{2,18},{3,19},{4,20},{5,21},{6,22},{7,23},{8,24},{9,... | collective-permute-start | bytes 294920 | tf_op jit(solution)/shard_map/ppermute | solution.py:233
  31.9 5.7 %collective-permute-start.14 = (bf16[128,384]{1,0:T(8,128)(2,1)S(1)}, bf16[128,384]{1,0:T(8,128)(2,1)S(1)}, u32[]{:S(2)}, u32[]{:S(2)}) collective-permute-start(bf16[128,384]{1,0:T(8,128)(2,1)S(1)} %get-tuple-element.24), channel_id=1, source_target_pairs={{0,0},{4,3},{1,5},{5,6},{6,2},{2,1},{7,7},{3,4},{8,8},{12,11},{9,1... | collective-permute-start | bytes 294920 | tf_op jit(solution)/shard_map/ppermute | solution.py:287
  32.5 12.4 %collective-permute-start.15 = (bf16[128,384]{1,0:T(8,128)(2,1)S(1)}, bf16[128,384]{1,0:T(8,128)(2,1)S(1)}, u32[]{:S(2)}, u32[]{:S(2)}) collective-permute-start(bf16[128,384]{1,0:T(8,128)(2,1)S(1)} %get-tuple-element.25), channel_id=1, source_target_pairs={{0,1},{4,2},{1,4},{5,7},{6,3},{2,0},{7,6},{3,5},{8,9},{12,10},{9,1... | collective-permute-start | bytes 294920 | tf_op jit(solution)/shard_map/ppermute | solution.py:288
  35.2 11.2 %collective-permute-start.13 = (f32[192,128]{1,0:T(8,128)S(1)}, f32[192,128]{1,0:T(8,128)S(1)}, u32[]{:S(2)}, u32[]{:S(2)}) collective-permute-start(f32[192,128]{1,0:T(8,128)S(1)} %shard_map.72.refs_0_), channel_id=1, source_target_pairs={{0,2},{1,3},{2,0},{3,1},{4,6},{5,7},{6,4},{7,5},{8,10},{9,11},{10,... | collective-permute-start | bytes 294920 | tf_op jit(solution)/shard_map/ppermute | solution.py:233
  44.9 4.7 %collective-permute-start.17 = (bf16[128,384]{1,0:T(8,128)(2,1)S(1)}, bf16[128,384]{1,0:T(8,128)(2,1)S(1)}, u32[]{:S(2)}, u32[]{:S(2)}) collective-permute-start(bf16[128,384]{1,0:T(8,128)(2,1)S(1)} %get-tuple-element.27), channel_id=1, source_target_pairs={{0,8},{1,9},{2,10},{3,11},{4,12},{5,13},{6,14},{7,15},{8,0},{9,1},... | collective-permute-start | bytes 294920 | tf_op jit(solution)/shard_map/ppermute | solution.py:233
  46.4 4.7 %collective-permute-start.16 = (f32[192,128]{1,0:T(8,128)S(1)}, f32[192,128]{1,0:T(8,128)S(1)}, u32[]{:S(2)}, u32[]{:S(2)}) collective-permute-start(f32[192,128]{1,0:T(8,128)S(1)} %shard_map.73.refs_0_), channel_id=1, source_target_pairs={{0,1},{1,0},{2,3},{3,2},{4,5},{5,4},{6,7},{7,6},{8,9},{9,8},{10,11... | collective-permute-start | bytes 294920 | tf_op jit(solution)/shard_map/ppermute | solution.py:233
  51.1 4.7 %collective-permute-start.18 = (f32[192,128]{1,0:T(8,128)S(1)}, f32[192,128]{1,0:T(8,128)S(1)}, u32[]{:S(2)}, u32[]{:S(2)}) collective-permute-start(f32[192,128]{1,0:T(8,128)S(1)} %shard_map.74.refs_0_), channel_id=1, source_target_pairs={{0,8},{1,9},{2,10},{3,11},{4,12},{5,13},{6,14},{7,15},{8,0},{9,1},... | collective-permute-start | bytes 294920 | tf_op jit(solution)/shard_map/ppermute | solution.py:233
  51.8 4.6 %collective-permute-start.19 = (f32[192,128]{1,0:T(8,128)S(1)}, f32[192,128]{1,0:T(8,128)S(1)}, u32[]{:S(2)}, u32[]{:S(2)}) collective-permute-start(f32[192,128]{1,0:T(8,128)S(1)} %shard_map.74.refs_0_), channel_id=1, source_target_pairs={{0,16},{1,17},{2,18},{3,19},{4,20},{5,21},{6,22},{7,23},{8,24},{9,... | collective-permute-start | bytes 294920 | tf_op jit(solution)/shard_map/ppermute | solution.py:233
  52.3 5.5 %collective-permute-start.20 = (f32[192,128]{1,0:T(8,128)S(1)}, f32[192,128]{1,0:T(8,128)S(1)}, u32[]{:S(2)}, u32[]{:S(2)}) collective-permute-start(f32[192,128]{1,0:T(8,128)S(1)} %shard_map.74.refs_0_), channel_id=1, source_target_pairs={{0,24},{1,25},{2,26},{3,27},{4,28},{5,29},{6,30},{7,31},{8,16},{9,... | collective-permute-start | bytes 294920 | tf_op jit(solution)/shard_map/ppermute | solution.py:233
  54.6 3.2 %collective-permute-start.21 = (f32[192,128]{1,0:T(8,128)S(1)}, f32[192,128]{1,0:T(8,128)S(1)}, u32[]{:S(2)}, u32[]{:S(2)}) collective-permute-start(f32[192,128]{1,0:T(8,128)S(1)} %shard_map.74.refs_0_), channel_id=1, source_target_pairs={{0,4},{1,5},{2,6},{3,7},{4,0},{5,1},{6,2},{7,3},{8,12},{9,13},{10,... | collective-permute-start | bytes 294920 | tf_op jit(solution)/shard_map/ppermute | solution.py:233
  55.8 2.1 %collective-permute-start.22 = (f32[192,128]{1,0:T(8,128)S(1)}, f32[192,128]{1,0:T(8,128)S(1)}, u32[]{:S(2)}, u32[]{:S(2)}) collective-permute-start(f32[192,128]{1,0:T(8,128)S(1)} %collective-permute-done.18.refs_1_), channel_id=1, source_target_pairs={{0,4},{1,5},{2,6},{3,7},{4,0},{5,1},{6,2},{7,3},{8,12},{9,13},{10,... | collective-permute-start | bytes 294920 | tf_op jit(solution)/shard_map/ppermute | solution.py:233
  56.4 1.4 %collective-permute-start.23 = (f32[192,128]{1,0:T(8,128)S(1)}, f32[192,128]{1,0:T(8,128)S(1)}, u32[]{:S(2)}, u32[]{:S(2)}) collective-permute-start(f32[192,128]{1,0:T(8,128)S(1)} %collective-permute-done.19.refs_2_), channel_id=1, source_target_pairs={{0,4},{1,5},{2,6},{3,7},{4,0},{5,1},{6,2},{7,3},{8,12},{9,13},{10,... | collective-permute-start | bytes 294920 | tf_op jit(solution)/shard_map/ppermute | solution.py:233
  57.8 1.3 %collective-permute-start.24 = (f32[192,128]{1,0:T(8,128)S(1)}, f32[192,128]{1,0:T(8,128)S(1)}, u32[]{:S(2)}, u32[]{:S(2)}) collective-permute-start(f32[192,128]{1,0:T(8,128)S(1)} %collective-permute-done.20.refs_3_), channel_id=1, source_target_pairs={{0,4},{1,5},{2,6},{3,7},{4,0},{5,1},{6,2},{7,3},{8,12},{9,13},{10,... | collective-permute-start | bytes 294920 | tf_op jit(solution)/shard_map/ppermute | solution.py:233

commit v7 on v6

--- a/solution.py
+++ b/solution.py
@@ -112,7 +112,9 @@
 
 
 def gather_kernel(*refs):
-    blocks, (own_inverse, got_inverse, rows, pack) = refs[:8], refs[8:]
+    blocks, (own_inverse, got_inverse, rows, pack) = [], refs[-4:]
+    for ref in refs[:-4]:
+        blocks += [ref] if len(ref.shape) == 2 else [ref.at[0], ref.at[1]]
     column = lax.axis_index("pcol")
     height = blocks[0].shape[0]
     for index, block in enumerate(blocks):
@@ -136,7 +138,7 @@
         at += own.shape[0]
 
 
-def couple_kernel(weight, mine, other, pack, got_pack, out_a, out_b, keep, send, half, packed):
+def couple_kernel(weight, mine, other, pack, got_pack, out_near, out_far, keep, send, half, packed):
     core, column, point = (lax.axis_index(name) for name in ("core", "pcol", "hyp"))
     applied = mine[...] + other[...]
     high = applied.astype(jnp.bfloat16)
@@ -170,10 +172,10 @@
     size = keep.shape[0]
     keep[...] = packed[pl.ds(pl.multiple_of(point * size, 8), size), :]
     send[...] = packed[pl.ds(pl.multiple_of((1 - point) * size, 8), size), :]
-    height = out_a.shape[0]
-    near = core == column // 2
-    for out, steps in ((out_a, (0, 3)), (out_b, (1, 2))):
-        spot = jnp.bitwise_xor(column, jnp.where(near, steps[0], steps[1]))
+    height = out_near.shape[0]
+    side = lax.axis_index("side")
+    for out, at in ((out_near, side), (out_far, 1 - side)):
+        spot = at * 2 + core
         out[...] = half[pl.ds(pl.multiple_of(spot * height, height), height), :]
 
 
@@ -182,7 +184,7 @@
 
 
 def finish_kernel(*refs):
-    parts, (live_hbm, mine, theirs, rows_out, out, live, block, lines, result, sems) = refs[:8], refs[8:]
+    parts, (live_hbm, near, far, rows_out, out, live, block, lines, result, sems) = refs[:8], refs[8:]
     point, side, core = (lax.axis_index(name) for name in ("hyp", "side", "core"))
     copy = pltpu.make_async_copy(live_hbm, live, sems.at[0])
     copy.start()
@@ -205,9 +207,9 @@
         copies.append(pltpu.make_async_copy(result.at[node], out.at[node], sems.at[1 + node]))
         copies[-1].start()
     copy.wait()
-    row = lax.broadcasted_iota(jnp.int32, mine.shape, 0)
-    first = side == 0
-    pair = (jnp.where(first, mine[...], theirs[...]), jnp.where(first, theirs[...], mine[...]))
+    row = lax.broadcasted_iota(jnp.int32, near.shape, 0)
+    first = lax.axis_index("pcol") // 2 == 0
+    pair = (jnp.where(first, near[...], far[...]), jnp.where(first, far[...], near[...]))
     for s, value in enumerate(pair):
         block[:, s, :] = jnp.where(row < live[s], value, jnp.zeros(value.shape, value.dtype))
     copies.append(pltpu.make_async_copy(block, rows_out.at[0], sems.at[3]))
@@ -220,7 +222,6 @@
     height, count, width = panel.shape[1:]
     grid = lax.axis_size("pcol")
     points = lax.axis_size("hyp")
-    point, side, core, column = (lax.axis_index(name) for name in AXES)
     f32, bf16 = jnp.float32, jnp.bfloat16
     shape = jax.ShapeDtypeStruct
     dma = pltpu.SemaphoreType.DMA
@@ -234,7 +235,7 @@
 
     extent = sigma_rows.shape[2]
     block = shape((height, width), bf16)
-    cuts = (extent * 9 // 16, extent * 7 // 32, extent * 7 // 32)
+    cuts = (extent * 25 // 32, extent * 7 // 32)
     size = pl.cdiv(inv_diag.shape[2], ROWS) * ROWS
     own, give, own_inverse, *pieces = call(
         start_kernel,
@@ -250,13 +251,13 @@
     got, got_inverse = got[:height], got[height:]
     blocks = []
     for start in (own, got):
-        second = swap(start, column=2)
-        blocks += [start, second, swap(start, column=1), swap(second, column=1)]
+        pair = jnp.stack([start, swap(start, column=2)])
+        blocks += [pair, swap(pair, column=1)]
     far = [swap(piece, side=1) for piece in pieces]
 
     pack = shape((extent + 2 * size, width), bf16)
     rows, pack = call(
-        gather_kernel, [shape((2, extent, width), bf16), pack], [VMEM] * 10,
+        gather_kernel, [shape((2, extent, width), bf16), pack], [VMEM] * (2 + len(blocks)),
         *blocks, own_inverse, got_inverse,
     )
     got_pack = swap(pack, core=1)
@@ -267,40 +268,32 @@
 
     lines = len(tiles(width)) // 2 * LANES
     part = shape((lines // 2, LANES), f32)
-    out_a, out_b, keep, send = call(
+    out_near, out_far, keep, send = call(
         couple_kernel, [block, block, part, part], [SMEM] + [VMEM] * 4,
         quad_weight, mine, other, pack, got_pack,
         scratch=[pltpu.VMEM((extent, width), bf16), pltpu.VMEM((lines, LANES), f32)],
     )
     came = swap(send, point=1)
 
-    def output_pairs(steps):
+    def deliver(x, flip):
         pairs = []
-        for h in range(points):
-            for s in range(2):
-                for c in range(grid):
-                    for core, step in ((c // 2, steps[0]), (1 - c // 2, steps[1])):
-                        base = (h * 2 + s) * 2
-                        pairs.append(((base + core) * grid + c, (base + c % 2) * grid + (c ^ step)))
-        return pairs
-
-    land_a = lax.ppermute(out_a, AXES, output_pairs((0, 3)))
-    land_b = lax.ppermute(out_b, AXES, output_pairs((1, 2)))
-    from_a = jnp.where(column % 2 == core, column, column ^ 3) // 2
-
+        for i in range(devices):
+            h, s, k, c = i // (4 * grid), i // (2 * grid) % 2, i // grid % 2, i % grid
+            pairs.append((i, (h * 4 + c) * grid + 2 * (s ^ flip) + k))
+        return lax.ppermute(x, AXES, pairs)
+
+    near, far = deliver(out_near, 0), deliver(out_far, 1)
     add = functools.partial(call, add_kernel, part, [VMEM] * 2)
     total = add(keep, came)
-    total = add(total, swap(total, column=2), after=[land_a, land_b])
-    theirs = swap(jnp.where(from_a == side, land_b, land_a), side=1)
-    total = add(total, swap(total, column=1), after=[theirs])
+    total = add(total, swap(total, column=1), after=[near, far])
+    total = add(total, swap(total, column=2))
     quarters = [total, swap(total, side=1), swap(total, point=1), swap(total, side=1, point=1)]
     quarters += [swap(x, core=1) for x in quarters]
-    mine = jnp.where(from_a == side, land_a, land_b)
     return call(
         finish_kernel,
         [shape((1, height, count, width), bf16), shape((count, width, width), f32)],
         [VMEM] * 8 + [HBM] + [VMEM] * 2,
-        *quarters, live, mine, theirs,
+        *quarters, live, near, far,
         scratch=[
             pltpu.SMEM((2,), jnp.int32),
             pltpu.VMEM((height, count, width), bf16),

time: 60.9 us -> 61.7 us (1.013)
  waiting for transfers between devices: 27.8 us -> 29.6 us
  starting transfers between devices: 26.4 us -> 25.6 us
    ppermute x23 -> x19, waiting for transfers between devices: 20.5 us -> 24.9 us  [swap(): return lax.ppermute(x, AXES, [(i, i ^ mask) for i in range(devices)])]
    ppermute x2, waiting for transfers between devices: 7.36 us -> 4.68 us  [deliver(): return lax.ppermute(x, AXES, pairs)]
    ppermute x23 -> x19, starting transfers between devices: 23.3 us -> 21.1 us  [swap(): return lax.ppermute(x, AXES, [(i, i ^ mask) for i in range(devices)])]
    ppermute x2, starting transfers between devices: 3.12 us -> 4.55 us  [deliver(): return lax.ppermute(x, AXES, pairs)]
  transfers between devices with their start and end apart: 25 -> 21, of which waited for: 14 -> 13; matrix products, arithmetic and copies ran while one was open for 0% -> 0% of each run, Pallas kernels for 0% -> 0%
where the time goes in v7:
time: 61.7 us; the launch traced here: 61.5 us
  waiting for transfers between devices  29.6 us (48%)
  starting transfers between devices  25.6 us (41%)
  Pallas kernels  4.87 us (8%)
  between operations  1.39 us (2%)
    ppermute x19, waiting for transfers between devices, swap(): return lax.ppermute(x, AXES, [(i, i ^ mask) for i in range(devices)])  24.9 us
    ppermute x19, starting transfers between devices, swap(): return lax.ppermute(x, AXES, [(i, i ^ mask) for i in range(devices)])  21.1 us
    pallas_call x8, Pallas kernels, call(): pl.pallas_call(body, out_shape=outs, in_specs=list(specs) + [ANY] * len(a...  4.87 us
    ppermute x2, waiting for transfers between devices, deliver(): return lax.ppermute(x, AXES, pairs)  4.68 us
    ppermute x2, starting transfers between devices, deliver(): return lax.ppermute(x, AXES, pairs)  4.55 us
  transfers between devices with their start and end apart: 21, of which 13 were waited for; matrix products, arithmetic and copies ran while one was open for 0% of the time, Pallas kernels for 0%

profile of v7, /device:TPU:0, one launch (start us, length us, event | category | flops | bytes accessed | tf_op | source)
XLA Modules:
  0.0 61.5 jit_solution(5374261790346699182)
XLA Ops:
  0.6 1.8 %shard_map.68 = (bf16[128,384]{1,0:T(8,128)(2,1)S(1)}, bf16[160,384]{1,0:T(8,128)(2,1)S(1)}, bf16[32,384]{1,0:T(8,128)(2,1)S(1)}, bf16[400,512]{1,0:T(8,128)(2,1)S(1)}, bf16[112,512]{1,0:T(8,128)(2,1)S(1)}) custom-call(s32[2]{0:T(128)} %bitcast.7, bf16[1,128,2,384]{3,2,1,0:T(2,128)(2,1)} %refs_1_.1, bf16[1,2,24,384]{3,2,1,0:T(8,128)(2,1)} %refs_2_.1, ...), custom_call_target="tpu_custom_call" | custom-call | tf_op jit(solution)/shard_map/pallas_call | solution.py:28
  2.5 3.0 %collective-permute-start.2 = (bf16[160,384]{1,0:T(8,128)(2,1)S(1)}, bf16[160,384]{1,0:T(8,128)(2,1)S(1)}, u32[]{:S(2)}, u32[]{:S(2)}) collective-permute-start(bf16[160,384]{1,0:T(8,128)(2,1)S(1)} %get-tuple-element.14), channel_id=1, source_target_pairs={{0,8},{1,9},{2,10},{3,11},{4,12},{5,13},{6,14},{7,15},{8,0},{9,1},... | collective-permute-start | bytes 368648 | tf_op jit(solution)/shard_map/ppermute | solution.py:234
  5.5 2.6 %collective-permute-start = (bf16[128,384]{1,0:T(8,128)(2,1)S(1)}, bf16[128,384]{1,0:T(8,128)(2,1)S(1)}, u32[]{:S(2)}, u32[]{:S(2)}) collective-permute-start(bf16[128,384]{1,0:T(8,128)(2,1)S(1)} %get-tuple-element.13), channel_id=1, source_target_pairs={{0,2},{1,3},{2,0},{3,1},{4,6},{5,7},{6,4},{7,5},{8,10},{9,11},{10,... | collective-permute-start | bytes 294920 | tf_op jit(solution)/shard_map/ppermute | solution.py:234
  8.1 0.5 collective-permute-start.5
  8.8 4.0 %collective-permute-start.3 = (bf16[128,384]{1,0:T(8,128)(2,1)S(1)}, bf16[128,384]{1,0:T(8,128)(2,1)S(1)}, u32[]{:S(2)}, u32[]{:S(2)}) collective-permute-start(bf16[128,384]{1,0:T(8,128)(2,1)S(1)} %get-tuple-element.25), channel_id=1, source_target_pairs={{0,2},{1,3},{2,0},{3,1},{4,6},{5,7},{6,4},{7,5},{8,10},{9,11},{10,... | collective-permute-start | bytes 294920 | tf_op jit(solution)/shard_map/ppermute | solution.py:234
  12.9 1.6 %collective-permute-done = bf16[128,384]{1,0:T(8,128)(2,1)S(1)} collective-permute-done((bf16[128,384]{1,0:T(8,128)(2,1)S(1)}, bf16[128,384]{1,0:T(8,128)(2,1)S(1)}, u32[]{:S(2)}, u32[]{:S(2)}) %collective-permute-start) | collective-permute-done | bytes 98336 | tf_op jit(solution)/shard_map/ppermute | solution.py:234
  14.5 0.4 collective-permute-start.1
  15.0 2.1 %collective-permute-done.3 = bf16[128,384]{1,0:T(8,128)(2,1)S(1)} collective-permute-done((bf16[128,384]{1,0:T(8,128)(2,1)S(1)}, bf16[128,384]{1,0:T(8,128)(2,1)S(1)}, u32[]{:S(2)}, u32[]{:S(2)}) %collective-permute-start.3) | collective-permute-done | bytes 98336 | tf_op jit(solution)/shard_map/ppermute | solution.py:234
  17.1 0.7 %collective-permute-start.4 = (bf16[2,128,384]{2,1,0:T(8,128)(2,1)S(1)}, bf16[2,128,384]{2,1,0:T(8,128)(2,1)S(1)}, u32[]{:S(2)}, u32[]{:S(2)}) collective-permute-start(bf16[2,128,384]{2,1,0:T(8,128)(2,1)S(1)} %pad_maximum_fusion.1.refs_2_), channel_id=1, source_target_pairs={{0,1},{1,0},{2,3},{3,2},{4,5},{5,4},{6,7},{7,6},{8,9},{9,8},{10,11... | collective-permute-start | bytes 589832 | tf_op jit(solution)/shard_map/ppermute | solution.py:234
  17.7 1.5 %collective-permute-start.6 = (bf16[112,512]{1,0:T(8,128)(2,1)S(1)}, bf16[112,512]{1,0:T(8,128)(2,1)S(1)}, u32[]{:S(2)}, u32[]{:S(2)}) collective-permute-start(bf16[112,512]{1,0:T(8,128)(2,1)S(1)} %get-tuple-element.18.refs_2_), channel_id=1, source_target_pairs={{0,8},{1,9},{2,10},{3,11},{4,12},{5,13},{6,14},{7,15},{8,0},{9,1},... | collective-permute-start | bytes 344072 | tf_op jit(solution)/shard_map/ppermute | solution.py:234
  19.2 3.0 %collective-permute-done.1.refs_1_ = bf16[2,128,384]{2,1,0:T(8,128)(2,1)S(1)} collective-permute-done((bf16[2,128,384]{2,1,0:T(8,128)(2,1)S(1)}, bf16[2,128,384]{2,1,0:T(8,128)(2,1)S(1)}, u32[]{:S(2)}, u32[]{:S(2)}) %collective-permute-start.1) | collective-permute-done | bytes 196640 | tf_op jit(solution)/shard_map/ppermute | solution.py:234
  22.2 2.1 %collective-permute-done.4.refs_3_ = bf16[2,128,384]{2,1,0:T(8,128)(2,1)S(1)} collective-permute-done((bf16[2,128,384]{2,1,0:T(8,128)(2,1)S(1)}, bf16[2,128,384]{2,1,0:T(8,128)(2,1)S(1)}, u32[]{:S(2)}, u32[]{:S(2)}) %collective-permute-start.4) | collective-permute-done | bytes 196640 | tf_op jit(solution)/shard_map/ppermute | solution.py:234
  24.4 0.7 %shard_map.70.refs_1_ = f32[512,384]{1,0:T(8,128)S(1)} custom-call(bf16[2,512,384]{2,1,0:T(8,128)(2,1)S(1)} %get-tuple-element.16.refs_0_, bf16[400,512]{1,0:T(8,128)(2,1)S(1)} %get-tuple-element.17.refs_1_, bf16[112,512]{1,0:T(8,128)(2,1)S(1)} %get-tuple-element.18.refs_2_, bf16[400,512]{1,0:T(8,128)(2,1)S(1)} %collective-permute-done.5.refs_3_, ...), custom_call_target="tpu_custom_call" | custom-call | tf_op jit(solution)/shard_map/pallas_call | solution.py:28
  25.3 0.5 collective-permute-start.8
  26.4 1.7 %collective-permute-done.8.refs_4_ = bf16[576,384]{1,0:T(8,128)(2,1)S(1)} collective-permute-done((bf16[576,384]{1,0:T(8,128)(2,1)S(1)}, bf16[576,384]{1,0:T(8,128)(2,1)S(1)}, u32[]{:S(2)}, u32[]{:S(2)}) %collective-permute-start.8) | collective-permute-done | bytes 442400 | tf_op jit(solution)/shard_map/ppermute | solution.py:234
  28.2 0.6 %shard_map.71 = (bf16[128,384]{1,0:T(8,128)(2,1)S(1)}, bf16[128,384]{1,0:T(8,128)(2,1)S(1)}, f32[192,128]{1,0:T(8,128)S(1)}, f32[192,128]{1,0:T(8,128)S(1)}) custom-call(f32[1]{0:T(128)S(6)} %copy.7.refs_0_, f32[512,384]{1,0:T(8,128)S(1)} %shard_map.70.refs_1_, f32[512,384]{1,0:T(8,128)S(1)} %collective-permute-done.7.refs_2_, ...), custom_call_target="tpu_custom_call" | custom-call | tf_op jit(solution)/shard_map/pallas_call | solution.py:28
  28.8 1.6 %collective-permute-start.9 = (f32[192,128]{1,0:T(8,128)S(1)}, f32[192,128]{1,0:T(8,128)S(1)}, u32[]{:S(2)}, u32[]{:S(2)}) collective-permute-start(f32[192,128]{1,0:T(8,128)S(1)} %get-tuple-element.21), channel_id=1, source_target_pairs={{0,16},{1,17},{2,18},{3,19},{4,20},{5,21},{6,22},{7,23},{8,24},{9,... | collective-permute-start | bytes 294920 | tf_op jit(solution)/shard_map/ppermute | solution.py:234
  30.4 0.7 %collective-permute-start.11 = (bf16[128,384]{1,0:T(8,128)(2,1)S(1)}, bf16[128,384]{1,0:T(8,128)(2,1)S(1)}, u32[]{:S(2)}, u32[]{:S(2)}) collective-permute-start(bf16[128,384]{1,0:T(8,128)(2,1)S(1)} %get-tuple-element.22), channel_id=1, source_target_pairs={{0,0},{1,4},{2,8},{3,12},{4,1},{5,5},{6,9},{7,13},{8,2},{9,6},{10,... | collective-permute-start | bytes 294920 | tf_op jit(solution)/shard_map/ppermute | solution.py:283
  31.0 3.9 %collective-permute-start.12 = (bf16[128,384]{1,0:T(8,128)(2,1)S(1)}, bf16[128,384]{1,0:T(8,128)(2,1)S(1)}, u32[]{:S(2)}, u32[]{:S(2)}) collective-permute-start(bf16[128,384]{1,0:T(8,128)(2,1)S(1)} %get-tuple-element.23), channel_id=1, source_target_pairs={{0,2},{1,6},{2,10},{3,14},{4,3},{5,7},{6,11},{7,15},{8,0},{9,4},{1... | collective-permute-start | bytes 294920 | tf_op jit(solution)/shard_map/ppermute | solution.py:283
  34.9 0.4 collective-permute-start.10
  35.4 4.7 %collective-permute-done.12.refs_3_.refs_10_ = bf16[128,384]{1,0:T(8,128)(2,1)S(1)} collective-permute-done((bf16[128,384]{1,0:T(8,128)(2,1)S(1)}, bf16[128,384]{1,0:T(8,128)(2,1)S(1)}, u32[]{:S(2)}, u32[]{:S(2)}) %collective-permute-start.12) | collective-permute-done | bytes 98336 | tf_op jit(solution)/shard_map/ppermute | solution.py:283
  40.0 1.7 %collective-permute-done.10.refs_1_ = f32[192,128]{1,0:T(8,128)S(1)} collective-permute-done((f32[192,128]{1,0:T(8,128)S(1)}, f32[192,128]{1,0:T(8,128)S(1)}, u32[]{:S(2)}, u32[]{:S(2)}) %collective-permute-start.10) | collective-permute-done | bytes 98336 | tf_op jit(solution)/shard_map/ppermute | solution.py:234
  41.7 1.5 %collective-permute-start.13 = (f32[192,128]{1,0:T(8,128)S(1)}, f32[192,128]{1,0:T(8,128)S(1)}, u32[]{:S(2)}, u32[]{:S(2)}) collective-permute-start(f32[192,128]{1,0:T(8,128)S(1)} %shard_map.73.refs_0_), channel_id=1, source_target_pairs={{0,2},{1,3},{2,0},{3,1},{4,6},{5,7},{6,4},{7,5},{8,10},{9,11},{10,... | collective-permute-start | bytes 294920 | tf_op jit(solution)/shard_map/ppermute | solution.py:234
  43.3 6.4 %collective-permute-done.13.refs_1_ = f32[192,128]{1,0:T(8,128)S(1)} collective-permute-done((f32[192,128]{1,0:T(8,128)S(1)}, f32[192,128]{1,0:T(8,128)S(1)}, u32[]{:S(2)}, u32[]{:S(2)}) %collective-permute-start.13) | collective-permute-done | bytes 98336 | tf_op jit(solution)/shard_map/ppermute | solution.py:234
  49.6 2.1 %collective-permute-start.14 = (f32[192,128]{1,0:T(8,128)S(1)}, f32[192,128]{1,0:T(8,128)S(1)}, u32[]{:S(2)}, u32[]{:S(2)}) collective-permute-start(f32[192,128]{1,0:T(8,128)S(1)} %shard_map.74.refs_0_), channel_id=1, source_target_pairs={{0,8},{1,9},{2,10},{3,11},{4,12},{5,13},{6,14},{7,15},{8,0},{9,1},... | collective-permute-start | bytes 294920 | tf_op jit(solution)/shard_map/ppermute | solution.py:234
  51.8 0.5 collective-permute-start.15
  52.3 1.0 %collective-permute-start.16 = (f32[192,128]{1,0:T(8,128)S(1)}, f32[192,128]{1,0:T(8,128)S(1)}, u32[]{:S(2)}, u32[]{:S(2)}) collective-permute-start(f32[192,128]{1,0:T(8,128)S(1)} %shard_map.74.refs_0_), channel_id=1, source_target_pairs={{0,24},{1,25},{2,26},{3,27},{4,28},{5,29},{6,30},{7,31},{8,16},{9,... | collective-permute-start | bytes 294920 | tf_op jit(solution)/shard_map/ppermute | solution.py:234
  53.3 1.6 %collective-permute-done.14.refs_1_ = f32[192,128]{1,0:T(8,128)S(1)} collective-permute-done((f32[192,128]{1,0:T(8,128)S(1)}, f32[192,128]{1,0:T(8,128)S(1)}, u32[]{:S(2)}, u32[]{:S(2)}) %collective-permute-start.14) | collective-permute-done | bytes 98336 | tf_op jit(solution)/shard_map/ppermute | solution.py:234
  54.9 3.5 %collective-permute-done.15.refs_2_ = f32[192,128]{1,0:T(8,128)S(1)} collective-permute-done((f32[192,128]{1,0:T(8,128)S(1)}, f32[192,128]{1,0:T(8,128)S(1)}, u32[]{:S(2)}, u32[]{:S(2)}) %collective-permute-start.15) | collective-permute-done | bytes 98336 | tf_op jit(solution)/shard_map/ppermute | solution.py:234
  58.5 0.5 collective-permute-start.20
  59.0 0.8 %collective-permute-done.19.refs_6_ = f32[192,128]{1,0:T(8,128)S(1)} collective-permute-done((f32[192,128]{1,0:T(8,128)S(1)}, f32[192,128]{1,0:T(8,128)S(1)}, u32[]{:S(2)}, u32[]{:S(2)}) %collective-permute-start.19) | collective-permute-done | bytes 98336 | tf_op jit(solution)/shard_map/ppermute | solution.py:234
  60.0 1.6 %shard_map.75 = (bf16[1,128,2,384]{3,2,1,0:T(2,128)(2,1)}, f32[2,384,384]{2,1,0:T(8,128)}) custom-call(f32[192,128]{1,0:T(8,128)S(1)} %shard_map.74.refs_0_, f32[192,128]{1,0:T(8,128)S(1)} %collective-permute-done.14.refs_1_, f32[192,128]{1,0:T(8,128)S(1)} %collective-permute-done.15.refs_2_, f32[192,128]{1,0:T(8,128)S(1)} %collective-permute-done.16.refs_3_, ...), custom_call_target="tpu_custom_call" | custom-call | tf_op jit(solution)/shard_map/pallas_call | solution.py:28
  (24 shorter events, 0.7 us)
Async XLA Ops:
  2.5 6.3 %collective-permute-start.2 = (bf16[160,384]{1,0:T(8,128)(2,1)S(1)}, bf16[160,384]{1,0:T(8,128)(2,1)S(1)}, u32[]{:S(2)}, u32[]{:S(2)}) collective-permute-start(bf16[160,384]{1,0:T(8,128)(2,1)S(1)} %get-tuple-element.14), channel_id=1, source_target_pairs={{0,8},{1,9},{2,10},{3,11},{4,12},{5,13},{6,14},{7,15},{8,0},{9,1},... | collective-permute-start | bytes 368648 | tf_op jit(solution)/shard_map/ppermute | solution.py:234
  5.5 9.0 %collective-permute-start = (bf16[128,384]{1,0:T(8,128)(2,1)S(1)}, bf16[128,384]{1,0:T(8,128)(2,1)S(1)}, u32[]{:S(2)}, u32[]{:S(2)}) collective-permute-start(bf16[128,384]{1,0:T(8,128)(2,1)S(1)} %get-tuple-element.13), channel_id=1, source_target_pairs={{0,2},{1,3},{2,0},{3,1},{4,6},{5,7},{6,4},{7,5},{8,10},{9,11},{10,... | collective-permute-start | bytes 294920 | tf_op jit(solution)/shard_map/ppermute | solution.py:234
  8.1 16.4 %collective-permute-start.5 = (bf16[400,512]{1,0:T(8,128)(2,1)S(1)}, bf16[400,512]{1,0:T(8,128)(2,1)S(1)}, u32[]{:S(2)}, u32[]{:S(2)}) collective-permute-start(bf16[400,512]{1,0:T(8,128)(2,1)S(1)} %get-tuple-element.17.refs_1_), channel_id=1, source_target_pairs={{0,8},{1,9},{2,10},{3,11},{4,12},{5,13},{6,14},{7,15},{8,0},{9,1},... | collective-permute-start | bytes 1228808 | tf_op jit(solution)/shard_map/ppermute | solution.py:234
  8.8 8.2 %collective-permute-start.3 = (bf16[128,384]{1,0:T(8,128)(2,1)S(1)}, bf16[128,384]{1,0:T(8,128)(2,1)S(1)}, u32[]{:S(2)}, u32[]{:S(2)}) collective-permute-start(bf16[128,384]{1,0:T(8,128)(2,1)S(1)} %get-tuple-element.25), channel_id=1, source_target_pairs={{0,2},{1,3},{2,0},{3,1},{4,6},{5,7},{6,4},{7,5},{8,10},{9,11},{10,... | collective-permute-start | bytes 294920 | tf_op jit(solution)/shard_map/ppermute | solution.py:234
  14.5 7.7 %collective-permute-start.1 = (bf16[2,128,384]{2,1,0:T(8,128)(2,1)S(1)}, bf16[2,128,384]{2,1,0:T(8,128)(2,1)S(1)}, u32[]{:S(2)}, u32[]{:S(2)}) collective-permute-start(bf16[2,128,384]{2,1,0:T(8,128)(2,1)S(1)} %pad_maximum_fusion.refs_0_), channel_id=1, source_target_pairs={{0,1},{1,0},{2,3},{3,2},{4,5},{5,4},{6,7},{7,6},{8,9},{9,8},{10,11... | collective-permute-start | bytes 589832 | tf_op jit(solution)/shard_map/ppermute | solution.py:234
  17.1 7.2 %collective-permute-start.4 = (bf16[2,128,384]{2,1,0:T(8,128)(2,1)S(1)}, bf16[2,128,384]{2,1,0:T(8,128)(2,1)S(1)}, u32[]{:S(2)}, u32[]{:S(2)}) collective-permute-start(bf16[2,128,384]{2,1,0:T(8,128)(2,1)S(1)} %pad_maximum_fusion.1.refs_2_), channel_id=1, source_target_pairs={{0,1},{1,0},{2,3},{3,2},{4,5},{5,4},{6,7},{7,6},{8,9},{9,8},{10,11... | collective-permute-start | bytes 589832 | tf_op jit(solution)/shard_map/ppermute | solution.py:234
  17.7 6.7 %collective-permute-start.6 = (bf16[112,512]{1,0:T(8,128)(2,1)S(1)}, bf16[112,512]{1,0:T(8,128)(2,1)S(1)}, u32[]{:S(2)}, u32[]{:S(2)}) collective-permute-start(bf16[112,512]{1,0:T(8,128)(2,1)S(1)} %get-tuple-element.18.refs_2_), channel_id=1, source_target_pairs={{0,8},{1,9},{2,10},{3,11},{4,12},{5,13},{6,14},{7,15},{8,0},{9,1},... | collective-permute-start | bytes 344072 | tf_op jit(solution)/shard_map/ppermute | solution.py:234
  25.2 3.0 %collective-permute-start.7 = (f32[512,384]{1,0:T(8,128)S(1)}, f32[512,384]{1,0:T(8,128)S(1)}, u32[]{:S(2)}, u32[]{:S(2)}) collective-permute-start(f32[512,384]{1,0:T(8,128)S(1)} %shard_map.70.refs_1_), channel_id=1, source_target_pairs={{0,4},{1,5},{2,6},{3,7},{4,0},{5,1},{6,2},{7,3},{8,12},{9,13},{10,... | collective-permute-start | bytes 2359304 | tf_op jit(solution)/shard_map/ppermute | solution.py:234
  25.3 2.9 %collective-permute-start.8 = (bf16[576,384]{1,0:T(8,128)(2,1)S(1)}, bf16[576,384]{1,0:T(8,128)(2,1)S(1)}, u32[]{:S(2)}, u32[]{:S(2)}) collective-permute-start(bf16[576,384]{1,0:T(8,128)(2,1)S(1)} %get-tuple-element.19.refs_3_), channel_id=1, source_target_pairs={{0,4},{1,5},{2,6},{3,7},{4,0},{5,1},{6,2},{7,3},{8,12},{9,13},{10,... | collective-permute-start | bytes 1327112 | tf_op jit(solution)/shard_map/ppermute | solution.py:234
  26.4 33.6 %copy-start = (s32[2,1]{0,1:T(1,128)S(1)}, s32[2,1]{0,1:T(1,128)}, u32[]{:S(2)}) copy-start(s32[2,1]{0,1:T(1,128)} %param.7) | copy-start | bytes 28
  28.8 6.1 %collective-permute-start.9 = (f32[192,128]{1,0:T(8,128)S(1)}, f32[192,128]{1,0:T(8,128)S(1)}, u32[]{:S(2)}, u32[]{:S(2)}) collective-permute-start(f32[192,128]{1,0:T(8,128)S(1)} %get-tuple-element.21), channel_id=1, source_target_pairs={{0,16},{1,17},{2,18},{3,19},{4,20},{5,21},{6,22},{7,23},{8,24},{9,... | collective-permute-start | bytes 294920 | tf_op jit(solution)/shard_map/ppermute | solution.py:234
  30.4 5.0 %collective-permute-start.11 = (bf16[128,384]{1,0:T(8,128)(2,1)S(1)}, bf16[128,384]{1,0:T(8,128)(2,1)S(1)}, u32[]{:S(2)}, u32[]{:S(2)}) collective-permute-start(bf16[128,384]{1,0:T(8,128)(2,1)S(1)} %get-tuple-element.22), channel_id=1, source_target_pairs={{0,0},{1,4},{2,8},{3,12},{4,1},{5,5},{6,9},{7,13},{8,2},{9,6},{10,... | collective-permute-start | bytes 294920 | tf_op jit(solution)/shard_map/ppermute | solution.py:283
  31.0 9.0 %collective-permute-start.12 = (bf16[128,384]{1,0:T(8,128)(2,1)S(1)}, bf16[128,384]{1,0:T(8,128)(2,1)S(1)}, u32[]{:S(2)}, u32[]{:S(2)}) collective-permute-start(bf16[128,384]{1,0:T(8,128)(2,1)S(1)} %get-tuple-element.23), channel_id=1, source_target_pairs={{0,2},{1,6},{2,10},{3,14},{4,3},{5,7},{6,11},{7,15},{8,0},{9,4},{1... | collective-permute-start | bytes 294920 | tf_op jit(solution)/shard_map/ppermute | solution.py:283
  34.9 6.8 %collective-permute-start.10 = (f32[192,128]{1,0:T(8,128)S(1)}, f32[192,128]{1,0:T(8,128)S(1)}, u32[]{:S(2)}, u32[]{:S(2)}) collective-permute-start(f32[192,128]{1,0:T(8,128)S(1)} %shard_map.72.refs_0_), channel_id=1, source_target_pairs={{0,1},{1,0},{2,3},{3,2},{4,5},{5,4},{6,7},{7,6},{8,9},{9,8},{10,11... | collective-permute-start | bytes 294920 | tf_op jit(solution)/shard_map/ppermute | solution.py:234
  41.7 7.9 %collective-permute-start.13 = (f32[192,128]{1,0:T(8,128)S(1)}, f32[192,128]{1,0:T(8,128)S(1)}, u32[]{:S(2)}, u32[]{:S(2)}) collective-permute-start(f32[192,128]{1,0:T(8,128)S(1)} %shard_map.73.refs_0_), channel_id=1, source_target_pairs={{0,2},{1,3},{2,0},{3,1},{4,6},{5,7},{6,4},{7,5},{8,10},{9,11},{10,... | collective-permute-start | bytes 294920 | tf_op jit(solution)/shard_map/ppermute | solution.py:234
  49.6 5.3 %collective-permute-start.14 = (f32[192,128]{1,0:T(8,128)S(1)}, f32[192,128]{1,0:T(8,128)S(1)}, u32[]{:S(2)}, u32[]{:S(2)}) collective-permute-start(f32[192,128]{1,0:T(8,128)S(1)} %shard_map.74.refs_0_), channel_id=1, source_target_pairs={{0,8},{1,9},{2,10},{3,11},{4,12},{5,13},{6,14},{7,15},{8,0},{9,1},... | collective-permute-start | bytes 294920 | tf_op jit(solution)/shard_map/ppermute | solution.py:234
  51.8 6.7 %collective-permute-start.15 = (f32[192,128]{1,0:T(8,128)S(1)}, f32[192,128]{1,0:T(8,128)S(1)}, u32[]{:S(2)}, u32[]{:S(2)}) collective-permute-start(f32[192,128]{1,0:T(8,128)S(1)} %shard_map.74.refs_0_), channel_id=1, source_target_pairs={{0,16},{1,17},{2,18},{3,19},{4,20},{5,21},{6,22},{7,23},{8,24},{9,... | collective-permute-start | bytes 294920 | tf_op jit(solution)/shard_map/ppermute | solution.py:234
  52.3 6.2 %collective-permute-start.16 = (f32[192,128]{1,0:T(8,128)S(1)}, f32[192,128]{1,0:T(8,128)S(1)}, u32[]{:S(2)}, u32[]{:S(2)}) collective-permute-start(f32[192,128]{1,0:T(8,128)S(1)} %shard_map.74.refs_0_), channel_id=1, source_target_pairs={{0,24},{1,25},{2,26},{3,27},{4,28},{5,29},{6,30},{7,31},{8,16},{9,... | collective-permute-start | bytes 294920 | tf_op jit(solution)/shard_map/ppermute | solution.py:234
  53.3 5.7 %collective-permute-start.17 = (f32[192,128]{1,0:T(8,128)S(1)}, f32[192,128]{1,0:T(8,128)S(1)}, u32[]{:S(2)}, u32[]{:S(2)}) collective-permute-start(f32[192,128]{1,0:T(8,128)S(1)} %shard_map.74.refs_0_), channel_id=1, source_target_pairs={{0,4},{1,5},{2,6},{3,7},{4,0},{5,1},{6,2},{7,3},{8,12},{9,13},{10,... | collective-permute-start | bytes 294920 | tf_op jit(solution)/shard_map/ppermute | solution.py:234
  54.9 4.1 %collective-permute-start.18 = (f32[192,128]{1,0:T(8,128)S(1)}, f32[192,128]{1,0:T(8,128)S(1)}, u32[]{:S(2)}, u32[]{:S(2)}) collective-permute-start(f32[192,128]{1,0:T(8,128)S(1)} %collective-permute-done.14.refs_1_), channel_id=1, source_target_pairs={{0,4},{1,5},{2,6},{3,7},{4,0},{5,1},{6,2},{7,3},{8,12},{9,13},{10,... | collective-permute-start | bytes 294920 | tf_op jit(solution)/shard_map/ppermute | solution.py:234
  58.5 1.3 %collective-permute-start.19 = (f32[192,128]{1,0:T(8,128)S(1)}, f32[192,128]{1,0:T(8,128)S(1)}, u32[]{:S(2)}, u32[]{:S(2)}) collective-permute-start(f32[192,128]{1,0:T(8,128)S(1)} %collective-permute-done.15.refs_2_), channel_id=1, source_target_pairs={{0,4},{1,5},{2,6},{3,7},{4,0},{5,1},{6,2},{7,3},{8,12},{9,13},{10,... | collective-permute-start | bytes 294920 | tf_op jit(solution)/shard_map/ppermute | solution.py:234
  58.5 1.5 %collective-permute-start.20 = (f32[192,128]{1,0:T(8,128)S(1)}, f32[192,128]{1,0:T(8,128)S(1)}, u32[]{:S(2)}, u32[]{:S(2)}) collective-permute-start(f32[192,128]{1,0:T(8,128)S(1)} %collective-permute-done.16.refs_3_), channel_id=1, source_target_pairs={{0,4},{1,5},{2,6},{3,7},{4,0},{5,1},{6,2},{7,3},{8,12},{9,13},{10,... | collective-permute-start | bytes 294920 | tf_op jit(solution)/shard_map/ppermute | solution.py:234

commit v8 on v7

--- a/solution.py
+++ b/solution.py
@@ -82,16 +82,16 @@
 
 
 def start_kernel(*refs):
-    sources, (own, give, own_inverse), pieces, buffers, sems = refs[:4], refs[4:7], refs[7:-5], refs[-5:-1], refs[-1]
+    sources, (own, give, own_inverse), buffers, sems = refs[:3], refs[3:6], refs[6:9], refs[9]
     copies = [
         pltpu.make_async_copy(source, buffer, sems.at[index])
         for index, (source, buffer) in enumerate(zip(sources, buffers))
     ]
     for copy in copies:
         copy.start()
-    for copy in copies[:3]:
+    for copy in copies:
         copy.wait()
-    live, panel, inverse, matrix = buffers
+    live, panel, inverse = buffers
     first = lax.axis_index("side") == 0
     row = lax.broadcasted_iota(jnp.int32, own.shape, 0)
     rows = panel[0]
@@ -104,11 +104,21 @@
     one, two = (jnp.concatenate([inverse[0, s], spare], 0) for s in range(2))
     own_inverse[...] = jnp.where(first, one, two)
     give[height:] = jnp.where(first, two, one)
-    copies[3].wait()
+
+
+def flip_kernel(source, *refs):
+    pieces, matrix, sem = refs[:-2], refs[-2], refs[-1]
+    copy = pltpu.make_async_copy(source, matrix, sem)
+    copy.start()
+    copy.wait()
     at = 0
     for piece in pieces:
         piece[...] = matrix[0, :, at : at + piece.shape[0]].T
         at += piece.shape[0]
+
+
+def hold_kernel(value, out):
+    del value, out
 
 
 def gather_kernel(*refs):
@@ -138,7 +148,7 @@
         at += own.shape[0]
 
 
-def couple_kernel(weight, mine, other, pack, got_pack, out_near, out_far, keep, send, half, packed):
+def couple_kernel(weight, mine, other, pack, got_pack, out_a, out_b, keep, send, half, packed):
     core, column, point = (lax.axis_index(name) for name in ("core", "pcol", "hyp"))
     applied = mine[...] + other[...]
     high = applied.astype(jnp.bfloat16)
@@ -172,10 +182,10 @@
     size = keep.shape[0]
     keep[...] = packed[pl.ds(pl.multiple_of(point * size, 8), size), :]
     send[...] = packed[pl.ds(pl.multiple_of((1 - point) * size, 8), size), :]
-    height = out_near.shape[0]
-    side = lax.axis_index("side")
-    for out, at in ((out_near, side), (out_far, 1 - side)):
-        spot = at * 2 + core
+    height = out_a.shape[0]
+    even = column % 2 == core
+    for out, steps in ((out_a, (2, 1)), (out_b, (0, 3))):
+        spot = jnp.bitwise_xor(column, jnp.where(even, steps[0], steps[1]))
         out[...] = half[pl.ds(pl.multiple_of(spot * height, height), height), :]
 
 
@@ -183,39 +193,57 @@
     out[...] = mine[...] + came[...]
 
 
-def finish_kernel(*refs):
-    parts, (live_hbm, near, far, rows_out, out, live, block, lines, result, sems) = refs[:8], refs[8:]
-    point, side, core = (lax.axis_index(name) for name in ("hyp", "side", "core"))
-    copy = pltpu.make_async_copy(live_hbm, live, sems.at[0])
-    copy.start()
-    width = result.shape[1]
-    blocks = tiles(width)
+def spread(parts, out, lines, result, sems, owner):
+    point, side = lax.axis_index("hyp"), lax.axis_index("side")
     size = parts[0].shape[0]
     for index, part in enumerate(parts):
-        owner = core if index < 4 else 1 - core
         node = 1 - side if index % 2 else side
-        slot = 1 - point if index // 2 % 2 else point
-        start = pl.multiple_of((owner * 2 + slot) * size, 8)
-        lines[node, pl.ds(start, size), :] = part[...]
-    copies = []
-    for node in range(2):
-        for index, (a, b) in enumerate(blocks):
-            tile = lines[node, index * LANES : (index + 1) * LANES, :]
-            result[node, a * LANES : (a + 1) * LANES, b * LANES : (b + 1) * LANES] = tile
-            if a != b:
-                result[node, b * LANES : (b + 1) * LANES, a * LANES : (a + 1) * LANES] = tile.T
-        copies.append(pltpu.make_async_copy(result.at[node], out.at[node], sems.at[1 + node]))
-        copies[-1].start()
-    copy.wait()
-    row = lax.broadcasted_iota(jnp.int32, near.shape, 0)
-    first = lax.axis_index("pcol") // 2 == 0
-    pair = (jnp.where(first, near[...], far[...]), jnp.where(first, far[...], near[...]))
+        slot = 1 - point if index // 2 else point
+        lines[node, pl.ds(pl.multiple_of(slot * size, 8), size), :] = part[...]
+    blocks = tiles(result.shape[1])
+    per = len(blocks) // 2
+    for core in range(2):
+
+        @pl.when(owner == core)
+        def _():
+            copies = []
+            for node in range(2):
+                for index, (a, b) in enumerate(blocks[core * per : (core + 1) * per]):
+                    rows, columns = (slice(i * LANES, (i + 1) * LANES) for i in (a, b))
+                    tile = lines[node, index * LANES : (index + 1) * LANES, :]
+                    result[node, rows, columns] = tile
+                    if a != b:
+                        result[node, columns, rows] = tile.T
+                first, rest = slice(0, LANES), slice(LANES, None)
+                for index, area in enumerate([(first, slice(None)), (rest, first)] if core == 0 else [(rest, rest)]):
+                    place = (node, *area)
+                    copy = pltpu.make_async_copy(result.at[place], out.at[place], sems.at[2 * node + index])
+                    copy.start()
+                    copies.append(copy)
+            for copy in copies:
+                copy.wait()
+
+
+def early_kernel(*refs):
+    parts, (live_hbm, mine, theirs, rows_out, out, live, block, lines, result, sems) = refs[:4], refs[4:]
+    load = pltpu.make_async_copy(live_hbm, live, sems.at[4])
+    load.start()
+    load.wait()
+    row = lax.broadcasted_iota(jnp.int32, mine.shape, 0)
+    first = lax.axis_index("side") == 0
+    pair = (jnp.where(first, mine[...], theirs[...]), jnp.where(first, theirs[...], mine[...]))
     for s, value in enumerate(pair):
         block[:, s, :] = jnp.where(row < live[s], value, jnp.zeros(value.shape, value.dtype))
-    copies.append(pltpu.make_async_copy(block, rows_out.at[0], sems.at[3]))
-    copies[-1].start()
-    for copy in copies:
-        copy.wait()
+    store = pltpu.make_async_copy(block, rows_out.at[0], sems.at[5])
+    store.start()
+    spread(parts, out, lines, result, sems, lax.axis_index("core"))
+    store.wait()
+
+
+def late_kernel(*refs):
+    parts, (before, out, lines, result, sems) = refs[:4], refs[4:]
+    del before
+    spread(parts, out, lines, result, sems, 1 - lax.axis_index("core"))
 
 
 def square(sigma_rows, panel, live_block_rows, inv_diag, quad_weight):
@@ -235,24 +263,35 @@
 
     extent = sigma_rows.shape[2]
     block = shape((height, width), bf16)
-    cuts = (extent * 25 // 32, extent * 7 // 32)
+    cuts = (extent // 2, extent // 2)
     size = pl.cdiv(inv_diag.shape[2], ROWS) * ROWS
-    own, give, own_inverse, *pieces = call(
+    own, give, own_inverse = call(
         start_kernel,
-        [block, shape((height + size, width), bf16), shape((size, width), bf16)]
-        + [shape((lines, extent), bf16) for lines in cuts],
-        [HBM] * 4,
-        *map(stay, (live, panel, inv_diag, sigma_rows)),
+        [block, shape((height + size, width), bf16), shape((size, width), bf16)],
+        [HBM] * 3,
+        *map(stay, (live, panel, inv_diag)),
         scratch=[pltpu.SMEM(live.shape, jnp.int32)]
-        + [pltpu.VMEM(x.shape, bf16) for x in (panel, inv_diag, sigma_rows)]
-        + [dma((4,))],
+        + [pltpu.VMEM(x.shape, bf16) for x in (panel, inv_diag)]
+        + [dma((3,))],
+    )
+    pieces = call(
+        flip_kernel,
+        [shape((lines, extent), bf16) for lines in cuts],
+        [HBM],
+        stay(sigma_rows),
+        scratch=[pltpu.VMEM(sigma_rows.shape, bf16), dma(())],
+        after=[own],
     )
     got = swap(give, side=1)
     got, got_inverse = got[:height], got[height:]
-    blocks = []
-    for start in (own, got):
-        pair = jnp.stack([start, swap(start, column=2)])
-        blocks += [pair, swap(pair, column=1)]
+    def hold(x, *after):
+        return call(hold_kernel, shape(x.shape, x.dtype), [ANY], x, out_specs=ANY, after=after, alias={0: 0})
+
+    own_two, got_two = swap(own, column=2), swap(got, column=2)
+    own_one = swap(own, column=1)
+    own_three = swap(hold(own_two, own_one), column=1)
+    blocks = [own, own_two, own_one, own_three]
+    blocks += [got, got_two, swap(got, column=1), swap(hold(got_two, own_three), column=1)]
     far = [swap(piece, side=1) for piece in pieces]
 
     pack = shape((extent + 2 * size, width), bf16)
@@ -268,41 +307,50 @@
 
     lines = len(tiles(width)) // 2 * LANES
     part = shape((lines // 2, LANES), f32)
-    out_near, out_far, keep, send = call(
+    out_a, out_b, keep, send = call(
         couple_kernel, [block, block, part, part], [SMEM] + [VMEM] * 4,
         quad_weight, mine, other, pack, got_pack,
         scratch=[pltpu.VMEM((extent, width), bf16), pltpu.VMEM((lines, LANES), f32)],
     )
     came = swap(send, point=1)
 
-    def deliver(x, flip):
+    def cross(x, even, odd):
         pairs = []
         for i in range(devices):
-            h, s, k, c = i // (4 * grid), i // (2 * grid) % 2, i // grid % 2, i % grid
-            pairs.append((i, (h * 4 + c) * grid + 2 * (s ^ flip) + k))
+            head, k, c = i // (2 * grid), i // grid % 2, i % grid
+            flip, step = even if k == c % 2 else odd
+            pairs.append((i, (head * 2 + (k ^ flip)) * grid + (c ^ step)))
         return lax.ppermute(x, AXES, pairs)
 
-    near, far = deliver(out_near, 0), deliver(out_far, 1)
+    land_a = cross(out_a, (0, 2), (1, 1))
+    land_b = cross(out_b, (0, 0), (1, 3))
     add = functools.partial(call, add_kernel, part, [VMEM] * 2)
     total = add(keep, came)
-    total = add(total, swap(total, column=1), after=[near, far])
     total = add(total, swap(total, column=2))
+    total = add(total, swap(total, column=1), after=[land_a, land_b])
     quarters = [total, swap(total, side=1), swap(total, point=1), swap(total, side=1, point=1)]
-    quarters += [swap(x, core=1) for x in quarters]
-    return call(
-        finish_kernel,
-        [shape((1, height, count, width), bf16), shape((count, width, width), f32)],
-        [VMEM] * 8 + [HBM] + [VMEM] * 2,
-        *quarters, live, near, far,
-        scratch=[
-            pltpu.SMEM((2,), jnp.int32),
-            pltpu.VMEM((height, count, width), bf16),
-            pltpu.VMEM((count, 2 * lines, LANES), f32),
-            pltpu.VMEM((count, width, width), f32),
-            dma((4,)),
-        ],
+    other_quarters = [swap(x, core=1) for x in quarters]
+
+    side, core, column = (lax.axis_index(name) for name in AXES[1:])
+    from_a = jnp.where(column % 2 == core, 1 - column // 2, column // 2)
+    mine = jnp.where(from_a == side, land_a, land_b)
+    theirs = swap(jnp.where(from_a == side, land_b, land_a), side=1)
+
+    square_shape = shape((count, width, width), f32)
+    spread_scratch = [pltpu.VMEM((count, lines, LANES), f32), pltpu.VMEM((count, width, width), f32), dma((6,))]
+    sigma_panel, marginal = call(
+        early_kernel,
+        [shape((1, height, count, width), bf16), square_shape],
+        [VMEM] * 4 + [HBM] + [VMEM] * 2,
+        *quarters, live, mine, theirs,
+        scratch=[pltpu.SMEM(live.shape, jnp.int32), pltpu.VMEM((height, count, width), bf16)] + spread_scratch,
         out_specs=[HBM, HBM],
     )
+    marginal = call(
+        late_kernel, square_shape, [VMEM] * 4 + [HBM], *other_quarters, marginal,
+        scratch=spread_scratch, out_specs=HBM, alias={4: 0},
+    )
+    return sigma_panel, marginal
 
 
 def solution(mesh):

time: 61.7 us -> 59.7 us (0.968)
  waiting for transfers between devices: 29.6 us -> 25.5 us
  Pallas kernels: 4.87 us -> 7.01 us
    ppermute x2, waiting for transfers between devices: 4.68 us -> 0.8 us  [cross(): return lax.ppermute(x, AXES, pairs)]
    ppermute x2, starting transfers between devices: 4.55 us -> 2.19 us  [cross(): return lax.ppermute(x, AXES, pairs)]
    pallas_call x8 -> x12, Pallas kernels: 4.87 us -> 7.01 us  [call(): pl.pallas_call(body, out_shape=outs, in_specs=list(specs) + [ANY] * len(a...]
    ppermute x19 -> x22, starting transfers between devices: 21.1 us -> 23.2 us  [swap(): return lax.ppermute(x, AXES, [(i, i ^ mask) for i in range(devices)])]
    ppermute x19 -> x22, waiting for transfers between devices: 24.9 us -> 24.7 us  [swap(): return lax.ppermute(x, AXES, [(i, i ^ mask) for i in range(devices)])]
  transfers between devices with their start and end apart: 21 -> 24, of which waited for: 13 -> 13; matrix products, arithmetic and copies ran while one was open for 0% -> 0% of each run, Pallas kernels for 0% -> 5%
where the time goes in v8:
time: 59.7 us; the launch traced here: 59.5 us
  waiting for transfers between devices  25.5 us (43%)
  starting transfers between devices  25.4 us (43%)
  Pallas kernels  7.01 us (12%)
  between operations  1.45 us (2%)
    ppermute x22, waiting for transfers between devices, swap(): return lax.ppermute(x, AXES, [(i, i ^ mask) for i in range(devices)])  24.7 us
    ppermute x22, starting transfers between devices, swap(): return lax.ppermute(x, AXES, [(i, i ^ mask) for i in range(devices)])  23.2 us
    pallas_call x12, Pallas kernels, call(): pl.pallas_call(body, out_shape=outs, in_specs=list(specs) + [ANY] * len(a...  7.01 us
    ppermute x2, starting transfers between devices, cross(): return lax.ppermute(x, AXES, pairs)  2.19 us
  transfers between devices with their start and end apart: 24, of which 13 were waited for; matrix products, arithmetic and copies ran while one was open for 0% of the time, Pallas kernels for 5%

profile of v8, /device:TPU:0, one launch (start us, length us, event | category | flops | bytes accessed | tf_op | source)
XLA Modules:
  0.0 59.5 jit_solution(4957663339130164710)
XLA Ops:
  0.6 1.5 %shard_map.68 = (bf16[128,384]{1,0:T(8,128)(2,1)S(1)}, bf16[160,384]{1,0:T(8,128)(2,1)S(1)}, bf16[32,384]{1,0:T(8,128)(2,1)S(1)}) custom-call(s32[2]{0:T(128)} %bitcast.1, bf16[1,128,2,384]{3,2,1,0:T(2,128)(2,1)} %refs_1_.1, bf16[1,2,24,384]{3,2,1,0:T(8,128)(2,1)} %refs_2_.1), custom_call_target="tpu_custom_call" | custom-call | tf_op jit(solution)/shard_map/pallas_call | solution.py:28
  2.1 3.0 %collective-permute-start.3 = (bf16[160,384]{1,0:T(8,128)(2,1)S(1)}, bf16[160,384]{1,0:T(8,128)(2,1)S(1)}, u32[]{:S(2)}, u32[]{:S(2)}) collective-permute-start(bf16[160,384]{1,0:T(8,128)(2,1)S(1)} %get-tuple-element.16), channel_id=1, source_target_pairs={{0,8},{1,9},{2,10},{3,11},{4,12},{5,13},{6,14},{7,15},{8,0},{9,1},... | collective-permute-start | bytes 368648 | tf_op jit(solution)/shard_map/ppermute | solution.py:262
  5.1 2.6 %collective-permute-start = (bf16[128,384]{1,0:T(8,128)(2,1)S(1)}, bf16[128,384]{1,0:T(8,128)(2,1)S(1)}, u32[]{:S(2)}, u32[]{:S(2)}) collective-permute-start(bf16[128,384]{1,0:T(8,128)(2,1)S(1)} %get-tuple-element.15.refs_0_.refs_1_), channel_id=1, source_target_pairs={{0,2},{1,3},{2,0},{3,1},{4,6},{5,7},{6,4},{7,5},{8,10},{9,11},{10,... | collective-permute-start | bytes 294920 | tf_op jit(solution)/shard_map/ppermute | solution.py:262
  7.7 1.6 %collective-permute-start.1 = (bf16[128,384]{1,0:T(8,128)(2,1)S(1)}, bf16[128,384]{1,0:T(8,128)(2,1)S(1)}, u32[]{:S(2)}, u32[]{:S(2)}) collective-permute-start(bf16[128,384]{1,0:T(8,128)(2,1)S(1)} %get-tuple-element.15.refs_0_.refs_1_), channel_id=1, source_target_pairs={{0,1},{1,0},{2,3},{3,2},{4,5},{5,4},{6,7},{7,6},{8,9},{9,8},{10,11... | collective-permute-start | bytes 294920 | tf_op jit(solution)/shard_map/ppermute | solution.py:262
  9.3 1.2 %shard_map.72 = (bf16[256,512]{1,0:T(8,128)(2,1)S(1)}, bf16[256,512]{1,0:T(8,128)(2,1)S(1)}) custom-call(bf16[1,512,512]{2,1,0:T(8,128)(2,1)} %refs_0_.2, bf16[128,384]{1,0:T(8,128)(2,1)S(1)} %get-tuple-element.15.refs_0_.refs_1_), custom_call_target="tpu_custom_call" | custom-call | tf_op jit(solution)/shard_map/pallas_call | solution.py:28
  10.6 0.6 %collective-permute-start.7 = (bf16[256,512]{1,0:T(8,128)(2,1)S(1)}, bf16[256,512]{1,0:T(8,128)(2,1)S(1)}, u32[]{:S(2)}, u32[]{:S(2)}) collective-permute-start(bf16[256,512]{1,0:T(8,128)(2,1)S(1)} %get-tuple-element.19.refs_1_), channel_id=1, source_target_pairs={{0,8},{1,9},{2,10},{3,11},{4,12},{5,13},{6,14},{7,15},{8,0},{9,1},... | collective-permute-start | bytes 786440 | tf_op jit(solution)/shard_map/ppermute | solution.py:262
  11.2 1.5 %collective-permute-start.8 = (bf16[256,512]{1,0:T(8,128)(2,1)S(1)}, bf16[256,512]{1,0:T(8,128)(2,1)S(1)}, u32[]{:S(2)}, u32[]{:S(2)}) collective-permute-start(bf16[256,512]{1,0:T(8,128)(2,1)S(1)} %get-tuple-element.20.refs_2_), channel_id=1, source_target_pairs={{0,8},{1,9},{2,10},{3,11},{4,12},{5,13},{6,14},{7,15},{8,0},{9,1},... | collective-permute-start | bytes 786440 | tf_op jit(solution)/shard_map/ppermute | solution.py:262
  12.7 1.6 %collective-permute-start.4 = (bf16[128,384]{1,0:T(8,128)(2,1)S(1)}, bf16[128,384]{1,0:T(8,128)(2,1)S(1)}, u32[]{:S(2)}, u32[]{:S(2)}) collective-permute-start(bf16[128,384]{1,0:T(8,128)(2,1)S(1)} %slice.8.refs_4_), channel_id=1, source_target_pairs={{0,2},{1,3},{2,0},{3,1},{4,6},{5,7},{6,4},{7,5},{8,10},{9,11},{10,... | collective-permute-start | bytes 294920 | tf_op jit(solution)/shard_map/ppermute | solution.py:262
  14.3 2.3 %collective-permute-start.2 = (bf16[128,384]{1,0:T(8,128)(2,1)S(1)}, bf16[128,384]{1,0:T(8,128)(2,1)S(1)}, u32[]{:S(2)}, u32[]{:S(2)}) collective-permute-start(bf16[128,384]{1,0:T(8,128)(2,1)S(1)} %shard_map.69), channel_id=1, source_target_pairs={{0,1},{1,0},{2,3},{3,2},{4,5},{5,4},{6,7},{7,6},{8,9},{9,8},{10,11... | collective-permute-start | bytes 294920 | tf_op jit(solution)/shard_map/ppermute | solution.py:262
  16.6 3.0 %collective-permute-done.4.refs_5_ = bf16[128,384]{1,0:T(8,128)(2,1)S(1)} collective-permute-done((bf16[128,384]{1,0:T(8,128)(2,1)S(1)}, bf16[128,384]{1,0:T(8,128)(2,1)S(1)}, u32[]{:S(2)}, u32[]{:S(2)}) %collective-permute-start.4) | collective-permute-done | bytes 98336 | tf_op jit(solution)/shard_map/ppermute | solution.py:262
  19.7 1.3 %collective-permute-done.2.refs_1_.refs_3_ = bf16[128,384]{1,0:T(8,128)(2,1)S(1)} collective-permute-done((bf16[128,384]{1,0:T(8,128)(2,1)S(1)}, bf16[128,384]{1,0:T(8,128)(2,1)S(1)}, u32[]{:S(2)}, u32[]{:S(2)}) %collective-permute-start.2) | collective-permute-done | bytes 98336 | tf_op jit(solution)/shard_map/ppermute | solution.py:262
  20.9 1.1 %collective-permute-start.6 = (bf16[128,384]{1,0:T(8,128)(2,1)S(1)}, bf16[128,384]{1,0:T(8,128)(2,1)S(1)}, u32[]{:S(2)}, u32[]{:S(2)}) collective-permute-start(bf16[128,384]{1,0:T(8,128)(2,1)S(1)} %shard_map.70), channel_id=1, source_target_pairs={{0,1},{1,0},{2,3},{3,2},{4,5},{5,4},{6,7},{7,6},{8,9},{9,8},{10,11... | collective-permute-start | bytes 294920 | tf_op jit(solution)/shard_map/ppermute | solution.py:262
  22.1 1.0 %collective-permute-done.5.refs_6_ = bf16[128,384]{1,0:T(8,128)(2,1)S(1)} collective-permute-done((bf16[128,384]{1,0:T(8,128)(2,1)S(1)}, bf16[128,384]{1,0:T(8,128)(2,1)S(1)}, u32[]{:S(2)}, u32[]{:S(2)}) %collective-permute-start.5) | collective-permute-done | bytes 98336 | tf_op jit(solution)/shard_map/ppermute | solution.py:262
  23.0 2.5 %collective-permute-done.6.refs_7_ = bf16[128,384]{1,0:T(8,128)(2,1)S(1)} collective-permute-done((bf16[128,384]{1,0:T(8,128)(2,1)S(1)}, bf16[128,384]{1,0:T(8,128)(2,1)S(1)}, u32[]{:S(2)}, u32[]{:S(2)}) %collective-permute-start.6) | collective-permute-done | bytes 98336 | tf_op jit(solution)/shard_map/ppermute | solution.py:262
  25.7 0.7 %shard_map.73.refs_1_ = f32[512,384]{1,0:T(8,128)S(1)} custom-call(bf16[2,512,384]{2,1,0:T(8,128)(2,1)S(1)} %get-tuple-element.18.refs_0_, bf16[256,512]{1,0:T(8,128)(2,1)S(1)} %get-tuple-element.19.refs_1_, bf16[256,512]{1,0:T(8,128)(2,1)S(1)} %get-tuple-element.20.refs_2_, bf16[256,512]{1,0:T(8,128)(2,1)S(1)} %collective-permute-done.7.refs_3_, ...), custom_call_target="tpu_custom_call" | custom-call | tf_op jit(solution)/shard_map/pallas_call | solution.py:28
  27.6 1.8 %collective-permute-done.10.refs_4_ = bf16[576,384]{1,0:T(8,128)(2,1)S(1)} collective-permute-done((bf16[576,384]{1,0:T(8,128)(2,1)S(1)}, bf16[576,384]{1,0:T(8,128)(2,1)S(1)}, u32[]{:S(2)}, u32[]{:S(2)}) %collective-permute-start.10) | collective-permute-done | bytes 442400 | tf_op jit(solution)/shard_map/ppermute | solution.py:262
  29.4 0.6 %shard_map.74 = (bf16[128,384]{1,0:T(8,128)(2,1)S(1)}, bf16[128,384]{1,0:T(8,128)(2,1)S(1)}, f32[192,128]{1,0:T(8,128)S(1)}, f32[192,128]{1,0:T(8,128)S(1)}) custom-call(f32[1]{0:T(128)S(6)} %copy.13.refs_0_, f32[512,384]{1,0:T(8,128)S(1)} %shard_map.73.refs_1_, f32[512,384]{1,0:T(8,128)S(1)} %collective-permute-done.9.refs_2_, ...), custom_call_target="tpu_custom_call" | custom-call | tf_op jit(solution)/shard_map/pallas_call | solution.py:28
  30.0 1.6 %collective-permute-start.11 = (f32[192,128]{1,0:T(8,128)S(1)}, f32[192,128]{1,0:T(8,128)S(1)}, u32[]{:S(2)}, u32[]{:S(2)}) collective-permute-start(f32[192,128]{1,0:T(8,128)S(1)} %get-tuple-element.23), channel_id=1, source_target_pairs={{0,16},{1,17},{2,18},{3,19},{4,20},{5,21},{6,22},{7,23},{8,24},{9,... | collective-permute-start | bytes 294920 | tf_op jit(solution)/shard_map/ppermute | solution.py:262
  31.6 3.3 %collective-permute-done.11.refs_1_ = f32[192,128]{1,0:T(8,128)S(1)} collective-permute-done((f32[192,128]{1,0:T(8,128)S(1)}, f32[192,128]{1,0:T(8,128)S(1)}, u32[]{:S(2)}, u32[]{:S(2)}) %collective-permute-start.11) | collective-permute-done | bytes 98336 | tf_op jit(solution)/shard_map/ppermute | solution.py:262
  34.9 1.5 %collective-permute-start.12 = (f32[192,128]{1,0:T(8,128)S(1)}, f32[192,128]{1,0:T(8,128)S(1)}, u32[]{:S(2)}, u32[]{:S(2)}) collective-permute-start(f32[192,128]{1,0:T(8,128)S(1)} %shard_map.75.refs_0_), channel_id=1, source_target_pairs={{0,2},{1,3},{2,0},{3,1},{4,6},{5,7},{6,4},{7,5},{8,10},{9,11},{10,... | collective-permute-start | bytes 294920 | tf_op jit(solution)/shard_map/ppermute | solution.py:262
  36.4 1.5 %collective-permute-start.14 = (bf16[128,384]{1,0:T(8,128)(2,1)S(1)}, bf16[128,384]{1,0:T(8,128)(2,1)S(1)}, u32[]{:S(2)}, u32[]{:S(2)}) collective-permute-start(bf16[128,384]{1,0:T(8,128)(2,1)S(1)} %get-tuple-element.24), channel_id=1, source_target_pairs={{0,2},{1,4},{2,0},{3,6},{4,1},{5,7},{6,3},{7,5},{8,10},{9,12},{10,... | collective-permute-start | bytes 294920 | tf_op jit(solution)/shard_map/ppermute | solution.py:323
  37.9 0.7 %collective-permute-start.15 = (bf16[128,384]{1,0:T(8,128)(2,1)S(1)}, bf16[128,384]{1,0:T(8,128)(2,1)S(1)}, u32[]{:S(2)}, u32[]{:S(2)}) collective-permute-start(bf16[128,384]{1,0:T(8,128)(2,1)S(1)} %get-tuple-element.25), channel_id=1, source_target_pairs={{0,0},{1,6},{2,2},{3,4},{4,3},{5,5},{6,1},{7,7},{8,8},{9,14},{10,1... | collective-permute-start | bytes 294920 | tf_op jit(solution)/shard_map/ppermute | solution.py:323
  38.6 5.0 %collective-permute-done.12.refs_1_ = f32[192,128]{1,0:T(8,128)S(1)} collective-permute-done((f32[192,128]{1,0:T(8,128)S(1)}, f32[192,128]{1,0:T(8,128)S(1)}, u32[]{:S(2)}, u32[]{:S(2)}) %collective-permute-start.12) | collective-permute-done | bytes 98336 | tf_op jit(solution)/shard_map/ppermute | solution.py:262
  43.6 0.8 %collective-permute-start.13 = (f32[192,128]{1,0:T(8,128)S(1)}, f32[192,128]{1,0:T(8,128)S(1)}, u32[]{:S(2)}, u32[]{:S(2)}) collective-permute-start(f32[192,128]{1,0:T(8,128)S(1)} %shard_map.76.refs_0_), channel_id=1, source_target_pairs={{0,1},{1,0},{2,3},{3,2},{4,5},{5,4},{6,7},{7,6},{8,9},{9,8},{10,11... | collective-permute-start | bytes 294920 | tf_op jit(solution)/shard_map/ppermute | solution.py:262
  44.4 0.8 %collective-permute-done.14.refs_2_ = bf16[128,384]{1,0:T(8,128)(2,1)S(1)} collective-permute-done((bf16[128,384]{1,0:T(8,128)(2,1)S(1)}, bf16[128,384]{1,0:T(8,128)(2,1)S(1)}, u32[]{:S(2)}, u32[]{:S(2)}) %collective-permute-start.14) | collective-permute-done | bytes 98336 | tf_op jit(solution)/shard_map/ppermute | solution.py:323
  45.2 3.1 %collective-permute-done.13.refs_1_ = f32[192,128]{1,0:T(8,128)S(1)} collective-permute-done((f32[192,128]{1,0:T(8,128)S(1)}, f32[192,128]{1,0:T(8,128)S(1)}, u32[]{:S(2)}, u32[]{:S(2)}) %collective-permute-start.13) | collective-permute-done | bytes 98336 | tf_op jit(solution)/shard_map/ppermute | solution.py:262
  48.9 1.5 %collective-permute-start.17 = (f32[192,128]{1,0:T(8,128)S(1)}, f32[192,128]{1,0:T(8,128)S(1)}, u32[]{:S(2)}, u32[]{:S(2)}) collective-permute-start(f32[192,128]{1,0:T(8,128)S(1)} %shard_map.77.refs_0_), channel_id=1, source_target_pairs={{0,16},{1,17},{2,18},{3,19},{4,20},{5,21},{6,22},{7,23},{8,24},{9,... | collective-permute-start | bytes 294920 | tf_op jit(solution)/shard_map/ppermute | solution.py:262
  50.5 1.4 %collective-permute-start.18 = (f32[192,128]{1,0:T(8,128)S(1)}, f32[192,128]{1,0:T(8,128)S(1)}, u32[]{:S(2)}, u32[]{:S(2)}) collective-permute-start(f32[192,128]{1,0:T(8,128)S(1)} %shard_map.77.refs_0_), channel_id=1, source_target_pairs={{0,24},{1,25},{2,26},{3,27},{4,28},{5,29},{6,30},{7,31},{8,16},{9,... | collective-permute-start | bytes 294920 | tf_op jit(solution)/shard_map/ppermute | solution.py:262
  52.5 1.5 %collective-permute-done.16.refs_1_ = f32[192,128]{1,0:T(8,128)S(1)} collective-permute-done((f32[192,128]{1,0:T(8,128)S(1)}, f32[192,128]{1,0:T(8,128)S(1)}, u32[]{:S(2)}, u32[]{:S(2)}) %collective-permute-start.16) | collective-permute-done | bytes 98336 | tf_op jit(solution)/shard_map/ppermute | solution.py:262
  54.6 1.8 %collective-permute-done.18.refs_3_ = f32[192,128]{1,0:T(8,128)S(1)} collective-permute-done((f32[192,128]{1,0:T(8,128)S(1)}, f32[192,128]{1,0:T(8,128)S(1)}, u32[]{:S(2)}, u32[]{:S(2)}) %collective-permute-start.18) | collective-permute-done | bytes 98336 | tf_op jit(solution)/shard_map/ppermute | solution.py:262
  56.6 1.8 %shard_map.78 = (bf16[1,128,2,384]{3,2,1,0:T(2,128)(2,1)}, f32[2,384,384]{2,1,0:T(8,128)}) custom-call(f32[192,128]{1,0:T(8,128)S(1)} %shard_map.77.refs_0_, f32[192,128]{1,0:T(8,128)S(1)} %collective-permute-done.16.refs_1_, f32[192,128]{1,0:T(8,128)S(1)} %collective-permute-done.17.refs_2_, f32[192,128]{1,0:T(8,128)S(1)} %collective-permute-done.18.refs_3_, ...), custom_call_target="tpu_custom_call" | custom-call | tf_op jit(solution)/shard_map/pallas_call | solution.py:28
  58.5 1.0 %shard_map.79 = f32[2,384,384]{2,1,0:T(8,128)} custom-call(f32[192,128]{1,0:T(8,128)S(1)} %collective-permute-done.20.refs_0_, f32[192,128]{1,0:T(8,128)S(1)} %collective-permute-done.21.refs_1_, f32[192,128]{1,0:T(8,128)S(1)} %collective-permute-done.22.refs_2_, f32[192,128]{1,0:T(8,128)S(1)} %collective-permute-done.23.refs_3_, ...), custom_call_target="tpu_custom_call", output_to_operand_aliasing={{}: (4, {})} | custom-call | tf_op jit(solution)/shard_map/pallas_call | solution.py:28
  (35 shorter events, 2.8 us)
Async XLA Ops:
  2.1 10.5 %collective-permute-start.3 = (bf16[160,384]{1,0:T(8,128)(2,1)S(1)}, bf16[160,384]{1,0:T(8,128)(2,1)S(1)}, u32[]{:S(2)}, u32[]{:S(2)}) collective-permute-start(bf16[160,384]{1,0:T(8,128)(2,1)S(1)} %get-tuple-element.16), channel_id=1, source_target_pairs={{0,8},{1,9},{2,10},{3,11},{4,12},{5,13},{6,14},{7,15},{8,0},{9,1},... | collective-permute-start | bytes 368648 | tf_op jit(solution)/shard_map/ppermute | solution.py:262
  5.1 7.5 %collective-permute-start = (bf16[128,384]{1,0:T(8,128)(2,1)S(1)}, bf16[128,384]{1,0:T(8,128)(2,1)S(1)}, u32[]{:S(2)}, u32[]{:S(2)}) collective-permute-start(bf16[128,384]{1,0:T(8,128)(2,1)S(1)} %get-tuple-element.15.refs_0_.refs_1_), channel_id=1, source_target_pairs={{0,2},{1,3},{2,0},{3,1},{4,6},{5,7},{6,4},{7,5},{8,10},{9,11},{10,... | collective-permute-start | bytes 294920 | tf_op jit(solution)/shard_map/ppermute | solution.py:262
  7.7 6.6 %collective-permute-start.1 = (bf16[128,384]{1,0:T(8,128)(2,1)S(1)}, bf16[128,384]{1,0:T(8,128)(2,1)S(1)}, u32[]{:S(2)}, u32[]{:S(2)}) collective-permute-start(bf16[128,384]{1,0:T(8,128)(2,1)S(1)} %get-tuple-element.15.refs_0_.refs_1_), channel_id=1, source_target_pairs={{0,1},{1,0},{2,3},{3,2},{4,5},{5,4},{6,7},{7,6},{8,9},{9,8},{10,11... | collective-permute-start | bytes 294920 | tf_op jit(solution)/shard_map/ppermute | solution.py:262
  10.6 15.1 %collective-permute-start.7 = (bf16[256,512]{1,0:T(8,128)(2,1)S(1)}, bf16[256,512]{1,0:T(8,128)(2,1)S(1)}, u32[]{:S(2)}, u32[]{:S(2)}) collective-permute-start(bf16[256,512]{1,0:T(8,128)(2,1)S(1)} %get-tuple-element.19.refs_1_), channel_id=1, source_target_pairs={{0,8},{1,9},{2,10},{3,11},{4,12},{5,13},{6,14},{7,15},{8,0},{9,1},... | collective-permute-start | bytes 786440 | tf_op jit(solution)/shard_map/ppermute | solution.py:262
  11.2 14.5 %collective-permute-start.8 = (bf16[256,512]{1,0:T(8,128)(2,1)S(1)}, bf16[256,512]{1,0:T(8,128)(2,1)S(1)}, u32[]{:S(2)}, u32[]{:S(2)}) collective-permute-start(bf16[256,512]{1,0:T(8,128)(2,1)S(1)} %get-tuple-element.20.refs_2_), channel_id=1, source_target_pairs={{0,8},{1,9},{2,10},{3,11},{4,12},{5,13},{6,14},{7,15},{8,0},{9,1},... | collective-permute-start | bytes 786440 | tf_op jit(solution)/shard_map/ppermute | solution.py:262
  12.7 7.0 %collective-permute-start.4 = (bf16[128,384]{1,0:T(8,128)(2,1)S(1)}, bf16[128,384]{1,0:T(8,128)(2,1)S(1)}, u32[]{:S(2)}, u32[]{:S(2)}) collective-permute-start(bf16[128,384]{1,0:T(8,128)(2,1)S(1)} %slice.8.refs_4_), channel_id=1, source_target_pairs={{0,2},{1,3},{2,0},{3,1},{4,6},{5,7},{6,4},{7,5},{8,10},{9,11},{10,... | collective-permute-start | bytes 294920 | tf_op jit(solution)/shard_map/ppermute | solution.py:262
  14.3 6.6 %collective-permute-start.2 = (bf16[128,384]{1,0:T(8,128)(2,1)S(1)}, bf16[128,384]{1,0:T(8,128)(2,1)S(1)}, u32[]{:S(2)}, u32[]{:S(2)}) collective-permute-start(bf16[128,384]{1,0:T(8,128)(2,1)S(1)} %shard_map.69), channel_id=1, source_target_pairs={{0,1},{1,0},{2,3},{3,2},{4,5},{5,4},{6,7},{7,6},{8,9},{9,8},{10,11... | collective-permute-start | bytes 294920 | tf_op jit(solution)/shard_map/ppermute | solution.py:262
  16.6 6.5 %collective-permute-start.5 = (bf16[128,384]{1,0:T(8,128)(2,1)S(1)}, bf16[128,384]{1,0:T(8,128)(2,1)S(1)}, u32[]{:S(2)}, u32[]{:S(2)}) collective-permute-start(bf16[128,384]{1,0:T(8,128)(2,1)S(1)} %slice.8.refs_4_), channel_id=1, source_target_pairs={{0,1},{1,0},{2,3},{3,2},{4,5},{5,4},{6,7},{7,6},{8,9},{9,8},{10,11... | collective-permute-start | bytes 294920 | tf_op jit(solution)/shard_map/ppermute | solution.py:262
  20.9 4.6 %collective-permute-start.6 = (bf16[128,384]{1,0:T(8,128)(2,1)S(1)}, bf16[128,384]{1,0:T(8,128)(2,1)S(1)}, u32[]{:S(2)}, u32[]{:S(2)}) collective-permute-start(bf16[128,384]{1,0:T(8,128)(2,1)S(1)} %shard_map.70), channel_id=1, source_target_pairs={{0,1},{1,0},{2,3},{3,2},{4,5},{5,4},{6,7},{7,6},{8,9},{9,8},{10,11... | collective-permute-start | bytes 294920 | tf_op jit(solution)/shard_map/ppermute | solution.py:262
  26.4 3.0 %collective-permute-start.9 = (f32[512,384]{1,0:T(8,128)S(1)}, f32[512,384]{1,0:T(8,128)S(1)}, u32[]{:S(2)}, u32[]{:S(2)}) collective-permute-start(f32[512,384]{1,0:T(8,128)S(1)} %shard_map.73.refs_1_), channel_id=1, source_target_pairs={{0,4},{1,5},{2,6},{3,7},{4,0},{5,1},{6,2},{7,3},{8,12},{9,13},{10,... | collective-permute-start | bytes 2359304 | tf_op jit(solution)/shard_map/ppermute | solution.py:262
  26.5 2.9 %collective-permute-start.10 = (bf16[576,384]{1,0:T(8,128)(2,1)S(1)}, bf16[576,384]{1,0:T(8,128)(2,1)S(1)}, u32[]{:S(2)}, u32[]{:S(2)}) collective-permute-start(bf16[576,384]{1,0:T(8,128)(2,1)S(1)} %get-tuple-element.21.refs_3_), channel_id=1, source_target_pairs={{0,4},{1,5},{2,6},{3,7},{4,0},{5,1},{6,2},{7,3},{8,12},{9,13},{10,... | collective-permute-start | bytes 1327112 | tf_op jit(solution)/shard_map/ppermute | solution.py:262
  30.0 26.6 %copy-start = (s32[2,1]{0,1:T(1,128)S(1)}, s32[2,1]{0,1:T(1,128)}, u32[]{:S(2)}) copy-start(s32[2,1]{0,1:T(1,128)} %param.7) | copy-start | bytes 28
  30.0 4.9 %collective-permute-start.11 = (f32[192,128]{1,0:T(8,128)S(1)}, f32[192,128]{1,0:T(8,128)S(1)}, u32[]{:S(2)}, u32[]{:S(2)}) collective-permute-start(f32[192,128]{1,0:T(8,128)S(1)} %get-tuple-element.23), channel_id=1, source_target_pairs={{0,16},{1,17},{2,18},{3,19},{4,20},{5,21},{6,22},{7,23},{8,24},{9,... | collective-permute-start | bytes 294920 | tf_op jit(solution)/shard_map/ppermute | solution.py:262
  34.9 8.7 %collective-permute-start.12 = (f32[192,128]{1,0:T(8,128)S(1)}, f32[192,128]{1,0:T(8,128)S(1)}, u32[]{:S(2)}, u32[]{:S(2)}) collective-permute-start(f32[192,128]{1,0:T(8,128)S(1)} %shard_map.75.refs_0_), channel_id=1, source_target_pairs={{0,2},{1,3},{2,0},{3,1},{4,6},{5,7},{6,4},{7,5},{8,10},{9,11},{10,... | collective-permute-start | bytes 294920 | tf_op jit(solution)/shard_map/ppermute | solution.py:262
  36.4 8.8 %collective-permute-start.14 = (bf16[128,384]{1,0:T(8,128)(2,1)S(1)}, bf16[128,384]{1,0:T(8,128)(2,1)S(1)}, u32[]{:S(2)}, u32[]{:S(2)}) collective-permute-start(bf16[128,384]{1,0:T(8,128)(2,1)S(1)} %get-tuple-element.24), channel_id=1, source_target_pairs={{0,2},{1,4},{2,0},{3,6},{4,1},{5,7},{6,3},{7,5},{8,10},{9,12},{10,... | collective-permute-start | bytes 294920 | tf_op jit(solution)/shard_map/ppermute | solution.py:323
  37.9 7.3 %collective-permute-start.15 = (bf16[128,384]{1,0:T(8,128)(2,1)S(1)}, bf16[128,384]{1,0:T(8,128)(2,1)S(1)}, u32[]{:S(2)}, u32[]{:S(2)}) collective-permute-start(bf16[128,384]{1,0:T(8,128)(2,1)S(1)} %get-tuple-element.25), channel_id=1, source_target_pairs={{0,0},{1,6},{2,2},{3,4},{4,3},{5,5},{6,1},{7,7},{8,8},{9,14},{10,1... | collective-permute-start | bytes 294920 | tf_op jit(solution)/shard_map/ppermute | solution.py:323
  43.6 4.7 %collective-permute-start.13 = (f32[192,128]{1,0:T(8,128)S(1)}, f32[192,128]{1,0:T(8,128)S(1)}, u32[]{:S(2)}, u32[]{:S(2)}) collective-permute-start(f32[192,128]{1,0:T(8,128)S(1)} %shard_map.76.refs_0_), channel_id=1, source_target_pairs={{0,1},{1,0},{2,3},{3,2},{4,5},{5,4},{6,7},{7,6},{8,9},{9,8},{10,11... | collective-permute-start | bytes 294920 | tf_op jit(solution)/shard_map/ppermute | solution.py:262
  48.3 5.7 %collective-permute-start.16 = (f32[192,128]{1,0:T(8,128)S(1)}, f32[192,128]{1,0:T(8,128)S(1)}, u32[]{:S(2)}, u32[]{:S(2)}) collective-permute-start(f32[192,128]{1,0:T(8,128)S(1)} %shard_map.77.refs_0_), channel_id=1, source_target_pairs={{0,8},{1,9},{2,10},{3,11},{4,12},{5,13},{6,14},{7,15},{8,0},{9,1},... | collective-permute-start | bytes 294920 | tf_op jit(solution)/shard_map/ppermute | solution.py:262
  48.9 5.3 %collective-permute-start.17 = (f32[192,128]{1,0:T(8,128)S(1)}, f32[192,128]{1,0:T(8,128)S(1)}, u32[]{:S(2)}, u32[]{:S(2)}) collective-permute-start(f32[192,128]{1,0:T(8,128)S(1)} %shard_map.77.refs_0_), channel_id=1, source_target_pairs={{0,16},{1,17},{2,18},{3,19},{4,20},{5,21},{6,22},{7,23},{8,24},{9,... | collective-permute-start | bytes 294920 | tf_op jit(solution)/shard_map/ppermute | solution.py:262
  50.5 5.9 %collective-permute-start.18 = (f32[192,128]{1,0:T(8,128)S(1)}, f32[192,128]{1,0:T(8,128)S(1)}, u32[]{:S(2)}, u32[]{:S(2)}) collective-permute-start(f32[192,128]{1,0:T(8,128)S(1)} %shard_map.77.refs_0_), channel_id=1, source_target_pairs={{0,24},{1,25},{2,26},{3,27},{4,28},{5,29},{6,30},{7,31},{8,16},{9,... | collective-permute-start | bytes 294920 | tf_op jit(solution)/shard_map/ppermute | solution.py:262
  51.9 4.7 %collective-permute-start.19 = (bf16[128,384]{1,0:T(8,128)(2,1)S(1)}, bf16[128,384]{1,0:T(8,128)(2,1)S(1)}, u32[]{:S(2)}, u32[]{:S(2)}) collective-permute-start(bf16[128,384]{1,0:T(8,128)(2,1)S(1)} %get-tuple-element.28), channel_id=1, source_target_pairs={{0,8},{1,9},{2,10},{3,11},{4,12},{5,13},{6,14},{7,15},{8,0},{9,1},... | collective-permute-start | bytes 294920 | tf_op jit(solution)/shard_map/ppermute | solution.py:262
  52.5 5.9 %collective-permute-start.20 = (f32[192,128]{1,0:T(8,128)S(1)}, f32[192,128]{1,0:T(8,128)S(1)}, u32[]{:S(2)}, u32[]{:S(2)}) collective-permute-start(f32[192,128]{1,0:T(8,128)S(1)} %shard_map.77.refs_0_), channel_id=1, source_target_pairs={{0,4},{1,5},{2,6},{3,7},{4,0},{5,1},{6,2},{7,3},{8,12},{9,13},{10,... | collective-permute-start | bytes 294920 | tf_op jit(solution)/shard_map/ppermute | solution.py:262
  54.0 4.4 %collective-permute-start.21 = (f32[192,128]{1,0:T(8,128)S(1)}, f32[192,128]{1,0:T(8,128)S(1)}, u32[]{:S(2)}, u32[]{:S(2)}) collective-permute-start(f32[192,128]{1,0:T(8,128)S(1)} %collective-permute-done.16.refs_1_), channel_id=1, source_target_pairs={{0,4},{1,5},{2,6},{3,7},{4,0},{5,1},{6,2},{7,3},{8,12},{9,13},{10,... | collective-permute-start | bytes 294920 | tf_op jit(solution)/shard_map/ppermute | solution.py:262
  54.3 4.2 %collective-permute-start.22 = (f32[192,128]{1,0:T(8,128)S(1)}, f32[192,128]{1,0:T(8,128)S(1)}, u32[]{:S(2)}, u32[]{:S(2)}) collective-permute-start(f32[192,128]{1,0:T(8,128)S(1)} %collective-permute-done.17.refs_2_), channel_id=1, source_target_pairs={{0,4},{1,5},{2,6},{3,7},{4,0},{5,1},{6,2},{7,3},{8,12},{9,13},{10,... | collective-permute-start | bytes 294920 | tf_op jit(solution)/shard_map/ppermute | solution.py:262
  56.4 2.1 %collective-permute-start.23 = (f32[192,128]{1,0:T(8,128)S(1)}, f32[192,128]{1,0:T(8,128)S(1)}, u32[]{:S(2)}, u32[]{:S(2)}) collective-permute-start(f32[192,128]{1,0:T(8,128)S(1)} %collective-permute-done.18.refs_3_), channel_id=1, source_target_pairs={{0,4},{1,5},{2,6},{3,7},{4,0},{5,1},{6,2},{7,3},{8,12},{9,13},{10,... | collective-permute-start | bytes 294920 | tf_op jit(solution)/shard_map/ppermute | solution.py:262

commit v9 on v7

--- a/solution.py
+++ b/solution.py
@@ -82,16 +82,16 @@
 
 
 def start_kernel(*refs):
-    sources, (own, give, own_inverse), pieces, buffers, sems = refs[:4], refs[4:7], refs[7:-5], refs[-5:-1], refs[-1]
+    sources, (own, give, own_inverse), buffers, sems = refs[:3], refs[3:6], refs[6:9], refs[9]
     copies = [
         pltpu.make_async_copy(source, buffer, sems.at[index])
         for index, (source, buffer) in enumerate(zip(sources, buffers))
     ]
     for copy in copies:
         copy.start()
-    for copy in copies[:3]:
+    for copy in copies:
         copy.wait()
-    live, panel, inverse, matrix = buffers
+    live, panel, inverse = buffers
     first = lax.axis_index("side") == 0
     row = lax.broadcasted_iota(jnp.int32, own.shape, 0)
     rows = panel[0]
@@ -104,7 +104,13 @@
     one, two = (jnp.concatenate([inverse[0, s], spare], 0) for s in range(2))
     own_inverse[...] = jnp.where(first, one, two)
     give[height:] = jnp.where(first, two, one)
-    copies[3].wait()
+
+
+def flip_kernel(source, *refs):
+    pieces, matrix, sem = refs[:-2], refs[-2], refs[-1]
+    copy = pltpu.make_async_copy(source, matrix, sem)
+    copy.start()
+    copy.wait()
     at = 0
     for piece in pieces:
         piece[...] = matrix[0, :, at : at + piece.shape[0]].T
@@ -235,24 +241,31 @@
 
     extent = sigma_rows.shape[2]
     block = shape((height, width), bf16)
-    cuts = (extent * 25 // 32, extent * 7 // 32)
+    cuts = (extent // 2, extent * 3 // 8, extent // 8)
     size = pl.cdiv(inv_diag.shape[2], ROWS) * ROWS
-    own, give, own_inverse, *pieces = call(
+    own, give, own_inverse = call(
         start_kernel,
-        [block, shape((height + size, width), bf16), shape((size, width), bf16)]
-        + [shape((lines, extent), bf16) for lines in cuts],
-        [HBM] * 4,
-        *map(stay, (live, panel, inv_diag, sigma_rows)),
+        [block, shape((height + size, width), bf16), shape((size, width), bf16)],
+        [HBM] * 3,
+        *map(stay, (live, panel, inv_diag)),
         scratch=[pltpu.SMEM(live.shape, jnp.int32)]
-        + [pltpu.VMEM(x.shape, bf16) for x in (panel, inv_diag, sigma_rows)]
-        + [dma((4,))],
+        + [pltpu.VMEM(x.shape, bf16) for x in (panel, inv_diag)]
+        + [dma((3,))],
+    )
+    pieces = call(
+        flip_kernel,
+        [shape((lines, extent), bf16) for lines in cuts],
+        [HBM],
+        stay(sigma_rows),
+        scratch=[pltpu.VMEM(sigma_rows.shape, bf16), dma(())],
+        after=[own],
     )
     got = swap(give, side=1)
     got, got_inverse = got[:height], got[height:]
     blocks = []
-    for start in (own, got):
-        pair = jnp.stack([start, swap(start, column=2)])
-        blocks += [pair, swap(pair, column=1)]
+    for one in (own, got):
+        two = swap(one, column=2)
+        blocks += [one, two, swap(one, column=1), swap(two, column=1)]
     far = [swap(piece, side=1) for piece in pieces]
 
     pack = shape((extent + 2 * size, width), bf16)
@@ -285,8 +298,8 @@
     near, far = deliver(out_near, 0), deliver(out_far, 1)
     add = functools.partial(call, add_kernel, part, [VMEM] * 2)
     total = add(keep, came)
+    total = add(total, swap(total, column=2))
     total = add(total, swap(total, column=1), after=[near, far])
-    total = add(total, swap(total, column=2))
     quarters = [total, swap(total, side=1), swap(total, point=1), swap(total, side=1, point=1)]
     quarters += [swap(x, core=1) for x in quarters]
     return call(

time: 61.7 us -> 58.8 us (0.953)
  waiting for transfers between devices: 29.6 us -> 25.2 us
  Pallas kernels: 4.87 us -> 5.91 us
    ppermute x2, waiting for transfers between devices: 4.68 us -> 0.41 us  [deliver(): return lax.ppermute(x, AXES, pairs)]
    pallas_call x8 -> x9, Pallas kernels: 4.87 us -> 5.91 us  [call(): pl.pallas_call(body, out_shape=outs, in_specs=list(specs) + [ANY] * len(a...]
    ppermute x2, starting transfers between devices: 4.55 us -> 5.3 us  [deliver(): return lax.ppermute(x, AXES, pairs)]
    ppermute x19 -> x22, starting transfers between devices: 21.1 us -> 20.7 us  [swap(): return lax.ppermute(x, AXES, [(i, i ^ mask) for i in range(devices)])]
    ppermute x19 -> x22, waiting for transfers between devices: 24.9 us -> 24.8 us  [swap(): return lax.ppermute(x, AXES, [(i, i ^ mask) for i in range(devices)])]
  transfers between devices with their start and end apart: 21 -> 24, of which waited for: 13 -> 15; matrix products, arithmetic and copies ran while one was open for 0% -> 0% of each run, Pallas kernels for 0% -> 3%
where the time goes in v9:
time: 58.8 us; the launch traced here: 58.6 us
  starting transfers between devices  26 us (44%)
  waiting for transfers between devices  25.2 us (43%)
  Pallas kernels  5.91 us (10%)
  between operations  1.4 us (2%)
    ppermute x22, waiting for transfers between devices, swap(): return lax.ppermute(x, AXES, [(i, i ^ mask) for i in range(devices)])  24.8 us
    ppermute x22, starting transfers between devices, swap(): return lax.ppermute(x, AXES, [(i, i ^ mask) for i in range(devices)])  20.7 us
    pallas_call x9, Pallas kernels, call(): pl.pallas_call(body, out_shape=outs, in_specs=list(specs) + [ANY] * len(a...  5.91 us
    ppermute x2, starting transfers between devices, deliver(): return lax.ppermute(x, AXES, pairs)  5.3 us
  transfers between devices with their start and end apart: 24, of which 15 were waited for; matrix products, arithmetic and copies ran while one was open for 0% of the time, Pallas kernels for 3%

profile of v9, /device:TPU:0, one launch (start us, length us, event | category | flops | bytes accessed | tf_op | source)
XLA Modules:
  0.0 58.6 jit_solution(1484294042670577615)
XLA Ops:
  0.6 1.5 %shard_map.68 = (bf16[128,384]{1,0:T(8,128)(2,1)S(1)}, bf16[160,384]{1,0:T(8,128)(2,1)S(1)}, bf16[32,384]{1,0:T(8,128)(2,1)S(1)}) custom-call(s32[2]{0:T(128)} %bitcast.1, bf16[1,128,2,384]{3,2,1,0:T(2,128)(2,1)} %refs_1_.1, bf16[1,2,24,384]{3,2,1,0:T(8,128)(2,1)} %refs_2_.1), custom_call_target="tpu_custom_call" | custom-call | tf_op jit(solution)/shard_map/pallas_call | solution.py:28
  2.1 3.0 %collective-permute-start.3 = (bf16[160,384]{1,0:T(8,128)(2,1)S(1)}, bf16[160,384]{1,0:T(8,128)(2,1)S(1)}, u32[]{:S(2)}, u32[]{:S(2)}) collective-permute-start(bf16[160,384]{1,0:T(8,128)(2,1)S(1)} %get-tuple-element.15), channel_id=1, source_target_pairs={{0,8},{1,9},{2,10},{3,11},{4,12},{5,13},{6,14},{7,15},{8,0},{9,1},... | collective-permute-start | bytes 368648 | tf_op jit(solution)/shard_map/ppermute | solution.py:240
  5.1 2.6 %collective-permute-start = (bf16[128,384]{1,0:T(8,128)(2,1)S(1)}, bf16[128,384]{1,0:T(8,128)(2,1)S(1)}, u32[]{:S(2)}, u32[]{:S(2)}) collective-permute-start(bf16[128,384]{1,0:T(8,128)(2,1)S(1)} %get-tuple-element.14.refs_0_.refs_1_), channel_id=1, source_target_pairs={{0,2},{1,3},{2,0},{3,1},{4,6},{5,7},{6,4},{7,5},{8,10},{9,11},{10,... | collective-permute-start | bytes 294920 | tf_op jit(solution)/shard_map/ppermute | solution.py:240
  7.7 1.3 %shard_map.70 = (bf16[256,512]{1,0:T(8,128)(2,1)S(1)}, bf16[192,512]{1,0:T(8,128)(2,1)S(1)}, bf16[64,512]{1,0:T(8,128)(2,1)S(1)}) custom-call(bf16[1,512,512]{2,1,0:T(8,128)(2,1)} %refs_0_.2, bf16[128,384]{1,0:T(8,128)(2,1)S(1)} %get-tuple-element.14.refs_0_.refs_1_), custom_call_target="tpu_custom_call" | custom-call | tf_op jit(solution)/shard_map/pallas_call | solution.py:28
  9.7 1.6 %collective-permute-start.1 = (bf16[128,384]{1,0:T(8,128)(2,1)S(1)}, bf16[128,384]{1,0:T(8,128)(2,1)S(1)}, u32[]{:S(2)}, u32[]{:S(2)}) collective-permute-start(bf16[128,384]{1,0:T(8,128)(2,1)S(1)} %get-tuple-element.14.refs_0_.refs_1_), channel_id=1, source_target_pairs={{0,1},{1,0},{2,3},{3,2},{4,5},{5,4},{6,7},{7,6},{8,9},{9,8},{10,11... | collective-permute-start | bytes 294920 | tf_op jit(solution)/shard_map/ppermute | solution.py:240
  11.7 2.2 %collective-permute-start.8 = (bf16[192,512]{1,0:T(8,128)(2,1)S(1)}, bf16[192,512]{1,0:T(8,128)(2,1)S(1)}, u32[]{:S(2)}, u32[]{:S(2)}) collective-permute-start(bf16[192,512]{1,0:T(8,128)(2,1)S(1)} %get-tuple-element.19.refs_2_), channel_id=1, source_target_pairs={{0,8},{1,9},{2,10},{3,11},{4,12},{5,13},{6,14},{7,15},{8,0},{9,1},... | collective-permute-start | bytes 589832 | tf_op jit(solution)/shard_map/ppermute | solution.py:240
  13.9 1.5 %collective-permute-start.2 = (bf16[128,384]{1,0:T(8,128)(2,1)S(1)}, bf16[128,384]{1,0:T(8,128)(2,1)S(1)}, u32[]{:S(2)}, u32[]{:S(2)}) collective-permute-start(bf16[128,384]{1,0:T(8,128)(2,1)S(1)} %collective-permute-done.refs_1_), channel_id=1, source_target_pairs={{0,1},{1,0},{2,3},{3,2},{4,5},{5,4},{6,7},{7,6},{8,9},{9,8},{10,11... | collective-permute-start | bytes 294920 | tf_op jit(solution)/shard_map/ppermute | solution.py:240
  16.0 0.8 %collective-permute-start.5 = (bf16[128,384]{1,0:T(8,128)(2,1)S(1)}, bf16[128,384]{1,0:T(8,128)(2,1)S(1)}, u32[]{:S(2)}, u32[]{:S(2)}) collective-permute-start(bf16[128,384]{1,0:T(8,128)(2,1)S(1)} %slice.8.refs_4_), channel_id=1, source_target_pairs={{0,1},{1,0},{2,3},{3,2},{4,5},{5,4},{6,7},{7,6},{8,9},{9,8},{10,11... | collective-permute-start | bytes 294920 | tf_op jit(solution)/shard_map/ppermute | solution.py:240
  16.7 1.1 %collective-permute-done.4.refs_5_ = bf16[128,384]{1,0:T(8,128)(2,1)S(1)} collective-permute-done((bf16[128,384]{1,0:T(8,128)(2,1)S(1)}, bf16[128,384]{1,0:T(8,128)(2,1)S(1)}, u32[]{:S(2)}, u32[]{:S(2)}) %collective-permute-start.4) | collective-permute-done | bytes 98336 | tf_op jit(solution)/shard_map/ppermute | solution.py:240
  18.0 2.0 %collective-permute-done.2.refs_3_ = bf16[128,384]{1,0:T(8,128)(2,1)S(1)} collective-permute-done((bf16[128,384]{1,0:T(8,128)(2,1)S(1)}, bf16[128,384]{1,0:T(8,128)(2,1)S(1)}, u32[]{:S(2)}, u32[]{:S(2)}) %collective-permute-start.2) | collective-permute-done | bytes 98336 | tf_op jit(solution)/shard_map/ppermute | solution.py:240
  20.0 1.1 %collective-permute-start.9 = (bf16[64,512]{1,0:T(8,128)(2,1)S(1)}, bf16[64,512]{1,0:T(8,128)(2,1)S(1)}, u32[]{:S(2)}, u32[]{:S(2)}) collective-permute-start(bf16[64,512]{1,0:T(8,128)(2,1)S(1)} %get-tuple-element.20.refs_3_), channel_id=1, source_target_pairs={{0,8},{1,9},{2,10},{3,11},{4,12},{5,13},{6,14},{7,15},{8,0},{9,1},... | collective-permute-start | bytes 196616 | tf_op jit(solution)/shard_map/ppermute | solution.py:240
  21.1 0.6 %collective-permute-done.5.refs_6_ = bf16[128,384]{1,0:T(8,128)(2,1)S(1)} collective-permute-done((bf16[128,384]{1,0:T(8,128)(2,1)S(1)}, bf16[128,384]{1,0:T(8,128)(2,1)S(1)}, u32[]{:S(2)}, u32[]{:S(2)}) %collective-permute-start.5) | collective-permute-done | bytes 98336 | tf_op jit(solution)/shard_map/ppermute | solution.py:240
  21.7 1.1 %collective-permute-done.6.refs_7_ = bf16[128,384]{1,0:T(8,128)(2,1)S(1)} collective-permute-done((bf16[128,384]{1,0:T(8,128)(2,1)S(1)}, bf16[128,384]{1,0:T(8,128)(2,1)S(1)}, u32[]{:S(2)}, u32[]{:S(2)}) %collective-permute-start.6) | collective-permute-done | bytes 98336 | tf_op jit(solution)/shard_map/ppermute | solution.py:240
  22.9 1.4 %collective-permute-done.9.refs_6_ = bf16[64,512]{1,0:T(8,128)(2,1)S(1)} collective-permute-done((bf16[64,512]{1,0:T(8,128)(2,1)S(1)}, bf16[64,512]{1,0:T(8,128)(2,1)S(1)}, u32[]{:S(2)}, u32[]{:S(2)}) %collective-permute-start.9) | collective-permute-done | bytes 65568 | tf_op jit(solution)/shard_map/ppermute | solution.py:240
  24.3 0.7 %shard_map.71.refs_1_ = f32[512,384]{1,0:T(8,128)S(1)} custom-call(bf16[2,512,384]{2,1,0:T(8,128)(2,1)S(1)} %get-tuple-element.17.refs_0_, bf16[256,512]{1,0:T(8,128)(2,1)S(1)} %get-tuple-element.18.refs_1_, bf16[192,512]{1,0:T(8,128)(2,1)S(1)} %get-tuple-element.19.refs_2_, bf16[64,512]{1,0:T(8,128)(2,1)S(1)} %get-tuple-element.20.refs_3_, ...), custom_call_target="tpu_custom_call" | custom-call | tf_op jit(solution)/shard_map/pallas_call | solution.py:28
  26.3 1.7 %collective-permute-done.11.refs_4_ = bf16[576,384]{1,0:T(8,128)(2,1)S(1)} collective-permute-done((bf16[576,384]{1,0:T(8,128)(2,1)S(1)}, bf16[576,384]{1,0:T(8,128)(2,1)S(1)}, u32[]{:S(2)}, u32[]{:S(2)}) %collective-permute-start.11) | collective-permute-done | bytes 442400 | tf_op jit(solution)/shard_map/ppermute | solution.py:240
  28.0 0.6 %shard_map.72 = (bf16[128,384]{1,0:T(8,128)(2,1)S(1)}, bf16[128,384]{1,0:T(8,128)(2,1)S(1)}, f32[192,128]{1,0:T(8,128)S(1)}, f32[192,128]{1,0:T(8,128)S(1)}) custom-call(f32[1]{0:T(128)S(6)} %copy.7.refs_0_, f32[512,384]{1,0:T(8,128)S(1)} %shard_map.71.refs_1_, f32[512,384]{1,0:T(8,128)S(1)} %collective-permute-done.10.refs_2_, ...), custom_call_target="tpu_custom_call" | custom-call | tf_op jit(solution)/shard_map/pallas_call | solution.py:28
  28.6 1.6 %collective-permute-start.12 = (f32[192,128]{1,0:T(8,128)S(1)}, f32[192,128]{1,0:T(8,128)S(1)}, u32[]{:S(2)}, u32[]{:S(2)}) collective-permute-start(f32[192,128]{1,0:T(8,128)S(1)} %get-tuple-element.23), channel_id=1, source_target_pairs={{0,16},{1,17},{2,18},{3,19},{4,20},{5,21},{6,22},{7,23},{8,24},{9,... | collective-permute-start | bytes 294920 | tf_op jit(solution)/shard_map/ppermute | solution.py:240
  30.2 3.3 %collective-permute-done.12.refs_1_ = f32[192,128]{1,0:T(8,128)S(1)} collective-permute-done((f32[192,128]{1,0:T(8,128)S(1)}, f32[192,128]{1,0:T(8,128)S(1)}, u32[]{:S(2)}, u32[]{:S(2)}) %collective-permute-start.12) | collective-permute-done | bytes 98336 | tf_op jit(solution)/shard_map/ppermute | solution.py:240
  33.5 1.1 %collective-permute-start.13 = (f32[192,128]{1,0:T(8,128)S(1)}, f32[192,128]{1,0:T(8,128)S(1)}, u32[]{:S(2)}, u32[]{:S(2)}) collective-permute-start(f32[192,128]{1,0:T(8,128)S(1)} %shard_map.73.refs_0_), channel_id=1, source_target_pairs={{0,2},{1,3},{2,0},{3,1},{4,6},{5,7},{6,4},{7,5},{8,10},{9,11},{10,... | collective-permute-start | bytes 294920 | tf_op jit(solution)/shard_map/ppermute | solution.py:240
  34.7 0.7 %collective-permute-start.15 = (bf16[128,384]{1,0:T(8,128)(2,1)S(1)}, bf16[128,384]{1,0:T(8,128)(2,1)S(1)}, u32[]{:S(2)}, u32[]{:S(2)}) collective-permute-start(bf16[128,384]{1,0:T(8,128)(2,1)S(1)} %get-tuple-element.24), channel_id=1, source_target_pairs={{0,0},{1,4},{2,8},{3,12},{4,1},{5,5},{6,9},{7,13},{8,2},{9,6},{10,... | collective-permute-start | bytes 294920 | tf_op jit(solution)/shard_map/ppermute | solution.py:296
  35.3 4.6 %collective-permute-start.16 = (bf16[128,384]{1,0:T(8,128)(2,1)S(1)}, bf16[128,384]{1,0:T(8,128)(2,1)S(1)}, u32[]{:S(2)}, u32[]{:S(2)}) collective-permute-start(bf16[128,384]{1,0:T(8,128)(2,1)S(1)} %get-tuple-element.25), channel_id=1, source_target_pairs={{0,2},{1,6},{2,10},{3,14},{4,3},{5,7},{6,11},{7,15},{8,0},{9,4},{1... | collective-permute-start | bytes 294920 | tf_op jit(solution)/shard_map/ppermute | solution.py:296
  40.0 2.8 %collective-permute-done.13.refs_1_ = f32[192,128]{1,0:T(8,128)S(1)} collective-permute-done((f32[192,128]{1,0:T(8,128)S(1)}, f32[192,128]{1,0:T(8,128)S(1)}, u32[]{:S(2)}, u32[]{:S(2)}) %collective-permute-start.13) | collective-permute-done | bytes 98336 | tf_op jit(solution)/shard_map/ppermute | solution.py:240
  43.3 4.2 %collective-permute-done.14.refs_1_ = f32[192,128]{1,0:T(8,128)S(1)} collective-permute-done((f32[192,128]{1,0:T(8,128)S(1)}, f32[192,128]{1,0:T(8,128)S(1)}, u32[]{:S(2)}, u32[]{:S(2)}) %collective-permute-start.14) | collective-permute-done | bytes 98336 | tf_op jit(solution)/shard_map/ppermute | solution.py:240
  47.5 1.2 %collective-permute-start.17 = (f32[192,128]{1,0:T(8,128)S(1)}, f32[192,128]{1,0:T(8,128)S(1)}, u32[]{:S(2)}, u32[]{:S(2)}) collective-permute-start(f32[192,128]{1,0:T(8,128)S(1)} %shard_map.75.refs_0_), channel_id=1, source_target_pairs={{0,8},{1,9},{2,10},{3,11},{4,12},{5,13},{6,14},{7,15},{8,0},{9,1},... | collective-permute-start | bytes 294920 | tf_op jit(solution)/shard_map/ppermute | solution.py:240
  48.7 1.5 %collective-permute-start.18 = (f32[192,128]{1,0:T(8,128)S(1)}, f32[192,128]{1,0:T(8,128)S(1)}, u32[]{:S(2)}, u32[]{:S(2)}) collective-permute-start(f32[192,128]{1,0:T(8,128)S(1)} %shard_map.75.refs_0_), channel_id=1, source_target_pairs={{0,16},{1,17},{2,18},{3,19},{4,20},{5,21},{6,22},{7,23},{8,24},{9,... | collective-permute-start | bytes 294920 | tf_op jit(solution)/shard_map/ppermute | solution.py:240
  50.2 0.8 %collective-permute-start.19 = (f32[192,128]{1,0:T(8,128)S(1)}, f32[192,128]{1,0:T(8,128)S(1)}, u32[]{:S(2)}, u32[]{:S(2)}) collective-permute-start(f32[192,128]{1,0:T(8,128)S(1)} %shard_map.75.refs_0_), channel_id=1, source_target_pairs={{0,24},{1,25},{2,26},{3,27},{4,28},{5,29},{6,30},{7,31},{8,16},{9,... | collective-permute-start | bytes 294920 | tf_op jit(solution)/shard_map/ppermute | solution.py:240
  51.0 1.9 %collective-permute-done.17.refs_1_ = f32[192,128]{1,0:T(8,128)S(1)} collective-permute-done((f32[192,128]{1,0:T(8,128)S(1)}, f32[192,128]{1,0:T(8,128)S(1)}, u32[]{:S(2)}, u32[]{:S(2)}) %collective-permute-start.17) | collective-permute-done | bytes 98336 | tf_op jit(solution)/shard_map/ppermute | solution.py:240
  52.9 1.1 %collective-permute-done.18.refs_2_ = f32[192,128]{1,0:T(8,128)S(1)} collective-permute-done((f32[192,128]{1,0:T(8,128)S(1)}, f32[192,128]{1,0:T(8,128)S(1)}, u32[]{:S(2)}, u32[]{:S(2)}) %collective-permute-start.18) | collective-permute-done | bytes 98336 | tf_op jit(solution)/shard_map/ppermute | solution.py:240
  54.0 1.8 %collective-permute-done.19.refs_3_ = f32[192,128]{1,0:T(8,128)S(1)} collective-permute-done((f32[192,128]{1,0:T(8,128)S(1)}, f32[192,128]{1,0:T(8,128)S(1)}, u32[]{:S(2)}, u32[]{:S(2)}) %collective-permute-start.19) | collective-permute-done | bytes 98336 | tf_op jit(solution)/shard_map/ppermute | solution.py:240
  55.8 1.3 %collective-permute-done.23.refs_7_ = f32[192,128]{1,0:T(8,128)S(1)} collective-permute-done((f32[192,128]{1,0:T(8,128)S(1)}, f32[192,128]{1,0:T(8,128)S(1)}, u32[]{:S(2)}, u32[]{:S(2)}) %collective-permute-start.23) | collective-permute-done | bytes 98336 | tf_op jit(solution)/shard_map/ppermute | solution.py:240
  57.0 1.6 %shard_map.76 = (bf16[1,128,2,384]{3,2,1,0:T(2,128)(2,1)}, f32[2,384,384]{2,1,0:T(8,128)}) custom-call(f32[192,128]{1,0:T(8,128)S(1)} %shard_map.75.refs_0_, f32[192,128]{1,0:T(8,128)S(1)} %collective-permute-done.17.refs_1_, f32[192,128]{1,0:T(8,128)S(1)} %collective-permute-done.18.refs_2_, f32[192,128]{1,0:T(8,128)S(1)} %collective-permute-done.19.refs_3_, ...), custom_call_target="tpu_custom_call" | custom-call | tf_op jit(solution)/shard_map/pallas_call | solution.py:28
  (29 shorter events, 2.9 us)
Async XLA Ops:
  2.1 9.1 %collective-permute-start.3 = (bf16[160,384]{1,0:T(8,128)(2,1)S(1)}, bf16[160,384]{1,0:T(8,128)(2,1)S(1)}, u32[]{:S(2)}, u32[]{:S(2)}) collective-permute-start(bf16[160,384]{1,0:T(8,128)(2,1)S(1)} %get-tuple-element.15), channel_id=1, source_target_pairs={{0,8},{1,9},{2,10},{3,11},{4,12},{5,13},{6,14},{7,15},{8,0},{9,1},... | collective-permute-start | bytes 368648 | tf_op jit(solution)/shard_map/ppermute | solution.py:240
  5.1 8.7 %collective-permute-start = (bf16[128,384]{1,0:T(8,128)(2,1)S(1)}, bf16[128,384]{1,0:T(8,128)(2,1)S(1)}, u32[]{:S(2)}, u32[]{:S(2)}) collective-permute-start(bf16[128,384]{1,0:T(8,128)(2,1)S(1)} %get-tuple-element.14.refs_0_.refs_1_), channel_id=1, source_target_pairs={{0,2},{1,3},{2,0},{3,1},{4,6},{5,7},{6,4},{7,5},{8,10},{9,11},{10,... | collective-permute-start | bytes 294920 | tf_op jit(solution)/shard_map/ppermute | solution.py:240
  9.1 15.2 %collective-permute-start.7 = (bf16[256,512]{1,0:T(8,128)(2,1)S(1)}, bf16[256,512]{1,0:T(8,128)(2,1)S(1)}, u32[]{:S(2)}, u32[]{:S(2)}) collective-permute-start(bf16[256,512]{1,0:T(8,128)(2,1)S(1)} %get-tuple-element.18.refs_1_), channel_id=1, source_target_pairs={{0,8},{1,9},{2,10},{3,11},{4,12},{5,13},{6,14},{7,15},{8,0},{9,1},... | collective-permute-start | bytes 786440 | tf_op jit(solution)/shard_map/ppermute | solution.py:240
  9.7 6.3 %collective-permute-start.1 = (bf16[128,384]{1,0:T(8,128)(2,1)S(1)}, bf16[128,384]{1,0:T(8,128)(2,1)S(1)}, u32[]{:S(2)}, u32[]{:S(2)}) collective-permute-start(bf16[128,384]{1,0:T(8,128)(2,1)S(1)} %get-tuple-element.14.refs_0_.refs_1_), channel_id=1, source_target_pairs={{0,1},{1,0},{2,3},{3,2},{4,5},{5,4},{6,7},{7,6},{8,9},{9,8},{10,11... | collective-permute-start | bytes 294920 | tf_op jit(solution)/shard_map/ppermute | solution.py:240
  11.3 6.6 %collective-permute-start.4 = (bf16[128,384]{1,0:T(8,128)(2,1)S(1)}, bf16[128,384]{1,0:T(8,128)(2,1)S(1)}, u32[]{:S(2)}, u32[]{:S(2)}) collective-permute-start(bf16[128,384]{1,0:T(8,128)(2,1)S(1)} %slice.8.refs_4_), channel_id=1, source_target_pairs={{0,2},{1,3},{2,0},{3,1},{4,6},{5,7},{6,4},{7,5},{8,10},{9,11},{10,... | collective-permute-start | bytes 294920 | tf_op jit(solution)/shard_map/ppermute | solution.py:240
  11.7 12.6 %collective-permute-start.8 = (bf16[192,512]{1,0:T(8,128)(2,1)S(1)}, bf16[192,512]{1,0:T(8,128)(2,1)S(1)}, u32[]{:S(2)}, u32[]{:S(2)}) collective-permute-start(bf16[192,512]{1,0:T(8,128)(2,1)S(1)} %get-tuple-element.19.refs_2_), channel_id=1, source_target_pairs={{0,8},{1,9},{2,10},{3,11},{4,12},{5,13},{6,14},{7,15},{8,0},{9,1},... | collective-permute-start | bytes 589832 | tf_op jit(solution)/shard_map/ppermute | solution.py:240
  13.9 6.1 %collective-permute-start.2 = (bf16[128,384]{1,0:T(8,128)(2,1)S(1)}, bf16[128,384]{1,0:T(8,128)(2,1)S(1)}, u32[]{:S(2)}, u32[]{:S(2)}) collective-permute-start(bf16[128,384]{1,0:T(8,128)(2,1)S(1)} %collective-permute-done.refs_1_), channel_id=1, source_target_pairs={{0,1},{1,0},{2,3},{3,2},{4,5},{5,4},{6,7},{7,6},{8,9},{9,8},{10,11... | collective-permute-start | bytes 294920 | tf_op jit(solution)/shard_map/ppermute | solution.py:240
  16.0 5.7 %collective-permute-start.5 = (bf16[128,384]{1,0:T(8,128)(2,1)S(1)}, bf16[128,384]{1,0:T(8,128)(2,1)S(1)}, u32[]{:S(2)}, u32[]{:S(2)}) collective-permute-start(bf16[128,384]{1,0:T(8,128)(2,1)S(1)} %slice.8.refs_4_), channel_id=1, source_target_pairs={{0,1},{1,0},{2,3},{3,2},{4,5},{5,4},{6,7},{7,6},{8,9},{9,8},{10,11... | collective-permute-start | bytes 294920 | tf_op jit(solution)/shard_map/ppermute | solution.py:240
  17.9 4.9 %collective-permute-start.6 = (bf16[128,384]{1,0:T(8,128)(2,1)S(1)}, bf16[128,384]{1,0:T(8,128)(2,1)S(1)}, u32[]{:S(2)}, u32[]{:S(2)}) collective-permute-start(bf16[128,384]{1,0:T(8,128)(2,1)S(1)} %collective-permute-done.4.refs_5_), channel_id=1, source_target_pairs={{0,1},{1,0},{2,3},{3,2},{4,5},{5,4},{6,7},{7,6},{8,9},{9,8},{10,11... | collective-permute-start | bytes 294920 | tf_op jit(solution)/shard_map/ppermute | solution.py:240
  20.0 4.3 %collective-permute-start.9 = (bf16[64,512]{1,0:T(8,128)(2,1)S(1)}, bf16[64,512]{1,0:T(8,128)(2,1)S(1)}, u32[]{:S(2)}, u32[]{:S(2)}) collective-permute-start(bf16[64,512]{1,0:T(8,128)(2,1)S(1)} %get-tuple-element.20.refs_3_), channel_id=1, source_target_pairs={{0,8},{1,9},{2,10},{3,11},{4,12},{5,13},{6,14},{7,15},{8,0},{9,1},... | collective-permute-start | bytes 196616 | tf_op jit(solution)/shard_map/ppermute | solution.py:240
  25.0 3.0 %collective-permute-start.10 = (f32[512,384]{1,0:T(8,128)S(1)}, f32[512,384]{1,0:T(8,128)S(1)}, u32[]{:S(2)}, u32[]{:S(2)}) collective-permute-start(f32[512,384]{1,0:T(8,128)S(1)} %shard_map.71.refs_1_), channel_id=1, source_target_pairs={{0,4},{1,5},{2,6},{3,7},{4,0},{5,1},{6,2},{7,3},{8,12},{9,13},{10,... | collective-permute-start | bytes 2359304 | tf_op jit(solution)/shard_map/ppermute | solution.py:240
  25.1 2.9 %collective-permute-start.11 = (bf16[576,384]{1,0:T(8,128)(2,1)S(1)}, bf16[576,384]{1,0:T(8,128)(2,1)S(1)}, u32[]{:S(2)}, u32[]{:S(2)}) collective-permute-start(bf16[576,384]{1,0:T(8,128)(2,1)S(1)} %get-tuple-element.21.refs_3_), channel_id=1, source_target_pairs={{0,4},{1,5},{2,6},{3,7},{4,0},{5,1},{6,2},{7,3},{8,12},{9,13},{10,... | collective-permute-start | bytes 1327112 | tf_op jit(solution)/shard_map/ppermute | solution.py:240
  26.2 30.8 %copy-start = (s32[2,1]{0,1:T(1,128)S(1)}, s32[2,1]{0,1:T(1,128)}, u32[]{:S(2)}) copy-start(s32[2,1]{0,1:T(1,128)} %param.7) | copy-start | bytes 28
  28.6 4.9 %collective-permute-start.12 = (f32[192,128]{1,0:T(8,128)S(1)}, f32[192,128]{1,0:T(8,128)S(1)}, u32[]{:S(2)}, u32[]{:S(2)}) collective-permute-start(f32[192,128]{1,0:T(8,128)S(1)} %get-tuple-element.23), channel_id=1, source_target_pairs={{0,16},{1,17},{2,18},{3,19},{4,20},{5,21},{6,22},{7,23},{8,24},{9,... | collective-permute-start | bytes 294920 | tf_op jit(solution)/shard_map/ppermute | solution.py:240
  33.5 9.2 %collective-permute-start.13 = (f32[192,128]{1,0:T(8,128)S(1)}, f32[192,128]{1,0:T(8,128)S(1)}, u32[]{:S(2)}, u32[]{:S(2)}) collective-permute-start(f32[192,128]{1,0:T(8,128)S(1)} %shard_map.73.refs_0_), channel_id=1, source_target_pairs={{0,2},{1,3},{2,0},{3,1},{4,6},{5,7},{6,4},{7,5},{8,10},{9,11},{10,... | collective-permute-start | bytes 294920 | tf_op jit(solution)/shard_map/ppermute | solution.py:240
  34.7 8.2 %collective-permute-start.15 = (bf16[128,384]{1,0:T(8,128)(2,1)S(1)}, bf16[128,384]{1,0:T(8,128)(2,1)S(1)}, u32[]{:S(2)}, u32[]{:S(2)}) collective-permute-start(bf16[128,384]{1,0:T(8,128)(2,1)S(1)} %get-tuple-element.24), channel_id=1, source_target_pairs={{0,0},{1,4},{2,8},{3,12},{4,1},{5,5},{6,9},{7,13},{8,2},{9,6},{10,... | collective-permute-start | bytes 294920 | tf_op jit(solution)/shard_map/ppermute | solution.py:296
  35.3 7.9 %collective-permute-start.16 = (bf16[128,384]{1,0:T(8,128)(2,1)S(1)}, bf16[128,384]{1,0:T(8,128)(2,1)S(1)}, u32[]{:S(2)}, u32[]{:S(2)}) collective-permute-start(bf16[128,384]{1,0:T(8,128)(2,1)S(1)} %get-tuple-element.25), channel_id=1, source_target_pairs={{0,2},{1,6},{2,10},{3,14},{4,3},{5,7},{6,11},{7,15},{8,0},{9,4},{1... | collective-permute-start | bytes 294920 | tf_op jit(solution)/shard_map/ppermute | solution.py:296
  42.8 4.7 %collective-permute-start.14 = (f32[192,128]{1,0:T(8,128)S(1)}, f32[192,128]{1,0:T(8,128)S(1)}, u32[]{:S(2)}, u32[]{:S(2)}) collective-permute-start(f32[192,128]{1,0:T(8,128)S(1)} %shard_map.74.refs_0_), channel_id=1, source_target_pairs={{0,1},{1,0},{2,3},{3,2},{4,5},{5,4},{6,7},{7,6},{8,9},{9,8},{10,11... | collective-permute-start | bytes 294920 | tf_op jit(solution)/shard_map/ppermute | solution.py:240
  47.5 5.4 %collective-permute-start.17 = (f32[192,128]{1,0:T(8,128)S(1)}, f32[192,128]{1,0:T(8,128)S(1)}, u32[]{:S(2)}, u32[]{:S(2)}) collective-permute-start(f32[192,128]{1,0:T(8,128)S(1)} %shard_map.75.refs_0_), channel_id=1, source_target_pairs={{0,8},{1,9},{2,10},{3,11},{4,12},{5,13},{6,14},{7,15},{8,0},{9,1},... | collective-permute-start | bytes 294920 | tf_op jit(solution)/shard_map/ppermute | solution.py:240
  48.7 5.2 %collective-permute-start.18 = (f32[192,128]{1,0:T(8,128)S(1)}, f32[192,128]{1,0:T(8,128)S(1)}, u32[]{:S(2)}, u32[]{:S(2)}) collective-permute-start(f32[192,128]{1,0:T(8,128)S(1)} %shard_map.75.refs_0_), channel_id=1, source_target_pairs={{0,16},{1,17},{2,18},{3,19},{4,20},{5,21},{6,22},{7,23},{8,24},{9,... | collective-permute-start | bytes 294920 | tf_op jit(solution)/shard_map/ppermute | solution.py:240
  50.2 5.5 %collective-permute-start.19 = (f32[192,128]{1,0:T(8,128)S(1)}, f32[192,128]{1,0:T(8,128)S(1)}, u32[]{:S(2)}, u32[]{:S(2)}) collective-permute-start(f32[192,128]{1,0:T(8,128)S(1)} %shard_map.75.refs_0_), channel_id=1, source_target_pairs={{0,24},{1,25},{2,26},{3,27},{4,28},{5,29},{6,30},{7,31},{8,16},{9,... | collective-permute-start | bytes 294920 | tf_op jit(solution)/shard_map/ppermute | solution.py:240
  51.0 4.7 %collective-permute-start.20 = (f32[192,128]{1,0:T(8,128)S(1)}, f32[192,128]{1,0:T(8,128)S(1)}, u32[]{:S(2)}, u32[]{:S(2)}) collective-permute-start(f32[192,128]{1,0:T(8,128)S(1)} %shard_map.75.refs_0_), channel_id=1, source_target_pairs={{0,4},{1,5},{2,6},{3,7},{4,0},{5,1},{6,2},{7,3},{8,12},{9,13},{10,... | collective-permute-start | bytes 294920 | tf_op jit(solution)/shard_map/ppermute | solution.py:240
  52.9 2.9 %collective-permute-start.21 = (f32[192,128]{1,0:T(8,128)S(1)}, f32[192,128]{1,0:T(8,128)S(1)}, u32[]{:S(2)}, u32[]{:S(2)}) collective-permute-start(f32[192,128]{1,0:T(8,128)S(1)} %collective-permute-done.17.refs_1_), channel_id=1, source_target_pairs={{0,4},{1,5},{2,6},{3,7},{4,0},{5,1},{6,2},{7,3},{8,12},{9,13},{10,... | collective-permute-start | bytes 294920 | tf_op jit(solution)/shard_map/ppermute | solution.py:240
  53.9 1.8 %collective-permute-start.22 = (f32[192,128]{1,0:T(8,128)S(1)}, f32[192,128]{1,0:T(8,128)S(1)}, u32[]{:S(2)}, u32[]{:S(2)}) collective-permute-start(f32[192,128]{1,0:T(8,128)S(1)} %collective-permute-done.18.refs_2_), channel_id=1, source_target_pairs={{0,4},{1,5},{2,6},{3,7},{4,0},{5,1},{6,2},{7,3},{8,12},{9,13},{10,... | collective-permute-start | bytes 294920 | tf_op jit(solution)/shard_map/ppermute | solution.py:240
  55.7 1.3 %collective-permute-start.23 = (f32[192,128]{1,0:T(8,128)S(1)}, f32[192,128]{1,0:T(8,128)S(1)}, u32[]{:S(2)}, u32[]{:S(2)}) collective-permute-start(f32[192,128]{1,0:T(8,128)S(1)} %collective-permute-done.19.refs_3_), channel_id=1, source_target_pairs={{0,4},{1,5},{2,6},{3,7},{4,0},{5,1},{6,2},{7,3},{8,12},{9,13},{10,... | collective-permute-start | bytes 294920 | tf_op jit(solution)/shard_map/ppermute | solution.py:240

commit v10 on v7

--- a/solution.py
+++ b/solution.py
@@ -16,7 +16,7 @@
 AXES = ("hyp", "side", "core", "pcol")
 
 
-def call(kernel, outs, specs, *operands, scratch=(), out_specs=None, after=(), alias={}):
+def call(kernel, outs, specs, *operands, scratch=(), out_specs=None, after=()):
     many = isinstance(outs, (list, tuple))
     count = len(specs)
 
@@ -31,7 +31,6 @@
         in_specs=list(specs) + [ANY] * len(after),
         out_specs=out_specs,
         scratch_shapes=scratch,
-        input_output_aliases=alias,
         compiler_params=pltpu.CompilerParams(vmem_limit_bytes=32 * 2**20),
     )(*operands, *after)
 
@@ -82,7 +81,8 @@
 
 
 def start_kernel(*refs):
-    sources, (own, give, own_inverse), pieces, buffers, sems = refs[:4], refs[4:7], refs[7:-5], refs[-5:-1], refs[-1]
+    sources, (own, give, own_inverse), pieces = refs[:4], refs[4:7], refs[7:-5]
+    buffers, sems = refs[-5:-1], refs[-1]
     copies = [
         pltpu.make_async_copy(source, buffer, sems.at[index])
         for index, (source, buffer) in enumerate(zip(sources, buffers))
@@ -112,19 +112,13 @@
 
 
 def gather_kernel(*refs):
-    blocks, (own_inverse, got_inverse, rows, pack) = [], refs[-4:]
-    for ref in refs[:-4]:
-        blocks += [ref] if len(ref.shape) == 2 else [ref.at[0], ref.at[1]]
+    blocks, (rows, pack) = refs[:-2], refs[-2:]
     column = lax.axis_index("pcol")
     height = blocks[0].shape[0]
     for index, block in enumerate(blocks):
         spot = jnp.bitwise_xor(column, (0, 2, 1, 3)[index % 4])
         rows[index // 4, pl.ds(pl.multiple_of(spot * height, height), height), :] = block[...]
-    extent = rows.shape[1]
-    size = own_inverse.shape[0]
-    pack[:extent] = rows[jnp.where(column // 2 == lax.axis_index("side"), 0, 1)]
-    pack[extent : extent + size] = own_inverse[...]
-    pack[extent + size :] = got_inverse[...]
+    pack[...] = rows[jnp.where(column // 2 == lax.axis_index("side"), 0, 1)]
 
 
 def apply_kernel(rows, *refs):
@@ -138,42 +132,36 @@
         at += own.shape[0]
 
 
-def couple_kernel(weight, mine, other, pack, got_pack, out_near, out_far, keep, send, half, packed):
-    core, column, point = (lax.axis_index(name) for name in ("core", "pcol", "hyp"))
-    applied = mine[...] + other[...]
-    high = applied.astype(jnp.bfloat16)
-    low = (applied - high.astype(jnp.float32)).astype(jnp.bfloat16)
-    half[...] = -high
-    extent = applied.shape[0]
-    rows = jnp.where(column % 2 == core, pack[:extent], got_pack[:extent])
-    inverse = (pack[extent:], got_pack[extent:])
-    blocks = tiles(applied.shape[1])
-    per = len(blocks) // 2
-    for part in range(2):
-
-        @pl.when(core == part)
-        def _():
-            mine_blocks = blocks[part * per : (part + 1) * per]
-            at = 0
-            for first in sorted({a for a, _ in mine_blocks}):
-                seconds = [b for a, b in mine_blocks if a == first]
-                left = slice(first * LANES, (first + 1) * LANES)
-                right = slice(seconds[0] * LANES, (seconds[-1] + 1) * LANES)
-                total = transposed_dot(rows[:, left], high[:, right])
-                total += transposed_dot(rows[:, left], low[:, right])
-                for lines in inverse:
-                    total += transposed_dot(lines[:, left], lines[:, right])
-                for index in range(len(seconds)):
-                    packed[at * LANES : (at + 1) * LANES, :] = (
-                        weight[0] * total[:, index * LANES : (index + 1) * LANES]
-                    )
-                    at += 1
-
+def couple_kernel(weight, applied, pack, got_pack, own_inverse, got_inverse, keep, send, packed):
+    core, column = lax.axis_index("core"), lax.axis_index("pcol")
+    high = applied[...].astype(jnp.bfloat16)
+    low = (applied[...] - high.astype(jnp.float32)).astype(jnp.bfloat16)
+    rows = jnp.where(column % 2 == core, pack[...], got_pack[...])
+    at = 0
+    for first in range(rows.shape[1] // LANES):
+        left, right = slice(first * LANES, (first + 1) * LANES), slice(first * LANES, None)
+        total = transposed_dot(rows[:, left], high[:, right])
+        total += transposed_dot(rows[:, left], low[:, right])
+        for lines in (own_inverse, got_inverse):
+            total += transposed_dot(lines[:, left], lines[:, right])
+        for index in range(total.shape[1] // LANES):
+            packed[at : at + LANES, :] = weight[0] * total[:, index * LANES : (index + 1) * LANES]
+            at += LANES
     size = keep.shape[0]
-    keep[...] = packed[pl.ds(pl.multiple_of(point * size, 8), size), :]
-    send[...] = packed[pl.ds(pl.multiple_of((1 - point) * size, 8), size), :]
-    height = out_near.shape[0]
-    side = lax.axis_index("side")
+    keep[...] = packed[pl.ds(pl.multiple_of(core * size, LANES), size), :]
+    send[...] = packed[pl.ds(pl.multiple_of((1 - core) * size, LANES), size), :]
+
+
+def halve_kernel(mine, came, keep, send, whole):
+    whole[...] = mine[...] + came[...]
+    size, point = keep.shape[0], lax.axis_index("hyp")
+    keep[...] = whole[pl.ds(pl.multiple_of(point * size, 8), size), :]
+    send[...] = whole[pl.ds(pl.multiple_of((1 - point) * size, 8), size), :]
+
+
+def output_kernel(mine, other, out_near, out_far, half):
+    half[...] = -(mine[...] + other[...]).astype(jnp.bfloat16)
+    height, side, core = out_near.shape[0], lax.axis_index("side"), lax.axis_index("core")
     for out, at in ((out_near, side), (out_far, 1 - side)):
         spot = at * 2 + core
         out[...] = half[pl.ds(pl.multiple_of(spot * height, height), height), :]
@@ -183,13 +171,21 @@
     out[...] = mine[...] + came[...]
 
 
-def finish_kernel(*refs):
-    parts, (live_hbm, near, far, rows_out, out, live, block, lines, result, sems) = refs[:8], refs[8:]
+def rows_kernel(live_hbm, near, far, out, live, sem):
+    copy = pltpu.make_async_copy(live_hbm, live, sem)
+    copy.start()
+    row = lax.broadcasted_iota(jnp.int32, near.shape, 0)
+    first = lax.axis_index("pcol") // 2 == 0
+    pair = (jnp.where(first, near[...], far[...]), jnp.where(first, far[...], near[...]))
+    copy.wait()
+    for s, value in enumerate(pair):
+        out[0, :, s, :] = jnp.where(row < live[s], value, jnp.zeros(value.shape, value.dtype))
+
+
+def spread_kernel(*refs):
+    parts, (out, lines, result, sems) = refs[:8], refs[8:]
     point, side, core = (lax.axis_index(name) for name in ("hyp", "side", "core"))
-    copy = pltpu.make_async_copy(live_hbm, live, sems.at[0])
-    copy.start()
-    width = result.shape[1]
-    blocks = tiles(width)
+    blocks = tiles(result.shape[1])
     size = parts[0].shape[0]
     for index, part in enumerate(parts):
         owner = core if index < 4 else 1 - core
@@ -199,21 +195,19 @@
         lines[node, pl.ds(start, size), :] = part[...]
     copies = []
     for node in range(2):
-        for index, (a, b) in enumerate(blocks):
-            tile = lines[node, index * LANES : (index + 1) * LANES, :]
-            result[node, a * LANES : (a + 1) * LANES, b * LANES : (b + 1) * LANES] = tile
-            if a != b:
-                result[node, b * LANES : (b + 1) * LANES, a * LANES : (a + 1) * LANES] = tile.T
-        copies.append(pltpu.make_async_copy(result.at[node], out.at[node], sems.at[1 + node]))
-        copies[-1].start()
-    copy.wait()
-    row = lax.broadcasted_iota(jnp.int32, near.shape, 0)
-    first = lax.axis_index("pcol") // 2 == 0
-    pair = (jnp.where(first, near[...], far[...]), jnp.where(first, far[...], near[...]))
-    for s, value in enumerate(pair):
-        block[:, s, :] = jnp.where(row < live[s], value, jnp.zeros(value.shape, value.dtype))
-    copies.append(pltpu.make_async_copy(block, rows_out.at[0], sems.at[3]))
-    copies[-1].start()
+        for first in range(result.shape[1] // LANES):
+            rows = slice(first * LANES, (first + 1) * LANES)
+            for index, (a, b) in enumerate(blocks):
+                if a != first:
+                    continue
+                columns = slice(b * LANES, (b + 1) * LANES)
+                tile = lines[node, index * LANES : (index + 1) * LANES, :]
+                result[node, rows, columns] = tile
+                if a != b:
+                    result[node, columns, rows] = tile.T
+            place = (node, rows)
+            copies.append(pltpu.make_async_copy(result.at[place], out.at[place], sems.at[len(copies)]))
+            copies[-1].start()
     for copy in copies:
         copy.wait()
 
@@ -235,7 +229,7 @@
 
     extent = sigma_rows.shape[2]
     block = shape((height, width), bf16)
-    cuts = (extent * 25 // 32, extent * 7 // 32)
+    cuts = (extent // 2, extent // 2)
     size = pl.cdiv(inv_diag.shape[2], ROWS) * ROWS
     own, give, own_inverse, *pieces = call(
         start_kernel,
@@ -250,31 +244,36 @@
     got = swap(give, side=1)
     got, got_inverse = got[:height], got[height:]
     blocks = []
-    for start in (own, got):
-        pair = jnp.stack([start, swap(start, column=2)])
-        blocks += [pair, swap(pair, column=1)]
+    for one in (own, got):
+        two = swap(one, column=2)
+        blocks += [one, two, swap(one, column=1), swap(two, column=1)]
     far = [swap(piece, side=1) for piece in pieces]
 
-    pack = shape((extent + 2 * size, width), bf16)
+
     rows, pack = call(
-        gather_kernel, [shape((2, extent, width), bf16), pack], [VMEM] * (2 + len(blocks)),
-        *blocks, own_inverse, got_inverse,
+        gather_kernel,
+        [shape((2, extent, width), bf16), shape((extent, width), bf16)],
+        [VMEM] * len(blocks),
+        *blocks,
+        after=far,
     )
     got_pack = swap(pack, core=1)
     mine = call(
         apply_kernel, shape((extent, width), f32), [VMEM] * (1 + 2 * len(cuts)), rows, *pieces, *far
     )
+    lines = len(tiles(width)) // 2 * LANES
+    part, half = shape((lines // 2, LANES), f32), shape((lines, LANES), f32)
     other = swap(mine, core=1)
-
-    lines = len(tiles(width)) // 2 * LANES
-    part = shape((lines // 2, LANES), f32)
-    out_near, out_far, keep, send = call(
-        couple_kernel, [block, block, part, part], [SMEM] + [VMEM] * 4,
-        quad_weight, mine, other, pack, got_pack,
-        scratch=[pltpu.VMEM((extent, width), bf16), pltpu.VMEM((lines, LANES), f32)],
+    keep, send = call(
+        couple_kernel, [half, half], [SMEM] + [VMEM] * 5,
+        quad_weight, mine, pack, got_pack, own_inverse, got_inverse,
+        scratch=[pltpu.VMEM((2 * lines, LANES), f32)],
+    )
+    keep, send = call(
+        halve_kernel, [part, part], [VMEM] * 2, keep, swap(send, core=1),
+        scratch=[pltpu.VMEM((lines, LANES), f32)],
     )
     came = swap(send, point=1)
-
     def deliver(x, flip):
         pairs = []
         for i in range(devices):
@@ -282,27 +281,32 @@
             pairs.append((i, (h * 4 + c) * grid + 2 * (s ^ flip) + k))
         return lax.ppermute(x, AXES, pairs)
 
-    near, far = deliver(out_near, 0), deliver(out_far, 1)
     add = functools.partial(call, add_kernel, part, [VMEM] * 2)
     total = add(keep, came)
-    total = add(total, swap(total, column=1), after=[near, far])
+    out_near, out_far = call(
+        output_kernel, [block, block], [VMEM] * 2, mine, other,
+        scratch=[pltpu.VMEM((extent, width), bf16)],
+        after=[total],
+    )
+    sigma_panel = call(
+        rows_kernel, shape((1, height, count, width), bf16), [HBM, VMEM, VMEM],
+        live, deliver(out_near, 0), deliver(out_far, 1),
+        scratch=[pltpu.SMEM(live.shape, jnp.int32), dma(())],
+    )
     total = add(total, swap(total, column=2))
+    total = add(total, swap(total, column=1), after=[stay(sigma_panel)])
     quarters = [total, swap(total, side=1), swap(total, point=1), swap(total, side=1, point=1)]
     quarters += [swap(x, core=1) for x in quarters]
-    return call(
-        finish_kernel,
-        [shape((1, height, count, width), bf16), shape((count, width, width), f32)],
-        [VMEM] * 8 + [HBM] + [VMEM] * 2,
-        *quarters, live, near, far,
+    marginal = call(
+        spread_kernel, shape((count, width, width), f32), [VMEM] * 8, *quarters,
         scratch=[
-            pltpu.SMEM((2,), jnp.int32),
-            pltpu.VMEM((height, count, width), bf16),
             pltpu.VMEM((count, 2 * lines, LANES), f32),
             pltpu.VMEM((count, width, width), f32),
-            dma((4,)),
+            dma((6,)),
         ],
-        out_specs=[HBM, HBM],
-    )
+        out_specs=HBM,
+    )
+    return sigma_panel, marginal
 
 
 def solution(mesh):

time: 61.7 us -> 58.2 us (0.943)
  waiting for transfers between devices: 29.6 us -> 18.1 us
  starting transfers between devices: 25.6 us -> 32.3 us
  Pallas kernels: 4.87 us -> 6.12 us
    ppermute x19 -> x22, waiting for transfers between devices: 24.9 us -> 15.6 us  [swap(): return lax.ppermute(x, AXES, [(i, i ^ mask) for i in range(devices)])]
    ppermute x19 -> x22, starting transfers between devices: 21.1 us -> 27.7 us  [swap(): return lax.ppermute(x, AXES, [(i, i ^ mask) for i in range(devices)])]
    ppermute x2, waiting for transfers between devices: 4.68 us -> 2.54 us  [deliver(): return lax.ppermute(x, AXES, pairs)]
    pallas_call x8 -> x11, Pallas kernels: 4.87 us -> 6.12 us  [call(): pl.pallas_call(body, out_shape=outs, in_specs=list(specs) + [ANY] * len(a...]
  transfers between devices with their start and end apart: 21 -> 24, of which waited for: 13 -> 13; matrix products, arithmetic and copies ran while one was open for 0% -> 0% of each run, Pallas kernels for 0% -> 5%
where the time goes in v10:
time: 58.2 us; the launch traced here: 58 us
  starting transfers between devices  32.3 us (55%)
  waiting for transfers between devices  18.1 us (31%)
  Pallas kernels  6.12 us (11%)
  between operations  1.4 us (2%)
    ppermute x22, starting transfers between devices, swap(): return lax.ppermute(x, AXES, [(i, i ^ mask) for i in range(devices)])  27.7 us
    ppermute x22, waiting for transfers between devices, swap(): return lax.ppermute(x, AXES, [(i, i ^ mask) for i in range(devices)])  15.6 us
    pallas_call x11, Pallas kernels, call(): pl.pallas_call(body, out_shape=outs, in_specs=list(specs) + [ANY] * len(a...  6.12 us
    ppermute x2, starting transfers between devices, deliver(): return lax.ppermute(x, AXES, pairs)  4.59 us
    ppermute x2, waiting for transfers between devices, deliver(): return lax.ppermute(x, AXES, pairs)  2.54 us
  transfers between devices with their start and end apart: 24, of which 13 were waited for; matrix products, arithmetic and copies ran while one was open for 0% of the time, Pallas kernels for 5%

profile of v10, /device:TPU:0, one launch (start us, length us, event | category | flops | bytes accessed | tf_op | source)
XLA Modules:
  0.0 58.0 jit_solution(5772925019283583681)
XLA Ops:
  0.6 1.7 %shard_map.68 = (bf16[128,384]{1,0:T(8,128)(2,1)S(1)}, bf16[160,384]{1,0:T(8,128)(2,1)S(1)}, bf16[32,384]{1,0:T(8,128)(2,1)S(1)}, bf16[256,512]{1,0:T(8,128)(2,1)S(1)}, bf16[256,512]{1,0:T(8,128)(2,1)S(1)}) custom-call(s32[2]{0:T(128)} %bitcast.1, bf16[1,128,2,384]{3,2,1,0:T(2,128)(2,1)} %refs_1_.1, bf16[1,2,24,384]{3,2,1,0:T(8,128)(2,1)} %refs_2_.1, ...), custom_call_target="tpu_custom_call" | custom-call | tf_op jit(solution)/shard_map/pallas_call | solution.py:28
  2.3 3.0 %collective-permute-start.3 = (bf16[160,384]{1,0:T(8,128)(2,1)S(1)}, bf16[160,384]{1,0:T(8,128)(2,1)S(1)}, u32[]{:S(2)}, u32[]{:S(2)}) collective-permute-start(bf16[160,384]{1,0:T(8,128)(2,1)S(1)} %get-tuple-element.16), channel_id=1, source_target_pairs={{0,8},{1,9},{2,10},{3,11},{4,12},{5,13},{6,14},{7,15},{8,0},{9,1},... | collective-permute-start | bytes 368648 | tf_op jit(solution)/shard_map/ppermute | solution.py:228
  5.4 1.9 %collective-permute-start.8 = (bf16[256,512]{1,0:T(8,128)(2,1)S(1)}, bf16[256,512]{1,0:T(8,128)(2,1)S(1)}, u32[]{:S(2)}, u32[]{:S(2)}) collective-permute-start(bf16[256,512]{1,0:T(8,128)(2,1)S(1)} %get-tuple-element.18.refs_2_), channel_id=1, source_target_pairs={{0,8},{1,9},{2,10},{3,11},{4,12},{5,13},{6,14},{7,15},{8,0},{9,1},... | collective-permute-start | bytes 786440 | tf_op jit(solution)/shard_map/ppermute | solution.py:228
  7.4 2.6 %collective-permute-start = (bf16[128,384]{1,0:T(8,128)(2,1)S(1)}, bf16[128,384]{1,0:T(8,128)(2,1)S(1)}, u32[]{:S(2)}, u32[]{:S(2)}) collective-permute-start(bf16[128,384]{1,0:T(8,128)(2,1)S(1)} %get-tuple-element.15.refs_0_), channel_id=1, source_target_pairs={{0,2},{1,3},{2,0},{3,1},{4,6},{5,7},{6,4},{7,5},{8,10},{9,11},{10,... | collective-permute-start | bytes 294920 | tf_op jit(solution)/shard_map/ppermute | solution.py:228
  10.0 1.6 %collective-permute-start.1 = (bf16[128,384]{1,0:T(8,128)(2,1)S(1)}, bf16[128,384]{1,0:T(8,128)(2,1)S(1)}, u32[]{:S(2)}, u32[]{:S(2)}) collective-permute-start(bf16[128,384]{1,0:T(8,128)(2,1)S(1)} %get-tuple-element.15.refs_0_), channel_id=1, source_target_pairs={{0,1},{1,0},{2,3},{3,2},{4,5},{5,4},{6,7},{7,6},{8,9},{9,8},{10,11... | collective-permute-start | bytes 294920 | tf_op jit(solution)/shard_map/ppermute | solution.py:228
  11.6 1.2 %collective-permute-start.4 = (bf16[128,384]{1,0:T(8,128)(2,1)S(1)}, bf16[128,384]{1,0:T(8,128)(2,1)S(1)}, u32[]{:S(2)}, u32[]{:S(2)}) collective-permute-start(bf16[128,384]{1,0:T(8,128)(2,1)S(1)} %slice.8.refs_4_), channel_id=1, source_target_pairs={{0,2},{1,3},{2,0},{3,1},{4,6},{5,7},{6,4},{7,5},{8,10},{9,11},{10,... | collective-permute-start | bytes 294920 | tf_op jit(solution)/shard_map/ppermute | solution.py:228
  13.1 3.8 %collective-permute-start.2 = (bf16[128,384]{1,0:T(8,128)(2,1)S(1)}, bf16[128,384]{1,0:T(8,128)(2,1)S(1)}, u32[]{:S(2)}, u32[]{:S(2)}) collective-permute-start(bf16[128,384]{1,0:T(8,128)(2,1)S(1)} %collective-permute-done.refs_1_), channel_id=1, source_target_pairs={{0,1},{1,0},{2,3},{3,2},{4,5},{5,4},{6,7},{7,6},{8,9},{9,8},{10,11... | collective-permute-start | bytes 294920 | tf_op jit(solution)/shard_map/ppermute | solution.py:228
  17.0 0.7 %collective-permute-start.5 = (bf16[128,384]{1,0:T(8,128)(2,1)S(1)}, bf16[128,384]{1,0:T(8,128)(2,1)S(1)}, u32[]{:S(2)}, u32[]{:S(2)}) collective-permute-start(bf16[128,384]{1,0:T(8,128)(2,1)S(1)} %slice.8.refs_4_), channel_id=1, source_target_pairs={{0,1},{1,0},{2,3},{3,2},{4,5},{5,4},{6,7},{7,6},{8,9},{9,8},{10,11... | collective-permute-start | bytes 294920 | tf_op jit(solution)/shard_map/ppermute | solution.py:228
  17.7 0.6 %collective-permute-done.4.refs_5_ = bf16[128,384]{1,0:T(8,128)(2,1)S(1)} collective-permute-done((bf16[128,384]{1,0:T(8,128)(2,1)S(1)}, bf16[128,384]{1,0:T(8,128)(2,1)S(1)}, u32[]{:S(2)}, u32[]{:S(2)}) %collective-permute-start.4) | collective-permute-done | bytes 98336 | tf_op jit(solution)/shard_map/ppermute | solution.py:228
  18.3 0.7 %collective-permute-start.6 = (bf16[128,384]{1,0:T(8,128)(2,1)S(1)}, bf16[128,384]{1,0:T(8,128)(2,1)S(1)}, u32[]{:S(2)}, u32[]{:S(2)}) collective-permute-start(bf16[128,384]{1,0:T(8,128)(2,1)S(1)} %collective-permute-done.4.refs_5_), channel_id=1, source_target_pairs={{0,1},{1,0},{2,3},{3,2},{4,5},{5,4},{6,7},{7,6},{8,9},{9,8},{10,11... | collective-permute-start | bytes 294920 | tf_op jit(solution)/shard_map/ppermute | solution.py:228
  19.0 1.6 %collective-permute-done.2.refs_3_ = bf16[128,384]{1,0:T(8,128)(2,1)S(1)} collective-permute-done((bf16[128,384]{1,0:T(8,128)(2,1)S(1)}, bf16[128,384]{1,0:T(8,128)(2,1)S(1)}, u32[]{:S(2)}, u32[]{:S(2)}) %collective-permute-start.2) | collective-permute-done | bytes 98336 | tf_op jit(solution)/shard_map/ppermute | solution.py:228
  20.7 1.3 %collective-permute-done.5.refs_6_ = bf16[128,384]{1,0:T(8,128)(2,1)S(1)} collective-permute-done((bf16[128,384]{1,0:T(8,128)(2,1)S(1)}, bf16[128,384]{1,0:T(8,128)(2,1)S(1)}, u32[]{:S(2)}, u32[]{:S(2)}) %collective-permute-start.5) | collective-permute-done | bytes 98336 | tf_op jit(solution)/shard_map/ppermute | solution.py:228
  22.0 1.0 %collective-permute-done.6.refs_7_ = bf16[128,384]{1,0:T(8,128)(2,1)S(1)} collective-permute-done((bf16[128,384]{1,0:T(8,128)(2,1)S(1)}, bf16[128,384]{1,0:T(8,128)(2,1)S(1)}, u32[]{:S(2)}, u32[]{:S(2)}) %collective-permute-start.6) | collective-permute-done | bytes 98336 | tf_op jit(solution)/shard_map/ppermute | solution.py:228
  23.2 0.7 %shard_map.70.refs_1_.refs_0_ = f32[512,384]{1,0:T(8,128)S(1)} custom-call(bf16[2,512,384]{2,1,0:T(8,128)(2,1)S(1)} %get-tuple-element.19.refs_0_, bf16[256,512]{1,0:T(8,128)(2,1)S(1)} %get-tuple-element.17.refs_1_, bf16[256,512]{1,0:T(8,128)(2,1)S(1)} %get-tuple-element.18.refs_2_, bf16[256,512]{1,0:T(8,128)(2,1)S(1)} %collective-permute-done.7.refs_8_.refs_3_, ...), custom_call_target="tpu_custom_call" | custom-call | tf_op jit(solution)/shard_map/pallas_call | solution.py:28
  23.9 0.6 collective-permute-start.9
  25.1 0.7 %shard_map.71 = (f32[384,128]{1,0:T(8,128)S(1)}, f32[384,128]{1,0:T(8,128)S(1)}) custom-call(f32[1]{0:T(128)S(6)} %copy.7.refs_0_, f32[512,384]{1,0:T(8,128)S(1)} %shard_map.70.refs_1_.refs_0_, bf16[512,384]{1,0:T(8,128)(2,1)S(1)} %get-tuple-element.20.refs_2_, bf16[512,384]{1,0:T(8,128)(2,1)S(1)} %collective-permute-done.10.refs_3_, ...), custom_call_target="tpu_custom_call" | custom-call | tf_op jit(solution)/shard_map/pallas_call | solution.py:28
  25.9 1.4 %collective-permute-done.11.refs_1_ = f32[384,128]{1,0:T(8,128)S(1)} collective-permute-done((f32[384,128]{1,0:T(8,128)S(1)}, f32[384,128]{1,0:T(8,128)S(1)}, u32[]{:S(2)}, u32[]{:S(2)}) %collective-permute-start.11) | collective-permute-done | bytes 196640 | tf_op jit(solution)/shard_map/ppermute | solution.py:228
  27.4 1.6 %collective-permute-start.12 = (f32[192,128]{1,0:T(8,128)S(1)}, f32[192,128]{1,0:T(8,128)S(1)}, u32[]{:S(2)}, u32[]{:S(2)}) collective-permute-start(f32[192,128]{1,0:T(8,128)S(1)} %get-tuple-element.25), channel_id=1, source_target_pairs={{0,16},{1,17},{2,18},{3,19},{4,20},{5,21},{6,22},{7,23},{8,24},{9,... | collective-permute-start | bytes 294920 | tf_op jit(solution)/shard_map/ppermute | solution.py:228
  29.0 3.3 %collective-permute-done.12.refs_1_ = f32[192,128]{1,0:T(8,128)S(1)} collective-permute-done((f32[192,128]{1,0:T(8,128)S(1)}, f32[192,128]{1,0:T(8,128)S(1)}, u32[]{:S(2)}, u32[]{:S(2)}) %collective-permute-start.12) | collective-permute-done | bytes 98336 | tf_op jit(solution)/shard_map/ppermute | solution.py:228
  32.3 3.2 %collective-permute-start.15 = (f32[192,128]{1,0:T(8,128)S(1)}, f32[192,128]{1,0:T(8,128)S(1)}, u32[]{:S(2)}, u32[]{:S(2)}) collective-permute-start(f32[192,128]{1,0:T(8,128)S(1)} %shard_map.73.refs_2_.refs_0_), channel_id=1, source_target_pairs={{0,2},{1,3},{2,0},{3,1},{4,6},{5,7},{6,4},{7,5},{8,10},{9,11},{10,... | collective-permute-start | bytes 294920 | tf_op jit(solution)/shard_map/ppermute | solution.py:228
  35.7 0.7 %collective-permute-start.13 = (bf16[128,384]{1,0:T(8,128)(2,1)S(1)}, bf16[128,384]{1,0:T(8,128)(2,1)S(1)}, u32[]{:S(2)}, u32[]{:S(2)}) collective-permute-start(bf16[128,384]{1,0:T(8,128)(2,1)S(1)} %get-tuple-element.26), channel_id=1, source_target_pairs={{0,0},{1,4},{2,8},{3,12},{4,1},{5,5},{6,9},{7,13},{8,2},{9,6},{10,... | collective-permute-start | bytes 294920 | tf_op jit(solution)/shard_map/ppermute | solution.py:282
  36.4 3.9 %collective-permute-start.14 = (bf16[128,384]{1,0:T(8,128)(2,1)S(1)}, bf16[128,384]{1,0:T(8,128)(2,1)S(1)}, u32[]{:S(2)}, u32[]{:S(2)}) collective-permute-start(bf16[128,384]{1,0:T(8,128)(2,1)S(1)} %get-tuple-element.27), channel_id=1, source_target_pairs={{0,2},{1,6},{2,10},{3,14},{4,3},{5,7},{6,11},{7,15},{8,0},{9,4},{1... | collective-permute-start | bytes 294920 | tf_op jit(solution)/shard_map/ppermute | solution.py:282
  40.3 0.8 %collective-permute-start.16 = (f32[192,128]{1,0:T(8,128)S(1)}, f32[192,128]{1,0:T(8,128)S(1)}, u32[]{:S(2)}, u32[]{:S(2)}) collective-permute-start(f32[192,128]{1,0:T(8,128)S(1)} %shard_map.76.refs_0_), channel_id=1, source_target_pairs={{0,1},{1,0},{2,3},{3,2},{4,5},{5,4},{6,7},{7,6},{8,9},{9,8},{10,11... | collective-permute-start | bytes 294920 | tf_op jit(solution)/shard_map/ppermute | solution.py:228
  41.1 2.5 %collective-permute-done.14.refs_2_ = bf16[128,384]{1,0:T(8,128)(2,1)S(1)} collective-permute-done((bf16[128,384]{1,0:T(8,128)(2,1)S(1)}, bf16[128,384]{1,0:T(8,128)(2,1)S(1)}, u32[]{:S(2)}, u32[]{:S(2)}) %collective-permute-start.14) | collective-permute-done | bytes 98336 | tf_op jit(solution)/shard_map/ppermute | solution.py:282
  43.6 1.5 %shard_map.75.refs_2_ = bf16[1,128,2,384]{3,2,1,0:T(2,128)(2,1)} custom-call(s32[2]{0:T(128)S(1)} %bitcast.2, bf16[128,384]{1,0:T(8,128)(2,1)S(1)} %collective-permute-done.13.refs_1_, bf16[128,384]{1,0:T(8,128)(2,1)S(1)} %collective-permute-done.14.refs_2_), custom_call_target="tpu_custom_call" | custom-call | tf_op jit(solution)/shard_map/pallas_call | solution.py:28
  45.1 1.1 %collective-permute-done.16.refs_1_ = f32[192,128]{1,0:T(8,128)S(1)} collective-permute-done((f32[192,128]{1,0:T(8,128)S(1)}, f32[192,128]{1,0:T(8,128)S(1)}, u32[]{:S(2)}, u32[]{:S(2)}) %collective-permute-start.16) | collective-permute-done | bytes 98336 | tf_op jit(solution)/shard_map/ppermute | solution.py:228
  46.2 3.4 %collective-permute-start.19 = (f32[192,128]{1,0:T(8,128)S(1)}, f32[192,128]{1,0:T(8,128)S(1)}, u32[]{:S(2)}, u32[]{:S(2)}) collective-permute-start(f32[192,128]{1,0:T(8,128)S(1)} %shard_map.77.refs_0_), channel_id=1, source_target_pairs={{0,24},{1,25},{2,26},{3,27},{4,28},{5,29},{6,30},{7,31},{8,16},{9,... | collective-permute-start | bytes 294920 | tf_op jit(solution)/shard_map/ppermute | solution.py:228
  50.2 0.8 %collective-permute-start.20 = (f32[192,128]{1,0:T(8,128)S(1)}, f32[192,128]{1,0:T(8,128)S(1)}, u32[]{:S(2)}, u32[]{:S(2)}) collective-permute-start(f32[192,128]{1,0:T(8,128)S(1)} %shard_map.77.refs_0_), channel_id=1, source_target_pairs={{0,4},{1,5},{2,6},{3,7},{4,0},{5,1},{6,2},{7,3},{8,12},{9,13},{10,... | collective-permute-start | bytes 294920 | tf_op jit(solution)/shard_map/ppermute | solution.py:228
  51.0 1.7 %collective-permute-done.19.refs_3_ = f32[192,128]{1,0:T(8,128)S(1)} collective-permute-done((f32[192,128]{1,0:T(8,128)S(1)}, f32[192,128]{1,0:T(8,128)S(1)}, u32[]{:S(2)}, u32[]{:S(2)}) %collective-permute-start.19) | collective-permute-done | bytes 98336 | tf_op jit(solution)/shard_map/ppermute | solution.py:228
  53.2 2.1 %collective-permute-done.18.refs_2_ = f32[192,128]{1,0:T(8,128)S(1)} collective-permute-done((f32[192,128]{1,0:T(8,128)S(1)}, f32[192,128]{1,0:T(8,128)S(1)}, u32[]{:S(2)}, u32[]{:S(2)}) %collective-permute-start.18) | collective-permute-done | bytes 98336 | tf_op jit(solution)/shard_map/ppermute | solution.py:228
  55.8 0.8 %collective-permute-done.22.refs_6_ = f32[192,128]{1,0:T(8,128)S(1)} collective-permute-done((f32[192,128]{1,0:T(8,128)S(1)}, f32[192,128]{1,0:T(8,128)S(1)}, u32[]{:S(2)}, u32[]{:S(2)}) %collective-permute-start.22) | collective-permute-done | bytes 98336 | tf_op jit(solution)/shard_map/ppermute | solution.py:228
  56.8 1.2 %shard_map.78 = f32[2,384,384]{2,1,0:T(8,128)} custom-call(f32[192,128]{1,0:T(8,128)S(1)} %shard_map.77.refs_0_, f32[192,128]{1,0:T(8,128)S(1)} %collective-permute-done.17.refs_1_, f32[192,128]{1,0:T(8,128)S(1)} %collective-permute-done.18.refs_2_, f32[192,128]{1,0:T(8,128)S(1)} %collective-permute-done.19.refs_3_, ...), custom_call_target="tpu_custom_call" | custom-call | tf_op jit(solution)/shard_map/pallas_call | solution.py:28
  (31 shorter events, 2.8 us)
Async XLA Ops:
  2.3 9.2 %collective-permute-start.3 = (bf16[160,384]{1,0:T(8,128)(2,1)S(1)}, bf16[160,384]{1,0:T(8,128)(2,1)S(1)}, u32[]{:S(2)}, u32[]{:S(2)}) collective-permute-start(bf16[160,384]{1,0:T(8,128)(2,1)S(1)} %get-tuple-element.16), channel_id=1, source_target_pairs={{0,8},{1,9},{2,10},{3,11},{4,12},{5,13},{6,14},{7,15},{8,0},{9,1},... | collective-permute-start | bytes 368648 | tf_op jit(solution)/shard_map/ppermute | solution.py:228
  5.3 16.6 %collective-permute-start.7 = (bf16[256,512]{1,0:T(8,128)(2,1)S(1)}, bf16[256,512]{1,0:T(8,128)(2,1)S(1)}, u32[]{:S(2)}, u32[]{:S(2)}) collective-permute-start(bf16[256,512]{1,0:T(8,128)(2,1)S(1)} %get-tuple-element.17.refs_1_), channel_id=1, source_target_pairs={{0,8},{1,9},{2,10},{3,11},{4,12},{5,13},{6,14},{7,15},{8,0},{9,1},... | collective-permute-start | bytes 786440 | tf_op jit(solution)/shard_map/ppermute | solution.py:228
  5.4 16.5 %collective-permute-start.8 = (bf16[256,512]{1,0:T(8,128)(2,1)S(1)}, bf16[256,512]{1,0:T(8,128)(2,1)S(1)}, u32[]{:S(2)}, u32[]{:S(2)}) collective-permute-start(bf16[256,512]{1,0:T(8,128)(2,1)S(1)} %get-tuple-element.18.refs_2_), channel_id=1, source_target_pairs={{0,8},{1,9},{2,10},{3,11},{4,12},{5,13},{6,14},{7,15},{8,0},{9,1},... | collective-permute-start | bytes 786440 | tf_op jit(solution)/shard_map/ppermute | solution.py:228
  7.4 5.8 %collective-permute-start = (bf16[128,384]{1,0:T(8,128)(2,1)S(1)}, bf16[128,384]{1,0:T(8,128)(2,1)S(1)}, u32[]{:S(2)}, u32[]{:S(2)}) collective-permute-start(bf16[128,384]{1,0:T(8,128)(2,1)S(1)} %get-tuple-element.15.refs_0_), channel_id=1, source_target_pairs={{0,2},{1,3},{2,0},{3,1},{4,6},{5,7},{6,4},{7,5},{8,10},{9,11},{10,... | collective-permute-start | bytes 294920 | tf_op jit(solution)/shard_map/ppermute | solution.py:228
  10.0 7.0 %collective-permute-start.1 = (bf16[128,384]{1,0:T(8,128)(2,1)S(1)}, bf16[128,384]{1,0:T(8,128)(2,1)S(1)}, u32[]{:S(2)}, u32[]{:S(2)}) collective-permute-start(bf16[128,384]{1,0:T(8,128)(2,1)S(1)} %get-tuple-element.15.refs_0_), channel_id=1, source_target_pairs={{0,1},{1,0},{2,3},{3,2},{4,5},{5,4},{6,7},{7,6},{8,9},{9,8},{10,11... | collective-permute-start | bytes 294920 | tf_op jit(solution)/shard_map/ppermute | solution.py:228
  11.6 6.8 %collective-permute-start.4 = (bf16[128,384]{1,0:T(8,128)(2,1)S(1)}, bf16[128,384]{1,0:T(8,128)(2,1)S(1)}, u32[]{:S(2)}, u32[]{:S(2)}) collective-permute-start(bf16[128,384]{1,0:T(8,128)(2,1)S(1)} %slice.8.refs_4_), channel_id=1, source_target_pairs={{0,2},{1,3},{2,0},{3,1},{4,6},{5,7},{6,4},{7,5},{8,10},{9,11},{10,... | collective-permute-start | bytes 294920 | tf_op jit(solution)/shard_map/ppermute | solution.py:228
  13.1 7.6 %collective-permute-start.2 = (bf16[128,384]{1,0:T(8,128)(2,1)S(1)}, bf16[128,384]{1,0:T(8,128)(2,1)S(1)}, u32[]{:S(2)}, u32[]{:S(2)}) collective-permute-start(bf16[128,384]{1,0:T(8,128)(2,1)S(1)} %collective-permute-done.refs_1_), channel_id=1, source_target_pairs={{0,1},{1,0},{2,3},{3,2},{4,5},{5,4},{6,7},{7,6},{8,9},{9,8},{10,11... | collective-permute-start | bytes 294920 | tf_op jit(solution)/shard_map/ppermute | solution.py:228
  17.0 5.0 %collective-permute-start.5 = (bf16[128,384]{1,0:T(8,128)(2,1)S(1)}, bf16[128,384]{1,0:T(8,128)(2,1)S(1)}, u32[]{:S(2)}, u32[]{:S(2)}) collective-permute-start(bf16[128,384]{1,0:T(8,128)(2,1)S(1)} %slice.8.refs_4_), channel_id=1, source_target_pairs={{0,1},{1,0},{2,3},{3,2},{4,5},{5,4},{6,7},{7,6},{8,9},{9,8},{10,11... | collective-permute-start | bytes 294920 | tf_op jit(solution)/shard_map/ppermute | solution.py:228
  18.3 4.7 %collective-permute-start.6 = (bf16[128,384]{1,0:T(8,128)(2,1)S(1)}, bf16[128,384]{1,0:T(8,128)(2,1)S(1)}, u32[]{:S(2)}, u32[]{:S(2)}) collective-permute-start(bf16[128,384]{1,0:T(8,128)(2,1)S(1)} %collective-permute-done.4.refs_5_), channel_id=1, source_target_pairs={{0,1},{1,0},{2,3},{3,2},{4,5},{5,4},{6,7},{7,6},{8,9},{9,8},{10,11... | collective-permute-start | bytes 294920 | tf_op jit(solution)/shard_map/ppermute | solution.py:228
  23.1 2.0 %collective-permute-start.10 = (bf16[512,384]{1,0:T(8,128)(2,1)S(1)}, bf16[512,384]{1,0:T(8,128)(2,1)S(1)}, u32[]{:S(2)}, u32[]{:S(2)}) collective-permute-start(bf16[512,384]{1,0:T(8,128)(2,1)S(1)} %get-tuple-element.20.refs_2_), channel_id=1, source_target_pairs={{0,4},{1,5},{2,6},{3,7},{4,0},{5,1},{6,2},{7,3},{8,12},{9,13},{10,... | collective-permute-start | bytes 1179656 | tf_op jit(solution)/shard_map/ppermute | solution.py:228
  23.9 11.6 %collective-permute-start.9 = (f32[512,384]{1,0:T(8,128)S(1)}, f32[512,384]{1,0:T(8,128)S(1)}, u32[]{:S(2)}, u32[]{:S(2)}) collective-permute-start(f32[512,384]{1,0:T(8,128)S(1)} %shard_map.70.refs_1_.refs_0_), channel_id=1, source_target_pairs={{0,4},{1,5},{2,6},{3,7},{4,0},{5,1},{6,2},{7,3},{8,12},{9,13},{10,... | collective-permute-start | bytes 2359304 | tf_op jit(solution)/shard_map/ppermute | solution.py:228
  25.8 1.5 %collective-permute-start.11 = (f32[384,128]{1,0:T(8,128)S(1)}, f32[384,128]{1,0:T(8,128)S(1)}, u32[]{:S(2)}, u32[]{:S(2)}) collective-permute-start(f32[384,128]{1,0:T(8,128)S(1)} %get-tuple-element.23), channel_id=1, source_target_pairs={{0,4},{1,5},{2,6},{3,7},{4,0},{5,1},{6,2},{7,3},{8,12},{9,13},{10,... | collective-permute-start | bytes 589832 | tf_op jit(solution)/shard_map/ppermute | solution.py:228
  27.4 16.3 %copy-start = (s32[2,1]{0,1:T(1,128)S(1)}, s32[2,1]{0,1:T(1,128)}, u32[]{:S(2)}) copy-start(s32[2,1]{0,1:T(1,128)} %param.7) | copy-start | bytes 28
  27.4 4.9 %collective-permute-start.12 = (f32[192,128]{1,0:T(8,128)S(1)}, f32[192,128]{1,0:T(8,128)S(1)}, u32[]{:S(2)}, u32[]{:S(2)}) collective-permute-start(f32[192,128]{1,0:T(8,128)S(1)} %get-tuple-element.25), channel_id=1, source_target_pairs={{0,16},{1,17},{2,18},{3,19},{4,20},{5,21},{6,22},{7,23},{8,24},{9,... | collective-permute-start | bytes 294920 | tf_op jit(solution)/shard_map/ppermute | solution.py:228
  32.3 8.0 %collective-permute-start.15 = (f32[192,128]{1,0:T(8,128)S(1)}, f32[192,128]{1,0:T(8,128)S(1)}, u32[]{:S(2)}, u32[]{:S(2)}) collective-permute-start(f32[192,128]{1,0:T(8,128)S(1)} %shard_map.73.refs_2_.refs_0_), channel_id=1, source_target_pairs={{0,2},{1,3},{2,0},{3,1},{4,6},{5,7},{6,4},{7,5},{8,10},{9,11},{10,... | collective-permute-start | bytes 294920 | tf_op jit(solution)/shard_map/ppermute | solution.py:228
  35.7 5.4 %collective-permute-start.13 = (bf16[128,384]{1,0:T(8,128)(2,1)S(1)}, bf16[128,384]{1,0:T(8,128)(2,1)S(1)}, u32[]{:S(2)}, u32[]{:S(2)}) collective-permute-start(bf16[128,384]{1,0:T(8,128)(2,1)S(1)} %get-tuple-element.26), channel_id=1, source_target_pairs={{0,0},{1,4},{2,8},{3,12},{4,1},{5,5},{6,9},{7,13},{8,2},{9,6},{10,... | collective-permute-start | bytes 294920 | tf_op jit(solution)/shard_map/ppermute | solution.py:282
  36.4 7.3 %collective-permute-start.14 = (bf16[128,384]{1,0:T(8,128)(2,1)S(1)}, bf16[128,384]{1,0:T(8,128)(2,1)S(1)}, u32[]{:S(2)}, u32[]{:S(2)}) collective-permute-start(bf16[128,384]{1,0:T(8,128)(2,1)S(1)} %get-tuple-element.27), channel_id=1, source_target_pairs={{0,2},{1,6},{2,10},{3,14},{4,3},{5,7},{6,11},{7,15},{8,0},{9,4},{1... | collective-permute-start | bytes 294920 | tf_op jit(solution)/shard_map/ppermute | solution.py:282
  40.3 5.9 %collective-permute-start.16 = (f32[192,128]{1,0:T(8,128)S(1)}, f32[192,128]{1,0:T(8,128)S(1)}, u32[]{:S(2)}, u32[]{:S(2)}) collective-permute-start(f32[192,128]{1,0:T(8,128)S(1)} %shard_map.76.refs_0_), channel_id=1, source_target_pairs={{0,1},{1,0},{2,3},{3,2},{4,5},{5,4},{6,7},{7,6},{8,9},{9,8},{10,11... | collective-permute-start | bytes 294920 | tf_op jit(solution)/shard_map/ppermute | solution.py:228
  46.2 6.5 %collective-permute-start.19 = (f32[192,128]{1,0:T(8,128)S(1)}, f32[192,128]{1,0:T(8,128)S(1)}, u32[]{:S(2)}, u32[]{:S(2)}) collective-permute-start(f32[192,128]{1,0:T(8,128)S(1)} %shard_map.77.refs_0_), channel_id=1, source_target_pairs={{0,24},{1,25},{2,26},{3,27},{4,28},{5,29},{6,30},{7,31},{8,16},{9,... | collective-permute-start | bytes 294920 | tf_op jit(solution)/shard_map/ppermute | solution.py:228
  49.6 5.7 %collective-permute-start.18 = (f32[192,128]{1,0:T(8,128)S(1)}, f32[192,128]{1,0:T(8,128)S(1)}, u32[]{:S(2)}, u32[]{:S(2)}) collective-permute-start(f32[192,128]{1,0:T(8,128)S(1)} %shard_map.77.refs_0_), channel_id=1, source_target_pairs={{0,16},{1,17},{2,18},{3,19},{4,20},{5,21},{6,22},{7,23},{8,24},{9,... | collective-permute-start | bytes 294920 | tf_op jit(solution)/shard_map/ppermute | solution.py:228
  50.1 5.2 %collective-permute-start.17 = (f32[192,128]{1,0:T(8,128)S(1)}, f32[192,128]{1,0:T(8,128)S(1)}, u32[]{:S(2)}, u32[]{:S(2)}) collective-permute-start(f32[192,128]{1,0:T(8,128)S(1)} %shard_map.77.refs_0_), channel_id=1, source_target_pairs={{0,8},{1,9},{2,10},{3,11},{4,12},{5,13},{6,14},{7,15},{8,0},{9,1},... | collective-permute-start | bytes 294920 | tf_op jit(solution)/shard_map/ppermute | solution.py:228
  50.2 5.6 %collective-permute-start.20 = (f32[192,128]{1,0:T(8,128)S(1)}, f32[192,128]{1,0:T(8,128)S(1)}, u32[]{:S(2)}, u32[]{:S(2)}) collective-permute-start(f32[192,128]{1,0:T(8,128)S(1)} %shard_map.77.refs_0_), channel_id=1, source_target_pairs={{0,4},{1,5},{2,6},{3,7},{4,0},{5,1},{6,2},{7,3},{8,12},{9,13},{10,... | collective-permute-start | bytes 294920 | tf_op jit(solution)/shard_map/ppermute | solution.py:228
  52.7 3.1 %collective-permute-start.23 = (f32[192,128]{1,0:T(8,128)S(1)}, f32[192,128]{1,0:T(8,128)S(1)}, u32[]{:S(2)}, u32[]{:S(2)}) collective-permute-start(f32[192,128]{1,0:T(8,128)S(1)} %collective-permute-done.19.refs_3_), channel_id=1, source_target_pairs={{0,4},{1,5},{2,6},{3,7},{4,0},{5,1},{6,2},{7,3},{8,12},{9,13},{10,... | collective-permute-start | bytes 294920 | tf_op jit(solution)/shard_map/ppermute | solution.py:228
  55.3 1.3 %collective-permute-start.22 = (f32[192,128]{1,0:T(8,128)S(1)}, f32[192,128]{1,0:T(8,128)S(1)}, u32[]{:S(2)}, u32[]{:S(2)}) collective-permute-start(f32[192,128]{1,0:T(8,128)S(1)} %collective-permute-done.18.refs_2_), channel_id=1, source_target_pairs={{0,4},{1,5},{2,6},{3,7},{4,0},{5,1},{6,2},{7,3},{8,12},{9,13},{10,... | collective-permute-start | bytes 294920 | tf_op jit(solution)/shard_map/ppermute | solution.py:228
  55.3 1.5 %collective-permute-start.21 = (f32[192,128]{1,0:T(8,128)S(1)}, f32[192,128]{1,0:T(8,128)S(1)}, u32[]{:S(2)}, u32[]{:S(2)}) collective-permute-start(f32[192,128]{1,0:T(8,128)S(1)} %collective-permute-done.17.refs_1_), channel_id=1, source_target_pairs={{0,4},{1,5},{2,6},{3,7},{4,0},{5,1},{6,2},{7,3},{8,12},{9,13},{10,... | collective-permute-start | bytes 294920 | tf_op jit(solution)/shard_map/ppermute | solution.py:228

commit v11 on v10

--- a/solution.py
+++ b/solution.py
@@ -16,7 +16,7 @@
 AXES = ("hyp", "side", "core", "pcol")
 
 
-def call(kernel, outs, specs, *operands, scratch=(), out_specs=None, after=()):
+def call(kernel, outs, specs, *operands, scratch=(), out_specs=None, after=(), alias={}):
     many = isinstance(outs, (list, tuple))
     count = len(specs)
 
@@ -31,6 +31,7 @@
         in_specs=list(specs) + [ANY] * len(after),
         out_specs=out_specs,
         scratch_shapes=scratch,
+        input_output_aliases=alias,
         compiler_params=pltpu.CompilerParams(vmem_limit_bytes=32 * 2**20),
     )(*operands, *after)
 
@@ -41,18 +42,39 @@
     )
 
 
-def tiles(width):
-    count = width // LANES
-    return [(a, b) for a in range(count) for b in range(a, count)]
-
-
-def general(sigma_rows, panel, live_block_rows, inv_diag, quad_weight):
+BLOCKS = 3
+ABOVE = ((0, 1), (0, 2), (1, 2))
+HELD = len(ABOVE) + 2
+
+
+def block_indices():
+    shape = (LANES, LANES)
+    return lax.broadcasted_iota(jnp.int32, shape, 0), lax.broadcasted_iota(jnp.int32, shape, 1)
+
+
+def hold_diagonal(first, second, third):
+    row, column = block_indices()
+    line = jnp.sum(jnp.where(row == column, second, 0.0), axis=0, keepdims=True)
+    last = line[:, LANES - 1 :]
+    below = jnp.where(row == LANES - 1, line, jnp.where((row == LANES - 2) & (column == 0), last, 0.0))
+    upper = column >= row
+    return jnp.where(upper, first, second), jnp.where(upper, third, below)
+
+
+def restore_diagonal(shared, single):
+    row, column = block_indices()
+    turned, upper = shared.T, column >= row
+    line = jnp.where(column[:1] == LANES - 1, single[LANES - 2 : LANES - 1, :1], single[LANES - 1 :, :])
+    second = jnp.where(row == column, line, jnp.where(upper, turned, shared))
+    return jnp.where(upper, shared, turned), second, jnp.where(upper, single, single.T)
+
+
+def general(prow, sigma_rows, panel, live_block_rows, inv_diag, quad_weight):
     height, count, width = panel.shape[1:]
     offsets = lax.broadcasted_iota(jnp.int32, (height, count), 0)
     active = offsets < live_block_rows[:, 0][None, :]
     masked = jnp.where(active[:, :, None], panel[0], jnp.zeros_like(panel[0]))
-    extent = height * lax.axis_size("prow")
-    gathered = lax.all_gather(masked, ("prow", "pcol"), axis=0, tiled=True)
+    gathered = lax.all_gather(masked, prow + ("pcol",), axis=0, tiled=True)
     start = lax.axis_index("pcol") * sigma_rows.shape[2]
     column_panel = lax.dynamic_slice_in_dim(gathered, start, sigma_rows.shape[2], 0)
     applied = lax.psum_scatter(
@@ -76,7 +98,7 @@
     diagonal = jnp.einsum(
         "skp,skq->spq", inv_diag[0], inv_diag[0], preferred_element_type=jnp.float32
     )
-    marginal = lax.psum(quad_weight[0] * (coupling + diagonal), ("hyp", "prow", "pcol"))
+    marginal = lax.psum(quad_weight[0] * (coupling + diagonal), ("hyp",) + prow + ("pcol",))
     return sigma_panel, marginal
 
 
@@ -132,24 +154,31 @@
         at += own.shape[0]
 
 
+def hold_kernel(value, out):
+    del value, out
+
+
 def couple_kernel(weight, applied, pack, got_pack, own_inverse, got_inverse, keep, send, packed):
     core, column = lax.axis_index("core"), lax.axis_index("pcol")
     high = applied[...].astype(jnp.bfloat16)
     low = (applied[...] - high.astype(jnp.float32)).astype(jnp.bfloat16)
     rows = jnp.where(column % 2 == core, pack[...], got_pack[...])
-    at = 0
-    for first in range(rows.shape[1] // LANES):
+    blocks = {}
+    for first in range(BLOCKS):
         left, right = slice(first * LANES, (first + 1) * LANES), slice(first * LANES, None)
         total = transposed_dot(rows[:, left], high[:, right])
         total += transposed_dot(rows[:, left], low[:, right])
         for lines in (own_inverse, got_inverse):
             total += transposed_dot(lines[:, left], lines[:, right])
-        for index in range(total.shape[1] // LANES):
-            packed[at : at + LANES, :] = weight[0] * total[:, index * LANES : (index + 1) * LANES]
-            at += LANES
+        for index in range(BLOCKS - first):
+            blocks[first, first + index] = weight[0] * total[:, index * LANES : (index + 1) * LANES]
+    held = [blocks[place] for place in ABOVE]
+    held += hold_diagonal(*(blocks[i, i] for i in range(BLOCKS)))
+    for index, block in enumerate(held):
+        packed[index * LANES : (index + 1) * LANES, :] = block
     size = keep.shape[0]
-    keep[...] = packed[pl.ds(pl.multiple_of(core * size, LANES), size), :]
-    send[...] = packed[pl.ds(pl.multiple_of((1 - core) * size, LANES), size), :]
+    keep[...] = packed[pl.ds(pl.multiple_of(core * size, 8), size), :]
+    send[...] = packed[pl.ds(pl.multiple_of((1 - core) * size, 8), size), :]
 
 
 def halve_kernel(mine, came, keep, send, whole):
@@ -171,21 +200,11 @@
     out[...] = mine[...] + came[...]
 
 
-def rows_kernel(live_hbm, near, far, out, live, sem):
-    copy = pltpu.make_async_copy(live_hbm, live, sem)
-    copy.start()
-    row = lax.broadcasted_iota(jnp.int32, near.shape, 0)
-    first = lax.axis_index("pcol") // 2 == 0
-    pair = (jnp.where(first, near[...], far[...]), jnp.where(first, far[...], near[...]))
-    copy.wait()
-    for s, value in enumerate(pair):
-        out[0, :, s, :] = jnp.where(row < live[s], value, jnp.zeros(value.shape, value.dtype))
-
-
-def spread_kernel(*refs):
-    parts, (out, lines, result, sems) = refs[:8], refs[8:]
+def finish_kernel(*refs):
+    parts, (live_hbm, near, far, rows_out, out, live, block, lines, result, sems) = refs[:8], refs[8:]
     point, side, core = (lax.axis_index(name) for name in ("hyp", "side", "core"))
-    blocks = tiles(result.shape[1])
+    load = pltpu.make_async_copy(live_hbm, live, sems.at[0])
+    load.start()
     size = parts[0].shape[0]
     for index, part in enumerate(parts):
         owner = core if index < 4 else 1 - core
@@ -195,19 +214,23 @@
         lines[node, pl.ds(start, size), :] = part[...]
     copies = []
     for node in range(2):
-        for first in range(result.shape[1] // LANES):
-            rows = slice(first * LANES, (first + 1) * LANES)
-            for index, (a, b) in enumerate(blocks):
-                if a != first:
-                    continue
-                columns = slice(b * LANES, (b + 1) * LANES)
-                tile = lines[node, index * LANES : (index + 1) * LANES, :]
-                result[node, rows, columns] = tile
-                if a != b:
-                    result[node, columns, rows] = tile.T
-            place = (node, rows)
-            copies.append(pltpu.make_async_copy(result.at[place], out.at[place], sems.at[len(copies)]))
-            copies[-1].start()
+        held = [lines[node, index * LANES : (index + 1) * LANES, :] for index in range(HELD)]
+        places = [slice(index * LANES, (index + 1) * LANES) for index in range(BLOCKS)]
+        for (a, b), tile in zip(ABOVE, held):
+            result[node, places[a], places[b]] = tile
+            result[node, places[b], places[a]] = tile.T
+        for place, tile in zip(places, restore_diagonal(*held[len(ABOVE) :])):
+            result[node, place, place] = tile
+        copies.append(pltpu.make_async_copy(result.at[node], out.at[node], sems.at[1 + node]))
+        copies[-1].start()
+    load.wait()
+    row = lax.broadcasted_iota(jnp.int32, near.shape, 0)
+    first = lax.axis_index("pcol") // 2 == 0
+    pair = (jnp.where(first, near[...], far[...]), jnp.where(first, far[...], near[...]))
+    for s, value in enumerate(pair):
+        block[:, s, :] = jnp.where(row < live[s], value, jnp.zeros(value.shape, value.dtype))
+    copies.append(pltpu.make_async_copy(block, rows_out.at[0], sems.at[3]))
+    copies[-1].start()
     for copy in copies:
         copy.wait()
 
@@ -261,8 +284,11 @@
     mine = call(
         apply_kernel, shape((extent, width), f32), [VMEM] * (1 + 2 * len(cuts)), rows, *pieces, *far
     )
-    lines = len(tiles(width)) // 2 * LANES
+    lines = HELD * LANES // 2
     part, half = shape((lines // 2, LANES), f32), shape((lines, LANES), f32)
+    mine = call(
+        hold_kernel, shape(mine.shape, f32), [ANY], mine, out_specs=ANY, after=[got_pack], alias={0: 0}
+    )
     other = swap(mine, core=1)
     keep, send = call(
         couple_kernel, [half, half], [SMEM] + [VMEM] * 5,
@@ -288,25 +314,25 @@
         scratch=[pltpu.VMEM((extent, width), bf16)],
         after=[total],
     )
-    sigma_panel = call(
-        rows_kernel, shape((1, height, count, width), bf16), [HBM, VMEM, VMEM],
-        live, deliver(out_near, 0), deliver(out_far, 1),
-        scratch=[pltpu.SMEM(live.shape, jnp.int32), dma(())],
-    )
+    near, far = deliver(out_near, 0), deliver(out_far, 1)
     total = add(total, swap(total, column=2))
-    total = add(total, swap(total, column=1), after=[stay(sigma_panel)])
+    total = add(total, swap(total, column=1), after=[near, far])
     quarters = [total, swap(total, side=1), swap(total, point=1), swap(total, side=1, point=1)]
     quarters += [swap(x, core=1) for x in quarters]
-    marginal = call(
-        spread_kernel, shape((count, width, width), f32), [VMEM] * 8, *quarters,
+    return call(
+        finish_kernel,
+        [shape((1, height, count, width), bf16), shape((count, width, width), f32)],
+        [VMEM] * 8 + [HBM] + [VMEM] * 2,
+        *quarters, live, near, far,
         scratch=[
+            pltpu.SMEM(live.shape, jnp.int32),
+            pltpu.VMEM((height, count, width), bf16),
             pltpu.VMEM((count, 2 * lines, LANES), f32),
             pltpu.VMEM((count, width, width), f32),
-            dma((6,)),
+            dma((4,)),
         ],
-        out_specs=HBM,
-    )
-    return sigma_panel, marginal
+        out_specs=[HBM, HBM],
+    )
 
 
 def solution(mesh):
@@ -314,7 +340,15 @@
     prow, pcol = ("prow",), ("pcol",)
 
     def on_device(sigma_rows, panel, live_block_rows, inv_diag, quad_weight):
-        body = square if split else general
+        height, count, width = panel.shape[1:]
+        fits = (
+            split
+            and sigma_rows.shape[1] == sigma_rows.shape[2] == sizes["pcol"] * height
+            and height % LANES == 0
+            and count == 2
+            and width == BLOCKS * LANES
+        )
+        body = square if fits else functools.partial(general, prow)
         return body(sigma_rows, panel, live_block_rows, inv_diag, quad_weight)
 
     split = sizes["hyp"] == 2 and sizes["pcol"] == 4 and sizes["prow"] == 4

time: 58.2 us -> 57.6 us (0.990)
  waiting for transfers between devices: 18.1 us -> 20.8 us
  starting transfers between devices: 32.3 us -> 30.2 us
  Pallas kernels: 6.12 us -> 5.02 us
    ppermute x22, waiting for transfers between devices: 15.6 us -> 20.8 us  [swap(): return lax.ppermute(x, AXES, [(i, i ^ mask) for i in range(devices)])]
    ppermute x2, waiting for transfers between devices: 2.54 us -> 0.01 us  [deliver(): return lax.ppermute(x, AXES, pairs)]
    ppermute x22, starting transfers between devices: 27.7 us -> 25.7 us  [swap(): return lax.ppermute(x, AXES, [(i, i ^ mask) for i in range(devices)])]
    pallas_call x11, Pallas kernels: 6.12 us -> 5.02 us  [call(): pl.pallas_call(body, out_shape=outs, in_specs=list(specs) + [ANY] * len(a...]
  transfers between devices with their start and end apart: 24 -> 24, of which waited for: 13 -> 14; matrix products, arithmetic and copies ran while one was open for 0% -> 0% of each run, Pallas kernels for 5% -> 3%
where the time goes in v11:
time: 57.6 us; the launch traced here: 57.4 us
  starting transfers between devices  30.2 us (52%)
  waiting for transfers between devices  20.8 us (36%)
  Pallas kernels  5.02 us (9%)
  between operations  1.38 us (2%)
    ppermute x22, starting transfers between devices, swap(): return lax.ppermute(x, AXES, [(i, i ^ mask) for i in range(devices)])  25.7 us
    ppermute x22, waiting for transfers between devices, swap(): return lax.ppermute(x, AXES, [(i, i ^ mask) for i in range(devices)])  20.8 us
    pallas_call x11, Pallas kernels, call(): pl.pallas_call(body, out_shape=outs, in_specs=list(specs) + [ANY] * len(a...  5.02 us
    ppermute x2, starting transfers between devices, deliver(): return lax.ppermute(x, AXES, pairs)  4.58 us
  transfers between devices with their start and end apart: 24, of which 14 were waited for; matrix products, arithmetic and copies ran while one was open for 0% of the time, Pallas kernels for 3%

profile of v11, /device:TPU:0, one launch (start us, length us, event | category | flops | bytes accessed | tf_op | source)
XLA Modules:
  0.0 57.4 jit_solution(15736106003176317451)
XLA Ops:
  0.6 1.7 %shard_map.68 = (bf16[128,384]{1,0:T(8,128)(2,1)S(1)}, bf16[160,384]{1,0:T(8,128)(2,1)S(1)}, bf16[32,384]{1,0:T(8,128)(2,1)S(1)}, bf16[256,512]{1,0:T(8,128)(2,1)S(1)}, bf16[256,512]{1,0:T(8,128)(2,1)S(1)}) custom-call(s32[2]{0:T(128)} %bitcast.1, bf16[1,128,2,384]{3,2,1,0:T(2,128)(2,1)} %refs_1_.1, bf16[1,2,24,384]{3,2,1,0:T(8,128)(2,1)} %refs_2_.1, ...), custom_call_target="tpu_custom_call" | custom-call | tf_op jit(solution)/shard_map/pallas_call | solution.py:28
  2.3 3.0 %collective-permute-start.3 = (bf16[160,384]{1,0:T(8,128)(2,1)S(1)}, bf16[160,384]{1,0:T(8,128)(2,1)S(1)}, u32[]{:S(2)}, u32[]{:S(2)}) collective-permute-start(bf16[160,384]{1,0:T(8,128)(2,1)S(1)} %get-tuple-element.16), channel_id=1, source_target_pairs={{0,8},{1,9},{2,10},{3,11},{4,12},{5,13},{6,14},{7,15},{8,0},{9,1},... | collective-permute-start | bytes 368648 | tf_op jit(solution)/shard_map/ppermute | solution.py:251
  5.4 1.9 %collective-permute-start.8 = (bf16[256,512]{1,0:T(8,128)(2,1)S(1)}, bf16[256,512]{1,0:T(8,128)(2,1)S(1)}, u32[]{:S(2)}, u32[]{:S(2)}) collective-permute-start(bf16[256,512]{1,0:T(8,128)(2,1)S(1)} %get-tuple-element.18.refs_2_), channel_id=1, source_target_pairs={{0,8},{1,9},{2,10},{3,11},{4,12},{5,13},{6,14},{7,15},{8,0},{9,1},... | collective-permute-start | bytes 786440 | tf_op jit(solution)/shard_map/ppermute | solution.py:251
  7.4 2.6 %collective-permute-start = (bf16[128,384]{1,0:T(8,128)(2,1)S(1)}, bf16[128,384]{1,0:T(8,128)(2,1)S(1)}, u32[]{:S(2)}, u32[]{:S(2)}) collective-permute-start(bf16[128,384]{1,0:T(8,128)(2,1)S(1)} %get-tuple-element.15.refs_0_), channel_id=1, source_target_pairs={{0,2},{1,3},{2,0},{3,1},{4,6},{5,7},{6,4},{7,5},{8,10},{9,11},{10,... | collective-permute-start | bytes 294920 | tf_op jit(solution)/shard_map/ppermute | solution.py:251
  10.0 1.6 %collective-permute-start.1 = (bf16[128,384]{1,0:T(8,128)(2,1)S(1)}, bf16[128,384]{1,0:T(8,128)(2,1)S(1)}, u32[]{:S(2)}, u32[]{:S(2)}) collective-permute-start(bf16[128,384]{1,0:T(8,128)(2,1)S(1)} %get-tuple-element.15.refs_0_), channel_id=1, source_target_pairs={{0,1},{1,0},{2,3},{3,2},{4,5},{5,4},{6,7},{7,6},{8,9},{9,8},{10,11... | collective-permute-start | bytes 294920 | tf_op jit(solution)/shard_map/ppermute | solution.py:251
  11.6 1.2 %collective-permute-start.4 = (bf16[128,384]{1,0:T(8,128)(2,1)S(1)}, bf16[128,384]{1,0:T(8,128)(2,1)S(1)}, u32[]{:S(2)}, u32[]{:S(2)}) collective-permute-start(bf16[128,384]{1,0:T(8,128)(2,1)S(1)} %slice.8.refs_4_), channel_id=1, source_target_pairs={{0,2},{1,3},{2,0},{3,1},{4,6},{5,7},{6,4},{7,5},{8,10},{9,11},{10,... | collective-permute-start | bytes 294920 | tf_op jit(solution)/shard_map/ppermute | solution.py:251
  13.1 3.8 %collective-permute-start.2 = (bf16[128,384]{1,0:T(8,128)(2,1)S(1)}, bf16[128,384]{1,0:T(8,128)(2,1)S(1)}, u32[]{:S(2)}, u32[]{:S(2)}) collective-permute-start(bf16[128,384]{1,0:T(8,128)(2,1)S(1)} %collective-permute-done.refs_1_), channel_id=1, source_target_pairs={{0,1},{1,0},{2,3},{3,2},{4,5},{5,4},{6,7},{7,6},{8,9},{9,8},{10,11... | collective-permute-start | bytes 294920 | tf_op jit(solution)/shard_map/ppermute | solution.py:251
  17.0 0.7 %collective-permute-start.5 = (bf16[128,384]{1,0:T(8,128)(2,1)S(1)}, bf16[128,384]{1,0:T(8,128)(2,1)S(1)}, u32[]{:S(2)}, u32[]{:S(2)}) collective-permute-start(bf16[128,384]{1,0:T(8,128)(2,1)S(1)} %slice.8.refs_4_), channel_id=1, source_target_pairs={{0,1},{1,0},{2,3},{3,2},{4,5},{5,4},{6,7},{7,6},{8,9},{9,8},{10,11... | collective-permute-start | bytes 294920 | tf_op jit(solution)/shard_map/ppermute | solution.py:251
  17.7 0.6 %collective-permute-done.4.refs_5_ = bf16[128,384]{1,0:T(8,128)(2,1)S(1)} collective-permute-done((bf16[128,384]{1,0:T(8,128)(2,1)S(1)}, bf16[128,384]{1,0:T(8,128)(2,1)S(1)}, u32[]{:S(2)}, u32[]{:S(2)}) %collective-permute-start.4) | collective-permute-done | bytes 98336 | tf_op jit(solution)/shard_map/ppermute | solution.py:251
  18.3 0.7 %collective-permute-start.6 = (bf16[128,384]{1,0:T(8,128)(2,1)S(1)}, bf16[128,384]{1,0:T(8,128)(2,1)S(1)}, u32[]{:S(2)}, u32[]{:S(2)}) collective-permute-start(bf16[128,384]{1,0:T(8,128)(2,1)S(1)} %collective-permute-done.4.refs_5_), channel_id=1, source_target_pairs={{0,1},{1,0},{2,3},{3,2},{4,5},{5,4},{6,7},{7,6},{8,9},{9,8},{10,11... | collective-permute-start | bytes 294920 | tf_op jit(solution)/shard_map/ppermute | solution.py:251
  19.0 1.6 %collective-permute-done.2.refs_3_ = bf16[128,384]{1,0:T(8,128)(2,1)S(1)} collective-permute-done((bf16[128,384]{1,0:T(8,128)(2,1)S(1)}, bf16[128,384]{1,0:T(8,128)(2,1)S(1)}, u32[]{:S(2)}, u32[]{:S(2)}) %collective-permute-start.2) | collective-permute-done | bytes 98336 | tf_op jit(solution)/shard_map/ppermute | solution.py:251
  20.7 1.3 %collective-permute-done.5.refs_6_ = bf16[128,384]{1,0:T(8,128)(2,1)S(1)} collective-permute-done((bf16[128,384]{1,0:T(8,128)(2,1)S(1)}, bf16[128,384]{1,0:T(8,128)(2,1)S(1)}, u32[]{:S(2)}, u32[]{:S(2)}) %collective-permute-start.5) | collective-permute-done | bytes 98336 | tf_op jit(solution)/shard_map/ppermute | solution.py:251
  22.0 1.0 %collective-permute-done.6.refs_7_ = bf16[128,384]{1,0:T(8,128)(2,1)S(1)} collective-permute-done((bf16[128,384]{1,0:T(8,128)(2,1)S(1)}, bf16[128,384]{1,0:T(8,128)(2,1)S(1)}, u32[]{:S(2)}, u32[]{:S(2)}) %collective-permute-start.6) | collective-permute-done | bytes 98336 | tf_op jit(solution)/shard_map/ppermute | solution.py:251
  23.2 0.7 %shard_map.70.refs_0_ = f32[512,384]{1,0:T(8,128)S(1)} custom-call(bf16[2,512,384]{2,1,0:T(8,128)(2,1)S(1)} %get-tuple-element.19.refs_0_, bf16[256,512]{1,0:T(8,128)(2,1)S(1)} %get-tuple-element.17.refs_1_, bf16[256,512]{1,0:T(8,128)(2,1)S(1)} %get-tuple-element.18.refs_2_, bf16[256,512]{1,0:T(8,128)(2,1)S(1)} %collective-permute-done.7.refs_8_.refs_3_, ...), custom_call_target="tpu_custom_call" | custom-call | tf_op jit(solution)/shard_map/pallas_call | solution.py:28
  23.9 1.0 %collective-permute-done.9.refs_1_.refs_3_ = bf16[512,384]{1,0:T(8,128)(2,1)S(1)} collective-permute-done((bf16[512,384]{1,0:T(8,128)(2,1)S(1)}, bf16[512,384]{1,0:T(8,128)(2,1)S(1)}, u32[]{:S(2)}, u32[]{:S(2)}) %collective-permute-start.9) | collective-permute-done | bytes 393248 | tf_op jit(solution)/shard_map/ppermute | solution.py:251
  25.7 0.7 %shard_map.72 = (f32[320,128]{1,0:T(8,128)S(1)}, f32[320,128]{1,0:T(8,128)S(1)}) custom-call(f32[1]{0:T(128)S(6)} %copy.9.refs_0_, f32[512,384]{1,0:T(8,128)S(1)} %shard_map.71.refs_1_.refs_0_, bf16[512,384]{1,0:T(8,128)(2,1)S(1)} %get-tuple-element.20.refs_2_, bf16[512,384]{1,0:T(8,128)(2,1)S(1)} %collective-permute-done.9.refs_1_.refs_3_, ...), custom_call_target="tpu_custom_call" | custom-call | tf_op jit(solution)/shard_map/pallas_call | solution.py:28
  26.8 1.0 %collective-permute-done.10.refs_1_ = f32[320,128]{1,0:T(8,128)S(1)} collective-permute-done((f32[320,128]{1,0:T(8,128)S(1)}, f32[320,128]{1,0:T(8,128)S(1)}, u32[]{:S(2)}, u32[]{:S(2)}) %collective-permute-start.10) | collective-permute-done | bytes 163872 | tf_op jit(solution)/shard_map/ppermute | solution.py:251
  27.9 1.6 %collective-permute-start.11 = (f32[160,128]{1,0:T(8,128)S(1)}, f32[160,128]{1,0:T(8,128)S(1)}, u32[]{:S(2)}, u32[]{:S(2)}) collective-permute-start(f32[160,128]{1,0:T(8,128)S(1)} %get-tuple-element.25), channel_id=1, source_target_pairs={{0,16},{1,17},{2,18},{3,19},{4,20},{5,21},{6,22},{7,23},{8,24},{9,... | collective-permute-start | bytes 245768 | tf_op jit(solution)/shard_map/ppermute | solution.py:251
  29.5 3.2 %collective-permute-done.11.refs_1_ = f32[160,128]{1,0:T(8,128)S(1)} collective-permute-done((f32[160,128]{1,0:T(8,128)S(1)}, f32[160,128]{1,0:T(8,128)S(1)}, u32[]{:S(2)}, u32[]{:S(2)}) %collective-permute-start.11) | collective-permute-done | bytes 81952 | tf_op jit(solution)/shard_map/ppermute | solution.py:251
  32.7 3.2 %collective-permute-start.12 = (f32[160,128]{1,0:T(8,128)S(1)}, f32[160,128]{1,0:T(8,128)S(1)}, u32[]{:S(2)}, u32[]{:S(2)}) collective-permute-start(f32[160,128]{1,0:T(8,128)S(1)} %shard_map.74.refs_0_.refs_2_), channel_id=1, source_target_pairs={{0,2},{1,3},{2,0},{3,1},{4,6},{5,7},{6,4},{7,5},{8,10},{9,11},{10,... | collective-permute-start | bytes 245768 | tf_op jit(solution)/shard_map/ppermute | solution.py:251
  36.1 0.7 %collective-permute-start.15 = (bf16[128,384]{1,0:T(8,128)(2,1)S(1)}, bf16[128,384]{1,0:T(8,128)(2,1)S(1)}, u32[]{:S(2)}, u32[]{:S(2)}) collective-permute-start(bf16[128,384]{1,0:T(8,128)(2,1)S(1)} %get-tuple-element.26), channel_id=1, source_target_pairs={{0,0},{1,4},{2,8},{3,12},{4,1},{5,5},{6,9},{7,13},{8,2},{9,6},{10,... | collective-permute-start | bytes 294920 | tf_op jit(solution)/shard_map/ppermute | solution.py:308
  36.8 3.9 %collective-permute-start.16 = (bf16[128,384]{1,0:T(8,128)(2,1)S(1)}, bf16[128,384]{1,0:T(8,128)(2,1)S(1)}, u32[]{:S(2)}, u32[]{:S(2)}) collective-permute-start(bf16[128,384]{1,0:T(8,128)(2,1)S(1)} %get-tuple-element.27), channel_id=1, source_target_pairs={{0,2},{1,6},{2,10},{3,14},{4,3},{5,7},{6,11},{7,15},{8,0},{9,4},{1... | collective-permute-start | bytes 294920 | tf_op jit(solution)/shard_map/ppermute | solution.py:308
  40.7 0.8 %collective-permute-start.13 = (f32[160,128]{1,0:T(8,128)S(1)}, f32[160,128]{1,0:T(8,128)S(1)}, u32[]{:S(2)}, u32[]{:S(2)}) collective-permute-start(f32[160,128]{1,0:T(8,128)S(1)} %shard_map.75.refs_0_), channel_id=1, source_target_pairs={{0,1},{1,0},{2,3},{3,2},{4,5},{5,4},{6,7},{7,6},{8,9},{9,8},{10,11... | collective-permute-start | bytes 245768 | tf_op jit(solution)/shard_map/ppermute | solution.py:251
  41.5 5.0 %collective-permute-done.13.refs_1_ = f32[160,128]{1,0:T(8,128)S(1)} collective-permute-done((f32[160,128]{1,0:T(8,128)S(1)}, f32[160,128]{1,0:T(8,128)S(1)}, u32[]{:S(2)}, u32[]{:S(2)}) %collective-permute-start.13) | collective-permute-done | bytes 81952 | tf_op jit(solution)/shard_map/ppermute | solution.py:251
  46.5 3.2 %collective-permute-start.19 = (f32[160,128]{1,0:T(8,128)S(1)}, f32[160,128]{1,0:T(8,128)S(1)}, u32[]{:S(2)}, u32[]{:S(2)}) collective-permute-start(f32[160,128]{1,0:T(8,128)S(1)} %shard_map.77.refs_0_), channel_id=1, source_target_pairs={{0,24},{1,25},{2,26},{3,27},{4,28},{5,29},{6,30},{7,31},{8,16},{9,... | collective-permute-start | bytes 245768 | tf_op jit(solution)/shard_map/ppermute | solution.py:251
  49.6 0.5 collective-permute-start.18
  50.3 2.6 %collective-permute-done.19.refs_3_ = f32[160,128]{1,0:T(8,128)S(1)} collective-permute-done((f32[160,128]{1,0:T(8,128)S(1)}, f32[160,128]{1,0:T(8,128)S(1)}, u32[]{:S(2)}, u32[]{:S(2)}) %collective-permute-start.19) | collective-permute-done | bytes 81952 | tf_op jit(solution)/shard_map/ppermute | solution.py:251
  52.9 1.2 %collective-permute-done.18.refs_2_ = f32[160,128]{1,0:T(8,128)S(1)} collective-permute-done((f32[160,128]{1,0:T(8,128)S(1)}, f32[160,128]{1,0:T(8,128)S(1)}, u32[]{:S(2)}, u32[]{:S(2)}) %collective-permute-start.18) | collective-permute-done | bytes 81952 | tf_op jit(solution)/shard_map/ppermute | solution.py:251
  54.1 0.5 collective-permute-done.17.refs_1_
  54.6 0.8 %collective-permute-done.22.refs_6_ = f32[160,128]{1,0:T(8,128)S(1)} collective-permute-done((f32[160,128]{1,0:T(8,128)S(1)}, f32[160,128]{1,0:T(8,128)S(1)}, u32[]{:S(2)}, u32[]{:S(2)}) %collective-permute-start.22) | collective-permute-done | bytes 81952 | tf_op jit(solution)/shard_map/ppermute | solution.py:251
  55.4 0.5 collective-permute-done.21.refs_5_
  55.9 1.5 %shard_map.78 = (bf16[1,128,2,384]{3,2,1,0:T(2,128)(2,1)}, f32[2,384,384]{2,1,0:T(8,128)}) custom-call(f32[160,128]{1,0:T(8,128)S(1)} %shard_map.77.refs_0_, f32[160,128]{1,0:T(8,128)S(1)} %collective-permute-done.17.refs_1_, f32[160,128]{1,0:T(8,128)S(1)} %collective-permute-done.18.refs_2_, f32[160,128]{1,0:T(8,128)S(1)} %collective-permute-done.19.refs_3_, ...), custom_call_target="tpu_custom_call" | custom-call | tf_op jit(solution)/shard_map/pallas_call | solution.py:28
  (31 shorter events, 1.6 us)
Async XLA Ops:
  2.3 9.2 %collective-permute-start.3 = (bf16[160,384]{1,0:T(8,128)(2,1)S(1)}, bf16[160,384]{1,0:T(8,128)(2,1)S(1)}, u32[]{:S(2)}, u32[]{:S(2)}) collective-permute-start(bf16[160,384]{1,0:T(8,128)(2,1)S(1)} %get-tuple-element.16), channel_id=1, source_target_pairs={{0,8},{1,9},{2,10},{3,11},{4,12},{5,13},{6,14},{7,15},{8,0},{9,1},... | collective-permute-start | bytes 368648 | tf_op jit(solution)/shard_map/ppermute | solution.py:251
  5.3 16.6 %collective-permute-start.7 = (bf16[256,512]{1,0:T(8,128)(2,1)S(1)}, bf16[256,512]{1,0:T(8,128)(2,1)S(1)}, u32[]{:S(2)}, u32[]{:S(2)}) collective-permute-start(bf16[256,512]{1,0:T(8,128)(2,1)S(1)} %get-tuple-element.17.refs_1_), channel_id=1, source_target_pairs={{0,8},{1,9},{2,10},{3,11},{4,12},{5,13},{6,14},{7,15},{8,0},{9,1},... | collective-permute-start | bytes 786440 | tf_op jit(solution)/shard_map/ppermute | solution.py:251
  5.4 16.5 %collective-permute-start.8 = (bf16[256,512]{1,0:T(8,128)(2,1)S(1)}, bf16[256,512]{1,0:T(8,128)(2,1)S(1)}, u32[]{:S(2)}, u32[]{:S(2)}) collective-permute-start(bf16[256,512]{1,0:T(8,128)(2,1)S(1)} %get-tuple-element.18.refs_2_), channel_id=1, source_target_pairs={{0,8},{1,9},{2,10},{3,11},{4,12},{5,13},{6,14},{7,15},{8,0},{9,1},... | collective-permute-start | bytes 786440 | tf_op jit(solution)/shard_map/ppermute | solution.py:251
  7.4 5.8 %collective-permute-start = (bf16[128,384]{1,0:T(8,128)(2,1)S(1)}, bf16[128,384]{1,0:T(8,128)(2,1)S(1)}, u32[]{:S(2)}, u32[]{:S(2)}) collective-permute-start(bf16[128,384]{1,0:T(8,128)(2,1)S(1)} %get-tuple-element.15.refs_0_), channel_id=1, source_target_pairs={{0,2},{1,3},{2,0},{3,1},{4,6},{5,7},{6,4},{7,5},{8,10},{9,11},{10,... | collective-permute-start | bytes 294920 | tf_op jit(solution)/shard_map/ppermute | solution.py:251
  10.0 7.0 %collective-permute-start.1 = (bf16[128,384]{1,0:T(8,128)(2,1)S(1)}, bf16[128,384]{1,0:T(8,128)(2,1)S(1)}, u32[]{:S(2)}, u32[]{:S(2)}) collective-permute-start(bf16[128,384]{1,0:T(8,128)(2,1)S(1)} %get-tuple-element.15.refs_0_), channel_id=1, source_target_pairs={{0,1},{1,0},{2,3},{3,2},{4,5},{5,4},{6,7},{7,6},{8,9},{9,8},{10,11... | collective-permute-start | bytes 294920 | tf_op jit(solution)/shard_map/ppermute | solution.py:251
  11.6 6.8 %collective-permute-start.4 = (bf16[128,384]{1,0:T(8,128)(2,1)S(1)}, bf16[128,384]{1,0:T(8,128)(2,1)S(1)}, u32[]{:S(2)}, u32[]{:S(2)}) collective-permute-start(bf16[128,384]{1,0:T(8,128)(2,1)S(1)} %slice.8.refs_4_), channel_id=1, source_target_pairs={{0,2},{1,3},{2,0},{3,1},{4,6},{5,7},{6,4},{7,5},{8,10},{9,11},{10,... | collective-permute-start | bytes 294920 | tf_op jit(solution)/shard_map/ppermute | solution.py:251
  13.1 7.6 %collective-permute-start.2 = (bf16[128,384]{1,0:T(8,128)(2,1)S(1)}, bf16[128,384]{1,0:T(8,128)(2,1)S(1)}, u32[]{:S(2)}, u32[]{:S(2)}) collective-permute-start(bf16[128,384]{1,0:T(8,128)(2,1)S(1)} %collective-permute-done.refs_1_), channel_id=1, source_target_pairs={{0,1},{1,0},{2,3},{3,2},{4,5},{5,4},{6,7},{7,6},{8,9},{9,8},{10,11... | collective-permute-start | bytes 294920 | tf_op jit(solution)/shard_map/ppermute | solution.py:251
  17.0 5.0 %collective-permute-start.5 = (bf16[128,384]{1,0:T(8,128)(2,1)S(1)}, bf16[128,384]{1,0:T(8,128)(2,1)S(1)}, u32[]{:S(2)}, u32[]{:S(2)}) collective-permute-start(bf16[128,384]{1,0:T(8,128)(2,1)S(1)} %slice.8.refs_4_), channel_id=1, source_target_pairs={{0,1},{1,0},{2,3},{3,2},{4,5},{5,4},{6,7},{7,6},{8,9},{9,8},{10,11... | collective-permute-start | bytes 294920 | tf_op jit(solution)/shard_map/ppermute | solution.py:251
  18.3 4.7 %collective-permute-start.6 = (bf16[128,384]{1,0:T(8,128)(2,1)S(1)}, bf16[128,384]{1,0:T(8,128)(2,1)S(1)}, u32[]{:S(2)}, u32[]{:S(2)}) collective-permute-start(bf16[128,384]{1,0:T(8,128)(2,1)S(1)} %collective-permute-done.4.refs_5_), channel_id=1, source_target_pairs={{0,1},{1,0},{2,3},{3,2},{4,5},{5,4},{6,7},{7,6},{8,9},{9,8},{10,11... | collective-permute-start | bytes 294920 | tf_op jit(solution)/shard_map/ppermute | solution.py:251
  23.1 1.8 %collective-permute-start.9 = (bf16[512,384]{1,0:T(8,128)(2,1)S(1)}, bf16[512,384]{1,0:T(8,128)(2,1)S(1)}, u32[]{:S(2)}, u32[]{:S(2)}) collective-permute-start(bf16[512,384]{1,0:T(8,128)(2,1)S(1)} %get-tuple-element.20.refs_2_), channel_id=1, source_target_pairs={{0,4},{1,5},{2,6},{3,7},{4,0},{5,1},{6,2},{7,3},{8,12},{9,13},{10,... | collective-permute-start | bytes 1179656 | tf_op jit(solution)/shard_map/ppermute | solution.py:251
  24.9 11.0 %collective-permute-start.14 = (f32[512,384]{1,0:T(8,128)S(1)}, f32[512,384]{1,0:T(8,128)S(1)}, u32[]{:S(2)}, u32[]{:S(2)}) collective-permute-start(f32[512,384]{1,0:T(8,128)S(1)} %shard_map.71.refs_1_.refs_0_), channel_id=1, source_target_pairs={{0,4},{1,5},{2,6},{3,7},{4,0},{5,1},{6,2},{7,3},{8,12},{9,13},{10,... | collective-permute-start | bytes 2359304 | tf_op jit(solution)/shard_map/ppermute | solution.py:251
  26.4 1.4 %collective-permute-start.10 = (f32[320,128]{1,0:T(8,128)S(1)}, f32[320,128]{1,0:T(8,128)S(1)}, u32[]{:S(2)}, u32[]{:S(2)}) collective-permute-start(f32[320,128]{1,0:T(8,128)S(1)} %get-tuple-element.23), channel_id=1, source_target_pairs={{0,4},{1,5},{2,6},{3,7},{4,0},{5,1},{6,2},{7,3},{8,12},{9,13},{10,... | collective-permute-start | bytes 491528 | tf_op jit(solution)/shard_map/ppermute | solution.py:251
  27.9 4.8 %collective-permute-start.11 = (f32[160,128]{1,0:T(8,128)S(1)}, f32[160,128]{1,0:T(8,128)S(1)}, u32[]{:S(2)}, u32[]{:S(2)}) collective-permute-start(f32[160,128]{1,0:T(8,128)S(1)} %get-tuple-element.25), channel_id=1, source_target_pairs={{0,16},{1,17},{2,18},{3,19},{4,20},{5,21},{6,22},{7,23},{8,24},{9,... | collective-permute-start | bytes 245768 | tf_op jit(solution)/shard_map/ppermute | solution.py:251
  32.7 23.2 %copy-start = (s32[2,1]{0,1:T(1,128)S(1)}, s32[2,1]{0,1:T(1,128)}, u32[]{:S(2)}) copy-start(s32[2,1]{0,1:T(1,128)} %param.7) | copy-start | bytes 28
  32.7 8.0 %collective-permute-start.12 = (f32[160,128]{1,0:T(8,128)S(1)}, f32[160,128]{1,0:T(8,128)S(1)}, u32[]{:S(2)}, u32[]{:S(2)}) collective-permute-start(f32[160,128]{1,0:T(8,128)S(1)} %shard_map.74.refs_0_.refs_2_), channel_id=1, source_target_pairs={{0,2},{1,3},{2,0},{3,1},{4,6},{5,7},{6,4},{7,5},{8,10},{9,11},{10,... | collective-permute-start | bytes 245768 | tf_op jit(solution)/shard_map/ppermute | solution.py:251
  36.1 10.4 %collective-permute-start.15 = (bf16[128,384]{1,0:T(8,128)(2,1)S(1)}, bf16[128,384]{1,0:T(8,128)(2,1)S(1)}, u32[]{:S(2)}, u32[]{:S(2)}) collective-permute-start(bf16[128,384]{1,0:T(8,128)(2,1)S(1)} %get-tuple-element.26), channel_id=1, source_target_pairs={{0,0},{1,4},{2,8},{3,12},{4,1},{5,5},{6,9},{7,13},{8,2},{9,6},{10,... | collective-permute-start | bytes 294920 | tf_op jit(solution)/shard_map/ppermute | solution.py:308
  36.8 9.7 %collective-permute-start.16 = (bf16[128,384]{1,0:T(8,128)(2,1)S(1)}, bf16[128,384]{1,0:T(8,128)(2,1)S(1)}, u32[]{:S(2)}, u32[]{:S(2)}) collective-permute-start(bf16[128,384]{1,0:T(8,128)(2,1)S(1)} %get-tuple-element.27), channel_id=1, source_target_pairs={{0,2},{1,6},{2,10},{3,14},{4,3},{5,7},{6,11},{7,15},{8,0},{9,4},{1... | collective-permute-start | bytes 294920 | tf_op jit(solution)/shard_map/ppermute | solution.py:308
  40.7 5.8 %collective-permute-start.13 = (f32[160,128]{1,0:T(8,128)S(1)}, f32[160,128]{1,0:T(8,128)S(1)}, u32[]{:S(2)}, u32[]{:S(2)}) collective-permute-start(f32[160,128]{1,0:T(8,128)S(1)} %shard_map.75.refs_0_), channel_id=1, source_target_pairs={{0,1},{1,0},{2,3},{3,2},{4,5},{5,4},{6,7},{7,6},{8,9},{9,8},{10,11... | collective-permute-start | bytes 245768 | tf_op jit(solution)/shard_map/ppermute | solution.py:251
  46.5 6.4 %collective-permute-start.19 = (f32[160,128]{1,0:T(8,128)S(1)}, f32[160,128]{1,0:T(8,128)S(1)}, u32[]{:S(2)}, u32[]{:S(2)}) collective-permute-start(f32[160,128]{1,0:T(8,128)S(1)} %shard_map.77.refs_0_), channel_id=1, source_target_pairs={{0,24},{1,25},{2,26},{3,27},{4,28},{5,29},{6,30},{7,31},{8,16},{9,... | collective-permute-start | bytes 245768 | tf_op jit(solution)/shard_map/ppermute | solution.py:251
  49.6 4.4 %collective-permute-start.18 = (f32[160,128]{1,0:T(8,128)S(1)}, f32[160,128]{1,0:T(8,128)S(1)}, u32[]{:S(2)}, u32[]{:S(2)}) collective-permute-start(f32[160,128]{1,0:T(8,128)S(1)} %shard_map.77.refs_0_), channel_id=1, source_target_pairs={{0,16},{1,17},{2,18},{3,19},{4,20},{5,21},{6,22},{7,23},{8,24},{9,... | collective-permute-start | bytes 245768 | tf_op jit(solution)/shard_map/ppermute | solution.py:251
  50.1 4.4 %collective-permute-start.17 = (f32[160,128]{1,0:T(8,128)S(1)}, f32[160,128]{1,0:T(8,128)S(1)}, u32[]{:S(2)}, u32[]{:S(2)}) collective-permute-start(f32[160,128]{1,0:T(8,128)S(1)} %shard_map.77.refs_0_), channel_id=1, source_target_pairs={{0,8},{1,9},{2,10},{3,11},{4,12},{5,13},{6,14},{7,15},{8,0},{9,1},... | collective-permute-start | bytes 245768 | tf_op jit(solution)/shard_map/ppermute | solution.py:251
  50.3 4.3 %collective-permute-start.20 = (f32[160,128]{1,0:T(8,128)S(1)}, f32[160,128]{1,0:T(8,128)S(1)}, u32[]{:S(2)}, u32[]{:S(2)}) collective-permute-start(f32[160,128]{1,0:T(8,128)S(1)} %shard_map.77.refs_0_), channel_id=1, source_target_pairs={{0,4},{1,5},{2,6},{3,7},{4,0},{5,1},{6,2},{7,3},{8,12},{9,13},{10,... | collective-permute-start | bytes 245768 | tf_op jit(solution)/shard_map/ppermute | solution.py:251
  52.9 1.7 %collective-permute-start.23 = (f32[160,128]{1,0:T(8,128)S(1)}, f32[160,128]{1,0:T(8,128)S(1)}, u32[]{:S(2)}, u32[]{:S(2)}) collective-permute-start(f32[160,128]{1,0:T(8,128)S(1)} %collective-permute-done.19.refs_3_), channel_id=1, source_target_pairs={{0,4},{1,5},{2,6},{3,7},{4,0},{5,1},{6,2},{7,3},{8,12},{9,13},{10,... | collective-permute-start | bytes 245768 | tf_op jit(solution)/shard_map/ppermute | solution.py:251
  54.1 1.3 %collective-permute-start.22 = (f32[160,128]{1,0:T(8,128)S(1)}, f32[160,128]{1,0:T(8,128)S(1)}, u32[]{:S(2)}, u32[]{:S(2)}) collective-permute-start(f32[160,128]{1,0:T(8,128)S(1)} %collective-permute-done.18.refs_2_), channel_id=1, source_target_pairs={{0,4},{1,5},{2,6},{3,7},{4,0},{5,1},{6,2},{7,3},{8,12},{9,13},{10,... | collective-permute-start | bytes 245768 | tf_op jit(solution)/shard_map/ppermute | solution.py:251
  54.6 1.3 %collective-permute-start.21 = (f32[160,128]{1,0:T(8,128)S(1)}, f32[160,128]{1,0:T(8,128)S(1)}, u32[]{:S(2)}, u32[]{:S(2)}) collective-permute-start(f32[160,128]{1,0:T(8,128)S(1)} %collective-permute-done.17.refs_1_), channel_id=1, source_target_pairs={{0,4},{1,5},{2,6},{3,7},{4,0},{5,1},{6,2},{7,3},{8,12},{9,13},{10,... | collective-permute-start | bytes 245768 | tf_op jit(solution)/shard_map/ppermute | solution.py:251

commit v12 on v11

--- a/solution.py
+++ b/solution.py
@@ -250,6 +250,9 @@
         mask = ((point * 2 + side) * 2 + core) * grid + column
         return lax.ppermute(x, AXES, [(i, i ^ mask) for i in range(devices)])
 
+    def swap_columns(x, steps):
+        return lax.ppermute(x, AXES, [(i, i ^ steps[i // grid % 2]) for i in range(devices)])
+
     extent = sigma_rows.shape[2]
     block = shape((height, width), bf16)
     cuts = (extent // 2, extent // 2)
@@ -315,8 +318,8 @@
         after=[total],
     )
     near, far = deliver(out_near, 0), deliver(out_far, 1)
-    total = add(total, swap(total, column=2))
-    total = add(total, swap(total, column=1), after=[near, far])
+    total = add(total, swap_columns(total, (1, 2)))
+    total = add(total, swap_columns(total, (2, 1)), after=[near, far])
     quarters = [total, swap(total, side=1), swap(total, point=1), swap(total, side=1, point=1)]
     quarters += [swap(x, core=1) for x in quarters]
     return call(

time: 57.6 us -> 58.2 us (1.010)
  starting transfers between devices: 30.2 us -> 31.3 us
    ppermute x22 -> x20, waiting for transfers between devices: 20.8 us -> 15.8 us  [swap(): return lax.ppermute(x, AXES, [(i, i ^ mask) for i in range(devices)])]
    ppermute x0 -> x2, waiting for transfers between devices: none -> 4.54 us  [swap_columns(): lax.ppermute(x, AXES, [(i, i ^ steps[i // grid % 2]) for i in range(devic...]
    ppermute x0 -> x2, starting transfers between devices: none -> 2.49 us  [swap_columns(): lax.ppermute(x, AXES, [(i, i ^ steps[i // grid % 2]) for i in range(devic...]
    ppermute x22 -> x20, starting transfers between devices: 25.7 us -> 23.7 us  [swap(): return lax.ppermute(x, AXES, [(i, i ^ mask) for i in range(devices)])]
where the time goes in v12:
time: 58.2 us; the launch traced here: 58 us
  starting transfers between devices  31.3 us (54%)
  waiting for transfers between devices  20.3 us (35%)
  Pallas kernels  5.02 us (9%)
  between operations  1.38 us (2%)
    ppermute x20, starting transfers between devices, swap(): return lax.ppermute(x, AXES, [(i, i ^ mask) for i in range(devices)])  23.7 us
    ppermute x20, waiting for transfers between devices, swap(): return lax.ppermute(x, AXES, [(i, i ^ mask) for i in range(devices)])  15.8 us
    ppermute x2, starting transfers between devices, deliver(): return lax.ppermute(x, AXES, pairs)  5.05 us
    pallas_call x11, Pallas kernels, call(): pl.pallas_call(body, out_shape=outs, in_specs=list(specs) + [ANY] * len(a...  5.02 us
    ppermute x2, waiting for transfers between devices, swap_columns(): lax.ppermute(x, AXES, [(i, i ^ steps[i // grid % 2]) for i in range(devic...  4.54 us
    ppermute x2, starting transfers between devices, swap_columns(): lax.ppermute(x, AXES, [(i, i ^ steps[i // grid % 2]) for i in range(devic...  2.49 us
  transfers between devices with their start and end apart: 24, of which 14 were waited for; matrix products, arithmetic and copies ran while one was open for 0% of the time, Pallas kernels for 3%

profile of v12, /device:TPU:0, one launch (start us, length us, event | category | flops | bytes accessed | tf_op | source)
XLA Modules:
  0.0 58.0 jit_solution(9224439611928819738)
XLA Ops:
  0.6 1.7 %shard_map.68 = (bf16[128,384]{1,0:T(8,128)(2,1)S(1)}, bf16[160,384]{1,0:T(8,128)(2,1)S(1)}, bf16[32,384]{1,0:T(8,128)(2,1)S(1)}, bf16[256,512]{1,0:T(8,128)(2,1)S(1)}, bf16[256,512]{1,0:T(8,128)(2,1)S(1)}) custom-call(s32[2]{0:T(128)} %bitcast.1, bf16[1,128,2,384]{3,2,1,0:T(2,128)(2,1)} %refs_1_.1, bf16[1,2,24,384]{3,2,1,0:T(8,128)(2,1)} %refs_2_.1, ...), custom_call_target="tpu_custom_call" | custom-call | tf_op jit(solution)/shard_map/pallas_call | solution.py:28
  2.3 3.0 %collective-permute-start.3 = (bf16[160,384]{1,0:T(8,128)(2,1)S(1)}, bf16[160,384]{1,0:T(8,128)(2,1)S(1)}, u32[]{:S(2)}, u32[]{:S(2)}) collective-permute-start(bf16[160,384]{1,0:T(8,128)(2,1)S(1)} %get-tuple-element.16), channel_id=1, source_target_pairs={{0,8},{1,9},{2,10},{3,11},{4,12},{5,13},{6,14},{7,15},{8,0},{9,1},... | collective-permute-start | bytes 368648 | tf_op jit(solution)/shard_map/ppermute | solution.py:251
  5.4 1.9 %collective-permute-start.8 = (bf16[256,512]{1,0:T(8,128)(2,1)S(1)}, bf16[256,512]{1,0:T(8,128)(2,1)S(1)}, u32[]{:S(2)}, u32[]{:S(2)}) collective-permute-start(bf16[256,512]{1,0:T(8,128)(2,1)S(1)} %get-tuple-element.18.refs_2_), channel_id=1, source_target_pairs={{0,8},{1,9},{2,10},{3,11},{4,12},{5,13},{6,14},{7,15},{8,0},{9,1},... | collective-permute-start | bytes 786440 | tf_op jit(solution)/shard_map/ppermute | solution.py:251
  7.4 2.6 %collective-permute-start = (bf16[128,384]{1,0:T(8,128)(2,1)S(1)}, bf16[128,384]{1,0:T(8,128)(2,1)S(1)}, u32[]{:S(2)}, u32[]{:S(2)}) collective-permute-start(bf16[128,384]{1,0:T(8,128)(2,1)S(1)} %get-tuple-element.15.refs_0_), channel_id=1, source_target_pairs={{0,2},{1,3},{2,0},{3,1},{4,6},{5,7},{6,4},{7,5},{8,10},{9,11},{10,... | collective-permute-start | bytes 294920 | tf_op jit(solution)/shard_map/ppermute | solution.py:251
  10.0 1.6 %collective-permute-start.1 = (bf16[128,384]{1,0:T(8,128)(2,1)S(1)}, bf16[128,384]{1,0:T(8,128)(2,1)S(1)}, u32[]{:S(2)}, u32[]{:S(2)}) collective-permute-start(bf16[128,384]{1,0:T(8,128)(2,1)S(1)} %get-tuple-element.15.refs_0_), channel_id=1, source_target_pairs={{0,1},{1,0},{2,3},{3,2},{4,5},{5,4},{6,7},{7,6},{8,9},{9,8},{10,11... | collective-permute-start | bytes 294920 | tf_op jit(solution)/shard_map/ppermute | solution.py:251
  11.6 1.2 %collective-permute-start.4 = (bf16[128,384]{1,0:T(8,128)(2,1)S(1)}, bf16[128,384]{1,0:T(8,128)(2,1)S(1)}, u32[]{:S(2)}, u32[]{:S(2)}) collective-permute-start(bf16[128,384]{1,0:T(8,128)(2,1)S(1)} %slice.8.refs_4_), channel_id=1, source_target_pairs={{0,2},{1,3},{2,0},{3,1},{4,6},{5,7},{6,4},{7,5},{8,10},{9,11},{10,... | collective-permute-start | bytes 294920 | tf_op jit(solution)/shard_map/ppermute | solution.py:251
  13.1 3.8 %collective-permute-start.2 = (bf16[128,384]{1,0:T(8,128)(2,1)S(1)}, bf16[128,384]{1,0:T(8,128)(2,1)S(1)}, u32[]{:S(2)}, u32[]{:S(2)}) collective-permute-start(bf16[128,384]{1,0:T(8,128)(2,1)S(1)} %collective-permute-done.refs_1_), channel_id=1, source_target_pairs={{0,1},{1,0},{2,3},{3,2},{4,5},{5,4},{6,7},{7,6},{8,9},{9,8},{10,11... | collective-permute-start | bytes 294920 | tf_op jit(solution)/shard_map/ppermute | solution.py:251
  17.0 0.7 %collective-permute-start.5 = (bf16[128,384]{1,0:T(8,128)(2,1)S(1)}, bf16[128,384]{1,0:T(8,128)(2,1)S(1)}, u32[]{:S(2)}, u32[]{:S(2)}) collective-permute-start(bf16[128,384]{1,0:T(8,128)(2,1)S(1)} %slice.8.refs_4_), channel_id=1, source_target_pairs={{0,1},{1,0},{2,3},{3,2},{4,5},{5,4},{6,7},{7,6},{8,9},{9,8},{10,11... | collective-permute-start | bytes 294920 | tf_op jit(solution)/shard_map/ppermute | solution.py:251
  17.7 0.6 %collective-permute-done.4.refs_5_ = bf16[128,384]{1,0:T(8,128)(2,1)S(1)} collective-permute-done((bf16[128,384]{1,0:T(8,128)(2,1)S(1)}, bf16[128,384]{1,0:T(8,128)(2,1)S(1)}, u32[]{:S(2)}, u32[]{:S(2)}) %collective-permute-start.4) | collective-permute-done | bytes 98336 | tf_op jit(solution)/shard_map/ppermute | solution.py:251
  18.3 0.7 %collective-permute-start.6 = (bf16[128,384]{1,0:T(8,128)(2,1)S(1)}, bf16[128,384]{1,0:T(8,128)(2,1)S(1)}, u32[]{:S(2)}, u32[]{:S(2)}) collective-permute-start(bf16[128,384]{1,0:T(8,128)(2,1)S(1)} %collective-permute-done.4.refs_5_), channel_id=1, source_target_pairs={{0,1},{1,0},{2,3},{3,2},{4,5},{5,4},{6,7},{7,6},{8,9},{9,8},{10,11... | collective-permute-start | bytes 294920 | tf_op jit(solution)/shard_map/ppermute | solution.py:251
  19.0 1.6 %collective-permute-done.2.refs_3_ = bf16[128,384]{1,0:T(8,128)(2,1)S(1)} collective-permute-done((bf16[128,384]{1,0:T(8,128)(2,1)S(1)}, bf16[128,384]{1,0:T(8,128)(2,1)S(1)}, u32[]{:S(2)}, u32[]{:S(2)}) %collective-permute-start.2) | collective-permute-done | bytes 98336 | tf_op jit(solution)/shard_map/ppermute | solution.py:251
  20.7 1.3 %collective-permute-done.5.refs_6_ = bf16[128,384]{1,0:T(8,128)(2,1)S(1)} collective-permute-done((bf16[128,384]{1,0:T(8,128)(2,1)S(1)}, bf16[128,384]{1,0:T(8,128)(2,1)S(1)}, u32[]{:S(2)}, u32[]{:S(2)}) %collective-permute-start.5) | collective-permute-done | bytes 98336 | tf_op jit(solution)/shard_map/ppermute | solution.py:251
  22.0 1.0 %collective-permute-done.6.refs_7_ = bf16[128,384]{1,0:T(8,128)(2,1)S(1)} collective-permute-done((bf16[128,384]{1,0:T(8,128)(2,1)S(1)}, bf16[128,384]{1,0:T(8,128)(2,1)S(1)}, u32[]{:S(2)}, u32[]{:S(2)}) %collective-permute-start.6) | collective-permute-done | bytes 98336 | tf_op jit(solution)/shard_map/ppermute | solution.py:251
  23.2 0.7 %shard_map.70.refs_0_ = f32[512,384]{1,0:T(8,128)S(1)} custom-call(bf16[2,512,384]{2,1,0:T(8,128)(2,1)S(1)} %get-tuple-element.19.refs_0_, bf16[256,512]{1,0:T(8,128)(2,1)S(1)} %get-tuple-element.17.refs_1_, bf16[256,512]{1,0:T(8,128)(2,1)S(1)} %get-tuple-element.18.refs_2_, bf16[256,512]{1,0:T(8,128)(2,1)S(1)} %collective-permute-done.7.refs_8_.refs_3_, ...), custom_call_target="tpu_custom_call" | custom-call | tf_op jit(solution)/shard_map/pallas_call | solution.py:28
  23.9 1.0 %collective-permute-done.9.refs_1_.refs_3_ = bf16[512,384]{1,0:T(8,128)(2,1)S(1)} collective-permute-done((bf16[512,384]{1,0:T(8,128)(2,1)S(1)}, bf16[512,384]{1,0:T(8,128)(2,1)S(1)}, u32[]{:S(2)}, u32[]{:S(2)}) %collective-permute-start.9) | collective-permute-done | bytes 393248 | tf_op jit(solution)/shard_map/ppermute | solution.py:251
  25.7 0.7 %shard_map.72 = (f32[320,128]{1,0:T(8,128)S(1)}, f32[320,128]{1,0:T(8,128)S(1)}) custom-call(f32[1]{0:T(128)S(6)} %copy.9.refs_0_, f32[512,384]{1,0:T(8,128)S(1)} %shard_map.71.refs_1_.refs_0_, bf16[512,384]{1,0:T(8,128)(2,1)S(1)} %get-tuple-element.20.refs_2_, bf16[512,384]{1,0:T(8,128)(2,1)S(1)} %collective-permute-done.9.refs_1_.refs_3_, ...), custom_call_target="tpu_custom_call" | custom-call | tf_op jit(solution)/shard_map/pallas_call | solution.py:28
  26.8 1.0 %collective-permute-done.10.refs_1_ = f32[320,128]{1,0:T(8,128)S(1)} collective-permute-done((f32[320,128]{1,0:T(8,128)S(1)}, f32[320,128]{1,0:T(8,128)S(1)}, u32[]{:S(2)}, u32[]{:S(2)}) %collective-permute-start.10) | collective-permute-done | bytes 163872 | tf_op jit(solution)/shard_map/ppermute | solution.py:251
  27.9 1.6 %collective-permute-start.11 = (f32[160,128]{1,0:T(8,128)S(1)}, f32[160,128]{1,0:T(8,128)S(1)}, u32[]{:S(2)}, u32[]{:S(2)}) collective-permute-start(f32[160,128]{1,0:T(8,128)S(1)} %get-tuple-element.25), channel_id=1, source_target_pairs={{0,16},{1,17},{2,18},{3,19},{4,20},{5,21},{6,22},{7,23},{8,24},{9,... | collective-permute-start | bytes 245768 | tf_op jit(solution)/shard_map/ppermute | solution.py:251
  29.5 3.2 %collective-permute-done.11.refs_1_ = f32[160,128]{1,0:T(8,128)S(1)} collective-permute-done((f32[160,128]{1,0:T(8,128)S(1)}, f32[160,128]{1,0:T(8,128)S(1)}, u32[]{:S(2)}, u32[]{:S(2)}) %collective-permute-start.11) | collective-permute-done | bytes 81952 | tf_op jit(solution)/shard_map/ppermute | solution.py:251
  32.7 1.5 %collective-permute-start.12 = (f32[160,128]{1,0:T(8,128)S(1)}, f32[160,128]{1,0:T(8,128)S(1)}, u32[]{:S(2)}, u32[]{:S(2)}) collective-permute-start(f32[160,128]{1,0:T(8,128)S(1)} %shard_map.74.refs_0_.refs_2_), channel_id=1, source_target_pairs={{0,1},{1,0},{2,3},{3,2},{4,6},{5,7},{6,4},{7,5},{8,9},{9,8},{10,11... | collective-permute-start | bytes 245768 | tf_op jit(solution)/shard_map/ppermute | solution.py:254
  34.4 0.7 %collective-permute-start.15 = (bf16[128,384]{1,0:T(8,128)(2,1)S(1)}, bf16[128,384]{1,0:T(8,128)(2,1)S(1)}, u32[]{:S(2)}, u32[]{:S(2)}) collective-permute-start(bf16[128,384]{1,0:T(8,128)(2,1)S(1)} %get-tuple-element.26), channel_id=1, source_target_pairs={{0,0},{1,4},{2,8},{3,12},{4,1},{5,5},{6,9},{7,13},{8,2},{9,6},{10,... | collective-permute-start | bytes 294920 | tf_op jit(solution)/shard_map/ppermute | solution.py:311
  35.0 4.4 %collective-permute-start.16 = (bf16[128,384]{1,0:T(8,128)(2,1)S(1)}, bf16[128,384]{1,0:T(8,128)(2,1)S(1)}, u32[]{:S(2)}, u32[]{:S(2)}) collective-permute-start(bf16[128,384]{1,0:T(8,128)(2,1)S(1)} %get-tuple-element.27), channel_id=1, source_target_pairs={{0,2},{1,6},{2,10},{3,14},{4,3},{5,7},{6,11},{7,15},{8,0},{9,4},{1... | collective-permute-start | bytes 294920 | tf_op jit(solution)/shard_map/ppermute | solution.py:311
  39.4 1.0 %collective-permute-start.13 = (f32[160,128]{1,0:T(8,128)S(1)}, f32[160,128]{1,0:T(8,128)S(1)}, u32[]{:S(2)}, u32[]{:S(2)}) collective-permute-start(f32[160,128]{1,0:T(8,128)S(1)} %shard_map.75.refs_0_), channel_id=1, source_target_pairs={{0,2},{1,3},{2,0},{3,1},{4,5},{5,4},{6,7},{7,6},{8,10},{9,11},{10,... | collective-permute-start | bytes 245768 | tf_op jit(solution)/shard_map/ppermute | solution.py:254
  40.4 4.5 %collective-permute-done.13.refs_1_ = f32[160,128]{1,0:T(8,128)S(1)} collective-permute-done((f32[160,128]{1,0:T(8,128)S(1)}, f32[160,128]{1,0:T(8,128)S(1)}, u32[]{:S(2)}, u32[]{:S(2)}) %collective-permute-start.13) | collective-permute-done | bytes 81952 | tf_op jit(solution)/shard_map/ppermute | solution.py:254
  45.0 5.2 %collective-permute-start.19 = (f32[160,128]{1,0:T(8,128)S(1)}, f32[160,128]{1,0:T(8,128)S(1)}, u32[]{:S(2)}, u32[]{:S(2)}) collective-permute-start(f32[160,128]{1,0:T(8,128)S(1)} %shard_map.77.refs_0_), channel_id=1, source_target_pairs={{0,24},{1,25},{2,26},{3,27},{4,28},{5,29},{6,30},{7,31},{8,16},{9,... | collective-permute-start | bytes 245768 | tf_op jit(solution)/shard_map/ppermute | solution.py:251
  50.2 0.5 collective-permute-start.18
  50.9 2.4 %collective-permute-done.19.refs_3_ = f32[160,128]{1,0:T(8,128)S(1)} collective-permute-done((f32[160,128]{1,0:T(8,128)S(1)}, f32[160,128]{1,0:T(8,128)S(1)}, u32[]{:S(2)}, u32[]{:S(2)}) %collective-permute-start.19) | collective-permute-done | bytes 81952 | tf_op jit(solution)/shard_map/ppermute | solution.py:251
  53.3 1.3 %collective-permute-done.18.refs_2_ = f32[160,128]{1,0:T(8,128)S(1)} collective-permute-done((f32[160,128]{1,0:T(8,128)S(1)}, f32[160,128]{1,0:T(8,128)S(1)}, u32[]{:S(2)}, u32[]{:S(2)}) %collective-permute-start.18) | collective-permute-done | bytes 81952 | tf_op jit(solution)/shard_map/ppermute | solution.py:251
  54.7 0.5 collective-permute-done.17.refs_1_
  55.2 0.8 %collective-permute-done.22.refs_6_ = f32[160,128]{1,0:T(8,128)S(1)} collective-permute-done((f32[160,128]{1,0:T(8,128)S(1)}, f32[160,128]{1,0:T(8,128)S(1)}, u32[]{:S(2)}, u32[]{:S(2)}) %collective-permute-start.22) | collective-permute-done | bytes 81952 | tf_op jit(solution)/shard_map/ppermute | solution.py:251
  56.0 0.5 collective-permute-done.21.refs_5_
  56.5 1.5 %shard_map.78 = (bf16[1,128,2,384]{3,2,1,0:T(2,128)(2,1)}, f32[2,384,384]{2,1,0:T(8,128)}) custom-call(f32[160,128]{1,0:T(8,128)S(1)} %shard_map.77.refs_0_, f32[160,128]{1,0:T(8,128)S(1)} %collective-permute-done.17.refs_1_, f32[160,128]{1,0:T(8,128)S(1)} %collective-permute-done.18.refs_2_, f32[160,128]{1,0:T(8,128)S(1)} %collective-permute-done.19.refs_3_, ...), custom_call_target="tpu_custom_call" | custom-call | tf_op jit(solution)/shard_map/pallas_call | solution.py:28
  (31 shorter events, 1.6 us)
Async XLA Ops:
  2.3 9.2 %collective-permute-start.3 = (bf16[160,384]{1,0:T(8,128)(2,1)S(1)}, bf16[160,384]{1,0:T(8,128)(2,1)S(1)}, u32[]{:S(2)}, u32[]{:S(2)}) collective-permute-start(bf16[160,384]{1,0:T(8,128)(2,1)S(1)} %get-tuple-element.16), channel_id=1, source_target_pairs={{0,8},{1,9},{2,10},{3,11},{4,12},{5,13},{6,14},{7,15},{8,0},{9,1},... | collective-permute-start | bytes 368648 | tf_op jit(solution)/shard_map/ppermute | solution.py:251
  5.3 16.6 %collective-permute-start.7 = (bf16[256,512]{1,0:T(8,128)(2,1)S(1)}, bf16[256,512]{1,0:T(8,128)(2,1)S(1)}, u32[]{:S(2)}, u32[]{:S(2)}) collective-permute-start(bf16[256,512]{1,0:T(8,128)(2,1)S(1)} %get-tuple-element.17.refs_1_), channel_id=1, source_target_pairs={{0,8},{1,9},{2,10},{3,11},{4,12},{5,13},{6,14},{7,15},{8,0},{9,1},... | collective-permute-start | bytes 786440 | tf_op jit(solution)/shard_map/ppermute | solution.py:251
  5.4 16.5 %collective-permute-start.8 = (bf16[256,512]{1,0:T(8,128)(2,1)S(1)}, bf16[256,512]{1,0:T(8,128)(2,1)S(1)}, u32[]{:S(2)}, u32[]{:S(2)}) collective-permute-start(bf16[256,512]{1,0:T(8,128)(2,1)S(1)} %get-tuple-element.18.refs_2_), channel_id=1, source_target_pairs={{0,8},{1,9},{2,10},{3,11},{4,12},{5,13},{6,14},{7,15},{8,0},{9,1},... | collective-permute-start | bytes 786440 | tf_op jit(solution)/shard_map/ppermute | solution.py:251
  7.4 5.8 %collective-permute-start = (bf16[128,384]{1,0:T(8,128)(2,1)S(1)}, bf16[128,384]{1,0:T(8,128)(2,1)S(1)}, u32[]{:S(2)}, u32[]{:S(2)}) collective-permute-start(bf16[128,384]{1,0:T(8,128)(2,1)S(1)} %get-tuple-element.15.refs_0_), channel_id=1, source_target_pairs={{0,2},{1,3},{2,0},{3,1},{4,6},{5,7},{6,4},{7,5},{8,10},{9,11},{10,... | collective-permute-start | bytes 294920 | tf_op jit(solution)/shard_map/ppermute | solution.py:251
  10.0 7.0 %collective-permute-start.1 = (bf16[128,384]{1,0:T(8,128)(2,1)S(1)}, bf16[128,384]{1,0:T(8,128)(2,1)S(1)}, u32[]{:S(2)}, u32[]{:S(2)}) collective-permute-start(bf16[128,384]{1,0:T(8,128)(2,1)S(1)} %get-tuple-element.15.refs_0_), channel_id=1, source_target_pairs={{0,1},{1,0},{2,3},{3,2},{4,5},{5,4},{6,7},{7,6},{8,9},{9,8},{10,11... | collective-permute-start | bytes 294920 | tf_op jit(solution)/shard_map/ppermute | solution.py:251
  11.6 6.8 %collective-permute-start.4 = (bf16[128,384]{1,0:T(8,128)(2,1)S(1)}, bf16[128,384]{1,0:T(8,128)(2,1)S(1)}, u32[]{:S(2)}, u32[]{:S(2)}) collective-permute-start(bf16[128,384]{1,0:T(8,128)(2,1)S(1)} %slice.8.refs_4_), channel_id=1, source_target_pairs={{0,2},{1,3},{2,0},{3,1},{4,6},{5,7},{6,4},{7,5},{8,10},{9,11},{10,... | collective-permute-start | bytes 294920 | tf_op jit(solution)/shard_map/ppermute | solution.py:251
  13.1 7.6 %collective-permute-start.2 = (bf16[128,384]{1,0:T(8,128)(2,1)S(1)}, bf16[128,384]{1,0:T(8,128)(2,1)S(1)}, u32[]{:S(2)}, u32[]{:S(2)}) collective-permute-start(bf16[128,384]{1,0:T(8,128)(2,1)S(1)} %collective-permute-done.refs_1_), channel_id=1, source_target_pairs={{0,1},{1,0},{2,3},{3,2},{4,5},{5,4},{6,7},{7,6},{8,9},{9,8},{10,11... | collective-permute-start | bytes 294920 | tf_op jit(solution)/shard_map/ppermute | solution.py:251
  17.0 5.0 %collective-permute-start.5 = (bf16[128,384]{1,0:T(8,128)(2,1)S(1)}, bf16[128,384]{1,0:T(8,128)(2,1)S(1)}, u32[]{:S(2)}, u32[]{:S(2)}) collective-permute-start(bf16[128,384]{1,0:T(8,128)(2,1)S(1)} %slice.8.refs_4_), channel_id=1, source_target_pairs={{0,1},{1,0},{2,3},{3,2},{4,5},{5,4},{6,7},{7,6},{8,9},{9,8},{10,11... | collective-permute-start | bytes 294920 | tf_op jit(solution)/shard_map/ppermute | solution.py:251
  18.3 4.7 %collective-permute-start.6 = (bf16[128,384]{1,0:T(8,128)(2,1)S(1)}, bf16[128,384]{1,0:T(8,128)(2,1)S(1)}, u32[]{:S(2)}, u32[]{:S(2)}) collective-permute-start(bf16[128,384]{1,0:T(8,128)(2,1)S(1)} %collective-permute-done.4.refs_5_), channel_id=1, source_target_pairs={{0,1},{1,0},{2,3},{3,2},{4,5},{5,4},{6,7},{7,6},{8,9},{9,8},{10,11... | collective-permute-start | bytes 294920 | tf_op jit(solution)/shard_map/ppermute | solution.py:251
  23.1 1.8 %collective-permute-start.9 = (bf16[512,384]{1,0:T(8,128)(2,1)S(1)}, bf16[512,384]{1,0:T(8,128)(2,1)S(1)}, u32[]{:S(2)}, u32[]{:S(2)}) collective-permute-start(bf16[512,384]{1,0:T(8,128)(2,1)S(1)} %get-tuple-element.20.refs_2_), channel_id=1, source_target_pairs={{0,4},{1,5},{2,6},{3,7},{4,0},{5,1},{6,2},{7,3},{8,12},{9,13},{10,... | collective-permute-start | bytes 1179656 | tf_op jit(solution)/shard_map/ppermute | solution.py:251
  24.9 9.3 %collective-permute-start.14 = (f32[512,384]{1,0:T(8,128)S(1)}, f32[512,384]{1,0:T(8,128)S(1)}, u32[]{:S(2)}, u32[]{:S(2)}) collective-permute-start(f32[512,384]{1,0:T(8,128)S(1)} %shard_map.71.refs_1_.refs_0_), channel_id=1, source_target_pairs={{0,4},{1,5},{2,6},{3,7},{4,0},{5,1},{6,2},{7,3},{8,12},{9,13},{10,... | collective-permute-start | bytes 2359304 | tf_op jit(solution)/shard_map/ppermute | solution.py:251
  26.4 1.4 %collective-permute-start.10 = (f32[320,128]{1,0:T(8,128)S(1)}, f32[320,128]{1,0:T(8,128)S(1)}, u32[]{:S(2)}, u32[]{:S(2)}) collective-permute-start(f32[320,128]{1,0:T(8,128)S(1)} %get-tuple-element.23), channel_id=1, source_target_pairs={{0,4},{1,5},{2,6},{3,7},{4,0},{5,1},{6,2},{7,3},{8,12},{9,13},{10,... | collective-permute-start | bytes 491528 | tf_op jit(solution)/shard_map/ppermute | solution.py:251
  27.9 4.8 %collective-permute-start.11 = (f32[160,128]{1,0:T(8,128)S(1)}, f32[160,128]{1,0:T(8,128)S(1)}, u32[]{:S(2)}, u32[]{:S(2)}) collective-permute-start(f32[160,128]{1,0:T(8,128)S(1)} %get-tuple-element.25), channel_id=1, source_target_pairs={{0,16},{1,17},{2,18},{3,19},{4,20},{5,21},{6,22},{7,23},{8,24},{9,... | collective-permute-start | bytes 245768 | tf_op jit(solution)/shard_map/ppermute | solution.py:251
  32.7 23.8 %copy-start = (s32[2,1]{0,1:T(1,128)S(1)}, s32[2,1]{0,1:T(1,128)}, u32[]{:S(2)}) copy-start(s32[2,1]{0,1:T(1,128)} %param.7) | copy-start | bytes 28
  32.7 6.7 %collective-permute-start.12 = (f32[160,128]{1,0:T(8,128)S(1)}, f32[160,128]{1,0:T(8,128)S(1)}, u32[]{:S(2)}, u32[]{:S(2)}) collective-permute-start(f32[160,128]{1,0:T(8,128)S(1)} %shard_map.74.refs_0_.refs_2_), channel_id=1, source_target_pairs={{0,1},{1,0},{2,3},{3,2},{4,6},{5,7},{6,4},{7,5},{8,9},{9,8},{10,11... | collective-permute-start | bytes 245768 | tf_op jit(solution)/shard_map/ppermute | solution.py:254
  34.4 10.6 %collective-permute-start.15 = (bf16[128,384]{1,0:T(8,128)(2,1)S(1)}, bf16[128,384]{1,0:T(8,128)(2,1)S(1)}, u32[]{:S(2)}, u32[]{:S(2)}) collective-permute-start(bf16[128,384]{1,0:T(8,128)(2,1)S(1)} %get-tuple-element.26), channel_id=1, source_target_pairs={{0,0},{1,4},{2,8},{3,12},{4,1},{5,5},{6,9},{7,13},{8,2},{9,6},{10,... | collective-permute-start | bytes 294920 | tf_op jit(solution)/shard_map/ppermute | solution.py:311
  35.0 9.9 %collective-permute-start.16 = (bf16[128,384]{1,0:T(8,128)(2,1)S(1)}, bf16[128,384]{1,0:T(8,128)(2,1)S(1)}, u32[]{:S(2)}, u32[]{:S(2)}) collective-permute-start(bf16[128,384]{1,0:T(8,128)(2,1)S(1)} %get-tuple-element.27), channel_id=1, source_target_pairs={{0,2},{1,6},{2,10},{3,14},{4,3},{5,7},{6,11},{7,15},{8,0},{9,4},{1... | collective-permute-start | bytes 294920 | tf_op jit(solution)/shard_map/ppermute | solution.py:311
  39.4 5.5 %collective-permute-start.13 = (f32[160,128]{1,0:T(8,128)S(1)}, f32[160,128]{1,0:T(8,128)S(1)}, u32[]{:S(2)}, u32[]{:S(2)}) collective-permute-start(f32[160,128]{1,0:T(8,128)S(1)} %shard_map.75.refs_0_), channel_id=1, source_target_pairs={{0,2},{1,3},{2,0},{3,1},{4,5},{5,4},{6,7},{7,6},{8,10},{9,11},{10,... | collective-permute-start | bytes 245768 | tf_op jit(solution)/shard_map/ppermute | solution.py:254
  45.0 8.3 %collective-permute-start.19 = (f32[160,128]{1,0:T(8,128)S(1)}, f32[160,128]{1,0:T(8,128)S(1)}, u32[]{:S(2)}, u32[]{:S(2)}) collective-permute-start(f32[160,128]{1,0:T(8,128)S(1)} %shard_map.77.refs_0_), channel_id=1, source_target_pairs={{0,24},{1,25},{2,26},{3,27},{4,28},{5,29},{6,30},{7,31},{8,16},{9,... | collective-permute-start | bytes 245768 | tf_op jit(solution)/shard_map/ppermute | solution.py:251
  50.2 4.4 %collective-permute-start.18 = (f32[160,128]{1,0:T(8,128)S(1)}, f32[160,128]{1,0:T(8,128)S(1)}, u32[]{:S(2)}, u32[]{:S(2)}) collective-permute-start(f32[160,128]{1,0:T(8,128)S(1)} %shard_map.77.refs_0_), channel_id=1, source_target_pairs={{0,16},{1,17},{2,18},{3,19},{4,20},{5,21},{6,22},{7,23},{8,24},{9,... | collective-permute-start | bytes 245768 | tf_op jit(solution)/shard_map/ppermute | solution.py:251
  50.8 4.4 %collective-permute-start.17 = (f32[160,128]{1,0:T(8,128)S(1)}, f32[160,128]{1,0:T(8,128)S(1)}, u32[]{:S(2)}, u32[]{:S(2)}) collective-permute-start(f32[160,128]{1,0:T(8,128)S(1)} %shard_map.77.refs_0_), channel_id=1, source_target_pairs={{0,8},{1,9},{2,10},{3,11},{4,12},{5,13},{6,14},{7,15},{8,0},{9,1},... | collective-permute-start | bytes 245768 | tf_op jit(solution)/shard_map/ppermute | solution.py:251
  50.9 4.3 %collective-permute-start.20 = (f32[160,128]{1,0:T(8,128)S(1)}, f32[160,128]{1,0:T(8,128)S(1)}, u32[]{:S(2)}, u32[]{:S(2)}) collective-permute-start(f32[160,128]{1,0:T(8,128)S(1)} %shard_map.77.refs_0_), channel_id=1, source_target_pairs={{0,4},{1,5},{2,6},{3,7},{4,0},{5,1},{6,2},{7,3},{8,12},{9,13},{10,... | collective-permute-start | bytes 245768 | tf_op jit(solution)/shard_map/ppermute | solution.py:251
  53.3 1.9 %collective-permute-start.23 = (f32[160,128]{1,0:T(8,128)S(1)}, f32[160,128]{1,0:T(8,128)S(1)}, u32[]{:S(2)}, u32[]{:S(2)}) collective-permute-start(f32[160,128]{1,0:T(8,128)S(1)} %collective-permute-done.19.refs_3_), channel_id=1, source_target_pairs={{0,4},{1,5},{2,6},{3,7},{4,0},{5,1},{6,2},{7,3},{8,12},{9,13},{10,... | collective-permute-start | bytes 245768 | tf_op jit(solution)/shard_map/ppermute | solution.py:251
  54.7 1.3 %collective-permute-start.22 = (f32[160,128]{1,0:T(8,128)S(1)}, f32[160,128]{1,0:T(8,128)S(1)}, u32[]{:S(2)}, u32[]{:S(2)}) collective-permute-start(f32[160,128]{1,0:T(8,128)S(1)} %collective-permute-done.18.refs_2_), channel_id=1, source_target_pairs={{0,4},{1,5},{2,6},{3,7},{4,0},{5,1},{6,2},{7,3},{8,12},{9,13},{10,... | collective-permute-start | bytes 245768 | tf_op jit(solution)/shard_map/ppermute | solution.py:251
  55.2 1.3 %collective-permute-start.21 = (f32[160,128]{1,0:T(8,128)S(1)}, f32[160,128]{1,0:T(8,128)S(1)}, u32[]{:S(2)}, u32[]{:S(2)}) collective-permute-start(f32[160,128]{1,0:T(8,128)S(1)} %collective-permute-done.17.refs_1_), channel_id=1, source_target_pairs={{0,4},{1,5},{2,6},{3,7},{4,0},{5,1},{6,2},{7,3},{8,12},{9,13},{10,... | collective-permute-start | bytes 245768 | tf_op jit(solution)/shard_map/ppermute | solution.py:251

commit v13 on v12

--- a/solution.py
+++ b/solution.py
@@ -315,11 +315,11 @@
     out_near, out_far = call(
         output_kernel, [block, block], [VMEM] * 2, mine, other,
         scratch=[pltpu.VMEM((extent, width), bf16)],
-        after=[total],
+        after=[keep],
     )
     near, far = deliver(out_near, 0), deliver(out_far, 1)
-    total = add(total, swap_columns(total, (1, 2)))
-    total = add(total, swap_columns(total, (2, 1)), after=[near, far])
+    total = add(total, swap_columns(total, (1, 2)), after=[near])
+    total = add(total, swap_columns(total, (2, 1)), after=[far])
     quarters = [total, swap(total, side=1), swap(total, point=1), swap(total, side=1, point=1)]
     quarters += [swap(x, core=1) for x in quarters]
     return call(

time: 58.2 us -> 58.2 us (level)
  waiting for transfers between devices: 20.3 us -> 17.8 us
  starting transfers between devices: 31.3 us -> 33.8 us
    ppermute x2, starting transfers between devices: 2.49 us -> 6.11 us  [swap_columns(): lax.ppermute(x, AXES, [(i, i ^ steps[i // grid % 2]) for i in range(devic...]
    ppermute x2, waiting for transfers between devices: 4.54 us -> 2.74 us  [swap_columns(): lax.ppermute(x, AXES, [(i, i ^ steps[i // grid % 2]) for i in range(devic...]
    ppermute x2, starting transfers between devices: 5.05 us -> 3.74 us  [deliver(): return lax.ppermute(x, AXES, pairs)]
    ppermute x20, waiting for transfers between devices: 15.8 us -> 15 us  [swap(): return lax.ppermute(x, AXES, [(i, i ^ mask) for i in range(devices)])]
where the time goes in v13:
time: 58.2 us; the launch traced here: 58 us
  starting transfers between devices  33.8 us (58%)
  waiting for transfers between devices  17.8 us (31%)
  Pallas kernels  5.02 us (9%)
  between operations  1.38 us (2%)
    ppermute x20, starting transfers between devices, swap(): return lax.ppermute(x, AXES, [(i, i ^ mask) for i in range(devices)])  23.9 us
    ppermute x20, waiting for transfers between devices, swap(): return lax.ppermute(x, AXES, [(i, i ^ mask) for i in range(devices)])  15 us
    ppermute x2, starting transfers between devices, swap_columns(): lax.ppermute(x, AXES, [(i, i ^ steps[i // grid % 2]) for i in range(devic...  6.11 us
    pallas_call x11, Pallas kernels, call(): pl.pallas_call(body, out_shape=outs, in_specs=list(specs) + [ANY] * len(a...  5.02 us
    ppermute x2, starting transfers between devices, deliver(): return lax.ppermute(x, AXES, pairs)  3.74 us
    ppermute x2, waiting for transfers between devices, swap_columns(): lax.ppermute(x, AXES, [(i, i ^ steps[i // grid % 2]) for i in range(devic...  2.74 us
  transfers between devices with their start and end apart: 24, of which 14 were waited for; matrix products, arithmetic and copies ran while one was open for 0% of the time, Pallas kernels for 3%

profile of v13, /device:TPU:0, one launch (start us, length us, event | category | flops | bytes accessed | tf_op | source)
XLA Modules:
  0.0 58.0 jit_solution(7625646091307905734)
XLA Ops:
  0.6 1.7 %shard_map.68 = (bf16[128,384]{1,0:T(8,128)(2,1)S(1)}, bf16[160,384]{1,0:T(8,128)(2,1)S(1)}, bf16[32,384]{1,0:T(8,128)(2,1)S(1)}, bf16[256,512]{1,0:T(8,128)(2,1)S(1)}, bf16[256,512]{1,0:T(8,128)(2,1)S(1)}) custom-call(s32[2]{0:T(128)} %bitcast.1, bf16[1,128,2,384]{3,2,1,0:T(2,128)(2,1)} %refs_1_.1, bf16[1,2,24,384]{3,2,1,0:T(8,128)(2,1)} %refs_2_.1, ...), custom_call_target="tpu_custom_call" | custom-call | tf_op jit(solution)/shard_map/pallas_call | solution.py:28
  2.3 3.0 %collective-permute-start.3 = (bf16[160,384]{1,0:T(8,128)(2,1)S(1)}, bf16[160,384]{1,0:T(8,128)(2,1)S(1)}, u32[]{:S(2)}, u32[]{:S(2)}) collective-permute-start(bf16[160,384]{1,0:T(8,128)(2,1)S(1)} %get-tuple-element.16), channel_id=1, source_target_pairs={{0,8},{1,9},{2,10},{3,11},{4,12},{5,13},{6,14},{7,15},{8,0},{9,1},... | collective-permute-start | bytes 368648 | tf_op jit(solution)/shard_map/ppermute | solution.py:251
  5.4 1.9 %collective-permute-start.8 = (bf16[256,512]{1,0:T(8,128)(2,1)S(1)}, bf16[256,512]{1,0:T(8,128)(2,1)S(1)}, u32[]{:S(2)}, u32[]{:S(2)}) collective-permute-start(bf16[256,512]{1,0:T(8,128)(2,1)S(1)} %get-tuple-element.18.refs_2_), channel_id=1, source_target_pairs={{0,8},{1,9},{2,10},{3,11},{4,12},{5,13},{6,14},{7,15},{8,0},{9,1},... | collective-permute-start | bytes 786440 | tf_op jit(solution)/shard_map/ppermute | solution.py:251
  7.4 2.6 %collective-permute-start = (bf16[128,384]{1,0:T(8,128)(2,1)S(1)}, bf16[128,384]{1,0:T(8,128)(2,1)S(1)}, u32[]{:S(2)}, u32[]{:S(2)}) collective-permute-start(bf16[128,384]{1,0:T(8,128)(2,1)S(1)} %get-tuple-element.15.refs_0_), channel_id=1, source_target_pairs={{0,2},{1,3},{2,0},{3,1},{4,6},{5,7},{6,4},{7,5},{8,10},{9,11},{10,... | collective-permute-start | bytes 294920 | tf_op jit(solution)/shard_map/ppermute | solution.py:251
  10.0 1.6 %collective-permute-start.1 = (bf16[128,384]{1,0:T(8,128)(2,1)S(1)}, bf16[128,384]{1,0:T(8,128)(2,1)S(1)}, u32[]{:S(2)}, u32[]{:S(2)}) collective-permute-start(bf16[128,384]{1,0:T(8,128)(2,1)S(1)} %get-tuple-element.15.refs_0_), channel_id=1, source_target_pairs={{0,1},{1,0},{2,3},{3,2},{4,5},{5,4},{6,7},{7,6},{8,9},{9,8},{10,11... | collective-permute-start | bytes 294920 | tf_op jit(solution)/shard_map/ppermute | solution.py:251
  11.6 1.2 %collective-permute-start.4 = (bf16[128,384]{1,0:T(8,128)(2,1)S(1)}, bf16[128,384]{1,0:T(8,128)(2,1)S(1)}, u32[]{:S(2)}, u32[]{:S(2)}) collective-permute-start(bf16[128,384]{1,0:T(8,128)(2,1)S(1)} %slice.8.refs_4_), channel_id=1, source_target_pairs={{0,2},{1,3},{2,0},{3,1},{4,6},{5,7},{6,4},{7,5},{8,10},{9,11},{10,... | collective-permute-start | bytes 294920 | tf_op jit(solution)/shard_map/ppermute | solution.py:251
  12.7 0.4 collective-permute-done.refs_1_
  13.1 3.8 %collective-permute-start.2 = (bf16[128,384]{1,0:T(8,128)(2,1)S(1)}, bf16[128,384]{1,0:T(8,128)(2,1)S(1)}, u32[]{:S(2)}, u32[]{:S(2)}) collective-permute-start(bf16[128,384]{1,0:T(8,128)(2,1)S(1)} %collective-permute-done.refs_1_), channel_id=1, source_target_pairs={{0,1},{1,0},{2,3},{3,2},{4,5},{5,4},{6,7},{7,6},{8,9},{9,8},{10,11... | collective-permute-start | bytes 294920 | tf_op jit(solution)/shard_map/ppermute | solution.py:251
  17.0 0.7 %collective-permute-start.5 = (bf16[128,384]{1,0:T(8,128)(2,1)S(1)}, bf16[128,384]{1,0:T(8,128)(2,1)S(1)}, u32[]{:S(2)}, u32[]{:S(2)}) collective-permute-start(bf16[128,384]{1,0:T(8,128)(2,1)S(1)} %slice.8.refs_4_), channel_id=1, source_target_pairs={{0,1},{1,0},{2,3},{3,2},{4,5},{5,4},{6,7},{7,6},{8,9},{9,8},{10,11... | collective-permute-start | bytes 294920 | tf_op jit(solution)/shard_map/ppermute | solution.py:251
  17.7 0.6 %collective-permute-done.4.refs_5_ = bf16[128,384]{1,0:T(8,128)(2,1)S(1)} collective-permute-done((bf16[128,384]{1,0:T(8,128)(2,1)S(1)}, bf16[128,384]{1,0:T(8,128)(2,1)S(1)}, u32[]{:S(2)}, u32[]{:S(2)}) %collective-permute-start.4) | collective-permute-done | bytes 98336 | tf_op jit(solution)/shard_map/ppermute | solution.py:251
  18.3 0.7 %collective-permute-start.6 = (bf16[128,384]{1,0:T(8,128)(2,1)S(1)}, bf16[128,384]{1,0:T(8,128)(2,1)S(1)}, u32[]{:S(2)}, u32[]{:S(2)}) collective-permute-start(bf16[128,384]{1,0:T(8,128)(2,1)S(1)} %collective-permute-done.4.refs_5_), channel_id=1, source_target_pairs={{0,1},{1,0},{2,3},{3,2},{4,5},{5,4},{6,7},{7,6},{8,9},{9,8},{10,11... | collective-permute-start | bytes 294920 | tf_op jit(solution)/shard_map/ppermute | solution.py:251
  19.0 1.6 %collective-permute-done.2.refs_3_ = bf16[128,384]{1,0:T(8,128)(2,1)S(1)} collective-permute-done((bf16[128,384]{1,0:T(8,128)(2,1)S(1)}, bf16[128,384]{1,0:T(8,128)(2,1)S(1)}, u32[]{:S(2)}, u32[]{:S(2)}) %collective-permute-start.2) | collective-permute-done | bytes 98336 | tf_op jit(solution)/shard_map/ppermute | solution.py:251
  20.7 1.3 %collective-permute-done.5.refs_6_ = bf16[128,384]{1,0:T(8,128)(2,1)S(1)} collective-permute-done((bf16[128,384]{1,0:T(8,128)(2,1)S(1)}, bf16[128,384]{1,0:T(8,128)(2,1)S(1)}, u32[]{:S(2)}, u32[]{:S(2)}) %collective-permute-start.5) | collective-permute-done | bytes 98336 | tf_op jit(solution)/shard_map/ppermute | solution.py:251
  22.0 1.0 %collective-permute-done.6.refs_7_ = bf16[128,384]{1,0:T(8,128)(2,1)S(1)} collective-permute-done((bf16[128,384]{1,0:T(8,128)(2,1)S(1)}, bf16[128,384]{1,0:T(8,128)(2,1)S(1)}, u32[]{:S(2)}, u32[]{:S(2)}) %collective-permute-start.6) | collective-permute-done | bytes 98336 | tf_op jit(solution)/shard_map/ppermute | solution.py:251
  23.2 0.7 %shard_map.70.refs_0_ = f32[512,384]{1,0:T(8,128)S(1)} custom-call(bf16[2,512,384]{2,1,0:T(8,128)(2,1)S(1)} %get-tuple-element.19.refs_0_, bf16[256,512]{1,0:T(8,128)(2,1)S(1)} %get-tuple-element.17.refs_1_, bf16[256,512]{1,0:T(8,128)(2,1)S(1)} %get-tuple-element.18.refs_2_, bf16[256,512]{1,0:T(8,128)(2,1)S(1)} %collective-permute-done.7.refs_8_.refs_3_, ...), custom_call_target="tpu_custom_call" | custom-call | tf_op jit(solution)/shard_map/pallas_call | solution.py:28
  23.9 1.0 %collective-permute-done.9.refs_1_.refs_3_ = bf16[512,384]{1,0:T(8,128)(2,1)S(1)} collective-permute-done((bf16[512,384]{1,0:T(8,128)(2,1)S(1)}, bf16[512,384]{1,0:T(8,128)(2,1)S(1)}, u32[]{:S(2)}, u32[]{:S(2)}) %collective-permute-start.9) | collective-permute-done | bytes 393248 | tf_op jit(solution)/shard_map/ppermute | solution.py:251
  25.7 0.7 %shard_map.72 = (f32[320,128]{1,0:T(8,128)S(1)}, f32[320,128]{1,0:T(8,128)S(1)}) custom-call(f32[1]{0:T(128)S(6)} %copy.9.refs_0_, f32[512,384]{1,0:T(8,128)S(1)} %shard_map.71.refs_1_.refs_0_, bf16[512,384]{1,0:T(8,128)(2,1)S(1)} %get-tuple-element.20.refs_2_, bf16[512,384]{1,0:T(8,128)(2,1)S(1)} %collective-permute-done.9.refs_1_.refs_3_, ...), custom_call_target="tpu_custom_call" | custom-call | tf_op jit(solution)/shard_map/pallas_call | solution.py:28
  26.8 1.0 %collective-permute-done.10.refs_1_ = f32[320,128]{1,0:T(8,128)S(1)} collective-permute-done((f32[320,128]{1,0:T(8,128)S(1)}, f32[320,128]{1,0:T(8,128)S(1)}, u32[]{:S(2)}, u32[]{:S(2)}) %collective-permute-start.10) | collective-permute-done | bytes 163872 | tf_op jit(solution)/shard_map/ppermute | solution.py:251
  27.9 1.6 %collective-permute-start.11 = (f32[160,128]{1,0:T(8,128)S(1)}, f32[160,128]{1,0:T(8,128)S(1)}, u32[]{:S(2)}, u32[]{:S(2)}) collective-permute-start(f32[160,128]{1,0:T(8,128)S(1)} %get-tuple-element.25), channel_id=1, source_target_pairs={{0,16},{1,17},{2,18},{3,19},{4,20},{5,21},{6,22},{7,23},{8,24},{9,... | collective-permute-start | bytes 245768 | tf_op jit(solution)/shard_map/ppermute | solution.py:251
  29.7 0.7 %collective-permute-start.14 = (bf16[128,384]{1,0:T(8,128)(2,1)S(1)}, bf16[128,384]{1,0:T(8,128)(2,1)S(1)}, u32[]{:S(2)}, u32[]{:S(2)}) collective-permute-start(bf16[128,384]{1,0:T(8,128)(2,1)S(1)} %get-tuple-element.26), channel_id=1, source_target_pairs={{0,0},{1,4},{2,8},{3,12},{4,1},{5,5},{6,9},{7,13},{8,2},{9,6},{10,... | collective-permute-start | bytes 294920 | tf_op jit(solution)/shard_map/ppermute | solution.py:311
  30.3 2.3 %collective-permute-done.11.refs_1_ = f32[160,128]{1,0:T(8,128)S(1)} collective-permute-done((f32[160,128]{1,0:T(8,128)S(1)}, f32[160,128]{1,0:T(8,128)S(1)}, u32[]{:S(2)}, u32[]{:S(2)}) %collective-permute-start.11) | collective-permute-done | bytes 81952 | tf_op jit(solution)/shard_map/ppermute | solution.py:251
  32.7 1.5 %collective-permute-start.12 = (f32[160,128]{1,0:T(8,128)S(1)}, f32[160,128]{1,0:T(8,128)S(1)}, u32[]{:S(2)}, u32[]{:S(2)}) collective-permute-start(f32[160,128]{1,0:T(8,128)S(1)} %shard_map.74.refs_0_), channel_id=1, source_target_pairs={{0,1},{1,0},{2,3},{3,2},{4,6},{5,7},{6,4},{7,5},{8,9},{9,8},{10,11... | collective-permute-start | bytes 245768 | tf_op jit(solution)/shard_map/ppermute | solution.py:254
  34.2 3.1 %collective-permute-start.16 = (bf16[128,384]{1,0:T(8,128)(2,1)S(1)}, bf16[128,384]{1,0:T(8,128)(2,1)S(1)}, u32[]{:S(2)}, u32[]{:S(2)}) collective-permute-start(bf16[128,384]{1,0:T(8,128)(2,1)S(1)} %get-tuple-element.27), channel_id=1, source_target_pairs={{0,2},{1,6},{2,10},{3,14},{4,3},{5,7},{6,11},{7,15},{8,0},{9,4},{1... | collective-permute-start | bytes 294920 | tf_op jit(solution)/shard_map/ppermute | solution.py:311
  37.5 4.6 %collective-permute-start.15 = (f32[160,128]{1,0:T(8,128)S(1)}, f32[160,128]{1,0:T(8,128)S(1)}, u32[]{:S(2)}, u32[]{:S(2)}) collective-permute-start(f32[160,128]{1,0:T(8,128)S(1)} %shard_map.76.refs_0_), channel_id=1, source_target_pairs={{0,2},{1,3},{2,0},{3,1},{4,5},{5,4},{6,7},{7,6},{8,10},{9,11},{10,... | collective-permute-start | bytes 245768 | tf_op jit(solution)/shard_map/ppermute | solution.py:254
  42.2 2.5 %collective-permute-done.15.refs_1_ = f32[160,128]{1,0:T(8,128)S(1)} collective-permute-done((f32[160,128]{1,0:T(8,128)S(1)}, f32[160,128]{1,0:T(8,128)S(1)}, u32[]{:S(2)}, u32[]{:S(2)}) %collective-permute-start.15) | collective-permute-done | bytes 81952 | tf_op jit(solution)/shard_map/ppermute | solution.py:254
  44.7 4.5 %collective-permute-start.19 = (f32[160,128]{1,0:T(8,128)S(1)}, f32[160,128]{1,0:T(8,128)S(1)}, u32[]{:S(2)}, u32[]{:S(2)}) collective-permute-start(f32[160,128]{1,0:T(8,128)S(1)} %shard_map.77.refs_0_), channel_id=1, source_target_pairs={{0,24},{1,25},{2,26},{3,27},{4,28},{5,29},{6,30},{7,31},{8,16},{9,... | collective-permute-start | bytes 245768 | tf_op jit(solution)/shard_map/ppermute | solution.py:251
  49.2 1.5 %collective-permute-start.18 = (f32[160,128]{1,0:T(8,128)S(1)}, f32[160,128]{1,0:T(8,128)S(1)}, u32[]{:S(2)}, u32[]{:S(2)}) collective-permute-start(f32[160,128]{1,0:T(8,128)S(1)} %shard_map.77.refs_0_), channel_id=1, source_target_pairs={{0,16},{1,17},{2,18},{3,19},{4,20},{5,21},{6,22},{7,23},{8,24},{9,... | collective-permute-start | bytes 245768 | tf_op jit(solution)/shard_map/ppermute | solution.py:251
  50.7 1.1 %collective-permute-done.19.refs_3_ = f32[160,128]{1,0:T(8,128)S(1)} collective-permute-done((f32[160,128]{1,0:T(8,128)S(1)}, f32[160,128]{1,0:T(8,128)S(1)}, u32[]{:S(2)}, u32[]{:S(2)}) %collective-permute-start.19) | collective-permute-done | bytes 81952 | tf_op jit(solution)/shard_map/ppermute | solution.py:251
  51.8 1.8 %collective-permute-done.18.refs_2_ = f32[160,128]{1,0:T(8,128)S(1)} collective-permute-done((f32[160,128]{1,0:T(8,128)S(1)}, f32[160,128]{1,0:T(8,128)S(1)}, u32[]{:S(2)}, u32[]{:S(2)}) %collective-permute-start.18) | collective-permute-done | bytes 81952 | tf_op jit(solution)/shard_map/ppermute | solution.py:251
  53.6 1.5 %collective-permute-done.17.refs_1_ = f32[160,128]{1,0:T(8,128)S(1)} collective-permute-done((f32[160,128]{1,0:T(8,128)S(1)}, f32[160,128]{1,0:T(8,128)S(1)}, u32[]{:S(2)}, u32[]{:S(2)}) %collective-permute-start.17) | collective-permute-done | bytes 81952 | tf_op jit(solution)/shard_map/ppermute | solution.py:251
  55.2 1.3 %collective-permute-done.21.refs_5_ = f32[160,128]{1,0:T(8,128)S(1)} collective-permute-done((f32[160,128]{1,0:T(8,128)S(1)}, f32[160,128]{1,0:T(8,128)S(1)}, u32[]{:S(2)}, u32[]{:S(2)}) %collective-permute-start.21) | collective-permute-done | bytes 81952 | tf_op jit(solution)/shard_map/ppermute | solution.py:251
  56.4 1.5 %shard_map.78 = (bf16[1,128,2,384]{3,2,1,0:T(2,128)(2,1)}, f32[2,384,384]{2,1,0:T(8,128)}) custom-call(f32[160,128]{1,0:T(8,128)S(1)} %shard_map.77.refs_0_, f32[160,128]{1,0:T(8,128)S(1)} %collective-permute-done.17.refs_1_, f32[160,128]{1,0:T(8,128)S(1)} %collective-permute-done.18.refs_2_, f32[160,128]{1,0:T(8,128)S(1)} %collective-permute-done.19.refs_3_, ...), custom_call_target="tpu_custom_call" | custom-call | tf_op jit(solution)/shard_map/pallas_call | solution.py:28
  (31 shorter events, 1.4 us)
Async XLA Ops:
  2.3 9.2 %collective-permute-start.3 = (bf16[160,384]{1,0:T(8,128)(2,1)S(1)}, bf16[160,384]{1,0:T(8,128)(2,1)S(1)}, u32[]{:S(2)}, u32[]{:S(2)}) collective-permute-start(bf16[160,384]{1,0:T(8,128)(2,1)S(1)} %get-tuple-element.16), channel_id=1, source_target_pairs={{0,8},{1,9},{2,10},{3,11},{4,12},{5,13},{6,14},{7,15},{8,0},{9,1},... | collective-permute-start | bytes 368648 | tf_op jit(solution)/shard_map/ppermute | solution.py:251
  5.3 16.6 %collective-permute-start.7 = (bf16[256,512]{1,0:T(8,128)(2,1)S(1)}, bf16[256,512]{1,0:T(8,128)(2,1)S(1)}, u32[]{:S(2)}, u32[]{:S(2)}) collective-permute-start(bf16[256,512]{1,0:T(8,128)(2,1)S(1)} %get-tuple-element.17.refs_1_), channel_id=1, source_target_pairs={{0,8},{1,9},{2,10},{3,11},{4,12},{5,13},{6,14},{7,15},{8,0},{9,1},... | collective-permute-start | bytes 786440 | tf_op jit(solution)/shard_map/ppermute | solution.py:251
  5.4 16.5 %collective-permute-start.8 = (bf16[256,512]{1,0:T(8,128)(2,1)S(1)}, bf16[256,512]{1,0:T(8,128)(2,1)S(1)}, u32[]{:S(2)}, u32[]{:S(2)}) collective-permute-start(bf16[256,512]{1,0:T(8,128)(2,1)S(1)} %get-tuple-element.18.refs_2_), channel_id=1, source_target_pairs={{0,8},{1,9},{2,10},{3,11},{4,12},{5,13},{6,14},{7,15},{8,0},{9,1},... | collective-permute-start | bytes 786440 | tf_op jit(solution)/shard_map/ppermute | solution.py:251
  7.4 5.8 %collective-permute-start = (bf16[128,384]{1,0:T(8,128)(2,1)S(1)}, bf16[128,384]{1,0:T(8,128)(2,1)S(1)}, u32[]{:S(2)}, u32[]{:S(2)}) collective-permute-start(bf16[128,384]{1,0:T(8,128)(2,1)S(1)} %get-tuple-element.15.refs_0_), channel_id=1, source_target_pairs={{0,2},{1,3},{2,0},{3,1},{4,6},{5,7},{6,4},{7,5},{8,10},{9,11},{10,... | collective-permute-start | bytes 294920 | tf_op jit(solution)/shard_map/ppermute | solution.py:251
  10.0 7.0 %collective-permute-start.1 = (bf16[128,384]{1,0:T(8,128)(2,1)S(1)}, bf16[128,384]{1,0:T(8,128)(2,1)S(1)}, u32[]{:S(2)}, u32[]{:S(2)}) collective-permute-start(bf16[128,384]{1,0:T(8,128)(2,1)S(1)} %get-tuple-element.15.refs_0_), channel_id=1, source_target_pairs={{0,1},{1,0},{2,3},{3,2},{4,5},{5,4},{6,7},{7,6},{8,9},{9,8},{10,11... | collective-permute-start | bytes 294920 | tf_op jit(solution)/shard_map/ppermute | solution.py:251
  11.6 6.8 %collective-permute-start.4 = (bf16[128,384]{1,0:T(8,128)(2,1)S(1)}, bf16[128,384]{1,0:T(8,128)(2,1)S(1)}, u32[]{:S(2)}, u32[]{:S(2)}) collective-permute-start(bf16[128,384]{1,0:T(8,128)(2,1)S(1)} %slice.8.refs_4_), channel_id=1, source_target_pairs={{0,2},{1,3},{2,0},{3,1},{4,6},{5,7},{6,4},{7,5},{8,10},{9,11},{10,... | collective-permute-start | bytes 294920 | tf_op jit(solution)/shard_map/ppermute | solution.py:251
  13.1 7.6 %collective-permute-start.2 = (bf16[128,384]{1,0:T(8,128)(2,1)S(1)}, bf16[128,384]{1,0:T(8,128)(2,1)S(1)}, u32[]{:S(2)}, u32[]{:S(2)}) collective-permute-start(bf16[128,384]{1,0:T(8,128)(2,1)S(1)} %collective-permute-done.refs_1_), channel_id=1, source_target_pairs={{0,1},{1,0},{2,3},{3,2},{4,5},{5,4},{6,7},{7,6},{8,9},{9,8},{10,11... | collective-permute-start | bytes 294920 | tf_op jit(solution)/shard_map/ppermute | solution.py:251
  17.0 5.0 %collective-permute-start.5 = (bf16[128,384]{1,0:T(8,128)(2,1)S(1)}, bf16[128,384]{1,0:T(8,128)(2,1)S(1)}, u32[]{:S(2)}, u32[]{:S(2)}) collective-permute-start(bf16[128,384]{1,0:T(8,128)(2,1)S(1)} %slice.8.refs_4_), channel_id=1, source_target_pairs={{0,1},{1,0},{2,3},{3,2},{4,5},{5,4},{6,7},{7,6},{8,9},{9,8},{10,11... | collective-permute-start | bytes 294920 | tf_op jit(solution)/shard_map/ppermute | solution.py:251
  18.3 4.7 %collective-permute-start.6 = (bf16[128,384]{1,0:T(8,128)(2,1)S(1)}, bf16[128,384]{1,0:T(8,128)(2,1)S(1)}, u32[]{:S(2)}, u32[]{:S(2)}) collective-permute-start(bf16[128,384]{1,0:T(8,128)(2,1)S(1)} %collective-permute-done.4.refs_5_), channel_id=1, source_target_pairs={{0,1},{1,0},{2,3},{3,2},{4,5},{5,4},{6,7},{7,6},{8,9},{9,8},{10,11... | collective-permute-start | bytes 294920 | tf_op jit(solution)/shard_map/ppermute | solution.py:251
  23.1 1.8 %collective-permute-start.9 = (bf16[512,384]{1,0:T(8,128)(2,1)S(1)}, bf16[512,384]{1,0:T(8,128)(2,1)S(1)}, u32[]{:S(2)}, u32[]{:S(2)}) collective-permute-start(bf16[512,384]{1,0:T(8,128)(2,1)S(1)} %get-tuple-element.20.refs_2_), channel_id=1, source_target_pairs={{0,4},{1,5},{2,6},{3,7},{4,0},{5,1},{6,2},{7,3},{8,12},{9,13},{10,... | collective-permute-start | bytes 1179656 | tf_op jit(solution)/shard_map/ppermute | solution.py:251
  24.9 4.6 %collective-permute-start.13 = (f32[512,384]{1,0:T(8,128)S(1)}, f32[512,384]{1,0:T(8,128)S(1)}, u32[]{:S(2)}, u32[]{:S(2)}) collective-permute-start(f32[512,384]{1,0:T(8,128)S(1)} %shard_map.71.refs_1_.refs_0_), channel_id=1, source_target_pairs={{0,4},{1,5},{2,6},{3,7},{4,0},{5,1},{6,2},{7,3},{8,12},{9,13},{10,... | collective-permute-start | bytes 2359304 | tf_op jit(solution)/shard_map/ppermute | solution.py:251
  26.4 1.4 %collective-permute-start.10 = (f32[320,128]{1,0:T(8,128)S(1)}, f32[320,128]{1,0:T(8,128)S(1)}, u32[]{:S(2)}, u32[]{:S(2)}) collective-permute-start(f32[320,128]{1,0:T(8,128)S(1)} %get-tuple-element.23), channel_id=1, source_target_pairs={{0,4},{1,5},{2,6},{3,7},{4,0},{5,1},{6,2},{7,3},{8,12},{9,13},{10,... | collective-permute-start | bytes 491528 | tf_op jit(solution)/shard_map/ppermute | solution.py:251
  27.9 4.8 %collective-permute-start.11 = (f32[160,128]{1,0:T(8,128)S(1)}, f32[160,128]{1,0:T(8,128)S(1)}, u32[]{:S(2)}, u32[]{:S(2)}) collective-permute-start(f32[160,128]{1,0:T(8,128)S(1)} %get-tuple-element.25), channel_id=1, source_target_pairs={{0,16},{1,17},{2,18},{3,19},{4,20},{5,21},{6,22},{7,23},{8,24},{9,... | collective-permute-start | bytes 245768 | tf_op jit(solution)/shard_map/ppermute | solution.py:251
  29.5 27.0 %copy-start = (s32[2,1]{0,1:T(1,128)S(1)}, s32[2,1]{0,1:T(1,128)}, u32[]{:S(2)}) copy-start(s32[2,1]{0,1:T(1,128)} %param.7) | copy-start | bytes 28
  29.7 7.9 %collective-permute-start.14 = (bf16[128,384]{1,0:T(8,128)(2,1)S(1)}, bf16[128,384]{1,0:T(8,128)(2,1)S(1)}, u32[]{:S(2)}, u32[]{:S(2)}) collective-permute-start(bf16[128,384]{1,0:T(8,128)(2,1)S(1)} %get-tuple-element.26), channel_id=1, source_target_pairs={{0,0},{1,4},{2,8},{3,12},{4,1},{5,5},{6,9},{7,13},{8,2},{9,6},{10,... | collective-permute-start | bytes 294920 | tf_op jit(solution)/shard_map/ppermute | solution.py:311
  32.7 4.8 %collective-permute-start.12 = (f32[160,128]{1,0:T(8,128)S(1)}, f32[160,128]{1,0:T(8,128)S(1)}, u32[]{:S(2)}, u32[]{:S(2)}) collective-permute-start(f32[160,128]{1,0:T(8,128)S(1)} %shard_map.74.refs_0_), channel_id=1, source_target_pairs={{0,1},{1,0},{2,3},{3,2},{4,6},{5,7},{6,4},{7,5},{8,9},{9,8},{10,11... | collective-permute-start | bytes 245768 | tf_op jit(solution)/shard_map/ppermute | solution.py:254
  34.2 8.0 %collective-permute-start.16 = (bf16[128,384]{1,0:T(8,128)(2,1)S(1)}, bf16[128,384]{1,0:T(8,128)(2,1)S(1)}, u32[]{:S(2)}, u32[]{:S(2)}) collective-permute-start(bf16[128,384]{1,0:T(8,128)(2,1)S(1)} %get-tuple-element.27), channel_id=1, source_target_pairs={{0,2},{1,6},{2,10},{3,14},{4,3},{5,7},{6,11},{7,15},{8,0},{9,4},{1... | collective-permute-start | bytes 294920 | tf_op jit(solution)/shard_map/ppermute | solution.py:311
  37.5 7.1 %collective-permute-start.15 = (f32[160,128]{1,0:T(8,128)S(1)}, f32[160,128]{1,0:T(8,128)S(1)}, u32[]{:S(2)}, u32[]{:S(2)}) collective-permute-start(f32[160,128]{1,0:T(8,128)S(1)} %shard_map.76.refs_0_), channel_id=1, source_target_pairs={{0,2},{1,3},{2,0},{3,1},{4,5},{5,4},{6,7},{7,6},{8,10},{9,11},{10,... | collective-permute-start | bytes 245768 | tf_op jit(solution)/shard_map/ppermute | solution.py:254
  44.7 7.2 %collective-permute-start.19 = (f32[160,128]{1,0:T(8,128)S(1)}, f32[160,128]{1,0:T(8,128)S(1)}, u32[]{:S(2)}, u32[]{:S(2)}) collective-permute-start(f32[160,128]{1,0:T(8,128)S(1)} %shard_map.77.refs_0_), channel_id=1, source_target_pairs={{0,24},{1,25},{2,26},{3,27},{4,28},{5,29},{6,30},{7,31},{8,16},{9,... | collective-permute-start | bytes 245768 | tf_op jit(solution)/shard_map/ppermute | solution.py:251
  49.2 4.4 %collective-permute-start.18 = (f32[160,128]{1,0:T(8,128)S(1)}, f32[160,128]{1,0:T(8,128)S(1)}, u32[]{:S(2)}, u32[]{:S(2)}) collective-permute-start(f32[160,128]{1,0:T(8,128)S(1)} %shard_map.77.refs_0_), channel_id=1, source_target_pairs={{0,16},{1,17},{2,18},{3,19},{4,20},{5,21},{6,22},{7,23},{8,24},{9,... | collective-permute-start | bytes 245768 | tf_op jit(solution)/shard_map/ppermute | solution.py:251
  50.7 4.4 %collective-permute-start.17 = (f32[160,128]{1,0:T(8,128)S(1)}, f32[160,128]{1,0:T(8,128)S(1)}, u32[]{:S(2)}, u32[]{:S(2)}) collective-permute-start(f32[160,128]{1,0:T(8,128)S(1)} %shard_map.77.refs_0_), channel_id=1, source_target_pairs={{0,8},{1,9},{2,10},{3,11},{4,12},{5,13},{6,14},{7,15},{8,0},{9,1},... | collective-permute-start | bytes 245768 | tf_op jit(solution)/shard_map/ppermute | solution.py:251
  50.7 4.4 %collective-permute-start.20 = (f32[160,128]{1,0:T(8,128)S(1)}, f32[160,128]{1,0:T(8,128)S(1)}, u32[]{:S(2)}, u32[]{:S(2)}) collective-permute-start(f32[160,128]{1,0:T(8,128)S(1)} %shard_map.77.refs_0_), channel_id=1, source_target_pairs={{0,4},{1,5},{2,6},{3,7},{4,0},{5,1},{6,2},{7,3},{8,12},{9,13},{10,... | collective-permute-start | bytes 245768 | tf_op jit(solution)/shard_map/ppermute | solution.py:251
  51.8 3.3 %collective-permute-start.23 = (f32[160,128]{1,0:T(8,128)S(1)}, f32[160,128]{1,0:T(8,128)S(1)}, u32[]{:S(2)}, u32[]{:S(2)}) collective-permute-start(f32[160,128]{1,0:T(8,128)S(1)} %collective-permute-done.19.refs_3_), channel_id=1, source_target_pairs={{0,4},{1,5},{2,6},{3,7},{4,0},{5,1},{6,2},{7,3},{8,12},{9,13},{10,... | collective-permute-start | bytes 245768 | tf_op jit(solution)/shard_map/ppermute | solution.py:251
  53.6 1.5 %collective-permute-start.22 = (f32[160,128]{1,0:T(8,128)S(1)}, f32[160,128]{1,0:T(8,128)S(1)}, u32[]{:S(2)}, u32[]{:S(2)}) collective-permute-start(f32[160,128]{1,0:T(8,128)S(1)} %collective-permute-done.18.refs_2_), channel_id=1, source_target_pairs={{0,4},{1,5},{2,6},{3,7},{4,0},{5,1},{6,2},{7,3},{8,12},{9,13},{10,... | collective-permute-start | bytes 245768 | tf_op jit(solution)/shard_map/ppermute | solution.py:251
  55.2 1.3 %collective-permute-start.21 = (f32[160,128]{1,0:T(8,128)S(1)}, f32[160,128]{1,0:T(8,128)S(1)}, u32[]{:S(2)}, u32[]{:S(2)}) collective-permute-start(f32[160,128]{1,0:T(8,128)S(1)} %collective-permute-done.17.refs_1_), channel_id=1, source_target_pairs={{0,4},{1,5},{2,6},{3,7},{4,0},{5,1},{6,2},{7,3},{8,12},{9,13},{10,... | collective-permute-start | bytes 245768 | tf_op jit(solution)/shard_map/ppermute | solution.py:251

commit v14 on v11

--- a/solution.py
+++ b/solution.py
@@ -158,7 +158,7 @@
     del value, out
 
 
-def couple_kernel(weight, applied, pack, got_pack, own_inverse, got_inverse, keep, send, packed):
+def couple_kernel(applied, pack, got_pack, own_inverse, got_inverse, keep, send, packed):
     core, column = lax.axis_index("core"), lax.axis_index("pcol")
     high = applied[...].astype(jnp.bfloat16)
     low = (applied[...] - high.astype(jnp.float32)).astype(jnp.bfloat16)
@@ -171,7 +171,7 @@
         for lines in (own_inverse, got_inverse):
             total += transposed_dot(lines[:, left], lines[:, right])
         for index in range(BLOCKS - first):
-            blocks[first, first + index] = weight[0] * total[:, index * LANES : (index + 1) * LANES]
+            blocks[first, first + index] = total[:, index * LANES : (index + 1) * LANES]
     held = [blocks[place] for place in ABOVE]
     held += hold_diagonal(*(blocks[i, i] for i in range(BLOCKS)))
     for index, block in enumerate(held):
@@ -181,8 +181,8 @@
     send[...] = packed[pl.ds(pl.multiple_of((1 - core) * size, 8), size), :]
 
 
-def halve_kernel(mine, came, keep, send, whole):
-    whole[...] = mine[...] + came[...]
+def halve_kernel(weight, mine, came, keep, send, whole):
+    whole[...] = weight[0] * (mine[...] + came[...])
     size, point = keep.shape[0], lax.axis_index("hyp")
     keep[...] = whole[pl.ds(pl.multiple_of(point * size, 8), size), :]
     send[...] = whole[pl.ds(pl.multiple_of((1 - point) * size, 8), size), :]
@@ -212,25 +212,29 @@
         slot = 1 - point if index // 2 % 2 else point
         start = pl.multiple_of((owner * 2 + slot) * size, 8)
         lines[node, pl.ds(start, size), :] = part[...]
-    copies = []
-    for node in range(2):
-        held = [lines[node, index * LANES : (index + 1) * LANES, :] for index in range(HELD)]
-        places = [slice(index * LANES, (index + 1) * LANES) for index in range(BLOCKS)]
-        for (a, b), tile in zip(ABOVE, held):
-            result[node, places[a], places[b]] = tile
-            result[node, places[b], places[a]] = tile.T
-        for place, tile in zip(places, restore_diagonal(*held[len(ABOVE) :])):
-            result[node, place, place] = tile
-        copies.append(pltpu.make_async_copy(result.at[node], out.at[node], sems.at[1 + node]))
-        copies[-1].start()
     load.wait()
     row = lax.broadcasted_iota(jnp.int32, near.shape, 0)
     first = lax.axis_index("pcol") // 2 == 0
     pair = (jnp.where(first, near[...], far[...]), jnp.where(first, far[...], near[...]))
     for s, value in enumerate(pair):
         block[:, s, :] = jnp.where(row < live[s], value, jnp.zeros(value.shape, value.dtype))
-    copies.append(pltpu.make_async_copy(block, rows_out.at[0], sems.at[3]))
-    copies[-1].start()
+    copies = [pltpu.make_async_copy(block, rows_out.at[0], sems.at[1])]
+    copies[0].start()
+    places = [slice(index * LANES, (index + 1) * LANES) for index in range(BLOCKS)]
+    for node in range(2):
+        held = [lines[node, index * LANES : (index + 1) * LANES, :] for index in range(HELD)]
+        diagonal = restore_diagonal(*held[len(ABOVE) :])
+        for a, rows in enumerate(places):
+            result[node, rows, rows] = diagonal[a]
+            for place, tile in zip(ABOVE, held):
+                if place[0] == a:
+                    result[node, rows, places[place[1]]] = tile
+                elif place[1] == a:
+                    result[node, rows, places[place[0]]] = tile.T
+            copies.append(
+                pltpu.make_async_copy(result.at[node, rows], out.at[node, rows], sems.at[len(copies) + 1])
+            )
+            copies[-1].start()
     for copy in copies:
         copy.wait()
 
@@ -291,12 +295,12 @@
     )
     other = swap(mine, core=1)
     keep, send = call(
-        couple_kernel, [half, half], [SMEM] + [VMEM] * 5,
-        quad_weight, mine, pack, got_pack, own_inverse, got_inverse,
+        couple_kernel, [half, half], [VMEM] * 5,
+        mine, pack, got_pack, own_inverse, got_inverse,
         scratch=[pltpu.VMEM((2 * lines, LANES), f32)],
     )
     keep, send = call(
-        halve_kernel, [part, part], [VMEM] * 2, keep, swap(send, core=1),
+        halve_kernel, [part, part], [SMEM] + [VMEM] * 2, quad_weight, keep, swap(send, core=1),
         scratch=[pltpu.VMEM((lines, LANES), f32)],
     )
     came = swap(send, point=1)
@@ -316,9 +320,10 @@
     )
     near, far = deliver(out_near, 0), deliver(out_far, 1)
     total = add(total, swap(total, column=2))
-    total = add(total, swap(total, column=1), after=[near, far])
+    total = add(total, swap(total, column=1), after=[near])
     quarters = [total, swap(total, side=1), swap(total, point=1), swap(total, side=1, point=1)]
-    quarters += [swap(x, core=1) for x in quarters]
+    held = call(hold_kernel, shape(total.shape, f32), [ANY], total, out_specs=ANY, after=[far], alias={0: 0})
+    quarters += [swap(x, core=1) for x in [held] + quarters[1:]]
     return call(
         finish_kernel,
         [shape((1, height, count, width), bf16), shape((count, width, width), f32)],
@@ -329,7 +334,7 @@
             pltpu.VMEM((height, count, width), bf16),
             pltpu.VMEM((count, 2 * lines, LANES), f32),
             pltpu.VMEM((count, width, width), f32),
-            dma((4,)),
+            dma((8,)),
         ],
         out_specs=[HBM, HBM],
     )

time: 57.6 us -> 55.9 us (0.970)
  waiting for transfers between devices: 20.8 us -> 19.6 us
  starting transfers between devices: 30.2 us -> 29.4 us
    ppermute x22, waiting for transfers between devices: 20.8 us -> 19.6 us  [swap(): return lax.ppermute(x, AXES, [(i, i ^ mask) for i in range(devices)])]
    pallas_call x11 -> x12, Pallas kernels: 5.02 us -> 5.37 us  [call(): pl.pallas_call(body, out_shape=outs, in_specs=list(specs) + [ANY] * len(a...]
  transfers between devices with their start and end apart: 24 -> 24, of which waited for: 14 -> 15; matrix products, arithmetic and copies ran while one was open for 0% -> 0% of each run, Pallas kernels for 3% -> 3%
where the time goes in v14:
time: 55.9 us; the launch traced here: 55.8 us
  starting transfers between devices  29.4 us (53%)
  waiting for transfers between devices  19.6 us (35%)
  Pallas kernels  5.37 us (10%)
  between operations  1.39 us (2%)
    ppermute x22, starting transfers between devices, swap(): return lax.ppermute(x, AXES, [(i, i ^ mask) for i in range(devices)])  25.4 us
    ppermute x22, waiting for transfers between devices, swap(): return lax.ppermute(x, AXES, [(i, i ^ mask) for i in range(devices)])  19.6 us
    pallas_call x12, Pallas kernels, call(): pl.pallas_call(body, out_shape=outs, in_specs=list(specs) + [ANY] * len(a...  5.37 us
    ppermute x2, starting transfers between devices, deliver(): return lax.ppermute(x, AXES, pairs)  4.05 us
  transfers between devices with their start and end apart: 24, of which 15 were waited for; matrix products, arithmetic and copies ran while one was open for 0% of the time, Pallas kernels for 3%

profile of v14, /device:TPU:0, one launch (start us, length us, event | category | flops | bytes accessed | tf_op | source)
XLA Modules:
  0.0 55.8 jit_solution(6761684652048766112)
XLA Ops:
  0.6 1.7 %shard_map.68 = (bf16[128,384]{1,0:T(8,128)(2,1)S(1)}, bf16[160,384]{1,0:T(8,128)(2,1)S(1)}, bf16[32,384]{1,0:T(8,128)(2,1)S(1)}, bf16[256,512]{1,0:T(8,128)(2,1)S(1)}, bf16[256,512]{1,0:T(8,128)(2,1)S(1)}) custom-call(s32[2]{0:T(128)} %bitcast.1, bf16[1,128,2,384]{3,2,1,0:T(2,128)(2,1)} %refs_1_.1, bf16[1,2,24,384]{3,2,1,0:T(8,128)(2,1)} %refs_2_.1, ...), custom_call_target="tpu_custom_call" | custom-call | tf_op jit(solution)/shard_map/pallas_call | solution.py:28
  2.3 3.0 %collective-permute-start.3 = (bf16[160,384]{1,0:T(8,128)(2,1)S(1)}, bf16[160,384]{1,0:T(8,128)(2,1)S(1)}, u32[]{:S(2)}, u32[]{:S(2)}) collective-permute-start(bf16[160,384]{1,0:T(8,128)(2,1)S(1)} %get-tuple-element.16), channel_id=1, source_target_pairs={{0,8},{1,9},{2,10},{3,11},{4,12},{5,13},{6,14},{7,15},{8,0},{9,1},... | collective-permute-start | bytes 368648 | tf_op jit(solution)/shard_map/ppermute | solution.py:255
  5.4 1.9 %collective-permute-start.8 = (bf16[256,512]{1,0:T(8,128)(2,1)S(1)}, bf16[256,512]{1,0:T(8,128)(2,1)S(1)}, u32[]{:S(2)}, u32[]{:S(2)}) collective-permute-start(bf16[256,512]{1,0:T(8,128)(2,1)S(1)} %get-tuple-element.18.refs_2_), channel_id=1, source_target_pairs={{0,8},{1,9},{2,10},{3,11},{4,12},{5,13},{6,14},{7,15},{8,0},{9,1},... | collective-permute-start | bytes 786440 | tf_op jit(solution)/shard_map/ppermute | solution.py:255
  7.4 2.6 %collective-permute-start = (bf16[128,384]{1,0:T(8,128)(2,1)S(1)}, bf16[128,384]{1,0:T(8,128)(2,1)S(1)}, u32[]{:S(2)}, u32[]{:S(2)}) collective-permute-start(bf16[128,384]{1,0:T(8,128)(2,1)S(1)} %get-tuple-element.15.refs_0_), channel_id=1, source_target_pairs={{0,2},{1,3},{2,0},{3,1},{4,6},{5,7},{6,4},{7,5},{8,10},{9,11},{10,... | collective-permute-start | bytes 294920 | tf_op jit(solution)/shard_map/ppermute | solution.py:255
  10.0 1.6 %collective-permute-start.1 = (bf16[128,384]{1,0:T(8,128)(2,1)S(1)}, bf16[128,384]{1,0:T(8,128)(2,1)S(1)}, u32[]{:S(2)}, u32[]{:S(2)}) collective-permute-start(bf16[128,384]{1,0:T(8,128)(2,1)S(1)} %get-tuple-element.15.refs_0_), channel_id=1, source_target_pairs={{0,1},{1,0},{2,3},{3,2},{4,5},{5,4},{6,7},{7,6},{8,9},{9,8},{10,11... | collective-permute-start | bytes 294920 | tf_op jit(solution)/shard_map/ppermute | solution.py:255
  11.6 1.2 %collective-permute-start.4 = (bf16[128,384]{1,0:T(8,128)(2,1)S(1)}, bf16[128,384]{1,0:T(8,128)(2,1)S(1)}, u32[]{:S(2)}, u32[]{:S(2)}) collective-permute-start(bf16[128,384]{1,0:T(8,128)(2,1)S(1)} %slice.8.refs_4_), channel_id=1, source_target_pairs={{0,2},{1,3},{2,0},{3,1},{4,6},{5,7},{6,4},{7,5},{8,10},{9,11},{10,... | collective-permute-start | bytes 294920 | tf_op jit(solution)/shard_map/ppermute | solution.py:255
  13.1 3.8 %collective-permute-start.2 = (bf16[128,384]{1,0:T(8,128)(2,1)S(1)}, bf16[128,384]{1,0:T(8,128)(2,1)S(1)}, u32[]{:S(2)}, u32[]{:S(2)}) collective-permute-start(bf16[128,384]{1,0:T(8,128)(2,1)S(1)} %collective-permute-done.refs_1_), channel_id=1, source_target_pairs={{0,1},{1,0},{2,3},{3,2},{4,5},{5,4},{6,7},{7,6},{8,9},{9,8},{10,11... | collective-permute-start | bytes 294920 | tf_op jit(solution)/shard_map/ppermute | solution.py:255
  17.0 0.7 %collective-permute-start.5 = (bf16[128,384]{1,0:T(8,128)(2,1)S(1)}, bf16[128,384]{1,0:T(8,128)(2,1)S(1)}, u32[]{:S(2)}, u32[]{:S(2)}) collective-permute-start(bf16[128,384]{1,0:T(8,128)(2,1)S(1)} %slice.8.refs_4_), channel_id=1, source_target_pairs={{0,1},{1,0},{2,3},{3,2},{4,5},{5,4},{6,7},{7,6},{8,9},{9,8},{10,11... | collective-permute-start | bytes 294920 | tf_op jit(solution)/shard_map/ppermute | solution.py:255
  17.7 0.6 %collective-permute-done.4.refs_5_ = bf16[128,384]{1,0:T(8,128)(2,1)S(1)} collective-permute-done((bf16[128,384]{1,0:T(8,128)(2,1)S(1)}, bf16[128,384]{1,0:T(8,128)(2,1)S(1)}, u32[]{:S(2)}, u32[]{:S(2)}) %collective-permute-start.4) | collective-permute-done | bytes 98336 | tf_op jit(solution)/shard_map/ppermute | solution.py:255
  18.3 0.7 %collective-permute-start.6 = (bf16[128,384]{1,0:T(8,128)(2,1)S(1)}, bf16[128,384]{1,0:T(8,128)(2,1)S(1)}, u32[]{:S(2)}, u32[]{:S(2)}) collective-permute-start(bf16[128,384]{1,0:T(8,128)(2,1)S(1)} %collective-permute-done.4.refs_5_), channel_id=1, source_target_pairs={{0,1},{1,0},{2,3},{3,2},{4,5},{5,4},{6,7},{7,6},{8,9},{9,8},{10,11... | collective-permute-start | bytes 294920 | tf_op jit(solution)/shard_map/ppermute | solution.py:255
  19.0 1.6 %collective-permute-done.2.refs_3_ = bf16[128,384]{1,0:T(8,128)(2,1)S(1)} collective-permute-done((bf16[128,384]{1,0:T(8,128)(2,1)S(1)}, bf16[128,384]{1,0:T(8,128)(2,1)S(1)}, u32[]{:S(2)}, u32[]{:S(2)}) %collective-permute-start.2) | collective-permute-done | bytes 98336 | tf_op jit(solution)/shard_map/ppermute | solution.py:255
  20.7 1.3 %collective-permute-done.5.refs_6_ = bf16[128,384]{1,0:T(8,128)(2,1)S(1)} collective-permute-done((bf16[128,384]{1,0:T(8,128)(2,1)S(1)}, bf16[128,384]{1,0:T(8,128)(2,1)S(1)}, u32[]{:S(2)}, u32[]{:S(2)}) %collective-permute-start.5) | collective-permute-done | bytes 98336 | tf_op jit(solution)/shard_map/ppermute | solution.py:255
  22.0 1.0 %collective-permute-done.6.refs_7_ = bf16[128,384]{1,0:T(8,128)(2,1)S(1)} collective-permute-done((bf16[128,384]{1,0:T(8,128)(2,1)S(1)}, bf16[128,384]{1,0:T(8,128)(2,1)S(1)}, u32[]{:S(2)}, u32[]{:S(2)}) %collective-permute-start.6) | collective-permute-done | bytes 98336 | tf_op jit(solution)/shard_map/ppermute | solution.py:255
  23.2 0.7 %shard_map.70.refs_0_ = f32[512,384]{1,0:T(8,128)S(1)} custom-call(bf16[2,512,384]{2,1,0:T(8,128)(2,1)S(1)} %get-tuple-element.19.refs_0_, bf16[256,512]{1,0:T(8,128)(2,1)S(1)} %get-tuple-element.17.refs_1_, bf16[256,512]{1,0:T(8,128)(2,1)S(1)} %get-tuple-element.18.refs_2_, bf16[256,512]{1,0:T(8,128)(2,1)S(1)} %collective-permute-done.7.refs_8_.refs_3_, ...), custom_call_target="tpu_custom_call" | custom-call | tf_op jit(solution)/shard_map/pallas_call | solution.py:28
  23.9 1.0 %collective-permute-done.9.refs_1_.refs_2_ = bf16[512,384]{1,0:T(8,128)(2,1)S(1)} collective-permute-done((bf16[512,384]{1,0:T(8,128)(2,1)S(1)}, bf16[512,384]{1,0:T(8,128)(2,1)S(1)}, u32[]{:S(2)}, u32[]{:S(2)}) %collective-permute-start.9) | collective-permute-done | bytes 393248 | tf_op jit(solution)/shard_map/ppermute | solution.py:255
  25.1 0.7 %shard_map.72 = (f32[320,128]{1,0:T(8,128)S(1)}, f32[320,128]{1,0:T(8,128)S(1)}) custom-call(f32[512,384]{1,0:T(8,128)S(1)} %shard_map.71.refs_0_, bf16[512,384]{1,0:T(8,128)(2,1)S(1)} %get-tuple-element.20.refs_1_, bf16[512,384]{1,0:T(8,128)(2,1)S(1)} %collective-permute-done.9.refs_1_.refs_2_, bf16[32,384]{1,0:T(8,128)(2,1)S(1)} %get-tuple-element.21.refs_3_, ...), custom_call_target="tpu_custom_call" | custom-call | tf_op jit(solution)/shard_map/pallas_call | solution.py:28
  26.8 0.6 %collective-permute-done.10.refs_2_ = f32[320,128]{1,0:T(8,128)S(1)} collective-permute-done((f32[320,128]{1,0:T(8,128)S(1)}, f32[320,128]{1,0:T(8,128)S(1)}, u32[]{:S(2)}, u32[]{:S(2)}) %collective-permute-start.10) | collective-permute-done | bytes 163872 | tf_op jit(solution)/shard_map/ppermute | solution.py:255
  27.5 1.6 %collective-permute-start.11 = (f32[160,128]{1,0:T(8,128)S(1)}, f32[160,128]{1,0:T(8,128)S(1)}, u32[]{:S(2)}, u32[]{:S(2)}) collective-permute-start(f32[160,128]{1,0:T(8,128)S(1)} %get-tuple-element.25), channel_id=1, source_target_pairs={{0,16},{1,17},{2,18},{3,19},{4,20},{5,21},{6,22},{7,23},{8,24},{9,... | collective-permute-start | bytes 245768 | tf_op jit(solution)/shard_map/ppermute | solution.py:255
  29.1 3.0 %collective-permute-done.11.refs_1_ = f32[160,128]{1,0:T(8,128)S(1)} collective-permute-done((f32[160,128]{1,0:T(8,128)S(1)}, f32[160,128]{1,0:T(8,128)S(1)}, u32[]{:S(2)}, u32[]{:S(2)}) %collective-permute-start.11) | collective-permute-done | bytes 81952 | tf_op jit(solution)/shard_map/ppermute | solution.py:255
  32.0 3.2 %collective-permute-start.12 = (f32[160,128]{1,0:T(8,128)S(1)}, f32[160,128]{1,0:T(8,128)S(1)}, u32[]{:S(2)}, u32[]{:S(2)}) collective-permute-start(f32[160,128]{1,0:T(8,128)S(1)} %shard_map.74.refs_0_.refs_2_), channel_id=1, source_target_pairs={{0,2},{1,3},{2,0},{3,1},{4,6},{5,7},{6,4},{7,5},{8,10},{9,11},{10,... | collective-permute-start | bytes 245768 | tf_op jit(solution)/shard_map/ppermute | solution.py:255
  35.5 0.7 %collective-permute-start.15 = (bf16[128,384]{1,0:T(8,128)(2,1)S(1)}, bf16[128,384]{1,0:T(8,128)(2,1)S(1)}, u32[]{:S(2)}, u32[]{:S(2)}) collective-permute-start(bf16[128,384]{1,0:T(8,128)(2,1)S(1)} %get-tuple-element.26), channel_id=1, source_target_pairs={{0,0},{1,4},{2,8},{3,12},{4,1},{5,5},{6,9},{7,13},{8,2},{9,6},{10,... | collective-permute-start | bytes 294920 | tf_op jit(solution)/shard_map/ppermute | solution.py:312
  36.1 2.8 %collective-permute-done.12.refs_1_ = f32[160,128]{1,0:T(8,128)S(1)} collective-permute-done((f32[160,128]{1,0:T(8,128)S(1)}, f32[160,128]{1,0:T(8,128)S(1)}, u32[]{:S(2)}, u32[]{:S(2)}) %collective-permute-start.12) | collective-permute-done | bytes 81952 | tf_op jit(solution)/shard_map/ppermute | solution.py:255
  39.0 0.7 %collective-permute-start.13 = (f32[160,128]{1,0:T(8,128)S(1)}, f32[160,128]{1,0:T(8,128)S(1)}, u32[]{:S(2)}, u32[]{:S(2)}) collective-permute-start(f32[160,128]{1,0:T(8,128)S(1)} %shard_map.75.refs_0_), channel_id=1, source_target_pairs={{0,1},{1,0},{2,3},{3,2},{4,5},{5,4},{6,7},{7,6},{8,9},{9,8},{10,11... | collective-permute-start | bytes 245768 | tf_op jit(solution)/shard_map/ppermute | solution.py:255
  39.6 3.4 %collective-permute-start.19 = (bf16[128,384]{1,0:T(8,128)(2,1)S(1)}, bf16[128,384]{1,0:T(8,128)(2,1)S(1)}, u32[]{:S(2)}, u32[]{:S(2)}) collective-permute-start(bf16[128,384]{1,0:T(8,128)(2,1)S(1)} %get-tuple-element.27), channel_id=1, source_target_pairs={{0,2},{1,6},{2,10},{3,14},{4,3},{5,7},{6,11},{7,15},{8,0},{9,4},{1... | collective-permute-start | bytes 294920 | tf_op jit(solution)/shard_map/ppermute | solution.py:312
  43.0 2.1 %collective-permute-done.13.refs_1_ = f32[160,128]{1,0:T(8,128)S(1)} collective-permute-done((f32[160,128]{1,0:T(8,128)S(1)}, f32[160,128]{1,0:T(8,128)S(1)}, u32[]{:S(2)}, u32[]{:S(2)}) %collective-permute-start.13) | collective-permute-done | bytes 81952 | tf_op jit(solution)/shard_map/ppermute | solution.py:255
  45.2 2.4 %collective-permute-start.18 = (f32[160,128]{1,0:T(8,128)S(1)}, f32[160,128]{1,0:T(8,128)S(1)}, u32[]{:S(2)}, u32[]{:S(2)}) collective-permute-start(f32[160,128]{1,0:T(8,128)S(1)} %shard_map.77.refs_0_), channel_id=1, source_target_pairs={{0,24},{1,25},{2,26},{3,27},{4,28},{5,29},{6,30},{7,31},{8,16},{9,... | collective-permute-start | bytes 245768 | tf_op jit(solution)/shard_map/ppermute | solution.py:255
  47.6 0.5 collective-permute-start.17
  48.1 0.6 %collective-permute-start.16 = (f32[160,128]{1,0:T(8,128)S(1)}, f32[160,128]{1,0:T(8,128)S(1)}, u32[]{:S(2)}, u32[]{:S(2)}) collective-permute-start(f32[160,128]{1,0:T(8,128)S(1)} %shard_map.77.refs_0_), channel_id=1, source_target_pairs={{0,8},{1,9},{2,10},{3,11},{4,12},{5,13},{6,14},{7,15},{8,0},{9,1},... | collective-permute-start | bytes 245768 | tf_op jit(solution)/shard_map/ppermute | solution.py:255
  48.8 2.0 %collective-permute-done.18.refs_3_ = f32[160,128]{1,0:T(8,128)S(1)} collective-permute-done((f32[160,128]{1,0:T(8,128)S(1)}, f32[160,128]{1,0:T(8,128)S(1)}, u32[]{:S(2)}, u32[]{:S(2)}) %collective-permute-start.18) | collective-permute-done | bytes 81952 | tf_op jit(solution)/shard_map/ppermute | solution.py:255
  50.8 1.3 %collective-permute-done.17.refs_2_ = f32[160,128]{1,0:T(8,128)S(1)} collective-permute-done((f32[160,128]{1,0:T(8,128)S(1)}, f32[160,128]{1,0:T(8,128)S(1)}, u32[]{:S(2)}, u32[]{:S(2)}) %collective-permute-start.17) | collective-permute-done | bytes 81952 | tf_op jit(solution)/shard_map/ppermute | solution.py:255
  52.6 0.8 %collective-permute-done.22.refs_6_ = f32[160,128]{1,0:T(8,128)S(1)} collective-permute-done((f32[160,128]{1,0:T(8,128)S(1)}, f32[160,128]{1,0:T(8,128)S(1)}, u32[]{:S(2)}, u32[]{:S(2)}) %collective-permute-start.22) | collective-permute-done | bytes 81952 | tf_op jit(solution)/shard_map/ppermute | solution.py:255
  53.8 1.9 %shard_map.79 = (bf16[1,128,2,384]{3,2,1,0:T(2,128)(2,1)}, f32[2,384,384]{2,1,0:T(8,128)}) custom-call(f32[160,128]{1,0:T(8,128)S(1)} %shard_map.77.refs_0_, f32[160,128]{1,0:T(8,128)S(1)} %collective-permute-done.16.refs_1_, f32[160,128]{1,0:T(8,128)S(1)} %collective-permute-done.17.refs_2_, f32[160,128]{1,0:T(8,128)S(1)} %collective-permute-done.18.refs_3_, ...), custom_call_target="tpu_custom_call" | custom-call | tf_op jit(solution)/shard_map/pallas_call | solution.py:28
  (33 shorter events, 2.6 us)
Async XLA Ops:
  2.3 9.2 %collective-permute-start.3 = (bf16[160,384]{1,0:T(8,128)(2,1)S(1)}, bf16[160,384]{1,0:T(8,128)(2,1)S(1)}, u32[]{:S(2)}, u32[]{:S(2)}) collective-permute-start(bf16[160,384]{1,0:T(8,128)(2,1)S(1)} %get-tuple-element.16), channel_id=1, source_target_pairs={{0,8},{1,9},{2,10},{3,11},{4,12},{5,13},{6,14},{7,15},{8,0},{9,1},... | collective-permute-start | bytes 368648 | tf_op jit(solution)/shard_map/ppermute | solution.py:255
  5.3 16.6 %collective-permute-start.7 = (bf16[256,512]{1,0:T(8,128)(2,1)S(1)}, bf16[256,512]{1,0:T(8,128)(2,1)S(1)}, u32[]{:S(2)}, u32[]{:S(2)}) collective-permute-start(bf16[256,512]{1,0:T(8,128)(2,1)S(1)} %get-tuple-element.17.refs_1_), channel_id=1, source_target_pairs={{0,8},{1,9},{2,10},{3,11},{4,12},{5,13},{6,14},{7,15},{8,0},{9,1},... | collective-permute-start | bytes 786440 | tf_op jit(solution)/shard_map/ppermute | solution.py:255
  5.4 16.5 %collective-permute-start.8 = (bf16[256,512]{1,0:T(8,128)(2,1)S(1)}, bf16[256,512]{1,0:T(8,128)(2,1)S(1)}, u32[]{:S(2)}, u32[]{:S(2)}) collective-permute-start(bf16[256,512]{1,0:T(8,128)(2,1)S(1)} %get-tuple-element.18.refs_2_), channel_id=1, source_target_pairs={{0,8},{1,9},{2,10},{3,11},{4,12},{5,13},{6,14},{7,15},{8,0},{9,1},... | collective-permute-start | bytes 786440 | tf_op jit(solution)/shard_map/ppermute | solution.py:255
  7.4 5.8 %collective-permute-start = (bf16[128,384]{1,0:T(8,128)(2,1)S(1)}, bf16[128,384]{1,0:T(8,128)(2,1)S(1)}, u32[]{:S(2)}, u32[]{:S(2)}) collective-permute-start(bf16[128,384]{1,0:T(8,128)(2,1)S(1)} %get-tuple-element.15.refs_0_), channel_id=1, source_target_pairs={{0,2},{1,3},{2,0},{3,1},{4,6},{5,7},{6,4},{7,5},{8,10},{9,11},{10,... | collective-permute-start | bytes 294920 | tf_op jit(solution)/shard_map/ppermute | solution.py:255
  10.0 7.0 %collective-permute-start.1 = (bf16[128,384]{1,0:T(8,128)(2,1)S(1)}, bf16[128,384]{1,0:T(8,128)(2,1)S(1)}, u32[]{:S(2)}, u32[]{:S(2)}) collective-permute-start(bf16[128,384]{1,0:T(8,128)(2,1)S(1)} %get-tuple-element.15.refs_0_), channel_id=1, source_target_pairs={{0,1},{1,0},{2,3},{3,2},{4,5},{5,4},{6,7},{7,6},{8,9},{9,8},{10,11... | collective-permute-start | bytes 294920 | tf_op jit(solution)/shard_map/ppermute | solution.py:255
  11.6 6.8 %collective-permute-start.4 = (bf16[128,384]{1,0:T(8,128)(2,1)S(1)}, bf16[128,384]{1,0:T(8,128)(2,1)S(1)}, u32[]{:S(2)}, u32[]{:S(2)}) collective-permute-start(bf16[128,384]{1,0:T(8,128)(2,1)S(1)} %slice.8.refs_4_), channel_id=1, source_target_pairs={{0,2},{1,3},{2,0},{3,1},{4,6},{5,7},{6,4},{7,5},{8,10},{9,11},{10,... | collective-permute-start | bytes 294920 | tf_op jit(solution)/shard_map/ppermute | solution.py:255
  13.1 7.6 %collective-permute-start.2 = (bf16[128,384]{1,0:T(8,128)(2,1)S(1)}, bf16[128,384]{1,0:T(8,128)(2,1)S(1)}, u32[]{:S(2)}, u32[]{:S(2)}) collective-permute-start(bf16[128,384]{1,0:T(8,128)(2,1)S(1)} %collective-permute-done.refs_1_), channel_id=1, source_target_pairs={{0,1},{1,0},{2,3},{3,2},{4,5},{5,4},{6,7},{7,6},{8,9},{9,8},{10,11... | collective-permute-start | bytes 294920 | tf_op jit(solution)/shard_map/ppermute | solution.py:255
  17.0 5.0 %collective-permute-start.5 = (bf16[128,384]{1,0:T(8,128)(2,1)S(1)}, bf16[128,384]{1,0:T(8,128)(2,1)S(1)}, u32[]{:S(2)}, u32[]{:S(2)}) collective-permute-start(bf16[128,384]{1,0:T(8,128)(2,1)S(1)} %slice.8.refs_4_), channel_id=1, source_target_pairs={{0,1},{1,0},{2,3},{3,2},{4,5},{5,4},{6,7},{7,6},{8,9},{9,8},{10,11... | collective-permute-start | bytes 294920 | tf_op jit(solution)/shard_map/ppermute | solution.py:255
  18.3 4.7 %collective-permute-start.6 = (bf16[128,384]{1,0:T(8,128)(2,1)S(1)}, bf16[128,384]{1,0:T(8,128)(2,1)S(1)}, u32[]{:S(2)}, u32[]{:S(2)}) collective-permute-start(bf16[128,384]{1,0:T(8,128)(2,1)S(1)} %collective-permute-done.4.refs_5_), channel_id=1, source_target_pairs={{0,1},{1,0},{2,3},{3,2},{4,5},{5,4},{6,7},{7,6},{8,9},{9,8},{10,11... | collective-permute-start | bytes 294920 | tf_op jit(solution)/shard_map/ppermute | solution.py:255
  23.1 1.8 %collective-permute-start.9 = (bf16[512,384]{1,0:T(8,128)(2,1)S(1)}, bf16[512,384]{1,0:T(8,128)(2,1)S(1)}, u32[]{:S(2)}, u32[]{:S(2)}) collective-permute-start(bf16[512,384]{1,0:T(8,128)(2,1)S(1)} %get-tuple-element.20.refs_1_), channel_id=1, source_target_pairs={{0,4},{1,5},{2,6},{3,7},{4,0},{5,1},{6,2},{7,3},{8,12},{9,13},{10,... | collective-permute-start | bytes 1179656 | tf_op jit(solution)/shard_map/ppermute | solution.py:255
  24.9 10.4 %collective-permute-start.14 = (f32[512,384]{1,0:T(8,128)S(1)}, f32[512,384]{1,0:T(8,128)S(1)}, u32[]{:S(2)}, u32[]{:S(2)}) collective-permute-start(f32[512,384]{1,0:T(8,128)S(1)} %shard_map.71.refs_0_), channel_id=1, source_target_pairs={{0,4},{1,5},{2,6},{3,7},{4,0},{5,1},{6,2},{7,3},{8,12},{9,13},{10,... | collective-permute-start | bytes 2359304 | tf_op jit(solution)/shard_map/ppermute | solution.py:255
  25.8 1.7 %collective-permute-start.10 = (f32[320,128]{1,0:T(8,128)S(1)}, f32[320,128]{1,0:T(8,128)S(1)}, u32[]{:S(2)}, u32[]{:S(2)}) collective-permute-start(f32[320,128]{1,0:T(8,128)S(1)} %get-tuple-element.23), channel_id=1, source_target_pairs={{0,4},{1,5},{2,6},{3,7},{4,0},{5,1},{6,2},{7,3},{8,12},{9,13},{10,... | collective-permute-start | bytes 491528 | tf_op jit(solution)/shard_map/ppermute | solution.py:255
  27.5 4.6 %collective-permute-start.11 = (f32[160,128]{1,0:T(8,128)S(1)}, f32[160,128]{1,0:T(8,128)S(1)}, u32[]{:S(2)}, u32[]{:S(2)}) collective-permute-start(f32[160,128]{1,0:T(8,128)S(1)} %get-tuple-element.25), channel_id=1, source_target_pairs={{0,16},{1,17},{2,18},{3,19},{4,20},{5,21},{6,22},{7,23},{8,24},{9,... | collective-permute-start | bytes 245768 | tf_op jit(solution)/shard_map/ppermute | solution.py:255
  32.0 21.8 %copy-start = (s32[2,1]{0,1:T(1,128)S(1)}, s32[2,1]{0,1:T(1,128)}, u32[]{:S(2)}) copy-start(s32[2,1]{0,1:T(1,128)} %param.7) | copy-start | bytes 28
  32.0 6.9 %collective-permute-start.12 = (f32[160,128]{1,0:T(8,128)S(1)}, f32[160,128]{1,0:T(8,128)S(1)}, u32[]{:S(2)}, u32[]{:S(2)}) collective-permute-start(f32[160,128]{1,0:T(8,128)S(1)} %shard_map.74.refs_0_.refs_2_), channel_id=1, source_target_pairs={{0,2},{1,3},{2,0},{3,1},{4,6},{5,7},{6,4},{7,5},{8,10},{9,11},{10,... | collective-permute-start | bytes 245768 | tf_op jit(solution)/shard_map/ppermute | solution.py:255
  35.5 9.7 %collective-permute-start.15 = (bf16[128,384]{1,0:T(8,128)(2,1)S(1)}, bf16[128,384]{1,0:T(8,128)(2,1)S(1)}, u32[]{:S(2)}, u32[]{:S(2)}) collective-permute-start(bf16[128,384]{1,0:T(8,128)(2,1)S(1)} %get-tuple-element.26), channel_id=1, source_target_pairs={{0,0},{1,4},{2,8},{3,12},{4,1},{5,5},{6,9},{7,13},{8,2},{9,6},{10,... | collective-permute-start | bytes 294920 | tf_op jit(solution)/shard_map/ppermute | solution.py:312
  39.0 6.2 %collective-permute-start.13 = (f32[160,128]{1,0:T(8,128)S(1)}, f32[160,128]{1,0:T(8,128)S(1)}, u32[]{:S(2)}, u32[]{:S(2)}) collective-permute-start(f32[160,128]{1,0:T(8,128)S(1)} %shard_map.75.refs_0_), channel_id=1, source_target_pairs={{0,1},{1,0},{2,3},{3,2},{4,5},{5,4},{6,7},{7,6},{8,9},{9,8},{10,11... | collective-permute-start | bytes 245768 | tf_op jit(solution)/shard_map/ppermute | solution.py:255
  39.6 9.1 %collective-permute-start.19 = (bf16[128,384]{1,0:T(8,128)(2,1)S(1)}, bf16[128,384]{1,0:T(8,128)(2,1)S(1)}, u32[]{:S(2)}, u32[]{:S(2)}) collective-permute-start(bf16[128,384]{1,0:T(8,128)(2,1)S(1)} %get-tuple-element.27), channel_id=1, source_target_pairs={{0,2},{1,6},{2,10},{3,14},{4,3},{5,7},{6,11},{7,15},{8,0},{9,4},{1... | collective-permute-start | bytes 294920 | tf_op jit(solution)/shard_map/ppermute | solution.py:312
  45.2 5.6 %collective-permute-start.18 = (f32[160,128]{1,0:T(8,128)S(1)}, f32[160,128]{1,0:T(8,128)S(1)}, u32[]{:S(2)}, u32[]{:S(2)}) collective-permute-start(f32[160,128]{1,0:T(8,128)S(1)} %shard_map.77.refs_0_), channel_id=1, source_target_pairs={{0,24},{1,25},{2,26},{3,27},{4,28},{5,29},{6,30},{7,31},{8,16},{9,... | collective-permute-start | bytes 245768 | tf_op jit(solution)/shard_map/ppermute | solution.py:255
  47.6 4.4 %collective-permute-start.17 = (f32[160,128]{1,0:T(8,128)S(1)}, f32[160,128]{1,0:T(8,128)S(1)}, u32[]{:S(2)}, u32[]{:S(2)}) collective-permute-start(f32[160,128]{1,0:T(8,128)S(1)} %shard_map.77.refs_0_), channel_id=1, source_target_pairs={{0,16},{1,17},{2,18},{3,19},{4,20},{5,21},{6,22},{7,23},{8,24},{9,... | collective-permute-start | bytes 245768 | tf_op jit(solution)/shard_map/ppermute | solution.py:255
  48.1 4.4 %collective-permute-start.16 = (f32[160,128]{1,0:T(8,128)S(1)}, f32[160,128]{1,0:T(8,128)S(1)}, u32[]{:S(2)}, u32[]{:S(2)}) collective-permute-start(f32[160,128]{1,0:T(8,128)S(1)} %shard_map.77.refs_0_), channel_id=1, source_target_pairs={{0,8},{1,9},{2,10},{3,11},{4,12},{5,13},{6,14},{7,15},{8,0},{9,1},... | collective-permute-start | bytes 245768 | tf_op jit(solution)/shard_map/ppermute | solution.py:255
  48.8 3.8 %collective-permute-start.20 = (f32[160,128]{1,0:T(8,128)S(1)}, f32[160,128]{1,0:T(8,128)S(1)}, u32[]{:S(2)}, u32[]{:S(2)}) collective-permute-start(f32[160,128]{1,0:T(8,128)S(1)} %shard_map.78), channel_id=1, source_target_pairs={{0,4},{1,5},{2,6},{3,7},{4,0},{5,1},{6,2},{7,3},{8,12},{9,13},{10,... | collective-permute-start | bytes 245768 | tf_op jit(solution)/shard_map/ppermute | solution.py:255
  50.8 1.8 %collective-permute-start.23 = (f32[160,128]{1,0:T(8,128)S(1)}, f32[160,128]{1,0:T(8,128)S(1)}, u32[]{:S(2)}, u32[]{:S(2)}) collective-permute-start(f32[160,128]{1,0:T(8,128)S(1)} %collective-permute-done.18.refs_3_), channel_id=1, source_target_pairs={{0,4},{1,5},{2,6},{3,7},{4,0},{5,1},{6,2},{7,3},{8,12},{9,13},{10,... | collective-permute-start | bytes 245768 | tf_op jit(solution)/shard_map/ppermute | solution.py:255
  52.1 1.3 %collective-permute-start.22 = (f32[160,128]{1,0:T(8,128)S(1)}, f32[160,128]{1,0:T(8,128)S(1)}, u32[]{:S(2)}, u32[]{:S(2)}) collective-permute-start(f32[160,128]{1,0:T(8,128)S(1)} %collective-permute-done.17.refs_2_), channel_id=1, source_target_pairs={{0,4},{1,5},{2,6},{3,7},{4,0},{5,1},{6,2},{7,3},{8,12},{9,13},{10,... | collective-permute-start | bytes 245768 | tf_op jit(solution)/shard_map/ppermute | solution.py:255
  52.6 1.3 %collective-permute-start.21 = (f32[160,128]{1,0:T(8,128)S(1)}, f32[160,128]{1,0:T(8,128)S(1)}, u32[]{:S(2)}, u32[]{:S(2)}) collective-permute-start(f32[160,128]{1,0:T(8,128)S(1)} %collective-permute-done.16.refs_1_), channel_id=1, source_target_pairs={{0,4},{1,5},{2,6},{3,7},{4,0},{5,1},{6,2},{7,3},{8,12},{9,13},{10,... | collective-permute-start | bytes 245768 | tf_op jit(solution)/shard_map/ppermute | solution.py:255

commit v15 on v14

--- a/solution.py
+++ b/solution.py
@@ -103,7 +103,7 @@
 
 
 def start_kernel(*refs):
-    sources, (own, give, own_inverse), pieces = refs[:4], refs[4:7], refs[7:-5]
+    sources, (own, give, own_inverse, limits), pieces = refs[:4], refs[4:8], refs[8:-5]
     buffers, sems = refs[-5:-1], refs[-1]
     copies = [
         pltpu.make_async_copy(source, buffer, sems.at[index])
@@ -126,6 +126,8 @@
     one, two = (jnp.concatenate([inverse[0, s], spare], 0) for s in range(2))
     own_inverse[...] = jnp.where(first, one, two)
     give[height:] = jnp.where(first, two, one)
+    for s in range(limits.shape[0]):
+        limits[s] = jnp.full(limits.shape[1:], live[s], limits.dtype)
     copies[3].wait()
     at = 0
     for piece in pieces:
@@ -200,11 +202,19 @@
     out[...] = mine[...] + came[...]
 
 
+def rows_kernel(limits, near, far, out):
+    row = lax.broadcasted_iota(jnp.int32, near.shape, 0)
+    first = lax.axis_index("pcol") // 2 == 0
+    pair = (jnp.where(first, near[...], far[...]), jnp.where(first, far[...], near[...]))
+    for s, value in enumerate(pair):
+        out[0, :, s, :] = jnp.where(row < limits[s, :1, :1], value, jnp.zeros(value.shape, value.dtype))
+
+
 def finish_kernel(*refs):
-    parts, (live_hbm, near, far, rows_out, out, live, block, lines, result, sems) = refs[:8], refs[8:]
+    parts, (rows, rows_out, out, lines, result, sems) = refs[:8], refs[8:]
+    copies = [pltpu.make_async_copy(rows, rows_out, sems.at[0])]
+    copies[0].start()
     point, side, core = (lax.axis_index(name) for name in ("hyp", "side", "core"))
-    load = pltpu.make_async_copy(live_hbm, live, sems.at[0])
-    load.start()
     size = parts[0].shape[0]
     for index, part in enumerate(parts):
         owner = core if index < 4 else 1 - core
@@ -212,29 +222,16 @@
         slot = 1 - point if index // 2 % 2 else point
         start = pl.multiple_of((owner * 2 + slot) * size, 8)
         lines[node, pl.ds(start, size), :] = part[...]
-    load.wait()
-    row = lax.broadcasted_iota(jnp.int32, near.shape, 0)
-    first = lax.axis_index("pcol") // 2 == 0
-    pair = (jnp.where(first, near[...], far[...]), jnp.where(first, far[...], near[...]))
-    for s, value in enumerate(pair):
-        block[:, s, :] = jnp.where(row < live[s], value, jnp.zeros(value.shape, value.dtype))
-    copies = [pltpu.make_async_copy(block, rows_out.at[0], sems.at[1])]
-    copies[0].start()
     places = [slice(index * LANES, (index + 1) * LANES) for index in range(BLOCKS)]
     for node in range(2):
         held = [lines[node, index * LANES : (index + 1) * LANES, :] for index in range(HELD)]
-        diagonal = restore_diagonal(*held[len(ABOVE) :])
-        for a, rows in enumerate(places):
-            result[node, rows, rows] = diagonal[a]
-            for place, tile in zip(ABOVE, held):
-                if place[0] == a:
-                    result[node, rows, places[place[1]]] = tile
-                elif place[1] == a:
-                    result[node, rows, places[place[0]]] = tile.T
-            copies.append(
-                pltpu.make_async_copy(result.at[node, rows], out.at[node, rows], sems.at[len(copies) + 1])
-            )
-            copies[-1].start()
+        for (a, b), tile in zip(ABOVE, held):
+            result[node, places[a], places[b]] = tile
+            result[node, places[b], places[a]] = tile.T
+        for place, tile in zip(places, restore_diagonal(*held[len(ABOVE) :])):
+            result[node, place, place] = tile
+        copies.append(pltpu.make_async_copy(result.at[node], out.at[node], sems.at[1 + node]))
+        copies[-1].start()
     for copy in copies:
         copy.wait()
 
@@ -258,9 +255,10 @@
     block = shape((height, width), bf16)
     cuts = (extent // 2, extent // 2)
     size = pl.cdiv(inv_diag.shape[2], ROWS) * ROWS
-    own, give, own_inverse, *pieces = call(
+    own, give, own_inverse, limits, *pieces = call(
         start_kernel,
         [block, shape((height + size, width), bf16), shape((size, width), bf16)]
+        + [shape((count, 8, LANES), jnp.int32)]
         + [shape((lines, extent), bf16) for lines in cuts],
         [HBM] * 4,
         *map(stay, (live, panel, inv_diag, sigma_rows)),
@@ -322,19 +320,20 @@
     total = add(total, swap(total, column=2))
     total = add(total, swap(total, column=1), after=[near])
     quarters = [total, swap(total, side=1), swap(total, point=1), swap(total, side=1, point=1)]
-    held = call(hold_kernel, shape(total.shape, f32), [ANY], total, out_specs=ANY, after=[far], alias={0: 0})
+    rows = call(
+        rows_kernel, shape((1, height, count, width), bf16), [VMEM] * 3, limits, near, far
+    )
+    held = call(hold_kernel, shape(total.shape, f32), [ANY], total, out_specs=ANY, after=[rows], alias={0: 0})
     quarters += [swap(x, core=1) for x in [held] + quarters[1:]]
     return call(
         finish_kernel,
         [shape((1, height, count, width), bf16), shape((count, width, width), f32)],
-        [VMEM] * 8 + [HBM] + [VMEM] * 2,
-        *quarters, live, near, far,
+        [VMEM] * 9,
+        *quarters, rows,
         scratch=[
-            pltpu.SMEM(live.shape, jnp.int32),
-            pltpu.VMEM((height, count, width), bf16),
             pltpu.VMEM((count, 2 * lines, LANES), f32),
             pltpu.VMEM((count, width, width), f32),
-            dma((8,)),
+            dma((3,)),
         ],
         out_specs=[HBM, HBM],
     )

time: 55.9 us -> 55.3 us (0.989)
    pallas_call x12 -> x13, Pallas kernels: 5.37 us -> 5 us  [call(): pl.pallas_call(body, out_shape=outs, in_specs=list(specs) + [ANY] * len(a...]
where the time goes in v15:
time: 55.3 us; the launch traced here: 55.1 us
  starting transfers between devices  29.4 us (53%)
  waiting for transfers between devices  19.3 us (35%)
  Pallas kernels  5 us (9%)
  between operations  1.39 us (3%)
    ppermute x22, starting transfers between devices, swap(): return lax.ppermute(x, AXES, [(i, i ^ mask) for i in range(devices)])  25.4 us
    ppermute x22, waiting for transfers between devices, swap(): return lax.ppermute(x, AXES, [(i, i ^ mask) for i in range(devices)])  19.3 us
    pallas_call x13, Pallas kernels, call(): pl.pallas_call(body, out_shape=outs, in_specs=list(specs) + [ANY] * len(a...  5 us
    ppermute x2, starting transfers between devices, deliver(): return lax.ppermute(x, AXES, pairs)  4.05 us
  transfers between devices with their start and end apart: 24, of which 15 were waited for; matrix products, arithmetic and copies ran while one was open for 0% of the time, Pallas kernels for 3%

profile of v15, /device:TPU:0, one launch (start us, length us, event | category | flops | bytes accessed | tf_op | source)
XLA Modules:
  0.0 55.1 jit_solution(11263075623771375633)
XLA Ops:
  0.6 1.7 %shard_map.68 = (bf16[128,384]{1,0:T(8,128)(2,1)S(1)}, bf16[160,384]{1,0:T(8,128)(2,1)S(1)}, bf16[32,384]{1,0:T(8,128)(2,1)S(1)}, s32[2,8,128]{2,1,0:T(8,128)S(1...) custom-call(s32[2]{0:T(128)} %bitcast.1, bf16[1,128,2,384]{3,2,1,0:T(2,128)(2,1)} %refs_1_.1, ...), custom_call_target="tpu_custom_call" | custom-call | tf_op jit(solution)/shard_map/pallas_call | solution.py:28
  2.3 3.0 %collective-permute-start.3 = (bf16[160,384]{1,0:T(8,128)(2,1)S(1)}, bf16[160,384]{1,0:T(8,128)(2,1)S(1)}, u32[]{:S(2)}, u32[]{:S(2)}) collective-permute-start(bf16[160,384]{1,0:T(8,128)(2,1)S(1)} %get-tuple-element.17), channel_id=1, source_target_pairs={{0,8},{1,9},{2,10},{3,11},{4,12},{5,13},{6,14},{7,15},{8,0},{9,1},... | collective-permute-start | bytes 368648 | tf_op jit(solution)/shard_map/ppermute | solution.py:252
  5.4 1.9 %collective-permute-start.8 = (bf16[256,512]{1,0:T(8,128)(2,1)S(1)}, bf16[256,512]{1,0:T(8,128)(2,1)S(1)}, u32[]{:S(2)}, u32[]{:S(2)}) collective-permute-start(bf16[256,512]{1,0:T(8,128)(2,1)S(1)} %get-tuple-element.19.refs_2_), channel_id=1, source_target_pairs={{0,8},{1,9},{2,10},{3,11},{4,12},{5,13},{6,14},{7,15},{8,0},{9,1},... | collective-permute-start | bytes 786440 | tf_op jit(solution)/shard_map/ppermute | solution.py:252
  7.4 2.6 %collective-permute-start = (bf16[128,384]{1,0:T(8,128)(2,1)S(1)}, bf16[128,384]{1,0:T(8,128)(2,1)S(1)}, u32[]{:S(2)}, u32[]{:S(2)}) collective-permute-start(bf16[128,384]{1,0:T(8,128)(2,1)S(1)} %get-tuple-element.16.refs_0_), channel_id=1, source_target_pairs={{0,2},{1,3},{2,0},{3,1},{4,6},{5,7},{6,4},{7,5},{8,10},{9,11},{10,... | collective-permute-start | bytes 294920 | tf_op jit(solution)/shard_map/ppermute | solution.py:252
  10.0 1.6 %collective-permute-start.1 = (bf16[128,384]{1,0:T(8,128)(2,1)S(1)}, bf16[128,384]{1,0:T(8,128)(2,1)S(1)}, u32[]{:S(2)}, u32[]{:S(2)}) collective-permute-start(bf16[128,384]{1,0:T(8,128)(2,1)S(1)} %get-tuple-element.16.refs_0_), channel_id=1, source_target_pairs={{0,1},{1,0},{2,3},{3,2},{4,5},{5,4},{6,7},{7,6},{8,9},{9,8},{10,11... | collective-permute-start | bytes 294920 | tf_op jit(solution)/shard_map/ppermute | solution.py:252
  11.6 1.2 %collective-permute-start.4 = (bf16[128,384]{1,0:T(8,128)(2,1)S(1)}, bf16[128,384]{1,0:T(8,128)(2,1)S(1)}, u32[]{:S(2)}, u32[]{:S(2)}) collective-permute-start(bf16[128,384]{1,0:T(8,128)(2,1)S(1)} %slice.8.refs_4_), channel_id=1, source_target_pairs={{0,2},{1,3},{2,0},{3,1},{4,6},{5,7},{6,4},{7,5},{8,10},{9,11},{10,... | collective-permute-start | bytes 294920 | tf_op jit(solution)/shard_map/ppermute | solution.py:252
  13.1 3.8 %collective-permute-start.2 = (bf16[128,384]{1,0:T(8,128)(2,1)S(1)}, bf16[128,384]{1,0:T(8,128)(2,1)S(1)}, u32[]{:S(2)}, u32[]{:S(2)}) collective-permute-start(bf16[128,384]{1,0:T(8,128)(2,1)S(1)} %collective-permute-done.refs_1_), channel_id=1, source_target_pairs={{0,1},{1,0},{2,3},{3,2},{4,5},{5,4},{6,7},{7,6},{8,9},{9,8},{10,11... | collective-permute-start | bytes 294920 | tf_op jit(solution)/shard_map/ppermute | solution.py:252
  17.0 0.7 %collective-permute-start.5 = (bf16[128,384]{1,0:T(8,128)(2,1)S(1)}, bf16[128,384]{1,0:T(8,128)(2,1)S(1)}, u32[]{:S(2)}, u32[]{:S(2)}) collective-permute-start(bf16[128,384]{1,0:T(8,128)(2,1)S(1)} %slice.8.refs_4_), channel_id=1, source_target_pairs={{0,1},{1,0},{2,3},{3,2},{4,5},{5,4},{6,7},{7,6},{8,9},{9,8},{10,11... | collective-permute-start | bytes 294920 | tf_op jit(solution)/shard_map/ppermute | solution.py:252
  17.7 0.6 %collective-permute-done.4.refs_5_ = bf16[128,384]{1,0:T(8,128)(2,1)S(1)} collective-permute-done((bf16[128,384]{1,0:T(8,128)(2,1)S(1)}, bf16[128,384]{1,0:T(8,128)(2,1)S(1)}, u32[]{:S(2)}, u32[]{:S(2)}) %collective-permute-start.4) | collective-permute-done | bytes 98336 | tf_op jit(solution)/shard_map/ppermute | solution.py:252
  18.3 0.7 %collective-permute-start.6 = (bf16[128,384]{1,0:T(8,128)(2,1)S(1)}, bf16[128,384]{1,0:T(8,128)(2,1)S(1)}, u32[]{:S(2)}, u32[]{:S(2)}) collective-permute-start(bf16[128,384]{1,0:T(8,128)(2,1)S(1)} %collective-permute-done.4.refs_5_), channel_id=1, source_target_pairs={{0,1},{1,0},{2,3},{3,2},{4,5},{5,4},{6,7},{7,6},{8,9},{9,8},{10,11... | collective-permute-start | bytes 294920 | tf_op jit(solution)/shard_map/ppermute | solution.py:252
  19.0 1.6 %collective-permute-done.2.refs_3_ = bf16[128,384]{1,0:T(8,128)(2,1)S(1)} collective-permute-done((bf16[128,384]{1,0:T(8,128)(2,1)S(1)}, bf16[128,384]{1,0:T(8,128)(2,1)S(1)}, u32[]{:S(2)}, u32[]{:S(2)}) %collective-permute-start.2) | collective-permute-done | bytes 98336 | tf_op jit(solution)/shard_map/ppermute | solution.py:252
  20.7 1.3 %collective-permute-done.5.refs_6_ = bf16[128,384]{1,0:T(8,128)(2,1)S(1)} collective-permute-done((bf16[128,384]{1,0:T(8,128)(2,1)S(1)}, bf16[128,384]{1,0:T(8,128)(2,1)S(1)}, u32[]{:S(2)}, u32[]{:S(2)}) %collective-permute-start.5) | collective-permute-done | bytes 98336 | tf_op jit(solution)/shard_map/ppermute | solution.py:252
  22.0 1.0 %collective-permute-done.6.refs_7_ = bf16[128,384]{1,0:T(8,128)(2,1)S(1)} collective-permute-done((bf16[128,384]{1,0:T(8,128)(2,1)S(1)}, bf16[128,384]{1,0:T(8,128)(2,1)S(1)}, u32[]{:S(2)}, u32[]{:S(2)}) %collective-permute-start.6) | collective-permute-done | bytes 98336 | tf_op jit(solution)/shard_map/ppermute | solution.py:252
  23.2 0.7 %shard_map.70.refs_0_ = f32[512,384]{1,0:T(8,128)S(1)} custom-call(bf16[2,512,384]{2,1,0:T(8,128)(2,1)S(1)} %get-tuple-element.20.refs_0_, bf16[256,512]{1,0:T(8,128)(2,1)S(1)} %get-tuple-element.18.refs_1_, bf16[256,512]{1,0:T(8,128)(2,1)S(1)} %get-tuple-element.19.refs_2_, bf16[256,512]{1,0:T(8,128)(2,1)S(1)} %collective-permute-done.7.refs_8_.refs_3_, ...), custom_call_target="tpu_custom_call" | custom-call | tf_op jit(solution)/shard_map/pallas_call | solution.py:28
  23.9 1.0 %collective-permute-done.9.refs_1_.refs_2_ = bf16[512,384]{1,0:T(8,128)(2,1)S(1)} collective-permute-done((bf16[512,384]{1,0:T(8,128)(2,1)S(1)}, bf16[512,384]{1,0:T(8,128)(2,1)S(1)}, u32[]{:S(2)}, u32[]{:S(2)}) %collective-permute-start.9) | collective-permute-done | bytes 393248 | tf_op jit(solution)/shard_map/ppermute | solution.py:252
  25.1 0.7 %shard_map.72 = (f32[320,128]{1,0:T(8,128)S(1)}, f32[320,128]{1,0:T(8,128)S(1)}) custom-call(f32[512,384]{1,0:T(8,128)S(1)} %shard_map.71.refs_0_, bf16[512,384]{1,0:T(8,128)(2,1)S(1)} %get-tuple-element.21.refs_1_, bf16[512,384]{1,0:T(8,128)(2,1)S(1)} %collective-permute-done.9.refs_1_.refs_2_, bf16[32,384]{1,0:T(8,128)(2,1)S(1)} %get-tuple-element.22.refs_3_, ...), custom_call_target="tpu_custom_call" | custom-call | tf_op jit(solution)/shard_map/pallas_call | solution.py:28
  26.8 0.6 %collective-permute-done.10.refs_2_ = f32[320,128]{1,0:T(8,128)S(1)} collective-permute-done((f32[320,128]{1,0:T(8,128)S(1)}, f32[320,128]{1,0:T(8,128)S(1)}, u32[]{:S(2)}, u32[]{:S(2)}) %collective-permute-start.10) | collective-permute-done | bytes 163872 | tf_op jit(solution)/shard_map/ppermute | solution.py:252
  27.5 1.6 %collective-permute-start.11 = (f32[160,128]{1,0:T(8,128)S(1)}, f32[160,128]{1,0:T(8,128)S(1)}, u32[]{:S(2)}, u32[]{:S(2)}) collective-permute-start(f32[160,128]{1,0:T(8,128)S(1)} %get-tuple-element.26), channel_id=1, source_target_pairs={{0,16},{1,17},{2,18},{3,19},{4,20},{5,21},{6,22},{7,23},{8,24},{9,... | collective-permute-start | bytes 245768 | tf_op jit(solution)/shard_map/ppermute | solution.py:252
  29.1 3.0 %collective-permute-done.11.refs_1_ = f32[160,128]{1,0:T(8,128)S(1)} collective-permute-done((f32[160,128]{1,0:T(8,128)S(1)}, f32[160,128]{1,0:T(8,128)S(1)}, u32[]{:S(2)}, u32[]{:S(2)}) %collective-permute-start.11) | collective-permute-done | bytes 81952 | tf_op jit(solution)/shard_map/ppermute | solution.py:252
  32.0 3.2 %collective-permute-start.12 = (f32[160,128]{1,0:T(8,128)S(1)}, f32[160,128]{1,0:T(8,128)S(1)}, u32[]{:S(2)}, u32[]{:S(2)}) collective-permute-start(f32[160,128]{1,0:T(8,128)S(1)} %shard_map.74.refs_0_.refs_2_), channel_id=1, source_target_pairs={{0,2},{1,3},{2,0},{3,1},{4,6},{5,7},{6,4},{7,5},{8,10},{9,11},{10,... | collective-permute-start | bytes 245768 | tf_op jit(solution)/shard_map/ppermute | solution.py:252
  35.4 0.7 %collective-permute-start.15 = (bf16[128,384]{1,0:T(8,128)(2,1)S(1)}, bf16[128,384]{1,0:T(8,128)(2,1)S(1)}, u32[]{:S(2)}, u32[]{:S(2)}) collective-permute-start(bf16[128,384]{1,0:T(8,128)(2,1)S(1)} %get-tuple-element.27), channel_id=1, source_target_pairs={{0,0},{1,4},{2,8},{3,12},{4,1},{5,5},{6,9},{7,13},{8,2},{9,6},{10,... | collective-permute-start | bytes 294920 | tf_op jit(solution)/shard_map/ppermute | solution.py:310
  36.1 2.8 %collective-permute-done.12.refs_1_ = f32[160,128]{1,0:T(8,128)S(1)} collective-permute-done((f32[160,128]{1,0:T(8,128)S(1)}, f32[160,128]{1,0:T(8,128)S(1)}, u32[]{:S(2)}, u32[]{:S(2)}) %collective-permute-start.12) | collective-permute-done | bytes 81952 | tf_op jit(solution)/shard_map/ppermute | solution.py:252
  39.0 0.7 %collective-permute-start.13 = (f32[160,128]{1,0:T(8,128)S(1)}, f32[160,128]{1,0:T(8,128)S(1)}, u32[]{:S(2)}, u32[]{:S(2)}) collective-permute-start(f32[160,128]{1,0:T(8,128)S(1)} %shard_map.75.refs_0_), channel_id=1, source_target_pairs={{0,1},{1,0},{2,3},{3,2},{4,5},{5,4},{6,7},{7,6},{8,9},{9,8},{10,11... | collective-permute-start | bytes 245768 | tf_op jit(solution)/shard_map/ppermute | solution.py:252
  39.6 3.4 %collective-permute-start.19 = (bf16[128,384]{1,0:T(8,128)(2,1)S(1)}, bf16[128,384]{1,0:T(8,128)(2,1)S(1)}, u32[]{:S(2)}, u32[]{:S(2)}) collective-permute-start(bf16[128,384]{1,0:T(8,128)(2,1)S(1)} %get-tuple-element.29), channel_id=1, source_target_pairs={{0,2},{1,6},{2,10},{3,14},{4,3},{5,7},{6,11},{7,15},{8,0},{9,4},{1... | collective-permute-start | bytes 294920 | tf_op jit(solution)/shard_map/ppermute | solution.py:310
  43.0 2.1 %collective-permute-done.13.refs_1_ = f32[160,128]{1,0:T(8,128)S(1)} collective-permute-done((f32[160,128]{1,0:T(8,128)S(1)}, f32[160,128]{1,0:T(8,128)S(1)}, u32[]{:S(2)}, u32[]{:S(2)}) %collective-permute-start.13) | collective-permute-done | bytes 81952 | tf_op jit(solution)/shard_map/ppermute | solution.py:252
  45.2 2.4 %collective-permute-start.18 = (f32[160,128]{1,0:T(8,128)S(1)}, f32[160,128]{1,0:T(8,128)S(1)}, u32[]{:S(2)}, u32[]{:S(2)}) collective-permute-start(f32[160,128]{1,0:T(8,128)S(1)} %shard_map.77.refs_0_), channel_id=1, source_target_pairs={{0,24},{1,25},{2,26},{3,27},{4,28},{5,29},{6,30},{7,31},{8,16},{9,... | collective-permute-start | bytes 245768 | tf_op jit(solution)/shard_map/ppermute | solution.py:252
  47.6 0.5 collective-permute-start.17
  48.1 0.6 %collective-permute-start.16 = (f32[160,128]{1,0:T(8,128)S(1)}, f32[160,128]{1,0:T(8,128)S(1)}, u32[]{:S(2)}, u32[]{:S(2)}) collective-permute-start(f32[160,128]{1,0:T(8,128)S(1)} %shard_map.77.refs_0_), channel_id=1, source_target_pairs={{0,8},{1,9},{2,10},{3,11},{4,12},{5,13},{6,14},{7,15},{8,0},{9,1},... | collective-permute-start | bytes 245768 | tf_op jit(solution)/shard_map/ppermute | solution.py:252
  49.1 1.7 %collective-permute-done.18.refs_3_ = f32[160,128]{1,0:T(8,128)S(1)} collective-permute-done((f32[160,128]{1,0:T(8,128)S(1)}, f32[160,128]{1,0:T(8,128)S(1)}, u32[]{:S(2)}, u32[]{:S(2)}) %collective-permute-start.18) | collective-permute-done | bytes 81952 | tf_op jit(solution)/shard_map/ppermute | solution.py:252
  50.8 1.3 %collective-permute-done.17.refs_2_ = f32[160,128]{1,0:T(8,128)S(1)} collective-permute-done((f32[160,128]{1,0:T(8,128)S(1)}, f32[160,128]{1,0:T(8,128)S(1)}, u32[]{:S(2)}, u32[]{:S(2)}) %collective-permute-start.17) | collective-permute-done | bytes 81952 | tf_op jit(solution)/shard_map/ppermute | solution.py:252
  52.6 0.8 %collective-permute-done.22.refs_6_ = f32[160,128]{1,0:T(8,128)S(1)} collective-permute-done((f32[160,128]{1,0:T(8,128)S(1)}, f32[160,128]{1,0:T(8,128)S(1)}, u32[]{:S(2)}, u32[]{:S(2)}) %collective-permute-start.22) | collective-permute-done | bytes 81952 | tf_op jit(solution)/shard_map/ppermute | solution.py:252
  53.8 1.3 %shard_map.80 = (bf16[1,128,2,384]{3,2,1,0:T(2,128)(2,1)}, f32[2,384,384]{2,1,0:T(8,128)}) custom-call(f32[160,128]{1,0:T(8,128)S(1)} %shard_map.77.refs_0_, f32[160,128]{1,0:T(8,128)S(1)} %collective-permute-done.16.refs_1_, f32[160,128]{1,0:T(8,128)S(1)} %collective-permute-done.17.refs_2_, f32[160,128]{1,0:T(8,128)S(1)} %collective-permute-done.18.refs_3_, ...), custom_call_target="tpu_custom_call" | custom-call | tf_op jit(solution)/shard_map/pallas_call | solution.py:28
  (32 shorter events, 2.8 us)
Async XLA Ops:
  2.3 9.2 %collective-permute-start.3 = (bf16[160,384]{1,0:T(8,128)(2,1)S(1)}, bf16[160,384]{1,0:T(8,128)(2,1)S(1)}, u32[]{:S(2)}, u32[]{:S(2)}) collective-permute-start(bf16[160,384]{1,0:T(8,128)(2,1)S(1)} %get-tuple-element.17), channel_id=1, source_target_pairs={{0,8},{1,9},{2,10},{3,11},{4,12},{5,13},{6,14},{7,15},{8,0},{9,1},... | collective-permute-start | bytes 368648 | tf_op jit(solution)/shard_map/ppermute | solution.py:252
  5.3 16.6 %collective-permute-start.7 = (bf16[256,512]{1,0:T(8,128)(2,1)S(1)}, bf16[256,512]{1,0:T(8,128)(2,1)S(1)}, u32[]{:S(2)}, u32[]{:S(2)}) collective-permute-start(bf16[256,512]{1,0:T(8,128)(2,1)S(1)} %get-tuple-element.18.refs_1_), channel_id=1, source_target_pairs={{0,8},{1,9},{2,10},{3,11},{4,12},{5,13},{6,14},{7,15},{8,0},{9,1},... | collective-permute-start | bytes 786440 | tf_op jit(solution)/shard_map/ppermute | solution.py:252
  5.4 16.5 %collective-permute-start.8 = (bf16[256,512]{1,0:T(8,128)(2,1)S(1)}, bf16[256,512]{1,0:T(8,128)(2,1)S(1)}, u32[]{:S(2)}, u32[]{:S(2)}) collective-permute-start(bf16[256,512]{1,0:T(8,128)(2,1)S(1)} %get-tuple-element.19.refs_2_), channel_id=1, source_target_pairs={{0,8},{1,9},{2,10},{3,11},{4,12},{5,13},{6,14},{7,15},{8,0},{9,1},... | collective-permute-start | bytes 786440 | tf_op jit(solution)/shard_map/ppermute | solution.py:252
  7.4 5.8 %collective-permute-start = (bf16[128,384]{1,0:T(8,128)(2,1)S(1)}, bf16[128,384]{1,0:T(8,128)(2,1)S(1)}, u32[]{:S(2)}, u32[]{:S(2)}) collective-permute-start(bf16[128,384]{1,0:T(8,128)(2,1)S(1)} %get-tuple-element.16.refs_0_), channel_id=1, source_target_pairs={{0,2},{1,3},{2,0},{3,1},{4,6},{5,7},{6,4},{7,5},{8,10},{9,11},{10,... | collective-permute-start | bytes 294920 | tf_op jit(solution)/shard_map/ppermute | solution.py:252
  10.0 7.0 %collective-permute-start.1 = (bf16[128,384]{1,0:T(8,128)(2,1)S(1)}, bf16[128,384]{1,0:T(8,128)(2,1)S(1)}, u32[]{:S(2)}, u32[]{:S(2)}) collective-permute-start(bf16[128,384]{1,0:T(8,128)(2,1)S(1)} %get-tuple-element.16.refs_0_), channel_id=1, source_target_pairs={{0,1},{1,0},{2,3},{3,2},{4,5},{5,4},{6,7},{7,6},{8,9},{9,8},{10,11... | collective-permute-start | bytes 294920 | tf_op jit(solution)/shard_map/ppermute | solution.py:252
  11.6 6.8 %collective-permute-start.4 = (bf16[128,384]{1,0:T(8,128)(2,1)S(1)}, bf16[128,384]{1,0:T(8,128)(2,1)S(1)}, u32[]{:S(2)}, u32[]{:S(2)}) collective-permute-start(bf16[128,384]{1,0:T(8,128)(2,1)S(1)} %slice.8.refs_4_), channel_id=1, source_target_pairs={{0,2},{1,3},{2,0},{3,1},{4,6},{5,7},{6,4},{7,5},{8,10},{9,11},{10,... | collective-permute-start | bytes 294920 | tf_op jit(solution)/shard_map/ppermute | solution.py:252
  13.1 7.6 %collective-permute-start.2 = (bf16[128,384]{1,0:T(8,128)(2,1)S(1)}, bf16[128,384]{1,0:T(8,128)(2,1)S(1)}, u32[]{:S(2)}, u32[]{:S(2)}) collective-permute-start(bf16[128,384]{1,0:T(8,128)(2,1)S(1)} %collective-permute-done.refs_1_), channel_id=1, source_target_pairs={{0,1},{1,0},{2,3},{3,2},{4,5},{5,4},{6,7},{7,6},{8,9},{9,8},{10,11... | collective-permute-start | bytes 294920 | tf_op jit(solution)/shard_map/ppermute | solution.py:252
  17.0 5.0 %collective-permute-start.5 = (bf16[128,384]{1,0:T(8,128)(2,1)S(1)}, bf16[128,384]{1,0:T(8,128)(2,1)S(1)}, u32[]{:S(2)}, u32[]{:S(2)}) collective-permute-start(bf16[128,384]{1,0:T(8,128)(2,1)S(1)} %slice.8.refs_4_), channel_id=1, source_target_pairs={{0,1},{1,0},{2,3},{3,2},{4,5},{5,4},{6,7},{7,6},{8,9},{9,8},{10,11... | collective-permute-start | bytes 294920 | tf_op jit(solution)/shard_map/ppermute | solution.py:252
  18.3 4.7 %collective-permute-start.6 = (bf16[128,384]{1,0:T(8,128)(2,1)S(1)}, bf16[128,384]{1,0:T(8,128)(2,1)S(1)}, u32[]{:S(2)}, u32[]{:S(2)}) collective-permute-start(bf16[128,384]{1,0:T(8,128)(2,1)S(1)} %collective-permute-done.4.refs_5_), channel_id=1, source_target_pairs={{0,1},{1,0},{2,3},{3,2},{4,5},{5,4},{6,7},{7,6},{8,9},{9,8},{10,11... | collective-permute-start | bytes 294920 | tf_op jit(solution)/shard_map/ppermute | solution.py:252
  23.1 1.8 %collective-permute-start.9 = (bf16[512,384]{1,0:T(8,128)(2,1)S(1)}, bf16[512,384]{1,0:T(8,128)(2,1)S(1)}, u32[]{:S(2)}, u32[]{:S(2)}) collective-permute-start(bf16[512,384]{1,0:T(8,128)(2,1)S(1)} %get-tuple-element.21.refs_1_), channel_id=1, source_target_pairs={{0,4},{1,5},{2,6},{3,7},{4,0},{5,1},{6,2},{7,3},{8,12},{9,13},{10,... | collective-permute-start | bytes 1179656 | tf_op jit(solution)/shard_map/ppermute | solution.py:252
  24.9 10.4 %collective-permute-start.14 = (f32[512,384]{1,0:T(8,128)S(1)}, f32[512,384]{1,0:T(8,128)S(1)}, u32[]{:S(2)}, u32[]{:S(2)}) collective-permute-start(f32[512,384]{1,0:T(8,128)S(1)} %shard_map.71.refs_0_), channel_id=1, source_target_pairs={{0,4},{1,5},{2,6},{3,7},{4,0},{5,1},{6,2},{7,3},{8,12},{9,13},{10,... | collective-permute-start | bytes 2359304 | tf_op jit(solution)/shard_map/ppermute | solution.py:252
  25.8 1.7 %collective-permute-start.10 = (f32[320,128]{1,0:T(8,128)S(1)}, f32[320,128]{1,0:T(8,128)S(1)}, u32[]{:S(2)}, u32[]{:S(2)}) collective-permute-start(f32[320,128]{1,0:T(8,128)S(1)} %get-tuple-element.24), channel_id=1, source_target_pairs={{0,4},{1,5},{2,6},{3,7},{4,0},{5,1},{6,2},{7,3},{8,12},{9,13},{10,... | collective-permute-start | bytes 491528 | tf_op jit(solution)/shard_map/ppermute | solution.py:252
  27.5 4.6 %collective-permute-start.11 = (f32[160,128]{1,0:T(8,128)S(1)}, f32[160,128]{1,0:T(8,128)S(1)}, u32[]{:S(2)}, u32[]{:S(2)}) collective-permute-start(f32[160,128]{1,0:T(8,128)S(1)} %get-tuple-element.26), channel_id=1, source_target_pairs={{0,16},{1,17},{2,18},{3,19},{4,20},{5,21},{6,22},{7,23},{8,24},{9,... | collective-permute-start | bytes 245768 | tf_op jit(solution)/shard_map/ppermute | solution.py:252
  32.0 6.9 %collective-permute-start.12 = (f32[160,128]{1,0:T(8,128)S(1)}, f32[160,128]{1,0:T(8,128)S(1)}, u32[]{:S(2)}, u32[]{:S(2)}) collective-permute-start(f32[160,128]{1,0:T(8,128)S(1)} %shard_map.74.refs_0_.refs_2_), channel_id=1, source_target_pairs={{0,2},{1,3},{2,0},{3,1},{4,6},{5,7},{6,4},{7,5},{8,10},{9,11},{10,... | collective-permute-start | bytes 245768 | tf_op jit(solution)/shard_map/ppermute | solution.py:252
  35.4 9.7 %collective-permute-start.15 = (bf16[128,384]{1,0:T(8,128)(2,1)S(1)}, bf16[128,384]{1,0:T(8,128)(2,1)S(1)}, u32[]{:S(2)}, u32[]{:S(2)}) collective-permute-start(bf16[128,384]{1,0:T(8,128)(2,1)S(1)} %get-tuple-element.27), channel_id=1, source_target_pairs={{0,0},{1,4},{2,8},{3,12},{4,1},{5,5},{6,9},{7,13},{8,2},{9,6},{10,... | collective-permute-start | bytes 294920 | tf_op jit(solution)/shard_map/ppermute | solution.py:310
  39.0 6.2 %collective-permute-start.13 = (f32[160,128]{1,0:T(8,128)S(1)}, f32[160,128]{1,0:T(8,128)S(1)}, u32[]{:S(2)}, u32[]{:S(2)}) collective-permute-start(f32[160,128]{1,0:T(8,128)S(1)} %shard_map.75.refs_0_), channel_id=1, source_target_pairs={{0,1},{1,0},{2,3},{3,2},{4,5},{5,4},{6,7},{7,6},{8,9},{9,8},{10,11... | collective-permute-start | bytes 245768 | tf_op jit(solution)/shard_map/ppermute | solution.py:252
  39.6 9.1 %collective-permute-start.19 = (bf16[128,384]{1,0:T(8,128)(2,1)S(1)}, bf16[128,384]{1,0:T(8,128)(2,1)S(1)}, u32[]{:S(2)}, u32[]{:S(2)}) collective-permute-start(bf16[128,384]{1,0:T(8,128)(2,1)S(1)} %get-tuple-element.29), channel_id=1, source_target_pairs={{0,2},{1,6},{2,10},{3,14},{4,3},{5,7},{6,11},{7,15},{8,0},{9,4},{1... | collective-permute-start | bytes 294920 | tf_op jit(solution)/shard_map/ppermute | solution.py:310
  45.2 5.6 %collective-permute-start.18 = (f32[160,128]{1,0:T(8,128)S(1)}, f32[160,128]{1,0:T(8,128)S(1)}, u32[]{:S(2)}, u32[]{:S(2)}) collective-permute-start(f32[160,128]{1,0:T(8,128)S(1)} %shard_map.77.refs_0_), channel_id=1, source_target_pairs={{0,24},{1,25},{2,26},{3,27},{4,28},{5,29},{6,30},{7,31},{8,16},{9,... | collective-permute-start | bytes 245768 | tf_op jit(solution)/shard_map/ppermute | solution.py:252
  47.6 4.4 %collective-permute-start.17 = (f32[160,128]{1,0:T(8,128)S(1)}, f32[160,128]{1,0:T(8,128)S(1)}, u32[]{:S(2)}, u32[]{:S(2)}) collective-permute-start(f32[160,128]{1,0:T(8,128)S(1)} %shard_map.77.refs_0_), channel_id=1, source_target_pairs={{0,16},{1,17},{2,18},{3,19},{4,20},{5,21},{6,22},{7,23},{8,24},{9,... | collective-permute-start | bytes 245768 | tf_op jit(solution)/shard_map/ppermute | solution.py:252
  48.1 4.4 %collective-permute-start.16 = (f32[160,128]{1,0:T(8,128)S(1)}, f32[160,128]{1,0:T(8,128)S(1)}, u32[]{:S(2)}, u32[]{:S(2)}) collective-permute-start(f32[160,128]{1,0:T(8,128)S(1)} %shard_map.77.refs_0_), channel_id=1, source_target_pairs={{0,8},{1,9},{2,10},{3,11},{4,12},{5,13},{6,14},{7,15},{8,0},{9,1},... | collective-permute-start | bytes 245768 | tf_op jit(solution)/shard_map/ppermute | solution.py:252
  49.0 3.5 %collective-permute-start.20 = (f32[160,128]{1,0:T(8,128)S(1)}, f32[160,128]{1,0:T(8,128)S(1)}, u32[]{:S(2)}, u32[]{:S(2)}) collective-permute-start(f32[160,128]{1,0:T(8,128)S(1)} %shard_map.79), channel_id=1, source_target_pairs={{0,4},{1,5},{2,6},{3,7},{4,0},{5,1},{6,2},{7,3},{8,12},{9,13},{10,... | collective-permute-start | bytes 245768 | tf_op jit(solution)/shard_map/ppermute | solution.py:252
  50.8 1.8 %collective-permute-start.23 = (f32[160,128]{1,0:T(8,128)S(1)}, f32[160,128]{1,0:T(8,128)S(1)}, u32[]{:S(2)}, u32[]{:S(2)}) collective-permute-start(f32[160,128]{1,0:T(8,128)S(1)} %collective-permute-done.18.refs_3_), channel_id=1, source_target_pairs={{0,4},{1,5},{2,6},{3,7},{4,0},{5,1},{6,2},{7,3},{8,12},{9,13},{10,... | collective-permute-start | bytes 245768 | tf_op jit(solution)/shard_map/ppermute | solution.py:252
  52.0 1.3 %collective-permute-start.22 = (f32[160,128]{1,0:T(8,128)S(1)}, f32[160,128]{1,0:T(8,128)S(1)}, u32[]{:S(2)}, u32[]{:S(2)}) collective-permute-start(f32[160,128]{1,0:T(8,128)S(1)} %collective-permute-done.17.refs_2_), channel_id=1, source_target_pairs={{0,4},{1,5},{2,6},{3,7},{4,0},{5,1},{6,2},{7,3},{8,12},{9,13},{10,... | collective-permute-start | bytes 245768 | tf_op jit(solution)/shard_map/ppermute | solution.py:252
  52.5 1.3 %collective-permute-start.21 = (f32[160,128]{1,0:T(8,128)S(1)}, f32[160,128]{1,0:T(8,128)S(1)}, u32[]{:S(2)}, u32[]{:S(2)}) collective-permute-start(f32[160,128]{1,0:T(8,128)S(1)} %collective-permute-done.16.refs_1_), channel_id=1, source_target_pairs={{0,4},{1,5},{2,6},{3,7},{4,0},{5,1},{6,2},{7,3},{8,12},{9,13},{10,... | collective-permute-start | bytes 245768 | tf_op jit(solution)/shard_map/ppermute | solution.py:252

commit v16 on v15

--- a/solution.py
+++ b/solution.py
@@ -210,18 +210,22 @@
         out[0, :, s, :] = jnp.where(row < limits[s, :1, :1], value, jnp.zeros(value.shape, value.dtype))
 
 
-def finish_kernel(*refs):
-    parts, (rows, rows_out, out, lines, result, sems) = refs[:8], refs[8:]
+def stack_kernel(*refs):
+    for index, ref in enumerate(refs[:-1]):
+        refs[-1][index] = ref[...]
+
+
+def finish_kernel(own, other, rows, rows_out, out, lines, result, sems):
     copies = [pltpu.make_async_copy(rows, rows_out, sems.at[0])]
     copies[0].start()
     point, side, core = (lax.axis_index(name) for name in ("hyp", "side", "core"))
-    size = parts[0].shape[0]
-    for index, part in enumerate(parts):
-        owner = core if index < 4 else 1 - core
-        node = 1 - side if index % 2 else side
-        slot = 1 - point if index // 2 % 2 else point
-        start = pl.multiple_of((owner * 2 + slot) * size, 8)
-        lines[node, pl.ds(start, size), :] = part[...]
+    size = own.shape[1]
+    for parts, owner in ((own, core), (other, 1 - core)):
+        for index in range(own.shape[0]):
+            node = 1 - side if index % 2 else side
+            slot = 1 - point if index // 2 else point
+            start = pl.multiple_of((owner * 2 + slot) * size, 8)
+            lines[node, pl.ds(start, size), :] = parts[index]
     places = [slice(index * LANES, (index + 1) * LANES) for index in range(BLOCKS)]
     for node in range(2):
         held = [lines[node, index * LANES : (index + 1) * LANES, :] for index in range(HELD)]
@@ -323,13 +327,14 @@
     rows = call(
         rows_kernel, shape((1, height, count, width), bf16), [VMEM] * 3, limits, near, far
     )
-    held = call(hold_kernel, shape(total.shape, f32), [ANY], total, out_specs=ANY, after=[rows], alias={0: 0})
-    quarters += [swap(x, core=1) for x in [held] + quarters[1:]]
+    quarters = call(
+        stack_kernel, shape((len(quarters), *part.shape), f32), [VMEM] * len(quarters), *quarters, after=[rows]
+    )
     return call(
         finish_kernel,
         [shape((1, height, count, width), bf16), shape((count, width, width), f32)],
-        [VMEM] * 9,
-        *quarters, rows,
+        [VMEM] * 3,
+        quarters, swap(quarters, core=1), rows,
         scratch=[
             pltpu.VMEM((count, 2 * lines, LANES), f32),
             pltpu.VMEM((count, width, width), f32),

time: 55.3 us -> 55.7 us (level)
    ppermute x22 -> x19, waiting for transfers between devices: 19.3 us -> 19.7 us  [swap(): return lax.ppermute(x, AXES, [(i, i ^ mask) for i in range(devices)])]
    ppermute x22 -> x19, starting transfers between devices: 25.4 us -> 25.3 us  [swap(): return lax.ppermute(x, AXES, [(i, i ^ mask) for i in range(devices)])]
  transfers between devices with their start and end apart: 24 -> 21, of which waited for: 15 -> 14; matrix products, arithmetic and copies ran while one was open for 0% -> 0% of each run, Pallas kernels for 3% -> 3%
where the time goes in v16:
time: 55.7 us; the launch traced here: 55.5 us
  starting transfers between devices  29.4 us (53%)
  waiting for transfers between devices  19.7 us (35%)
  Pallas kernels  5.02 us (9%)
  between operations  1.38 us (2%)
    ppermute x19, starting transfers between devices, swap(): return lax.ppermute(x, AXES, [(i, i ^ mask) for i in range(devices)])  25.3 us
    ppermute x19, waiting for transfers between devices, swap(): return lax.ppermute(x, AXES, [(i, i ^ mask) for i in range(devices)])  19.7 us
    pallas_call x13, Pallas kernels, call(): pl.pallas_call(body, out_shape=outs, in_specs=list(specs) + [ANY] * len(a...  5.02 us
    ppermute x2, starting transfers between devices, deliver(): return lax.ppermute(x, AXES, pairs)  4.05 us
  transfers between devices with their start and end apart: 21, of which 14 were waited for; matrix products, arithmetic and copies ran while one was open for 0% of the time, Pallas kernels for 3%

profile of v16, /device:TPU:0, one launch (start us, length us, event | category | flops | bytes accessed | tf_op | source)
XLA Modules:
  0.0 55.5 jit_solution(6960725454614062630)
XLA Ops:
  0.6 1.7 %shard_map.68 = (bf16[128,384]{1,0:T(8,128)(2,1)S(1)}, bf16[160,384]{1,0:T(8,128)(2,1)S(1)}, bf16[32,384]{1,0:T(8,128)(2,1)S(1)}, s32[2,8,128]{2,1,0:T(8,128)S(1...) custom-call(s32[2]{0:T(128)} %bitcast.1, bf16[1,128,2,384]{3,2,1,0:T(2,128)(2,1)} %refs_1_.1, ...), custom_call_target="tpu_custom_call" | custom-call | tf_op jit(solution)/shard_map/pallas_call | solution.py:28
  2.3 3.0 %collective-permute-start.3 = (bf16[160,384]{1,0:T(8,128)(2,1)S(1)}, bf16[160,384]{1,0:T(8,128)(2,1)S(1)}, u32[]{:S(2)}, u32[]{:S(2)}) collective-permute-start(bf16[160,384]{1,0:T(8,128)(2,1)S(1)} %get-tuple-element.17), channel_id=1, source_target_pairs={{0,8},{1,9},{2,10},{3,11},{4,12},{5,13},{6,14},{7,15},{8,0},{9,1},... | collective-permute-start | bytes 368648 | tf_op jit(solution)/shard_map/ppermute | solution.py:256
  5.4 1.9 %collective-permute-start.8 = (bf16[256,512]{1,0:T(8,128)(2,1)S(1)}, bf16[256,512]{1,0:T(8,128)(2,1)S(1)}, u32[]{:S(2)}, u32[]{:S(2)}) collective-permute-start(bf16[256,512]{1,0:T(8,128)(2,1)S(1)} %get-tuple-element.19.refs_2_), channel_id=1, source_target_pairs={{0,8},{1,9},{2,10},{3,11},{4,12},{5,13},{6,14},{7,15},{8,0},{9,1},... | collective-permute-start | bytes 786440 | tf_op jit(solution)/shard_map/ppermute | solution.py:256
  7.4 2.6 %collective-permute-start = (bf16[128,384]{1,0:T(8,128)(2,1)S(1)}, bf16[128,384]{1,0:T(8,128)(2,1)S(1)}, u32[]{:S(2)}, u32[]{:S(2)}) collective-permute-start(bf16[128,384]{1,0:T(8,128)(2,1)S(1)} %get-tuple-element.16.refs_0_), channel_id=1, source_target_pairs={{0,2},{1,3},{2,0},{3,1},{4,6},{5,7},{6,4},{7,5},{8,10},{9,11},{10,... | collective-permute-start | bytes 294920 | tf_op jit(solution)/shard_map/ppermute | solution.py:256
  10.0 1.6 %collective-permute-start.1 = (bf16[128,384]{1,0:T(8,128)(2,1)S(1)}, bf16[128,384]{1,0:T(8,128)(2,1)S(1)}, u32[]{:S(2)}, u32[]{:S(2)}) collective-permute-start(bf16[128,384]{1,0:T(8,128)(2,1)S(1)} %get-tuple-element.16.refs_0_), channel_id=1, source_target_pairs={{0,1},{1,0},{2,3},{3,2},{4,5},{5,4},{6,7},{7,6},{8,9},{9,8},{10,11... | collective-permute-start | bytes 294920 | tf_op jit(solution)/shard_map/ppermute | solution.py:256
  11.6 1.2 %collective-permute-start.4 = (bf16[128,384]{1,0:T(8,128)(2,1)S(1)}, bf16[128,384]{1,0:T(8,128)(2,1)S(1)}, u32[]{:S(2)}, u32[]{:S(2)}) collective-permute-start(bf16[128,384]{1,0:T(8,128)(2,1)S(1)} %slice.8.refs_4_), channel_id=1, source_target_pairs={{0,2},{1,3},{2,0},{3,1},{4,6},{5,7},{6,4},{7,5},{8,10},{9,11},{10,... | collective-permute-start | bytes 294920 | tf_op jit(solution)/shard_map/ppermute | solution.py:256
  13.1 3.8 %collective-permute-start.2 = (bf16[128,384]{1,0:T(8,128)(2,1)S(1)}, bf16[128,384]{1,0:T(8,128)(2,1)S(1)}, u32[]{:S(2)}, u32[]{:S(2)}) collective-permute-start(bf16[128,384]{1,0:T(8,128)(2,1)S(1)} %collective-permute-done.refs_1_), channel_id=1, source_target_pairs={{0,1},{1,0},{2,3},{3,2},{4,5},{5,4},{6,7},{7,6},{8,9},{9,8},{10,11... | collective-permute-start | bytes 294920 | tf_op jit(solution)/shard_map/ppermute | solution.py:256
  17.0 0.7 %collective-permute-start.5 = (bf16[128,384]{1,0:T(8,128)(2,1)S(1)}, bf16[128,384]{1,0:T(8,128)(2,1)S(1)}, u32[]{:S(2)}, u32[]{:S(2)}) collective-permute-start(bf16[128,384]{1,0:T(8,128)(2,1)S(1)} %slice.8.refs_4_), channel_id=1, source_target_pairs={{0,1},{1,0},{2,3},{3,2},{4,5},{5,4},{6,7},{7,6},{8,9},{9,8},{10,11... | collective-permute-start | bytes 294920 | tf_op jit(solution)/shard_map/ppermute | solution.py:256
  17.7 0.6 %collective-permute-done.4.refs_5_ = bf16[128,384]{1,0:T(8,128)(2,1)S(1)} collective-permute-done((bf16[128,384]{1,0:T(8,128)(2,1)S(1)}, bf16[128,384]{1,0:T(8,128)(2,1)S(1)}, u32[]{:S(2)}, u32[]{:S(2)}) %collective-permute-start.4) | collective-permute-done | bytes 98336 | tf_op jit(solution)/shard_map/ppermute | solution.py:256
  18.3 0.7 %collective-permute-start.6 = (bf16[128,384]{1,0:T(8,128)(2,1)S(1)}, bf16[128,384]{1,0:T(8,128)(2,1)S(1)}, u32[]{:S(2)}, u32[]{:S(2)}) collective-permute-start(bf16[128,384]{1,0:T(8,128)(2,1)S(1)} %collective-permute-done.4.refs_5_), channel_id=1, source_target_pairs={{0,1},{1,0},{2,3},{3,2},{4,5},{5,4},{6,7},{7,6},{8,9},{9,8},{10,11... | collective-permute-start | bytes 294920 | tf_op jit(solution)/shard_map/ppermute | solution.py:256
  19.0 1.6 %collective-permute-done.2.refs_3_ = bf16[128,384]{1,0:T(8,128)(2,1)S(1)} collective-permute-done((bf16[128,384]{1,0:T(8,128)(2,1)S(1)}, bf16[128,384]{1,0:T(8,128)(2,1)S(1)}, u32[]{:S(2)}, u32[]{:S(2)}) %collective-permute-start.2) | collective-permute-done | bytes 98336 | tf_op jit(solution)/shard_map/ppermute | solution.py:256
  20.7 1.3 %collective-permute-done.5.refs_6_ = bf16[128,384]{1,0:T(8,128)(2,1)S(1)} collective-permute-done((bf16[128,384]{1,0:T(8,128)(2,1)S(1)}, bf16[128,384]{1,0:T(8,128)(2,1)S(1)}, u32[]{:S(2)}, u32[]{:S(2)}) %collective-permute-start.5) | collective-permute-done | bytes 98336 | tf_op jit(solution)/shard_map/ppermute | solution.py:256
  22.0 1.0 %collective-permute-done.6.refs_7_ = bf16[128,384]{1,0:T(8,128)(2,1)S(1)} collective-permute-done((bf16[128,384]{1,0:T(8,128)(2,1)S(1)}, bf16[128,384]{1,0:T(8,128)(2,1)S(1)}, u32[]{:S(2)}, u32[]{:S(2)}) %collective-permute-start.6) | collective-permute-done | bytes 98336 | tf_op jit(solution)/shard_map/ppermute | solution.py:256
  23.2 0.7 %shard_map.70.refs_0_ = f32[512,384]{1,0:T(8,128)S(1)} custom-call(bf16[2,512,384]{2,1,0:T(8,128)(2,1)S(1)} %get-tuple-element.20.refs_0_, bf16[256,512]{1,0:T(8,128)(2,1)S(1)} %get-tuple-element.18.refs_1_, bf16[256,512]{1,0:T(8,128)(2,1)S(1)} %get-tuple-element.19.refs_2_, bf16[256,512]{1,0:T(8,128)(2,1)S(1)} %collective-permute-done.7.refs_8_.refs_3_, ...), custom_call_target="tpu_custom_call" | custom-call | tf_op jit(solution)/shard_map/pallas_call | solution.py:28
  23.9 1.0 %collective-permute-done.9.refs_1_.refs_2_ = bf16[512,384]{1,0:T(8,128)(2,1)S(1)} collective-permute-done((bf16[512,384]{1,0:T(8,128)(2,1)S(1)}, bf16[512,384]{1,0:T(8,128)(2,1)S(1)}, u32[]{:S(2)}, u32[]{:S(2)}) %collective-permute-start.9) | collective-permute-done | bytes 393248 | tf_op jit(solution)/shard_map/ppermute | solution.py:256
  25.1 0.7 %shard_map.72 = (f32[320,128]{1,0:T(8,128)S(1)}, f32[320,128]{1,0:T(8,128)S(1)}) custom-call(f32[512,384]{1,0:T(8,128)S(1)} %shard_map.71.refs_0_, bf16[512,384]{1,0:T(8,128)(2,1)S(1)} %get-tuple-element.21.refs_1_, bf16[512,384]{1,0:T(8,128)(2,1)S(1)} %collective-permute-done.9.refs_1_.refs_2_, bf16[32,384]{1,0:T(8,128)(2,1)S(1)} %get-tuple-element.22.refs_3_, ...), custom_call_target="tpu_custom_call" | custom-call | tf_op jit(solution)/shard_map/pallas_call | solution.py:28
  26.8 0.6 %collective-permute-done.10.refs_2_ = f32[320,128]{1,0:T(8,128)S(1)} collective-permute-done((f32[320,128]{1,0:T(8,128)S(1)}, f32[320,128]{1,0:T(8,128)S(1)}, u32[]{:S(2)}, u32[]{:S(2)}) %collective-permute-start.10) | collective-permute-done | bytes 163872 | tf_op jit(solution)/shard_map/ppermute | solution.py:256
  27.5 1.6 %collective-permute-start.11 = (f32[160,128]{1,0:T(8,128)S(1)}, f32[160,128]{1,0:T(8,128)S(1)}, u32[]{:S(2)}, u32[]{:S(2)}) collective-permute-start(f32[160,128]{1,0:T(8,128)S(1)} %get-tuple-element.26), channel_id=1, source_target_pairs={{0,16},{1,17},{2,18},{3,19},{4,20},{5,21},{6,22},{7,23},{8,24},{9,... | collective-permute-start | bytes 245768 | tf_op jit(solution)/shard_map/ppermute | solution.py:256
  29.1 3.0 %collective-permute-done.11.refs_1_ = f32[160,128]{1,0:T(8,128)S(1)} collective-permute-done((f32[160,128]{1,0:T(8,128)S(1)}, f32[160,128]{1,0:T(8,128)S(1)}, u32[]{:S(2)}, u32[]{:S(2)}) %collective-permute-start.11) | collective-permute-done | bytes 81952 | tf_op jit(solution)/shard_map/ppermute | solution.py:256
  32.0 3.2 %collective-permute-start.12 = (f32[160,128]{1,0:T(8,128)S(1)}, f32[160,128]{1,0:T(8,128)S(1)}, u32[]{:S(2)}, u32[]{:S(2)}) collective-permute-start(f32[160,128]{1,0:T(8,128)S(1)} %shard_map.74.refs_0_.refs_2_), channel_id=1, source_target_pairs={{0,2},{1,3},{2,0},{3,1},{4,6},{5,7},{6,4},{7,5},{8,10},{9,11},{10,... | collective-permute-start | bytes 245768 | tf_op jit(solution)/shard_map/ppermute | solution.py:256
  35.4 0.7 %collective-permute-start.15 = (bf16[128,384]{1,0:T(8,128)(2,1)S(1)}, bf16[128,384]{1,0:T(8,128)(2,1)S(1)}, u32[]{:S(2)}, u32[]{:S(2)}) collective-permute-start(bf16[128,384]{1,0:T(8,128)(2,1)S(1)} %get-tuple-element.27), channel_id=1, source_target_pairs={{0,0},{1,4},{2,8},{3,12},{4,1},{5,5},{6,9},{7,13},{8,2},{9,6},{10,... | collective-permute-start | bytes 294920 | tf_op jit(solution)/shard_map/ppermute | solution.py:314
  36.1 2.8 %collective-permute-done.12.refs_1_ = f32[160,128]{1,0:T(8,128)S(1)} collective-permute-done((f32[160,128]{1,0:T(8,128)S(1)}, f32[160,128]{1,0:T(8,128)S(1)}, u32[]{:S(2)}, u32[]{:S(2)}) %collective-permute-start.12) | collective-permute-done | bytes 81952 | tf_op jit(solution)/shard_map/ppermute | solution.py:256
  39.0 0.7 %collective-permute-start.13 = (f32[160,128]{1,0:T(8,128)S(1)}, f32[160,128]{1,0:T(8,128)S(1)}, u32[]{:S(2)}, u32[]{:S(2)}) collective-permute-start(f32[160,128]{1,0:T(8,128)S(1)} %shard_map.75.refs_0_), channel_id=1, source_target_pairs={{0,1},{1,0},{2,3},{3,2},{4,5},{5,4},{6,7},{7,6},{8,9},{9,8},{10,11... | collective-permute-start | bytes 245768 | tf_op jit(solution)/shard_map/ppermute | solution.py:256
  39.6 3.4 %collective-permute-start.19 = (bf16[128,384]{1,0:T(8,128)(2,1)S(1)}, bf16[128,384]{1,0:T(8,128)(2,1)S(1)}, u32[]{:S(2)}, u32[]{:S(2)}) collective-permute-start(bf16[128,384]{1,0:T(8,128)(2,1)S(1)} %get-tuple-element.29), channel_id=1, source_target_pairs={{0,2},{1,6},{2,10},{3,14},{4,3},{5,7},{6,11},{7,15},{8,0},{9,4},{1... | collective-permute-start | bytes 294920 | tf_op jit(solution)/shard_map/ppermute | solution.py:314
  43.0 2.1 %collective-permute-done.13.refs_1_ = f32[160,128]{1,0:T(8,128)S(1)} collective-permute-done((f32[160,128]{1,0:T(8,128)S(1)}, f32[160,128]{1,0:T(8,128)S(1)}, u32[]{:S(2)}, u32[]{:S(2)}) %collective-permute-start.13) | collective-permute-done | bytes 81952 | tf_op jit(solution)/shard_map/ppermute | solution.py:256
  45.2 2.4 %collective-permute-start.18 = (f32[160,128]{1,0:T(8,128)S(1)}, f32[160,128]{1,0:T(8,128)S(1)}, u32[]{:S(2)}, u32[]{:S(2)}) collective-permute-start(f32[160,128]{1,0:T(8,128)S(1)} %shard_map.77.refs_0_), channel_id=1, source_target_pairs={{0,24},{1,25},{2,26},{3,27},{4,28},{5,29},{6,30},{7,31},{8,16},{9,... | collective-permute-start | bytes 245768 | tf_op jit(solution)/shard_map/ppermute | solution.py:256
  47.6 0.5 collective-permute-start.17
  48.1 0.6 %collective-permute-start.16 = (f32[160,128]{1,0:T(8,128)S(1)}, f32[160,128]{1,0:T(8,128)S(1)}, u32[]{:S(2)}, u32[]{:S(2)}) collective-permute-start(f32[160,128]{1,0:T(8,128)S(1)} %shard_map.77.refs_0_), channel_id=1, source_target_pairs={{0,8},{1,9},{2,10},{3,11},{4,12},{5,13},{6,14},{7,15},{8,0},{9,1},... | collective-permute-start | bytes 245768 | tf_op jit(solution)/shard_map/ppermute | solution.py:256
  49.0 1.8 %collective-permute-done.18.refs_3_ = f32[160,128]{1,0:T(8,128)S(1)} collective-permute-done((f32[160,128]{1,0:T(8,128)S(1)}, f32[160,128]{1,0:T(8,128)S(1)}, u32[]{:S(2)}, u32[]{:S(2)}) %collective-permute-start.18) | collective-permute-done | bytes 81952 | tf_op jit(solution)/shard_map/ppermute | solution.py:256
  50.8 1.3 %collective-permute-done.17.refs_2_ = f32[160,128]{1,0:T(8,128)S(1)} collective-permute-done((f32[160,128]{1,0:T(8,128)S(1)}, f32[160,128]{1,0:T(8,128)S(1)}, u32[]{:S(2)}, u32[]{:S(2)}) %collective-permute-start.17) | collective-permute-done | bytes 81952 | tf_op jit(solution)/shard_map/ppermute | solution.py:256
  52.7 1.6 %collective-permute-done.20.refs_1_ = f32[4,160,128]{2,1,0:T(8,128)S(1)} collective-permute-done((f32[4,160,128]{2,1,0:T(8,128)S(1)}, f32[4,160,128]{2,1,0:T(8,128)S(1)}, u32[]{:S(2)}, u32[]{:S(2)}) %collective-permute-start.20) | collective-permute-done | bytes 327712 | tf_op jit(solution)/shard_map/ppermute | solution.py:256
  54.3 1.3 %shard_map.80 = (bf16[1,128,2,384]{3,2,1,0:T(2,128)(2,1)}, f32[2,384,384]{2,1,0:T(8,128)}) custom-call(f32[4,160,128]{2,1,0:T(8,128)S(1)} %shard_map.79.refs_0_, f32[4,160,128]{2,1,0:T(8,128)S(1)} %collective-permute-done.20.refs_1_, bf16[1,128,2,384]{3,2,1,0:T(2,128)(2,1)S(1)} %shard_map.78.refs_4_.refs_2_), custom_call_target="tpu_custom_call" | custom-call | tf_op jit(solution)/shard_map/pallas_call | solution.py:28
  (25 shorter events, 2.3 us)
Async XLA Ops:
  2.3 9.2 %collective-permute-start.3 = (bf16[160,384]{1,0:T(8,128)(2,1)S(1)}, bf16[160,384]{1,0:T(8,128)(2,1)S(1)}, u32[]{:S(2)}, u32[]{:S(2)}) collective-permute-start(bf16[160,384]{1,0:T(8,128)(2,1)S(1)} %get-tuple-element.17), channel_id=1, source_target_pairs={{0,8},{1,9},{2,10},{3,11},{4,12},{5,13},{6,14},{7,15},{8,0},{9,1},... | collective-permute-start | bytes 368648 | tf_op jit(solution)/shard_map/ppermute | solution.py:256
  5.3 16.6 %collective-permute-start.7 = (bf16[256,512]{1,0:T(8,128)(2,1)S(1)}, bf16[256,512]{1,0:T(8,128)(2,1)S(1)}, u32[]{:S(2)}, u32[]{:S(2)}) collective-permute-start(bf16[256,512]{1,0:T(8,128)(2,1)S(1)} %get-tuple-element.18.refs_1_), channel_id=1, source_target_pairs={{0,8},{1,9},{2,10},{3,11},{4,12},{5,13},{6,14},{7,15},{8,0},{9,1},... | collective-permute-start | bytes 786440 | tf_op jit(solution)/shard_map/ppermute | solution.py:256
  5.4 16.5 %collective-permute-start.8 = (bf16[256,512]{1,0:T(8,128)(2,1)S(1)}, bf16[256,512]{1,0:T(8,128)(2,1)S(1)}, u32[]{:S(2)}, u32[]{:S(2)}) collective-permute-start(bf16[256,512]{1,0:T(8,128)(2,1)S(1)} %get-tuple-element.19.refs_2_), channel_id=1, source_target_pairs={{0,8},{1,9},{2,10},{3,11},{4,12},{5,13},{6,14},{7,15},{8,0},{9,1},... | collective-permute-start | bytes 786440 | tf_op jit(solution)/shard_map/ppermute | solution.py:256
  7.4 5.8 %collective-permute-start = (bf16[128,384]{1,0:T(8,128)(2,1)S(1)}, bf16[128,384]{1,0:T(8,128)(2,1)S(1)}, u32[]{:S(2)}, u32[]{:S(2)}) collective-permute-start(bf16[128,384]{1,0:T(8,128)(2,1)S(1)} %get-tuple-element.16.refs_0_), channel_id=1, source_target_pairs={{0,2},{1,3},{2,0},{3,1},{4,6},{5,7},{6,4},{7,5},{8,10},{9,11},{10,... | collective-permute-start | bytes 294920 | tf_op jit(solution)/shard_map/ppermute | solution.py:256
  10.0 7.0 %collective-permute-start.1 = (bf16[128,384]{1,0:T(8,128)(2,1)S(1)}, bf16[128,384]{1,0:T(8,128)(2,1)S(1)}, u32[]{:S(2)}, u32[]{:S(2)}) collective-permute-start(bf16[128,384]{1,0:T(8,128)(2,1)S(1)} %get-tuple-element.16.refs_0_), channel_id=1, source_target_pairs={{0,1},{1,0},{2,3},{3,2},{4,5},{5,4},{6,7},{7,6},{8,9},{9,8},{10,11... | collective-permute-start | bytes 294920 | tf_op jit(solution)/shard_map/ppermute | solution.py:256
  11.6 6.8 %collective-permute-start.4 = (bf16[128,384]{1,0:T(8,128)(2,1)S(1)}, bf16[128,384]{1,0:T(8,128)(2,1)S(1)}, u32[]{:S(2)}, u32[]{:S(2)}) collective-permute-start(bf16[128,384]{1,0:T(8,128)(2,1)S(1)} %slice.8.refs_4_), channel_id=1, source_target_pairs={{0,2},{1,3},{2,0},{3,1},{4,6},{5,7},{6,4},{7,5},{8,10},{9,11},{10,... | collective-permute-start | bytes 294920 | tf_op jit(solution)/shard_map/ppermute | solution.py:256
  13.1 7.6 %collective-permute-start.2 = (bf16[128,384]{1,0:T(8,128)(2,1)S(1)}, bf16[128,384]{1,0:T(8,128)(2,1)S(1)}, u32[]{:S(2)}, u32[]{:S(2)}) collective-permute-start(bf16[128,384]{1,0:T(8,128)(2,1)S(1)} %collective-permute-done.refs_1_), channel_id=1, source_target_pairs={{0,1},{1,0},{2,3},{3,2},{4,5},{5,4},{6,7},{7,6},{8,9},{9,8},{10,11... | collective-permute-start | bytes 294920 | tf_op jit(solution)/shard_map/ppermute | solution.py:256
  17.0 5.0 %collective-permute-start.5 = (bf16[128,384]{1,0:T(8,128)(2,1)S(1)}, bf16[128,384]{1,0:T(8,128)(2,1)S(1)}, u32[]{:S(2)}, u32[]{:S(2)}) collective-permute-start(bf16[128,384]{1,0:T(8,128)(2,1)S(1)} %slice.8.refs_4_), channel_id=1, source_target_pairs={{0,1},{1,0},{2,3},{3,2},{4,5},{5,4},{6,7},{7,6},{8,9},{9,8},{10,11... | collective-permute-start | bytes 294920 | tf_op jit(solution)/shard_map/ppermute | solution.py:256
  18.3 4.7 %collective-permute-start.6 = (bf16[128,384]{1,0:T(8,128)(2,1)S(1)}, bf16[128,384]{1,0:T(8,128)(2,1)S(1)}, u32[]{:S(2)}, u32[]{:S(2)}) collective-permute-start(bf16[128,384]{1,0:T(8,128)(2,1)S(1)} %collective-permute-done.4.refs_5_), channel_id=1, source_target_pairs={{0,1},{1,0},{2,3},{3,2},{4,5},{5,4},{6,7},{7,6},{8,9},{9,8},{10,11... | collective-permute-start | bytes 294920 | tf_op jit(solution)/shard_map/ppermute | solution.py:256
  23.1 1.8 %collective-permute-start.9 = (bf16[512,384]{1,0:T(8,128)(2,1)S(1)}, bf16[512,384]{1,0:T(8,128)(2,1)S(1)}, u32[]{:S(2)}, u32[]{:S(2)}) collective-permute-start(bf16[512,384]{1,0:T(8,128)(2,1)S(1)} %get-tuple-element.21.refs_1_), channel_id=1, source_target_pairs={{0,4},{1,5},{2,6},{3,7},{4,0},{5,1},{6,2},{7,3},{8,12},{9,13},{10,... | collective-permute-start | bytes 1179656 | tf_op jit(solution)/shard_map/ppermute | solution.py:256
  24.9 10.4 %collective-permute-start.14 = (f32[512,384]{1,0:T(8,128)S(1)}, f32[512,384]{1,0:T(8,128)S(1)}, u32[]{:S(2)}, u32[]{:S(2)}) collective-permute-start(f32[512,384]{1,0:T(8,128)S(1)} %shard_map.71.refs_0_), channel_id=1, source_target_pairs={{0,4},{1,5},{2,6},{3,7},{4,0},{5,1},{6,2},{7,3},{8,12},{9,13},{10,... | collective-permute-start | bytes 2359304 | tf_op jit(solution)/shard_map/ppermute | solution.py:256
  25.8 1.7 %collective-permute-start.10 = (f32[320,128]{1,0:T(8,128)S(1)}, f32[320,128]{1,0:T(8,128)S(1)}, u32[]{:S(2)}, u32[]{:S(2)}) collective-permute-start(f32[320,128]{1,0:T(8,128)S(1)} %get-tuple-element.24), channel_id=1, source_target_pairs={{0,4},{1,5},{2,6},{3,7},{4,0},{5,1},{6,2},{7,3},{8,12},{9,13},{10,... | collective-permute-start | bytes 491528 | tf_op jit(solution)/shard_map/ppermute | solution.py:256
  27.5 4.6 %collective-permute-start.11 = (f32[160,128]{1,0:T(8,128)S(1)}, f32[160,128]{1,0:T(8,128)S(1)}, u32[]{:S(2)}, u32[]{:S(2)}) collective-permute-start(f32[160,128]{1,0:T(8,128)S(1)} %get-tuple-element.26), channel_id=1, source_target_pairs={{0,16},{1,17},{2,18},{3,19},{4,20},{5,21},{6,22},{7,23},{8,24},{9,... | collective-permute-start | bytes 245768 | tf_op jit(solution)/shard_map/ppermute | solution.py:256
  32.0 6.9 %collective-permute-start.12 = (f32[160,128]{1,0:T(8,128)S(1)}, f32[160,128]{1,0:T(8,128)S(1)}, u32[]{:S(2)}, u32[]{:S(2)}) collective-permute-start(f32[160,128]{1,0:T(8,128)S(1)} %shard_map.74.refs_0_.refs_2_), channel_id=1, source_target_pairs={{0,2},{1,3},{2,0},{3,1},{4,6},{5,7},{6,4},{7,5},{8,10},{9,11},{10,... | collective-permute-start | bytes 245768 | tf_op jit(solution)/shard_map/ppermute | solution.py:256
  35.4 9.7 %collective-permute-start.15 = (bf16[128,384]{1,0:T(8,128)(2,1)S(1)}, bf16[128,384]{1,0:T(8,128)(2,1)S(1)}, u32[]{:S(2)}, u32[]{:S(2)}) collective-permute-start(bf16[128,384]{1,0:T(8,128)(2,1)S(1)} %get-tuple-element.27), channel_id=1, source_target_pairs={{0,0},{1,4},{2,8},{3,12},{4,1},{5,5},{6,9},{7,13},{8,2},{9,6},{10,... | collective-permute-start | bytes 294920 | tf_op jit(solution)/shard_map/ppermute | solution.py:314
  39.0 6.2 %collective-permute-start.13 = (f32[160,128]{1,0:T(8,128)S(1)}, f32[160,128]{1,0:T(8,128)S(1)}, u32[]{:S(2)}, u32[]{:S(2)}) collective-permute-start(f32[160,128]{1,0:T(8,128)S(1)} %shard_map.75.refs_0_), channel_id=1, source_target_pairs={{0,1},{1,0},{2,3},{3,2},{4,5},{5,4},{6,7},{7,6},{8,9},{9,8},{10,11... | collective-permute-start | bytes 245768 | tf_op jit(solution)/shard_map/ppermute | solution.py:256
  39.6 9.1 %collective-permute-start.19 = (bf16[128,384]{1,0:T(8,128)(2,1)S(1)}, bf16[128,384]{1,0:T(8,128)(2,1)S(1)}, u32[]{:S(2)}, u32[]{:S(2)}) collective-permute-start(bf16[128,384]{1,0:T(8,128)(2,1)S(1)} %get-tuple-element.29), channel_id=1, source_target_pairs={{0,2},{1,6},{2,10},{3,14},{4,3},{5,7},{6,11},{7,15},{8,0},{9,4},{1... | collective-permute-start | bytes 294920 | tf_op jit(solution)/shard_map/ppermute | solution.py:314
  45.2 5.6 %collective-permute-start.18 = (f32[160,128]{1,0:T(8,128)S(1)}, f32[160,128]{1,0:T(8,128)S(1)}, u32[]{:S(2)}, u32[]{:S(2)}) collective-permute-start(f32[160,128]{1,0:T(8,128)S(1)} %shard_map.77.refs_0_), channel_id=1, source_target_pairs={{0,24},{1,25},{2,26},{3,27},{4,28},{5,29},{6,30},{7,31},{8,16},{9,... | collective-permute-start | bytes 245768 | tf_op jit(solution)/shard_map/ppermute | solution.py:256
  47.6 4.4 %collective-permute-start.17 = (f32[160,128]{1,0:T(8,128)S(1)}, f32[160,128]{1,0:T(8,128)S(1)}, u32[]{:S(2)}, u32[]{:S(2)}) collective-permute-start(f32[160,128]{1,0:T(8,128)S(1)} %shard_map.77.refs_0_), channel_id=1, source_target_pairs={{0,16},{1,17},{2,18},{3,19},{4,20},{5,21},{6,22},{7,23},{8,24},{9,... | collective-permute-start | bytes 245768 | tf_op jit(solution)/shard_map/ppermute | solution.py:256
  48.1 4.4 %collective-permute-start.16 = (f32[160,128]{1,0:T(8,128)S(1)}, f32[160,128]{1,0:T(8,128)S(1)}, u32[]{:S(2)}, u32[]{:S(2)}) collective-permute-start(f32[160,128]{1,0:T(8,128)S(1)} %shard_map.77.refs_0_), channel_id=1, source_target_pairs={{0,8},{1,9},{2,10},{3,11},{4,12},{5,13},{6,14},{7,15},{8,0},{9,1},... | collective-permute-start | bytes 245768 | tf_op jit(solution)/shard_map/ppermute | solution.py:256
  52.6 1.7 %collective-permute-start.20 = (f32[4,160,128]{2,1,0:T(8,128)S(1)}, f32[4,160,128]{2,1,0:T(8,128)S(1)}, u32[]{:S(2)}, u32[]{:S(2)}) collective-permute-start(f32[4,160,128]{2,1,0:T(8,128)S(1)} %shard_map.79.refs_0_), channel_id=1, source_target_pairs={{0,4},{1,5},{2,6},{3,7},{4,0},{5,1},{6,2},{7,3},{8,12},{9,13},{10,... | collective-permute-start | bytes 983048 | tf_op jit(solution)/shard_map/ppermute | solution.py:256

commit v17 on v16

--- a/solution.py
+++ b/solution.py
@@ -210,6 +210,10 @@
         out[0, :, s, :] = jnp.where(row < limits[s, :1, :1], value, jnp.zeros(value.shape, value.dtype))
 
 
+def add_four_kernel(a, b, c, d, out):
+    out[...] = (a[...] + b[...]) + (c[...] + d[...])
+
+
 def stack_kernel(*refs):
     for index, ref in enumerate(refs[:-1]):
         refs[-1][index] = ref[...]
@@ -305,7 +309,6 @@
         halve_kernel, [part, part], [SMEM] + [VMEM] * 2, quad_weight, keep, swap(send, core=1),
         scratch=[pltpu.VMEM((lines, LANES), f32)],
     )
-    came = swap(send, point=1)
     def deliver(x, flip):
         pairs = []
         for i in range(devices):
@@ -313,16 +316,17 @@
             pairs.append((i, (h * 4 + c) * grid + 2 * (s ^ flip) + k))
         return lax.ppermute(x, AXES, pairs)
 
-    add = functools.partial(call, add_kernel, part, [VMEM] * 2)
-    total = add(keep, came)
+    total = call(
+        add_four_kernel, part, [VMEM] * 4,
+        keep, swap(send, point=1), swap(keep, column=1), swap(send, point=1, column=1),
+    )
     out_near, out_far = call(
         output_kernel, [block, block], [VMEM] * 2, mine, other,
         scratch=[pltpu.VMEM((extent, width), bf16)],
         after=[total],
     )
     near, far = deliver(out_near, 0), deliver(out_far, 1)
-    total = add(total, swap(total, column=2))
-    total = add(total, swap(total, column=1), after=[near])
+    total = call(add_kernel, part, [VMEM] * 2, total, swap(total, column=2))
     quarters = [total, swap(total, side=1), swap(total, point=1), swap(total, side=1, point=1)]
     rows = call(
         rows_kernel, shape((1, height, count, width), bf16), [VMEM] * 3, limits, near, far

time: 55.7 us -> 54.3 us (0.975)
  waiting for transfers between devices: 19.7 us -> 16.2 us
  starting transfers between devices: 29.4 us -> 31.5 us
    ppermute x19 -> x20, waiting for transfers between devices: 19.7 us -> 16.1 us  [swap(): return lax.ppermute(x, AXES, [(i, i ^ mask) for i in range(devices)])]
    ppermute x19 -> x20, starting transfers between devices: 25.3 us -> 26.6 us  [swap(): return lax.ppermute(x, AXES, [(i, i ^ mask) for i in range(devices)])]
    ppermute x2, starting transfers between devices: 4.05 us -> 4.95 us  [deliver(): return lax.ppermute(x, AXES, pairs)]
    pallas_call x13 -> x12, Pallas kernels: 5.02 us -> 5.02 us  [call(): pl.pallas_call(body, out_shape=outs, in_specs=list(specs) + [ANY] * len(a...]
  transfers between devices with their start and end apart: 21 -> 22, of which waited for: 14 -> 13; matrix products, arithmetic and copies ran while one was open for 0% -> 0% of each run, Pallas kernels for 3% -> 4%
where the time goes in v17:
time: 54.3 us; the launch traced here: 54.1 us
  starting transfers between devices  31.5 us (58%)
  waiting for transfers between devices  16.2 us (30%)
  Pallas kernels  5.02 us (9%)
  between operations  1.38 us (3%)
    ppermute x20, starting transfers between devices, swap(): return lax.ppermute(x, AXES, [(i, i ^ mask) for i in range(devices)])  26.6 us
    ppermute x20, waiting for transfers between devices, swap(): return lax.ppermute(x, AXES, [(i, i ^ mask) for i in range(devices)])  16.1 us
    pallas_call x12, Pallas kernels, call(): pl.pallas_call(body, out_shape=outs, in_specs=list(specs) + [ANY] * len(a...  5.02 us
    ppermute x2, starting transfers between devices, deliver(): return lax.ppermute(x, AXES, pairs)  4.95 us
  transfers between devices with their start and end apart: 22, of which 13 were waited for; matrix products, arithmetic and copies ran while one was open for 0% of the time, Pallas kernels for 4%

profile of v17, /device:TPU:0, one launch (start us, length us, event | category | flops | bytes accessed | tf_op | source)
XLA Modules:
  0.0 54.1 jit_solution(14011391723050244796)
XLA Ops:
  0.6 1.7 %shard_map.68 = (bf16[128,384]{1,0:T(8,128)(2,1)S(1)}, bf16[160,384]{1,0:T(8,128)(2,1)S(1)}, bf16[32,384]{1,0:T(8,128)(2,1)S(1)}, s32[2,8,128]{2,1,0:T(8,128)S(1...) custom-call(s32[2]{0:T(128)} %bitcast.1, bf16[1,128,2,384]{3,2,1,0:T(2,128)(2,1)} %refs_1_.1, ...), custom_call_target="tpu_custom_call" | custom-call | tf_op jit(solution)/shard_map/pallas_call | solution.py:28
  2.3 3.0 %collective-permute-start.3 = (bf16[160,384]{1,0:T(8,128)(2,1)S(1)}, bf16[160,384]{1,0:T(8,128)(2,1)S(1)}, u32[]{:S(2)}, u32[]{:S(2)}) collective-permute-start(bf16[160,384]{1,0:T(8,128)(2,1)S(1)} %get-tuple-element.17), channel_id=1, source_target_pairs={{0,8},{1,9},{2,10},{3,11},{4,12},{5,13},{6,14},{7,15},{8,0},{9,1},... | collective-permute-start | bytes 368648 | tf_op jit(solution)/shard_map/ppermute | solution.py:260
  5.4 1.9 %collective-permute-start.8 = (bf16[256,512]{1,0:T(8,128)(2,1)S(1)}, bf16[256,512]{1,0:T(8,128)(2,1)S(1)}, u32[]{:S(2)}, u32[]{:S(2)}) collective-permute-start(bf16[256,512]{1,0:T(8,128)(2,1)S(1)} %get-tuple-element.19.refs_2_), channel_id=1, source_target_pairs={{0,8},{1,9},{2,10},{3,11},{4,12},{5,13},{6,14},{7,15},{8,0},{9,1},... | collective-permute-start | bytes 786440 | tf_op jit(solution)/shard_map/ppermute | solution.py:260
  7.4 2.6 %collective-permute-start = (bf16[128,384]{1,0:T(8,128)(2,1)S(1)}, bf16[128,384]{1,0:T(8,128)(2,1)S(1)}, u32[]{:S(2)}, u32[]{:S(2)}) collective-permute-start(bf16[128,384]{1,0:T(8,128)(2,1)S(1)} %get-tuple-element.16.refs_0_), channel_id=1, source_target_pairs={{0,2},{1,3},{2,0},{3,1},{4,6},{5,7},{6,4},{7,5},{8,10},{9,11},{10,... | collective-permute-start | bytes 294920 | tf_op jit(solution)/shard_map/ppermute | solution.py:260
  10.0 1.6 %collective-permute-start.1 = (bf16[128,384]{1,0:T(8,128)(2,1)S(1)}, bf16[128,384]{1,0:T(8,128)(2,1)S(1)}, u32[]{:S(2)}, u32[]{:S(2)}) collective-permute-start(bf16[128,384]{1,0:T(8,128)(2,1)S(1)} %get-tuple-element.16.refs_0_), channel_id=1, source_target_pairs={{0,1},{1,0},{2,3},{3,2},{4,5},{5,4},{6,7},{7,6},{8,9},{9,8},{10,11... | collective-permute-start | bytes 294920 | tf_op jit(solution)/shard_map/ppermute | solution.py:260
  11.6 1.2 %collective-permute-start.4 = (bf16[128,384]{1,0:T(8,128)(2,1)S(1)}, bf16[128,384]{1,0:T(8,128)(2,1)S(1)}, u32[]{:S(2)}, u32[]{:S(2)}) collective-permute-start(bf16[128,384]{1,0:T(8,128)(2,1)S(1)} %slice.8.refs_4_), channel_id=1, source_target_pairs={{0,2},{1,3},{2,0},{3,1},{4,6},{5,7},{6,4},{7,5},{8,10},{9,11},{10,... | collective-permute-start | bytes 294920 | tf_op jit(solution)/shard_map/ppermute | solution.py:260
  13.1 3.8 %collective-permute-start.2 = (bf16[128,384]{1,0:T(8,128)(2,1)S(1)}, bf16[128,384]{1,0:T(8,128)(2,1)S(1)}, u32[]{:S(2)}, u32[]{:S(2)}) collective-permute-start(bf16[128,384]{1,0:T(8,128)(2,1)S(1)} %collective-permute-done.refs_1_), channel_id=1, source_target_pairs={{0,1},{1,0},{2,3},{3,2},{4,5},{5,4},{6,7},{7,6},{8,9},{9,8},{10,11... | collective-permute-start | bytes 294920 | tf_op jit(solution)/shard_map/ppermute | solution.py:260
  17.0 0.7 %collective-permute-start.5 = (bf16[128,384]{1,0:T(8,128)(2,1)S(1)}, bf16[128,384]{1,0:T(8,128)(2,1)S(1)}, u32[]{:S(2)}, u32[]{:S(2)}) collective-permute-start(bf16[128,384]{1,0:T(8,128)(2,1)S(1)} %slice.8.refs_4_), channel_id=1, source_target_pairs={{0,1},{1,0},{2,3},{3,2},{4,5},{5,4},{6,7},{7,6},{8,9},{9,8},{10,11... | collective-permute-start | bytes 294920 | tf_op jit(solution)/shard_map/ppermute | solution.py:260
  17.7 0.6 %collective-permute-done.4.refs_5_ = bf16[128,384]{1,0:T(8,128)(2,1)S(1)} collective-permute-done((bf16[128,384]{1,0:T(8,128)(2,1)S(1)}, bf16[128,384]{1,0:T(8,128)(2,1)S(1)}, u32[]{:S(2)}, u32[]{:S(2)}) %collective-permute-start.4) | collective-permute-done | bytes 98336 | tf_op jit(solution)/shard_map/ppermute | solution.py:260
  18.3 0.7 %collective-permute-start.6 = (bf16[128,384]{1,0:T(8,128)(2,1)S(1)}, bf16[128,384]{1,0:T(8,128)(2,1)S(1)}, u32[]{:S(2)}, u32[]{:S(2)}) collective-permute-start(bf16[128,384]{1,0:T(8,128)(2,1)S(1)} %collective-permute-done.4.refs_5_), channel_id=1, source_target_pairs={{0,1},{1,0},{2,3},{3,2},{4,5},{5,4},{6,7},{7,6},{8,9},{9,8},{10,11... | collective-permute-start | bytes 294920 | tf_op jit(solution)/shard_map/ppermute | solution.py:260
  19.0 1.6 %collective-permute-done.2.refs_3_ = bf16[128,384]{1,0:T(8,128)(2,1)S(1)} collective-permute-done((bf16[128,384]{1,0:T(8,128)(2,1)S(1)}, bf16[128,384]{1,0:T(8,128)(2,1)S(1)}, u32[]{:S(2)}, u32[]{:S(2)}) %collective-permute-start.2) | collective-permute-done | bytes 98336 | tf_op jit(solution)/shard_map/ppermute | solution.py:260
  20.7 1.3 %collective-permute-done.5.refs_6_ = bf16[128,384]{1,0:T(8,128)(2,1)S(1)} collective-permute-done((bf16[128,384]{1,0:T(8,128)(2,1)S(1)}, bf16[128,384]{1,0:T(8,128)(2,1)S(1)}, u32[]{:S(2)}, u32[]{:S(2)}) %collective-permute-start.5) | collective-permute-done | bytes 98336 | tf_op jit(solution)/shard_map/ppermute | solution.py:260
  22.0 1.0 %collective-permute-done.6.refs_7_ = bf16[128,384]{1,0:T(8,128)(2,1)S(1)} collective-permute-done((bf16[128,384]{1,0:T(8,128)(2,1)S(1)}, bf16[128,384]{1,0:T(8,128)(2,1)S(1)}, u32[]{:S(2)}, u32[]{:S(2)}) %collective-permute-start.6) | collective-permute-done | bytes 98336 | tf_op jit(solution)/shard_map/ppermute | solution.py:260
  23.2 0.7 %shard_map.70.refs_0_ = f32[512,384]{1,0:T(8,128)S(1)} custom-call(bf16[2,512,384]{2,1,0:T(8,128)(2,1)S(1)} %get-tuple-element.20.refs_0_, bf16[256,512]{1,0:T(8,128)(2,1)S(1)} %get-tuple-element.18.refs_1_, bf16[256,512]{1,0:T(8,128)(2,1)S(1)} %get-tuple-element.19.refs_2_, bf16[256,512]{1,0:T(8,128)(2,1)S(1)} %collective-permute-done.7.refs_8_.refs_3_, ...), custom_call_target="tpu_custom_call" | custom-call | tf_op jit(solution)/shard_map/pallas_call | solution.py:28
  23.9 1.0 %collective-permute-done.9.refs_1_.refs_2_ = bf16[512,384]{1,0:T(8,128)(2,1)S(1)} collective-permute-done((bf16[512,384]{1,0:T(8,128)(2,1)S(1)}, bf16[512,384]{1,0:T(8,128)(2,1)S(1)}, u32[]{:S(2)}, u32[]{:S(2)}) %collective-permute-start.9) | collective-permute-done | bytes 393248 | tf_op jit(solution)/shard_map/ppermute | solution.py:260
  25.1 0.7 %shard_map.72 = (f32[320,128]{1,0:T(8,128)S(1)}, f32[320,128]{1,0:T(8,128)S(1)}) custom-call(f32[512,384]{1,0:T(8,128)S(1)} %shard_map.71.refs_0_, bf16[512,384]{1,0:T(8,128)(2,1)S(1)} %get-tuple-element.21.refs_1_, bf16[512,384]{1,0:T(8,128)(2,1)S(1)} %collective-permute-done.9.refs_1_.refs_2_, bf16[32,384]{1,0:T(8,128)(2,1)S(1)} %get-tuple-element.22.refs_3_, ...), custom_call_target="tpu_custom_call" | custom-call | tf_op jit(solution)/shard_map/pallas_call | solution.py:28
  25.8 0.4 collective-permute-start.10
  26.8 0.6 %collective-permute-done.10.refs_2_ = f32[320,128]{1,0:T(8,128)S(1)} collective-permute-done((f32[320,128]{1,0:T(8,128)S(1)}, f32[320,128]{1,0:T(8,128)S(1)}, u32[]{:S(2)}, u32[]{:S(2)}) %collective-permute-start.10) | collective-permute-done | bytes 163872 | tf_op jit(solution)/shard_map/ppermute | solution.py:260
  27.5 1.5 %collective-permute-start.12 = (f32[160,128]{1,0:T(8,128)S(1)}, f32[160,128]{1,0:T(8,128)S(1)}, u32[]{:S(2)}, u32[]{:S(2)}) collective-permute-start(f32[160,128]{1,0:T(8,128)S(1)} %get-tuple-element.25.refs_0_), channel_id=1, source_target_pairs={{0,1},{1,0},{2,3},{3,2},{4,5},{5,4},{6,7},{7,6},{8,9},{9,8},{10,11... | collective-permute-start | bytes 245768 | tf_op jit(solution)/shard_map/ppermute | solution.py:260
  29.0 1.6 %collective-permute-start.13 = (f32[160,128]{1,0:T(8,128)S(1)}, f32[160,128]{1,0:T(8,128)S(1)}, u32[]{:S(2)}, u32[]{:S(2)}) collective-permute-start(f32[160,128]{1,0:T(8,128)S(1)} %get-tuple-element.26), channel_id=1, source_target_pairs={{0,17},{1,16},{2,19},{3,18},{4,21},{5,20},{6,23},{7,22},{8,25},{9,... | collective-permute-start | bytes 245768 | tf_op jit(solution)/shard_map/ppermute | solution.py:260
  30.5 0.5 collective-permute-start.11
  31.0 1.0 %collective-permute-done.12.refs_2_ = f32[160,128]{1,0:T(8,128)S(1)} collective-permute-done((f32[160,128]{1,0:T(8,128)S(1)}, f32[160,128]{1,0:T(8,128)S(1)}, u32[]{:S(2)}, u32[]{:S(2)}) %collective-permute-start.12) | collective-permute-done | bytes 81952 | tf_op jit(solution)/shard_map/ppermute | solution.py:260
  32.0 2.8 %collective-permute-done.13.refs_3_ = f32[160,128]{1,0:T(8,128)S(1)} collective-permute-done((f32[160,128]{1,0:T(8,128)S(1)}, f32[160,128]{1,0:T(8,128)S(1)}, u32[]{:S(2)}, u32[]{:S(2)}) %collective-permute-start.13) | collective-permute-done | bytes 81952 | tf_op jit(solution)/shard_map/ppermute | solution.py:260
  34.8 1.2 %collective-permute-done.11.refs_1_ = f32[160,128]{1,0:T(8,128)S(1)} collective-permute-done((f32[160,128]{1,0:T(8,128)S(1)}, f32[160,128]{1,0:T(8,128)S(1)}, u32[]{:S(2)}, u32[]{:S(2)}) %collective-permute-start.11) | collective-permute-done | bytes 81952 | tf_op jit(solution)/shard_map/ppermute | solution.py:260
  36.0 3.2 %collective-permute-start.14 = (f32[160,128]{1,0:T(8,128)S(1)}, f32[160,128]{1,0:T(8,128)S(1)}, u32[]{:S(2)}, u32[]{:S(2)}) collective-permute-start(f32[160,128]{1,0:T(8,128)S(1)} %shard_map.74.refs_0_.refs_2_), channel_id=1, source_target_pairs={{0,2},{1,3},{2,0},{3,1},{4,6},{5,7},{6,4},{7,5},{8,10},{9,11},{10,... | collective-permute-start | bytes 245768 | tf_op jit(solution)/shard_map/ppermute | solution.py:260
  39.4 0.7 %collective-permute-start.19 = (bf16[128,384]{1,0:T(8,128)(2,1)S(1)}, bf16[128,384]{1,0:T(8,128)(2,1)S(1)}, u32[]{:S(2)}, u32[]{:S(2)}) collective-permute-start(bf16[128,384]{1,0:T(8,128)(2,1)S(1)} %get-tuple-element.28), channel_id=1, source_target_pairs={{0,0},{1,4},{2,8},{3,12},{4,1},{5,5},{6,9},{7,13},{8,2},{9,6},{10,... | collective-permute-start | bytes 294920 | tf_op jit(solution)/shard_map/ppermute | solution.py:317
  40.1 4.3 %collective-permute-start.20 = (bf16[128,384]{1,0:T(8,128)(2,1)S(1)}, bf16[128,384]{1,0:T(8,128)(2,1)S(1)}, u32[]{:S(2)}, u32[]{:S(2)}) collective-permute-start(bf16[128,384]{1,0:T(8,128)(2,1)S(1)} %get-tuple-element.29), channel_id=1, source_target_pairs={{0,2},{1,6},{2,10},{3,14},{4,3},{5,7},{6,11},{7,15},{8,0},{9,4},{1... | collective-permute-start | bytes 294920 | tf_op jit(solution)/shard_map/ppermute | solution.py:317
  44.5 1.0 %collective-permute-start.16 = (f32[160,128]{1,0:T(8,128)S(1)}, f32[160,128]{1,0:T(8,128)S(1)}, u32[]{:S(2)}, u32[]{:S(2)}) collective-permute-start(f32[160,128]{1,0:T(8,128)S(1)} %shard_map.75.refs_0_), channel_id=1, source_target_pairs={{0,16},{1,17},{2,18},{3,19},{4,20},{5,21},{6,22},{7,23},{8,24},{9,... | collective-permute-start | bytes 245768 | tf_op jit(solution)/shard_map/ppermute | solution.py:260
  45.5 2.5 %collective-permute-start.15 = (f32[160,128]{1,0:T(8,128)S(1)}, f32[160,128]{1,0:T(8,128)S(1)}, u32[]{:S(2)}, u32[]{:S(2)}) collective-permute-start(f32[160,128]{1,0:T(8,128)S(1)} %shard_map.75.refs_0_), channel_id=1, source_target_pairs={{0,8},{1,9},{2,10},{3,11},{4,12},{5,13},{6,14},{7,15},{8,0},{9,1},... | collective-permute-start | bytes 245768 | tf_op jit(solution)/shard_map/ppermute | solution.py:260
  48.2 2.8 %collective-permute-done.17.refs_3_ = f32[160,128]{1,0:T(8,128)S(1)} collective-permute-done((f32[160,128]{1,0:T(8,128)S(1)}, f32[160,128]{1,0:T(8,128)S(1)}, u32[]{:S(2)}, u32[]{:S(2)}) %collective-permute-start.17) | collective-permute-done | bytes 81952 | tf_op jit(solution)/shard_map/ppermute | solution.py:260
  51.2 1.6 %collective-permute-done.21.refs_1_ = f32[4,160,128]{2,1,0:T(8,128)S(1)} collective-permute-done((f32[4,160,128]{2,1,0:T(8,128)S(1)}, f32[4,160,128]{2,1,0:T(8,128)S(1)}, u32[]{:S(2)}, u32[]{:S(2)}) %collective-permute-start.21) | collective-permute-done | bytes 327712 | tf_op jit(solution)/shard_map/ppermute | solution.py:260
  52.9 1.3 %shard_map.79 = (bf16[1,128,2,384]{3,2,1,0:T(2,128)(2,1)}, f32[2,384,384]{2,1,0:T(8,128)}) custom-call(f32[4,160,128]{2,1,0:T(8,128)S(1)} %shard_map.78.refs_0_, f32[4,160,128]{2,1,0:T(8,128)S(1)} %collective-permute-done.21.refs_1_, bf16[1,128,2,384]{3,2,1,0:T(2,128)(2,1)S(1)} %shard_map.77.refs_4_.refs_2_), custom_call_target="tpu_custom_call" | custom-call | tf_op jit(solution)/shard_map/pallas_call | solution.py:28
  (26 shorter events, 1.6 us)
Async XLA Ops:
  2.3 9.2 %collective-permute-start.3 = (bf16[160,384]{1,0:T(8,128)(2,1)S(1)}, bf16[160,384]{1,0:T(8,128)(2,1)S(1)}, u32[]{:S(2)}, u32[]{:S(2)}) collective-permute-start(bf16[160,384]{1,0:T(8,128)(2,1)S(1)} %get-tuple-element.17), channel_id=1, source_target_pairs={{0,8},{1,9},{2,10},{3,11},{4,12},{5,13},{6,14},{7,15},{8,0},{9,1},... | collective-permute-start | bytes 368648 | tf_op jit(solution)/shard_map/ppermute | solution.py:260
  5.3 16.6 %collective-permute-start.7 = (bf16[256,512]{1,0:T(8,128)(2,1)S(1)}, bf16[256,512]{1,0:T(8,128)(2,1)S(1)}, u32[]{:S(2)}, u32[]{:S(2)}) collective-permute-start(bf16[256,512]{1,0:T(8,128)(2,1)S(1)} %get-tuple-element.18.refs_1_), channel_id=1, source_target_pairs={{0,8},{1,9},{2,10},{3,11},{4,12},{5,13},{6,14},{7,15},{8,0},{9,1},... | collective-permute-start | bytes 786440 | tf_op jit(solution)/shard_map/ppermute | solution.py:260
  5.4 16.5 %collective-permute-start.8 = (bf16[256,512]{1,0:T(8,128)(2,1)S(1)}, bf16[256,512]{1,0:T(8,128)(2,1)S(1)}, u32[]{:S(2)}, u32[]{:S(2)}) collective-permute-start(bf16[256,512]{1,0:T(8,128)(2,1)S(1)} %get-tuple-element.19.refs_2_), channel_id=1, source_target_pairs={{0,8},{1,9},{2,10},{3,11},{4,12},{5,13},{6,14},{7,15},{8,0},{9,1},... | collective-permute-start | bytes 786440 | tf_op jit(solution)/shard_map/ppermute | solution.py:260
  7.4 5.8 %collective-permute-start = (bf16[128,384]{1,0:T(8,128)(2,1)S(1)}, bf16[128,384]{1,0:T(8,128)(2,1)S(1)}, u32[]{:S(2)}, u32[]{:S(2)}) collective-permute-start(bf16[128,384]{1,0:T(8,128)(2,1)S(1)} %get-tuple-element.16.refs_0_), channel_id=1, source_target_pairs={{0,2},{1,3},{2,0},{3,1},{4,6},{5,7},{6,4},{7,5},{8,10},{9,11},{10,... | collective-permute-start | bytes 294920 | tf_op jit(solution)/shard_map/ppermute | solution.py:260
  10.0 7.0 %collective-permute-start.1 = (bf16[128,384]{1,0:T(8,128)(2,1)S(1)}, bf16[128,384]{1,0:T(8,128)(2,1)S(1)}, u32[]{:S(2)}, u32[]{:S(2)}) collective-permute-start(bf16[128,384]{1,0:T(8,128)(2,1)S(1)} %get-tuple-element.16.refs_0_), channel_id=1, source_target_pairs={{0,1},{1,0},{2,3},{3,2},{4,5},{5,4},{6,7},{7,6},{8,9},{9,8},{10,11... | collective-permute-start | bytes 294920 | tf_op jit(solution)/shard_map/ppermute | solution.py:260
  11.6 6.8 %collective-permute-start.4 = (bf16[128,384]{1,0:T(8,128)(2,1)S(1)}, bf16[128,384]{1,0:T(8,128)(2,1)S(1)}, u32[]{:S(2)}, u32[]{:S(2)}) collective-permute-start(bf16[128,384]{1,0:T(8,128)(2,1)S(1)} %slice.8.refs_4_), channel_id=1, source_target_pairs={{0,2},{1,3},{2,0},{3,1},{4,6},{5,7},{6,4},{7,5},{8,10},{9,11},{10,... | collective-permute-start | bytes 294920 | tf_op jit(solution)/shard_map/ppermute | solution.py:260
  13.1 7.6 %collective-permute-start.2 = (bf16[128,384]{1,0:T(8,128)(2,1)S(1)}, bf16[128,384]{1,0:T(8,128)(2,1)S(1)}, u32[]{:S(2)}, u32[]{:S(2)}) collective-permute-start(bf16[128,384]{1,0:T(8,128)(2,1)S(1)} %collective-permute-done.refs_1_), channel_id=1, source_target_pairs={{0,1},{1,0},{2,3},{3,2},{4,5},{5,4},{6,7},{7,6},{8,9},{9,8},{10,11... | collective-permute-start | bytes 294920 | tf_op jit(solution)/shard_map/ppermute | solution.py:260
  17.0 5.0 %collective-permute-start.5 = (bf16[128,384]{1,0:T(8,128)(2,1)S(1)}, bf16[128,384]{1,0:T(8,128)(2,1)S(1)}, u32[]{:S(2)}, u32[]{:S(2)}) collective-permute-start(bf16[128,384]{1,0:T(8,128)(2,1)S(1)} %slice.8.refs_4_), channel_id=1, source_target_pairs={{0,1},{1,0},{2,3},{3,2},{4,5},{5,4},{6,7},{7,6},{8,9},{9,8},{10,11... | collective-permute-start | bytes 294920 | tf_op jit(solution)/shard_map/ppermute | solution.py:260
  18.3 4.7 %collective-permute-start.6 = (bf16[128,384]{1,0:T(8,128)(2,1)S(1)}, bf16[128,384]{1,0:T(8,128)(2,1)S(1)}, u32[]{:S(2)}, u32[]{:S(2)}) collective-permute-start(bf16[128,384]{1,0:T(8,128)(2,1)S(1)} %collective-permute-done.4.refs_5_), channel_id=1, source_target_pairs={{0,1},{1,0},{2,3},{3,2},{4,5},{5,4},{6,7},{7,6},{8,9},{9,8},{10,11... | collective-permute-start | bytes 294920 | tf_op jit(solution)/shard_map/ppermute | solution.py:260
  23.1 1.8 %collective-permute-start.9 = (bf16[512,384]{1,0:T(8,128)(2,1)S(1)}, bf16[512,384]{1,0:T(8,128)(2,1)S(1)}, u32[]{:S(2)}, u32[]{:S(2)}) collective-permute-start(bf16[512,384]{1,0:T(8,128)(2,1)S(1)} %get-tuple-element.21.refs_1_), channel_id=1, source_target_pairs={{0,4},{1,5},{2,6},{3,7},{4,0},{5,1},{6,2},{7,3},{8,12},{9,13},{10,... | collective-permute-start | bytes 1179656 | tf_op jit(solution)/shard_map/ppermute | solution.py:260
  24.9 14.3 %collective-permute-start.18 = (f32[512,384]{1,0:T(8,128)S(1)}, f32[512,384]{1,0:T(8,128)S(1)}, u32[]{:S(2)}, u32[]{:S(2)}) collective-permute-start(f32[512,384]{1,0:T(8,128)S(1)} %shard_map.71.refs_0_), channel_id=1, source_target_pairs={{0,4},{1,5},{2,6},{3,7},{4,0},{5,1},{6,2},{7,3},{8,12},{9,13},{10,... | collective-permute-start | bytes 2359304 | tf_op jit(solution)/shard_map/ppermute | solution.py:260
  25.8 1.7 %collective-permute-start.10 = (f32[320,128]{1,0:T(8,128)S(1)}, f32[320,128]{1,0:T(8,128)S(1)}, u32[]{:S(2)}, u32[]{:S(2)}) collective-permute-start(f32[320,128]{1,0:T(8,128)S(1)} %get-tuple-element.24), channel_id=1, source_target_pairs={{0,4},{1,5},{2,6},{3,7},{4,0},{5,1},{6,2},{7,3},{8,12},{9,13},{10,... | collective-permute-start | bytes 491528 | tf_op jit(solution)/shard_map/ppermute | solution.py:260
  27.5 4.6 %collective-permute-start.12 = (f32[160,128]{1,0:T(8,128)S(1)}, f32[160,128]{1,0:T(8,128)S(1)}, u32[]{:S(2)}, u32[]{:S(2)}) collective-permute-start(f32[160,128]{1,0:T(8,128)S(1)} %get-tuple-element.25.refs_0_), channel_id=1, source_target_pairs={{0,1},{1,0},{2,3},{3,2},{4,5},{5,4},{6,7},{7,6},{8,9},{9,8},{10,11... | collective-permute-start | bytes 245768 | tf_op jit(solution)/shard_map/ppermute | solution.py:260
  29.0 5.9 %collective-permute-start.13 = (f32[160,128]{1,0:T(8,128)S(1)}, f32[160,128]{1,0:T(8,128)S(1)}, u32[]{:S(2)}, u32[]{:S(2)}) collective-permute-start(f32[160,128]{1,0:T(8,128)S(1)} %get-tuple-element.26), channel_id=1, source_target_pairs={{0,17},{1,16},{2,19},{3,18},{4,21},{5,20},{6,23},{7,22},{8,25},{9,... | collective-permute-start | bytes 245768 | tf_op jit(solution)/shard_map/ppermute | solution.py:260
  30.5 5.5 %collective-permute-start.11 = (f32[160,128]{1,0:T(8,128)S(1)}, f32[160,128]{1,0:T(8,128)S(1)}, u32[]{:S(2)}, u32[]{:S(2)}) collective-permute-start(f32[160,128]{1,0:T(8,128)S(1)} %get-tuple-element.26), channel_id=1, source_target_pairs={{0,16},{1,17},{2,18},{3,19},{4,20},{5,21},{6,22},{7,23},{8,24},{9,... | collective-permute-start | bytes 245768 | tf_op jit(solution)/shard_map/ppermute | solution.py:260
  36.0 8.3 %collective-permute-start.14 = (f32[160,128]{1,0:T(8,128)S(1)}, f32[160,128]{1,0:T(8,128)S(1)}, u32[]{:S(2)}, u32[]{:S(2)}) collective-permute-start(f32[160,128]{1,0:T(8,128)S(1)} %shard_map.74.refs_0_.refs_2_), channel_id=1, source_target_pairs={{0,2},{1,3},{2,0},{3,1},{4,6},{5,7},{6,4},{7,5},{8,10},{9,11},{10,... | collective-permute-start | bytes 245768 | tf_op jit(solution)/shard_map/ppermute | solution.py:260
  39.4 8.5 %collective-permute-start.19 = (bf16[128,384]{1,0:T(8,128)(2,1)S(1)}, bf16[128,384]{1,0:T(8,128)(2,1)S(1)}, u32[]{:S(2)}, u32[]{:S(2)}) collective-permute-start(bf16[128,384]{1,0:T(8,128)(2,1)S(1)} %get-tuple-element.28), channel_id=1, source_target_pairs={{0,0},{1,4},{2,8},{3,12},{4,1},{5,5},{6,9},{7,13},{8,2},{9,6},{10,... | collective-permute-start | bytes 294920 | tf_op jit(solution)/shard_map/ppermute | solution.py:317
  40.1 7.9 %collective-permute-start.20 = (bf16[128,384]{1,0:T(8,128)(2,1)S(1)}, bf16[128,384]{1,0:T(8,128)(2,1)S(1)}, u32[]{:S(2)}, u32[]{:S(2)}) collective-permute-start(bf16[128,384]{1,0:T(8,128)(2,1)S(1)} %get-tuple-element.29), channel_id=1, source_target_pairs={{0,2},{1,6},{2,10},{3,14},{4,3},{5,7},{6,11},{7,15},{8,0},{9,4},{1... | collective-permute-start | bytes 294920 | tf_op jit(solution)/shard_map/ppermute | solution.py:317
  44.4 6.7 %collective-permute-start.17 = (f32[160,128]{1,0:T(8,128)S(1)}, f32[160,128]{1,0:T(8,128)S(1)}, u32[]{:S(2)}, u32[]{:S(2)}) collective-permute-start(f32[160,128]{1,0:T(8,128)S(1)} %shard_map.75.refs_0_), channel_id=1, source_target_pairs={{0,24},{1,25},{2,26},{3,27},{4,28},{5,29},{6,30},{7,31},{8,16},{9,... | collective-permute-start | bytes 245768 | tf_op jit(solution)/shard_map/ppermute | solution.py:260
  44.5 6.6 %collective-permute-start.16 = (f32[160,128]{1,0:T(8,128)S(1)}, f32[160,128]{1,0:T(8,128)S(1)}, u32[]{:S(2)}, u32[]{:S(2)}) collective-permute-start(f32[160,128]{1,0:T(8,128)S(1)} %shard_map.75.refs_0_), channel_id=1, source_target_pairs={{0,16},{1,17},{2,18},{3,19},{4,20},{5,21},{6,22},{7,23},{8,24},{9,... | collective-permute-start | bytes 245768 | tf_op jit(solution)/shard_map/ppermute | solution.py:260
  45.5 5.7 %collective-permute-start.15 = (f32[160,128]{1,0:T(8,128)S(1)}, f32[160,128]{1,0:T(8,128)S(1)}, u32[]{:S(2)}, u32[]{:S(2)}) collective-permute-start(f32[160,128]{1,0:T(8,128)S(1)} %shard_map.75.refs_0_), channel_id=1, source_target_pairs={{0,8},{1,9},{2,10},{3,11},{4,12},{5,13},{6,14},{7,15},{8,0},{9,1},... | collective-permute-start | bytes 245768 | tf_op jit(solution)/shard_map/ppermute | solution.py:260
  51.2 1.7 %collective-permute-start.21 = (f32[4,160,128]{2,1,0:T(8,128)S(1)}, f32[4,160,128]{2,1,0:T(8,128)S(1)}, u32[]{:S(2)}, u32[]{:S(2)}) collective-permute-start(f32[4,160,128]{2,1,0:T(8,128)S(1)} %shard_map.78.refs_0_), channel_id=1, source_target_pairs={{0,4},{1,5},{2,6},{3,7},{4,0},{5,1},{6,2},{7,3},{8,12},{9,13},{10,... | collective-permute-start | bytes 983048 | tf_op jit(solution)/shard_map/ppermute | solution.py:260

commit v18 on v17

--- a/solution.py
+++ b/solution.py
@@ -323,10 +323,10 @@
     out_near, out_far = call(
         output_kernel, [block, block], [VMEM] * 2, mine, other,
         scratch=[pltpu.VMEM((extent, width), bf16)],
-        after=[total],
+        after=[keep],
     )
     near, far = deliver(out_near, 0), deliver(out_far, 1)
-    total = call(add_kernel, part, [VMEM] * 2, total, swap(total, column=2))
+    total = call(add_kernel, part, [VMEM] * 2, total, swap(total, column=2), after=[near])
     quarters = [total, swap(total, side=1), swap(total, point=1), swap(total, side=1, point=1)]
     rows = call(
         rows_kernel, shape((1, height, count, width), bf16), [VMEM] * 3, limits, near, far

time: 54.3 us -> 55.9 us (1.029)
  waiting for transfers between devices: 16.2 us -> 21.6 us
  starting transfers between devices: 31.5 us -> 27.8 us
    ppermute x20, waiting for transfers between devices: 16.1 us -> 21.6 us  [swap(): return lax.ppermute(x, AXES, [(i, i ^ mask) for i in range(devices)])]
    ppermute x2, starting transfers between devices: 4.95 us -> 0.73 us  [deliver(): return lax.ppermute(x, AXES, pairs)]
  transfers between devices with their start and end apart: 22 -> 22, of which waited for: 13 -> 15; matrix products, arithmetic and copies ran while one was open for 0% -> 0% of each run, Pallas kernels for 4% -> 3%
where the time goes in v18:
time: 55.9 us; the launch traced here: 55.7 us
  starting transfers between devices  27.8 us (50%)
  waiting for transfers between devices  21.6 us (39%)
  Pallas kernels  5.02 us (9%)
  between operations  1.37 us (2%)
    ppermute x20, starting transfers between devices, swap(): return lax.ppermute(x, AXES, [(i, i ^ mask) for i in range(devices)])  27 us
    ppermute x20, waiting for transfers between devices, swap(): return lax.ppermute(x, AXES, [(i, i ^ mask) for i in range(devices)])  21.6 us
    pallas_call x12, Pallas kernels, call(): pl.pallas_call(body, out_shape=outs, in_specs=list(specs) + [ANY] * len(a...  5.02 us
  transfers between devices with their start and end apart: 22, of which 15 were waited for; matrix products, arithmetic and copies ran while one was open for 0% of the time, Pallas kernels for 3%

profile of v18, /device:TPU:0, one launch (start us, length us, event | category | flops | bytes accessed | tf_op | source)
XLA Modules:
  0.0 55.7 jit_solution(3131336122240351695)
XLA Ops:
  0.6 1.7 %shard_map.68 = (bf16[128,384]{1,0:T(8,128)(2,1)S(1)}, bf16[160,384]{1,0:T(8,128)(2,1)S(1)}, bf16[32,384]{1,0:T(8,128)(2,1)S(1)}, s32[2,8,128]{2,1,0:T(8,128)S(1...) custom-call(s32[2]{0:T(128)} %bitcast.1, bf16[1,128,2,384]{3,2,1,0:T(2,128)(2,1)} %refs_1_.1, ...), custom_call_target="tpu_custom_call" | custom-call | tf_op jit(solution)/shard_map/pallas_call | solution.py:28
  2.3 3.0 %collective-permute-start.3 = (bf16[160,384]{1,0:T(8,128)(2,1)S(1)}, bf16[160,384]{1,0:T(8,128)(2,1)S(1)}, u32[]{:S(2)}, u32[]{:S(2)}) collective-permute-start(bf16[160,384]{1,0:T(8,128)(2,1)S(1)} %get-tuple-element.17), channel_id=1, source_target_pairs={{0,8},{1,9},{2,10},{3,11},{4,12},{5,13},{6,14},{7,15},{8,0},{9,1},... | collective-permute-start | bytes 368648 | tf_op jit(solution)/shard_map/ppermute | solution.py:260
  5.4 1.9 %collective-permute-start.8 = (bf16[256,512]{1,0:T(8,128)(2,1)S(1)}, bf16[256,512]{1,0:T(8,128)(2,1)S(1)}, u32[]{:S(2)}, u32[]{:S(2)}) collective-permute-start(bf16[256,512]{1,0:T(8,128)(2,1)S(1)} %get-tuple-element.19.refs_2_), channel_id=1, source_target_pairs={{0,8},{1,9},{2,10},{3,11},{4,12},{5,13},{6,14},{7,15},{8,0},{9,1},... | collective-permute-start | bytes 786440 | tf_op jit(solution)/shard_map/ppermute | solution.py:260
  7.4 2.6 %collective-permute-start = (bf16[128,384]{1,0:T(8,128)(2,1)S(1)}, bf16[128,384]{1,0:T(8,128)(2,1)S(1)}, u32[]{:S(2)}, u32[]{:S(2)}) collective-permute-start(bf16[128,384]{1,0:T(8,128)(2,1)S(1)} %get-tuple-element.16.refs_0_), channel_id=1, source_target_pairs={{0,2},{1,3},{2,0},{3,1},{4,6},{5,7},{6,4},{7,5},{8,10},{9,11},{10,... | collective-permute-start | bytes 294920 | tf_op jit(solution)/shard_map/ppermute | solution.py:260
  10.0 1.6 %collective-permute-start.1 = (bf16[128,384]{1,0:T(8,128)(2,1)S(1)}, bf16[128,384]{1,0:T(8,128)(2,1)S(1)}, u32[]{:S(2)}, u32[]{:S(2)}) collective-permute-start(bf16[128,384]{1,0:T(8,128)(2,1)S(1)} %get-tuple-element.16.refs_0_), channel_id=1, source_target_pairs={{0,1},{1,0},{2,3},{3,2},{4,5},{5,4},{6,7},{7,6},{8,9},{9,8},{10,11... | collective-permute-start | bytes 294920 | tf_op jit(solution)/shard_map/ppermute | solution.py:260
  11.6 1.2 %collective-permute-start.4 = (bf16[128,384]{1,0:T(8,128)(2,1)S(1)}, bf16[128,384]{1,0:T(8,128)(2,1)S(1)}, u32[]{:S(2)}, u32[]{:S(2)}) collective-permute-start(bf16[128,384]{1,0:T(8,128)(2,1)S(1)} %slice.8.refs_4_), channel_id=1, source_target_pairs={{0,2},{1,3},{2,0},{3,1},{4,6},{5,7},{6,4},{7,5},{8,10},{9,11},{10,... | collective-permute-start | bytes 294920 | tf_op jit(solution)/shard_map/ppermute | solution.py:260
  13.1 3.8 %collective-permute-start.2 = (bf16[128,384]{1,0:T(8,128)(2,1)S(1)}, bf16[128,384]{1,0:T(8,128)(2,1)S(1)}, u32[]{:S(2)}, u32[]{:S(2)}) collective-permute-start(bf16[128,384]{1,0:T(8,128)(2,1)S(1)} %collective-permute-done.refs_1_), channel_id=1, source_target_pairs={{0,1},{1,0},{2,3},{3,2},{4,5},{5,4},{6,7},{7,6},{8,9},{9,8},{10,11... | collective-permute-start | bytes 294920 | tf_op jit(solution)/shard_map/ppermute | solution.py:260
  17.0 0.7 %collective-permute-start.5 = (bf16[128,384]{1,0:T(8,128)(2,1)S(1)}, bf16[128,384]{1,0:T(8,128)(2,1)S(1)}, u32[]{:S(2)}, u32[]{:S(2)}) collective-permute-start(bf16[128,384]{1,0:T(8,128)(2,1)S(1)} %slice.8.refs_4_), channel_id=1, source_target_pairs={{0,1},{1,0},{2,3},{3,2},{4,5},{5,4},{6,7},{7,6},{8,9},{9,8},{10,11... | collective-permute-start | bytes 294920 | tf_op jit(solution)/shard_map/ppermute | solution.py:260
  17.7 0.6 %collective-permute-done.4.refs_5_ = bf16[128,384]{1,0:T(8,128)(2,1)S(1)} collective-permute-done((bf16[128,384]{1,0:T(8,128)(2,1)S(1)}, bf16[128,384]{1,0:T(8,128)(2,1)S(1)}, u32[]{:S(2)}, u32[]{:S(2)}) %collective-permute-start.4) | collective-permute-done | bytes 98336 | tf_op jit(solution)/shard_map/ppermute | solution.py:260
  18.3 0.7 %collective-permute-start.6 = (bf16[128,384]{1,0:T(8,128)(2,1)S(1)}, bf16[128,384]{1,0:T(8,128)(2,1)S(1)}, u32[]{:S(2)}, u32[]{:S(2)}) collective-permute-start(bf16[128,384]{1,0:T(8,128)(2,1)S(1)} %collective-permute-done.4.refs_5_), channel_id=1, source_target_pairs={{0,1},{1,0},{2,3},{3,2},{4,5},{5,4},{6,7},{7,6},{8,9},{9,8},{10,11... | collective-permute-start | bytes 294920 | tf_op jit(solution)/shard_map/ppermute | solution.py:260
  19.0 1.6 %collective-permute-done.2.refs_3_ = bf16[128,384]{1,0:T(8,128)(2,1)S(1)} collective-permute-done((bf16[128,384]{1,0:T(8,128)(2,1)S(1)}, bf16[128,384]{1,0:T(8,128)(2,1)S(1)}, u32[]{:S(2)}, u32[]{:S(2)}) %collective-permute-start.2) | collective-permute-done | bytes 98336 | tf_op jit(solution)/shard_map/ppermute | solution.py:260
  20.7 1.3 %collective-permute-done.5.refs_6_ = bf16[128,384]{1,0:T(8,128)(2,1)S(1)} collective-permute-done((bf16[128,384]{1,0:T(8,128)(2,1)S(1)}, bf16[128,384]{1,0:T(8,128)(2,1)S(1)}, u32[]{:S(2)}, u32[]{:S(2)}) %collective-permute-start.5) | collective-permute-done | bytes 98336 | tf_op jit(solution)/shard_map/ppermute | solution.py:260
  22.0 1.0 %collective-permute-done.6.refs_7_ = bf16[128,384]{1,0:T(8,128)(2,1)S(1)} collective-permute-done((bf16[128,384]{1,0:T(8,128)(2,1)S(1)}, bf16[128,384]{1,0:T(8,128)(2,1)S(1)}, u32[]{:S(2)}, u32[]{:S(2)}) %collective-permute-start.6) | collective-permute-done | bytes 98336 | tf_op jit(solution)/shard_map/ppermute | solution.py:260
  23.2 0.7 %shard_map.70.refs_0_ = f32[512,384]{1,0:T(8,128)S(1)} custom-call(bf16[2,512,384]{2,1,0:T(8,128)(2,1)S(1)} %get-tuple-element.20.refs_0_, bf16[256,512]{1,0:T(8,128)(2,1)S(1)} %get-tuple-element.18.refs_1_, bf16[256,512]{1,0:T(8,128)(2,1)S(1)} %get-tuple-element.19.refs_2_, bf16[256,512]{1,0:T(8,128)(2,1)S(1)} %collective-permute-done.7.refs_8_.refs_3_, ...), custom_call_target="tpu_custom_call" | custom-call | tf_op jit(solution)/shard_map/pallas_call | solution.py:28
  23.9 1.0 %collective-permute-done.9.refs_1_.refs_2_ = bf16[512,384]{1,0:T(8,128)(2,1)S(1)} collective-permute-done((bf16[512,384]{1,0:T(8,128)(2,1)S(1)}, bf16[512,384]{1,0:T(8,128)(2,1)S(1)}, u32[]{:S(2)}, u32[]{:S(2)}) %collective-permute-start.9) | collective-permute-done | bytes 393248 | tf_op jit(solution)/shard_map/ppermute | solution.py:260
  25.1 0.7 %shard_map.72 = (f32[320,128]{1,0:T(8,128)S(1)}, f32[320,128]{1,0:T(8,128)S(1)}) custom-call(f32[512,384]{1,0:T(8,128)S(1)} %shard_map.71.refs_0_, bf16[512,384]{1,0:T(8,128)(2,1)S(1)} %get-tuple-element.21.refs_1_, bf16[512,384]{1,0:T(8,128)(2,1)S(1)} %collective-permute-done.9.refs_1_.refs_2_, bf16[32,384]{1,0:T(8,128)(2,1)S(1)} %get-tuple-element.22.refs_3_, ...), custom_call_target="tpu_custom_call" | custom-call | tf_op jit(solution)/shard_map/pallas_call | solution.py:28
  26.8 0.6 %collective-permute-done.10.refs_2_ = f32[320,128]{1,0:T(8,128)S(1)} collective-permute-done((f32[320,128]{1,0:T(8,128)S(1)}, f32[320,128]{1,0:T(8,128)S(1)}, u32[]{:S(2)}, u32[]{:S(2)}) %collective-permute-start.10) | collective-permute-done | bytes 163872 | tf_op jit(solution)/shard_map/ppermute | solution.py:260
  27.5 2.4 %collective-permute-start.13 = (f32[160,128]{1,0:T(8,128)S(1)}, f32[160,128]{1,0:T(8,128)S(1)}, u32[]{:S(2)}, u32[]{:S(2)}) collective-permute-start(f32[160,128]{1,0:T(8,128)S(1)} %get-tuple-element.26), channel_id=1, source_target_pairs={{0,17},{1,16},{2,19},{3,18},{4,21},{5,20},{6,23},{7,22},{8,25},{9,... | collective-permute-start | bytes 245768 | tf_op jit(solution)/shard_map/ppermute | solution.py:260
  29.9 0.5 collective-permute-start.11
  30.4 0.6 %collective-permute-start.12 = (f32[160,128]{1,0:T(8,128)S(1)}, f32[160,128]{1,0:T(8,128)S(1)}, u32[]{:S(2)}, u32[]{:S(2)}) collective-permute-start(f32[160,128]{1,0:T(8,128)S(1)} %get-tuple-element.25.refs_0_.refs_2_), channel_id=1, source_target_pairs={{0,1},{1,0},{2,3},{3,2},{4,5},{5,4},{6,7},{7,6},{8,9},{9,8},{10,11... | collective-permute-start | bytes 245768 | tf_op jit(solution)/shard_map/ppermute | solution.py:260
  31.2 0.7 %collective-permute-start.16 = (bf16[128,384]{1,0:T(8,128)(2,1)S(1)}, bf16[128,384]{1,0:T(8,128)(2,1)S(1)}, u32[]{:S(2)}, u32[]{:S(2)}) collective-permute-start(bf16[128,384]{1,0:T(8,128)(2,1)S(1)} %get-tuple-element.27), channel_id=1, source_target_pairs={{0,0},{1,4},{2,8},{3,12},{4,1},{5,5},{6,9},{7,13},{8,2},{9,6},{10,... | collective-permute-start | bytes 294920 | tf_op jit(solution)/shard_map/ppermute | solution.py:317
  31.9 1.1 %collective-permute-done.13.refs_3_ = f32[160,128]{1,0:T(8,128)S(1)} collective-permute-done((f32[160,128]{1,0:T(8,128)S(1)}, f32[160,128]{1,0:T(8,128)S(1)}, u32[]{:S(2)}, u32[]{:S(2)}) %collective-permute-start.13) | collective-permute-done | bytes 81952 | tf_op jit(solution)/shard_map/ppermute | solution.py:260
  33.0 1.7 %collective-permute-done.11.refs_1_ = f32[160,128]{1,0:T(8,128)S(1)} collective-permute-done((f32[160,128]{1,0:T(8,128)S(1)}, f32[160,128]{1,0:T(8,128)S(1)}, u32[]{:S(2)}, u32[]{:S(2)}) %collective-permute-start.11) | collective-permute-done | bytes 81952 | tf_op jit(solution)/shard_map/ppermute | solution.py:260
  34.9 3.4 %collective-permute-start.14 = (f32[160,128]{1,0:T(8,128)S(1)}, f32[160,128]{1,0:T(8,128)S(1)}, u32[]{:S(2)}, u32[]{:S(2)}) collective-permute-start(f32[160,128]{1,0:T(8,128)S(1)} %shard_map.74.refs_0_), channel_id=1, source_target_pairs={{0,2},{1,3},{2,0},{3,1},{4,6},{5,7},{6,4},{7,5},{8,10},{9,11},{10,... | collective-permute-start | bytes 245768 | tf_op jit(solution)/shard_map/ppermute | solution.py:260
  38.3 6.3 %collective-permute-done.14.refs_1_ = f32[160,128]{1,0:T(8,128)S(1)} collective-permute-done((f32[160,128]{1,0:T(8,128)S(1)}, f32[160,128]{1,0:T(8,128)S(1)}, u32[]{:S(2)}, u32[]{:S(2)}) %collective-permute-start.14) | collective-permute-done | bytes 81952 | tf_op jit(solution)/shard_map/ppermute | solution.py:260
  44.7 3.2 %collective-permute-start.19 = (f32[160,128]{1,0:T(8,128)S(1)}, f32[160,128]{1,0:T(8,128)S(1)}, u32[]{:S(2)}, u32[]{:S(2)}) collective-permute-start(f32[160,128]{1,0:T(8,128)S(1)} %shard_map.76.refs_0_), channel_id=1, source_target_pairs={{0,24},{1,25},{2,26},{3,27},{4,28},{5,29},{6,30},{7,31},{8,16},{9,... | collective-permute-start | bytes 245768 | tf_op jit(solution)/shard_map/ppermute | solution.py:260
  47.8 0.5 collective-permute-start.18
  48.7 1.9 %collective-permute-done.19.refs_3_ = f32[160,128]{1,0:T(8,128)S(1)} collective-permute-done((f32[160,128]{1,0:T(8,128)S(1)}, f32[160,128]{1,0:T(8,128)S(1)}, u32[]{:S(2)}, u32[]{:S(2)}) %collective-permute-start.19) | collective-permute-done | bytes 81952 | tf_op jit(solution)/shard_map/ppermute | solution.py:260
  50.6 1.7 %collective-permute-done.18.refs_2_ = f32[160,128]{1,0:T(8,128)S(1)} collective-permute-done((f32[160,128]{1,0:T(8,128)S(1)}, f32[160,128]{1,0:T(8,128)S(1)}, u32[]{:S(2)}, u32[]{:S(2)}) %collective-permute-start.18) | collective-permute-done | bytes 81952 | tf_op jit(solution)/shard_map/ppermute | solution.py:260
  52.3 0.5 collective-permute-done.17.refs_1_
  52.9 1.6 %collective-permute-done.21.refs_1_ = f32[4,160,128]{2,1,0:T(8,128)S(1)} collective-permute-done((f32[4,160,128]{2,1,0:T(8,128)S(1)}, f32[4,160,128]{2,1,0:T(8,128)S(1)}, u32[]{:S(2)}, u32[]{:S(2)}) %collective-permute-start.21) | collective-permute-done | bytes 327712 | tf_op jit(solution)/shard_map/ppermute | solution.py:260
  54.5 1.3 %shard_map.79 = (bf16[1,128,2,384]{3,2,1,0:T(2,128)(2,1)}, f32[2,384,384]{2,1,0:T(8,128)}) custom-call(f32[4,160,128]{2,1,0:T(8,128)S(1)} %shard_map.78.refs_0_, f32[4,160,128]{2,1,0:T(8,128)S(1)} %collective-permute-done.21.refs_1_, bf16[1,128,2,384]{3,2,1,0:T(2,128)(2,1)S(1)} %shard_map.77.refs_4_.refs_2_), custom_call_target="tpu_custom_call" | custom-call | tf_op jit(solution)/shard_map/pallas_call | solution.py:28
  (26 shorter events, 2.2 us)
Async XLA Ops:
  2.3 9.2 %collective-permute-start.3 = (bf16[160,384]{1,0:T(8,128)(2,1)S(1)}, bf16[160,384]{1,0:T(8,128)(2,1)S(1)}, u32[]{:S(2)}, u32[]{:S(2)}) collective-permute-start(bf16[160,384]{1,0:T(8,128)(2,1)S(1)} %get-tuple-element.17), channel_id=1, source_target_pairs={{0,8},{1,9},{2,10},{3,11},{4,12},{5,13},{6,14},{7,15},{8,0},{9,1},... | collective-permute-start | bytes 368648 | tf_op jit(solution)/shard_map/ppermute | solution.py:260
  5.3 16.6 %collective-permute-start.7 = (bf16[256,512]{1,0:T(8,128)(2,1)S(1)}, bf16[256,512]{1,0:T(8,128)(2,1)S(1)}, u32[]{:S(2)}, u32[]{:S(2)}) collective-permute-start(bf16[256,512]{1,0:T(8,128)(2,1)S(1)} %get-tuple-element.18.refs_1_), channel_id=1, source_target_pairs={{0,8},{1,9},{2,10},{3,11},{4,12},{5,13},{6,14},{7,15},{8,0},{9,1},... | collective-permute-start | bytes 786440 | tf_op jit(solution)/shard_map/ppermute | solution.py:260
  5.4 16.5 %collective-permute-start.8 = (bf16[256,512]{1,0:T(8,128)(2,1)S(1)}, bf16[256,512]{1,0:T(8,128)(2,1)S(1)}, u32[]{:S(2)}, u32[]{:S(2)}) collective-permute-start(bf16[256,512]{1,0:T(8,128)(2,1)S(1)} %get-tuple-element.19.refs_2_), channel_id=1, source_target_pairs={{0,8},{1,9},{2,10},{3,11},{4,12},{5,13},{6,14},{7,15},{8,0},{9,1},... | collective-permute-start | bytes 786440 | tf_op jit(solution)/shard_map/ppermute | solution.py:260
  7.4 5.8 %collective-permute-start = (bf16[128,384]{1,0:T(8,128)(2,1)S(1)}, bf16[128,384]{1,0:T(8,128)(2,1)S(1)}, u32[]{:S(2)}, u32[]{:S(2)}) collective-permute-start(bf16[128,384]{1,0:T(8,128)(2,1)S(1)} %get-tuple-element.16.refs_0_), channel_id=1, source_target_pairs={{0,2},{1,3},{2,0},{3,1},{4,6},{5,7},{6,4},{7,5},{8,10},{9,11},{10,... | collective-permute-start | bytes 294920 | tf_op jit(solution)/shard_map/ppermute | solution.py:260
  10.0 7.0 %collective-permute-start.1 = (bf16[128,384]{1,0:T(8,128)(2,1)S(1)}, bf16[128,384]{1,0:T(8,128)(2,1)S(1)}, u32[]{:S(2)}, u32[]{:S(2)}) collective-permute-start(bf16[128,384]{1,0:T(8,128)(2,1)S(1)} %get-tuple-element.16.refs_0_), channel_id=1, source_target_pairs={{0,1},{1,0},{2,3},{3,2},{4,5},{5,4},{6,7},{7,6},{8,9},{9,8},{10,11... | collective-permute-start | bytes 294920 | tf_op jit(solution)/shard_map/ppermute | solution.py:260
  11.6 6.8 %collective-permute-start.4 = (bf16[128,384]{1,0:T(8,128)(2,1)S(1)}, bf16[128,384]{1,0:T(8,128)(2,1)S(1)}, u32[]{:S(2)}, u32[]{:S(2)}) collective-permute-start(bf16[128,384]{1,0:T(8,128)(2,1)S(1)} %slice.8.refs_4_), channel_id=1, source_target_pairs={{0,2},{1,3},{2,0},{3,1},{4,6},{5,7},{6,4},{7,5},{8,10},{9,11},{10,... | collective-permute-start | bytes 294920 | tf_op jit(solution)/shard_map/ppermute | solution.py:260
  13.1 7.6 %collective-permute-start.2 = (bf16[128,384]{1,0:T(8,128)(2,1)S(1)}, bf16[128,384]{1,0:T(8,128)(2,1)S(1)}, u32[]{:S(2)}, u32[]{:S(2)}) collective-permute-start(bf16[128,384]{1,0:T(8,128)(2,1)S(1)} %collective-permute-done.refs_1_), channel_id=1, source_target_pairs={{0,1},{1,0},{2,3},{3,2},{4,5},{5,4},{6,7},{7,6},{8,9},{9,8},{10,11... | collective-permute-start | bytes 294920 | tf_op jit(solution)/shard_map/ppermute | solution.py:260
  17.0 5.0 %collective-permute-start.5 = (bf16[128,384]{1,0:T(8,128)(2,1)S(1)}, bf16[128,384]{1,0:T(8,128)(2,1)S(1)}, u32[]{:S(2)}, u32[]{:S(2)}) collective-permute-start(bf16[128,384]{1,0:T(8,128)(2,1)S(1)} %slice.8.refs_4_), channel_id=1, source_target_pairs={{0,1},{1,0},{2,3},{3,2},{4,5},{5,4},{6,7},{7,6},{8,9},{9,8},{10,11... | collective-permute-start | bytes 294920 | tf_op jit(solution)/shard_map/ppermute | solution.py:260
  18.3 4.7 %collective-permute-start.6 = (bf16[128,384]{1,0:T(8,128)(2,1)S(1)}, bf16[128,384]{1,0:T(8,128)(2,1)S(1)}, u32[]{:S(2)}, u32[]{:S(2)}) collective-permute-start(bf16[128,384]{1,0:T(8,128)(2,1)S(1)} %collective-permute-done.4.refs_5_), channel_id=1, source_target_pairs={{0,1},{1,0},{2,3},{3,2},{4,5},{5,4},{6,7},{7,6},{8,9},{9,8},{10,11... | collective-permute-start | bytes 294920 | tf_op jit(solution)/shard_map/ppermute | solution.py:260
  23.1 1.8 %collective-permute-start.9 = (bf16[512,384]{1,0:T(8,128)(2,1)S(1)}, bf16[512,384]{1,0:T(8,128)(2,1)S(1)}, u32[]{:S(2)}, u32[]{:S(2)}) collective-permute-start(bf16[512,384]{1,0:T(8,128)(2,1)S(1)} %get-tuple-element.21.refs_1_), channel_id=1, source_target_pairs={{0,4},{1,5},{2,6},{3,7},{4,0},{5,1},{6,2},{7,3},{8,12},{9,13},{10,... | collective-permute-start | bytes 1179656 | tf_op jit(solution)/shard_map/ppermute | solution.py:260
  24.9 6.1 %collective-permute-start.15 = (f32[512,384]{1,0:T(8,128)S(1)}, f32[512,384]{1,0:T(8,128)S(1)}, u32[]{:S(2)}, u32[]{:S(2)}) collective-permute-start(f32[512,384]{1,0:T(8,128)S(1)} %shard_map.71.refs_0_), channel_id=1, source_target_pairs={{0,4},{1,5},{2,6},{3,7},{4,0},{5,1},{6,2},{7,3},{8,12},{9,13},{10,... | collective-permute-start | bytes 2359304 | tf_op jit(solution)/shard_map/ppermute | solution.py:260
  25.8 1.7 %collective-permute-start.10 = (f32[320,128]{1,0:T(8,128)S(1)}, f32[320,128]{1,0:T(8,128)S(1)}, u32[]{:S(2)}, u32[]{:S(2)}) collective-permute-start(f32[320,128]{1,0:T(8,128)S(1)} %get-tuple-element.24), channel_id=1, source_target_pairs={{0,4},{1,5},{2,6},{3,7},{4,0},{5,1},{6,2},{7,3},{8,12},{9,13},{10,... | collective-permute-start | bytes 491528 | tf_op jit(solution)/shard_map/ppermute | solution.py:260
  27.5 5.5 %collective-permute-start.13 = (f32[160,128]{1,0:T(8,128)S(1)}, f32[160,128]{1,0:T(8,128)S(1)}, u32[]{:S(2)}, u32[]{:S(2)}) collective-permute-start(f32[160,128]{1,0:T(8,128)S(1)} %get-tuple-element.26), channel_id=1, source_target_pairs={{0,17},{1,16},{2,19},{3,18},{4,21},{5,20},{6,23},{7,22},{8,25},{9,... | collective-permute-start | bytes 245768 | tf_op jit(solution)/shard_map/ppermute | solution.py:260
  29.9 4.8 %collective-permute-start.11 = (f32[160,128]{1,0:T(8,128)S(1)}, f32[160,128]{1,0:T(8,128)S(1)}, u32[]{:S(2)}, u32[]{:S(2)}) collective-permute-start(f32[160,128]{1,0:T(8,128)S(1)} %get-tuple-element.26), channel_id=1, source_target_pairs={{0,16},{1,17},{2,18},{3,19},{4,20},{5,21},{6,22},{7,23},{8,24},{9,... | collective-permute-start | bytes 245768 | tf_op jit(solution)/shard_map/ppermute | solution.py:260
  30.4 4.4 %collective-permute-start.12 = (f32[160,128]{1,0:T(8,128)S(1)}, f32[160,128]{1,0:T(8,128)S(1)}, u32[]{:S(2)}, u32[]{:S(2)}) collective-permute-start(f32[160,128]{1,0:T(8,128)S(1)} %get-tuple-element.25.refs_0_.refs_2_), channel_id=1, source_target_pairs={{0,1},{1,0},{2,3},{3,2},{4,5},{5,4},{6,7},{7,6},{8,9},{9,8},{10,11... | collective-permute-start | bytes 245768 | tf_op jit(solution)/shard_map/ppermute | solution.py:260
  31.2 13.4 %collective-permute-start.16 = (bf16[128,384]{1,0:T(8,128)(2,1)S(1)}, bf16[128,384]{1,0:T(8,128)(2,1)S(1)}, u32[]{:S(2)}, u32[]{:S(2)}) collective-permute-start(bf16[128,384]{1,0:T(8,128)(2,1)S(1)} %get-tuple-element.27), channel_id=1, source_target_pairs={{0,0},{1,4},{2,8},{3,12},{4,1},{5,5},{6,9},{7,13},{8,2},{9,6},{10,... | collective-permute-start | bytes 294920 | tf_op jit(solution)/shard_map/ppermute | solution.py:317
  34.9 9.8 %collective-permute-start.14 = (f32[160,128]{1,0:T(8,128)S(1)}, f32[160,128]{1,0:T(8,128)S(1)}, u32[]{:S(2)}, u32[]{:S(2)}) collective-permute-start(f32[160,128]{1,0:T(8,128)S(1)} %shard_map.74.refs_0_), channel_id=1, source_target_pairs={{0,2},{1,3},{2,0},{3,1},{4,6},{5,7},{6,4},{7,5},{8,10},{9,11},{10,... | collective-permute-start | bytes 245768 | tf_op jit(solution)/shard_map/ppermute | solution.py:260
  38.3 10.2 %collective-permute-start.20 = (bf16[128,384]{1,0:T(8,128)(2,1)S(1)}, bf16[128,384]{1,0:T(8,128)(2,1)S(1)}, u32[]{:S(2)}, u32[]{:S(2)}) collective-permute-start(bf16[128,384]{1,0:T(8,128)(2,1)S(1)} %get-tuple-element.29), channel_id=1, source_target_pairs={{0,2},{1,6},{2,10},{3,14},{4,3},{5,7},{6,11},{7,15},{8,0},{9,4},{1... | collective-permute-start | bytes 294920 | tf_op jit(solution)/shard_map/ppermute | solution.py:317
  44.7 6.0 %collective-permute-start.19 = (f32[160,128]{1,0:T(8,128)S(1)}, f32[160,128]{1,0:T(8,128)S(1)}, u32[]{:S(2)}, u32[]{:S(2)}) collective-permute-start(f32[160,128]{1,0:T(8,128)S(1)} %shard_map.76.refs_0_), channel_id=1, source_target_pairs={{0,24},{1,25},{2,26},{3,27},{4,28},{5,29},{6,30},{7,31},{8,16},{9,... | collective-permute-start | bytes 245768 | tf_op jit(solution)/shard_map/ppermute | solution.py:260
  47.8 4.5 %collective-permute-start.18 = (f32[160,128]{1,0:T(8,128)S(1)}, f32[160,128]{1,0:T(8,128)S(1)}, u32[]{:S(2)}, u32[]{:S(2)}) collective-permute-start(f32[160,128]{1,0:T(8,128)S(1)} %shard_map.76.refs_0_), channel_id=1, source_target_pairs={{0,16},{1,17},{2,18},{3,19},{4,20},{5,21},{6,22},{7,23},{8,24},{9,... | collective-permute-start | bytes 245768 | tf_op jit(solution)/shard_map/ppermute | solution.py:260
  48.3 4.4 %collective-permute-start.17 = (f32[160,128]{1,0:T(8,128)S(1)}, f32[160,128]{1,0:T(8,128)S(1)}, u32[]{:S(2)}, u32[]{:S(2)}) collective-permute-start(f32[160,128]{1,0:T(8,128)S(1)} %shard_map.76.refs_0_), channel_id=1, source_target_pairs={{0,8},{1,9},{2,10},{3,11},{4,12},{5,13},{6,14},{7,15},{8,0},{9,1},... | collective-permute-start | bytes 245768 | tf_op jit(solution)/shard_map/ppermute | solution.py:260
  52.8 1.7 %collective-permute-start.21 = (f32[4,160,128]{2,1,0:T(8,128)S(1)}, f32[4,160,128]{2,1,0:T(8,128)S(1)}, u32[]{:S(2)}, u32[]{:S(2)}) collective-permute-start(f32[4,160,128]{2,1,0:T(8,128)S(1)} %shard_map.78.refs_0_), channel_id=1, source_target_pairs={{0,4},{1,5},{2,6},{3,7},{4,0},{5,1},{6,2},{7,3},{8,12},{9,13},{10,... | collective-permute-start | bytes 983048 | tf_op jit(solution)/shard_map/ppermute | solution.py:260

commit v19 on v18

--- a/solution.py
+++ b/solution.py
@@ -219,28 +219,91 @@
         refs[-1][index] = ref[...]
 
 
-def finish_kernel(own, other, rows, rows_out, out, lines, result, sems):
-    copies = [pltpu.make_async_copy(rows, rows_out, sems.at[0])]
-    copies[0].start()
-    point, side, core = (lax.axis_index(name) for name in ("hyp", "side", "core"))
-    size = own.shape[1]
-    for parts, owner in ((own, core), (other, 1 - core)):
-        for index in range(own.shape[0]):
-            node = 1 - side if index % 2 else side
-            slot = 1 - point if index // 2 else point
-            start = pl.multiple_of((owner * 2 + slot) * size, 8)
-            lines[node, pl.ds(start, size), :] = parts[index]
-    places = [slice(index * LANES, (index + 1) * LANES) for index in range(BLOCKS)]
+def set_lines(parts, lines, first):
+    point, side, size = lax.axis_index("hyp"), lax.axis_index("side"), parts.shape[1]
+    for index in range(parts.shape[0]):
+        node = 1 - side if index % 2 else side
+        slot = 1 - point if index // 2 else point
+        lines[node, pl.ds(pl.multiple_of(first + slot * size, 8), size), :] = parts[index]
+
+
+def copy_out(areas, result, out, sems):
+    copies = [
+        pltpu.make_async_copy(result.at[area], out.at[area], sems.at[index]) for index, area in enumerate(areas)
+    ]
+    for copy in copies:
+        copy.start()
+    return copies
+
+
+def first_core_blocks(lines, result, out, sems):
+    first, rest = slice(0, LANES), slice(LANES, BLOCKS * LANES)
+    areas = []
     for node in range(2):
-        held = [lines[node, index * LANES : (index + 1) * LANES, :] for index in range(HELD)]
-        for (a, b), tile in zip(ABOVE, held):
-            result[node, places[a], places[b]] = tile
-            result[node, places[b], places[a]] = tile.T
-        for place, tile in zip(places, restore_diagonal(*held[len(ABOVE) :])):
+        for index in range(2):
+            place = slice((index + 1) * LANES, (index + 2) * LANES)
+            tile = lines[node, index * LANES : (index + 1) * LANES, :]
+            result[node, first, place] = tile
+            result[node, place, first] = tile.T
+        areas += [(node, first, rest), (node, rest, first)]
+    return copy_out(areas, result, out, sems)
+
+
+def second_core_blocks(lines, at, result, out, sems):
+    areas = []
+    for node in range(2):
+        held = (lines[node, at + index * LANES : at + (index + 1) * LANES, :] for index in range(2))
+        for index, tile in enumerate(restore_diagonal(*held)):
+            place = slice(index * LANES, (index + 1) * LANES)
             result[node, place, place] = tile
-        copies.append(pltpu.make_async_copy(result.at[node], out.at[node], sems.at[1 + node]))
-        copies[-1].start()
-    for copy in copies:
+            areas.append((node, place, place))
+    return copy_out(areas, result, out, sems)
+
+
+def early_kernel(own, rows, rows_out, out, lines, result, sems, rows_sem):
+    store = pltpu.make_async_copy(rows, rows_out, rows_sem)
+    store.start()
+    core = lax.axis_index("core")
+    set_lines(own, lines, 0)
+
+    @pl.when(core == 0)
+    def _():
+        for copy in first_core_blocks(lines, result, out, sems):
+            copy.wait()
+
+    @pl.when(core == 1)
+    def _():
+        for copy in second_core_blocks(lines, LANES // 2, result, out, sems):
+            copy.wait()
+
+    store.wait()
+
+
+def late_kernel(own, other, before, out, lines, result, sems, middle_sems):
+    del before
+    core, half = lax.axis_index("core"), lines.shape[1] // 2
+    set_lines(own, lines, core * half)
+    set_lines(other, lines, (1 - core) * half)
+    middle, last = (slice(i * LANES, (i + 1) * LANES) for i in (1, 2))
+    areas = []
+    for node in range(2):
+        tile = lines[node, 2 * LANES : 3 * LANES, :]
+        result[node, middle, last] = tile
+        result[node, last, middle] = tile.T
+        areas += [(node, middle, last), (node, last, middle)]
+    shared = copy_out(areas, result, out, middle_sems)
+
+    @pl.when(core == 1)
+    def _():
+        for copy in first_core_blocks(lines, result, out, sems):
+            copy.wait()
+
+    @pl.when(core == 0)
+    def _():
+        for copy in second_core_blocks(lines, len(ABOVE) * LANES, result, out, sems):
+            copy.wait()
+
+    for copy in shared:
         copy.wait()
 
 
@@ -326,7 +389,7 @@
         after=[keep],
     )
     near, far = deliver(out_near, 0), deliver(out_far, 1)
-    total = call(add_kernel, part, [VMEM] * 2, total, swap(total, column=2), after=[near])
+    total = call(add_kernel, part, [VMEM] * 2, total, swap(total, column=2))
     quarters = [total, swap(total, side=1), swap(total, point=1), swap(total, side=1, point=1)]
     rows = call(
         rows_kernel, shape((1, height, count, width), bf16), [VMEM] * 3, limits, near, far
@@ -334,18 +397,19 @@
     quarters = call(
         stack_kernel, shape((len(quarters), *part.shape), f32), [VMEM] * len(quarters), *quarters, after=[rows]
     )
-    return call(
-        finish_kernel,
-        [shape((1, height, count, width), bf16), shape((count, width, width), f32)],
-        [VMEM] * 3,
-        quarters, swap(quarters, core=1), rows,
-        scratch=[
-            pltpu.VMEM((count, 2 * lines, LANES), f32),
-            pltpu.VMEM((count, width, width), f32),
-            dma((3,)),
-        ],
+    whole = shape((count, width, width), f32)
+    sigma_panel, marginal = call(
+        early_kernel, [shape(rows.shape, bf16), whole], [VMEM] * 2, quarters, rows,
+        scratch=[pltpu.VMEM((count, lines, LANES), f32), pltpu.VMEM(whole.shape, f32), dma((6,)), dma(())],
         out_specs=[HBM, HBM],
     )
+    marginal = call(
+        late_kernel, whole, [VMEM, VMEM, HBM], quarters, swap(quarters, core=1), marginal,
+        scratch=[pltpu.VMEM((count, 2 * lines, LANES), f32), pltpu.VMEM(whole.shape, f32), dma((6,)), dma((4,))],
+        out_specs=HBM,
+        alias={2: 0},
+    )
+    return sigma_panel, marginal
 
 
 def solution(mesh):

time: 55.9 us -> 53.6 us (0.959)
  waiting for transfers between devices: 21.6 us -> 14.4 us
  starting transfers between devices: 27.8 us -> 31.7 us
  Pallas kernels: 5.02 us -> 5.94 us
    ppermute x20, waiting for transfers between devices: 21.6 us -> 14.4 us  [swap(): return lax.ppermute(x, AXES, [(i, i ^ mask) for i in range(devices)])]
    ppermute x2, starting transfers between devices: 0.73 us -> 5.13 us  [deliver(): return lax.ppermute(x, AXES, pairs)]
    pallas_call x12 -> x13, Pallas kernels: 5.02 us -> 5.94 us  [call(): pl.pallas_call(body, out_shape=outs, in_specs=list(specs) + [ANY] * len(a...]
  transfers between devices with their start and end apart: 22 -> 22, of which waited for: 15 -> 13; matrix products, arithmetic and copies ran while one was open for 0% -> 0% of each run, Pallas kernels for 3% -> 6%
where the time goes in v19:
time: 53.6 us; the launch traced here: 53.4 us
  starting transfers between devices  31.7 us (59%)
  waiting for transfers between devices  14.4 us (27%)
  Pallas kernels  5.94 us (11%)
  between operations  1.39 us (3%)
    ppermute x20, starting transfers between devices, swap(): return lax.ppermute(x, AXES, [(i, i ^ mask) for i in range(devices)])  26.6 us
    ppermute x20, waiting for transfers between devices, swap(): return lax.ppermute(x, AXES, [(i, i ^ mask) for i in range(devices)])  14.4 us
    pallas_call x13, Pallas kernels, call(): pl.pallas_call(body, out_shape=outs, in_specs=list(specs) + [ANY] * len(a...  5.94 us
    ppermute x2, starting transfers between devices, deliver(): return lax.ppermute(x, AXES, pairs)  5.13 us
  transfers between devices with their start and end apart: 22, of which 13 were waited for; matrix products, arithmetic and copies ran while one was open for 0% of the time, Pallas kernels for 6%

profile of v19, /device:TPU:0, one launch (start us, length us, event | category | flops | bytes accessed | tf_op | source)
XLA Modules:
  0.0 53.4 jit_solution(11523363569743507760)
XLA Ops:
  0.6 1.7 %shard_map.68 = (bf16[128,384]{1,0:T(8,128)(2,1)S(1)}, bf16[160,384]{1,0:T(8,128)(2,1)S(1)}, bf16[32,384]{1,0:T(8,128)(2,1)S(1)}, s32[2,8,128]{2,1,0:T(8,128)S(1...) custom-call(s32[2]{0:T(128)} %bitcast.1, bf16[1,128,2,384]{3,2,1,0:T(2,128)(2,1)} %refs_1_.1, ...), custom_call_target="tpu_custom_call" | custom-call | tf_op jit(solution)/shard_map/pallas_call | solution.py:28
  2.3 3.0 %collective-permute-start.3 = (bf16[160,384]{1,0:T(8,128)(2,1)S(1)}, bf16[160,384]{1,0:T(8,128)(2,1)S(1)}, u32[]{:S(2)}, u32[]{:S(2)}) collective-permute-start(bf16[160,384]{1,0:T(8,128)(2,1)S(1)} %get-tuple-element.19), channel_id=1, source_target_pairs={{0,8},{1,9},{2,10},{3,11},{4,12},{5,13},{6,14},{7,15},{8,0},{9,1},... | collective-permute-start | bytes 368648 | tf_op jit(solution)/shard_map/ppermute | solution.py:323
  5.4 1.9 %collective-permute-start.8 = (bf16[256,512]{1,0:T(8,128)(2,1)S(1)}, bf16[256,512]{1,0:T(8,128)(2,1)S(1)}, u32[]{:S(2)}, u32[]{:S(2)}) collective-permute-start(bf16[256,512]{1,0:T(8,128)(2,1)S(1)} %get-tuple-element.21.refs_2_), channel_id=1, source_target_pairs={{0,8},{1,9},{2,10},{3,11},{4,12},{5,13},{6,14},{7,15},{8,0},{9,1},... | collective-permute-start | bytes 786440 | tf_op jit(solution)/shard_map/ppermute | solution.py:323
  7.4 2.6 %collective-permute-start = (bf16[128,384]{1,0:T(8,128)(2,1)S(1)}, bf16[128,384]{1,0:T(8,128)(2,1)S(1)}, u32[]{:S(2)}, u32[]{:S(2)}) collective-permute-start(bf16[128,384]{1,0:T(8,128)(2,1)S(1)} %get-tuple-element.18.refs_0_), channel_id=1, source_target_pairs={{0,2},{1,3},{2,0},{3,1},{4,6},{5,7},{6,4},{7,5},{8,10},{9,11},{10,... | collective-permute-start | bytes 294920 | tf_op jit(solution)/shard_map/ppermute | solution.py:323
  10.0 1.6 %collective-permute-start.1 = (bf16[128,384]{1,0:T(8,128)(2,1)S(1)}, bf16[128,384]{1,0:T(8,128)(2,1)S(1)}, u32[]{:S(2)}, u32[]{:S(2)}) collective-permute-start(bf16[128,384]{1,0:T(8,128)(2,1)S(1)} %get-tuple-element.18.refs_0_), channel_id=1, source_target_pairs={{0,1},{1,0},{2,3},{3,2},{4,5},{5,4},{6,7},{7,6},{8,9},{9,8},{10,11... | collective-permute-start | bytes 294920 | tf_op jit(solution)/shard_map/ppermute | solution.py:323
  11.6 1.2 %collective-permute-start.4 = (bf16[128,384]{1,0:T(8,128)(2,1)S(1)}, bf16[128,384]{1,0:T(8,128)(2,1)S(1)}, u32[]{:S(2)}, u32[]{:S(2)}) collective-permute-start(bf16[128,384]{1,0:T(8,128)(2,1)S(1)} %slice.8.refs_4_), channel_id=1, source_target_pairs={{0,2},{1,3},{2,0},{3,1},{4,6},{5,7},{6,4},{7,5},{8,10},{9,11},{10,... | collective-permute-start | bytes 294920 | tf_op jit(solution)/shard_map/ppermute | solution.py:323
  13.1 3.8 %collective-permute-start.2 = (bf16[128,384]{1,0:T(8,128)(2,1)S(1)}, bf16[128,384]{1,0:T(8,128)(2,1)S(1)}, u32[]{:S(2)}, u32[]{:S(2)}) collective-permute-start(bf16[128,384]{1,0:T(8,128)(2,1)S(1)} %collective-permute-done.refs_1_), channel_id=1, source_target_pairs={{0,1},{1,0},{2,3},{3,2},{4,5},{5,4},{6,7},{7,6},{8,9},{9,8},{10,11... | collective-permute-start | bytes 294920 | tf_op jit(solution)/shard_map/ppermute | solution.py:323
  17.0 0.7 %collective-permute-start.5 = (bf16[128,384]{1,0:T(8,128)(2,1)S(1)}, bf16[128,384]{1,0:T(8,128)(2,1)S(1)}, u32[]{:S(2)}, u32[]{:S(2)}) collective-permute-start(bf16[128,384]{1,0:T(8,128)(2,1)S(1)} %slice.8.refs_4_), channel_id=1, source_target_pairs={{0,1},{1,0},{2,3},{3,2},{4,5},{5,4},{6,7},{7,6},{8,9},{9,8},{10,11... | collective-permute-start | bytes 294920 | tf_op jit(solution)/shard_map/ppermute | solution.py:323
  17.7 0.6 %collective-permute-done.4.refs_5_ = bf16[128,384]{1,0:T(8,128)(2,1)S(1)} collective-permute-done((bf16[128,384]{1,0:T(8,128)(2,1)S(1)}, bf16[128,384]{1,0:T(8,128)(2,1)S(1)}, u32[]{:S(2)}, u32[]{:S(2)}) %collective-permute-start.4) | collective-permute-done | bytes 98336 | tf_op jit(solution)/shard_map/ppermute | solution.py:323
  18.3 0.7 %collective-permute-start.6 = (bf16[128,384]{1,0:T(8,128)(2,1)S(1)}, bf16[128,384]{1,0:T(8,128)(2,1)S(1)}, u32[]{:S(2)}, u32[]{:S(2)}) collective-permute-start(bf16[128,384]{1,0:T(8,128)(2,1)S(1)} %collective-permute-done.4.refs_5_), channel_id=1, source_target_pairs={{0,1},{1,0},{2,3},{3,2},{4,5},{5,4},{6,7},{7,6},{8,9},{9,8},{10,11... | collective-permute-start | bytes 294920 | tf_op jit(solution)/shard_map/ppermute | solution.py:323
  19.0 1.6 %collective-permute-done.2.refs_3_ = bf16[128,384]{1,0:T(8,128)(2,1)S(1)} collective-permute-done((bf16[128,384]{1,0:T(8,128)(2,1)S(1)}, bf16[128,384]{1,0:T(8,128)(2,1)S(1)}, u32[]{:S(2)}, u32[]{:S(2)}) %collective-permute-start.2) | collective-permute-done | bytes 98336 | tf_op jit(solution)/shard_map/ppermute | solution.py:323
  20.7 1.3 %collective-permute-done.5.refs_6_ = bf16[128,384]{1,0:T(8,128)(2,1)S(1)} collective-permute-done((bf16[128,384]{1,0:T(8,128)(2,1)S(1)}, bf16[128,384]{1,0:T(8,128)(2,1)S(1)}, u32[]{:S(2)}, u32[]{:S(2)}) %collective-permute-start.5) | collective-permute-done | bytes 98336 | tf_op jit(solution)/shard_map/ppermute | solution.py:323
  22.0 1.0 %collective-permute-done.6.refs_7_ = bf16[128,384]{1,0:T(8,128)(2,1)S(1)} collective-permute-done((bf16[128,384]{1,0:T(8,128)(2,1)S(1)}, bf16[128,384]{1,0:T(8,128)(2,1)S(1)}, u32[]{:S(2)}, u32[]{:S(2)}) %collective-permute-start.6) | collective-permute-done | bytes 98336 | tf_op jit(solution)/shard_map/ppermute | solution.py:323
  23.2 0.7 %shard_map.70.refs_0_ = f32[512,384]{1,0:T(8,128)S(1)} custom-call(bf16[2,512,384]{2,1,0:T(8,128)(2,1)S(1)} %get-tuple-element.22.refs_0_, bf16[256,512]{1,0:T(8,128)(2,1)S(1)} %get-tuple-element.20.refs_1_, bf16[256,512]{1,0:T(8,128)(2,1)S(1)} %get-tuple-element.21.refs_2_, bf16[256,512]{1,0:T(8,128)(2,1)S(1)} %collective-permute-done.7.refs_8_.refs_3_, ...), custom_call_target="tpu_custom_call" | custom-call | tf_op jit(solution)/shard_map/pallas_call | solution.py:28
  23.9 1.0 %collective-permute-done.9.refs_1_.refs_2_ = bf16[512,384]{1,0:T(8,128)(2,1)S(1)} collective-permute-done((bf16[512,384]{1,0:T(8,128)(2,1)S(1)}, bf16[512,384]{1,0:T(8,128)(2,1)S(1)}, u32[]{:S(2)}, u32[]{:S(2)}) %collective-permute-start.9) | collective-permute-done | bytes 393248 | tf_op jit(solution)/shard_map/ppermute | solution.py:323
  25.1 0.7 %shard_map.72 = (f32[320,128]{1,0:T(8,128)S(1)}, f32[320,128]{1,0:T(8,128)S(1)}) custom-call(f32[512,384]{1,0:T(8,128)S(1)} %shard_map.71.refs_0_, bf16[512,384]{1,0:T(8,128)(2,1)S(1)} %get-tuple-element.23.refs_1_, bf16[512,384]{1,0:T(8,128)(2,1)S(1)} %collective-permute-done.9.refs_1_.refs_2_, bf16[32,384]{1,0:T(8,128)(2,1)S(1)} %get-tuple-element.24.refs_3_, ...), custom_call_target="tpu_custom_call" | custom-call | tf_op jit(solution)/shard_map/pallas_call | solution.py:28
  26.8 0.6 %collective-permute-done.10.refs_2_ = f32[320,128]{1,0:T(8,128)S(1)} collective-permute-done((f32[320,128]{1,0:T(8,128)S(1)}, f32[320,128]{1,0:T(8,128)S(1)}, u32[]{:S(2)}, u32[]{:S(2)}) %collective-permute-start.10) | collective-permute-done | bytes 163872 | tf_op jit(solution)/shard_map/ppermute | solution.py:323
  27.5 2.4 %collective-permute-start.13 = (f32[160,128]{1,0:T(8,128)S(1)}, f32[160,128]{1,0:T(8,128)S(1)}, u32[]{:S(2)}, u32[]{:S(2)}) collective-permute-start(f32[160,128]{1,0:T(8,128)S(1)} %get-tuple-element.28), channel_id=1, source_target_pairs={{0,17},{1,16},{2,19},{3,18},{4,21},{5,20},{6,23},{7,22},{8,25},{9,... | collective-permute-start | bytes 245768 | tf_op jit(solution)/shard_map/ppermute | solution.py:323
  29.9 0.5 collective-permute-start.11
  30.4 0.6 %collective-permute-start.12 = (f32[160,128]{1,0:T(8,128)S(1)}, f32[160,128]{1,0:T(8,128)S(1)}, u32[]{:S(2)}, u32[]{:S(2)}) collective-permute-start(f32[160,128]{1,0:T(8,128)S(1)} %get-tuple-element.27.refs_0_.refs_2_), channel_id=1, source_target_pairs={{0,1},{1,0},{2,3},{3,2},{4,5},{5,4},{6,7},{7,6},{8,9},{9,8},{10,11... | collective-permute-start | bytes 245768 | tf_op jit(solution)/shard_map/ppermute | solution.py:323
  31.0 1.9 %collective-permute-done.13.refs_3_ = f32[160,128]{1,0:T(8,128)S(1)} collective-permute-done((f32[160,128]{1,0:T(8,128)S(1)}, f32[160,128]{1,0:T(8,128)S(1)}, u32[]{:S(2)}, u32[]{:S(2)}) %collective-permute-start.13) | collective-permute-done | bytes 81952 | tf_op jit(solution)/shard_map/ppermute | solution.py:323
  33.0 1.7 %collective-permute-done.11.refs_1_ = f32[160,128]{1,0:T(8,128)S(1)} collective-permute-done((f32[160,128]{1,0:T(8,128)S(1)}, f32[160,128]{1,0:T(8,128)S(1)}, u32[]{:S(2)}, u32[]{:S(2)}) %collective-permute-start.11) | collective-permute-done | bytes 81952 | tf_op jit(solution)/shard_map/ppermute | solution.py:323
  34.9 3.1 %collective-permute-start.14 = (f32[160,128]{1,0:T(8,128)S(1)}, f32[160,128]{1,0:T(8,128)S(1)}, u32[]{:S(2)}, u32[]{:S(2)}) collective-permute-start(f32[160,128]{1,0:T(8,128)S(1)} %shard_map.74.refs_0_), channel_id=1, source_target_pairs={{0,2},{1,3},{2,0},{3,1},{4,6},{5,7},{6,4},{7,5},{8,10},{9,11},{10,... | collective-permute-start | bytes 245768 | tf_op jit(solution)/shard_map/ppermute | solution.py:323
  38.2 0.7 %collective-permute-start.19 = (bf16[128,384]{1,0:T(8,128)(2,1)S(1)}, bf16[128,384]{1,0:T(8,128)(2,1)S(1)}, u32[]{:S(2)}, u32[]{:S(2)}) collective-permute-start(bf16[128,384]{1,0:T(8,128)(2,1)S(1)} %get-tuple-element.30), channel_id=1, source_target_pairs={{0,0},{1,4},{2,8},{3,12},{4,1},{5,5},{6,9},{7,13},{8,2},{9,6},{10,... | collective-permute-start | bytes 294920 | tf_op jit(solution)/shard_map/ppermute | solution.py:380
  38.9 4.5 %collective-permute-start.20 = (bf16[128,384]{1,0:T(8,128)(2,1)S(1)}, bf16[128,384]{1,0:T(8,128)(2,1)S(1)}, u32[]{:S(2)}, u32[]{:S(2)}) collective-permute-start(bf16[128,384]{1,0:T(8,128)(2,1)S(1)} %get-tuple-element.31), channel_id=1, source_target_pairs={{0,2},{1,6},{2,10},{3,14},{4,3},{5,7},{6,11},{7,15},{8,0},{9,4},{1... | collective-permute-start | bytes 294920 | tf_op jit(solution)/shard_map/ppermute | solution.py:380
  43.5 1.6 %collective-permute-start.16 = (f32[160,128]{1,0:T(8,128)S(1)}, f32[160,128]{1,0:T(8,128)S(1)}, u32[]{:S(2)}, u32[]{:S(2)}) collective-permute-start(f32[160,128]{1,0:T(8,128)S(1)} %shard_map.75.refs_0_), channel_id=1, source_target_pairs={{0,16},{1,17},{2,18},{3,19},{4,20},{5,21},{6,22},{7,23},{8,24},{9,... | collective-permute-start | bytes 245768 | tf_op jit(solution)/shard_map/ppermute | solution.py:323
  45.0 1.9 %collective-permute-start.15 = (f32[160,128]{1,0:T(8,128)S(1)}, f32[160,128]{1,0:T(8,128)S(1)}, u32[]{:S(2)}, u32[]{:S(2)}) collective-permute-start(f32[160,128]{1,0:T(8,128)S(1)} %shard_map.75.refs_0_), channel_id=1, source_target_pairs={{0,8},{1,9},{2,10},{3,11},{4,12},{5,13},{6,14},{7,15},{8,0},{9,1},... | collective-permute-start | bytes 245768 | tf_op jit(solution)/shard_map/ppermute | solution.py:323
  47.2 2.7 %collective-permute-done.17.refs_3_ = f32[160,128]{1,0:T(8,128)S(1)} collective-permute-done((f32[160,128]{1,0:T(8,128)S(1)}, f32[160,128]{1,0:T(8,128)S(1)}, u32[]{:S(2)}, u32[]{:S(2)}) %collective-permute-start.17) | collective-permute-done | bytes 81952 | tf_op jit(solution)/shard_map/ppermute | solution.py:323
  49.9 0.6 %collective-permute-done.15.refs_1_ = f32[160,128]{1,0:T(8,128)S(1)} collective-permute-done((f32[160,128]{1,0:T(8,128)S(1)}, f32[160,128]{1,0:T(8,128)S(1)}, u32[]{:S(2)}, u32[]{:S(2)}) %collective-permute-start.15) | collective-permute-done | bytes 81952 | tf_op jit(solution)/shard_map/ppermute | solution.py:323
  50.6 1.0 %shard_map.79 = (bf16[1,128,2,384]{3,2,1,0:T(2,128)(2,1)}, f32[2,384,384]{2,1,0:T(8,128)}) custom-call(f32[4,160,128]{2,1,0:T(8,128)S(1)} %shard_map.78.refs_0_, bf16[1,128,2,384]{3,2,1,0:T(2,128)(2,1)S(1)} %shard_map.77.refs_4_.refs_1_), custom_call_target="tpu_custom_call" | custom-call | tf_op jit(solution)/shard_map/pallas_call | solution.py:28
  51.7 0.6 %collective-permute-done.21.refs_1_ = f32[4,160,128]{2,1,0:T(8,128)S(1)} collective-permute-done((f32[4,160,128]{2,1,0:T(8,128)S(1)}, f32[4,160,128]{2,1,0:T(8,128)S(1)}, u32[]{:S(2)}, u32[]{:S(2)}) %collective-permute-start.21) | collective-permute-done | bytes 327712 | tf_op jit(solution)/shard_map/ppermute | solution.py:323
  52.3 1.2 %shard_map.80 = f32[2,384,384]{2,1,0:T(8,128)} custom-call(f32[4,160,128]{2,1,0:T(8,128)S(1)} %shard_map.78.refs_0_, f32[4,160,128]{2,1,0:T(8,128)S(1)} %collective-permute-done.21.refs_1_, f32[2,384,384]{2,1,0:T(8,128)} %get-tuple-element.33.refs_2_), custom_call_target="tpu_custom_call", output_to_operand_aliasing={{}: (2, {})} | custom-call | tf_op jit(solution)/shard_map/pallas_call | solution.py:28
  (27 shorter events, 2.1 us)
Async XLA Ops:
  2.3 9.2 %collective-permute-start.3 = (bf16[160,384]{1,0:T(8,128)(2,1)S(1)}, bf16[160,384]{1,0:T(8,128)(2,1)S(1)}, u32[]{:S(2)}, u32[]{:S(2)}) collective-permute-start(bf16[160,384]{1,0:T(8,128)(2,1)S(1)} %get-tuple-element.19), channel_id=1, source_target_pairs={{0,8},{1,9},{2,10},{3,11},{4,12},{5,13},{6,14},{7,15},{8,0},{9,1},... | collective-permute-start | bytes 368648 | tf_op jit(solution)/shard_map/ppermute | solution.py:323
  5.3 16.6 %collective-permute-start.7 = (bf16[256,512]{1,0:T(8,128)(2,1)S(1)}, bf16[256,512]{1,0:T(8,128)(2,1)S(1)}, u32[]{:S(2)}, u32[]{:S(2)}) collective-permute-start(bf16[256,512]{1,0:T(8,128)(2,1)S(1)} %get-tuple-element.20.refs_1_), channel_id=1, source_target_pairs={{0,8},{1,9},{2,10},{3,11},{4,12},{5,13},{6,14},{7,15},{8,0},{9,1},... | collective-permute-start | bytes 786440 | tf_op jit(solution)/shard_map/ppermute | solution.py:323
  5.4 16.5 %collective-permute-start.8 = (bf16[256,512]{1,0:T(8,128)(2,1)S(1)}, bf16[256,512]{1,0:T(8,128)(2,1)S(1)}, u32[]{:S(2)}, u32[]{:S(2)}) collective-permute-start(bf16[256,512]{1,0:T(8,128)(2,1)S(1)} %get-tuple-element.21.refs_2_), channel_id=1, source_target_pairs={{0,8},{1,9},{2,10},{3,11},{4,12},{5,13},{6,14},{7,15},{8,0},{9,1},... | collective-permute-start | bytes 786440 | tf_op jit(solution)/shard_map/ppermute | solution.py:323
  7.4 5.8 %collective-permute-start = (bf16[128,384]{1,0:T(8,128)(2,1)S(1)}, bf16[128,384]{1,0:T(8,128)(2,1)S(1)}, u32[]{:S(2)}, u32[]{:S(2)}) collective-permute-start(bf16[128,384]{1,0:T(8,128)(2,1)S(1)} %get-tuple-element.18.refs_0_), channel_id=1, source_target_pairs={{0,2},{1,3},{2,0},{3,1},{4,6},{5,7},{6,4},{7,5},{8,10},{9,11},{10,... | collective-permute-start | bytes 294920 | tf_op jit(solution)/shard_map/ppermute | solution.py:323
  10.0 7.0 %collective-permute-start.1 = (bf16[128,384]{1,0:T(8,128)(2,1)S(1)}, bf16[128,384]{1,0:T(8,128)(2,1)S(1)}, u32[]{:S(2)}, u32[]{:S(2)}) collective-permute-start(bf16[128,384]{1,0:T(8,128)(2,1)S(1)} %get-tuple-element.18.refs_0_), channel_id=1, source_target_pairs={{0,1},{1,0},{2,3},{3,2},{4,5},{5,4},{6,7},{7,6},{8,9},{9,8},{10,11... | collective-permute-start | bytes 294920 | tf_op jit(solution)/shard_map/ppermute | solution.py:323
  11.6 6.8 %collective-permute-start.4 = (bf16[128,384]{1,0:T(8,128)(2,1)S(1)}, bf16[128,384]{1,0:T(8,128)(2,1)S(1)}, u32[]{:S(2)}, u32[]{:S(2)}) collective-permute-start(bf16[128,384]{1,0:T(8,128)(2,1)S(1)} %slice.8.refs_4_), channel_id=1, source_target_pairs={{0,2},{1,3},{2,0},{3,1},{4,6},{5,7},{6,4},{7,5},{8,10},{9,11},{10,... | collective-permute-start | bytes 294920 | tf_op jit(solution)/shard_map/ppermute | solution.py:323
  13.1 7.6 %collective-permute-start.2 = (bf16[128,384]{1,0:T(8,128)(2,1)S(1)}, bf16[128,384]{1,0:T(8,128)(2,1)S(1)}, u32[]{:S(2)}, u32[]{:S(2)}) collective-permute-start(bf16[128,384]{1,0:T(8,128)(2,1)S(1)} %collective-permute-done.refs_1_), channel_id=1, source_target_pairs={{0,1},{1,0},{2,3},{3,2},{4,5},{5,4},{6,7},{7,6},{8,9},{9,8},{10,11... | collective-permute-start | bytes 294920 | tf_op jit(solution)/shard_map/ppermute | solution.py:323
  17.0 5.0 %collective-permute-start.5 = (bf16[128,384]{1,0:T(8,128)(2,1)S(1)}, bf16[128,384]{1,0:T(8,128)(2,1)S(1)}, u32[]{:S(2)}, u32[]{:S(2)}) collective-permute-start(bf16[128,384]{1,0:T(8,128)(2,1)S(1)} %slice.8.refs_4_), channel_id=1, source_target_pairs={{0,1},{1,0},{2,3},{3,2},{4,5},{5,4},{6,7},{7,6},{8,9},{9,8},{10,11... | collective-permute-start | bytes 294920 | tf_op jit(solution)/shard_map/ppermute | solution.py:323
  18.3 4.7 %collective-permute-start.6 = (bf16[128,384]{1,0:T(8,128)(2,1)S(1)}, bf16[128,384]{1,0:T(8,128)(2,1)S(1)}, u32[]{:S(2)}, u32[]{:S(2)}) collective-permute-start(bf16[128,384]{1,0:T(8,128)(2,1)S(1)} %collective-permute-done.4.refs_5_), channel_id=1, source_target_pairs={{0,1},{1,0},{2,3},{3,2},{4,5},{5,4},{6,7},{7,6},{8,9},{9,8},{10,11... | collective-permute-start | bytes 294920 | tf_op jit(solution)/shard_map/ppermute | solution.py:323
  23.1 1.8 %collective-permute-start.9 = (bf16[512,384]{1,0:T(8,128)(2,1)S(1)}, bf16[512,384]{1,0:T(8,128)(2,1)S(1)}, u32[]{:S(2)}, u32[]{:S(2)}) collective-permute-start(bf16[512,384]{1,0:T(8,128)(2,1)S(1)} %get-tuple-element.23.refs_1_), channel_id=1, source_target_pairs={{0,4},{1,5},{2,6},{3,7},{4,0},{5,1},{6,2},{7,3},{8,12},{9,13},{10,... | collective-permute-start | bytes 1179656 | tf_op jit(solution)/shard_map/ppermute | solution.py:323
  24.9 13.1 %collective-permute-start.18 = (f32[512,384]{1,0:T(8,128)S(1)}, f32[512,384]{1,0:T(8,128)S(1)}, u32[]{:S(2)}, u32[]{:S(2)}) collective-permute-start(f32[512,384]{1,0:T(8,128)S(1)} %shard_map.71.refs_0_), channel_id=1, source_target_pairs={{0,4},{1,5},{2,6},{3,7},{4,0},{5,1},{6,2},{7,3},{8,12},{9,13},{10,... | collective-permute-start | bytes 2359304 | tf_op jit(solution)/shard_map/ppermute | solution.py:323
  25.8 1.7 %collective-permute-start.10 = (f32[320,128]{1,0:T(8,128)S(1)}, f32[320,128]{1,0:T(8,128)S(1)}, u32[]{:S(2)}, u32[]{:S(2)}) collective-permute-start(f32[320,128]{1,0:T(8,128)S(1)} %get-tuple-element.26), channel_id=1, source_target_pairs={{0,4},{1,5},{2,6},{3,7},{4,0},{5,1},{6,2},{7,3},{8,12},{9,13},{10,... | collective-permute-start | bytes 491528 | tf_op jit(solution)/shard_map/ppermute | solution.py:323
  27.5 5.5 %collective-permute-start.13 = (f32[160,128]{1,0:T(8,128)S(1)}, f32[160,128]{1,0:T(8,128)S(1)}, u32[]{:S(2)}, u32[]{:S(2)}) collective-permute-start(f32[160,128]{1,0:T(8,128)S(1)} %get-tuple-element.28), channel_id=1, source_target_pairs={{0,17},{1,16},{2,19},{3,18},{4,21},{5,20},{6,23},{7,22},{8,25},{9,... | collective-permute-start | bytes 245768 | tf_op jit(solution)/shard_map/ppermute | solution.py:323
  29.9 4.8 %collective-permute-start.11 = (f32[160,128]{1,0:T(8,128)S(1)}, f32[160,128]{1,0:T(8,128)S(1)}, u32[]{:S(2)}, u32[]{:S(2)}) collective-permute-start(f32[160,128]{1,0:T(8,128)S(1)} %get-tuple-element.28), channel_id=1, source_target_pairs={{0,16},{1,17},{2,18},{3,19},{4,20},{5,21},{6,22},{7,23},{8,24},{9,... | collective-permute-start | bytes 245768 | tf_op jit(solution)/shard_map/ppermute | solution.py:323
  30.4 4.4 %collective-permute-start.12 = (f32[160,128]{1,0:T(8,128)S(1)}, f32[160,128]{1,0:T(8,128)S(1)}, u32[]{:S(2)}, u32[]{:S(2)}) collective-permute-start(f32[160,128]{1,0:T(8,128)S(1)} %get-tuple-element.27.refs_0_.refs_2_), channel_id=1, source_target_pairs={{0,1},{1,0},{2,3},{3,2},{4,5},{5,4},{6,7},{7,6},{8,9},{9,8},{10,11... | collective-permute-start | bytes 245768 | tf_op jit(solution)/shard_map/ppermute | solution.py:323
  34.9 8.5 %collective-permute-start.14 = (f32[160,128]{1,0:T(8,128)S(1)}, f32[160,128]{1,0:T(8,128)S(1)}, u32[]{:S(2)}, u32[]{:S(2)}) collective-permute-start(f32[160,128]{1,0:T(8,128)S(1)} %shard_map.74.refs_0_), channel_id=1, source_target_pairs={{0,2},{1,3},{2,0},{3,1},{4,6},{5,7},{6,4},{7,5},{8,10},{9,11},{10,... | collective-permute-start | bytes 245768 | tf_op jit(solution)/shard_map/ppermute | solution.py:323
  38.2 8.7 %collective-permute-start.19 = (bf16[128,384]{1,0:T(8,128)(2,1)S(1)}, bf16[128,384]{1,0:T(8,128)(2,1)S(1)}, u32[]{:S(2)}, u32[]{:S(2)}) collective-permute-start(bf16[128,384]{1,0:T(8,128)(2,1)S(1)} %get-tuple-element.30), channel_id=1, source_target_pairs={{0,0},{1,4},{2,8},{3,12},{4,1},{5,5},{6,9},{7,13},{8,2},{9,6},{10,... | collective-permute-start | bytes 294920 | tf_op jit(solution)/shard_map/ppermute | solution.py:380
  38.9 8.0 %collective-permute-start.20 = (bf16[128,384]{1,0:T(8,128)(2,1)S(1)}, bf16[128,384]{1,0:T(8,128)(2,1)S(1)}, u32[]{:S(2)}, u32[]{:S(2)}) collective-permute-start(bf16[128,384]{1,0:T(8,128)(2,1)S(1)} %get-tuple-element.31), channel_id=1, source_target_pairs={{0,2},{1,6},{2,10},{3,14},{4,3},{5,7},{6,11},{7,15},{8,0},{9,4},{1... | collective-permute-start | bytes 294920 | tf_op jit(solution)/shard_map/ppermute | solution.py:380
  43.4 6.6 %collective-permute-start.17 = (f32[160,128]{1,0:T(8,128)S(1)}, f32[160,128]{1,0:T(8,128)S(1)}, u32[]{:S(2)}, u32[]{:S(2)}) collective-permute-start(f32[160,128]{1,0:T(8,128)S(1)} %shard_map.75.refs_0_), channel_id=1, source_target_pairs={{0,24},{1,25},{2,26},{3,27},{4,28},{5,29},{6,30},{7,31},{8,16},{9,... | collective-permute-start | bytes 245768 | tf_op jit(solution)/shard_map/ppermute | solution.py:323
  43.5 6.5 %collective-permute-start.16 = (f32[160,128]{1,0:T(8,128)S(1)}, f32[160,128]{1,0:T(8,128)S(1)}, u32[]{:S(2)}, u32[]{:S(2)}) collective-permute-start(f32[160,128]{1,0:T(8,128)S(1)} %shard_map.75.refs_0_), channel_id=1, source_target_pairs={{0,16},{1,17},{2,18},{3,19},{4,20},{5,21},{6,22},{7,23},{8,24},{9,... | collective-permute-start | bytes 245768 | tf_op jit(solution)/shard_map/ppermute | solution.py:323
  45.0 5.5 %collective-permute-start.15 = (f32[160,128]{1,0:T(8,128)S(1)}, f32[160,128]{1,0:T(8,128)S(1)}, u32[]{:S(2)}, u32[]{:S(2)}) collective-permute-start(f32[160,128]{1,0:T(8,128)S(1)} %shard_map.75.refs_0_), channel_id=1, source_target_pairs={{0,8},{1,9},{2,10},{3,11},{4,12},{5,13},{6,14},{7,15},{8,0},{9,1},... | collective-permute-start | bytes 245768 | tf_op jit(solution)/shard_map/ppermute | solution.py:323
  50.6 1.7 %collective-permute-start.21 = (f32[4,160,128]{2,1,0:T(8,128)S(1)}, f32[4,160,128]{2,1,0:T(8,128)S(1)}, u32[]{:S(2)}, u32[]{:S(2)}) collective-permute-start(f32[4,160,128]{2,1,0:T(8,128)S(1)} %shard_map.78.refs_0_), channel_id=1, source_target_pairs={{0,4},{1,5},{2,6},{3,7},{4,0},{5,1},{6,2},{7,3},{8,12},{9,13},{10,... | collective-permute-start | bytes 983048 | tf_op jit(solution)/shard_map/ppermute | solution.py:323

commit v20 on v19

--- a/solution.py
+++ b/solution.py
@@ -135,25 +135,36 @@
         at += piece.shape[0]
 
 
+def set_rows(blocks, rows):
+    column, height = lax.axis_index("pcol"), blocks[0].shape[0]
+    for step, block in zip((0, 2, 1, 3), blocks):
+        spot = jnp.bitwise_xor(column, step)
+        rows[pl.ds(pl.multiple_of(spot * height, height), height), :] = block[...]
+
+
+def own_kernel(*refs):
+    blocks, pieces, (rows, applied) = refs[:4], refs[4:-2], refs[-2:]
+    set_rows(blocks, rows)
+    at = 0
+    for piece in pieces:
+        applied[at : at + piece.shape[0]] = jnp.dot(piece[...], rows[...], preferred_element_type=jnp.float32)
+        at += piece.shape[0]
+
+
 def gather_kernel(*refs):
-    blocks, (rows, pack) = refs[:-2], refs[-2:]
-    column = lax.axis_index("pcol")
-    height = blocks[0].shape[0]
-    for index, block in enumerate(blocks):
-        spot = jnp.bitwise_xor(column, (0, 2, 1, 3)[index % 4])
-        rows[index // 4, pl.ds(pl.multiple_of(spot * height, height), height), :] = block[...]
-    pack[...] = rows[jnp.where(column // 2 == lax.axis_index("side"), 0, 1)]
-
-
-def apply_kernel(rows, *refs):
+    blocks, (own_rows, rows, pack) = refs[:4], refs[4:]
+    set_rows(blocks, rows)
+    same = lax.axis_index("pcol") // 2 == lax.axis_index("side")
+    pack[...] = jnp.where(same, own_rows[...], rows[...])
+
+
+def apply_kernel(own, rows, *refs):
     pieces, applied = refs[:-1], refs[-1]
-    count = len(pieces) // 2
     at = 0
-    for own, far in zip(pieces[:count], pieces[count:]):
-        total = jnp.dot(own[...], rows[0], preferred_element_type=jnp.float32)
-        total += jnp.dot(far[...], rows[1], preferred_element_type=jnp.float32)
-        applied[at : at + own.shape[0]] = total
-        at += own.shape[0]
+    for piece in pieces:
+        lines = slice(at, at + piece.shape[0])
+        applied[lines] = own[lines] + jnp.dot(piece[...], rows[...], preferred_element_type=jnp.float32)
+        at += piece.shape[0]
 
 
 def hold_kernel(value, out):
@@ -346,17 +357,15 @@
     far = [swap(piece, side=1) for piece in pieces]
 
 
+    product, line_shape = shape((extent, width), f32), shape((extent, width), bf16)
+    own_rows, own_product = call(
+        own_kernel, [line_shape, product], [VMEM] * (4 + len(cuts)), *blocks[:4], *pieces
+    )
     rows, pack = call(
-        gather_kernel,
-        [shape((2, extent, width), bf16), shape((extent, width), bf16)],
-        [VMEM] * len(blocks),
-        *blocks,
-        after=far,
+        gather_kernel, [line_shape] * 2, [VMEM] * 5, *blocks[4:], own_rows, after=far
     )
     got_pack = swap(pack, core=1)
-    mine = call(
-        apply_kernel, shape((extent, width), f32), [VMEM] * (1 + 2 * len(cuts)), rows, *pieces, *far
-    )
+    mine = call(apply_kernel, product, [VMEM] * (2 + len(cuts)), own_product, rows, *far)
     lines = HELD * LANES // 2
     part, half = shape((lines // 2, LANES), f32), shape((lines, LANES), f32)
     mine = call(

time: 53.6 us -> 53.6 us (level)
    pallas_call x13 -> x14, Pallas kernels: 5.94 us -> 6.12 us  [call(): pl.pallas_call(body, out_shape=outs, in_specs=list(specs) + [ANY] * len(a...]
where the time goes in v20:
time: 53.6 us; the launch traced here: 53.4 us
  starting transfers between devices  31.7 us (59%)
  waiting for transfers between devices  14.2 us (26%)
  Pallas kernels  6.12 us (11%)
  between operations  1.4 us (3%)
    ppermute x20, starting transfers between devices, swap(): return lax.ppermute(x, AXES, [(i, i ^ mask) for i in range(devices)])  26.6 us
    ppermute x20, waiting for transfers between devices, swap(): return lax.ppermute(x, AXES, [(i, i ^ mask) for i in range(devices)])  14.2 us
    pallas_call x14, Pallas kernels, call(): pl.pallas_call(body, out_shape=outs, in_specs=list(specs) + [ANY] * len(a...  6.12 us
    ppermute x2, starting transfers between devices, deliver(): return lax.ppermute(x, AXES, pairs)  5.13 us
  transfers between devices with their start and end apart: 22, of which 13 were waited for; matrix products, arithmetic and copies ran while one was open for 0% of the time, Pallas kernels for 6%

profile of v20, /device:TPU:0, one launch (start us, length us, event | category | flops | bytes accessed | tf_op | source)
XLA Modules:
  0.0 53.4 jit_solution(16502656031299939160)
XLA Ops:
  0.6 1.7 %shard_map.68 = (bf16[128,384]{1,0:T(8,128)(2,1)S(1)}, bf16[160,384]{1,0:T(8,128)(2,1)S(1)}, bf16[32,384]{1,0:T(8,128)(2,1)S(1)}, s32[2,8,128]{2,1,0:T(8,128)S(1...) custom-call(s32[2]{0:T(128)} %bitcast.1, bf16[1,128,2,384]{3,2,1,0:T(2,128)(2,1)} %refs_1_.1, ...), custom_call_target="tpu_custom_call" | custom-call | tf_op jit(solution)/shard_map/pallas_call | solution.py:28
  2.3 3.0 %collective-permute-start.3 = (bf16[160,384]{1,0:T(8,128)(2,1)S(1)}, bf16[160,384]{1,0:T(8,128)(2,1)S(1)}, u32[]{:S(2)}, u32[]{:S(2)}) collective-permute-start(bf16[160,384]{1,0:T(8,128)(2,1)S(1)} %get-tuple-element.24), channel_id=1, source_target_pairs={{0,8},{1,9},{2,10},{3,11},{4,12},{5,13},{6,14},{7,15},{8,0},{9,1},... | collective-permute-start | bytes 368648 | tf_op jit(solution)/shard_map/ppermute | solution.py:334
  5.4 1.9 %collective-permute-start.8 = (bf16[256,512]{1,0:T(8,128)(2,1)S(1)}, bf16[256,512]{1,0:T(8,128)(2,1)S(1)}, u32[]{:S(2)}, u32[]{:S(2)}) collective-permute-start(bf16[256,512]{1,0:T(8,128)(2,1)S(1)} %get-tuple-element.22.refs_5_), channel_id=1, source_target_pairs={{0,8},{1,9},{2,10},{3,11},{4,12},{5,13},{6,14},{7,15},{8,0},{9,1},... | collective-permute-start | bytes 786440 | tf_op jit(solution)/shard_map/ppermute | solution.py:334
  7.4 2.6 %collective-permute-start = (bf16[128,384]{1,0:T(8,128)(2,1)S(1)}, bf16[128,384]{1,0:T(8,128)(2,1)S(1)}, u32[]{:S(2)}, u32[]{:S(2)}) collective-permute-start(bf16[128,384]{1,0:T(8,128)(2,1)S(1)} %get-tuple-element.20.refs_0_), channel_id=1, source_target_pairs={{0,2},{1,3},{2,0},{3,1},{4,6},{5,7},{6,4},{7,5},{8,10},{9,11},{10,... | collective-permute-start | bytes 294920 | tf_op jit(solution)/shard_map/ppermute | solution.py:334
  10.0 1.6 %collective-permute-start.1 = (bf16[128,384]{1,0:T(8,128)(2,1)S(1)}, bf16[128,384]{1,0:T(8,128)(2,1)S(1)}, u32[]{:S(2)}, u32[]{:S(2)}) collective-permute-start(bf16[128,384]{1,0:T(8,128)(2,1)S(1)} %get-tuple-element.20.refs_0_), channel_id=1, source_target_pairs={{0,1},{1,0},{2,3},{3,2},{4,5},{5,4},{6,7},{7,6},{8,9},{9,8},{10,11... | collective-permute-start | bytes 294920 | tf_op jit(solution)/shard_map/ppermute | solution.py:334
  11.6 1.2 %collective-permute-start.4 = (bf16[128,384]{1,0:T(8,128)(2,1)S(1)}, bf16[128,384]{1,0:T(8,128)(2,1)S(1)}, u32[]{:S(2)}, u32[]{:S(2)}) collective-permute-start(bf16[128,384]{1,0:T(8,128)(2,1)S(1)} %slice.8.refs_0_), channel_id=1, source_target_pairs={{0,2},{1,3},{2,0},{3,1},{4,6},{5,7},{6,4},{7,5},{8,10},{9,11},{10,... | collective-permute-start | bytes 294920 | tf_op jit(solution)/shard_map/ppermute | solution.py:334
  13.1 3.8 %collective-permute-start.2 = (bf16[128,384]{1,0:T(8,128)(2,1)S(1)}, bf16[128,384]{1,0:T(8,128)(2,1)S(1)}, u32[]{:S(2)}, u32[]{:S(2)}) collective-permute-start(bf16[128,384]{1,0:T(8,128)(2,1)S(1)} %collective-permute-done.refs_1_), channel_id=1, source_target_pairs={{0,1},{1,0},{2,3},{3,2},{4,5},{5,4},{6,7},{7,6},{8,9},{9,8},{10,11... | collective-permute-start | bytes 294920 | tf_op jit(solution)/shard_map/ppermute | solution.py:334
  17.0 0.7 %collective-permute-start.5 = (bf16[128,384]{1,0:T(8,128)(2,1)S(1)}, bf16[128,384]{1,0:T(8,128)(2,1)S(1)}, u32[]{:S(2)}, u32[]{:S(2)}) collective-permute-start(bf16[128,384]{1,0:T(8,128)(2,1)S(1)} %slice.8.refs_0_), channel_id=1, source_target_pairs={{0,1},{1,0},{2,3},{3,2},{4,5},{5,4},{6,7},{7,6},{8,9},{9,8},{10,11... | collective-permute-start | bytes 294920 | tf_op jit(solution)/shard_map/ppermute | solution.py:334
  17.7 0.6 %collective-permute-done.4.refs_1_ = bf16[128,384]{1,0:T(8,128)(2,1)S(1)} collective-permute-done((bf16[128,384]{1,0:T(8,128)(2,1)S(1)}, bf16[128,384]{1,0:T(8,128)(2,1)S(1)}, u32[]{:S(2)}, u32[]{:S(2)}) %collective-permute-start.4) | collective-permute-done | bytes 98336 | tf_op jit(solution)/shard_map/ppermute | solution.py:334
  18.3 0.7 %collective-permute-start.6 = (bf16[128,384]{1,0:T(8,128)(2,1)S(1)}, bf16[128,384]{1,0:T(8,128)(2,1)S(1)}, u32[]{:S(2)}, u32[]{:S(2)}) collective-permute-start(bf16[128,384]{1,0:T(8,128)(2,1)S(1)} %collective-permute-done.4.refs_1_), channel_id=1, source_target_pairs={{0,1},{1,0},{2,3},{3,2},{4,5},{5,4},{6,7},{7,6},{8,9},{9,8},{10,11... | collective-permute-start | bytes 294920 | tf_op jit(solution)/shard_map/ppermute | solution.py:334
  19.0 1.6 %collective-permute-done.2.refs_3_ = bf16[128,384]{1,0:T(8,128)(2,1)S(1)} collective-permute-done((bf16[128,384]{1,0:T(8,128)(2,1)S(1)}, bf16[128,384]{1,0:T(8,128)(2,1)S(1)}, u32[]{:S(2)}, u32[]{:S(2)}) %collective-permute-start.2) | collective-permute-done | bytes 98336 | tf_op jit(solution)/shard_map/ppermute | solution.py:334
  20.7 0.5 shard_map.69
  21.2 0.8 %collective-permute-done.5.refs_2_ = bf16[128,384]{1,0:T(8,128)(2,1)S(1)} collective-permute-done((bf16[128,384]{1,0:T(8,128)(2,1)S(1)}, bf16[128,384]{1,0:T(8,128)(2,1)S(1)}, u32[]{:S(2)}, u32[]{:S(2)}) %collective-permute-start.5) | collective-permute-done | bytes 98336 | tf_op jit(solution)/shard_map/ppermute | solution.py:334
  22.0 1.0 %collective-permute-done.6.refs_3_ = bf16[128,384]{1,0:T(8,128)(2,1)S(1)} collective-permute-done((bf16[128,384]{1,0:T(8,128)(2,1)S(1)}, bf16[128,384]{1,0:T(8,128)(2,1)S(1)}, u32[]{:S(2)}, u32[]{:S(2)}) %collective-permute-start.6) | collective-permute-done | bytes 98336 | tf_op jit(solution)/shard_map/ppermute | solution.py:334
  23.6 1.3 %collective-permute-done.9.refs_1_.refs_2_ = bf16[512,384]{1,0:T(8,128)(2,1)S(1)} collective-permute-done((bf16[512,384]{1,0:T(8,128)(2,1)S(1)}, bf16[512,384]{1,0:T(8,128)(2,1)S(1)}, u32[]{:S(2)}, u32[]{:S(2)}) %collective-permute-start.9) | collective-permute-done | bytes 393248 | tf_op jit(solution)/shard_map/ppermute | solution.py:334
  25.0 0.7 %shard_map.73 = (f32[320,128]{1,0:T(8,128)S(1)}, f32[320,128]{1,0:T(8,128)S(1)}) custom-call(f32[512,384]{1,0:T(8,128)S(1)} %shard_map.72.refs_0_, bf16[512,384]{1,0:T(8,128)(2,1)S(1)} %get-tuple-element.27.refs_1_, bf16[512,384]{1,0:T(8,128)(2,1)S(1)} %collective-permute-done.9.refs_1_.refs_2_, bf16[32,384]{1,0:T(8,128)(2,1)S(1)} %get-tuple-element.28.refs_3_, ...), custom_call_target="tpu_custom_call" | custom-call | tf_op jit(solution)/shard_map/pallas_call | solution.py:28
  26.8 0.6 %collective-permute-done.10.refs_2_ = f32[320,128]{1,0:T(8,128)S(1)} collective-permute-done((f32[320,128]{1,0:T(8,128)S(1)}, f32[320,128]{1,0:T(8,128)S(1)}, u32[]{:S(2)}, u32[]{:S(2)}) %collective-permute-start.10) | collective-permute-done | bytes 163872 | tf_op jit(solution)/shard_map/ppermute | solution.py:334
  27.5 2.4 %collective-permute-start.13 = (f32[160,128]{1,0:T(8,128)S(1)}, f32[160,128]{1,0:T(8,128)S(1)}, u32[]{:S(2)}, u32[]{:S(2)}) collective-permute-start(f32[160,128]{1,0:T(8,128)S(1)} %get-tuple-element.32), channel_id=1, source_target_pairs={{0,17},{1,16},{2,19},{3,18},{4,21},{5,20},{6,23},{7,22},{8,25},{9,... | collective-permute-start | bytes 245768 | tf_op jit(solution)/shard_map/ppermute | solution.py:334
  29.9 0.5 collective-permute-start.11
  30.4 0.6 %collective-permute-start.12 = (f32[160,128]{1,0:T(8,128)S(1)}, f32[160,128]{1,0:T(8,128)S(1)}, u32[]{:S(2)}, u32[]{:S(2)}) collective-permute-start(f32[160,128]{1,0:T(8,128)S(1)} %get-tuple-element.31.refs_0_.refs_2_), channel_id=1, source_target_pairs={{0,1},{1,0},{2,3},{3,2},{4,5},{5,4},{6,7},{7,6},{8,9},{9,8},{10,11... | collective-permute-start | bytes 245768 | tf_op jit(solution)/shard_map/ppermute | solution.py:334
  31.0 1.9 %collective-permute-done.13.refs_3_ = f32[160,128]{1,0:T(8,128)S(1)} collective-permute-done((f32[160,128]{1,0:T(8,128)S(1)}, f32[160,128]{1,0:T(8,128)S(1)}, u32[]{:S(2)}, u32[]{:S(2)}) %collective-permute-start.13) | collective-permute-done | bytes 81952 | tf_op jit(solution)/shard_map/ppermute | solution.py:334
  33.0 1.7 %collective-permute-done.11.refs_1_ = f32[160,128]{1,0:T(8,128)S(1)} collective-permute-done((f32[160,128]{1,0:T(8,128)S(1)}, f32[160,128]{1,0:T(8,128)S(1)}, u32[]{:S(2)}, u32[]{:S(2)}) %collective-permute-start.11) | collective-permute-done | bytes 81952 | tf_op jit(solution)/shard_map/ppermute | solution.py:334
  34.9 3.1 %collective-permute-start.14 = (f32[160,128]{1,0:T(8,128)S(1)}, f32[160,128]{1,0:T(8,128)S(1)}, u32[]{:S(2)}, u32[]{:S(2)}) collective-permute-start(f32[160,128]{1,0:T(8,128)S(1)} %shard_map.75.refs_0_), channel_id=1, source_target_pairs={{0,2},{1,3},{2,0},{3,1},{4,6},{5,7},{6,4},{7,5},{8,10},{9,11},{10,... | collective-permute-start | bytes 245768 | tf_op jit(solution)/shard_map/ppermute | solution.py:334
  38.2 0.7 %collective-permute-start.19 = (bf16[128,384]{1,0:T(8,128)(2,1)S(1)}, bf16[128,384]{1,0:T(8,128)(2,1)S(1)}, u32[]{:S(2)}, u32[]{:S(2)}) collective-permute-start(bf16[128,384]{1,0:T(8,128)(2,1)S(1)} %get-tuple-element.34), channel_id=1, source_target_pairs={{0,0},{1,4},{2,8},{3,12},{4,1},{5,5},{6,9},{7,13},{8,2},{9,6},{10,... | collective-permute-start | bytes 294920 | tf_op jit(solution)/shard_map/ppermute | solution.py:389
  38.9 4.5 %collective-permute-start.20 = (bf16[128,384]{1,0:T(8,128)(2,1)S(1)}, bf16[128,384]{1,0:T(8,128)(2,1)S(1)}, u32[]{:S(2)}, u32[]{:S(2)}) collective-permute-start(bf16[128,384]{1,0:T(8,128)(2,1)S(1)} %get-tuple-element.35), channel_id=1, source_target_pairs={{0,2},{1,6},{2,10},{3,14},{4,3},{5,7},{6,11},{7,15},{8,0},{9,4},{1... | collective-permute-start | bytes 294920 | tf_op jit(solution)/shard_map/ppermute | solution.py:389
  43.4 1.6 %collective-permute-start.16 = (f32[160,128]{1,0:T(8,128)S(1)}, f32[160,128]{1,0:T(8,128)S(1)}, u32[]{:S(2)}, u32[]{:S(2)}) collective-permute-start(f32[160,128]{1,0:T(8,128)S(1)} %shard_map.76.refs_0_), channel_id=1, source_target_pairs={{0,16},{1,17},{2,18},{3,19},{4,20},{5,21},{6,22},{7,23},{8,24},{9,... | collective-permute-start | bytes 245768 | tf_op jit(solution)/shard_map/ppermute | solution.py:334
  45.0 1.9 %collective-permute-start.15 = (f32[160,128]{1,0:T(8,128)S(1)}, f32[160,128]{1,0:T(8,128)S(1)}, u32[]{:S(2)}, u32[]{:S(2)}) collective-permute-start(f32[160,128]{1,0:T(8,128)S(1)} %shard_map.76.refs_0_), channel_id=1, source_target_pairs={{0,8},{1,9},{2,10},{3,11},{4,12},{5,13},{6,14},{7,15},{8,0},{9,1},... | collective-permute-start | bytes 245768 | tf_op jit(solution)/shard_map/ppermute | solution.py:334
  47.2 2.7 %collective-permute-done.17.refs_3_ = f32[160,128]{1,0:T(8,128)S(1)} collective-permute-done((f32[160,128]{1,0:T(8,128)S(1)}, f32[160,128]{1,0:T(8,128)S(1)}, u32[]{:S(2)}, u32[]{:S(2)}) %collective-permute-start.17) | collective-permute-done | bytes 81952 | tf_op jit(solution)/shard_map/ppermute | solution.py:334
  49.9 0.6 %collective-permute-done.15.refs_1_ = f32[160,128]{1,0:T(8,128)S(1)} collective-permute-done((f32[160,128]{1,0:T(8,128)S(1)}, f32[160,128]{1,0:T(8,128)S(1)}, u32[]{:S(2)}, u32[]{:S(2)}) %collective-permute-start.15) | collective-permute-done | bytes 81952 | tf_op jit(solution)/shard_map/ppermute | solution.py:334
  50.6 1.0 %shard_map.80 = (bf16[1,128,2,384]{3,2,1,0:T(2,128)(2,1)}, f32[2,384,384]{2,1,0:T(8,128)}) custom-call(f32[4,160,128]{2,1,0:T(8,128)S(1)} %shard_map.79.refs_0_, bf16[1,128,2,384]{3,2,1,0:T(2,128)(2,1)S(1)} %shard_map.78.refs_4_.refs_1_), custom_call_target="tpu_custom_call" | custom-call | tf_op jit(solution)/shard_map/pallas_call | solution.py:28
  51.7 0.6 %collective-permute-done.21.refs_1_ = f32[4,160,128]{2,1,0:T(8,128)S(1)} collective-permute-done((f32[4,160,128]{2,1,0:T(8,128)S(1)}, f32[4,160,128]{2,1,0:T(8,128)S(1)}, u32[]{:S(2)}, u32[]{:S(2)}) %collective-permute-start.21) | collective-permute-done | bytes 327712 | tf_op jit(solution)/shard_map/ppermute | solution.py:334
  52.2 1.2 %shard_map.81 = f32[2,384,384]{2,1,0:T(8,128)} custom-call(f32[4,160,128]{2,1,0:T(8,128)S(1)} %shard_map.79.refs_0_, f32[4,160,128]{2,1,0:T(8,128)S(1)} %collective-permute-done.21.refs_1_, f32[2,384,384]{2,1,0:T(8,128)} %get-tuple-element.37.refs_2_), custom_call_target="tpu_custom_call", output_to_operand_aliasing={{}: (2, {})} | custom-call | tf_op jit(solution)/shard_map/pallas_call | solution.py:28
  (28 shorter events, 2.5 us)
Async XLA Ops:
  2.3 9.2 %collective-permute-start.3 = (bf16[160,384]{1,0:T(8,128)(2,1)S(1)}, bf16[160,384]{1,0:T(8,128)(2,1)S(1)}, u32[]{:S(2)}, u32[]{:S(2)}) collective-permute-start(bf16[160,384]{1,0:T(8,128)(2,1)S(1)} %get-tuple-element.24), channel_id=1, source_target_pairs={{0,8},{1,9},{2,10},{3,11},{4,12},{5,13},{6,14},{7,15},{8,0},{9,1},... | collective-permute-start | bytes 368648 | tf_op jit(solution)/shard_map/ppermute | solution.py:334
  5.3 16.6 %collective-permute-start.7 = (bf16[256,512]{1,0:T(8,128)(2,1)S(1)}, bf16[256,512]{1,0:T(8,128)(2,1)S(1)}, u32[]{:S(2)}, u32[]{:S(2)}) collective-permute-start(bf16[256,512]{1,0:T(8,128)(2,1)S(1)} %get-tuple-element.21.refs_4_), channel_id=1, source_target_pairs={{0,8},{1,9},{2,10},{3,11},{4,12},{5,13},{6,14},{7,15},{8,0},{9,1},... | collective-permute-start | bytes 786440 | tf_op jit(solution)/shard_map/ppermute | solution.py:334
  5.4 16.5 %collective-permute-start.8 = (bf16[256,512]{1,0:T(8,128)(2,1)S(1)}, bf16[256,512]{1,0:T(8,128)(2,1)S(1)}, u32[]{:S(2)}, u32[]{:S(2)}) collective-permute-start(bf16[256,512]{1,0:T(8,128)(2,1)S(1)} %get-tuple-element.22.refs_5_), channel_id=1, source_target_pairs={{0,8},{1,9},{2,10},{3,11},{4,12},{5,13},{6,14},{7,15},{8,0},{9,1},... | collective-permute-start | bytes 786440 | tf_op jit(solution)/shard_map/ppermute | solution.py:334
  7.4 5.8 %collective-permute-start = (bf16[128,384]{1,0:T(8,128)(2,1)S(1)}, bf16[128,384]{1,0:T(8,128)(2,1)S(1)}, u32[]{:S(2)}, u32[]{:S(2)}) collective-permute-start(bf16[128,384]{1,0:T(8,128)(2,1)S(1)} %get-tuple-element.20.refs_0_), channel_id=1, source_target_pairs={{0,2},{1,3},{2,0},{3,1},{4,6},{5,7},{6,4},{7,5},{8,10},{9,11},{10,... | collective-permute-start | bytes 294920 | tf_op jit(solution)/shard_map/ppermute | solution.py:334
  10.0 7.0 %collective-permute-start.1 = (bf16[128,384]{1,0:T(8,128)(2,1)S(1)}, bf16[128,384]{1,0:T(8,128)(2,1)S(1)}, u32[]{:S(2)}, u32[]{:S(2)}) collective-permute-start(bf16[128,384]{1,0:T(8,128)(2,1)S(1)} %get-tuple-element.20.refs_0_), channel_id=1, source_target_pairs={{0,1},{1,0},{2,3},{3,2},{4,5},{5,4},{6,7},{7,6},{8,9},{9,8},{10,11... | collective-permute-start | bytes 294920 | tf_op jit(solution)/shard_map/ppermute | solution.py:334
  11.6 6.8 %collective-permute-start.4 = (bf16[128,384]{1,0:T(8,128)(2,1)S(1)}, bf16[128,384]{1,0:T(8,128)(2,1)S(1)}, u32[]{:S(2)}, u32[]{:S(2)}) collective-permute-start(bf16[128,384]{1,0:T(8,128)(2,1)S(1)} %slice.8.refs_0_), channel_id=1, source_target_pairs={{0,2},{1,3},{2,0},{3,1},{4,6},{5,7},{6,4},{7,5},{8,10},{9,11},{10,... | collective-permute-start | bytes 294920 | tf_op jit(solution)/shard_map/ppermute | solution.py:334
  13.1 7.6 %collective-permute-start.2 = (bf16[128,384]{1,0:T(8,128)(2,1)S(1)}, bf16[128,384]{1,0:T(8,128)(2,1)S(1)}, u32[]{:S(2)}, u32[]{:S(2)}) collective-permute-start(bf16[128,384]{1,0:T(8,128)(2,1)S(1)} %collective-permute-done.refs_1_), channel_id=1, source_target_pairs={{0,1},{1,0},{2,3},{3,2},{4,5},{5,4},{6,7},{7,6},{8,9},{9,8},{10,11... | collective-permute-start | bytes 294920 | tf_op jit(solution)/shard_map/ppermute | solution.py:334
  17.0 5.0 %collective-permute-start.5 = (bf16[128,384]{1,0:T(8,128)(2,1)S(1)}, bf16[128,384]{1,0:T(8,128)(2,1)S(1)}, u32[]{:S(2)}, u32[]{:S(2)}) collective-permute-start(bf16[128,384]{1,0:T(8,128)(2,1)S(1)} %slice.8.refs_0_), channel_id=1, source_target_pairs={{0,1},{1,0},{2,3},{3,2},{4,5},{5,4},{6,7},{7,6},{8,9},{9,8},{10,11... | collective-permute-start | bytes 294920 | tf_op jit(solution)/shard_map/ppermute | solution.py:334
  18.3 4.7 %collective-permute-start.6 = (bf16[128,384]{1,0:T(8,128)(2,1)S(1)}, bf16[128,384]{1,0:T(8,128)(2,1)S(1)}, u32[]{:S(2)}, u32[]{:S(2)}) collective-permute-start(bf16[128,384]{1,0:T(8,128)(2,1)S(1)} %collective-permute-done.4.refs_1_), channel_id=1, source_target_pairs={{0,1},{1,0},{2,3},{3,2},{4,5},{5,4},{6,7},{7,6},{8,9},{9,8},{10,11... | collective-permute-start | bytes 294920 | tf_op jit(solution)/shard_map/ppermute | solution.py:334
  23.1 1.8 %collective-permute-start.9 = (bf16[512,384]{1,0:T(8,128)(2,1)S(1)}, bf16[512,384]{1,0:T(8,128)(2,1)S(1)}, u32[]{:S(2)}, u32[]{:S(2)}) collective-permute-start(bf16[512,384]{1,0:T(8,128)(2,1)S(1)} %get-tuple-element.27.refs_1_), channel_id=1, source_target_pairs={{0,4},{1,5},{2,6},{3,7},{4,0},{5,1},{6,2},{7,3},{8,12},{9,13},{10,... | collective-permute-start | bytes 1179656 | tf_op jit(solution)/shard_map/ppermute | solution.py:334
  24.9 13.1 %collective-permute-start.18 = (f32[512,384]{1,0:T(8,128)S(1)}, f32[512,384]{1,0:T(8,128)S(1)}, u32[]{:S(2)}, u32[]{:S(2)}) collective-permute-start(f32[512,384]{1,0:T(8,128)S(1)} %shard_map.72.refs_0_), channel_id=1, source_target_pairs={{0,4},{1,5},{2,6},{3,7},{4,0},{5,1},{6,2},{7,3},{8,12},{9,13},{10,... | collective-permute-start | bytes 2359304 | tf_op jit(solution)/shard_map/ppermute | solution.py:334
  25.7 1.7 %collective-permute-start.10 = (f32[320,128]{1,0:T(8,128)S(1)}, f32[320,128]{1,0:T(8,128)S(1)}, u32[]{:S(2)}, u32[]{:S(2)}) collective-permute-start(f32[320,128]{1,0:T(8,128)S(1)} %get-tuple-element.30), channel_id=1, source_target_pairs={{0,4},{1,5},{2,6},{3,7},{4,0},{5,1},{6,2},{7,3},{8,12},{9,13},{10,... | collective-permute-start | bytes 491528 | tf_op jit(solution)/shard_map/ppermute | solution.py:334
  27.5 5.5 %collective-permute-start.13 = (f32[160,128]{1,0:T(8,128)S(1)}, f32[160,128]{1,0:T(8,128)S(1)}, u32[]{:S(2)}, u32[]{:S(2)}) collective-permute-start(f32[160,128]{1,0:T(8,128)S(1)} %get-tuple-element.32), channel_id=1, source_target_pairs={{0,17},{1,16},{2,19},{3,18},{4,21},{5,20},{6,23},{7,22},{8,25},{9,... | collective-permute-start | bytes 245768 | tf_op jit(solution)/shard_map/ppermute | solution.py:334
  29.9 4.8 %collective-permute-start.11 = (f32[160,128]{1,0:T(8,128)S(1)}, f32[160,128]{1,0:T(8,128)S(1)}, u32[]{:S(2)}, u32[]{:S(2)}) collective-permute-start(f32[160,128]{1,0:T(8,128)S(1)} %get-tuple-element.32), channel_id=1, source_target_pairs={{0,16},{1,17},{2,18},{3,19},{4,20},{5,21},{6,22},{7,23},{8,24},{9,... | collective-permute-start | bytes 245768 | tf_op jit(solution)/shard_map/ppermute | solution.py:334
  30.4 4.4 %collective-permute-start.12 = (f32[160,128]{1,0:T(8,128)S(1)}, f32[160,128]{1,0:T(8,128)S(1)}, u32[]{:S(2)}, u32[]{:S(2)}) collective-permute-start(f32[160,128]{1,0:T(8,128)S(1)} %get-tuple-element.31.refs_0_.refs_2_), channel_id=1, source_target_pairs={{0,1},{1,0},{2,3},{3,2},{4,5},{5,4},{6,7},{7,6},{8,9},{9,8},{10,11... | collective-permute-start | bytes 245768 | tf_op jit(solution)/shard_map/ppermute | solution.py:334
  34.9 8.5 %collective-permute-start.14 = (f32[160,128]{1,0:T(8,128)S(1)}, f32[160,128]{1,0:T(8,128)S(1)}, u32[]{:S(2)}, u32[]{:S(2)}) collective-permute-start(f32[160,128]{1,0:T(8,128)S(1)} %shard_map.75.refs_0_), channel_id=1, source_target_pairs={{0,2},{1,3},{2,0},{3,1},{4,6},{5,7},{6,4},{7,5},{8,10},{9,11},{10,... | collective-permute-start | bytes 245768 | tf_op jit(solution)/shard_map/ppermute | solution.py:334
  38.2 8.7 %collective-permute-start.19 = (bf16[128,384]{1,0:T(8,128)(2,1)S(1)}, bf16[128,384]{1,0:T(8,128)(2,1)S(1)}, u32[]{:S(2)}, u32[]{:S(2)}) collective-permute-start(bf16[128,384]{1,0:T(8,128)(2,1)S(1)} %get-tuple-element.34), channel_id=1, source_target_pairs={{0,0},{1,4},{2,8},{3,12},{4,1},{5,5},{6,9},{7,13},{8,2},{9,6},{10,... | collective-permute-start | bytes 294920 | tf_op jit(solution)/shard_map/ppermute | solution.py:389
  38.9 8.0 %collective-permute-start.20 = (bf16[128,384]{1,0:T(8,128)(2,1)S(1)}, bf16[128,384]{1,0:T(8,128)(2,1)S(1)}, u32[]{:S(2)}, u32[]{:S(2)}) collective-permute-start(bf16[128,384]{1,0:T(8,128)(2,1)S(1)} %get-tuple-element.35), channel_id=1, source_target_pairs={{0,2},{1,6},{2,10},{3,14},{4,3},{5,7},{6,11},{7,15},{8,0},{9,4},{1... | collective-permute-start | bytes 294920 | tf_op jit(solution)/shard_map/ppermute | solution.py:389
  43.4 6.6 %collective-permute-start.17 = (f32[160,128]{1,0:T(8,128)S(1)}, f32[160,128]{1,0:T(8,128)S(1)}, u32[]{:S(2)}, u32[]{:S(2)}) collective-permute-start(f32[160,128]{1,0:T(8,128)S(1)} %shard_map.76.refs_0_), channel_id=1, source_target_pairs={{0,24},{1,25},{2,26},{3,27},{4,28},{5,29},{6,30},{7,31},{8,16},{9,... | collective-permute-start | bytes 245768 | tf_op jit(solution)/shard_map/ppermute | solution.py:334
  43.4 6.5 %collective-permute-start.16 = (f32[160,128]{1,0:T(8,128)S(1)}, f32[160,128]{1,0:T(8,128)S(1)}, u32[]{:S(2)}, u32[]{:S(2)}) collective-permute-start(f32[160,128]{1,0:T(8,128)S(1)} %shard_map.76.refs_0_), channel_id=1, source_target_pairs={{0,16},{1,17},{2,18},{3,19},{4,20},{5,21},{6,22},{7,23},{8,24},{9,... | collective-permute-start | bytes 245768 | tf_op jit(solution)/shard_map/ppermute | solution.py:334
  45.0 5.5 %collective-permute-start.15 = (f32[160,128]{1,0:T(8,128)S(1)}, f32[160,128]{1,0:T(8,128)S(1)}, u32[]{:S(2)}, u32[]{:S(2)}) collective-permute-start(f32[160,128]{1,0:T(8,128)S(1)} %shard_map.76.refs_0_), channel_id=1, source_target_pairs={{0,8},{1,9},{2,10},{3,11},{4,12},{5,13},{6,14},{7,15},{8,0},{9,1},... | collective-permute-start | bytes 245768 | tf_op jit(solution)/shard_map/ppermute | solution.py:334
  50.6 1.7 %collective-permute-start.21 = (f32[4,160,128]{2,1,0:T(8,128)S(1)}, f32[4,160,128]{2,1,0:T(8,128)S(1)}, u32[]{:S(2)}, u32[]{:S(2)}) collective-permute-start(f32[4,160,128]{2,1,0:T(8,128)S(1)} %shard_map.79.refs_0_), channel_id=1, source_target_pairs={{0,4},{1,5},{2,6},{3,7},{4,0},{5,1},{6,2},{7,3},{8,12},{9,13},{10,... | collective-permute-start | bytes 983048 | tf_op jit(solution)/shard_map/ppermute | solution.py:334

commit v21 on v20

--- a/solution.py
+++ b/solution.py
@@ -159,22 +159,19 @@
 
 
 def apply_kernel(own, rows, *refs):
-    pieces, applied = refs[:-1], refs[-1]
-    at = 0
-    for piece in pieces:
+    count, at = len(refs) // 2, 0
+    for piece, applied in zip(refs[:count], refs[count:]):
         lines = slice(at, at + piece.shape[0])
-        applied[lines] = own[lines] + jnp.dot(piece[...], rows[...], preferred_element_type=jnp.float32)
+        applied[...] = own[lines] + jnp.dot(piece[...], rows[...], preferred_element_type=jnp.float32)
         at += piece.shape[0]
 
 
-def hold_kernel(value, out):
-    del value, out
-
-
-def couple_kernel(applied, pack, got_pack, own_inverse, got_inverse, keep, send, packed):
+def couple_kernel(pack, got_pack, own_inverse, got_inverse, *refs):
     core, column = lax.axis_index("core"), lax.axis_index("pcol")
-    high = applied[...].astype(jnp.bfloat16)
-    low = (applied[...] - high.astype(jnp.float32)).astype(jnp.bfloat16)
+    parts, (keep, send, packed) = refs[:-3], refs[-3:]
+    applied = jnp.concatenate([part[...] for part in parts], 0)
+    high = applied.astype(jnp.bfloat16)
+    low = (applied - high.astype(jnp.float32)).astype(jnp.bfloat16)
     rows = jnp.where(column % 2 == core, pack[...], got_pack[...])
     blocks = {}
     for first in range(BLOCKS):
@@ -201,8 +198,12 @@
     send[...] = whole[pl.ds(pl.multiple_of((1 - point) * size, 8), size), :]
 
 
-def output_kernel(mine, other, out_near, out_far, half):
-    half[...] = -(mine[...] + other[...]).astype(jnp.bfloat16)
+def output_kernel(*refs):
+    parts, (out_near, out_far, half) = refs[:-3], refs[-3:]
+    count, at = len(parts) // 2, 0
+    for mine, other in zip(parts[:count], parts[count:]):
+        half[at : at + mine.shape[0]] = -(mine[...] + other[...]).astype(jnp.bfloat16)
+        at += mine.shape[0]
     height, side, core = out_near.shape[0], lax.axis_index("side"), lax.axis_index("core")
     for out, at in ((out_near, side), (out_far, 1 - side)):
         spot = at * 2 + core
@@ -365,16 +366,16 @@
         gather_kernel, [line_shape] * 2, [VMEM] * 5, *blocks[4:], own_rows, after=far
     )
     got_pack = swap(pack, core=1)
-    mine = call(apply_kernel, product, [VMEM] * (2 + len(cuts)), own_product, rows, *far)
+    mine = call(
+        apply_kernel, [shape((lines, width), f32) for lines in cuts], [VMEM] * (2 + len(cuts)),
+        own_product, rows, *far,
+    )
     lines = HELD * LANES // 2
     part, half = shape((lines // 2, LANES), f32), shape((lines, LANES), f32)
-    mine = call(
-        hold_kernel, shape(mine.shape, f32), [ANY], mine, out_specs=ANY, after=[got_pack], alias={0: 0}
-    )
-    other = swap(mine, core=1)
+    other = [swap(x, core=1) for x in mine]
     keep, send = call(
-        couple_kernel, [half, half], [VMEM] * 5,
-        mine, pack, got_pack, own_inverse, got_inverse,
+        couple_kernel, [half, half], [VMEM] * (4 + len(cuts)),
+        pack, got_pack, own_inverse, got_inverse, *mine,
         scratch=[pltpu.VMEM((2 * lines, LANES), f32)],
     )
     keep, send = call(
@@ -393,7 +394,7 @@
         keep, swap(send, point=1), swap(keep, column=1), swap(send, point=1, column=1),
     )
     out_near, out_far = call(
-        output_kernel, [block, block], [VMEM] * 2, mine, other,
+        output_kernel, [block, block], [VMEM] * (2 * len(cuts)), *mine, *other,
         scratch=[pltpu.VMEM((extent, width), bf16)],
         after=[keep],
     )

time: 53.6 us -> 53.2 us (level)
  waiting for transfers between devices: 14.2 us -> 13.5 us
    ppermute x20 -> x21, waiting for transfers between devices: 14.2 us -> 13.5 us  [swap(): return lax.ppermute(x, AXES, [(i, i ^ mask) for i in range(devices)])]
    ppermute x20 -> x21, starting transfers between devices: 26.6 us -> 26.8 us  [swap(): return lax.ppermute(x, AXES, [(i, i ^ mask) for i in range(devices)])]
    pallas_call x14 -> x13, Pallas kernels: 6.12 us -> 6.12 us  [call(): pl.pallas_call(body, out_shape=outs, in_specs=list(specs) + [ANY] * len(a...]
  transfers between devices with their start and end apart: 22 -> 23, of which waited for: 13 -> 13; matrix products, arithmetic and copies ran while one was open for 0% -> 0% of each run, Pallas kernels for 6% -> 6%
where the time goes in v21:
time: 53.2 us; the launch traced here: 53 us
  starting transfers between devices  31.9 us (60%)
  waiting for transfers between devices  13.5 us (25%)
  Pallas kernels  6.12 us (12%)
  between operations  1.4 us (3%)
    ppermute x21, starting transfers between devices, swap(): return lax.ppermute(x, AXES, [(i, i ^ mask) for i in range(devices)])  26.8 us
    ppermute x21, waiting for transfers between devices, swap(): return lax.ppermute(x, AXES, [(i, i ^ mask) for i in range(devices)])  13.5 us
    pallas_call x13, Pallas kernels, call(): pl.pallas_call(body, out_shape=outs, in_specs=list(specs) + [ANY] * len(a...  6.12 us
    ppermute x2, starting transfers between devices, deliver(): return lax.ppermute(x, AXES, pairs)  5.13 us
  transfers between devices with their start and end apart: 23, of which 13 were waited for; matrix products, arithmetic and copies ran while one was open for 0% of the time, Pallas kernels for 6%

profile of v21, /device:TPU:0, one launch (start us, length us, event | category | flops | bytes accessed | tf_op | source)
XLA Modules:
  0.0 53.0 jit_solution(17262936787129434080)
XLA Ops:
  0.6 1.7 %shard_map.68 = (bf16[128,384]{1,0:T(8,128)(2,1)S(1)}, bf16[160,384]{1,0:T(8,128)(2,1)S(1)}, bf16[32,384]{1,0:T(8,128)(2,1)S(1)}, s32[2,8,128]{2,1,0:T(8,128)S(1...) custom-call(s32[2]{0:T(128)} %bitcast.1, bf16[1,128,2,384]{3,2,1,0:T(2,128)(2,1)} %refs_1_.1, ...), custom_call_target="tpu_custom_call" | custom-call | tf_op jit(solution)/shard_map/pallas_call | solution.py:28
  2.3 3.0 %collective-permute-start = (bf16[160,384]{1,0:T(8,128)(2,1)S(1)}, bf16[160,384]{1,0:T(8,128)(2,1)S(1)}, u32[]{:S(2)}, u32[]{:S(2)}) collective-permute-start(bf16[160,384]{1,0:T(8,128)(2,1)S(1)} %get-tuple-element.22), channel_id=1, source_target_pairs={{0,8},{1,9},{2,10},{3,11},{4,12},{5,13},{6,14},{7,15},{8,0},{9,1},... | collective-permute-start | bytes 368648 | tf_op jit(solution)/shard_map/ppermute | solution.py:335
  5.4 1.9 %collective-permute-start.8 = (bf16[256,512]{1,0:T(8,128)(2,1)S(1)}, bf16[256,512]{1,0:T(8,128)(2,1)S(1)}, u32[]{:S(2)}, u32[]{:S(2)}) collective-permute-start(bf16[256,512]{1,0:T(8,128)(2,1)S(1)} %get-tuple-element.25.refs_5_), channel_id=1, source_target_pairs={{0,8},{1,9},{2,10},{3,11},{4,12},{5,13},{6,14},{7,15},{8,0},{9,1},... | collective-permute-start | bytes 786440 | tf_op jit(solution)/shard_map/ppermute | solution.py:335
  7.4 2.6 %collective-permute-start.4 = (bf16[128,384]{1,0:T(8,128)(2,1)S(1)}, bf16[128,384]{1,0:T(8,128)(2,1)S(1)}, u32[]{:S(2)}, u32[]{:S(2)}) collective-permute-start(bf16[128,384]{1,0:T(8,128)(2,1)S(1)} %get-tuple-element.23.refs_0_), channel_id=1, source_target_pairs={{0,2},{1,3},{2,0},{3,1},{4,6},{5,7},{6,4},{7,5},{8,10},{9,11},{10,... | collective-permute-start | bytes 294920 | tf_op jit(solution)/shard_map/ppermute | solution.py:335
  10.0 1.6 %collective-permute-start.5 = (bf16[128,384]{1,0:T(8,128)(2,1)S(1)}, bf16[128,384]{1,0:T(8,128)(2,1)S(1)}, u32[]{:S(2)}, u32[]{:S(2)}) collective-permute-start(bf16[128,384]{1,0:T(8,128)(2,1)S(1)} %get-tuple-element.23.refs_0_), channel_id=1, source_target_pairs={{0,1},{1,0},{2,3},{3,2},{4,5},{5,4},{6,7},{7,6},{8,9},{9,8},{10,11... | collective-permute-start | bytes 294920 | tf_op jit(solution)/shard_map/ppermute | solution.py:335
  11.6 1.2 %collective-permute-start.1 = (bf16[128,384]{1,0:T(8,128)(2,1)S(1)}, bf16[128,384]{1,0:T(8,128)(2,1)S(1)}, u32[]{:S(2)}, u32[]{:S(2)}) collective-permute-start(bf16[128,384]{1,0:T(8,128)(2,1)S(1)} %slice.8.refs_0_), channel_id=1, source_target_pairs={{0,2},{1,3},{2,0},{3,1},{4,6},{5,7},{6,4},{7,5},{8,10},{9,11},{10,... | collective-permute-start | bytes 294920 | tf_op jit(solution)/shard_map/ppermute | solution.py:335
  13.1 3.8 %collective-permute-start.6 = (bf16[128,384]{1,0:T(8,128)(2,1)S(1)}, bf16[128,384]{1,0:T(8,128)(2,1)S(1)}, u32[]{:S(2)}, u32[]{:S(2)}) collective-permute-start(bf16[128,384]{1,0:T(8,128)(2,1)S(1)} %collective-permute-done.4.refs_1_), channel_id=1, source_target_pairs={{0,1},{1,0},{2,3},{3,2},{4,5},{5,4},{6,7},{7,6},{8,9},{9,8},{10,11... | collective-permute-start | bytes 294920 | tf_op jit(solution)/shard_map/ppermute | solution.py:335
  17.0 0.7 %collective-permute-start.2 = (bf16[128,384]{1,0:T(8,128)(2,1)S(1)}, bf16[128,384]{1,0:T(8,128)(2,1)S(1)}, u32[]{:S(2)}, u32[]{:S(2)}) collective-permute-start(bf16[128,384]{1,0:T(8,128)(2,1)S(1)} %slice.8.refs_0_), channel_id=1, source_target_pairs={{0,1},{1,0},{2,3},{3,2},{4,5},{5,4},{6,7},{7,6},{8,9},{9,8},{10,11... | collective-permute-start | bytes 294920 | tf_op jit(solution)/shard_map/ppermute | solution.py:335
  17.7 0.6 %collective-permute-done.1.refs_1_ = bf16[128,384]{1,0:T(8,128)(2,1)S(1)} collective-permute-done((bf16[128,384]{1,0:T(8,128)(2,1)S(1)}, bf16[128,384]{1,0:T(8,128)(2,1)S(1)}, u32[]{:S(2)}, u32[]{:S(2)}) %collective-permute-start.1) | collective-permute-done | bytes 98336 | tf_op jit(solution)/shard_map/ppermute | solution.py:335
  18.3 0.7 %collective-permute-start.3 = (bf16[128,384]{1,0:T(8,128)(2,1)S(1)}, bf16[128,384]{1,0:T(8,128)(2,1)S(1)}, u32[]{:S(2)}, u32[]{:S(2)}) collective-permute-start(bf16[128,384]{1,0:T(8,128)(2,1)S(1)} %collective-permute-done.1.refs_1_), channel_id=1, source_target_pairs={{0,1},{1,0},{2,3},{3,2},{4,5},{5,4},{6,7},{7,6},{8,9},{9,8},{10,11... | collective-permute-start | bytes 294920 | tf_op jit(solution)/shard_map/ppermute | solution.py:335
  19.0 1.6 %collective-permute-done.6.refs_3_ = bf16[128,384]{1,0:T(8,128)(2,1)S(1)} collective-permute-done((bf16[128,384]{1,0:T(8,128)(2,1)S(1)}, bf16[128,384]{1,0:T(8,128)(2,1)S(1)}, u32[]{:S(2)}, u32[]{:S(2)}) %collective-permute-start.6) | collective-permute-done | bytes 98336 | tf_op jit(solution)/shard_map/ppermute | solution.py:335
  21.2 0.8 %collective-permute-done.2.refs_2_ = bf16[128,384]{1,0:T(8,128)(2,1)S(1)} collective-permute-done((bf16[128,384]{1,0:T(8,128)(2,1)S(1)}, bf16[128,384]{1,0:T(8,128)(2,1)S(1)}, u32[]{:S(2)}, u32[]{:S(2)}) %collective-permute-start.2) | collective-permute-done | bytes 98336 | tf_op jit(solution)/shard_map/ppermute | solution.py:335
  22.0 1.0 %collective-permute-done.3.refs_3_ = bf16[128,384]{1,0:T(8,128)(2,1)S(1)} collective-permute-done((bf16[128,384]{1,0:T(8,128)(2,1)S(1)}, bf16[128,384]{1,0:T(8,128)(2,1)S(1)}, u32[]{:S(2)}, u32[]{:S(2)}) %collective-permute-start.3) | collective-permute-done | bytes 98336 | tf_op jit(solution)/shard_map/ppermute | solution.py:335
  23.6 0.6 %collective-permute-start.18 = (f32[256,384]{1,0:T(8,128)S(1)}, f32[256,384]{1,0:T(8,128)S(1)}, u32[]{:S(2)}, u32[]{:S(2)}) collective-permute-start(f32[256,384]{1,0:T(8,128)S(1)} %get-tuple-element.31.refs_4_.refs_0_), channel_id=1, source_target_pairs={{0,4},{1,5},{2,6},{3,7},{4,0},{5,1},{6,2},{7,3},{8,12},{9,13},{10,... | collective-permute-start | bytes 1179656 | tf_op jit(solution)/shard_map/ppermute | solution.py:335
  24.3 0.6 %collective-permute-done.9.refs_1_ = bf16[512,384]{1,0:T(8,128)(2,1)S(1)} collective-permute-done((bf16[512,384]{1,0:T(8,128)(2,1)S(1)}, bf16[512,384]{1,0:T(8,128)(2,1)S(1)}, u32[]{:S(2)}, u32[]{:S(2)}) %collective-permute-start.9) | collective-permute-done | bytes 393248 | tf_op jit(solution)/shard_map/ppermute | solution.py:335
  24.9 0.7 %shard_map.72 = (f32[320,128]{1,0:T(8,128)S(1)}, f32[320,128]{1,0:T(8,128)S(1)}) custom-call(bf16[512,384]{1,0:T(8,128)(2,1)S(1)} %get-tuple-element.27.refs_0_, bf16[512,384]{1,0:T(8,128)(2,1)S(1)} %collective-permute-done.9.refs_1_, bf16[32,384]{1,0:T(8,128)(2,1)S(1)} %get-tuple-element.28.refs_2_, bf16[32,384]{1,0:T(8,128)(2,1)S(1)} %slice.9.refs_3_, ...), custom_call_target="tpu_custom_call" | custom-call | tf_op jit(solution)/shard_map/pallas_call | solution.py:28
  26.4 0.6 %collective-permute-done.10.refs_2_ = f32[320,128]{1,0:T(8,128)S(1)} collective-permute-done((f32[320,128]{1,0:T(8,128)S(1)}, f32[320,128]{1,0:T(8,128)S(1)}, u32[]{:S(2)}, u32[]{:S(2)}) %collective-permute-start.10) | collective-permute-done | bytes 163872 | tf_op jit(solution)/shard_map/ppermute | solution.py:335
  27.1 2.5 %collective-permute-start.13 = (f32[160,128]{1,0:T(8,128)S(1)}, f32[160,128]{1,0:T(8,128)S(1)}, u32[]{:S(2)}, u32[]{:S(2)}) collective-permute-start(f32[160,128]{1,0:T(8,128)S(1)} %get-tuple-element.36), channel_id=1, source_target_pairs={{0,17},{1,16},{2,19},{3,18},{4,21},{5,20},{6,23},{7,22},{8,25},{9,... | collective-permute-start | bytes 245768 | tf_op jit(solution)/shard_map/ppermute | solution.py:335
  29.5 0.5 collective-permute-start.11
  30.0 0.6 %collective-permute-start.12 = (f32[160,128]{1,0:T(8,128)S(1)}, f32[160,128]{1,0:T(8,128)S(1)}, u32[]{:S(2)}, u32[]{:S(2)}) collective-permute-start(f32[160,128]{1,0:T(8,128)S(1)} %get-tuple-element.35.refs_0_.refs_4_), channel_id=1, source_target_pairs={{0,1},{1,0},{2,3},{3,2},{4,5},{5,4},{6,7},{7,6},{8,9},{9,8},{10,11... | collective-permute-start | bytes 245768 | tf_op jit(solution)/shard_map/ppermute | solution.py:335
  30.6 2.0 %collective-permute-done.13.refs_3_ = f32[160,128]{1,0:T(8,128)S(1)} collective-permute-done((f32[160,128]{1,0:T(8,128)S(1)}, f32[160,128]{1,0:T(8,128)S(1)}, u32[]{:S(2)}, u32[]{:S(2)}) %collective-permute-start.13) | collective-permute-done | bytes 81952 | tf_op jit(solution)/shard_map/ppermute | solution.py:335
  32.6 1.7 %collective-permute-done.11.refs_1_ = f32[160,128]{1,0:T(8,128)S(1)} collective-permute-done((f32[160,128]{1,0:T(8,128)S(1)}, f32[160,128]{1,0:T(8,128)S(1)}, u32[]{:S(2)}, u32[]{:S(2)}) %collective-permute-start.11) | collective-permute-done | bytes 81952 | tf_op jit(solution)/shard_map/ppermute | solution.py:335
  34.5 3.1 %collective-permute-start.14 = (f32[160,128]{1,0:T(8,128)S(1)}, f32[160,128]{1,0:T(8,128)S(1)}, u32[]{:S(2)}, u32[]{:S(2)}) collective-permute-start(f32[160,128]{1,0:T(8,128)S(1)} %shard_map.74.refs_0_), channel_id=1, source_target_pairs={{0,2},{1,3},{2,0},{3,1},{4,6},{5,7},{6,4},{7,5},{8,10},{9,11},{10,... | collective-permute-start | bytes 245768 | tf_op jit(solution)/shard_map/ppermute | solution.py:335
  37.8 0.7 %collective-permute-start.20 = (bf16[128,384]{1,0:T(8,128)(2,1)S(1)}, bf16[128,384]{1,0:T(8,128)(2,1)S(1)}, u32[]{:S(2)}, u32[]{:S(2)}) collective-permute-start(bf16[128,384]{1,0:T(8,128)(2,1)S(1)} %get-tuple-element.38), channel_id=1, source_target_pairs={{0,0},{1,4},{2,8},{3,12},{4,1},{5,5},{6,9},{7,13},{8,2},{9,6},{10,... | collective-permute-start | bytes 294920 | tf_op jit(solution)/shard_map/ppermute | solution.py:390
  38.5 4.5 %collective-permute-start.21 = (bf16[128,384]{1,0:T(8,128)(2,1)S(1)}, bf16[128,384]{1,0:T(8,128)(2,1)S(1)}, u32[]{:S(2)}, u32[]{:S(2)}) collective-permute-start(bf16[128,384]{1,0:T(8,128)(2,1)S(1)} %get-tuple-element.39), channel_id=1, source_target_pairs={{0,2},{1,6},{2,10},{3,14},{4,3},{5,7},{6,11},{7,15},{8,0},{9,4},{1... | collective-permute-start | bytes 294920 | tf_op jit(solution)/shard_map/ppermute | solution.py:390
  43.0 1.6 %collective-permute-start.16 = (f32[160,128]{1,0:T(8,128)S(1)}, f32[160,128]{1,0:T(8,128)S(1)}, u32[]{:S(2)}, u32[]{:S(2)}) collective-permute-start(f32[160,128]{1,0:T(8,128)S(1)} %shard_map.75.refs_0_), channel_id=1, source_target_pairs={{0,16},{1,17},{2,18},{3,19},{4,20},{5,21},{6,22},{7,23},{8,24},{9,... | collective-permute-start | bytes 245768 | tf_op jit(solution)/shard_map/ppermute | solution.py:335
  44.6 1.9 %collective-permute-start.15 = (f32[160,128]{1,0:T(8,128)S(1)}, f32[160,128]{1,0:T(8,128)S(1)}, u32[]{:S(2)}, u32[]{:S(2)}) collective-permute-start(f32[160,128]{1,0:T(8,128)S(1)} %shard_map.75.refs_0_), channel_id=1, source_target_pairs={{0,8},{1,9},{2,10},{3,11},{4,12},{5,13},{6,14},{7,15},{8,0},{9,1},... | collective-permute-start | bytes 245768 | tf_op jit(solution)/shard_map/ppermute | solution.py:335
  46.8 2.7 %collective-permute-done.17.refs_3_ = f32[160,128]{1,0:T(8,128)S(1)} collective-permute-done((f32[160,128]{1,0:T(8,128)S(1)}, f32[160,128]{1,0:T(8,128)S(1)}, u32[]{:S(2)}, u32[]{:S(2)}) %collective-permute-start.17) | collective-permute-done | bytes 81952 | tf_op jit(solution)/shard_map/ppermute | solution.py:335
  49.5 0.6 %collective-permute-done.15.refs_1_ = f32[160,128]{1,0:T(8,128)S(1)} collective-permute-done((f32[160,128]{1,0:T(8,128)S(1)}, f32[160,128]{1,0:T(8,128)S(1)}, u32[]{:S(2)}, u32[]{:S(2)}) %collective-permute-start.15) | collective-permute-done | bytes 81952 | tf_op jit(solution)/shard_map/ppermute | solution.py:335
  50.2 1.0 %shard_map.79 = (bf16[1,128,2,384]{3,2,1,0:T(2,128)(2,1)}, f32[2,384,384]{2,1,0:T(8,128)}) custom-call(f32[4,160,128]{2,1,0:T(8,128)S(1)} %shard_map.78.refs_0_, bf16[1,128,2,384]{3,2,1,0:T(2,128)(2,1)S(1)} %shard_map.77.refs_4_.refs_1_), custom_call_target="tpu_custom_call" | custom-call | tf_op jit(solution)/shard_map/pallas_call | solution.py:28
  51.3 0.6 %collective-permute-done.22.refs_1_ = f32[4,160,128]{2,1,0:T(8,128)S(1)} collective-permute-done((f32[4,160,128]{2,1,0:T(8,128)S(1)}, f32[4,160,128]{2,1,0:T(8,128)S(1)}, u32[]{:S(2)}, u32[]{:S(2)}) %collective-permute-start.22) | collective-permute-done | bytes 327712 | tf_op jit(solution)/shard_map/ppermute | solution.py:335
  51.9 1.2 %shard_map.80 = f32[2,384,384]{2,1,0:T(8,128)} custom-call(f32[4,160,128]{2,1,0:T(8,128)S(1)} %shard_map.78.refs_0_, f32[4,160,128]{2,1,0:T(8,128)S(1)} %collective-permute-done.22.refs_1_, f32[2,384,384]{2,1,0:T(8,128)} %get-tuple-element.41.refs_2_), custom_call_target="tpu_custom_call", output_to_operand_aliasing={{}: (2, {})} | custom-call | tf_op jit(solution)/shard_map/pallas_call | solution.py:28
  (29 shorter events, 2.6 us)
Async XLA Ops:
  2.3 9.2 %collective-permute-start = (bf16[160,384]{1,0:T(8,128)(2,1)S(1)}, bf16[160,384]{1,0:T(8,128)(2,1)S(1)}, u32[]{:S(2)}, u32[]{:S(2)}) collective-permute-start(bf16[160,384]{1,0:T(8,128)(2,1)S(1)} %get-tuple-element.22), channel_id=1, source_target_pairs={{0,8},{1,9},{2,10},{3,11},{4,12},{5,13},{6,14},{7,15},{8,0},{9,1},... | collective-permute-start | bytes 368648 | tf_op jit(solution)/shard_map/ppermute | solution.py:335
  5.3 16.6 %collective-permute-start.7 = (bf16[256,512]{1,0:T(8,128)(2,1)S(1)}, bf16[256,512]{1,0:T(8,128)(2,1)S(1)}, u32[]{:S(2)}, u32[]{:S(2)}) collective-permute-start(bf16[256,512]{1,0:T(8,128)(2,1)S(1)} %get-tuple-element.24.refs_4_), channel_id=1, source_target_pairs={{0,8},{1,9},{2,10},{3,11},{4,12},{5,13},{6,14},{7,15},{8,0},{9,1},... | collective-permute-start | bytes 786440 | tf_op jit(solution)/shard_map/ppermute | solution.py:335
  5.4 16.5 %collective-permute-start.8 = (bf16[256,512]{1,0:T(8,128)(2,1)S(1)}, bf16[256,512]{1,0:T(8,128)(2,1)S(1)}, u32[]{:S(2)}, u32[]{:S(2)}) collective-permute-start(bf16[256,512]{1,0:T(8,128)(2,1)S(1)} %get-tuple-element.25.refs_5_), channel_id=1, source_target_pairs={{0,8},{1,9},{2,10},{3,11},{4,12},{5,13},{6,14},{7,15},{8,0},{9,1},... | collective-permute-start | bytes 786440 | tf_op jit(solution)/shard_map/ppermute | solution.py:335
  7.4 5.8 %collective-permute-start.4 = (bf16[128,384]{1,0:T(8,128)(2,1)S(1)}, bf16[128,384]{1,0:T(8,128)(2,1)S(1)}, u32[]{:S(2)}, u32[]{:S(2)}) collective-permute-start(bf16[128,384]{1,0:T(8,128)(2,1)S(1)} %get-tuple-element.23.refs_0_), channel_id=1, source_target_pairs={{0,2},{1,3},{2,0},{3,1},{4,6},{5,7},{6,4},{7,5},{8,10},{9,11},{10,... | collective-permute-start | bytes 294920 | tf_op jit(solution)/shard_map/ppermute | solution.py:335
  10.0 7.0 %collective-permute-start.5 = (bf16[128,384]{1,0:T(8,128)(2,1)S(1)}, bf16[128,384]{1,0:T(8,128)(2,1)S(1)}, u32[]{:S(2)}, u32[]{:S(2)}) collective-permute-start(bf16[128,384]{1,0:T(8,128)(2,1)S(1)} %get-tuple-element.23.refs_0_), channel_id=1, source_target_pairs={{0,1},{1,0},{2,3},{3,2},{4,5},{5,4},{6,7},{7,6},{8,9},{9,8},{10,11... | collective-permute-start | bytes 294920 | tf_op jit(solution)/shard_map/ppermute | solution.py:335
  11.6 6.8 %collective-permute-start.1 = (bf16[128,384]{1,0:T(8,128)(2,1)S(1)}, bf16[128,384]{1,0:T(8,128)(2,1)S(1)}, u32[]{:S(2)}, u32[]{:S(2)}) collective-permute-start(bf16[128,384]{1,0:T(8,128)(2,1)S(1)} %slice.8.refs_0_), channel_id=1, source_target_pairs={{0,2},{1,3},{2,0},{3,1},{4,6},{5,7},{6,4},{7,5},{8,10},{9,11},{10,... | collective-permute-start | bytes 294920 | tf_op jit(solution)/shard_map/ppermute | solution.py:335
  13.1 7.6 %collective-permute-start.6 = (bf16[128,384]{1,0:T(8,128)(2,1)S(1)}, bf16[128,384]{1,0:T(8,128)(2,1)S(1)}, u32[]{:S(2)}, u32[]{:S(2)}) collective-permute-start(bf16[128,384]{1,0:T(8,128)(2,1)S(1)} %collective-permute-done.4.refs_1_), channel_id=1, source_target_pairs={{0,1},{1,0},{2,3},{3,2},{4,5},{5,4},{6,7},{7,6},{8,9},{9,8},{10,11... | collective-permute-start | bytes 294920 | tf_op jit(solution)/shard_map/ppermute | solution.py:335
  17.0 5.0 %collective-permute-start.2 = (bf16[128,384]{1,0:T(8,128)(2,1)S(1)}, bf16[128,384]{1,0:T(8,128)(2,1)S(1)}, u32[]{:S(2)}, u32[]{:S(2)}) collective-permute-start(bf16[128,384]{1,0:T(8,128)(2,1)S(1)} %slice.8.refs_0_), channel_id=1, source_target_pairs={{0,1},{1,0},{2,3},{3,2},{4,5},{5,4},{6,7},{7,6},{8,9},{9,8},{10,11... | collective-permute-start | bytes 294920 | tf_op jit(solution)/shard_map/ppermute | solution.py:335
  18.3 4.7 %collective-permute-start.3 = (bf16[128,384]{1,0:T(8,128)(2,1)S(1)}, bf16[128,384]{1,0:T(8,128)(2,1)S(1)}, u32[]{:S(2)}, u32[]{:S(2)}) collective-permute-start(bf16[128,384]{1,0:T(8,128)(2,1)S(1)} %collective-permute-done.1.refs_1_), channel_id=1, source_target_pairs={{0,1},{1,0},{2,3},{3,2},{4,5},{5,4},{6,7},{7,6},{8,9},{9,8},{10,11... | collective-permute-start | bytes 294920 | tf_op jit(solution)/shard_map/ppermute | solution.py:335
  23.1 1.8 %collective-permute-start.9 = (bf16[512,384]{1,0:T(8,128)(2,1)S(1)}, bf16[512,384]{1,0:T(8,128)(2,1)S(1)}, u32[]{:S(2)}, u32[]{:S(2)}) collective-permute-start(bf16[512,384]{1,0:T(8,128)(2,1)S(1)} %get-tuple-element.27.refs_0_), channel_id=1, source_target_pairs={{0,4},{1,5},{2,6},{3,7},{4,0},{5,1},{6,2},{7,3},{8,12},{9,13},{10,... | collective-permute-start | bytes 1179656 | tf_op jit(solution)/shard_map/ppermute | solution.py:335
  23.6 14.0 %collective-permute-start.18 = (f32[256,384]{1,0:T(8,128)S(1)}, f32[256,384]{1,0:T(8,128)S(1)}, u32[]{:S(2)}, u32[]{:S(2)}) collective-permute-start(f32[256,384]{1,0:T(8,128)S(1)} %get-tuple-element.31.refs_4_.refs_0_), channel_id=1, source_target_pairs={{0,4},{1,5},{2,6},{3,7},{4,0},{5,1},{6,2},{7,3},{8,12},{9,13},{10,... | collective-permute-start | bytes 1179656 | tf_op jit(solution)/shard_map/ppermute | solution.py:335
  24.2 13.5 %collective-permute-start.19 = (f32[256,384]{1,0:T(8,128)S(1)}, f32[256,384]{1,0:T(8,128)S(1)}, u32[]{:S(2)}, u32[]{:S(2)}) collective-permute-start(f32[256,384]{1,0:T(8,128)S(1)} %get-tuple-element.32.refs_5_.refs_1_), channel_id=1, source_target_pairs={{0,4},{1,5},{2,6},{3,7},{4,0},{5,1},{6,2},{7,3},{8,12},{9,13},{10,... | collective-permute-start | bytes 1179656 | tf_op jit(solution)/shard_map/ppermute | solution.py:335
  25.6 1.4 %collective-permute-start.10 = (f32[320,128]{1,0:T(8,128)S(1)}, f32[320,128]{1,0:T(8,128)S(1)}, u32[]{:S(2)}, u32[]{:S(2)}) collective-permute-start(f32[320,128]{1,0:T(8,128)S(1)} %get-tuple-element.34), channel_id=1, source_target_pairs={{0,4},{1,5},{2,6},{3,7},{4,0},{5,1},{6,2},{7,3},{8,12},{9,13},{10,... | collective-permute-start | bytes 491528 | tf_op jit(solution)/shard_map/ppermute | solution.py:335
  27.1 5.5 %collective-permute-start.13 = (f32[160,128]{1,0:T(8,128)S(1)}, f32[160,128]{1,0:T(8,128)S(1)}, u32[]{:S(2)}, u32[]{:S(2)}) collective-permute-start(f32[160,128]{1,0:T(8,128)S(1)} %get-tuple-element.36), channel_id=1, source_target_pairs={{0,17},{1,16},{2,19},{3,18},{4,21},{5,20},{6,23},{7,22},{8,25},{9,... | collective-permute-start | bytes 245768 | tf_op jit(solution)/shard_map/ppermute | solution.py:335
  29.5 4.8 %collective-permute-start.11 = (f32[160,128]{1,0:T(8,128)S(1)}, f32[160,128]{1,0:T(8,128)S(1)}, u32[]{:S(2)}, u32[]{:S(2)}) collective-permute-start(f32[160,128]{1,0:T(8,128)S(1)} %get-tuple-element.36), channel_id=1, source_target_pairs={{0,16},{1,17},{2,18},{3,19},{4,20},{5,21},{6,22},{7,23},{8,24},{9,... | collective-permute-start | bytes 245768 | tf_op jit(solution)/shard_map/ppermute | solution.py:335
  30.0 4.4 %collective-permute-start.12 = (f32[160,128]{1,0:T(8,128)S(1)}, f32[160,128]{1,0:T(8,128)S(1)}, u32[]{:S(2)}, u32[]{:S(2)}) collective-permute-start(f32[160,128]{1,0:T(8,128)S(1)} %get-tuple-element.35.refs_0_.refs_4_), channel_id=1, source_target_pairs={{0,1},{1,0},{2,3},{3,2},{4,5},{5,4},{6,7},{7,6},{8,9},{9,8},{10,11... | collective-permute-start | bytes 245768 | tf_op jit(solution)/shard_map/ppermute | solution.py:335
  34.5 8.4 %collective-permute-start.14 = (f32[160,128]{1,0:T(8,128)S(1)}, f32[160,128]{1,0:T(8,128)S(1)}, u32[]{:S(2)}, u32[]{:S(2)}) collective-permute-start(f32[160,128]{1,0:T(8,128)S(1)} %shard_map.74.refs_0_), channel_id=1, source_target_pairs={{0,2},{1,3},{2,0},{3,1},{4,6},{5,7},{6,4},{7,5},{8,10},{9,11},{10,... | collective-permute-start | bytes 245768 | tf_op jit(solution)/shard_map/ppermute | solution.py:335
  37.8 8.7 %collective-permute-start.20 = (bf16[128,384]{1,0:T(8,128)(2,1)S(1)}, bf16[128,384]{1,0:T(8,128)(2,1)S(1)}, u32[]{:S(2)}, u32[]{:S(2)}) collective-permute-start(bf16[128,384]{1,0:T(8,128)(2,1)S(1)} %get-tuple-element.38), channel_id=1, source_target_pairs={{0,0},{1,4},{2,8},{3,12},{4,1},{5,5},{6,9},{7,13},{8,2},{9,6},{10,... | collective-permute-start | bytes 294920 | tf_op jit(solution)/shard_map/ppermute | solution.py:390
  38.5 8.0 %collective-permute-start.21 = (bf16[128,384]{1,0:T(8,128)(2,1)S(1)}, bf16[128,384]{1,0:T(8,128)(2,1)S(1)}, u32[]{:S(2)}, u32[]{:S(2)}) collective-permute-start(bf16[128,384]{1,0:T(8,128)(2,1)S(1)} %get-tuple-element.39), channel_id=1, source_target_pairs={{0,2},{1,6},{2,10},{3,14},{4,3},{5,7},{6,11},{7,15},{8,0},{9,4},{1... | collective-permute-start | bytes 294920 | tf_op jit(solution)/shard_map/ppermute | solution.py:390
  43.0 6.6 %collective-permute-start.17 = (f32[160,128]{1,0:T(8,128)S(1)}, f32[160,128]{1,0:T(8,128)S(1)}, u32[]{:S(2)}, u32[]{:S(2)}) collective-permute-start(f32[160,128]{1,0:T(8,128)S(1)} %shard_map.75.refs_0_), channel_id=1, source_target_pairs={{0,24},{1,25},{2,26},{3,27},{4,28},{5,29},{6,30},{7,31},{8,16},{9,... | collective-permute-start | bytes 245768 | tf_op jit(solution)/shard_map/ppermute | solution.py:335
  43.0 6.5 %collective-permute-start.16 = (f32[160,128]{1,0:T(8,128)S(1)}, f32[160,128]{1,0:T(8,128)S(1)}, u32[]{:S(2)}, u32[]{:S(2)}) collective-permute-start(f32[160,128]{1,0:T(8,128)S(1)} %shard_map.75.refs_0_), channel_id=1, source_target_pairs={{0,16},{1,17},{2,18},{3,19},{4,20},{5,21},{6,22},{7,23},{8,24},{9,... | collective-permute-start | bytes 245768 | tf_op jit(solution)/shard_map/ppermute | solution.py:335
  44.6 5.5 %collective-permute-start.15 = (f32[160,128]{1,0:T(8,128)S(1)}, f32[160,128]{1,0:T(8,128)S(1)}, u32[]{:S(2)}, u32[]{:S(2)}) collective-permute-start(f32[160,128]{1,0:T(8,128)S(1)} %shard_map.75.refs_0_), channel_id=1, source_target_pairs={{0,8},{1,9},{2,10},{3,11},{4,12},{5,13},{6,14},{7,15},{8,0},{9,1},... | collective-permute-start | bytes 245768 | tf_op jit(solution)/shard_map/ppermute | solution.py:335
  50.2 1.7 %collective-permute-start.22 = (f32[4,160,128]{2,1,0:T(8,128)S(1)}, f32[4,160,128]{2,1,0:T(8,128)S(1)}, u32[]{:S(2)}, u32[]{:S(2)}) collective-permute-start(f32[4,160,128]{2,1,0:T(8,128)S(1)} %shard_map.78.refs_0_), channel_id=1, source_target_pairs={{0,4},{1,5},{2,6},{3,7},{4,0},{5,1},{6,2},{7,3},{8,12},{9,13},{10,... | collective-permute-start | bytes 983048 | tf_op jit(solution)/shard_map/ppermute | solution.py:335

commit v22 on v21

--- a/solution.py
+++ b/solution.py
@@ -143,7 +143,8 @@
 
 
 def own_kernel(*refs):
-    blocks, pieces, (rows, applied) = refs[:4], refs[4:-2], refs[-2:]
+    weight, blocks, pieces, (rows, applied, tile) = refs[0], refs[1:5], refs[5:-3], refs[-3:]
+    tile[...] = jnp.full(tile.shape, weight[0], tile.dtype)
     set_rows(blocks, rows)
     at = 0
     for piece in pieces:
@@ -192,7 +193,7 @@
 
 
 def halve_kernel(weight, mine, came, keep, send, whole):
-    whole[...] = weight[0] * (mine[...] + came[...])
+    whole[...] = weight[:1] * (mine[...] + came[...])
     size, point = keep.shape[0], lax.axis_index("hyp")
     keep[...] = whole[pl.ds(pl.multiple_of(point * size, 8), size), :]
     send[...] = whole[pl.ds(pl.multiple_of((1 - point) * size, 8), size), :]
@@ -359,8 +360,9 @@
 
 
     product, line_shape = shape((extent, width), f32), shape((extent, width), bf16)
-    own_rows, own_product = call(
-        own_kernel, [line_shape, product], [VMEM] * (4 + len(cuts)), *blocks[:4], *pieces
+    own_rows, own_product, weight = call(
+        own_kernel, [line_shape, product, shape((8, LANES), f32)], [SMEM] + [VMEM] * (4 + len(cuts)),
+        quad_weight, *blocks[:4], *pieces,
     )
     rows, pack = call(
         gather_kernel, [line_shape] * 2, [VMEM] * 5, *blocks[4:], own_rows, after=far
@@ -379,7 +381,7 @@
         scratch=[pltpu.VMEM((2 * lines, LANES), f32)],
     )
     keep, send = call(
-        halve_kernel, [part, part], [SMEM] + [VMEM] * 2, quad_weight, keep, swap(send, core=1),
+        halve_kernel, [part, part], [VMEM] * 3, weight, keep, swap(send, core=1),
         scratch=[pltpu.VMEM((lines, LANES), f32)],
     )
     def deliver(x, flip):

time: 53.2 us -> 53.2 us (level)
  no operation moved by 1% of the time
where the time goes in v22:
time: 53.2 us; the launch traced here: 53 us
  starting transfers between devices  31.9 us (60%)
  waiting for transfers between devices  13.6 us (26%)
  Pallas kernels  6.13 us (12%)
  between operations  1.4 us (3%)
    ppermute x21, starting transfers between devices, swap(): return lax.ppermute(x, AXES, [(i, i ^ mask) for i in range(devices)])  26.8 us
    ppermute x21, waiting for transfers between devices, swap(): return lax.ppermute(x, AXES, [(i, i ^ mask) for i in range(devices)])  13.5 us
    pallas_call x13, Pallas kernels, call(): pl.pallas_call(body, out_shape=outs, in_specs=list(specs) + [ANY] * len(a...  6.13 us
    ppermute x2, starting transfers between devices, deliver(): return lax.ppermute(x, AXES, pairs)  5.13 us
  transfers between devices with their start and end apart: 23, of which 13 were waited for; matrix products, arithmetic and copies ran while one was open for 0% of the time, Pallas kernels for 6%

profile of v22, /device:TPU:0, one launch (start us, length us, event | category | flops | bytes accessed | tf_op | source)
XLA Modules:
  0.0 53.0 jit_solution(6676352441108594461)
XLA Ops:
  0.6 1.7 %shard_map.68 = (bf16[128,384]{1,0:T(8,128)(2,1)S(1)}, bf16[160,384]{1,0:T(8,128)(2,1)S(1)}, bf16[32,384]{1,0:T(8,128)(2,1)S(1)}, s32[2,8,128]{2,1,0:T(8,128)S(1...) custom-call(s32[2]{0:T(128)} %bitcast.1, bf16[1,128,2,384]{3,2,1,0:T(2,128)(2,1)} %refs_1_.1, ...), custom_call_target="tpu_custom_call" | custom-call | tf_op jit(solution)/shard_map/pallas_call | solution.py:28
  2.3 3.0 %collective-permute-start.3 = (bf16[160,384]{1,0:T(8,128)(2,1)S(1)}, bf16[160,384]{1,0:T(8,128)(2,1)S(1)}, u32[]{:S(2)}, u32[]{:S(2)}) collective-permute-start(bf16[160,384]{1,0:T(8,128)(2,1)S(1)} %get-tuple-element.27), channel_id=1, source_target_pairs={{0,8},{1,9},{2,10},{3,11},{4,12},{5,13},{6,14},{7,15},{8,0},{9,1},... | collective-permute-start | bytes 368648 | tf_op jit(solution)/shard_map/ppermute | solution.py:336
  5.4 1.9 %collective-permute-start.8 = (bf16[256,512]{1,0:T(8,128)(2,1)S(1)}, bf16[256,512]{1,0:T(8,128)(2,1)S(1)}, u32[]{:S(2)}, u32[]{:S(2)}) collective-permute-start(bf16[256,512]{1,0:T(8,128)(2,1)S(1)} %get-tuple-element.25.refs_6_), channel_id=1, source_target_pairs={{0,8},{1,9},{2,10},{3,11},{4,12},{5,13},{6,14},{7,15},{8,0},{9,1},... | collective-permute-start | bytes 786440 | tf_op jit(solution)/shard_map/ppermute | solution.py:336
  7.4 2.6 %collective-permute-start = (bf16[128,384]{1,0:T(8,128)(2,1)S(1)}, bf16[128,384]{1,0:T(8,128)(2,1)S(1)}, u32[]{:S(2)}, u32[]{:S(2)}) collective-permute-start(bf16[128,384]{1,0:T(8,128)(2,1)S(1)} %get-tuple-element.23.refs_1_), channel_id=1, source_target_pairs={{0,2},{1,3},{2,0},{3,1},{4,6},{5,7},{6,4},{7,5},{8,10},{9,11},{10,... | collective-permute-start | bytes 294920 | tf_op jit(solution)/shard_map/ppermute | solution.py:336
  10.0 1.6 %collective-permute-start.1 = (bf16[128,384]{1,0:T(8,128)(2,1)S(1)}, bf16[128,384]{1,0:T(8,128)(2,1)S(1)}, u32[]{:S(2)}, u32[]{:S(2)}) collective-permute-start(bf16[128,384]{1,0:T(8,128)(2,1)S(1)} %get-tuple-element.23.refs_1_), channel_id=1, source_target_pairs={{0,1},{1,0},{2,3},{3,2},{4,5},{5,4},{6,7},{7,6},{8,9},{9,8},{10,11... | collective-permute-start | bytes 294920 | tf_op jit(solution)/shard_map/ppermute | solution.py:336
  11.6 1.2 %collective-permute-start.4 = (bf16[128,384]{1,0:T(8,128)(2,1)S(1)}, bf16[128,384]{1,0:T(8,128)(2,1)S(1)}, u32[]{:S(2)}, u32[]{:S(2)}) collective-permute-start(bf16[128,384]{1,0:T(8,128)(2,1)S(1)} %slice.8.refs_0_), channel_id=1, source_target_pairs={{0,2},{1,3},{2,0},{3,1},{4,6},{5,7},{6,4},{7,5},{8,10},{9,11},{10,... | collective-permute-start | bytes 294920 | tf_op jit(solution)/shard_map/ppermute | solution.py:336
  13.1 3.8 %collective-permute-start.2 = (bf16[128,384]{1,0:T(8,128)(2,1)S(1)}, bf16[128,384]{1,0:T(8,128)(2,1)S(1)}, u32[]{:S(2)}, u32[]{:S(2)}) collective-permute-start(bf16[128,384]{1,0:T(8,128)(2,1)S(1)} %collective-permute-done.refs_2_), channel_id=1, source_target_pairs={{0,1},{1,0},{2,3},{3,2},{4,5},{5,4},{6,7},{7,6},{8,9},{9,8},{10,11... | collective-permute-start | bytes 294920 | tf_op jit(solution)/shard_map/ppermute | solution.py:336
  17.0 0.7 %collective-permute-start.5 = (bf16[128,384]{1,0:T(8,128)(2,1)S(1)}, bf16[128,384]{1,0:T(8,128)(2,1)S(1)}, u32[]{:S(2)}, u32[]{:S(2)}) collective-permute-start(bf16[128,384]{1,0:T(8,128)(2,1)S(1)} %slice.8.refs_0_), channel_id=1, source_target_pairs={{0,1},{1,0},{2,3},{3,2},{4,5},{5,4},{6,7},{7,6},{8,9},{9,8},{10,11... | collective-permute-start | bytes 294920 | tf_op jit(solution)/shard_map/ppermute | solution.py:336
  17.7 0.6 %collective-permute-done.4.refs_1_ = bf16[128,384]{1,0:T(8,128)(2,1)S(1)} collective-permute-done((bf16[128,384]{1,0:T(8,128)(2,1)S(1)}, bf16[128,384]{1,0:T(8,128)(2,1)S(1)}, u32[]{:S(2)}, u32[]{:S(2)}) %collective-permute-start.4) | collective-permute-done | bytes 98336 | tf_op jit(solution)/shard_map/ppermute | solution.py:336
  18.3 0.7 %collective-permute-start.6 = (bf16[128,384]{1,0:T(8,128)(2,1)S(1)}, bf16[128,384]{1,0:T(8,128)(2,1)S(1)}, u32[]{:S(2)}, u32[]{:S(2)}) collective-permute-start(bf16[128,384]{1,0:T(8,128)(2,1)S(1)} %collective-permute-done.4.refs_1_), channel_id=1, source_target_pairs={{0,1},{1,0},{2,3},{3,2},{4,5},{5,4},{6,7},{7,6},{8,9},{9,8},{10,11... | collective-permute-start | bytes 294920 | tf_op jit(solution)/shard_map/ppermute | solution.py:336
  19.7 1.0 %collective-permute-done.2.refs_4_ = bf16[128,384]{1,0:T(8,128)(2,1)S(1)} collective-permute-done((bf16[128,384]{1,0:T(8,128)(2,1)S(1)}, bf16[128,384]{1,0:T(8,128)(2,1)S(1)}, u32[]{:S(2)}, u32[]{:S(2)}) %collective-permute-start.2) | collective-permute-done | bytes 98336 | tf_op jit(solution)/shard_map/ppermute | solution.py:336
  21.2 0.8 %collective-permute-done.5.refs_2_ = bf16[128,384]{1,0:T(8,128)(2,1)S(1)} collective-permute-done((bf16[128,384]{1,0:T(8,128)(2,1)S(1)}, bf16[128,384]{1,0:T(8,128)(2,1)S(1)}, u32[]{:S(2)}, u32[]{:S(2)}) %collective-permute-start.5) | collective-permute-done | bytes 98336 | tf_op jit(solution)/shard_map/ppermute | solution.py:336
  22.0 1.0 %collective-permute-done.6.refs_3_ = bf16[128,384]{1,0:T(8,128)(2,1)S(1)} collective-permute-done((bf16[128,384]{1,0:T(8,128)(2,1)S(1)}, bf16[128,384]{1,0:T(8,128)(2,1)S(1)}, u32[]{:S(2)}, u32[]{:S(2)}) %collective-permute-start.6) | collective-permute-done | bytes 98336 | tf_op jit(solution)/shard_map/ppermute | solution.py:336
  23.6 0.6 %collective-permute-start.18 = (f32[256,384]{1,0:T(8,128)S(1)}, f32[256,384]{1,0:T(8,128)S(1)}, u32[]{:S(2)}, u32[]{:S(2)}) collective-permute-start(f32[256,384]{1,0:T(8,128)S(1)} %get-tuple-element.33.refs_4_.refs_0_), channel_id=1, source_target_pairs={{0,4},{1,5},{2,6},{3,7},{4,0},{5,1},{6,2},{7,3},{8,12},{9,13},{10,... | collective-permute-start | bytes 1179656 | tf_op jit(solution)/shard_map/ppermute | solution.py:336
  24.3 0.6 %collective-permute-done.9.refs_1_ = bf16[512,384]{1,0:T(8,128)(2,1)S(1)} collective-permute-done((bf16[512,384]{1,0:T(8,128)(2,1)S(1)}, bf16[512,384]{1,0:T(8,128)(2,1)S(1)}, u32[]{:S(2)}, u32[]{:S(2)}) %collective-permute-start.9) | collective-permute-done | bytes 393248 | tf_op jit(solution)/shard_map/ppermute | solution.py:336
  24.9 0.7 %shard_map.72 = (f32[320,128]{1,0:T(8,128)S(1)}, f32[320,128]{1,0:T(8,128)S(1)}) custom-call(bf16[512,384]{1,0:T(8,128)(2,1)S(1)} %get-tuple-element.29.refs_0_, bf16[512,384]{1,0:T(8,128)(2,1)S(1)} %collective-permute-done.9.refs_1_, bf16[32,384]{1,0:T(8,128)(2,1)S(1)} %get-tuple-element.30.refs_2_, bf16[32,384]{1,0:T(8,128)(2,1)S(1)} %slice.9.refs_3_, ...), custom_call_target="tpu_custom_call" | custom-call | tf_op jit(solution)/shard_map/pallas_call | solution.py:28
  25.8 1.3 %collective-permute-done.10.refs_2_ = f32[320,128]{1,0:T(8,128)S(1)} collective-permute-done((f32[320,128]{1,0:T(8,128)S(1)}, f32[320,128]{1,0:T(8,128)S(1)}, u32[]{:S(2)}, u32[]{:S(2)}) %collective-permute-start.10) | collective-permute-done | bytes 163872 | tf_op jit(solution)/shard_map/ppermute | solution.py:336
  27.1 2.4 %collective-permute-start.13 = (f32[160,128]{1,0:T(8,128)S(1)}, f32[160,128]{1,0:T(8,128)S(1)}, u32[]{:S(2)}, u32[]{:S(2)}) collective-permute-start(f32[160,128]{1,0:T(8,128)S(1)} %get-tuple-element.38), channel_id=1, source_target_pairs={{0,17},{1,16},{2,19},{3,18},{4,21},{5,20},{6,23},{7,22},{8,25},{9,... | collective-permute-start | bytes 245768 | tf_op jit(solution)/shard_map/ppermute | solution.py:336
  29.5 0.5 collective-permute-start.11
  30.1 0.6 %collective-permute-start.12 = (f32[160,128]{1,0:T(8,128)S(1)}, f32[160,128]{1,0:T(8,128)S(1)}, u32[]{:S(2)}, u32[]{:S(2)}) collective-permute-start(f32[160,128]{1,0:T(8,128)S(1)} %get-tuple-element.37.refs_0_.refs_4_), channel_id=1, source_target_pairs={{0,1},{1,0},{2,3},{3,2},{4,5},{5,4},{6,7},{7,6},{8,9},{9,8},{10,11... | collective-permute-start | bytes 245768 | tf_op jit(solution)/shard_map/ppermute | solution.py:336
  30.6 2.0 %collective-permute-done.13.refs_3_ = f32[160,128]{1,0:T(8,128)S(1)} collective-permute-done((f32[160,128]{1,0:T(8,128)S(1)}, f32[160,128]{1,0:T(8,128)S(1)}, u32[]{:S(2)}, u32[]{:S(2)}) %collective-permute-start.13) | collective-permute-done | bytes 81952 | tf_op jit(solution)/shard_map/ppermute | solution.py:336
  32.6 1.7 %collective-permute-done.11.refs_1_ = f32[160,128]{1,0:T(8,128)S(1)} collective-permute-done((f32[160,128]{1,0:T(8,128)S(1)}, f32[160,128]{1,0:T(8,128)S(1)}, u32[]{:S(2)}, u32[]{:S(2)}) %collective-permute-start.11) | collective-permute-done | bytes 81952 | tf_op jit(solution)/shard_map/ppermute | solution.py:336
  34.5 3.1 %collective-permute-start.14 = (f32[160,128]{1,0:T(8,128)S(1)}, f32[160,128]{1,0:T(8,128)S(1)}, u32[]{:S(2)}, u32[]{:S(2)}) collective-permute-start(f32[160,128]{1,0:T(8,128)S(1)} %shard_map.74.refs_0_), channel_id=1, source_target_pairs={{0,2},{1,3},{2,0},{3,1},{4,6},{5,7},{6,4},{7,5},{8,10},{9,11},{10,... | collective-permute-start | bytes 245768 | tf_op jit(solution)/shard_map/ppermute | solution.py:336
  37.8 0.7 %collective-permute-start.20 = (bf16[128,384]{1,0:T(8,128)(2,1)S(1)}, bf16[128,384]{1,0:T(8,128)(2,1)S(1)}, u32[]{:S(2)}, u32[]{:S(2)}) collective-permute-start(bf16[128,384]{1,0:T(8,128)(2,1)S(1)} %get-tuple-element.40), channel_id=1, source_target_pairs={{0,0},{1,4},{2,8},{3,12},{4,1},{5,5},{6,9},{7,13},{8,2},{9,6},{10,... | collective-permute-start | bytes 294920 | tf_op jit(solution)/shard_map/ppermute | solution.py:392
  38.5 4.5 %collective-permute-start.21 = (bf16[128,384]{1,0:T(8,128)(2,1)S(1)}, bf16[128,384]{1,0:T(8,128)(2,1)S(1)}, u32[]{:S(2)}, u32[]{:S(2)}) collective-permute-start(bf16[128,384]{1,0:T(8,128)(2,1)S(1)} %get-tuple-element.41), channel_id=1, source_target_pairs={{0,2},{1,6},{2,10},{3,14},{4,3},{5,7},{6,11},{7,15},{8,0},{9,4},{1... | collective-permute-start | bytes 294920 | tf_op jit(solution)/shard_map/ppermute | solution.py:392
  43.0 1.6 %collective-permute-start.16 = (f32[160,128]{1,0:T(8,128)S(1)}, f32[160,128]{1,0:T(8,128)S(1)}, u32[]{:S(2)}, u32[]{:S(2)}) collective-permute-start(f32[160,128]{1,0:T(8,128)S(1)} %shard_map.75.refs_0_), channel_id=1, source_target_pairs={{0,16},{1,17},{2,18},{3,19},{4,20},{5,21},{6,22},{7,23},{8,24},{9,... | collective-permute-start | bytes 245768 | tf_op jit(solution)/shard_map/ppermute | solution.py:336
  44.6 1.9 %collective-permute-start.15 = (f32[160,128]{1,0:T(8,128)S(1)}, f32[160,128]{1,0:T(8,128)S(1)}, u32[]{:S(2)}, u32[]{:S(2)}) collective-permute-start(f32[160,128]{1,0:T(8,128)S(1)} %shard_map.75.refs_0_), channel_id=1, source_target_pairs={{0,8},{1,9},{2,10},{3,11},{4,12},{5,13},{6,14},{7,15},{8,0},{9,1},... | collective-permute-start | bytes 245768 | tf_op jit(solution)/shard_map/ppermute | solution.py:336
  46.8 2.7 %collective-permute-done.17.refs_3_ = f32[160,128]{1,0:T(8,128)S(1)} collective-permute-done((f32[160,128]{1,0:T(8,128)S(1)}, f32[160,128]{1,0:T(8,128)S(1)}, u32[]{:S(2)}, u32[]{:S(2)}) %collective-permute-start.17) | collective-permute-done | bytes 81952 | tf_op jit(solution)/shard_map/ppermute | solution.py:336
  49.5 0.6 %collective-permute-done.15.refs_1_ = f32[160,128]{1,0:T(8,128)S(1)} collective-permute-done((f32[160,128]{1,0:T(8,128)S(1)}, f32[160,128]{1,0:T(8,128)S(1)}, u32[]{:S(2)}, u32[]{:S(2)}) %collective-permute-start.15) | collective-permute-done | bytes 81952 | tf_op jit(solution)/shard_map/ppermute | solution.py:336
  50.3 1.0 %shard_map.79 = (bf16[1,128,2,384]{3,2,1,0:T(2,128)(2,1)}, f32[2,384,384]{2,1,0:T(8,128)}) custom-call(f32[4,160,128]{2,1,0:T(8,128)S(1)} %shard_map.78.refs_0_, bf16[1,128,2,384]{3,2,1,0:T(2,128)(2,1)S(1)} %shard_map.77.refs_4_.refs_1_), custom_call_target="tpu_custom_call" | custom-call | tf_op jit(solution)/shard_map/pallas_call | solution.py:28
  51.3 0.6 %collective-permute-done.22.refs_1_ = f32[4,160,128]{2,1,0:T(8,128)S(1)} collective-permute-done((f32[4,160,128]{2,1,0:T(8,128)S(1)}, f32[4,160,128]{2,1,0:T(8,128)S(1)}, u32[]{:S(2)}, u32[]{:S(2)}) %collective-permute-start.22) | collective-permute-done | bytes 327712 | tf_op jit(solution)/shard_map/ppermute | solution.py:336
  51.9 1.2 %shard_map.80 = f32[2,384,384]{2,1,0:T(8,128)} custom-call(f32[4,160,128]{2,1,0:T(8,128)S(1)} %shard_map.78.refs_0_, f32[4,160,128]{2,1,0:T(8,128)S(1)} %collective-permute-done.22.refs_1_, f32[2,384,384]{2,1,0:T(8,128)} %get-tuple-element.43.refs_2_), custom_call_target="tpu_custom_call", output_to_operand_aliasing={{}: (2, {})} | custom-call | tf_op jit(solution)/shard_map/pallas_call | solution.py:28
  (29 shorter events, 2.7 us)
Async XLA Ops:
  2.3 9.2 %collective-permute-start.3 = (bf16[160,384]{1,0:T(8,128)(2,1)S(1)}, bf16[160,384]{1,0:T(8,128)(2,1)S(1)}, u32[]{:S(2)}, u32[]{:S(2)}) collective-permute-start(bf16[160,384]{1,0:T(8,128)(2,1)S(1)} %get-tuple-element.27), channel_id=1, source_target_pairs={{0,8},{1,9},{2,10},{3,11},{4,12},{5,13},{6,14},{7,15},{8,0},{9,1},... | collective-permute-start | bytes 368648 | tf_op jit(solution)/shard_map/ppermute | solution.py:336
  5.3 16.6 %collective-permute-start.7 = (bf16[256,512]{1,0:T(8,128)(2,1)S(1)}, bf16[256,512]{1,0:T(8,128)(2,1)S(1)}, u32[]{:S(2)}, u32[]{:S(2)}) collective-permute-start(bf16[256,512]{1,0:T(8,128)(2,1)S(1)} %get-tuple-element.24.refs_5_), channel_id=1, source_target_pairs={{0,8},{1,9},{2,10},{3,11},{4,12},{5,13},{6,14},{7,15},{8,0},{9,1},... | collective-permute-start | bytes 786440 | tf_op jit(solution)/shard_map/ppermute | solution.py:336
  5.4 16.5 %collective-permute-start.8 = (bf16[256,512]{1,0:T(8,128)(2,1)S(1)}, bf16[256,512]{1,0:T(8,128)(2,1)S(1)}, u32[]{:S(2)}, u32[]{:S(2)}) collective-permute-start(bf16[256,512]{1,0:T(8,128)(2,1)S(1)} %get-tuple-element.25.refs_6_), channel_id=1, source_target_pairs={{0,8},{1,9},{2,10},{3,11},{4,12},{5,13},{6,14},{7,15},{8,0},{9,1},... | collective-permute-start | bytes 786440 | tf_op jit(solution)/shard_map/ppermute | solution.py:336
  7.4 5.8 %collective-permute-start = (bf16[128,384]{1,0:T(8,128)(2,1)S(1)}, bf16[128,384]{1,0:T(8,128)(2,1)S(1)}, u32[]{:S(2)}, u32[]{:S(2)}) collective-permute-start(bf16[128,384]{1,0:T(8,128)(2,1)S(1)} %get-tuple-element.23.refs_1_), channel_id=1, source_target_pairs={{0,2},{1,3},{2,0},{3,1},{4,6},{5,7},{6,4},{7,5},{8,10},{9,11},{10,... | collective-permute-start | bytes 294920 | tf_op jit(solution)/shard_map/ppermute | solution.py:336
  10.0 7.0 %collective-permute-start.1 = (bf16[128,384]{1,0:T(8,128)(2,1)S(1)}, bf16[128,384]{1,0:T(8,128)(2,1)S(1)}, u32[]{:S(2)}, u32[]{:S(2)}) collective-permute-start(bf16[128,384]{1,0:T(8,128)(2,1)S(1)} %get-tuple-element.23.refs_1_), channel_id=1, source_target_pairs={{0,1},{1,0},{2,3},{3,2},{4,5},{5,4},{6,7},{7,6},{8,9},{9,8},{10,11... | collective-permute-start | bytes 294920 | tf_op jit(solution)/shard_map/ppermute | solution.py:336
  11.6 6.8 %collective-permute-start.4 = (bf16[128,384]{1,0:T(8,128)(2,1)S(1)}, bf16[128,384]{1,0:T(8,128)(2,1)S(1)}, u32[]{:S(2)}, u32[]{:S(2)}) collective-permute-start(bf16[128,384]{1,0:T(8,128)(2,1)S(1)} %slice.8.refs_0_), channel_id=1, source_target_pairs={{0,2},{1,3},{2,0},{3,1},{4,6},{5,7},{6,4},{7,5},{8,10},{9,11},{10,... | collective-permute-start | bytes 294920 | tf_op jit(solution)/shard_map/ppermute | solution.py:336
  13.1 7.6 %collective-permute-start.2 = (bf16[128,384]{1,0:T(8,128)(2,1)S(1)}, bf16[128,384]{1,0:T(8,128)(2,1)S(1)}, u32[]{:S(2)}, u32[]{:S(2)}) collective-permute-start(bf16[128,384]{1,0:T(8,128)(2,1)S(1)} %collective-permute-done.refs_2_), channel_id=1, source_target_pairs={{0,1},{1,0},{2,3},{3,2},{4,5},{5,4},{6,7},{7,6},{8,9},{9,8},{10,11... | collective-permute-start | bytes 294920 | tf_op jit(solution)/shard_map/ppermute | solution.py:336
  17.0 5.0 %collective-permute-start.5 = (bf16[128,384]{1,0:T(8,128)(2,1)S(1)}, bf16[128,384]{1,0:T(8,128)(2,1)S(1)}, u32[]{:S(2)}, u32[]{:S(2)}) collective-permute-start(bf16[128,384]{1,0:T(8,128)(2,1)S(1)} %slice.8.refs_0_), channel_id=1, source_target_pairs={{0,1},{1,0},{2,3},{3,2},{4,5},{5,4},{6,7},{7,6},{8,9},{9,8},{10,11... | collective-permute-start | bytes 294920 | tf_op jit(solution)/shard_map/ppermute | solution.py:336
  18.3 4.7 %collective-permute-start.6 = (bf16[128,384]{1,0:T(8,128)(2,1)S(1)}, bf16[128,384]{1,0:T(8,128)(2,1)S(1)}, u32[]{:S(2)}, u32[]{:S(2)}) collective-permute-start(bf16[128,384]{1,0:T(8,128)(2,1)S(1)} %collective-permute-done.4.refs_1_), channel_id=1, source_target_pairs={{0,1},{1,0},{2,3},{3,2},{4,5},{5,4},{6,7},{7,6},{8,9},{9,8},{10,11... | collective-permute-start | bytes 294920 | tf_op jit(solution)/shard_map/ppermute | solution.py:336
  23.1 1.8 %collective-permute-start.9 = (bf16[512,384]{1,0:T(8,128)(2,1)S(1)}, bf16[512,384]{1,0:T(8,128)(2,1)S(1)}, u32[]{:S(2)}, u32[]{:S(2)}) collective-permute-start(bf16[512,384]{1,0:T(8,128)(2,1)S(1)} %get-tuple-element.29.refs_0_), channel_id=1, source_target_pairs={{0,4},{1,5},{2,6},{3,7},{4,0},{5,1},{6,2},{7,3},{8,12},{9,13},{10,... | collective-permute-start | bytes 1179656 | tf_op jit(solution)/shard_map/ppermute | solution.py:336
  23.6 14.0 %collective-permute-start.18 = (f32[256,384]{1,0:T(8,128)S(1)}, f32[256,384]{1,0:T(8,128)S(1)}, u32[]{:S(2)}, u32[]{:S(2)}) collective-permute-start(f32[256,384]{1,0:T(8,128)S(1)} %get-tuple-element.33.refs_4_.refs_0_), channel_id=1, source_target_pairs={{0,4},{1,5},{2,6},{3,7},{4,0},{5,1},{6,2},{7,3},{8,12},{9,13},{10,... | collective-permute-start | bytes 1179656 | tf_op jit(solution)/shard_map/ppermute | solution.py:336
  24.2 13.5 %collective-permute-start.19 = (f32[256,384]{1,0:T(8,128)S(1)}, f32[256,384]{1,0:T(8,128)S(1)}, u32[]{:S(2)}, u32[]{:S(2)}) collective-permute-start(f32[256,384]{1,0:T(8,128)S(1)} %get-tuple-element.34.refs_5_.refs_1_), channel_id=1, source_target_pairs={{0,4},{1,5},{2,6},{3,7},{4,0},{5,1},{6,2},{7,3},{8,12},{9,13},{10,... | collective-permute-start | bytes 1179656 | tf_op jit(solution)/shard_map/ppermute | solution.py:336
  25.6 1.4 %collective-permute-start.10 = (f32[320,128]{1,0:T(8,128)S(1)}, f32[320,128]{1,0:T(8,128)S(1)}, u32[]{:S(2)}, u32[]{:S(2)}) collective-permute-start(f32[320,128]{1,0:T(8,128)S(1)} %get-tuple-element.36), channel_id=1, source_target_pairs={{0,4},{1,5},{2,6},{3,7},{4,0},{5,1},{6,2},{7,3},{8,12},{9,13},{10,... | collective-permute-start | bytes 491528 | tf_op jit(solution)/shard_map/ppermute | solution.py:336
  27.1 5.5 %collective-permute-start.13 = (f32[160,128]{1,0:T(8,128)S(1)}, f32[160,128]{1,0:T(8,128)S(1)}, u32[]{:S(2)}, u32[]{:S(2)}) collective-permute-start(f32[160,128]{1,0:T(8,128)S(1)} %get-tuple-element.38), channel_id=1, source_target_pairs={{0,17},{1,16},{2,19},{3,18},{4,21},{5,20},{6,23},{7,22},{8,25},{9,... | collective-permute-start | bytes 245768 | tf_op jit(solution)/shard_map/ppermute | solution.py:336
  29.5 4.8 %collective-permute-start.11 = (f32[160,128]{1,0:T(8,128)S(1)}, f32[160,128]{1,0:T(8,128)S(1)}, u32[]{:S(2)}, u32[]{:S(2)}) collective-permute-start(f32[160,128]{1,0:T(8,128)S(1)} %get-tuple-element.38), channel_id=1, source_target_pairs={{0,16},{1,17},{2,18},{3,19},{4,20},{5,21},{6,22},{7,23},{8,24},{9,... | collective-permute-start | bytes 245768 | tf_op jit(solution)/shard_map/ppermute | solution.py:336
  30.1 4.4 %collective-permute-start.12 = (f32[160,128]{1,0:T(8,128)S(1)}, f32[160,128]{1,0:T(8,128)S(1)}, u32[]{:S(2)}, u32[]{:S(2)}) collective-permute-start(f32[160,128]{1,0:T(8,128)S(1)} %get-tuple-element.37.refs_0_.refs_4_), channel_id=1, source_target_pairs={{0,1},{1,0},{2,3},{3,2},{4,5},{5,4},{6,7},{7,6},{8,9},{9,8},{10,11... | collective-permute-start | bytes 245768 | tf_op jit(solution)/shard_map/ppermute | solution.py:336
  34.5 8.4 %collective-permute-start.14 = (f32[160,128]{1,0:T(8,128)S(1)}, f32[160,128]{1,0:T(8,128)S(1)}, u32[]{:S(2)}, u32[]{:S(2)}) collective-permute-start(f32[160,128]{1,0:T(8,128)S(1)} %shard_map.74.refs_0_), channel_id=1, source_target_pairs={{0,2},{1,3},{2,0},{3,1},{4,6},{5,7},{6,4},{7,5},{8,10},{9,11},{10,... | collective-permute-start | bytes 245768 | tf_op jit(solution)/shard_map/ppermute | solution.py:336
  37.8 8.7 %collective-permute-start.20 = (bf16[128,384]{1,0:T(8,128)(2,1)S(1)}, bf16[128,384]{1,0:T(8,128)(2,1)S(1)}, u32[]{:S(2)}, u32[]{:S(2)}) collective-permute-start(bf16[128,384]{1,0:T(8,128)(2,1)S(1)} %get-tuple-element.40), channel_id=1, source_target_pairs={{0,0},{1,4},{2,8},{3,12},{4,1},{5,5},{6,9},{7,13},{8,2},{9,6},{10,... | collective-permute-start | bytes 294920 | tf_op jit(solution)/shard_map/ppermute | solution.py:392
  38.5 8.0 %collective-permute-start.21 = (bf16[128,384]{1,0:T(8,128)(2,1)S(1)}, bf16[128,384]{1,0:T(8,128)(2,1)S(1)}, u32[]{:S(2)}, u32[]{:S(2)}) collective-permute-start(bf16[128,384]{1,0:T(8,128)(2,1)S(1)} %get-tuple-element.41), channel_id=1, source_target_pairs={{0,2},{1,6},{2,10},{3,14},{4,3},{5,7},{6,11},{7,15},{8,0},{9,4},{1... | collective-permute-start | bytes 294920 | tf_op jit(solution)/shard_map/ppermute | solution.py:392
  43.0 6.6 %collective-permute-start.17 = (f32[160,128]{1,0:T(8,128)S(1)}, f32[160,128]{1,0:T(8,128)S(1)}, u32[]{:S(2)}, u32[]{:S(2)}) collective-permute-start(f32[160,128]{1,0:T(8,128)S(1)} %shard_map.75.refs_0_), channel_id=1, source_target_pairs={{0,24},{1,25},{2,26},{3,27},{4,28},{5,29},{6,30},{7,31},{8,16},{9,... | collective-permute-start | bytes 245768 | tf_op jit(solution)/shard_map/ppermute | solution.py:336
  43.0 6.5 %collective-permute-start.16 = (f32[160,128]{1,0:T(8,128)S(1)}, f32[160,128]{1,0:T(8,128)S(1)}, u32[]{:S(2)}, u32[]{:S(2)}) collective-permute-start(f32[160,128]{1,0:T(8,128)S(1)} %shard_map.75.refs_0_), channel_id=1, source_target_pairs={{0,16},{1,17},{2,18},{3,19},{4,20},{5,21},{6,22},{7,23},{8,24},{9,... | collective-permute-start | bytes 245768 | tf_op jit(solution)/shard_map/ppermute | solution.py:336
  44.6 5.5 %collective-permute-start.15 = (f32[160,128]{1,0:T(8,128)S(1)}, f32[160,128]{1,0:T(8,128)S(1)}, u32[]{:S(2)}, u32[]{:S(2)}) collective-permute-start(f32[160,128]{1,0:T(8,128)S(1)} %shard_map.75.refs_0_), channel_id=1, source_target_pairs={{0,8},{1,9},{2,10},{3,11},{4,12},{5,13},{6,14},{7,15},{8,0},{9,1},... | collective-permute-start | bytes 245768 | tf_op jit(solution)/shard_map/ppermute | solution.py:336
  50.2 1.7 %collective-permute-start.22 = (f32[4,160,128]{2,1,0:T(8,128)S(1)}, f32[4,160,128]{2,1,0:T(8,128)S(1)}, u32[]{:S(2)}, u32[]{:S(2)}) collective-permute-start(f32[4,160,128]{2,1,0:T(8,128)S(1)} %shard_map.78.refs_0_), channel_id=1, source_target_pairs={{0,4},{1,5},{2,6},{3,7},{4,0},{5,1},{6,2},{7,3},{8,12},{9,13},{10,... | collective-permute-start | bytes 983048 | tf_op jit(solution)/shard_map/ppermute | solution.py:336

commit v23 on v22

--- a/solution.py
+++ b/solution.py
@@ -143,8 +143,10 @@
 
 
 def own_kernel(*refs):
-    weight, blocks, pieces, (rows, applied, tile) = refs[0], refs[1:5], refs[5:-3], refs[-3:]
+    weight, inverses, blocks, pieces = refs[0], refs[1:3], refs[3:7], refs[7:-4]
+    rows, applied, tile, base = refs[-4:]
     tile[...] = jnp.full(tile.shape, weight[0], tile.dtype)
+    base[...] = sum(transposed_dot(lines[...], lines[...]) for lines in inverses)
     set_rows(blocks, rows)
     at = 0
     for piece in pieces:
@@ -160,27 +162,26 @@
 
 
 def apply_kernel(own, rows, *refs):
-    count, at = len(refs) // 2, 0
-    for piece, applied in zip(refs[:count], refs[count:]):
+    pieces, outs, (high, low) = refs[: len(refs) // 2 - 1], refs[len(refs) // 2 - 1 : -2], refs[-2:]
+    at = 0
+    for piece, out in zip(pieces, outs):
         lines = slice(at, at + piece.shape[0])
-        applied[...] = own[lines] + jnp.dot(piece[...], rows[...], preferred_element_type=jnp.float32)
+        applied = own[lines] + jnp.dot(piece[...], rows[...], preferred_element_type=jnp.float32)
+        out[...] = applied
+        high[lines] = applied.astype(jnp.bfloat16)
+        low[lines] = (applied - applied.astype(jnp.bfloat16).astype(jnp.float32)).astype(jnp.bfloat16)
         at += piece.shape[0]
 
 
-def couple_kernel(pack, got_pack, own_inverse, got_inverse, *refs):
+def couple_kernel(pack, got_pack, high, low, base, keep, send, packed):
     core, column = lax.axis_index("core"), lax.axis_index("pcol")
-    parts, (keep, send, packed) = refs[:-3], refs[-3:]
-    applied = jnp.concatenate([part[...] for part in parts], 0)
-    high = applied.astype(jnp.bfloat16)
-    low = (applied - high.astype(jnp.float32)).astype(jnp.bfloat16)
     rows = jnp.where(column % 2 == core, pack[...], got_pack[...])
     blocks = {}
     for first in range(BLOCKS):
         left, right = slice(first * LANES, (first + 1) * LANES), slice(first * LANES, None)
         total = transposed_dot(rows[:, left], high[:, right])
         total += transposed_dot(rows[:, left], low[:, right])
-        for lines in (own_inverse, got_inverse):
-            total += transposed_dot(lines[:, left], lines[:, right])
+        total += base[left, right]
         for index in range(BLOCKS - first):
             blocks[first, first + index] = total[:, index * LANES : (index + 1) * LANES]
     held = [blocks[place] for place in ABOVE]
@@ -360,24 +361,26 @@
 
 
     product, line_shape = shape((extent, width), f32), shape((extent, width), bf16)
-    own_rows, own_product, weight = call(
-        own_kernel, [line_shape, product, shape((8, LANES), f32)], [SMEM] + [VMEM] * (4 + len(cuts)),
-        quad_weight, *blocks[:4], *pieces,
+    own_rows, own_product, weight, base = call(
+        own_kernel,
+        [line_shape, product, shape((8, LANES), f32), shape((width, width), f32)],
+        [SMEM] + [VMEM] * (6 + len(cuts)),
+        quad_weight, own_inverse, got_inverse, *blocks[:4], *pieces,
     )
     rows, pack = call(
         gather_kernel, [line_shape] * 2, [VMEM] * 5, *blocks[4:], own_rows, after=far
     )
     got_pack = swap(pack, core=1)
-    mine = call(
-        apply_kernel, [shape((lines, width), f32) for lines in cuts], [VMEM] * (2 + len(cuts)),
+    *mine, high, low = call(
+        apply_kernel, [shape((lines, width), f32) for lines in cuts] + [line_shape] * 2, [VMEM] * (2 + len(cuts)),
         own_product, rows, *far,
     )
     lines = HELD * LANES // 2
     part, half = shape((lines // 2, LANES), f32), shape((lines, LANES), f32)
     other = [swap(x, core=1) for x in mine]
     keep, send = call(
-        couple_kernel, [half, half], [VMEM] * (4 + len(cuts)),
-        pack, got_pack, own_inverse, got_inverse, *mine,
+        couple_kernel, [half, half], [VMEM] * 5,
+        pack, got_pack, high, low, base,
         scratch=[pltpu.VMEM((2 * lines, LANES), f32)],
     )
     keep, send = call(

time: 53.2 us -> 53.1 us (level)
  no operation moved by 1% of the time
where the time goes in v23:
time: 53.1 us; the launch traced here: 52.9 us
  starting transfers between devices  31.9 us (60%)
  waiting for transfers between devices  13.4 us (25%)
  Pallas kernels  6.16 us (12%)
  between operations  1.4 us (3%)
    ppermute x21, starting transfers between devices, swap(): return lax.ppermute(x, AXES, [(i, i ^ mask) for i in range(devices)])  26.8 us
    ppermute x21, waiting for transfers between devices, swap(): return lax.ppermute(x, AXES, [(i, i ^ mask) for i in range(devices)])  13.4 us
    pallas_call x13, Pallas kernels, call(): pl.pallas_call(body, out_shape=outs, in_specs=list(specs) + [ANY] * len(a...  6.16 us
    ppermute x2, starting transfers between devices, deliver(): return lax.ppermute(x, AXES, pairs)  5.14 us
  transfers between devices with their start and end apart: 23, of which 13 were waited for; matrix products, arithmetic and copies ran while one was open for 0% of the time, Pallas kernels for 6%

profile of v23, /device:TPU:0, one launch (start us, length us, event | category | flops | bytes accessed | tf_op | source)
XLA Modules:
  0.0 52.9 jit_solution(2706591987453018622)
XLA Ops:
  0.6 1.7 %shard_map.68 = (bf16[128,384]{1,0:T(8,128)(2,1)S(1)}, bf16[160,384]{1,0:T(8,128)(2,1)S(1)}, bf16[32,384]{1,0:T(8,128)(2,1)S(1)}, s32[2,8,128]{2,1,0:T(8,128)S(1...) custom-call(s32[2]{0:T(128)} %bitcast.1, bf16[1,128,2,384]{3,2,1,0:T(2,128)(2,1)} %refs_1_.1, ...), custom_call_target="tpu_custom_call" | custom-call | tf_op jit(solution)/shard_map/pallas_call | solution.py:28
  2.3 3.0 %collective-permute-start = (bf16[160,384]{1,0:T(8,128)(2,1)S(1)}, bf16[160,384]{1,0:T(8,128)(2,1)S(1)}, u32[]{:S(2)}, u32[]{:S(2)}) collective-permute-start(bf16[160,384]{1,0:T(8,128)(2,1)S(1)} %get-tuple-element.27), channel_id=1, source_target_pairs={{0,8},{1,9},{2,10},{3,11},{4,12},{5,13},{6,14},{7,15},{8,0},{9,1},... | collective-permute-start | bytes 368648 | tf_op jit(solution)/shard_map/ppermute | solution.py:337
  5.4 1.9 %collective-permute-start.8 = (bf16[256,512]{1,0:T(8,128)(2,1)S(1)}, bf16[256,512]{1,0:T(8,128)(2,1)S(1)}, u32[]{:S(2)}, u32[]{:S(2)}) collective-permute-start(bf16[256,512]{1,0:T(8,128)(2,1)S(1)} %get-tuple-element.30.refs_8_), channel_id=1, source_target_pairs={{0,8},{1,9},{2,10},{3,11},{4,12},{5,13},{6,14},{7,15},{8,0},{9,1},... | collective-permute-start | bytes 786440 | tf_op jit(solution)/shard_map/ppermute | solution.py:337
  7.4 2.6 %collective-permute-start.1 = (bf16[128,384]{1,0:T(8,128)(2,1)S(1)}, bf16[128,384]{1,0:T(8,128)(2,1)S(1)}, u32[]{:S(2)}, u32[]{:S(2)}) collective-permute-start(bf16[128,384]{1,0:T(8,128)(2,1)S(1)} %get-tuple-element.28.refs_3_), channel_id=1, source_target_pairs={{0,2},{1,3},{2,0},{3,1},{4,6},{5,7},{6,4},{7,5},{8,10},{9,11},{10,... | collective-permute-start | bytes 294920 | tf_op jit(solution)/shard_map/ppermute | solution.py:337
  10.0 1.6 %collective-permute-start.2 = (bf16[128,384]{1,0:T(8,128)(2,1)S(1)}, bf16[128,384]{1,0:T(8,128)(2,1)S(1)}, u32[]{:S(2)}, u32[]{:S(2)}) collective-permute-start(bf16[128,384]{1,0:T(8,128)(2,1)S(1)} %get-tuple-element.28.refs_3_), channel_id=1, source_target_pairs={{0,1},{1,0},{2,3},{3,2},{4,5},{5,4},{6,7},{7,6},{8,9},{9,8},{10,11... | collective-permute-start | bytes 294920 | tf_op jit(solution)/shard_map/ppermute | solution.py:337
  11.6 1.2 %collective-permute-start.4 = (bf16[128,384]{1,0:T(8,128)(2,1)S(1)}, bf16[128,384]{1,0:T(8,128)(2,1)S(1)}, u32[]{:S(2)}, u32[]{:S(2)}) collective-permute-start(bf16[128,384]{1,0:T(8,128)(2,1)S(1)} %slice.9.refs_0_), channel_id=1, source_target_pairs={{0,2},{1,3},{2,0},{3,1},{4,6},{5,7},{6,4},{7,5},{8,10},{9,11},{10,... | collective-permute-start | bytes 294920 | tf_op jit(solution)/shard_map/ppermute | solution.py:337
  13.1 3.8 %collective-permute-start.3 = (bf16[128,384]{1,0:T(8,128)(2,1)S(1)}, bf16[128,384]{1,0:T(8,128)(2,1)S(1)}, u32[]{:S(2)}, u32[]{:S(2)}) collective-permute-start(bf16[128,384]{1,0:T(8,128)(2,1)S(1)} %collective-permute-done.1.refs_4_), channel_id=1, source_target_pairs={{0,1},{1,0},{2,3},{3,2},{4,5},{5,4},{6,7},{7,6},{8,9},{9,8},{10,11... | collective-permute-start | bytes 294920 | tf_op jit(solution)/shard_map/ppermute | solution.py:337
  17.0 0.7 %collective-permute-start.5 = (bf16[128,384]{1,0:T(8,128)(2,1)S(1)}, bf16[128,384]{1,0:T(8,128)(2,1)S(1)}, u32[]{:S(2)}, u32[]{:S(2)}) collective-permute-start(bf16[128,384]{1,0:T(8,128)(2,1)S(1)} %slice.9.refs_0_), channel_id=1, source_target_pairs={{0,1},{1,0},{2,3},{3,2},{4,5},{5,4},{6,7},{7,6},{8,9},{9,8},{10,11... | collective-permute-start | bytes 294920 | tf_op jit(solution)/shard_map/ppermute | solution.py:337
  17.7 0.6 %collective-permute-done.4.refs_1_ = bf16[128,384]{1,0:T(8,128)(2,1)S(1)} collective-permute-done((bf16[128,384]{1,0:T(8,128)(2,1)S(1)}, bf16[128,384]{1,0:T(8,128)(2,1)S(1)}, u32[]{:S(2)}, u32[]{:S(2)}) %collective-permute-start.4) | collective-permute-done | bytes 98336 | tf_op jit(solution)/shard_map/ppermute | solution.py:337
  18.3 0.7 %collective-permute-start.6 = (bf16[128,384]{1,0:T(8,128)(2,1)S(1)}, bf16[128,384]{1,0:T(8,128)(2,1)S(1)}, u32[]{:S(2)}, u32[]{:S(2)}) collective-permute-start(bf16[128,384]{1,0:T(8,128)(2,1)S(1)} %collective-permute-done.4.refs_1_), channel_id=1, source_target_pairs={{0,1},{1,0},{2,3},{3,2},{4,5},{5,4},{6,7},{7,6},{8,9},{9,8},{10,11... | collective-permute-start | bytes 294920 | tf_op jit(solution)/shard_map/ppermute | solution.py:337
  19.7 1.0 %collective-permute-done.3.refs_6_ = bf16[128,384]{1,0:T(8,128)(2,1)S(1)} collective-permute-done((bf16[128,384]{1,0:T(8,128)(2,1)S(1)}, bf16[128,384]{1,0:T(8,128)(2,1)S(1)}, u32[]{:S(2)}, u32[]{:S(2)}) %collective-permute-start.3) | collective-permute-done | bytes 98336 | tf_op jit(solution)/shard_map/ppermute | solution.py:337
  20.7 0.6 %shard_map.69 = (bf16[512,384]{1,0:T(8,128)(2,1)S(1)}, f32[512,384]{1,0:T(8,128)S(1)}, f32[8,128]{1,0:T(8,128)S(1)}, f32[384,384]{1,0:T(8,128)S(1)}) custom-call(f32[1]{0:T(128)S(6)} %copy.9.refs_0_, bf16[32,384]{1,0:T(8,128)(2,1)S(1)} %get-tuple-element.26.refs_1_, bf16[32,384]{1,0:T(8,128)(2,1)S(1)} %slice.8.refs_2_, ...), custom_call_target="tpu_custom_call" | custom-call | tf_op jit(solution)/shard_map/pallas_call | solution.py:28
  21.3 0.6 %collective-permute-done.5.refs_2_ = bf16[128,384]{1,0:T(8,128)(2,1)S(1)} collective-permute-done((bf16[128,384]{1,0:T(8,128)(2,1)S(1)}, bf16[128,384]{1,0:T(8,128)(2,1)S(1)}, u32[]{:S(2)}, u32[]{:S(2)}) %collective-permute-start.5) | collective-permute-done | bytes 98336 | tf_op jit(solution)/shard_map/ppermute | solution.py:337
  22.0 1.0 %collective-permute-done.6.refs_3_ = bf16[128,384]{1,0:T(8,128)(2,1)S(1)} collective-permute-done((bf16[128,384]{1,0:T(8,128)(2,1)S(1)}, bf16[128,384]{1,0:T(8,128)(2,1)S(1)}, u32[]{:S(2)}, u32[]{:S(2)}) %collective-permute-start.6) | collective-permute-done | bytes 98336 | tf_op jit(solution)/shard_map/ppermute | solution.py:337
  23.6 0.6 %collective-permute-start.18 = (f32[256,384]{1,0:T(8,128)S(1)}, f32[256,384]{1,0:T(8,128)S(1)}, u32[]{:S(2)}, u32[]{:S(2)}) collective-permute-start(f32[256,384]{1,0:T(8,128)S(1)} %get-tuple-element.44.refs_0_), channel_id=1, source_target_pairs={{0,4},{1,5},{2,6},{3,7},{4,0},{5,1},{6,2},{7,3},{8,12},{9,13},{10,... | collective-permute-start | bytes 1179656 | tf_op jit(solution)/shard_map/ppermute | solution.py:337
  24.3 0.6 %collective-permute-done.9.refs_1_ = bf16[512,384]{1,0:T(8,128)(2,1)S(1)} collective-permute-done((bf16[512,384]{1,0:T(8,128)(2,1)S(1)}, bf16[512,384]{1,0:T(8,128)(2,1)S(1)}, u32[]{:S(2)}, u32[]{:S(2)}) %collective-permute-start.9) | collective-permute-done | bytes 393248 | tf_op jit(solution)/shard_map/ppermute | solution.py:337
  24.9 0.6 %shard_map.72 = (f32[320,128]{1,0:T(8,128)S(1)}, f32[320,128]{1,0:T(8,128)S(1)}) custom-call(bf16[512,384]{1,0:T(8,128)(2,1)S(1)} %get-tuple-element.33.refs_0_, bf16[512,384]{1,0:T(8,128)(2,1)S(1)} %collective-permute-done.9.refs_1_, bf16[512,384]{1,0:T(8,128)(2,1)S(1)} %get-tuple-element.36.refs_2_, bf16[512,384]{1,0:T(8,128)(2,1)S(1)} %get-tuple-element.37.refs_3_, ...), custom_call_target="tpu_custom_call" | custom-call | tf_op jit(solution)/shard_map/pallas_call | solution.py:28
  25.7 1.3 %collective-permute-done.10.refs_2_ = f32[320,128]{1,0:T(8,128)S(1)} collective-permute-done((f32[320,128]{1,0:T(8,128)S(1)}, f32[320,128]{1,0:T(8,128)S(1)}, u32[]{:S(2)}, u32[]{:S(2)}) %collective-permute-start.10) | collective-permute-done | bytes 163872 | tf_op jit(solution)/shard_map/ppermute | solution.py:337
  27.0 2.5 %collective-permute-start.13 = (f32[160,128]{1,0:T(8,128)S(1)}, f32[160,128]{1,0:T(8,128)S(1)}, u32[]{:S(2)}, u32[]{:S(2)}) collective-permute-start(f32[160,128]{1,0:T(8,128)S(1)} %get-tuple-element.42), channel_id=1, source_target_pairs={{0,17},{1,16},{2,19},{3,18},{4,21},{5,20},{6,23},{7,22},{8,25},{9,... | collective-permute-start | bytes 245768 | tf_op jit(solution)/shard_map/ppermute | solution.py:337
  29.9 0.6 %collective-permute-start.12 = (f32[160,128]{1,0:T(8,128)S(1)}, f32[160,128]{1,0:T(8,128)S(1)}, u32[]{:S(2)}, u32[]{:S(2)}) collective-permute-start(f32[160,128]{1,0:T(8,128)S(1)} %get-tuple-element.41.refs_0_.refs_4_), channel_id=1, source_target_pairs={{0,1},{1,0},{2,3},{3,2},{4,5},{5,4},{6,7},{7,6},{8,9},{9,8},{10,11... | collective-permute-start | bytes 245768 | tf_op jit(solution)/shard_map/ppermute | solution.py:337
  30.5 2.0 %collective-permute-done.13.refs_3_ = f32[160,128]{1,0:T(8,128)S(1)} collective-permute-done((f32[160,128]{1,0:T(8,128)S(1)}, f32[160,128]{1,0:T(8,128)S(1)}, u32[]{:S(2)}, u32[]{:S(2)}) %collective-permute-start.13) | collective-permute-done | bytes 81952 | tf_op jit(solution)/shard_map/ppermute | solution.py:337
  32.5 1.7 %collective-permute-done.11.refs_1_ = f32[160,128]{1,0:T(8,128)S(1)} collective-permute-done((f32[160,128]{1,0:T(8,128)S(1)}, f32[160,128]{1,0:T(8,128)S(1)}, u32[]{:S(2)}, u32[]{:S(2)}) %collective-permute-start.11) | collective-permute-done | bytes 81952 | tf_op jit(solution)/shard_map/ppermute | solution.py:337
  34.4 3.1 %collective-permute-start.14 = (f32[160,128]{1,0:T(8,128)S(1)}, f32[160,128]{1,0:T(8,128)S(1)}, u32[]{:S(2)}, u32[]{:S(2)}) collective-permute-start(f32[160,128]{1,0:T(8,128)S(1)} %shard_map.74.refs_0_), channel_id=1, source_target_pairs={{0,2},{1,3},{2,0},{3,1},{4,6},{5,7},{6,4},{7,5},{8,10},{9,11},{10,... | collective-permute-start | bytes 245768 | tf_op jit(solution)/shard_map/ppermute | solution.py:337
  37.7 0.7 %collective-permute-start.20 = (bf16[128,384]{1,0:T(8,128)(2,1)S(1)}, bf16[128,384]{1,0:T(8,128)(2,1)S(1)}, u32[]{:S(2)}, u32[]{:S(2)}) collective-permute-start(bf16[128,384]{1,0:T(8,128)(2,1)S(1)} %get-tuple-element.46), channel_id=1, source_target_pairs={{0,0},{1,4},{2,8},{3,12},{4,1},{5,5},{6,9},{7,13},{8,2},{9,6},{10,... | collective-permute-start | bytes 294920 | tf_op jit(solution)/shard_map/ppermute | solution.py:395
  38.3 4.5 %collective-permute-start.21 = (bf16[128,384]{1,0:T(8,128)(2,1)S(1)}, bf16[128,384]{1,0:T(8,128)(2,1)S(1)}, u32[]{:S(2)}, u32[]{:S(2)}) collective-permute-start(bf16[128,384]{1,0:T(8,128)(2,1)S(1)} %get-tuple-element.47), channel_id=1, source_target_pairs={{0,2},{1,6},{2,10},{3,14},{4,3},{5,7},{6,11},{7,15},{8,0},{9,4},{1... | collective-permute-start | bytes 294920 | tf_op jit(solution)/shard_map/ppermute | solution.py:395
  42.9 1.6 %collective-permute-start.16 = (f32[160,128]{1,0:T(8,128)S(1)}, f32[160,128]{1,0:T(8,128)S(1)}, u32[]{:S(2)}, u32[]{:S(2)}) collective-permute-start(f32[160,128]{1,0:T(8,128)S(1)} %shard_map.75.refs_0_), channel_id=1, source_target_pairs={{0,16},{1,17},{2,18},{3,19},{4,20},{5,21},{6,22},{7,23},{8,24},{9,... | collective-permute-start | bytes 245768 | tf_op jit(solution)/shard_map/ppermute | solution.py:337
  44.5 1.9 %collective-permute-start.15 = (f32[160,128]{1,0:T(8,128)S(1)}, f32[160,128]{1,0:T(8,128)S(1)}, u32[]{:S(2)}, u32[]{:S(2)}) collective-permute-start(f32[160,128]{1,0:T(8,128)S(1)} %shard_map.75.refs_0_), channel_id=1, source_target_pairs={{0,8},{1,9},{2,10},{3,11},{4,12},{5,13},{6,14},{7,15},{8,0},{9,1},... | collective-permute-start | bytes 245768 | tf_op jit(solution)/shard_map/ppermute | solution.py:337
  46.7 2.7 %collective-permute-done.17.refs_3_ = f32[160,128]{1,0:T(8,128)S(1)} collective-permute-done((f32[160,128]{1,0:T(8,128)S(1)}, f32[160,128]{1,0:T(8,128)S(1)}, u32[]{:S(2)}, u32[]{:S(2)}) %collective-permute-start.17) | collective-permute-done | bytes 81952 | tf_op jit(solution)/shard_map/ppermute | solution.py:337
  49.4 0.6 %collective-permute-done.15.refs_1_ = f32[160,128]{1,0:T(8,128)S(1)} collective-permute-done((f32[160,128]{1,0:T(8,128)S(1)}, f32[160,128]{1,0:T(8,128)S(1)}, u32[]{:S(2)}, u32[]{:S(2)}) %collective-permute-start.15) | collective-permute-done | bytes 81952 | tf_op jit(solution)/shard_map/ppermute | solution.py:337
  50.1 1.0 %shard_map.79 = (bf16[1,128,2,384]{3,2,1,0:T(2,128)(2,1)}, f32[2,384,384]{2,1,0:T(8,128)}) custom-call(f32[4,160,128]{2,1,0:T(8,128)S(1)} %shard_map.78.refs_0_, bf16[1,128,2,384]{3,2,1,0:T(2,128)(2,1)S(1)} %shard_map.77.refs_4_.refs_1_), custom_call_target="tpu_custom_call" | custom-call | tf_op jit(solution)/shard_map/pallas_call | solution.py:28
  51.2 0.6 %collective-permute-done.22.refs_1_ = f32[4,160,128]{2,1,0:T(8,128)S(1)} collective-permute-done((f32[4,160,128]{2,1,0:T(8,128)S(1)}, f32[4,160,128]{2,1,0:T(8,128)S(1)}, u32[]{:S(2)}, u32[]{:S(2)}) %collective-permute-start.22) | collective-permute-done | bytes 327712 | tf_op jit(solution)/shard_map/ppermute | solution.py:337
  51.7 1.2 %shard_map.80 = f32[2,384,384]{2,1,0:T(8,128)} custom-call(f32[4,160,128]{2,1,0:T(8,128)S(1)} %shard_map.78.refs_0_, f32[4,160,128]{2,1,0:T(8,128)S(1)} %collective-permute-done.22.refs_1_, f32[2,384,384]{2,1,0:T(8,128)} %get-tuple-element.49.refs_2_), custom_call_target="tpu_custom_call", output_to_operand_aliasing={{}: (2, {})} | custom-call | tf_op jit(solution)/shard_map/pallas_call | solution.py:28
  (29 shorter events, 2.7 us)
Async XLA Ops:
  2.3 9.2 %collective-permute-start = (bf16[160,384]{1,0:T(8,128)(2,1)S(1)}, bf16[160,384]{1,0:T(8,128)(2,1)S(1)}, u32[]{:S(2)}, u32[]{:S(2)}) collective-permute-start(bf16[160,384]{1,0:T(8,128)(2,1)S(1)} %get-tuple-element.27), channel_id=1, source_target_pairs={{0,8},{1,9},{2,10},{3,11},{4,12},{5,13},{6,14},{7,15},{8,0},{9,1},... | collective-permute-start | bytes 368648 | tf_op jit(solution)/shard_map/ppermute | solution.py:337
  5.3 16.6 %collective-permute-start.7 = (bf16[256,512]{1,0:T(8,128)(2,1)S(1)}, bf16[256,512]{1,0:T(8,128)(2,1)S(1)}, u32[]{:S(2)}, u32[]{:S(2)}) collective-permute-start(bf16[256,512]{1,0:T(8,128)(2,1)S(1)} %get-tuple-element.29.refs_7_), channel_id=1, source_target_pairs={{0,8},{1,9},{2,10},{3,11},{4,12},{5,13},{6,14},{7,15},{8,0},{9,1},... | collective-permute-start | bytes 786440 | tf_op jit(solution)/shard_map/ppermute | solution.py:337
  5.4 16.5 %collective-permute-start.8 = (bf16[256,512]{1,0:T(8,128)(2,1)S(1)}, bf16[256,512]{1,0:T(8,128)(2,1)S(1)}, u32[]{:S(2)}, u32[]{:S(2)}) collective-permute-start(bf16[256,512]{1,0:T(8,128)(2,1)S(1)} %get-tuple-element.30.refs_8_), channel_id=1, source_target_pairs={{0,8},{1,9},{2,10},{3,11},{4,12},{5,13},{6,14},{7,15},{8,0},{9,1},... | collective-permute-start | bytes 786440 | tf_op jit(solution)/shard_map/ppermute | solution.py:337
  7.4 5.8 %collective-permute-start.1 = (bf16[128,384]{1,0:T(8,128)(2,1)S(1)}, bf16[128,384]{1,0:T(8,128)(2,1)S(1)}, u32[]{:S(2)}, u32[]{:S(2)}) collective-permute-start(bf16[128,384]{1,0:T(8,128)(2,1)S(1)} %get-tuple-element.28.refs_3_), channel_id=1, source_target_pairs={{0,2},{1,3},{2,0},{3,1},{4,6},{5,7},{6,4},{7,5},{8,10},{9,11},{10,... | collective-permute-start | bytes 294920 | tf_op jit(solution)/shard_map/ppermute | solution.py:337
  10.0 7.0 %collective-permute-start.2 = (bf16[128,384]{1,0:T(8,128)(2,1)S(1)}, bf16[128,384]{1,0:T(8,128)(2,1)S(1)}, u32[]{:S(2)}, u32[]{:S(2)}) collective-permute-start(bf16[128,384]{1,0:T(8,128)(2,1)S(1)} %get-tuple-element.28.refs_3_), channel_id=1, source_target_pairs={{0,1},{1,0},{2,3},{3,2},{4,5},{5,4},{6,7},{7,6},{8,9},{9,8},{10,11... | collective-permute-start | bytes 294920 | tf_op jit(solution)/shard_map/ppermute | solution.py:337
  11.6 6.8 %collective-permute-start.4 = (bf16[128,384]{1,0:T(8,128)(2,1)S(1)}, bf16[128,384]{1,0:T(8,128)(2,1)S(1)}, u32[]{:S(2)}, u32[]{:S(2)}) collective-permute-start(bf16[128,384]{1,0:T(8,128)(2,1)S(1)} %slice.9.refs_0_), channel_id=1, source_target_pairs={{0,2},{1,3},{2,0},{3,1},{4,6},{5,7},{6,4},{7,5},{8,10},{9,11},{10,... | collective-permute-start | bytes 294920 | tf_op jit(solution)/shard_map/ppermute | solution.py:337
  13.1 7.6 %collective-permute-start.3 = (bf16[128,384]{1,0:T(8,128)(2,1)S(1)}, bf16[128,384]{1,0:T(8,128)(2,1)S(1)}, u32[]{:S(2)}, u32[]{:S(2)}) collective-permute-start(bf16[128,384]{1,0:T(8,128)(2,1)S(1)} %collective-permute-done.1.refs_4_), channel_id=1, source_target_pairs={{0,1},{1,0},{2,3},{3,2},{4,5},{5,4},{6,7},{7,6},{8,9},{9,8},{10,11... | collective-permute-start | bytes 294920 | tf_op jit(solution)/shard_map/ppermute | solution.py:337
  17.0 5.0 %collective-permute-start.5 = (bf16[128,384]{1,0:T(8,128)(2,1)S(1)}, bf16[128,384]{1,0:T(8,128)(2,1)S(1)}, u32[]{:S(2)}, u32[]{:S(2)}) collective-permute-start(bf16[128,384]{1,0:T(8,128)(2,1)S(1)} %slice.9.refs_0_), channel_id=1, source_target_pairs={{0,1},{1,0},{2,3},{3,2},{4,5},{5,4},{6,7},{7,6},{8,9},{9,8},{10,11... | collective-permute-start | bytes 294920 | tf_op jit(solution)/shard_map/ppermute | solution.py:337
  18.3 4.7 %collective-permute-start.6 = (bf16[128,384]{1,0:T(8,128)(2,1)S(1)}, bf16[128,384]{1,0:T(8,128)(2,1)S(1)}, u32[]{:S(2)}, u32[]{:S(2)}) collective-permute-start(bf16[128,384]{1,0:T(8,128)(2,1)S(1)} %collective-permute-done.4.refs_1_), channel_id=1, source_target_pairs={{0,1},{1,0},{2,3},{3,2},{4,5},{5,4},{6,7},{7,6},{8,9},{9,8},{10,11... | collective-permute-start | bytes 294920 | tf_op jit(solution)/shard_map/ppermute | solution.py:337
  23.1 1.8 %collective-permute-start.9 = (bf16[512,384]{1,0:T(8,128)(2,1)S(1)}, bf16[512,384]{1,0:T(8,128)(2,1)S(1)}, u32[]{:S(2)}, u32[]{:S(2)}) collective-permute-start(bf16[512,384]{1,0:T(8,128)(2,1)S(1)} %get-tuple-element.33.refs_0_), channel_id=1, source_target_pairs={{0,4},{1,5},{2,6},{3,7},{4,0},{5,1},{6,2},{7,3},{8,12},{9,13},{10,... | collective-permute-start | bytes 1179656 | tf_op jit(solution)/shard_map/ppermute | solution.py:337
  23.6 13.9 %collective-permute-start.18 = (f32[256,384]{1,0:T(8,128)S(1)}, f32[256,384]{1,0:T(8,128)S(1)}, u32[]{:S(2)}, u32[]{:S(2)}) collective-permute-start(f32[256,384]{1,0:T(8,128)S(1)} %get-tuple-element.44.refs_0_), channel_id=1, source_target_pairs={{0,4},{1,5},{2,6},{3,7},{4,0},{5,1},{6,2},{7,3},{8,12},{9,13},{10,... | collective-permute-start | bytes 1179656 | tf_op jit(solution)/shard_map/ppermute | solution.py:337
  24.2 13.3 %collective-permute-start.19 = (f32[256,384]{1,0:T(8,128)S(1)}, f32[256,384]{1,0:T(8,128)S(1)}, u32[]{:S(2)}, u32[]{:S(2)}) collective-permute-start(f32[256,384]{1,0:T(8,128)S(1)} %get-tuple-element.45.refs_1_), channel_id=1, source_target_pairs={{0,4},{1,5},{2,6},{3,7},{4,0},{5,1},{6,2},{7,3},{8,12},{9,13},{10,... | collective-permute-start | bytes 1179656 | tf_op jit(solution)/shard_map/ppermute | solution.py:337
  25.5 1.4 %collective-permute-start.10 = (f32[320,128]{1,0:T(8,128)S(1)}, f32[320,128]{1,0:T(8,128)S(1)}, u32[]{:S(2)}, u32[]{:S(2)}) collective-permute-start(f32[320,128]{1,0:T(8,128)S(1)} %get-tuple-element.40), channel_id=1, source_target_pairs={{0,4},{1,5},{2,6},{3,7},{4,0},{5,1},{6,2},{7,3},{8,12},{9,13},{10,... | collective-permute-start | bytes 491528 | tf_op jit(solution)/shard_map/ppermute | solution.py:337
  27.0 5.5 %collective-permute-start.13 = (f32[160,128]{1,0:T(8,128)S(1)}, f32[160,128]{1,0:T(8,128)S(1)}, u32[]{:S(2)}, u32[]{:S(2)}) collective-permute-start(f32[160,128]{1,0:T(8,128)S(1)} %get-tuple-element.42), channel_id=1, source_target_pairs={{0,17},{1,16},{2,19},{3,18},{4,21},{5,20},{6,23},{7,22},{8,25},{9,... | collective-permute-start | bytes 245768 | tf_op jit(solution)/shard_map/ppermute | solution.py:337
  29.4 4.8 %collective-permute-start.11 = (f32[160,128]{1,0:T(8,128)S(1)}, f32[160,128]{1,0:T(8,128)S(1)}, u32[]{:S(2)}, u32[]{:S(2)}) collective-permute-start(f32[160,128]{1,0:T(8,128)S(1)} %get-tuple-element.42), channel_id=1, source_target_pairs={{0,16},{1,17},{2,18},{3,19},{4,20},{5,21},{6,22},{7,23},{8,24},{9,... | collective-permute-start | bytes 245768 | tf_op jit(solution)/shard_map/ppermute | solution.py:337
  29.9 4.4 %collective-permute-start.12 = (f32[160,128]{1,0:T(8,128)S(1)}, f32[160,128]{1,0:T(8,128)S(1)}, u32[]{:S(2)}, u32[]{:S(2)}) collective-permute-start(f32[160,128]{1,0:T(8,128)S(1)} %get-tuple-element.41.refs_0_.refs_4_), channel_id=1, source_target_pairs={{0,1},{1,0},{2,3},{3,2},{4,5},{5,4},{6,7},{7,6},{8,9},{9,8},{10,11... | collective-permute-start | bytes 245768 | tf_op jit(solution)/shard_map/ppermute | solution.py:337
  34.4 8.4 %collective-permute-start.14 = (f32[160,128]{1,0:T(8,128)S(1)}, f32[160,128]{1,0:T(8,128)S(1)}, u32[]{:S(2)}, u32[]{:S(2)}) collective-permute-start(f32[160,128]{1,0:T(8,128)S(1)} %shard_map.74.refs_0_), channel_id=1, source_target_pairs={{0,2},{1,3},{2,0},{3,1},{4,6},{5,7},{6,4},{7,5},{8,10},{9,11},{10,... | collective-permute-start | bytes 245768 | tf_op jit(solution)/shard_map/ppermute | solution.py:337
  37.7 8.7 %collective-permute-start.20 = (bf16[128,384]{1,0:T(8,128)(2,1)S(1)}, bf16[128,384]{1,0:T(8,128)(2,1)S(1)}, u32[]{:S(2)}, u32[]{:S(2)}) collective-permute-start(bf16[128,384]{1,0:T(8,128)(2,1)S(1)} %get-tuple-element.46), channel_id=1, source_target_pairs={{0,0},{1,4},{2,8},{3,12},{4,1},{5,5},{6,9},{7,13},{8,2},{9,6},{10,... | collective-permute-start | bytes 294920 | tf_op jit(solution)/shard_map/ppermute | solution.py:395
  38.3 8.1 %collective-permute-start.21 = (bf16[128,384]{1,0:T(8,128)(2,1)S(1)}, bf16[128,384]{1,0:T(8,128)(2,1)S(1)}, u32[]{:S(2)}, u32[]{:S(2)}) collective-permute-start(bf16[128,384]{1,0:T(8,128)(2,1)S(1)} %get-tuple-element.47), channel_id=1, source_target_pairs={{0,2},{1,6},{2,10},{3,14},{4,3},{5,7},{6,11},{7,15},{8,0},{9,4},{1... | collective-permute-start | bytes 294920 | tf_op jit(solution)/shard_map/ppermute | solution.py:395
  42.8 6.6 %collective-permute-start.17 = (f32[160,128]{1,0:T(8,128)S(1)}, f32[160,128]{1,0:T(8,128)S(1)}, u32[]{:S(2)}, u32[]{:S(2)}) collective-permute-start(f32[160,128]{1,0:T(8,128)S(1)} %shard_map.75.refs_0_), channel_id=1, source_target_pairs={{0,24},{1,25},{2,26},{3,27},{4,28},{5,29},{6,30},{7,31},{8,16},{9,... | collective-permute-start | bytes 245768 | tf_op jit(solution)/shard_map/ppermute | solution.py:337
  42.9 6.5 %collective-permute-start.16 = (f32[160,128]{1,0:T(8,128)S(1)}, f32[160,128]{1,0:T(8,128)S(1)}, u32[]{:S(2)}, u32[]{:S(2)}) collective-permute-start(f32[160,128]{1,0:T(8,128)S(1)} %shard_map.75.refs_0_), channel_id=1, source_target_pairs={{0,16},{1,17},{2,18},{3,19},{4,20},{5,21},{6,22},{7,23},{8,24},{9,... | collective-permute-start | bytes 245768 | tf_op jit(solution)/shard_map/ppermute | solution.py:337
  44.5 5.5 %collective-permute-start.15 = (f32[160,128]{1,0:T(8,128)S(1)}, f32[160,128]{1,0:T(8,128)S(1)}, u32[]{:S(2)}, u32[]{:S(2)}) collective-permute-start(f32[160,128]{1,0:T(8,128)S(1)} %shard_map.75.refs_0_), channel_id=1, source_target_pairs={{0,8},{1,9},{2,10},{3,11},{4,12},{5,13},{6,14},{7,15},{8,0},{9,1},... | collective-permute-start | bytes 245768 | tf_op jit(solution)/shard_map/ppermute | solution.py:337
  50.0 1.7 %collective-permute-start.22 = (f32[4,160,128]{2,1,0:T(8,128)S(1)}, f32[4,160,128]{2,1,0:T(8,128)S(1)}, u32[]{:S(2)}, u32[]{:S(2)}) collective-permute-start(f32[4,160,128]{2,1,0:T(8,128)S(1)} %shard_map.78.refs_0_), channel_id=1, source_target_pairs={{0,4},{1,5},{2,6},{3,7},{4,0},{5,1},{6,2},{7,3},{8,12},{9,13},{10,... | collective-permute-start | bytes 983048 | tf_op jit(solution)/shard_map/ppermute | solution.py:337

commit v24 on v23

--- a/solution.py
+++ b/solution.py
@@ -154,15 +154,23 @@
         at += piece.shape[0]
 
 
-def gather_kernel(*refs):
-    blocks, (own_rows, rows, pack) = refs[:4], refs[4:]
+def select_kernel(*refs):
+    blocks, (own_rows, pack) = refs[:4], refs[4:]
+    same = lax.axis_index("pcol") // 2 == lax.axis_index("side")
+
+    @pl.when(same)
+    def _():
+        pack[...] = own_rows[...]
+
+    @pl.when(jnp.logical_not(same))
+    def _():
+        set_rows(blocks, pack)
+
+
+def apply_kernel(own, *refs):
+    blocks, refs, (high, low, rows) = refs[:4], refs[4:-3], refs[-3:]
+    pieces, outs = refs[: len(refs) // 2], refs[len(refs) // 2 :]
     set_rows(blocks, rows)
-    same = lax.axis_index("pcol") // 2 == lax.axis_index("side")
-    pack[...] = jnp.where(same, own_rows[...], rows[...])
-
-
-def apply_kernel(own, rows, *refs):
-    pieces, outs, (high, low) = refs[: len(refs) // 2 - 1], refs[len(refs) // 2 - 1 : -2], refs[-2:]
     at = 0
     for piece, out in zip(pieces, outs):
         lines = slice(at, at + piece.shape[0])
@@ -367,13 +375,13 @@
         [SMEM] + [VMEM] * (6 + len(cuts)),
         quad_weight, own_inverse, got_inverse, *blocks[:4], *pieces,
     )
-    rows, pack = call(
-        gather_kernel, [line_shape] * 2, [VMEM] * 5, *blocks[4:], own_rows, after=far
-    )
+    pack = call(select_kernel, line_shape, [VMEM] * 5, *blocks[4:], own_rows, after=far)
     got_pack = swap(pack, core=1)
     *mine, high, low = call(
-        apply_kernel, [shape((lines, width), f32) for lines in cuts] + [line_shape] * 2, [VMEM] * (2 + len(cuts)),
-        own_product, rows, *far,
+        apply_kernel, [shape((lines, width), f32) for lines in cuts] + [line_shape] * 2, [VMEM] * (5 + len(cuts)),
+        own_product, *blocks[4:], *far,
+        scratch=[pltpu.VMEM((extent, width), bf16)],
+        after=[pack],
     )
     lines = HELD * LANES // 2
     part, half = shape((lines // 2, LANES), f32), shape((lines, LANES), f32)
@@ -394,16 +402,17 @@
             pairs.append((i, (h * 4 + c) * grid + 2 * (s ^ flip) + k))
         return lax.ppermute(x, AXES, pairs)
 
-    total = call(
-        add_four_kernel, part, [VMEM] * 4,
-        keep, swap(send, point=1), swap(keep, column=1), swap(send, point=1, column=1),
-    )
     out_near, out_far = call(
         output_kernel, [block, block], [VMEM] * (2 * len(cuts)), *mine, *other,
         scratch=[pltpu.VMEM((extent, width), bf16)],
         after=[keep],
     )
     near, far = deliver(out_near, 0), deliver(out_far, 1)
+    total = call(
+        add_four_kernel, part, [VMEM] * 4,
+        keep, swap(send, point=1), swap(keep, column=1), swap(send, point=1, column=1),
+        after=[out_near],
+    )
     total = call(add_kernel, part, [VMEM] * 2, total, swap(total, column=2))
     quarters = [total, swap(total, side=1), swap(total, point=1), swap(total, side=1, point=1)]
     rows = call(

time: 53.1 us -> 53.8 us (1.013)
  waiting for transfers between devices: 13.4 us -> 17.4 us
  starting transfers between devices: 31.9 us -> 28.7 us
    ppermute x2, starting transfers between devices: 5.14 us -> 0.72 us  [deliver(): return lax.ppermute(x, AXES, pairs)]
    ppermute x21, waiting for transfers between devices: 13.4 us -> 17.4 us  [swap(): return lax.ppermute(x, AXES, [(i, i ^ mask) for i in range(devices)])]
    ppermute x21, starting transfers between devices: 26.8 us -> 27.9 us  [swap(): return lax.ppermute(x, AXES, [(i, i ^ mask) for i in range(devices)])]
  transfers between devices with their start and end apart: 23 -> 23, of which waited for: 13 -> 15; matrix products, arithmetic and copies ran while one was open for 0% -> 0% of each run, Pallas kernels for 6% -> 6%
where the time goes in v24:
time: 53.8 us; the launch traced here: 53.6 us
  starting transfers between devices  28.7 us (53%)
  waiting for transfers between devices  17.4 us (32%)
  Pallas kernels  6.14 us (11%)
  between operations  1.41 us (3%)
    ppermute x21, starting transfers between devices, swap(): return lax.ppermute(x, AXES, [(i, i ^ mask) for i in range(devices)])  27.9 us
    ppermute x21, waiting for transfers between devices, swap(): return lax.ppermute(x, AXES, [(i, i ^ mask) for i in range(devices)])  17.4 us
    pallas_call x13, Pallas kernels, call(): pl.pallas_call(body, out_shape=outs, in_specs=list(specs) + [ANY] * len(a...  6.14 us
  transfers between devices with their start and end apart: 23, of which 15 were waited for; matrix products, arithmetic and copies ran while one was open for 0% of the time, Pallas kernels for 6%

profile of v24, /device:TPU:0, one launch (start us, length us, event | category | flops | bytes accessed | tf_op | source)
XLA Modules:
  0.0 53.6 jit_solution(1180380058368617434)
XLA Ops:
  0.6 1.7 %shard_map.68 = (bf16[128,384]{1,0:T(8,128)(2,1)S(1)}, bf16[160,384]{1,0:T(8,128)(2,1)S(1)}, bf16[32,384]{1,0:T(8,128)(2,1)S(1)}, s32[2,8,128]{2,1,0:T(8,128)S(1...) custom-call(s32[2]{0:T(128)} %bitcast.1, bf16[1,128,2,384]{3,2,1,0:T(2,128)(2,1)} %refs_1_.1, ...), custom_call_target="tpu_custom_call" | custom-call | tf_op jit(solution)/shard_map/pallas_call | solution.py:28
  2.3 3.0 %collective-permute-start = (bf16[160,384]{1,0:T(8,128)(2,1)S(1)}, bf16[160,384]{1,0:T(8,128)(2,1)S(1)}, u32[]{:S(2)}, u32[]{:S(2)}) collective-permute-start(bf16[160,384]{1,0:T(8,128)(2,1)S(1)} %get-tuple-element.25), channel_id=1, source_target_pairs={{0,8},{1,9},{2,10},{3,11},{4,12},{5,13},{6,14},{7,15},{8,0},{9,1},... | collective-permute-start | bytes 368648 | tf_op jit(solution)/shard_map/ppermute | solution.py:345
  5.4 1.9 %collective-permute-start.8 = (bf16[256,512]{1,0:T(8,128)(2,1)S(1)}, bf16[256,512]{1,0:T(8,128)(2,1)S(1)}, u32[]{:S(2)}, u32[]{:S(2)}) collective-permute-start(bf16[256,512]{1,0:T(8,128)(2,1)S(1)} %get-tuple-element.28.refs_8_), channel_id=1, source_target_pairs={{0,8},{1,9},{2,10},{3,11},{4,12},{5,13},{6,14},{7,15},{8,0},{9,1},... | collective-permute-start | bytes 786440 | tf_op jit(solution)/shard_map/ppermute | solution.py:345
  7.4 2.6 %collective-permute-start.1 = (bf16[128,384]{1,0:T(8,128)(2,1)S(1)}, bf16[128,384]{1,0:T(8,128)(2,1)S(1)}, u32[]{:S(2)}, u32[]{:S(2)}) collective-permute-start(bf16[128,384]{1,0:T(8,128)(2,1)S(1)} %get-tuple-element.26.refs_3_), channel_id=1, source_target_pairs={{0,2},{1,3},{2,0},{3,1},{4,6},{5,7},{6,4},{7,5},{8,10},{9,11},{10,... | collective-permute-start | bytes 294920 | tf_op jit(solution)/shard_map/ppermute | solution.py:345
  10.0 1.6 %collective-permute-start.2 = (bf16[128,384]{1,0:T(8,128)(2,1)S(1)}, bf16[128,384]{1,0:T(8,128)(2,1)S(1)}, u32[]{:S(2)}, u32[]{:S(2)}) collective-permute-start(bf16[128,384]{1,0:T(8,128)(2,1)S(1)} %get-tuple-element.26.refs_3_), channel_id=1, source_target_pairs={{0,1},{1,0},{2,3},{3,2},{4,5},{5,4},{6,7},{7,6},{8,9},{9,8},{10,11... | collective-permute-start | bytes 294920 | tf_op jit(solution)/shard_map/ppermute | solution.py:345
  11.6 1.2 %collective-permute-start.4 = (bf16[128,384]{1,0:T(8,128)(2,1)S(1)}, bf16[128,384]{1,0:T(8,128)(2,1)S(1)}, u32[]{:S(2)}, u32[]{:S(2)}) collective-permute-start(bf16[128,384]{1,0:T(8,128)(2,1)S(1)} %slice.9.refs_0_.refs_1_), channel_id=1, source_target_pairs={{0,2},{1,3},{2,0},{3,1},{4,6},{5,7},{6,4},{7,5},{8,10},{9,11},{10,... | collective-permute-start | bytes 294920 | tf_op jit(solution)/shard_map/ppermute | solution.py:345
  13.1 3.8 %collective-permute-start.3 = (bf16[128,384]{1,0:T(8,128)(2,1)S(1)}, bf16[128,384]{1,0:T(8,128)(2,1)S(1)}, u32[]{:S(2)}, u32[]{:S(2)}) collective-permute-start(bf16[128,384]{1,0:T(8,128)(2,1)S(1)} %collective-permute-done.1.refs_4_), channel_id=1, source_target_pairs={{0,1},{1,0},{2,3},{3,2},{4,5},{5,4},{6,7},{7,6},{8,9},{9,8},{10,11... | collective-permute-start | bytes 294920 | tf_op jit(solution)/shard_map/ppermute | solution.py:345
  17.0 0.7 %collective-permute-start.5 = (bf16[128,384]{1,0:T(8,128)(2,1)S(1)}, bf16[128,384]{1,0:T(8,128)(2,1)S(1)}, u32[]{:S(2)}, u32[]{:S(2)}) collective-permute-start(bf16[128,384]{1,0:T(8,128)(2,1)S(1)} %slice.9.refs_0_.refs_1_), channel_id=1, source_target_pairs={{0,1},{1,0},{2,3},{3,2},{4,5},{5,4},{6,7},{7,6},{8,9},{9,8},{10,11... | collective-permute-start | bytes 294920 | tf_op jit(solution)/shard_map/ppermute | solution.py:345
  17.7 0.6 %collective-permute-done.4.refs_1_.refs_2_ = bf16[128,384]{1,0:T(8,128)(2,1)S(1)} collective-permute-done((bf16[128,384]{1,0:T(8,128)(2,1)S(1)}, bf16[128,384]{1,0:T(8,128)(2,1)S(1)}, u32[]{:S(2)}, u32[]{:S(2)}) %collective-permute-start.4) | collective-permute-done | bytes 98336 | tf_op jit(solution)/shard_map/ppermute | solution.py:345
  18.3 0.7 %collective-permute-start.6 = (bf16[128,384]{1,0:T(8,128)(2,1)S(1)}, bf16[128,384]{1,0:T(8,128)(2,1)S(1)}, u32[]{:S(2)}, u32[]{:S(2)}) collective-permute-start(bf16[128,384]{1,0:T(8,128)(2,1)S(1)} %collective-permute-done.4.refs_1_.refs_2_), channel_id=1, source_target_pairs={{0,1},{1,0},{2,3},{3,2},{4,5},{5,4},{6,7},{7,6},{8,9},{9,8},{10,11... | collective-permute-start | bytes 294920 | tf_op jit(solution)/shard_map/ppermute | solution.py:345
  19.7 1.0 %collective-permute-done.3.refs_6_ = bf16[128,384]{1,0:T(8,128)(2,1)S(1)} collective-permute-done((bf16[128,384]{1,0:T(8,128)(2,1)S(1)}, bf16[128,384]{1,0:T(8,128)(2,1)S(1)}, u32[]{:S(2)}, u32[]{:S(2)}) %collective-permute-start.3) | collective-permute-done | bytes 98336 | tf_op jit(solution)/shard_map/ppermute | solution.py:345
  20.7 0.6 %shard_map.69 = (bf16[512,384]{1,0:T(8,128)(2,1)S(1)}, f32[512,384]{1,0:T(8,128)S(1)}, f32[8,128]{1,0:T(8,128)S(1)}, f32[384,384]{1,0:T(8,128)S(1)}) custom-call(f32[1]{0:T(128)S(6)} %copy.9.refs_0_, bf16[32,384]{1,0:T(8,128)(2,1)S(1)} %get-tuple-element.24.refs_1_, bf16[32,384]{1,0:T(8,128)(2,1)S(1)} %slice.8.refs_2_, ...), custom_call_target="tpu_custom_call" | custom-call | tf_op jit(solution)/shard_map/pallas_call | solution.py:28
  21.3 0.7 %collective-permute-done.5.refs_2_.refs_3_ = bf16[128,384]{1,0:T(8,128)(2,1)S(1)} collective-permute-done((bf16[128,384]{1,0:T(8,128)(2,1)S(1)}, bf16[128,384]{1,0:T(8,128)(2,1)S(1)}, u32[]{:S(2)}, u32[]{:S(2)}) %collective-permute-start.5) | collective-permute-done | bytes 98336 | tf_op jit(solution)/shard_map/ppermute | solution.py:345
  22.0 1.0 %collective-permute-done.6.refs_3_.refs_4_ = bf16[128,384]{1,0:T(8,128)(2,1)S(1)} collective-permute-done((bf16[128,384]{1,0:T(8,128)(2,1)S(1)}, bf16[128,384]{1,0:T(8,128)(2,1)S(1)}, u32[]{:S(2)}, u32[]{:S(2)}) %collective-permute-start.6) | collective-permute-done | bytes 98336 | tf_op jit(solution)/shard_map/ppermute | solution.py:345
  24.3 0.6 %collective-permute-done.9.refs_1_ = bf16[512,384]{1,0:T(8,128)(2,1)S(1)} collective-permute-done((bf16[512,384]{1,0:T(8,128)(2,1)S(1)}, bf16[512,384]{1,0:T(8,128)(2,1)S(1)}, u32[]{:S(2)}, u32[]{:S(2)}) %collective-permute-start.9) | collective-permute-done | bytes 393248 | tf_op jit(solution)/shard_map/ppermute | solution.py:345
  24.8 0.6 %shard_map.72 = (f32[320,128]{1,0:T(8,128)S(1)}, f32[320,128]{1,0:T(8,128)S(1)}) custom-call(bf16[512,384]{1,0:T(8,128)(2,1)S(1)} %shard_map.70.refs_7_.refs_0_, bf16[512,384]{1,0:T(8,128)(2,1)S(1)} %collective-permute-done.9.refs_1_, bf16[512,384]{1,0:T(8,128)(2,1)S(1)} %get-tuple-element.32.refs_2_, bf16[512,384]{1,0:T(8,128)(2,1)S(1)} %get-tuple-element.33.refs_3_, ...), custom_call_target="tpu_custom_call" | custom-call | tf_op jit(solution)/shard_map/pallas_call | solution.py:28
  25.6 1.3 %collective-permute-done.10.refs_2_ = f32[320,128]{1,0:T(8,128)S(1)} collective-permute-done((f32[320,128]{1,0:T(8,128)S(1)}, f32[320,128]{1,0:T(8,128)S(1)}, u32[]{:S(2)}, u32[]{:S(2)}) %collective-permute-start.10) | collective-permute-done | bytes 163872 | tf_op jit(solution)/shard_map/ppermute | solution.py:345
  26.9 2.4 %collective-permute-start.13 = (f32[160,128]{1,0:T(8,128)S(1)}, f32[160,128]{1,0:T(8,128)S(1)}, u32[]{:S(2)}, u32[]{:S(2)}) collective-permute-start(f32[160,128]{1,0:T(8,128)S(1)} %get-tuple-element.38), channel_id=1, source_target_pairs={{0,17},{1,16},{2,19},{3,18},{4,21},{5,20},{6,23},{7,22},{8,25},{9,... | collective-permute-start | bytes 245768 | tf_op jit(solution)/shard_map/ppermute | solution.py:345
  29.9 0.6 %collective-permute-start.12 = (f32[160,128]{1,0:T(8,128)S(1)}, f32[160,128]{1,0:T(8,128)S(1)}, u32[]{:S(2)}, u32[]{:S(2)}) collective-permute-start(f32[160,128]{1,0:T(8,128)S(1)} %get-tuple-element.37.refs_4_.refs_0_), channel_id=1, source_target_pairs={{0,1},{1,0},{2,3},{3,2},{4,5},{5,4},{6,7},{7,6},{8,9},{9,8},{10,11... | collective-permute-start | bytes 245768 | tf_op jit(solution)/shard_map/ppermute | solution.py:345
  30.6 1.8 %collective-permute-done.13.refs_3_ = f32[160,128]{1,0:T(8,128)S(1)} collective-permute-done((f32[160,128]{1,0:T(8,128)S(1)}, f32[160,128]{1,0:T(8,128)S(1)}, u32[]{:S(2)}, u32[]{:S(2)}) %collective-permute-start.13) | collective-permute-done | bytes 81952 | tf_op jit(solution)/shard_map/ppermute | solution.py:345
  32.4 1.7 %collective-permute-done.11.refs_1_ = f32[160,128]{1,0:T(8,128)S(1)} collective-permute-done((f32[160,128]{1,0:T(8,128)S(1)}, f32[160,128]{1,0:T(8,128)S(1)}, u32[]{:S(2)}, u32[]{:S(2)}) %collective-permute-start.11) | collective-permute-done | bytes 81952 | tf_op jit(solution)/shard_map/ppermute | solution.py:345
  34.3 3.1 %collective-permute-start.16 = (f32[160,128]{1,0:T(8,128)S(1)}, f32[160,128]{1,0:T(8,128)S(1)}, u32[]{:S(2)}, u32[]{:S(2)}) collective-permute-start(f32[160,128]{1,0:T(8,128)S(1)} %shard_map.75.refs_0_), channel_id=1, source_target_pairs={{0,2},{1,3},{2,0},{3,1},{4,6},{5,7},{6,4},{7,5},{8,10},{9,11},{10,... | collective-permute-start | bytes 245768 | tf_op jit(solution)/shard_map/ppermute | solution.py:345
  37.5 0.7 %collective-permute-start.20 = (bf16[128,384]{1,0:T(8,128)(2,1)S(1)}, bf16[128,384]{1,0:T(8,128)(2,1)S(1)}, u32[]{:S(2)}, u32[]{:S(2)}) collective-permute-start(bf16[128,384]{1,0:T(8,128)(2,1)S(1)} %get-tuple-element.41.refs_4_), channel_id=1, source_target_pairs={{0,0},{1,4},{2,8},{3,12},{4,1},{5,5},{6,9},{7,13},{8,2},{9,6},{10,... | collective-permute-start | bytes 294920 | tf_op jit(solution)/shard_map/ppermute | solution.py:403
  38.2 3.4 %collective-permute-done.16.refs_1_ = f32[160,128]{1,0:T(8,128)S(1)} collective-permute-done((f32[160,128]{1,0:T(8,128)S(1)}, f32[160,128]{1,0:T(8,128)S(1)}, u32[]{:S(2)}, u32[]{:S(2)}) %collective-permute-start.16) | collective-permute-done | bytes 81952 | tf_op jit(solution)/shard_map/ppermute | solution.py:345
  41.6 3.8 %collective-permute-start.19 = (f32[160,128]{1,0:T(8,128)S(1)}, f32[160,128]{1,0:T(8,128)S(1)}, u32[]{:S(2)}, u32[]{:S(2)}) collective-permute-start(f32[160,128]{1,0:T(8,128)S(1)} %shard_map.76.refs_0_), channel_id=1, source_target_pairs={{0,24},{1,25},{2,26},{3,27},{4,28},{5,29},{6,30},{7,31},{8,16},{9,... | collective-permute-start | bytes 245768 | tf_op jit(solution)/shard_map/ppermute | solution.py:345
  45.5 0.8 %collective-permute-start.18 = (f32[160,128]{1,0:T(8,128)S(1)}, f32[160,128]{1,0:T(8,128)S(1)}, u32[]{:S(2)}, u32[]{:S(2)}) collective-permute-start(f32[160,128]{1,0:T(8,128)S(1)} %shard_map.76.refs_0_), channel_id=1, source_target_pairs={{0,16},{1,17},{2,18},{3,19},{4,20},{5,21},{6,22},{7,23},{8,24},{9,... | collective-permute-start | bytes 245768 | tf_op jit(solution)/shard_map/ppermute | solution.py:345
  46.6 2.1 %collective-permute-done.19.refs_3_ = f32[160,128]{1,0:T(8,128)S(1)} collective-permute-done((f32[160,128]{1,0:T(8,128)S(1)}, f32[160,128]{1,0:T(8,128)S(1)}, u32[]{:S(2)}, u32[]{:S(2)}) %collective-permute-start.19) | collective-permute-done | bytes 81952 | tf_op jit(solution)/shard_map/ppermute | solution.py:345
  48.7 1.2 %collective-permute-done.18.refs_2_ = f32[160,128]{1,0:T(8,128)S(1)} collective-permute-done((f32[160,128]{1,0:T(8,128)S(1)}, f32[160,128]{1,0:T(8,128)S(1)}, u32[]{:S(2)}, u32[]{:S(2)}) %collective-permute-start.18) | collective-permute-done | bytes 81952 | tf_op jit(solution)/shard_map/ppermute | solution.py:345
  49.9 0.8 %collective-permute-done.17.refs_1_ = f32[160,128]{1,0:T(8,128)S(1)} collective-permute-done((f32[160,128]{1,0:T(8,128)S(1)}, f32[160,128]{1,0:T(8,128)S(1)}, u32[]{:S(2)}, u32[]{:S(2)}) %collective-permute-start.17) | collective-permute-done | bytes 81952 | tf_op jit(solution)/shard_map/ppermute | solution.py:345
  50.9 1.0 %shard_map.79 = (bf16[1,128,2,384]{3,2,1,0:T(2,128)(2,1)}, f32[2,384,384]{2,1,0:T(8,128)}) custom-call(f32[4,160,128]{2,1,0:T(8,128)S(1)} %shard_map.78.refs_0_, bf16[1,128,2,384]{3,2,1,0:T(2,128)(2,1)S(1)} %shard_map.77.refs_4_.refs_1_), custom_call_target="tpu_custom_call" | custom-call | tf_op jit(solution)/shard_map/pallas_call | solution.py:28
  51.9 0.6 %collective-permute-done.22.refs_1_ = f32[4,160,128]{2,1,0:T(8,128)S(1)} collective-permute-done((f32[4,160,128]{2,1,0:T(8,128)S(1)}, f32[4,160,128]{2,1,0:T(8,128)S(1)}, u32[]{:S(2)}, u32[]{:S(2)}) %collective-permute-start.22) | collective-permute-done | bytes 327712 | tf_op jit(solution)/shard_map/ppermute | solution.py:345
  52.5 1.2 %shard_map.80 = f32[2,384,384]{2,1,0:T(8,128)} custom-call(f32[4,160,128]{2,1,0:T(8,128)S(1)} %shard_map.78.refs_0_, f32[4,160,128]{2,1,0:T(8,128)S(1)} %collective-permute-done.22.refs_1_, f32[2,384,384]{2,1,0:T(8,128)} %get-tuple-element.45.refs_2_), custom_call_target="tpu_custom_call", output_to_operand_aliasing={{}: (2, {})} | custom-call | tf_op jit(solution)/shard_map/pallas_call | solution.py:28
  (29 shorter events, 3.2 us)
Async XLA Ops:
  2.3 9.2 %collective-permute-start = (bf16[160,384]{1,0:T(8,128)(2,1)S(1)}, bf16[160,384]{1,0:T(8,128)(2,1)S(1)}, u32[]{:S(2)}, u32[]{:S(2)}) collective-permute-start(bf16[160,384]{1,0:T(8,128)(2,1)S(1)} %get-tuple-element.25), channel_id=1, source_target_pairs={{0,8},{1,9},{2,10},{3,11},{4,12},{5,13},{6,14},{7,15},{8,0},{9,1},... | collective-permute-start | bytes 368648 | tf_op jit(solution)/shard_map/ppermute | solution.py:345
  5.3 16.6 %collective-permute-start.7 = (bf16[256,512]{1,0:T(8,128)(2,1)S(1)}, bf16[256,512]{1,0:T(8,128)(2,1)S(1)}, u32[]{:S(2)}, u32[]{:S(2)}) collective-permute-start(bf16[256,512]{1,0:T(8,128)(2,1)S(1)} %get-tuple-element.27.refs_7_), channel_id=1, source_target_pairs={{0,8},{1,9},{2,10},{3,11},{4,12},{5,13},{6,14},{7,15},{8,0},{9,1},... | collective-permute-start | bytes 786440 | tf_op jit(solution)/shard_map/ppermute | solution.py:345
  5.4 16.5 %collective-permute-start.8 = (bf16[256,512]{1,0:T(8,128)(2,1)S(1)}, bf16[256,512]{1,0:T(8,128)(2,1)S(1)}, u32[]{:S(2)}, u32[]{:S(2)}) collective-permute-start(bf16[256,512]{1,0:T(8,128)(2,1)S(1)} %get-tuple-element.28.refs_8_), channel_id=1, source_target_pairs={{0,8},{1,9},{2,10},{3,11},{4,12},{5,13},{6,14},{7,15},{8,0},{9,1},... | collective-permute-start | bytes 786440 | tf_op jit(solution)/shard_map/ppermute | solution.py:345
  7.4 5.8 %collective-permute-start.1 = (bf16[128,384]{1,0:T(8,128)(2,1)S(1)}, bf16[128,384]{1,0:T(8,128)(2,1)S(1)}, u32[]{:S(2)}, u32[]{:S(2)}) collective-permute-start(bf16[128,384]{1,0:T(8,128)(2,1)S(1)} %get-tuple-element.26.refs_3_), channel_id=1, source_target_pairs={{0,2},{1,3},{2,0},{3,1},{4,6},{5,7},{6,4},{7,5},{8,10},{9,11},{10,... | collective-permute-start | bytes 294920 | tf_op jit(solution)/shard_map/ppermute | solution.py:345
  10.0 7.0 %collective-permute-start.2 = (bf16[128,384]{1,0:T(8,128)(2,1)S(1)}, bf16[128,384]{1,0:T(8,128)(2,1)S(1)}, u32[]{:S(2)}, u32[]{:S(2)}) collective-permute-start(bf16[128,384]{1,0:T(8,128)(2,1)S(1)} %get-tuple-element.26.refs_3_), channel_id=1, source_target_pairs={{0,1},{1,0},{2,3},{3,2},{4,5},{5,4},{6,7},{7,6},{8,9},{9,8},{10,11... | collective-permute-start | bytes 294920 | tf_op jit(solution)/shard_map/ppermute | solution.py:345
  11.6 6.8 %collective-permute-start.4 = (bf16[128,384]{1,0:T(8,128)(2,1)S(1)}, bf16[128,384]{1,0:T(8,128)(2,1)S(1)}, u32[]{:S(2)}, u32[]{:S(2)}) collective-permute-start(bf16[128,384]{1,0:T(8,128)(2,1)S(1)} %slice.9.refs_0_.refs_1_), channel_id=1, source_target_pairs={{0,2},{1,3},{2,0},{3,1},{4,6},{5,7},{6,4},{7,5},{8,10},{9,11},{10,... | collective-permute-start | bytes 294920 | tf_op jit(solution)/shard_map/ppermute | solution.py:345
  13.1 7.6 %collective-permute-start.3 = (bf16[128,384]{1,0:T(8,128)(2,1)S(1)}, bf16[128,384]{1,0:T(8,128)(2,1)S(1)}, u32[]{:S(2)}, u32[]{:S(2)}) collective-permute-start(bf16[128,384]{1,0:T(8,128)(2,1)S(1)} %collective-permute-done.1.refs_4_), channel_id=1, source_target_pairs={{0,1},{1,0},{2,3},{3,2},{4,5},{5,4},{6,7},{7,6},{8,9},{9,8},{10,11... | collective-permute-start | bytes 294920 | tf_op jit(solution)/shard_map/ppermute | solution.py:345
  17.0 5.0 %collective-permute-start.5 = (bf16[128,384]{1,0:T(8,128)(2,1)S(1)}, bf16[128,384]{1,0:T(8,128)(2,1)S(1)}, u32[]{:S(2)}, u32[]{:S(2)}) collective-permute-start(bf16[128,384]{1,0:T(8,128)(2,1)S(1)} %slice.9.refs_0_.refs_1_), channel_id=1, source_target_pairs={{0,1},{1,0},{2,3},{3,2},{4,5},{5,4},{6,7},{7,6},{8,9},{9,8},{10,11... | collective-permute-start | bytes 294920 | tf_op jit(solution)/shard_map/ppermute | solution.py:345
  18.3 4.7 %collective-permute-start.6 = (bf16[128,384]{1,0:T(8,128)(2,1)S(1)}, bf16[128,384]{1,0:T(8,128)(2,1)S(1)}, u32[]{:S(2)}, u32[]{:S(2)}) collective-permute-start(bf16[128,384]{1,0:T(8,128)(2,1)S(1)} %collective-permute-done.4.refs_1_.refs_2_), channel_id=1, source_target_pairs={{0,1},{1,0},{2,3},{3,2},{4,5},{5,4},{6,7},{7,6},{8,9},{9,8},{10,11... | collective-permute-start | bytes 294920 | tf_op jit(solution)/shard_map/ppermute | solution.py:345
  23.0 1.8 %collective-permute-start.9 = (bf16[512,384]{1,0:T(8,128)(2,1)S(1)}, bf16[512,384]{1,0:T(8,128)(2,1)S(1)}, u32[]{:S(2)}, u32[]{:S(2)}) collective-permute-start(bf16[512,384]{1,0:T(8,128)(2,1)S(1)} %shard_map.70.refs_7_.refs_0_), channel_id=1, source_target_pairs={{0,4},{1,5},{2,6},{3,7},{4,0},{5,1},{6,2},{7,3},{8,12},{9,13},{10,... | collective-permute-start | bytes 1179656 | tf_op jit(solution)/shard_map/ppermute | solution.py:345
  23.6 6.8 %collective-permute-start.14 = (f32[256,384]{1,0:T(8,128)S(1)}, f32[256,384]{1,0:T(8,128)S(1)}, u32[]{:S(2)}, u32[]{:S(2)}) collective-permute-start(f32[256,384]{1,0:T(8,128)S(1)} %get-tuple-element.39.refs_0_), channel_id=1, source_target_pairs={{0,4},{1,5},{2,6},{3,7},{4,0},{5,1},{6,2},{7,3},{8,12},{9,13},{10,... | collective-permute-start | bytes 1179656 | tf_op jit(solution)/shard_map/ppermute | solution.py:345
  24.2 6.3 %collective-permute-start.15 = (f32[256,384]{1,0:T(8,128)S(1)}, f32[256,384]{1,0:T(8,128)S(1)}, u32[]{:S(2)}, u32[]{:S(2)}) collective-permute-start(f32[256,384]{1,0:T(8,128)S(1)} %get-tuple-element.40.refs_1_), channel_id=1, source_target_pairs={{0,4},{1,5},{2,6},{3,7},{4,0},{5,1},{6,2},{7,3},{8,12},{9,13},{10,... | collective-permute-start | bytes 1179656 | tf_op jit(solution)/shard_map/ppermute | solution.py:345
  25.4 1.4 %collective-permute-start.10 = (f32[320,128]{1,0:T(8,128)S(1)}, f32[320,128]{1,0:T(8,128)S(1)}, u32[]{:S(2)}, u32[]{:S(2)}) collective-permute-start(f32[320,128]{1,0:T(8,128)S(1)} %get-tuple-element.36), channel_id=1, source_target_pairs={{0,4},{1,5},{2,6},{3,7},{4,0},{5,1},{6,2},{7,3},{8,12},{9,13},{10,... | collective-permute-start | bytes 491528 | tf_op jit(solution)/shard_map/ppermute | solution.py:345
  26.9 5.5 %collective-permute-start.13 = (f32[160,128]{1,0:T(8,128)S(1)}, f32[160,128]{1,0:T(8,128)S(1)}, u32[]{:S(2)}, u32[]{:S(2)}) collective-permute-start(f32[160,128]{1,0:T(8,128)S(1)} %get-tuple-element.38), channel_id=1, source_target_pairs={{0,17},{1,16},{2,19},{3,18},{4,21},{5,20},{6,23},{7,22},{8,25},{9,... | collective-permute-start | bytes 245768 | tf_op jit(solution)/shard_map/ppermute | solution.py:345
  29.3 4.8 %collective-permute-start.11 = (f32[160,128]{1,0:T(8,128)S(1)}, f32[160,128]{1,0:T(8,128)S(1)}, u32[]{:S(2)}, u32[]{:S(2)}) collective-permute-start(f32[160,128]{1,0:T(8,128)S(1)} %get-tuple-element.38), channel_id=1, source_target_pairs={{0,16},{1,17},{2,18},{3,19},{4,20},{5,21},{6,22},{7,23},{8,24},{9,... | collective-permute-start | bytes 245768 | tf_op jit(solution)/shard_map/ppermute | solution.py:345
  29.9 4.4 %collective-permute-start.12 = (f32[160,128]{1,0:T(8,128)S(1)}, f32[160,128]{1,0:T(8,128)S(1)}, u32[]{:S(2)}, u32[]{:S(2)}) collective-permute-start(f32[160,128]{1,0:T(8,128)S(1)} %get-tuple-element.37.refs_4_.refs_0_), channel_id=1, source_target_pairs={{0,1},{1,0},{2,3},{3,2},{4,5},{5,4},{6,7},{7,6},{8,9},{9,8},{10,11... | collective-permute-start | bytes 245768 | tf_op jit(solution)/shard_map/ppermute | solution.py:345
  34.3 7.3 %collective-permute-start.16 = (f32[160,128]{1,0:T(8,128)S(1)}, f32[160,128]{1,0:T(8,128)S(1)}, u32[]{:S(2)}, u32[]{:S(2)}) collective-permute-start(f32[160,128]{1,0:T(8,128)S(1)} %shard_map.75.refs_0_), channel_id=1, source_target_pairs={{0,2},{1,3},{2,0},{3,1},{4,6},{5,7},{6,4},{7,5},{8,10},{9,11},{10,... | collective-permute-start | bytes 245768 | tf_op jit(solution)/shard_map/ppermute | solution.py:345
  37.5 8.9 %collective-permute-start.21 = (bf16[128,384]{1,0:T(8,128)(2,1)S(1)}, bf16[128,384]{1,0:T(8,128)(2,1)S(1)}, u32[]{:S(2)}, u32[]{:S(2)}) collective-permute-start(bf16[128,384]{1,0:T(8,128)(2,1)S(1)} %get-tuple-element.43), channel_id=1, source_target_pairs={{0,2},{1,6},{2,10},{3,14},{4,3},{5,7},{6,11},{7,15},{8,0},{9,4},{1... | collective-permute-start | bytes 294920 | tf_op jit(solution)/shard_map/ppermute | solution.py:403
  37.5 8.8 %collective-permute-start.20 = (bf16[128,384]{1,0:T(8,128)(2,1)S(1)}, bf16[128,384]{1,0:T(8,128)(2,1)S(1)}, u32[]{:S(2)}, u32[]{:S(2)}) collective-permute-start(bf16[128,384]{1,0:T(8,128)(2,1)S(1)} %get-tuple-element.41.refs_4_), channel_id=1, source_target_pairs={{0,0},{1,4},{2,8},{3,12},{4,1},{5,5},{6,9},{7,13},{8,2},{9,6},{10,... | collective-permute-start | bytes 294920 | tf_op jit(solution)/shard_map/ppermute | solution.py:403
  41.6 7.1 %collective-permute-start.19 = (f32[160,128]{1,0:T(8,128)S(1)}, f32[160,128]{1,0:T(8,128)S(1)}, u32[]{:S(2)}, u32[]{:S(2)}) collective-permute-start(f32[160,128]{1,0:T(8,128)S(1)} %shard_map.76.refs_0_), channel_id=1, source_target_pairs={{0,24},{1,25},{2,26},{3,27},{4,28},{5,29},{6,30},{7,31},{8,16},{9,... | collective-permute-start | bytes 245768 | tf_op jit(solution)/shard_map/ppermute | solution.py:345
  45.5 4.4 %collective-permute-start.18 = (f32[160,128]{1,0:T(8,128)S(1)}, f32[160,128]{1,0:T(8,128)S(1)}, u32[]{:S(2)}, u32[]{:S(2)}) collective-permute-start(f32[160,128]{1,0:T(8,128)S(1)} %shard_map.76.refs_0_), channel_id=1, source_target_pairs={{0,16},{1,17},{2,18},{3,19},{4,20},{5,21},{6,22},{7,23},{8,24},{9,... | collective-permute-start | bytes 245768 | tf_op jit(solution)/shard_map/ppermute | solution.py:345
  46.3 4.4 %collective-permute-start.17 = (f32[160,128]{1,0:T(8,128)S(1)}, f32[160,128]{1,0:T(8,128)S(1)}, u32[]{:S(2)}, u32[]{:S(2)}) collective-permute-start(f32[160,128]{1,0:T(8,128)S(1)} %shard_map.76.refs_0_), channel_id=1, source_target_pairs={{0,8},{1,9},{2,10},{3,11},{4,12},{5,13},{6,14},{7,15},{8,0},{9,1},... | collective-permute-start | bytes 245768 | tf_op jit(solution)/shard_map/ppermute | solution.py:345
  50.8 1.7 %collective-permute-start.22 = (f32[4,160,128]{2,1,0:T(8,128)S(1)}, f32[4,160,128]{2,1,0:T(8,128)S(1)}, u32[]{:S(2)}, u32[]{:S(2)}) collective-permute-start(f32[4,160,128]{2,1,0:T(8,128)S(1)} %shard_map.78.refs_0_), channel_id=1, source_target_pairs={{0,4},{1,5},{2,6},{3,7},{4,0},{5,1},{6,2},{7,3},{8,12},{9,13},{10,... | collective-permute-start | bytes 983048 | tf_op jit(solution)/shard_map/ppermute | solution.py:345

commit v25 on v24

--- a/solution.py
+++ b/solution.py
@@ -402,17 +402,16 @@
             pairs.append((i, (h * 4 + c) * grid + 2 * (s ^ flip) + k))
         return lax.ppermute(x, AXES, pairs)
 
+    total = call(
+        add_four_kernel, part, [VMEM] * 4,
+        keep, swap(send, point=1), swap(keep, column=1), swap(send, point=1, column=1),
+    )
     out_near, out_far = call(
         output_kernel, [block, block], [VMEM] * (2 * len(cuts)), *mine, *other,
         scratch=[pltpu.VMEM((extent, width), bf16)],
         after=[keep],
     )
     near, far = deliver(out_near, 0), deliver(out_far, 1)
-    total = call(
-        add_four_kernel, part, [VMEM] * 4,
-        keep, swap(send, point=1), swap(keep, column=1), swap(send, point=1, column=1),
-        after=[out_near],
-    )
     total = call(add_kernel, part, [VMEM] * 2, total, swap(total, column=2))
     quarters = [total, swap(total, side=1), swap(total, point=1), swap(total, side=1, point=1)]
     rows = call(

time: 53.8 us -> 53 us (0.985)
  waiting for transfers between devices: 17.4 us -> 13.3 us
  starting transfers between devices: 28.7 us -> 31.9 us
    ppermute x2, starting transfers between devices: 0.72 us -> 5.14 us  [deliver(): return lax.ppermute(x, AXES, pairs)]
    ppermute x21, waiting for transfers between devices: 17.4 us -> 13.3 us  [swap(): return lax.ppermute(x, AXES, [(i, i ^ mask) for i in range(devices)])]
    ppermute x21, starting transfers between devices: 27.9 us -> 26.8 us  [swap(): return lax.ppermute(x, AXES, [(i, i ^ mask) for i in range(devices)])]
  transfers between devices with their start and end apart: 23 -> 23, of which waited for: 15 -> 13; matrix products, arithmetic and copies ran while one was open for 0% -> 0% of each run, Pallas kernels for 6% -> 6%
where the time goes in v25:
time: 53 us; the launch traced here: 52.8 us
  starting transfers between devices  31.9 us (60%)
  waiting for transfers between devices  13.3 us (25%)
  Pallas kernels  6.14 us (12%)
  between operations  1.41 us (3%)
    ppermute x21, starting transfers between devices, swap(): return lax.ppermute(x, AXES, [(i, i ^ mask) for i in range(devices)])  26.8 us
    ppermute x21, waiting for transfers between devices, swap(): return lax.ppermute(x, AXES, [(i, i ^ mask) for i in range(devices)])  13.3 us
    pallas_call x13, Pallas kernels, call(): pl.pallas_call(body, out_shape=outs, in_specs=list(specs) + [ANY] * len(a...  6.14 us
    ppermute x2, starting transfers between devices, deliver(): return lax.ppermute(x, AXES, pairs)  5.14 us
  transfers between devices with their start and end apart: 23, of which 13 were waited for; matrix products, arithmetic and copies ran while one was open for 0% of the time, Pallas kernels for 6%

profile of v25, /device:TPU:0, one launch (start us, length us, event | category | flops | bytes accessed | tf_op | source)
XLA Modules:
  0.0 52.8 jit_solution(16598763710072688374)
XLA Ops:
  0.6 1.7 %shard_map.68 = (bf16[128,384]{1,0:T(8,128)(2,1)S(1)}, bf16[160,384]{1,0:T(8,128)(2,1)S(1)}, bf16[32,384]{1,0:T(8,128)(2,1)S(1)}, s32[2,8,128]{2,1,0:T(8,128)S(1...) custom-call(s32[2]{0:T(128)} %bitcast.1, bf16[1,128,2,384]{3,2,1,0:T(2,128)(2,1)} %refs_1_.1, ...), custom_call_target="tpu_custom_call" | custom-call | tf_op jit(solution)/shard_map/pallas_call | solution.py:28
  2.3 3.0 %collective-permute-start = (bf16[160,384]{1,0:T(8,128)(2,1)S(1)}, bf16[160,384]{1,0:T(8,128)(2,1)S(1)}, u32[]{:S(2)}, u32[]{:S(2)}) collective-permute-start(bf16[160,384]{1,0:T(8,128)(2,1)S(1)} %get-tuple-element.25), channel_id=1, source_target_pairs={{0,8},{1,9},{2,10},{3,11},{4,12},{5,13},{6,14},{7,15},{8,0},{9,1},... | collective-permute-start | bytes 368648 | tf_op jit(solution)/shard_map/ppermute | solution.py:345
  5.4 1.9 %collective-permute-start.8 = (bf16[256,512]{1,0:T(8,128)(2,1)S(1)}, bf16[256,512]{1,0:T(8,128)(2,1)S(1)}, u32[]{:S(2)}, u32[]{:S(2)}) collective-permute-start(bf16[256,512]{1,0:T(8,128)(2,1)S(1)} %get-tuple-element.28.refs_8_), channel_id=1, source_target_pairs={{0,8},{1,9},{2,10},{3,11},{4,12},{5,13},{6,14},{7,15},{8,0},{9,1},... | collective-permute-start | bytes 786440 | tf_op jit(solution)/shard_map/ppermute | solution.py:345
  7.4 2.6 %collective-permute-start.1 = (bf16[128,384]{1,0:T(8,128)(2,1)S(1)}, bf16[128,384]{1,0:T(8,128)(2,1)S(1)}, u32[]{:S(2)}, u32[]{:S(2)}) collective-permute-start(bf16[128,384]{1,0:T(8,128)(2,1)S(1)} %get-tuple-element.26.refs_3_), channel_id=1, source_target_pairs={{0,2},{1,3},{2,0},{3,1},{4,6},{5,7},{6,4},{7,5},{8,10},{9,11},{10,... | collective-permute-start | bytes 294920 | tf_op jit(solution)/shard_map/ppermute | solution.py:345
  10.0 1.6 %collective-permute-start.2 = (bf16[128,384]{1,0:T(8,128)(2,1)S(1)}, bf16[128,384]{1,0:T(8,128)(2,1)S(1)}, u32[]{:S(2)}, u32[]{:S(2)}) collective-permute-start(bf16[128,384]{1,0:T(8,128)(2,1)S(1)} %get-tuple-element.26.refs_3_), channel_id=1, source_target_pairs={{0,1},{1,0},{2,3},{3,2},{4,5},{5,4},{6,7},{7,6},{8,9},{9,8},{10,11... | collective-permute-start | bytes 294920 | tf_op jit(solution)/shard_map/ppermute | solution.py:345
  11.6 1.2 %collective-permute-start.4 = (bf16[128,384]{1,0:T(8,128)(2,1)S(1)}, bf16[128,384]{1,0:T(8,128)(2,1)S(1)}, u32[]{:S(2)}, u32[]{:S(2)}) collective-permute-start(bf16[128,384]{1,0:T(8,128)(2,1)S(1)} %slice.9.refs_0_.refs_1_), channel_id=1, source_target_pairs={{0,2},{1,3},{2,0},{3,1},{4,6},{5,7},{6,4},{7,5},{8,10},{9,11},{10,... | collective-permute-start | bytes 294920 | tf_op jit(solution)/shard_map/ppermute | solution.py:345
  13.1 3.8 %collective-permute-start.3 = (bf16[128,384]{1,0:T(8,128)(2,1)S(1)}, bf16[128,384]{1,0:T(8,128)(2,1)S(1)}, u32[]{:S(2)}, u32[]{:S(2)}) collective-permute-start(bf16[128,384]{1,0:T(8,128)(2,1)S(1)} %collective-permute-done.1.refs_4_), channel_id=1, source_target_pairs={{0,1},{1,0},{2,3},{3,2},{4,5},{5,4},{6,7},{7,6},{8,9},{9,8},{10,11... | collective-permute-start | bytes 294920 | tf_op jit(solution)/shard_map/ppermute | solution.py:345
  17.0 0.7 %collective-permute-start.5 = (bf16[128,384]{1,0:T(8,128)(2,1)S(1)}, bf16[128,384]{1,0:T(8,128)(2,1)S(1)}, u32[]{:S(2)}, u32[]{:S(2)}) collective-permute-start(bf16[128,384]{1,0:T(8,128)(2,1)S(1)} %slice.9.refs_0_.refs_1_), channel_id=1, source_target_pairs={{0,1},{1,0},{2,3},{3,2},{4,5},{5,4},{6,7},{7,6},{8,9},{9,8},{10,11... | collective-permute-start | bytes 294920 | tf_op jit(solution)/shard_map/ppermute | solution.py:345
  17.7 0.6 %collective-permute-done.4.refs_1_.refs_2_ = bf16[128,384]{1,0:T(8,128)(2,1)S(1)} collective-permute-done((bf16[128,384]{1,0:T(8,128)(2,1)S(1)}, bf16[128,384]{1,0:T(8,128)(2,1)S(1)}, u32[]{:S(2)}, u32[]{:S(2)}) %collective-permute-start.4) | collective-permute-done | bytes 98336 | tf_op jit(solution)/shard_map/ppermute | solution.py:345
  18.3 0.7 %collective-permute-start.6 = (bf16[128,384]{1,0:T(8,128)(2,1)S(1)}, bf16[128,384]{1,0:T(8,128)(2,1)S(1)}, u32[]{:S(2)}, u32[]{:S(2)}) collective-permute-start(bf16[128,384]{1,0:T(8,128)(2,1)S(1)} %collective-permute-done.4.refs_1_.refs_2_), channel_id=1, source_target_pairs={{0,1},{1,0},{2,3},{3,2},{4,5},{5,4},{6,7},{7,6},{8,9},{9,8},{10,11... | collective-permute-start | bytes 294920 | tf_op jit(solution)/shard_map/ppermute | solution.py:345
  19.7 1.0 %collective-permute-done.3.refs_6_ = bf16[128,384]{1,0:T(8,128)(2,1)S(1)} collective-permute-done((bf16[128,384]{1,0:T(8,128)(2,1)S(1)}, bf16[128,384]{1,0:T(8,128)(2,1)S(1)}, u32[]{:S(2)}, u32[]{:S(2)}) %collective-permute-start.3) | collective-permute-done | bytes 98336 | tf_op jit(solution)/shard_map/ppermute | solution.py:345
  20.7 0.6 %shard_map.69 = (bf16[512,384]{1,0:T(8,128)(2,1)S(1)}, f32[512,384]{1,0:T(8,128)S(1)}, f32[8,128]{1,0:T(8,128)S(1)}, f32[384,384]{1,0:T(8,128)S(1)}) custom-call(f32[1]{0:T(128)S(6)} %copy.9.refs_0_, bf16[32,384]{1,0:T(8,128)(2,1)S(1)} %get-tuple-element.24.refs_1_, bf16[32,384]{1,0:T(8,128)(2,1)S(1)} %slice.8.refs_2_, ...), custom_call_target="tpu_custom_call" | custom-call | tf_op jit(solution)/shard_map/pallas_call | solution.py:28
  21.3 0.7 %collective-permute-done.5.refs_2_.refs_3_ = bf16[128,384]{1,0:T(8,128)(2,1)S(1)} collective-permute-done((bf16[128,384]{1,0:T(8,128)(2,1)S(1)}, bf16[128,384]{1,0:T(8,128)(2,1)S(1)}, u32[]{:S(2)}, u32[]{:S(2)}) %collective-permute-start.5) | collective-permute-done | bytes 98336 | tf_op jit(solution)/shard_map/ppermute | solution.py:345
  22.0 1.0 %collective-permute-done.6.refs_3_.refs_4_ = bf16[128,384]{1,0:T(8,128)(2,1)S(1)} collective-permute-done((bf16[128,384]{1,0:T(8,128)(2,1)S(1)}, bf16[128,384]{1,0:T(8,128)(2,1)S(1)}, u32[]{:S(2)}, u32[]{:S(2)}) %collective-permute-start.6) | collective-permute-done | bytes 98336 | tf_op jit(solution)/shard_map/ppermute | solution.py:345
  23.6 0.6 %collective-permute-start.18 = (f32[256,384]{1,0:T(8,128)S(1)}, f32[256,384]{1,0:T(8,128)S(1)}, u32[]{:S(2)}, u32[]{:S(2)}) collective-permute-start(f32[256,384]{1,0:T(8,128)S(1)} %get-tuple-element.40.refs_0_), channel_id=1, source_target_pairs={{0,4},{1,5},{2,6},{3,7},{4,0},{5,1},{6,2},{7,3},{8,12},{9,13},{10,... | collective-permute-start | bytes 1179656 | tf_op jit(solution)/shard_map/ppermute | solution.py:345
  24.3 0.6 %collective-permute-done.9.refs_1_ = bf16[512,384]{1,0:T(8,128)(2,1)S(1)} collective-permute-done((bf16[512,384]{1,0:T(8,128)(2,1)S(1)}, bf16[512,384]{1,0:T(8,128)(2,1)S(1)}, u32[]{:S(2)}, u32[]{:S(2)}) %collective-permute-start.9) | collective-permute-done | bytes 393248 | tf_op jit(solution)/shard_map/ppermute | solution.py:345
  24.8 0.6 %shard_map.72 = (f32[320,128]{1,0:T(8,128)S(1)}, f32[320,128]{1,0:T(8,128)S(1)}) custom-call(bf16[512,384]{1,0:T(8,128)(2,1)S(1)} %shard_map.70.refs_7_.refs_0_, bf16[512,384]{1,0:T(8,128)(2,1)S(1)} %collective-permute-done.9.refs_1_, bf16[512,384]{1,0:T(8,128)(2,1)S(1)} %get-tuple-element.32.refs_2_, bf16[512,384]{1,0:T(8,128)(2,1)S(1)} %get-tuple-element.33.refs_3_, ...), custom_call_target="tpu_custom_call" | custom-call | tf_op jit(solution)/shard_map/pallas_call | solution.py:28
  25.6 1.3 %collective-permute-done.10.refs_2_ = f32[320,128]{1,0:T(8,128)S(1)} collective-permute-done((f32[320,128]{1,0:T(8,128)S(1)}, f32[320,128]{1,0:T(8,128)S(1)}, u32[]{:S(2)}, u32[]{:S(2)}) %collective-permute-start.10) | collective-permute-done | bytes 163872 | tf_op jit(solution)/shard_map/ppermute | solution.py:345
  26.9 2.4 %collective-permute-start.13 = (f32[160,128]{1,0:T(8,128)S(1)}, f32[160,128]{1,0:T(8,128)S(1)}, u32[]{:S(2)}, u32[]{:S(2)}) collective-permute-start(f32[160,128]{1,0:T(8,128)S(1)} %get-tuple-element.38), channel_id=1, source_target_pairs={{0,17},{1,16},{2,19},{3,18},{4,21},{5,20},{6,23},{7,22},{8,25},{9,... | collective-permute-start | bytes 245768 | tf_op jit(solution)/shard_map/ppermute | solution.py:345
  29.9 0.6 %collective-permute-start.12 = (f32[160,128]{1,0:T(8,128)S(1)}, f32[160,128]{1,0:T(8,128)S(1)}, u32[]{:S(2)}, u32[]{:S(2)}) collective-permute-start(f32[160,128]{1,0:T(8,128)S(1)} %get-tuple-element.37.refs_0_.refs_4_), channel_id=1, source_target_pairs={{0,1},{1,0},{2,3},{3,2},{4,5},{5,4},{6,7},{7,6},{8,9},{9,8},{10,11... | collective-permute-start | bytes 245768 | tf_op jit(solution)/shard_map/ppermute | solution.py:345
  30.5 2.0 %collective-permute-done.13.refs_3_ = f32[160,128]{1,0:T(8,128)S(1)} collective-permute-done((f32[160,128]{1,0:T(8,128)S(1)}, f32[160,128]{1,0:T(8,128)S(1)}, u32[]{:S(2)}, u32[]{:S(2)}) %collective-permute-start.13) | collective-permute-done | bytes 81952 | tf_op jit(solution)/shard_map/ppermute | solution.py:345
  32.4 1.7 %collective-permute-done.11.refs_1_ = f32[160,128]{1,0:T(8,128)S(1)} collective-permute-done((f32[160,128]{1,0:T(8,128)S(1)}, f32[160,128]{1,0:T(8,128)S(1)}, u32[]{:S(2)}, u32[]{:S(2)}) %collective-permute-start.11) | collective-permute-done | bytes 81952 | tf_op jit(solution)/shard_map/ppermute | solution.py:345
  34.3 3.1 %collective-permute-start.14 = (f32[160,128]{1,0:T(8,128)S(1)}, f32[160,128]{1,0:T(8,128)S(1)}, u32[]{:S(2)}, u32[]{:S(2)}) collective-permute-start(f32[160,128]{1,0:T(8,128)S(1)} %shard_map.74.refs_0_), channel_id=1, source_target_pairs={{0,2},{1,3},{2,0},{3,1},{4,6},{5,7},{6,4},{7,5},{8,10},{9,11},{10,... | collective-permute-start | bytes 245768 | tf_op jit(solution)/shard_map/ppermute | solution.py:345
  37.6 0.7 %collective-permute-start.20 = (bf16[128,384]{1,0:T(8,128)(2,1)S(1)}, bf16[128,384]{1,0:T(8,128)(2,1)S(1)}, u32[]{:S(2)}, u32[]{:S(2)}) collective-permute-start(bf16[128,384]{1,0:T(8,128)(2,1)S(1)} %get-tuple-element.42), channel_id=1, source_target_pairs={{0,0},{1,4},{2,8},{3,12},{4,1},{5,5},{6,9},{7,13},{8,2},{9,6},{10,... | collective-permute-start | bytes 294920 | tf_op jit(solution)/shard_map/ppermute | solution.py:403
  38.3 4.5 %collective-permute-start.21 = (bf16[128,384]{1,0:T(8,128)(2,1)S(1)}, bf16[128,384]{1,0:T(8,128)(2,1)S(1)}, u32[]{:S(2)}, u32[]{:S(2)}) collective-permute-start(bf16[128,384]{1,0:T(8,128)(2,1)S(1)} %get-tuple-element.43), channel_id=1, source_target_pairs={{0,2},{1,6},{2,10},{3,14},{4,3},{5,7},{6,11},{7,15},{8,0},{9,4},{1... | collective-permute-start | bytes 294920 | tf_op jit(solution)/shard_map/ppermute | solution.py:403
  42.9 1.6 %collective-permute-start.16 = (f32[160,128]{1,0:T(8,128)S(1)}, f32[160,128]{1,0:T(8,128)S(1)}, u32[]{:S(2)}, u32[]{:S(2)}) collective-permute-start(f32[160,128]{1,0:T(8,128)S(1)} %shard_map.75.refs_0_), channel_id=1, source_target_pairs={{0,16},{1,17},{2,18},{3,19},{4,20},{5,21},{6,22},{7,23},{8,24},{9,... | collective-permute-start | bytes 245768 | tf_op jit(solution)/shard_map/ppermute | solution.py:345
  44.4 1.9 %collective-permute-start.15 = (f32[160,128]{1,0:T(8,128)S(1)}, f32[160,128]{1,0:T(8,128)S(1)}, u32[]{:S(2)}, u32[]{:S(2)}) collective-permute-start(f32[160,128]{1,0:T(8,128)S(1)} %shard_map.75.refs_0_), channel_id=1, source_target_pairs={{0,8},{1,9},{2,10},{3,11},{4,12},{5,13},{6,14},{7,15},{8,0},{9,1},... | collective-permute-start | bytes 245768 | tf_op jit(solution)/shard_map/ppermute | solution.py:345
  46.6 2.7 %collective-permute-done.17.refs_3_ = f32[160,128]{1,0:T(8,128)S(1)} collective-permute-done((f32[160,128]{1,0:T(8,128)S(1)}, f32[160,128]{1,0:T(8,128)S(1)}, u32[]{:S(2)}, u32[]{:S(2)}) %collective-permute-start.17) | collective-permute-done | bytes 81952 | tf_op jit(solution)/shard_map/ppermute | solution.py:345
  49.4 0.6 %collective-permute-done.15.refs_1_ = f32[160,128]{1,0:T(8,128)S(1)} collective-permute-done((f32[160,128]{1,0:T(8,128)S(1)}, f32[160,128]{1,0:T(8,128)S(1)}, u32[]{:S(2)}, u32[]{:S(2)}) %collective-permute-start.15) | collective-permute-done | bytes 81952 | tf_op jit(solution)/shard_map/ppermute | solution.py:345
  50.1 1.0 %shard_map.79 = (bf16[1,128,2,384]{3,2,1,0:T(2,128)(2,1)}, f32[2,384,384]{2,1,0:T(8,128)}) custom-call(f32[4,160,128]{2,1,0:T(8,128)S(1)} %shard_map.78.refs_0_, bf16[1,128,2,384]{3,2,1,0:T(2,128)(2,1)S(1)} %shard_map.77.refs_4_.refs_1_), custom_call_target="tpu_custom_call" | custom-call | tf_op jit(solution)/shard_map/pallas_call | solution.py:28
  51.1 0.6 %collective-permute-done.22.refs_1_ = f32[4,160,128]{2,1,0:T(8,128)S(1)} collective-permute-done((f32[4,160,128]{2,1,0:T(8,128)S(1)}, f32[4,160,128]{2,1,0:T(8,128)S(1)}, u32[]{:S(2)}, u32[]{:S(2)}) %collective-permute-start.22) | collective-permute-done | bytes 327712 | tf_op jit(solution)/shard_map/ppermute | solution.py:345
  51.7 1.2 %shard_map.80 = f32[2,384,384]{2,1,0:T(8,128)} custom-call(f32[4,160,128]{2,1,0:T(8,128)S(1)} %shard_map.78.refs_0_, f32[4,160,128]{2,1,0:T(8,128)S(1)} %collective-permute-done.22.refs_1_, f32[2,384,384]{2,1,0:T(8,128)} %get-tuple-element.45.refs_2_), custom_call_target="tpu_custom_call", output_to_operand_aliasing={{}: (2, {})} | custom-call | tf_op jit(solution)/shard_map/pallas_call | solution.py:28
  (29 shorter events, 2.7 us)
Async XLA Ops:
  2.3 9.2 %collective-permute-start = (bf16[160,384]{1,0:T(8,128)(2,1)S(1)}, bf16[160,384]{1,0:T(8,128)(2,1)S(1)}, u32[]{:S(2)}, u32[]{:S(2)}) collective-permute-start(bf16[160,384]{1,0:T(8,128)(2,1)S(1)} %get-tuple-element.25), channel_id=1, source_target_pairs={{0,8},{1,9},{2,10},{3,11},{4,12},{5,13},{6,14},{7,15},{8,0},{9,1},... | collective-permute-start | bytes 368648 | tf_op jit(solution)/shard_map/ppermute | solution.py:345
  5.3 16.6 %collective-permute-start.7 = (bf16[256,512]{1,0:T(8,128)(2,1)S(1)}, bf16[256,512]{1,0:T(8,128)(2,1)S(1)}, u32[]{:S(2)}, u32[]{:S(2)}) collective-permute-start(bf16[256,512]{1,0:T(8,128)(2,1)S(1)} %get-tuple-element.27.refs_7_), channel_id=1, source_target_pairs={{0,8},{1,9},{2,10},{3,11},{4,12},{5,13},{6,14},{7,15},{8,0},{9,1},... | collective-permute-start | bytes 786440 | tf_op jit(solution)/shard_map/ppermute | solution.py:345
  5.4 16.5 %collective-permute-start.8 = (bf16[256,512]{1,0:T(8,128)(2,1)S(1)}, bf16[256,512]{1,0:T(8,128)(2,1)S(1)}, u32[]{:S(2)}, u32[]{:S(2)}) collective-permute-start(bf16[256,512]{1,0:T(8,128)(2,1)S(1)} %get-tuple-element.28.refs_8_), channel_id=1, source_target_pairs={{0,8},{1,9},{2,10},{3,11},{4,12},{5,13},{6,14},{7,15},{8,0},{9,1},... | collective-permute-start | bytes 786440 | tf_op jit(solution)/shard_map/ppermute | solution.py:345
  7.4 5.8 %collective-permute-start.1 = (bf16[128,384]{1,0:T(8,128)(2,1)S(1)}, bf16[128,384]{1,0:T(8,128)(2,1)S(1)}, u32[]{:S(2)}, u32[]{:S(2)}) collective-permute-start(bf16[128,384]{1,0:T(8,128)(2,1)S(1)} %get-tuple-element.26.refs_3_), channel_id=1, source_target_pairs={{0,2},{1,3},{2,0},{3,1},{4,6},{5,7},{6,4},{7,5},{8,10},{9,11},{10,... | collective-permute-start | bytes 294920 | tf_op jit(solution)/shard_map/ppermute | solution.py:345
  10.0 7.0 %collective-permute-start.2 = (bf16[128,384]{1,0:T(8,128)(2,1)S(1)}, bf16[128,384]{1,0:T(8,128)(2,1)S(1)}, u32[]{:S(2)}, u32[]{:S(2)}) collective-permute-start(bf16[128,384]{1,0:T(8,128)(2,1)S(1)} %get-tuple-element.26.refs_3_), channel_id=1, source_target_pairs={{0,1},{1,0},{2,3},{3,2},{4,5},{5,4},{6,7},{7,6},{8,9},{9,8},{10,11... | collective-permute-start | bytes 294920 | tf_op jit(solution)/shard_map/ppermute | solution.py:345
  11.6 6.8 %collective-permute-start.4 = (bf16[128,384]{1,0:T(8,128)(2,1)S(1)}, bf16[128,384]{1,0:T(8,128)(2,1)S(1)}, u32[]{:S(2)}, u32[]{:S(2)}) collective-permute-start(bf16[128,384]{1,0:T(8,128)(2,1)S(1)} %slice.9.refs_0_.refs_1_), channel_id=1, source_target_pairs={{0,2},{1,3},{2,0},{3,1},{4,6},{5,7},{6,4},{7,5},{8,10},{9,11},{10,... | collective-permute-start | bytes 294920 | tf_op jit(solution)/shard_map/ppermute | solution.py:345
  13.1 7.6 %collective-permute-start.3 = (bf16[128,384]{1,0:T(8,128)(2,1)S(1)}, bf16[128,384]{1,0:T(8,128)(2,1)S(1)}, u32[]{:S(2)}, u32[]{:S(2)}) collective-permute-start(bf16[128,384]{1,0:T(8,128)(2,1)S(1)} %collective-permute-done.1.refs_4_), channel_id=1, source_target_pairs={{0,1},{1,0},{2,3},{3,2},{4,5},{5,4},{6,7},{7,6},{8,9},{9,8},{10,11... | collective-permute-start | bytes 294920 | tf_op jit(solution)/shard_map/ppermute | solution.py:345
  17.0 5.0 %collective-permute-start.5 = (bf16[128,384]{1,0:T(8,128)(2,1)S(1)}, bf16[128,384]{1,0:T(8,128)(2,1)S(1)}, u32[]{:S(2)}, u32[]{:S(2)}) collective-permute-start(bf16[128,384]{1,0:T(8,128)(2,1)S(1)} %slice.9.refs_0_.refs_1_), channel_id=1, source_target_pairs={{0,1},{1,0},{2,3},{3,2},{4,5},{5,4},{6,7},{7,6},{8,9},{9,8},{10,11... | collective-permute-start | bytes 294920 | tf_op jit(solution)/shard_map/ppermute | solution.py:345
  18.3 4.7 %collective-permute-start.6 = (bf16[128,384]{1,0:T(8,128)(2,1)S(1)}, bf16[128,384]{1,0:T(8,128)(2,1)S(1)}, u32[]{:S(2)}, u32[]{:S(2)}) collective-permute-start(bf16[128,384]{1,0:T(8,128)(2,1)S(1)} %collective-permute-done.4.refs_1_.refs_2_), channel_id=1, source_target_pairs={{0,1},{1,0},{2,3},{3,2},{4,5},{5,4},{6,7},{7,6},{8,9},{9,8},{10,11... | collective-permute-start | bytes 294920 | tf_op jit(solution)/shard_map/ppermute | solution.py:345
  23.0 1.8 %collective-permute-start.9 = (bf16[512,384]{1,0:T(8,128)(2,1)S(1)}, bf16[512,384]{1,0:T(8,128)(2,1)S(1)}, u32[]{:S(2)}, u32[]{:S(2)}) collective-permute-start(bf16[512,384]{1,0:T(8,128)(2,1)S(1)} %shard_map.70.refs_7_.refs_0_), channel_id=1, source_target_pairs={{0,4},{1,5},{2,6},{3,7},{4,0},{5,1},{6,2},{7,3},{8,12},{9,13},{10,... | collective-permute-start | bytes 1179656 | tf_op jit(solution)/shard_map/ppermute | solution.py:345
  23.6 13.8 %collective-permute-start.18 = (f32[256,384]{1,0:T(8,128)S(1)}, f32[256,384]{1,0:T(8,128)S(1)}, u32[]{:S(2)}, u32[]{:S(2)}) collective-permute-start(f32[256,384]{1,0:T(8,128)S(1)} %get-tuple-element.40.refs_0_), channel_id=1, source_target_pairs={{0,4},{1,5},{2,6},{3,7},{4,0},{5,1},{6,2},{7,3},{8,12},{9,13},{10,... | collective-permute-start | bytes 1179656 | tf_op jit(solution)/shard_map/ppermute | solution.py:345
  24.2 13.3 %collective-permute-start.19 = (f32[256,384]{1,0:T(8,128)S(1)}, f32[256,384]{1,0:T(8,128)S(1)}, u32[]{:S(2)}, u32[]{:S(2)}) collective-permute-start(f32[256,384]{1,0:T(8,128)S(1)} %get-tuple-element.41.refs_1_), channel_id=1, source_target_pairs={{0,4},{1,5},{2,6},{3,7},{4,0},{5,1},{6,2},{7,3},{8,12},{9,13},{10,... | collective-permute-start | bytes 1179656 | tf_op jit(solution)/shard_map/ppermute | solution.py:345
  25.4 1.4 %collective-permute-start.10 = (f32[320,128]{1,0:T(8,128)S(1)}, f32[320,128]{1,0:T(8,128)S(1)}, u32[]{:S(2)}, u32[]{:S(2)}) collective-permute-start(f32[320,128]{1,0:T(8,128)S(1)} %get-tuple-element.36), channel_id=1, source_target_pairs={{0,4},{1,5},{2,6},{3,7},{4,0},{5,1},{6,2},{7,3},{8,12},{9,13},{10,... | collective-permute-start | bytes 491528 | tf_op jit(solution)/shard_map/ppermute | solution.py:345
  26.9 5.5 %collective-permute-start.13 = (f32[160,128]{1,0:T(8,128)S(1)}, f32[160,128]{1,0:T(8,128)S(1)}, u32[]{:S(2)}, u32[]{:S(2)}) collective-permute-start(f32[160,128]{1,0:T(8,128)S(1)} %get-tuple-element.38), channel_id=1, source_target_pairs={{0,17},{1,16},{2,19},{3,18},{4,21},{5,20},{6,23},{7,22},{8,25},{9,... | collective-permute-start | bytes 245768 | tf_op jit(solution)/shard_map/ppermute | solution.py:345
  29.3 4.8 %collective-permute-start.11 = (f32[160,128]{1,0:T(8,128)S(1)}, f32[160,128]{1,0:T(8,128)S(1)}, u32[]{:S(2)}, u32[]{:S(2)}) collective-permute-start(f32[160,128]{1,0:T(8,128)S(1)} %get-tuple-element.38), channel_id=1, source_target_pairs={{0,16},{1,17},{2,18},{3,19},{4,20},{5,21},{6,22},{7,23},{8,24},{9,... | collective-permute-start | bytes 245768 | tf_op jit(solution)/shard_map/ppermute | solution.py:345
  29.9 4.4 %collective-permute-start.12 = (f32[160,128]{1,0:T(8,128)S(1)}, f32[160,128]{1,0:T(8,128)S(1)}, u32[]{:S(2)}, u32[]{:S(2)}) collective-permute-start(f32[160,128]{1,0:T(8,128)S(1)} %get-tuple-element.37.refs_0_.refs_4_), channel_id=1, source_target_pairs={{0,1},{1,0},{2,3},{3,2},{4,5},{5,4},{6,7},{7,6},{8,9},{9,8},{10,11... | collective-permute-start | bytes 245768 | tf_op jit(solution)/shard_map/ppermute | solution.py:345
  34.3 8.4 %collective-permute-start.14 = (f32[160,128]{1,0:T(8,128)S(1)}, f32[160,128]{1,0:T(8,128)S(1)}, u32[]{:S(2)}, u32[]{:S(2)}) collective-permute-start(f32[160,128]{1,0:T(8,128)S(1)} %shard_map.74.refs_0_), channel_id=1, source_target_pairs={{0,2},{1,3},{2,0},{3,1},{4,6},{5,7},{6,4},{7,5},{8,10},{9,11},{10,... | collective-permute-start | bytes 245768 | tf_op jit(solution)/shard_map/ppermute | solution.py:345
  37.6 8.7 %collective-permute-start.20 = (bf16[128,384]{1,0:T(8,128)(2,1)S(1)}, bf16[128,384]{1,0:T(8,128)(2,1)S(1)}, u32[]{:S(2)}, u32[]{:S(2)}) collective-permute-start(bf16[128,384]{1,0:T(8,128)(2,1)S(1)} %get-tuple-element.42), channel_id=1, source_target_pairs={{0,0},{1,4},{2,8},{3,12},{4,1},{5,5},{6,9},{7,13},{8,2},{9,6},{10,... | collective-permute-start | bytes 294920 | tf_op jit(solution)/shard_map/ppermute | solution.py:403
  38.3 8.1 %collective-permute-start.21 = (bf16[128,384]{1,0:T(8,128)(2,1)S(1)}, bf16[128,384]{1,0:T(8,128)(2,1)S(1)}, u32[]{:S(2)}, u32[]{:S(2)}) collective-permute-start(bf16[128,384]{1,0:T(8,128)(2,1)S(1)} %get-tuple-element.43), channel_id=1, source_target_pairs={{0,2},{1,6},{2,10},{3,14},{4,3},{5,7},{6,11},{7,15},{8,0},{9,4},{1... | collective-permute-start | bytes 294920 | tf_op jit(solution)/shard_map/ppermute | solution.py:403
  42.8 6.6 %collective-permute-start.17 = (f32[160,128]{1,0:T(8,128)S(1)}, f32[160,128]{1,0:T(8,128)S(1)}, u32[]{:S(2)}, u32[]{:S(2)}) collective-permute-start(f32[160,128]{1,0:T(8,128)S(1)} %shard_map.75.refs_0_), channel_id=1, source_target_pairs={{0,24},{1,25},{2,26},{3,27},{4,28},{5,29},{6,30},{7,31},{8,16},{9,... | collective-permute-start | bytes 245768 | tf_op jit(solution)/shard_map/ppermute | solution.py:345
  42.9 6.5 %collective-permute-start.16 = (f32[160,128]{1,0:T(8,128)S(1)}, f32[160,128]{1,0:T(8,128)S(1)}, u32[]{:S(2)}, u32[]{:S(2)}) collective-permute-start(f32[160,128]{1,0:T(8,128)S(1)} %shard_map.75.refs_0_), channel_id=1, source_target_pairs={{0,16},{1,17},{2,18},{3,19},{4,20},{5,21},{6,22},{7,23},{8,24},{9,... | collective-permute-start | bytes 245768 | tf_op jit(solution)/shard_map/ppermute | solution.py:345
  44.4 5.5 %collective-permute-start.15 = (f32[160,128]{1,0:T(8,128)S(1)}, f32[160,128]{1,0:T(8,128)S(1)}, u32[]{:S(2)}, u32[]{:S(2)}) collective-permute-start(f32[160,128]{1,0:T(8,128)S(1)} %shard_map.75.refs_0_), channel_id=1, source_target_pairs={{0,8},{1,9},{2,10},{3,11},{4,12},{5,13},{6,14},{7,15},{8,0},{9,1},... | collective-permute-start | bytes 245768 | tf_op jit(solution)/shard_map/ppermute | solution.py:345
  50.0 1.7 %collective-permute-start.22 = (f32[4,160,128]{2,1,0:T(8,128)S(1)}, f32[4,160,128]{2,1,0:T(8,128)S(1)}, u32[]{:S(2)}, u32[]{:S(2)}) collective-permute-start(f32[4,160,128]{2,1,0:T(8,128)S(1)} %shard_map.78.refs_0_), channel_id=1, source_target_pairs={{0,4},{1,5},{2,6},{3,7},{4,0},{5,1},{6,2},{7,3},{8,12},{9,13},{10,... | collective-permute-start | bytes 983048 | tf_op jit(solution)/shard_map/ppermute | solution.py:345

commit v26 on v25

--- a/solution.py
+++ b/solution.py
@@ -304,7 +304,11 @@
 def late_kernel(own, other, before, out, lines, result, sems, middle_sems):
     del before
     core, half = lax.axis_index("core"), lines.shape[1] // 2
-    set_lines(own, lines, core * half)
+    size, slot, side = own.shape[1], 1 - core, lax.axis_index("side")
+    other_point = jnp.where(slot == lax.axis_index("hyp"), 0, 2)
+    for index in range(2):
+        start = pl.multiple_of(core * half + slot * size, 8)
+        lines[jnp.bitwise_xor(side, index), pl.ds(start, size), :] = own[other_point + index]
     set_lines(other, lines, (1 - core) * half)
     middle, last = (slice(i * LANES, (i + 1) * LANES) for i in (1, 2))
     areas = []

time: 53 us -> 53 us (level)
  no operation moved by 1% of the time
where the time goes in v26:
time: 53 us; the launch traced here: 52.8 us
  starting transfers between devices  31.9 us (60%)
  waiting for transfers between devices  13.3 us (25%)
  Pallas kernels  6.13 us (12%)
  between operations  1.41 us (3%)
    ppermute x21, starting transfers between devices, swap(): return lax.ppermute(x, AXES, [(i, i ^ mask) for i in range(devices)])  26.8 us
    ppermute x21, waiting for transfers between devices, swap(): return lax.ppermute(x, AXES, [(i, i ^ mask) for i in range(devices)])  13.3 us
    pallas_call x13, Pallas kernels, call(): pl.pallas_call(body, out_shape=outs, in_specs=list(specs) + [ANY] * len(a...  6.13 us
    ppermute x2, starting transfers between devices, deliver(): return lax.ppermute(x, AXES, pairs)  5.14 us
  transfers between devices with their start and end apart: 23, of which 13 were waited for; matrix products, arithmetic and copies ran while one was open for 0% of the time, Pallas kernels for 6%

profile of v26, /device:TPU:0, one launch (start us, length us, event | category | flops | bytes accessed | tf_op | source)
XLA Modules:
  0.0 52.8 jit_solution(14998592959786298991)
XLA Ops:
  0.6 1.7 %shard_map.68 = (bf16[128,384]{1,0:T(8,128)(2,1)S(1)}, bf16[160,384]{1,0:T(8,128)(2,1)S(1)}, bf16[32,384]{1,0:T(8,128)(2,1)S(1)}, s32[2,8,128]{2,1,0:T(8,128)S(1...) custom-call(s32[2]{0:T(128)} %bitcast.1, bf16[1,128,2,384]{3,2,1,0:T(2,128)(2,1)} %refs_1_.1, ...), custom_call_target="tpu_custom_call" | custom-call | tf_op jit(solution)/shard_map/pallas_call | solution.py:28
  2.3 3.0 %collective-permute-start = (bf16[160,384]{1,0:T(8,128)(2,1)S(1)}, bf16[160,384]{1,0:T(8,128)(2,1)S(1)}, u32[]{:S(2)}, u32[]{:S(2)}) collective-permute-start(bf16[160,384]{1,0:T(8,128)(2,1)S(1)} %get-tuple-element.25), channel_id=1, source_target_pairs={{0,8},{1,9},{2,10},{3,11},{4,12},{5,13},{6,14},{7,15},{8,0},{9,1},... | collective-permute-start | bytes 368648 | tf_op jit(solution)/shard_map/ppermute | solution.py:349
  5.4 1.9 %collective-permute-start.8 = (bf16[256,512]{1,0:T(8,128)(2,1)S(1)}, bf16[256,512]{1,0:T(8,128)(2,1)S(1)}, u32[]{:S(2)}, u32[]{:S(2)}) collective-permute-start(bf16[256,512]{1,0:T(8,128)(2,1)S(1)} %get-tuple-element.28.refs_8_), channel_id=1, source_target_pairs={{0,8},{1,9},{2,10},{3,11},{4,12},{5,13},{6,14},{7,15},{8,0},{9,1},... | collective-permute-start | bytes 786440 | tf_op jit(solution)/shard_map/ppermute | solution.py:349
  7.4 2.6 %collective-permute-start.1 = (bf16[128,384]{1,0:T(8,128)(2,1)S(1)}, bf16[128,384]{1,0:T(8,128)(2,1)S(1)}, u32[]{:S(2)}, u32[]{:S(2)}) collective-permute-start(bf16[128,384]{1,0:T(8,128)(2,1)S(1)} %get-tuple-element.26.refs_3_), channel_id=1, source_target_pairs={{0,2},{1,3},{2,0},{3,1},{4,6},{5,7},{6,4},{7,5},{8,10},{9,11},{10,... | collective-permute-start | bytes 294920 | tf_op jit(solution)/shard_map/ppermute | solution.py:349
  10.0 1.6 %collective-permute-start.2 = (bf16[128,384]{1,0:T(8,128)(2,1)S(1)}, bf16[128,384]{1,0:T(8,128)(2,1)S(1)}, u32[]{:S(2)}, u32[]{:S(2)}) collective-permute-start(bf16[128,384]{1,0:T(8,128)(2,1)S(1)} %get-tuple-element.26.refs_3_), channel_id=1, source_target_pairs={{0,1},{1,0},{2,3},{3,2},{4,5},{5,4},{6,7},{7,6},{8,9},{9,8},{10,11... | collective-permute-start | bytes 294920 | tf_op jit(solution)/shard_map/ppermute | solution.py:349
  11.6 1.2 %collective-permute-start.4 = (bf16[128,384]{1,0:T(8,128)(2,1)S(1)}, bf16[128,384]{1,0:T(8,128)(2,1)S(1)}, u32[]{:S(2)}, u32[]{:S(2)}) collective-permute-start(bf16[128,384]{1,0:T(8,128)(2,1)S(1)} %slice.9.refs_0_.refs_1_), channel_id=1, source_target_pairs={{0,2},{1,3},{2,0},{3,1},{4,6},{5,7},{6,4},{7,5},{8,10},{9,11},{10,... | collective-permute-start | bytes 294920 | tf_op jit(solution)/shard_map/ppermute | solution.py:349
  13.1 3.8 %collective-permute-start.3 = (bf16[128,384]{1,0:T(8,128)(2,1)S(1)}, bf16[128,384]{1,0:T(8,128)(2,1)S(1)}, u32[]{:S(2)}, u32[]{:S(2)}) collective-permute-start(bf16[128,384]{1,0:T(8,128)(2,1)S(1)} %collective-permute-done.1.refs_4_), channel_id=1, source_target_pairs={{0,1},{1,0},{2,3},{3,2},{4,5},{5,4},{6,7},{7,6},{8,9},{9,8},{10,11... | collective-permute-start | bytes 294920 | tf_op jit(solution)/shard_map/ppermute | solution.py:349
  17.0 0.7 %collective-permute-start.5 = (bf16[128,384]{1,0:T(8,128)(2,1)S(1)}, bf16[128,384]{1,0:T(8,128)(2,1)S(1)}, u32[]{:S(2)}, u32[]{:S(2)}) collective-permute-start(bf16[128,384]{1,0:T(8,128)(2,1)S(1)} %slice.9.refs_0_.refs_1_), channel_id=1, source_target_pairs={{0,1},{1,0},{2,3},{3,2},{4,5},{5,4},{6,7},{7,6},{8,9},{9,8},{10,11... | collective-permute-start | bytes 294920 | tf_op jit(solution)/shard_map/ppermute | solution.py:349
  17.7 0.6 %collective-permute-done.4.refs_1_.refs_2_ = bf16[128,384]{1,0:T(8,128)(2,1)S(1)} collective-permute-done((bf16[128,384]{1,0:T(8,128)(2,1)S(1)}, bf16[128,384]{1,0:T(8,128)(2,1)S(1)}, u32[]{:S(2)}, u32[]{:S(2)}) %collective-permute-start.4) | collective-permute-done | bytes 98336 | tf_op jit(solution)/shard_map/ppermute | solution.py:349
  18.3 0.7 %collective-permute-start.6 = (bf16[128,384]{1,0:T(8,128)(2,1)S(1)}, bf16[128,384]{1,0:T(8,128)(2,1)S(1)}, u32[]{:S(2)}, u32[]{:S(2)}) collective-permute-start(bf16[128,384]{1,0:T(8,128)(2,1)S(1)} %collective-permute-done.4.refs_1_.refs_2_), channel_id=1, source_target_pairs={{0,1},{1,0},{2,3},{3,2},{4,5},{5,4},{6,7},{7,6},{8,9},{9,8},{10,11... | collective-permute-start | bytes 294920 | tf_op jit(solution)/shard_map/ppermute | solution.py:349
  19.7 1.0 %collective-permute-done.3.refs_6_ = bf16[128,384]{1,0:T(8,128)(2,1)S(1)} collective-permute-done((bf16[128,384]{1,0:T(8,128)(2,1)S(1)}, bf16[128,384]{1,0:T(8,128)(2,1)S(1)}, u32[]{:S(2)}, u32[]{:S(2)}) %collective-permute-start.3) | collective-permute-done | bytes 98336 | tf_op jit(solution)/shard_map/ppermute | solution.py:349
  20.7 0.6 %shard_map.69 = (bf16[512,384]{1,0:T(8,128)(2,1)S(1)}, f32[512,384]{1,0:T(8,128)S(1)}, f32[8,128]{1,0:T(8,128)S(1)}, f32[384,384]{1,0:T(8,128)S(1)}) custom-call(f32[1]{0:T(128)S(6)} %copy.9.refs_0_, bf16[32,384]{1,0:T(8,128)(2,1)S(1)} %get-tuple-element.24.refs_1_, bf16[32,384]{1,0:T(8,128)(2,1)S(1)} %slice.8.refs_2_, ...), custom_call_target="tpu_custom_call" | custom-call | tf_op jit(solution)/shard_map/pallas_call | solution.py:28
  21.3 0.7 %collective-permute-done.5.refs_2_.refs_3_ = bf16[128,384]{1,0:T(8,128)(2,1)S(1)} collective-permute-done((bf16[128,384]{1,0:T(8,128)(2,1)S(1)}, bf16[128,384]{1,0:T(8,128)(2,1)S(1)}, u32[]{:S(2)}, u32[]{:S(2)}) %collective-permute-start.5) | collective-permute-done | bytes 98336 | tf_op jit(solution)/shard_map/ppermute | solution.py:349
  22.0 1.0 %collective-permute-done.6.refs_3_.refs_4_ = bf16[128,384]{1,0:T(8,128)(2,1)S(1)} collective-permute-done((bf16[128,384]{1,0:T(8,128)(2,1)S(1)}, bf16[128,384]{1,0:T(8,128)(2,1)S(1)}, u32[]{:S(2)}, u32[]{:S(2)}) %collective-permute-start.6) | collective-permute-done | bytes 98336 | tf_op jit(solution)/shard_map/ppermute | solution.py:349
  23.6 0.6 %collective-permute-start.18 = (f32[256,384]{1,0:T(8,128)S(1)}, f32[256,384]{1,0:T(8,128)S(1)}, u32[]{:S(2)}, u32[]{:S(2)}) collective-permute-start(f32[256,384]{1,0:T(8,128)S(1)} %get-tuple-element.40.refs_0_), channel_id=1, source_target_pairs={{0,4},{1,5},{2,6},{3,7},{4,0},{5,1},{6,2},{7,3},{8,12},{9,13},{10,... | collective-permute-start | bytes 1179656 | tf_op jit(solution)/shard_map/ppermute | solution.py:349
  24.3 0.6 %collective-permute-done.9.refs_1_ = bf16[512,384]{1,0:T(8,128)(2,1)S(1)} collective-permute-done((bf16[512,384]{1,0:T(8,128)(2,1)S(1)}, bf16[512,384]{1,0:T(8,128)(2,1)S(1)}, u32[]{:S(2)}, u32[]{:S(2)}) %collective-permute-start.9) | collective-permute-done | bytes 393248 | tf_op jit(solution)/shard_map/ppermute | solution.py:349
  24.8 0.6 %shard_map.72 = (f32[320,128]{1,0:T(8,128)S(1)}, f32[320,128]{1,0:T(8,128)S(1)}) custom-call(bf16[512,384]{1,0:T(8,128)(2,1)S(1)} %shard_map.70.refs_7_.refs_0_, bf16[512,384]{1,0:T(8,128)(2,1)S(1)} %collective-permute-done.9.refs_1_, bf16[512,384]{1,0:T(8,128)(2,1)S(1)} %get-tuple-element.32.refs_2_, bf16[512,384]{1,0:T(8,128)(2,1)S(1)} %get-tuple-element.33.refs_3_, ...), custom_call_target="tpu_custom_call" | custom-call | tf_op jit(solution)/shard_map/pallas_call | solution.py:28
  25.6 1.3 %collective-permute-done.10.refs_2_ = f32[320,128]{1,0:T(8,128)S(1)} collective-permute-done((f32[320,128]{1,0:T(8,128)S(1)}, f32[320,128]{1,0:T(8,128)S(1)}, u32[]{:S(2)}, u32[]{:S(2)}) %collective-permute-start.10) | collective-permute-done | bytes 163872 | tf_op jit(solution)/shard_map/ppermute | solution.py:349
  26.9 2.4 %collective-permute-start.13 = (f32[160,128]{1,0:T(8,128)S(1)}, f32[160,128]{1,0:T(8,128)S(1)}, u32[]{:S(2)}, u32[]{:S(2)}) collective-permute-start(f32[160,128]{1,0:T(8,128)S(1)} %get-tuple-element.38), channel_id=1, source_target_pairs={{0,17},{1,16},{2,19},{3,18},{4,21},{5,20},{6,23},{7,22},{8,25},{9,... | collective-permute-start | bytes 245768 | tf_op jit(solution)/shard_map/ppermute | solution.py:349
  29.9 0.6 %collective-permute-start.12 = (f32[160,128]{1,0:T(8,128)S(1)}, f32[160,128]{1,0:T(8,128)S(1)}, u32[]{:S(2)}, u32[]{:S(2)}) collective-permute-start(f32[160,128]{1,0:T(8,128)S(1)} %get-tuple-element.37.refs_0_.refs_4_), channel_id=1, source_target_pairs={{0,1},{1,0},{2,3},{3,2},{4,5},{5,4},{6,7},{7,6},{8,9},{9,8},{10,11... | collective-permute-start | bytes 245768 | tf_op jit(solution)/shard_map/ppermute | solution.py:349
  30.5 2.0 %collective-permute-done.13.refs_3_ = f32[160,128]{1,0:T(8,128)S(1)} collective-permute-done((f32[160,128]{1,0:T(8,128)S(1)}, f32[160,128]{1,0:T(8,128)S(1)}, u32[]{:S(2)}, u32[]{:S(2)}) %collective-permute-start.13) | collective-permute-done | bytes 81952 | tf_op jit(solution)/shard_map/ppermute | solution.py:349
  32.4 1.7 %collective-permute-done.11.refs_1_ = f32[160,128]{1,0:T(8,128)S(1)} collective-permute-done((f32[160,128]{1,0:T(8,128)S(1)}, f32[160,128]{1,0:T(8,128)S(1)}, u32[]{:S(2)}, u32[]{:S(2)}) %collective-permute-start.11) | collective-permute-done | bytes 81952 | tf_op jit(solution)/shard_map/ppermute | solution.py:349
  34.3 3.1 %collective-permute-start.14 = (f32[160,128]{1,0:T(8,128)S(1)}, f32[160,128]{1,0:T(8,128)S(1)}, u32[]{:S(2)}, u32[]{:S(2)}) collective-permute-start(f32[160,128]{1,0:T(8,128)S(1)} %shard_map.74.refs_0_), channel_id=1, source_target_pairs={{0,2},{1,3},{2,0},{3,1},{4,6},{5,7},{6,4},{7,5},{8,10},{9,11},{10,... | collective-permute-start | bytes 245768 | tf_op jit(solution)/shard_map/ppermute | solution.py:349
  37.6 0.7 %collective-permute-start.20 = (bf16[128,384]{1,0:T(8,128)(2,1)S(1)}, bf16[128,384]{1,0:T(8,128)(2,1)S(1)}, u32[]{:S(2)}, u32[]{:S(2)}) collective-permute-start(bf16[128,384]{1,0:T(8,128)(2,1)S(1)} %get-tuple-element.42), channel_id=1, source_target_pairs={{0,0},{1,4},{2,8},{3,12},{4,1},{5,5},{6,9},{7,13},{8,2},{9,6},{10,... | collective-permute-start | bytes 294920 | tf_op jit(solution)/shard_map/ppermute | solution.py:407
  38.3 4.5 %collective-permute-start.21 = (bf16[128,384]{1,0:T(8,128)(2,1)S(1)}, bf16[128,384]{1,0:T(8,128)(2,1)S(1)}, u32[]{:S(2)}, u32[]{:S(2)}) collective-permute-start(bf16[128,384]{1,0:T(8,128)(2,1)S(1)} %get-tuple-element.43), channel_id=1, source_target_pairs={{0,2},{1,6},{2,10},{3,14},{4,3},{5,7},{6,11},{7,15},{8,0},{9,4},{1... | collective-permute-start | bytes 294920 | tf_op jit(solution)/shard_map/ppermute | solution.py:407
  42.9 1.6 %collective-permute-start.16 = (f32[160,128]{1,0:T(8,128)S(1)}, f32[160,128]{1,0:T(8,128)S(1)}, u32[]{:S(2)}, u32[]{:S(2)}) collective-permute-start(f32[160,128]{1,0:T(8,128)S(1)} %shard_map.75.refs_0_), channel_id=1, source_target_pairs={{0,16},{1,17},{2,18},{3,19},{4,20},{5,21},{6,22},{7,23},{8,24},{9,... | collective-permute-start | bytes 245768 | tf_op jit(solution)/shard_map/ppermute | solution.py:349
  44.4 1.9 %collective-permute-start.15 = (f32[160,128]{1,0:T(8,128)S(1)}, f32[160,128]{1,0:T(8,128)S(1)}, u32[]{:S(2)}, u32[]{:S(2)}) collective-permute-start(f32[160,128]{1,0:T(8,128)S(1)} %shard_map.75.refs_0_), channel_id=1, source_target_pairs={{0,8},{1,9},{2,10},{3,11},{4,12},{5,13},{6,14},{7,15},{8,0},{9,1},... | collective-permute-start | bytes 245768 | tf_op jit(solution)/shard_map/ppermute | solution.py:349
  46.6 2.7 %collective-permute-done.17.refs_3_ = f32[160,128]{1,0:T(8,128)S(1)} collective-permute-done((f32[160,128]{1,0:T(8,128)S(1)}, f32[160,128]{1,0:T(8,128)S(1)}, u32[]{:S(2)}, u32[]{:S(2)}) %collective-permute-start.17) | collective-permute-done | bytes 81952 | tf_op jit(solution)/shard_map/ppermute | solution.py:349
  49.4 0.6 %collective-permute-done.15.refs_1_ = f32[160,128]{1,0:T(8,128)S(1)} collective-permute-done((f32[160,128]{1,0:T(8,128)S(1)}, f32[160,128]{1,0:T(8,128)S(1)}, u32[]{:S(2)}, u32[]{:S(2)}) %collective-permute-start.15) | collective-permute-done | bytes 81952 | tf_op jit(solution)/shard_map/ppermute | solution.py:349
  50.1 1.0 %shard_map.79 = (bf16[1,128,2,384]{3,2,1,0:T(2,128)(2,1)}, f32[2,384,384]{2,1,0:T(8,128)}) custom-call(f32[4,160,128]{2,1,0:T(8,128)S(1)} %shard_map.78.refs_0_, bf16[1,128,2,384]{3,2,1,0:T(2,128)(2,1)S(1)} %shard_map.77.refs_4_.refs_1_), custom_call_target="tpu_custom_call" | custom-call | tf_op jit(solution)/shard_map/pallas_call | solution.py:28
  51.1 0.6 %collective-permute-done.22.refs_1_ = f32[4,160,128]{2,1,0:T(8,128)S(1)} collective-permute-done((f32[4,160,128]{2,1,0:T(8,128)S(1)}, f32[4,160,128]{2,1,0:T(8,128)S(1)}, u32[]{:S(2)}, u32[]{:S(2)}) %collective-permute-start.22) | collective-permute-done | bytes 327712 | tf_op jit(solution)/shard_map/ppermute | solution.py:349
  51.7 1.1 %shard_map.80 = f32[2,384,384]{2,1,0:T(8,128)} custom-call(f32[4,160,128]{2,1,0:T(8,128)S(1)} %shard_map.78.refs_0_, f32[4,160,128]{2,1,0:T(8,128)S(1)} %collective-permute-done.22.refs_1_, f32[2,384,384]{2,1,0:T(8,128)} %get-tuple-element.45.refs_2_), custom_call_target="tpu_custom_call", output_to_operand_aliasing={{}: (2, {})} | custom-call | tf_op jit(solution)/shard_map/pallas_call | solution.py:28
  (29 shorter events, 2.7 us)
Async XLA Ops:
  2.3 9.2 %collective-permute-start = (bf16[160,384]{1,0:T(8,128)(2,1)S(1)}, bf16[160,384]{1,0:T(8,128)(2,1)S(1)}, u32[]{:S(2)}, u32[]{:S(2)}) collective-permute-start(bf16[160,384]{1,0:T(8,128)(2,1)S(1)} %get-tuple-element.25), channel_id=1, source_target_pairs={{0,8},{1,9},{2,10},{3,11},{4,12},{5,13},{6,14},{7,15},{8,0},{9,1},... | collective-permute-start | bytes 368648 | tf_op jit(solution)/shard_map/ppermute | solution.py:349
  5.3 16.6 %collective-permute-start.7 = (bf16[256,512]{1,0:T(8,128)(2,1)S(1)}, bf16[256,512]{1,0:T(8,128)(2,1)S(1)}, u32[]{:S(2)}, u32[]{:S(2)}) collective-permute-start(bf16[256,512]{1,0:T(8,128)(2,1)S(1)} %get-tuple-element.27.refs_7_), channel_id=1, source_target_pairs={{0,8},{1,9},{2,10},{3,11},{4,12},{5,13},{6,14},{7,15},{8,0},{9,1},... | collective-permute-start | bytes 786440 | tf_op jit(solution)/shard_map/ppermute | solution.py:349
  5.4 16.5 %collective-permute-start.8 = (bf16[256,512]{1,0:T(8,128)(2,1)S(1)}, bf16[256,512]{1,0:T(8,128)(2,1)S(1)}, u32[]{:S(2)}, u32[]{:S(2)}) collective-permute-start(bf16[256,512]{1,0:T(8,128)(2,1)S(1)} %get-tuple-element.28.refs_8_), channel_id=1, source_target_pairs={{0,8},{1,9},{2,10},{3,11},{4,12},{5,13},{6,14},{7,15},{8,0},{9,1},... | collective-permute-start | bytes 786440 | tf_op jit(solution)/shard_map/ppermute | solution.py:349
  7.4 5.8 %collective-permute-start.1 = (bf16[128,384]{1,0:T(8,128)(2,1)S(1)}, bf16[128,384]{1,0:T(8,128)(2,1)S(1)}, u32[]{:S(2)}, u32[]{:S(2)}) collective-permute-start(bf16[128,384]{1,0:T(8,128)(2,1)S(1)} %get-tuple-element.26.refs_3_), channel_id=1, source_target_pairs={{0,2},{1,3},{2,0},{3,1},{4,6},{5,7},{6,4},{7,5},{8,10},{9,11},{10,... | collective-permute-start | bytes 294920 | tf_op jit(solution)/shard_map/ppermute | solution.py:349
  10.0 7.0 %collective-permute-start.2 = (bf16[128,384]{1,0:T(8,128)(2,1)S(1)}, bf16[128,384]{1,0:T(8,128)(2,1)S(1)}, u32[]{:S(2)}, u32[]{:S(2)}) collective-permute-start(bf16[128,384]{1,0:T(8,128)(2,1)S(1)} %get-tuple-element.26.refs_3_), channel_id=1, source_target_pairs={{0,1},{1,0},{2,3},{3,2},{4,5},{5,4},{6,7},{7,6},{8,9},{9,8},{10,11... | collective-permute-start | bytes 294920 | tf_op jit(solution)/shard_map/ppermute | solution.py:349
  11.6 6.8 %collective-permute-start.4 = (bf16[128,384]{1,0:T(8,128)(2,1)S(1)}, bf16[128,384]{1,0:T(8,128)(2,1)S(1)}, u32[]{:S(2)}, u32[]{:S(2)}) collective-permute-start(bf16[128,384]{1,0:T(8,128)(2,1)S(1)} %slice.9.refs_0_.refs_1_), channel_id=1, source_target_pairs={{0,2},{1,3},{2,0},{3,1},{4,6},{5,7},{6,4},{7,5},{8,10},{9,11},{10,... | collective-permute-start | bytes 294920 | tf_op jit(solution)/shard_map/ppermute | solution.py:349
  13.1 7.6 %collective-permute-start.3 = (bf16[128,384]{1,0:T(8,128)(2,1)S(1)}, bf16[128,384]{1,0:T(8,128)(2,1)S(1)}, u32[]{:S(2)}, u32[]{:S(2)}) collective-permute-start(bf16[128,384]{1,0:T(8,128)(2,1)S(1)} %collective-permute-done.1.refs_4_), channel_id=1, source_target_pairs={{0,1},{1,0},{2,3},{3,2},{4,5},{5,4},{6,7},{7,6},{8,9},{9,8},{10,11... | collective-permute-start | bytes 294920 | tf_op jit(solution)/shard_map/ppermute | solution.py:349
  17.0 5.0 %collective-permute-start.5 = (bf16[128,384]{1,0:T(8,128)(2,1)S(1)}, bf16[128,384]{1,0:T(8,128)(2,1)S(1)}, u32[]{:S(2)}, u32[]{:S(2)}) collective-permute-start(bf16[128,384]{1,0:T(8,128)(2,1)S(1)} %slice.9.refs_0_.refs_1_), channel_id=1, source_target_pairs={{0,1},{1,0},{2,3},{3,2},{4,5},{5,4},{6,7},{7,6},{8,9},{9,8},{10,11... | collective-permute-start | bytes 294920 | tf_op jit(solution)/shard_map/ppermute | solution.py:349
  18.3 4.7 %collective-permute-start.6 = (bf16[128,384]{1,0:T(8,128)(2,1)S(1)}, bf16[128,384]{1,0:T(8,128)(2,1)S(1)}, u32[]{:S(2)}, u32[]{:S(2)}) collective-permute-start(bf16[128,384]{1,0:T(8,128)(2,1)S(1)} %collective-permute-done.4.refs_1_.refs_2_), channel_id=1, source_target_pairs={{0,1},{1,0},{2,3},{3,2},{4,5},{5,4},{6,7},{7,6},{8,9},{9,8},{10,11... | collective-permute-start | bytes 294920 | tf_op jit(solution)/shard_map/ppermute | solution.py:349
  23.0 1.8 %collective-permute-start.9 = (bf16[512,384]{1,0:T(8,128)(2,1)S(1)}, bf16[512,384]{1,0:T(8,128)(2,1)S(1)}, u32[]{:S(2)}, u32[]{:S(2)}) collective-permute-start(bf16[512,384]{1,0:T(8,128)(2,1)S(1)} %shard_map.70.refs_7_.refs_0_), channel_id=1, source_target_pairs={{0,4},{1,5},{2,6},{3,7},{4,0},{5,1},{6,2},{7,3},{8,12},{9,13},{10,... | collective-permute-start | bytes 1179656 | tf_op jit(solution)/shard_map/ppermute | solution.py:349
  23.6 13.8 %collective-permute-start.18 = (f32[256,384]{1,0:T(8,128)S(1)}, f32[256,384]{1,0:T(8,128)S(1)}, u32[]{:S(2)}, u32[]{:S(2)}) collective-permute-start(f32[256,384]{1,0:T(8,128)S(1)} %get-tuple-element.40.refs_0_), channel_id=1, source_target_pairs={{0,4},{1,5},{2,6},{3,7},{4,0},{5,1},{6,2},{7,3},{8,12},{9,13},{10,... | collective-permute-start | bytes 1179656 | tf_op jit(solution)/shard_map/ppermute | solution.py:349
  24.2 13.3 %collective-permute-start.19 = (f32[256,384]{1,0:T(8,128)S(1)}, f32[256,384]{1,0:T(8,128)S(1)}, u32[]{:S(2)}, u32[]{:S(2)}) collective-permute-start(f32[256,384]{1,0:T(8,128)S(1)} %get-tuple-element.41.refs_1_), channel_id=1, source_target_pairs={{0,4},{1,5},{2,6},{3,7},{4,0},{5,1},{6,2},{7,3},{8,12},{9,13},{10,... | collective-permute-start | bytes 1179656 | tf_op jit(solution)/shard_map/ppermute | solution.py:349
  25.4 1.4 %collective-permute-start.10 = (f32[320,128]{1,0:T(8,128)S(1)}, f32[320,128]{1,0:T(8,128)S(1)}, u32[]{:S(2)}, u32[]{:S(2)}) collective-permute-start(f32[320,128]{1,0:T(8,128)S(1)} %get-tuple-element.36), channel_id=1, source_target_pairs={{0,4},{1,5},{2,6},{3,7},{4,0},{5,1},{6,2},{7,3},{8,12},{9,13},{10,... | collective-permute-start | bytes 491528 | tf_op jit(solution)/shard_map/ppermute | solution.py:349
  26.9 5.5 %collective-permute-start.13 = (f32[160,128]{1,0:T(8,128)S(1)}, f32[160,128]{1,0:T(8,128)S(1)}, u32[]{:S(2)}, u32[]{:S(2)}) collective-permute-start(f32[160,128]{1,0:T(8,128)S(1)} %get-tuple-element.38), channel_id=1, source_target_pairs={{0,17},{1,16},{2,19},{3,18},{4,21},{5,20},{6,23},{7,22},{8,25},{9,... | collective-permute-start | bytes 245768 | tf_op jit(solution)/shard_map/ppermute | solution.py:349
  29.3 4.8 %collective-permute-start.11 = (f32[160,128]{1,0:T(8,128)S(1)}, f32[160,128]{1,0:T(8,128)S(1)}, u32[]{:S(2)}, u32[]{:S(2)}) collective-permute-start(f32[160,128]{1,0:T(8,128)S(1)} %get-tuple-element.38), channel_id=1, source_target_pairs={{0,16},{1,17},{2,18},{3,19},{4,20},{5,21},{6,22},{7,23},{8,24},{9,... | collective-permute-start | bytes 245768 | tf_op jit(solution)/shard_map/ppermute | solution.py:349
  29.9 4.4 %collective-permute-start.12 = (f32[160,128]{1,0:T(8,128)S(1)}, f32[160,128]{1,0:T(8,128)S(1)}, u32[]{:S(2)}, u32[]{:S(2)}) collective-permute-start(f32[160,128]{1,0:T(8,128)S(1)} %get-tuple-element.37.refs_0_.refs_4_), channel_id=1, source_target_pairs={{0,1},{1,0},{2,3},{3,2},{4,5},{5,4},{6,7},{7,6},{8,9},{9,8},{10,11... | collective-permute-start | bytes 245768 | tf_op jit(solution)/shard_map/ppermute | solution.py:349
  34.3 8.4 %collective-permute-start.14 = (f32[160,128]{1,0:T(8,128)S(1)}, f32[160,128]{1,0:T(8,128)S(1)}, u32[]{:S(2)}, u32[]{:S(2)}) collective-permute-start(f32[160,128]{1,0:T(8,128)S(1)} %shard_map.74.refs_0_), channel_id=1, source_target_pairs={{0,2},{1,3},{2,0},{3,1},{4,6},{5,7},{6,4},{7,5},{8,10},{9,11},{10,... | collective-permute-start | bytes 245768 | tf_op jit(solution)/shard_map/ppermute | solution.py:349
  37.6 8.7 %collective-permute-start.20 = (bf16[128,384]{1,0:T(8,128)(2,1)S(1)}, bf16[128,384]{1,0:T(8,128)(2,1)S(1)}, u32[]{:S(2)}, u32[]{:S(2)}) collective-permute-start(bf16[128,384]{1,0:T(8,128)(2,1)S(1)} %get-tuple-element.42), channel_id=1, source_target_pairs={{0,0},{1,4},{2,8},{3,12},{4,1},{5,5},{6,9},{7,13},{8,2},{9,6},{10,... | collective-permute-start | bytes 294920 | tf_op jit(solution)/shard_map/ppermute | solution.py:407
  38.3 8.1 %collective-permute-start.21 = (bf16[128,384]{1,0:T(8,128)(2,1)S(1)}, bf16[128,384]{1,0:T(8,128)(2,1)S(1)}, u32[]{:S(2)}, u32[]{:S(2)}) collective-permute-start(bf16[128,384]{1,0:T(8,128)(2,1)S(1)} %get-tuple-element.43), channel_id=1, source_target_pairs={{0,2},{1,6},{2,10},{3,14},{4,3},{5,7},{6,11},{7,15},{8,0},{9,4},{1... | collective-permute-start | bytes 294920 | tf_op jit(solution)/shard_map/ppermute | solution.py:407
  42.8 6.6 %collective-permute-start.17 = (f32[160,128]{1,0:T(8,128)S(1)}, f32[160,128]{1,0:T(8,128)S(1)}, u32[]{:S(2)}, u32[]{:S(2)}) collective-permute-start(f32[160,128]{1,0:T(8,128)S(1)} %shard_map.75.refs_0_), channel_id=1, source_target_pairs={{0,24},{1,25},{2,26},{3,27},{4,28},{5,29},{6,30},{7,31},{8,16},{9,... | collective-permute-start | bytes 245768 | tf_op jit(solution)/shard_map/ppermute | solution.py:349
  42.9 6.5 %collective-permute-start.16 = (f32[160,128]{1,0:T(8,128)S(1)}, f32[160,128]{1,0:T(8,128)S(1)}, u32[]{:S(2)}, u32[]{:S(2)}) collective-permute-start(f32[160,128]{1,0:T(8,128)S(1)} %shard_map.75.refs_0_), channel_id=1, source_target_pairs={{0,16},{1,17},{2,18},{3,19},{4,20},{5,21},{6,22},{7,23},{8,24},{9,... | collective-permute-start | bytes 245768 | tf_op jit(solution)/shard_map/ppermute | solution.py:349
  44.4 5.5 %collective-permute-start.15 = (f32[160,128]{1,0:T(8,128)S(1)}, f32[160,128]{1,0:T(8,128)S(1)}, u32[]{:S(2)}, u32[]{:S(2)}) collective-permute-start(f32[160,128]{1,0:T(8,128)S(1)} %shard_map.75.refs_0_), channel_id=1, source_target_pairs={{0,8},{1,9},{2,10},{3,11},{4,12},{5,13},{6,14},{7,15},{8,0},{9,1},... | collective-permute-start | bytes 245768 | tf_op jit(solution)/shard_map/ppermute | solution.py:349
  50.0 1.7 %collective-permute-start.22 = (f32[4,160,128]{2,1,0:T(8,128)S(1)}, f32[4,160,128]{2,1,0:T(8,128)S(1)}, u32[]{:S(2)}, u32[]{:S(2)}) collective-permute-start(f32[4,160,128]{2,1,0:T(8,128)S(1)} %shard_map.78.refs_0_), channel_id=1, source_target_pairs={{0,4},{1,5},{2,6},{3,7},{4,0},{5,1},{6,2},{7,3},{8,12},{9,13},{10,... | collective-permute-start | bytes 983048 | tf_op jit(solution)/shard_map/ppermute | solution.py:349
